TPU v7x, 32 devices: a whole 2x2x4 slice. The times are simulated.
32 devices in a mesh: grp: 4 (over z), mem: 8 (over y, x, core).
Axes of the slice: x: 2, y: 2, z: 4, core: 2. Of those that a mesh axis runs over, the one named last changes fastest.
Arguments:
- candidates: bfloat16 [32768, 4096], P(('grp', 'mem')), may hold values from -1 to 1
- round_one: bfloat16 [2048, 4096], P(('grp', 'mem')), may hold values from -1 to 1
- counts: int32 [4, 8], P('grp', 'mem'), may hold values from 1 to 64, 192 in all within a row
- chosen: int32 [4, 128], P('grp'), may hold values from 0 to 191, as said below
Outputs:
- group_dist: float32 [32768], P(('grp', 'mem'))
- final_dist: float32 [32768], P(('grp', 'mem'))
Inputs may be any that keep to these rules, and one draw needn't show every extreme that they name: In each group the counts sum to 192, and some device of each group has exactly 64. `chosen`: within a group the 128 positions are distinct, each below 192.
All inputs are finite; a program needn't handle non-finite values.
Results may differ from a plain program's by a relative error of at most 0.0003.
Values may be sent and summed in bfloat16 or wider, within the bound.
No kernel may reach another device: no remote copies, remote signals or barrier semaphores. Data moves between devices by JAX's collectives and lax.ppermute only.
A program may use at most 128 MiB of HBM per device.

v0:
```python
import jax
import jax.numpy as jnp
from jax import lax
from jax.sharding import PartitionSpec as P


def sq_norms(matrix):
    return jnp.sum(jnp.square(matrix.astype(jnp.float32)), axis=1)


def distances(cand_rows, cand_norm, center_rows):
    inner = lax.dot_general(
        cand_rows, center_rows, (((1,), (1,)), ((), ())), preferred_element_type=jnp.float32
    )
    return cand_norm[:, None] + sq_norms(center_rows)[None, :] - 2.0 * inner


def lookup(table, index_values):
    entries = jnp.arange(table.shape[0], dtype=jnp.int32)
    match = index_values[:, None] == entries[None, :]
    return jnp.sum(jnp.where(match, table[None, :], 0), axis=1)


def body(candidates, round_one, counts, chosen):
    mem_size = lax.axis_size("mem")
    my_index = lax.axis_index("mem")
    slot_max = round_one.shape[0]
    width = round_one.shape[1]
    picks_total = chosen.shape[1]
    group_counts = lax.all_gather(counts, "mem", axis=1, tiled=True)[0]
    offsets = jnp.cumsum(group_counts) - group_counts
    picked_ids = chosen[0]
    cand_norm = sq_norms(candidates)
    start_state = (
        jnp.full((candidates.shape[0],), jnp.inf, jnp.float32),
        jnp.zeros((picks_total, width), jnp.float32),
    )
    block_rows = lax.all_gather(round_one, "mem", axis=0, tiled=True)
    slot_ids = jnp.arange(block_rows.shape[0], dtype=jnp.int32)
    holder = slot_ids // slot_max
    within = slot_ids % slot_max
    usable = within < lookup(group_counts, holder)
    position = lookup(offsets, holder) + within
    gaps = distances(candidates, cand_norm, block_rows)
    gaps = jnp.where(usable[None, :], gaps, jnp.inf)
    nearest = jnp.minimum(start_state[0], jnp.min(gaps, axis=1))
    select = ((picked_ids[:, None] == position[None, :]) & usable[None, :]).astype(jnp.bfloat16)
    collected = jnp.dot(select, block_rows, preferred_element_type=jnp.float32)
    nearest, collected = (nearest, collected)
    picked = collected.astype(jnp.bfloat16)
    final_start = jnp.full((candidates.shape[0],), jnp.inf, jnp.float32)
    share = picks_total // mem_size
    my_share = lax.dynamic_slice_in_dim(picked, my_index * share, share, 0)
    final = jnp.minimum(
        final_start,
        jnp.min(
            distances(
                candidates, cand_norm, lax.all_gather(my_share, ("grp", "mem"), axis=0, tiled=True)
            ),
            axis=1,
        ),
    )
    return (nearest, final)


def solution(mesh):
    in_specs = (P(("grp", "mem"), None), P(("grp", "mem"), None), P("grp", "mem"), P("grp", None))
    out_specs = (P(("grp", "mem")), P(("grp", "mem")))
    return jax.shard_map(body, mesh=mesh, in_specs=in_specs, out_specs=out_specs, check_vma=False)
```

profile of v0, /device:TPU:0, one launch (start us, length us, event | category | flops | bytes accessed | tf_op | source)
XLA Modules:
  0.0 134.0 jit_solution(6255073963605706535)
XLA Ops:
  7.2 0.0 all-gather.3.cloned.1.call-start
  7.2 0.7 all-gather.3.cloned.1.call-update
  7.9 0.0 all-gather.5.cloned.1.call-start
  8.6 1.2 dynamic-slice
  9.8 0.7 bitcast_dynamic-update-slice_fusion
  10.5 9.5 %all-reduce = s32[8]{0:T(128)S(1)} all-reduce(s32[8]{0:T(128)S(1)} %bitcast_dynamic-update-slice_fusion), channel_id=1, replica_groups=mesh['grp'=4,'mem'=8] {'mem'}, use_global_device_ids=true, to_apply=%add | all-reduce | flops 8 | bytes 64
  20.0 0.2 reduce-window_clone.1
  20.2 0.1 select_reduce_fusion.1
  20.3 29.0 %all-gather.3.cloned.1.call-done = bf16[512,4096]{1,0:T(8,128)(2,1)} async-done(((bf16[64,4096]{1,0:T(8,128)(2,1)}), bf16[512,4096]{1,0:T(8,128)(2,1)}) %all-gather.3.cloned.1.call-update) | async-done | bytes 4194320 | tf_op jit(solution)/shard_map/all_gather | solution.py:38
  49.3 3.0 %fusion.1 = bf16[128,4096]{1,0:T(8,128)(2,1)S(1)} fusion(bf16[512,4096]{1,0:T(8,128)(2,1)} %all-gather.3.cloned.1.call-done, s32[512]{0:T(512)S(1)} %fusion.10, s32[128]{0:T(128)} %bitcast.18, pred[512]{0:T(512)(128)(4,1)S(1)} %fusion.11), kind=kOutput, calls=%fused_computation.7 | convolution fusion | flops 537001984 | bytes 5245952 | tf_op jit(solution)/shard_map/dot_general | solution.py:48
  52.3 0.7 dynamic-slice_convert_fusion
  53.0 0.0 all-gather.5.cloned.1.call-update
  53.0 0.0 copy-start
  53.0 0.0 copy-start.1
  53.0 5.2 %multiply_reduce_fusion = f32[1024]{0:T(1024)S(1)} fusion(bf16[1024,4096]{1,0:T(8,128)(2,1)} %param.4), kind=kLoop, calls=%fused_computation | loop fusion | flops 12581888 | bytes 8392704 | tf_op jit(solution)/shard_map/reduce_sum | solution.py:8
  58.2 0.0 copy-done
  58.2 0.9 multiply_reduce_fusion.2
  59.1 0.9 copy-done.1
  60.0 5.2 %select_reduce_fusion = f32[1024]{0:T(1024)} fusion(bf16[1024,4096]{1,0:T(8,128)(2,1)S(1)} %copy-done.1, bf16[512,4096]{1,0:T(8,128)(2,1)S(1)} %copy-done, f32[512]{0:T(512)S(1)} %multiply_reduce_fusion.2, f32[1024]{0:T(1024)S(1)} %multiply_reduce_fusion, pred[512]{0:T(512)(128)(4,1)S(1)} %fusion.11), kind=kOutput, calls=%fused_computation.5 | convolution fusion | flops 4297587712 | bytes 12593664 | tf_op jit(solution)/shard_map/dot_general | solution.py:12
  65.3 49.9 %all-gather.5.cloned.1.call-done = bf16[512,4096]{1,0:T(8,128)(2,1)} async-done(((bf16[16,4096]{1,0:T(8,128)(2,1)}), bf16[512,4096]{1,0:T(8,128)(2,1)}) %all-gather.5.cloned.1.call-update) | async-done | bytes 4194320 | tf_op jit(solution)/shard_map/all_gather | solution.py:58
  115.2 0.0 copy-start.2
  115.2 3.2 %multiply_reduce_fusion.1 = f32[512]{0:T(512)S(1)} fusion(bf16[512,4096]{1,0:T(8,128)(2,1)} %all-gather.5.cloned.1.call-done), kind=kLoop, calls=%fused_computation.1 | loop fusion | flops 6290944 | bytes 4196352 | tf_op jit(solution)/shard_map/reduce_sum | solution.py:8
  118.4 0.2 copy-done.2
  118.6 8.5 %fusion = f32[1024]{0:T(1024)} fusion(bf16[512,4096]{1,0:T(8,128)(2,1)S(1)} %copy-done.2, bf16[1024,4096]{1,0:T(8,128)(2,1)} %param.4, f32[512]{0:T(512)S(1)} %multiply_reduce_fusion.1, f32[1024]{0:T(1024)S(1)} %multiply_reduce_fusion), kind=kOutput, calls=%fused_computation.4 | convolution fusion | flops 4297063424 | bytes 12593152 | tf_op jit(solution)/shard_map/dot_general | solution.py:12
  (5 shorter events, 0.0 us)
Async XLA Ops:
  7.2 42.2 %all-gather.3.cloned.1.call-start = ((), (), s32[]{:S(2)}) async-start(), calls=%async_computation | async-start | bytes 4718592 | tf_op jit(solution)/shard_map/all_gather | solution.py:38
  7.9 107.3 %all-gather.5.cloned.1.call-start = ((), (), s32[]{:S(2)}) async-start(), calls=%async_computation.1 | async-start | bytes 4325376 | tf_op jit(solution)/shard_map/all_gather | solution.py:58
  53.0 5.2 %copy-start = (bf16[512,4096]{1,0:T(8,128)(2,1)S(1)}, bf16[512,4096]{1,0:T(8,128)(2,1)}, u32[]{:S(2)}) copy-start(bf16[512,4096]{1,0:T(8,128)(2,1)} %all-gather.3.cloned.1.call-done) | copy-start | bytes 12582916
  53.0 7.0 %copy-start.1 = (bf16[1024,4096]{1,0:T(8,128)(2,1)S(1)}, bf16[1024,4096]{1,0:T(8,128)(2,1)}, u32[]{:S(2)}) copy-start(bf16[1024,4096]{1,0:T(8,128)(2,1)} %param.4) | copy-start | bytes 25165828
  115.2 3.4 %copy-start.2 = (bf16[512,4096]{1,0:T(8,128)(2,1)S(1)}, bf16[512,4096]{1,0:T(8,128)(2,1)}, u32[]{:S(2)}) copy-start(bf16[512,4096]{1,0:T(8,128)(2,1)} %all-gather.5.cloned.1.call-done) | copy-start | bytes 12582916
Sparse Core Ops, SparseCore 0:
  9.9 39.4 all-gather.2
  53.1 62.0 all-gather.4
where the time goes:
time: 134 us
  waiting for transfers between devices  79.6 us (59%)
  matrix products  16.7 us (12%)
  between operations  14.7 us (11%)
  other arithmetic  9.64 us (7%)
  blocking collectives  9.48 us (7%)
  local copies, waits for them, and re-layouts  3.72 us (3%)
    all_gather x1, waiting for transfers between devices, body(): lax.all_gather(my_share, ('grp', 'mem'), axis=0, tiled=True)  49.9 us
    all_gather x1, waiting for transfers between devices, body(): block_rows = lax.all_gather(round_one, 'mem', axis=0, tiled=True)  29 us
    dot_general x2, matrix products, distances(): lax.dot_general(cand_rows, center_rows, (((1,), (1,)), ((), ())), preferr...  13.8 us
    unnamed x1, blocking collectives  9.48 us
    reduce_sum x3, other arithmetic, sq_norms(): return jnp.sum(jnp.square(matrix.astype(jnp.float32)), axis=1)  9.35 us
    unnamed x9, local copies, waits for them, and re-layouts  3.05 us
    dot_general x1, matrix products, body(): collected = jnp.dot(select, block_rows, preferred_element_type=jnp.float32)  2.95 us
  transfers between devices with their start and end apart: 2, of which 2 were waited for; matrix products, arithmetic and copies ran while one was open for 10% of the time, Pallas kernels for 0%

commit v1 on v0

v1 whole, which is shorter than its diff:
```python
import jax
import jax.numpy as jnp
from jax import lax
from jax.sharding import PartitionSpec as P


def sq_norms(matrix):
    return jnp.sum(jnp.square(matrix.astype(jnp.float32)), axis=1)


def axis_bits(size):
    return [1 << b for b in range(size.bit_length() - 1)]


def flips(size):
    chip_bits = [b for b in axis_bits(size) if b > 1]
    turned = chip_bits[1:] + chip_bits[:1]
    return chip_bits, turned


def mixed_permute(block, size, stage):
    even, odd = flips(size)
    pairs = [(m, m ^ (odd[stage] if m & 1 else even[stage])) for m in range(size)]
    return lax.ppermute(block, "mem", pairs)


def core_permute(block, size):
    return lax.ppermute(block, "mem", [(m, m ^ 1) for m in range(size)])


def gather_blocks(block, size, me):
    even, odd = flips(size)
    odd_core = me & 1
    held = [(block, me)]
    for stage in range(len(even)):
        step = jnp.where(odd_core == 1, odd[stage], even[stage])
        held = held + [(mixed_permute(b, size, stage), o ^ step) for b, o in held]
    other = []
    for stage_count, (b, _) in enumerate(held):
        other.append(core_permute(b, size))
    sib = me ^ 1
    origins = [sib]
    for stage in range(len(even)):
        step = jnp.where(odd_core == 1, even[stage], odd[stage])
        origins = origins + [o ^ step for o in origins]
    return held + list(zip(other, origins))


def body(candidates, round_one, counts, chosen):
    mem_size = lax.axis_size("mem")
    grp_size = lax.axis_size("grp")
    me = lax.axis_index("mem")
    slot_max, width = round_one.shape
    picks_total = chosen.shape[1]
    share = picks_total // mem_size
    row_ids = jnp.arange(slot_max, dtype=jnp.int32)

    mark = (row_ids[:, None] >= counts[0, 0]) & (jnp.arange(width) == 0)[None, :]
    marked = jnp.where(mark, jnp.bfloat16(2.0), round_one)
    held = gather_blocks(marked, mem_size, me)
    cand_norm = sq_norms(candidates)

    live_counts = [jnp.sum((b[:, 0] < 1.5).astype(jnp.int32)) for b, _ in held]
    origins = [o for _, o in held]
    offsets = [
        sum(jnp.where(o2 < o1, n2, 0) for n2, o2 in zip(live_counts, origins)) for o1 in origins
    ]
    usable = jnp.concatenate([row_ids < n for n in live_counts])
    position = jnp.concatenate([row_ids + o for o in offsets])
    rows = jnp.concatenate([b for b, _ in held], axis=0)

    my_ids = lax.dynamic_slice_in_dim(chosen[0], me * share, share, 0)
    select = ((my_ids[:, None] == position[None, :]) & usable[None, :]).astype(jnp.bfloat16)
    picked = jnp.dot(select, rows, preferred_element_type=jnp.float32).astype(jnp.bfloat16)

    far = [
        lax.ppermute(picked, "grp", [(g, (g + k) % grp_size) for g in range(grp_size)])
        for k in range(1, grp_size)
    ]
    far_rows = jnp.concatenate(far, axis=0)
    far_blocks = [b for b, _ in gather_blocks(far_rows, mem_size, me)]

    inner = lax.dot_general(
        candidates, rows, (((1,), (1,)), ((), ())), preferred_element_type=jnp.float32
    )
    gaps = cand_norm[:, None] + sq_norms(rows)[None, :] - 2.0 * inner
    nearest = jnp.min(jnp.where(usable[None, :], gaps, jnp.inf), axis=1)
    is_pick = jnp.any((chosen[0][:, None] == position[None, :]) & usable[None, :], axis=0)
    own_final = jnp.min(jnp.where(is_pick[None, :], gaps, jnp.inf), axis=1)

    far_all = jnp.concatenate(far_blocks, axis=0)
    far_inner = lax.dot_general(
        candidates, far_all, (((1,), (1,)), ((), ())), preferred_element_type=jnp.float32
    )
    far_gaps = cand_norm[:, None] + sq_norms(far_all)[None, :] - 2.0 * far_inner
    final = jnp.minimum(own_final, jnp.min(far_gaps, axis=1))
    return nearest, final


def solution(mesh):
    in_specs = (P(("grp", "mem"), None), P(("grp", "mem"), None), P("grp", "mem"), P("grp", None))
    out_specs = (P(("grp", "mem")), P(("grp", "mem")))
    return jax.shard_map(body, mesh=mesh, in_specs=in_specs, out_specs=out_specs, check_vma=False)
```

time: 134 us -> 113 us (0.84)
  waiting for transfers between devices: 79.6 us -> 18.4 us
  between operations: 14.7 us -> 38.2 us
  starting transfers between devices: 0.08 us -> 14.3 us
  other arithmetic: 9.64 us -> 19.8 us
  blocking collectives: 9.48 us -> 0 us
  local copies, waits for them, and re-layouts: 3.72 us -> 6.42 us
    all_gather x2 -> x0, waiting for transfers between devices: 78.9 us -> none  [the longest x1 49.9 us: body(): lax.all_gather(my_share, ('grp', 'mem'), axis=0, tiled=True)]
    ppermute x0 -> x17, waiting for transfers between devices: none -> 18.4 us  [the longest x3 10.3 us: body(): lax.ppermute(picked, 'grp', [(g, (g + k) % grp_size) for g in range(grp_s...]
    ppermute x0 -> x17, starting transfers between devices: none -> 14.3 us  [the longest x6 7.83 us: mixed_permute(): return lax.ppermute(block, 'mem', pairs)]
    unnamed x1 -> x0, blocking collectives: 9.48 us -> none
    lt x1 -> x8, other arithmetic: 0.01 us -> 5.21 us  [body(): usable = jnp.concatenate([row_ids < n for n in live_counts])]
    reduce_sum x1 -> x8, other arithmetic: 0.09 us -> 5.12 us  [body(): live_counts = [jnp.sum((b[:, 0] < 1.5).astype(jnp.int32)) for b, _ in held]]
    reduce_sum x3, other arithmetic: 9.35 us -> 6.66 us  [sq_norms(): return jnp.sum(jnp.square(matrix.astype(jnp.float32)), axis=1)]
    unnamed x9 -> x22, local copies, waits for them, and re-layouts: 3.05 us -> 5.27 us
  transfers between devices with their start and end apart: 2 -> 17, of which waited for: 2 -> 4; matrix products, arithmetic and copies ran while one was open for 10% -> 24% of each run, Pallas kernels for 0% -> 0%
where the time goes in v1:
time: 113 us
  between operations  38.2 us (34%)
  other arithmetic  19.8 us (18%)
  waiting for transfers between devices  18.4 us (16%)
  matrix products  15.6 us (14%)
  starting transfers between devices  14.3 us (13%)
  local copies, waits for them, and re-layouts  6.42 us (6%)
    ppermute x3, waiting for transfers between devices, body(): lax.ppermute(picked, 'grp', [(g, (g + k) % grp_size) for g in range(grp_s...  10.3 us
    dot_general x1, matrix products, body(): lax.dot_general(candidates, rows, (((1,), (1,)), ((), ())), preferred_ele...  9.05 us
    ppermute x6, starting transfers between devices, mixed_permute(): return lax.ppermute(block, 'mem', pairs)  7.83 us
    reduce_sum x3, other arithmetic, sq_norms(): return jnp.sum(jnp.square(matrix.astype(jnp.float32)), axis=1)  6.66 us
    ppermute x6, waiting for transfers between devices, mixed_permute(): return lax.ppermute(block, 'mem', pairs)  6.52 us
    unnamed x22, local copies, waits for them, and re-layouts  5.27 us
    lt x8, other arithmetic, body(): usable = jnp.concatenate([row_ids < n for n in live_counts])  5.21 us
    reduce_sum x8, other arithmetic, body(): live_counts = [jnp.sum((b[:, 0] < 1.5).astype(jnp.int32)) for b, _ in held]  5.12 us
  transfers between devices with their start and end apart: 17, of which 4 were waited for; matrix products, arithmetic and copies ran while one was open for 24% of the time, Pallas kernels for 0%

profile of v1, /device:TPU:0, one launch (start us, length us, event | category | flops | bytes accessed | tf_op | source)
XLA Modules:
  0.0 112.6 jit_solution(6603441087956577249)
XLA Ops:
  1.3 2.1 %constant_dynamic-update-slice_fusion.7 = (bf16[512,4096]{1,0:T(8,128)(2,1)}, bf16[64,4096]{1,0:T(8,128)(2,1)S(1)}) fusion(bf16[64,4096]{1,0:T(8,128)(2,1)} %param.5, pred[4096]{0:T(1024)(128)(4,1)S(1)} %iota_compare_fusion, pred[64]{0:T(512)(128)(4,1)S(1)} %iota_compare_fusion.8), kind=kLoop, calls=%fused_computation.18 | loop fusion | flops 524287 | bytes 1577024
  3.8 2.5 %collective-permute-start.1 = (bf16[64,4096]{1,0:T(8,128)(2,1)S(1)}, bf16[64,4096]{1,0:T(8,128)(2,1)S(1)}, u32[]{:S(2)}, u32[]{:S(2)}) collective-permute-start(bf16[64,4096]{1,0:T(8,128)(2,1)S(1)} %get-tuple-element.5), channel_id=1, source_target_pairs={{0,4},{1,3},{2,6},{3,1},{4,0},{5,7},{6,2},{7,5},{8,12},{9,11},{10,... | collective-permute-start | bytes 1572872 | tf_op jit(solution)/shard_map/ppermute | solution.py:24
  6.4 1.5 %collective-permute-start = (bf16[64,4096]{1,0:T(8,128)(2,1)S(1)}, bf16[64,4096]{1,0:T(8,128)(2,1)S(1)}, u32[]{:S(2)}, u32[]{:S(2)}) collective-permute-start(bf16[64,4096]{1,0:T(8,128)(2,1)S(1)} %get-tuple-element.5), channel_id=1, source_target_pairs={{0,2},{1,5},{2,0},{3,7},{4,6},{5,1},{6,4},{7,3},{8,10},{9,13},{10,... | collective-permute-start | bytes 1572872 | tf_op jit(solution)/shard_map/ppermute | solution.py:24
  7.9 5.1 %multiply_reduce_fusion = f32[1024]{0:T(1024)S(1)} fusion(bf16[1024,4096]{1,0:T(8,128)(2,1)} %param.4), kind=kLoop, calls=%fused_computation | loop fusion | flops 12581888 | bytes 8392704 | tf_op jit(solution)/shard_map/reduce_sum | solution.py:8
  37.0 0.8 constant_dynamic-update-slice_fusion.6
  37.8 0.9 constant_dynamic-update-slice_fusion.5
  57.0 0.8 constant_dynamic-update-slice_fusion.4
  57.9 0.8 constant_dynamic-update-slice_fusion.3
  58.7 0.8 constant_dynamic-update-slice_fusion.2
  59.6 0.8 constant_dynamic-update-slice_fusion.1
  66.5 0.8 constant_dynamic-update-slice_fusion
  67.3 3.0 %convolution_convert_fusion = bf16[16,4096]{1,0:T(8,128)(2,1)S(1)} fusion(bf16[512,4096]{1,0:T(8,128)(2,1)} %constant_dynamic-update-slice_fusion, s32[512]{0:T(512)S(1)} %concatenate.18, s32[16]{0:T(128)S(1)} %dynamic-slice_bitcast_fusion, pred[512]{0:T(512)(128)(4,1)S(1)} %concatenate.16), kind=kOutput, calls=%fused_computation.3 | convolution fusion | flops 67190784 | bytes 4328000 | tf_op jit(solution)/shard_map/dot_general | solution.py:74
  70.4 1.6 %collective-permute-start.7 = (bf16[16,4096]{1,0:T(8,128)(2,1)S(1)}, bf16[16,4096]{1,0:T(8,128)(2,1)S(1)}, u32[]{:S(2)}, u32[]{:S(2)}) collective-permute-start(bf16[16,4096]{1,0:T(8,128)(2,1)S(1)} %convolution_convert_fusion), channel_id=1, source_target_pairs={{0,8},{8,16},{16,24},{24,0},{1,9},{9,17},{17,25},{25,1},{2,10},{10... | collective-permute-start | bytes 393224 | tf_op jit(solution)/shard_map/ppermute | solution.py:77
  71.9 0.9 multiply_reduce_fusion.1
  72.8 2.7 %collective-permute-start.9 = (bf16[16,4096]{1,0:T(8,128)(2,1)S(1)}, bf16[16,4096]{1,0:T(8,128)(2,1)S(1)}, u32[]{:S(2)}, u32[]{:S(2)}) collective-permute-start(bf16[16,4096]{1,0:T(8,128)(2,1)S(1)} %convolution_convert_fusion), channel_id=1, source_target_pairs={{0,24},{8,0},{16,8},{24,16},{1,25},{9,1},{17,9},{25,17},{2,26},{10... | collective-permute-start | bytes 393224 | tf_op jit(solution)/shard_map/ppermute | solution.py:77
  76.2 2.1 %collective-permute-done.7 = bf16[16,4096]{1,0:T(8,128)(2,1)S(1)} collective-permute-done((bf16[16,4096]{1,0:T(8,128)(2,1)S(1)}, bf16[16,4096]{1,0:T(8,128)(2,1)S(1)}, u32[]{:S(2)}, u32[]{:S(2)}) %collective-permute-start.7) | collective-permute-done | bytes 131104 | tf_op jit(solution)/shard_map/ppermute | solution.py:77
  78.3 8.2 %collective-permute-done.8 = bf16[16,4096]{1,0:T(8,128)(2,1)S(1)} collective-permute-done((bf16[16,4096]{1,0:T(8,128)(2,1)S(1)}, bf16[16,4096]{1,0:T(8,128)(2,1)S(1)}, u32[]{:S(2)}, u32[]{:S(2)}) %collective-permute-start.8) | collective-permute-done | bytes 131104 | tf_op jit(solution)/shard_map/ppermute | solution.py:77
  86.6 1.6 %collective-permute-start.11 = (bf16[48,4096]{1,0:T(8,128)(2,1)S(1)}, bf16[48,4096]{1,0:T(8,128)(2,1)S(1)}, u32[]{:S(2)}, u32[]{:S(2)}) collective-permute-start(bf16[48,4096]{1,0:T(8,128)(2,1)S(1)} %get-tuple-element.6), channel_id=1, source_target_pairs={{0,4},{1,3},{2,6},{3,1},{4,0},{5,7},{6,2},{7,5},{8,12},{9,11},{10,... | collective-permute-start | bytes 1179656 | tf_op jit(solution)/shard_map/ppermute | solution.py:24
  88.8 9.1 %select_reduce_fusion = (f32[1024]{0:T(1024)S(1)}, f32[1024]{0:T(1024)}) fusion(f32[512]{0:T(512)S(1)} %multiply_reduce_fusion.1, f32[1024]{0:T(1024)S(1)} %multiply_reduce_fusion, pred[512]{0:T(512)(128)(4,1)S(1)} %and_reduce_fusion, pred[512]{0:T(512)(128)(4,1)S(1)} %concatenate.16, bf16[512,4096]{1,0:T(8,128)(2,1)S(1)} %copy-done, ...), kind=kOutput, calls=%fused_computation.5 | convolution fusion | flops 4298635264 | bytes 12598272 | tf_op jit(solution)/shard_map/dot_general | solution.py:83
  98.3 1.2 %collective-permute-start.12 = (bf16[48,4096]{1,0:T(8,128)(2,1)S(1)}, bf16[48,4096]{1,0:T(8,128)(2,1)S(1)}, u32[]{:S(2)}, u32[]{:S(2)}) collective-permute-start(bf16[48,4096]{1,0:T(8,128)(2,1)S(1)} %collective-permute-done.10), channel_id=1, source_target_pairs={{0,4},{1,3},{2,6},{3,1},{4,0},{5,7},{6,2},{7,5},{8,12},{9,11},{10,... | collective-permute-start | bytes 1179656 | tf_op jit(solution)/shard_map/ppermute | solution.py:24
  99.6 6.5 %collective-permute-done.12 = bf16[48,4096]{1,0:T(8,128)(2,1)S(1)} collective-permute-done((bf16[48,4096]{1,0:T(8,128)(2,1)S(1)}, bf16[48,4096]{1,0:T(8,128)(2,1)S(1)}, u32[]{:S(2)}, u32[]{:S(2)}) %collective-permute-start.12) | collective-permute-done | bytes 393248 | tf_op jit(solution)/shard_map/ppermute | solution.py:24
  106.3 1.6 %collective-permute-done.16 = bf16[48,4096]{1,0:T(8,128)(2,1)S(1)} collective-permute-done((bf16[48,4096]{1,0:T(8,128)(2,1)S(1)}, bf16[48,4096]{1,0:T(8,128)(2,1)S(1)}, u32[]{:S(2)}, u32[]{:S(2)}) %collective-permute-start.16) | collective-permute-done | bytes 393248 | tf_op jit(solution)/shard_map/ppermute | solution.py:28
  107.9 0.7 multiply_reduce_fusion.2
  108.6 3.5 %fusion = f32[1024]{0:T(1024)S(1)} fusion(bf16[384,4096]{1,0:T(8,128)(2,1)S(1)} %constant_dynamic-update-slice_fusion.11, bf16[1024,4096]{1,0:T(8,128)(2,1)S(1)} %bitcast.21, f32[384]{0:T(512)S(1)} %multiply_reduce_fusion.2, f32[1024]{0:T(1024)S(1)} %multiply_reduce_fusion), kind=kOutput, calls=%fused_computation.8 | convolution fusion | flops 3222797312 | bytes 11544064 | tf_op jit(solution)/shard_map/dot_general | solution.py:92
  (72 shorter events, 14.9 us)
Async XLA Ops:
  3.4 15.5 %copy-start.1 = (s32[1,128]{1,0:T(1,128)S(1)}, s32[1,128]{1,0:T(1,128)}, u32[]{:S(2)}) copy-start(s32[1,128]{1,0:T(1,128)} %param.7) | copy-start | bytes 1540
  3.4 15.6 %collective-permute-start.3 = (bf16[64,4096]{1,0:T(8,128)(2,1)S(1)}, bf16[64,4096]{1,0:T(8,128)(2,1)S(1)}, u32[]{:S(2)}, u32[]{:S(2)}) collective-permute-start(bf16[64,4096]{1,0:T(8,128)(2,1)S(1)} %get-tuple-element.5), channel_id=1, source_target_pairs={{0,1},{1,0},{2,3},{3,2},{4,5},{5,4},{6,7},{7,6},{8,9},{9,8},{10,11... | collective-permute-start | bytes 1572872 | tf_op jit(solution)/shard_map/ppermute | solution.py:28
  3.8 20.3 %collective-permute-start.1 = (bf16[64,4096]{1,0:T(8,128)(2,1)S(1)}, bf16[64,4096]{1,0:T(8,128)(2,1)S(1)}, u32[]{:S(2)}, u32[]{:S(2)}) collective-permute-start(bf16[64,4096]{1,0:T(8,128)(2,1)S(1)} %get-tuple-element.5), channel_id=1, source_target_pairs={{0,4},{1,3},{2,6},{3,1},{4,0},{5,7},{6,2},{7,5},{8,12},{9,11},{10,... | collective-permute-start | bytes 1572872 | tf_op jit(solution)/shard_map/ppermute | solution.py:24
  6.4 24.3 %collective-permute-start = (bf16[64,4096]{1,0:T(8,128)(2,1)S(1)}, bf16[64,4096]{1,0:T(8,128)(2,1)S(1)}, u32[]{:S(2)}, u32[]{:S(2)}) collective-permute-start(bf16[64,4096]{1,0:T(8,128)(2,1)S(1)} %get-tuple-element.5), channel_id=1, source_target_pairs={{0,2},{1,5},{2,0},{3,7},{4,6},{5,1},{6,4},{7,3},{8,10},{9,13},{10,... | collective-permute-start | bytes 1572872 | tf_op jit(solution)/shard_map/ppermute | solution.py:24
  35.9 3.4 %collective-permute-start.5 = (bf16[64,4096]{1,0:T(8,128)(2,1)S(1)}, bf16[64,4096]{1,0:T(8,128)(2,1)S(1)}, u32[]{:S(2)}, u32[]{:S(2)}) collective-permute-start(bf16[64,4096]{1,0:T(8,128)(2,1)S(1)} %collective-permute-done.1), channel_id=1, source_target_pairs={{0,1},{1,0},{2,3},{3,2},{4,5},{5,4},{6,7},{7,6},{8,9},{9,8},{10,11... | collective-permute-start | bytes 1572872 | tf_op jit(solution)/shard_map/ppermute | solution.py:28
  36.0 8.5 %collective-permute-start.4 = (bf16[64,4096]{1,0:T(8,128)(2,1)S(1)}, bf16[64,4096]{1,0:T(8,128)(2,1)S(1)}, u32[]{:S(2)}, u32[]{:S(2)}) collective-permute-start(bf16[64,4096]{1,0:T(8,128)(2,1)S(1)} %collective-permute-done), channel_id=1, source_target_pairs={{0,1},{1,0},{2,3},{3,2},{4,5},{5,4},{6,7},{7,6},{8,9},{9,8},{10,11... | collective-permute-start | bytes 1572872 | tf_op jit(solution)/shard_map/ppermute | solution.py:28
  36.5 14.5 %collective-permute-start.2 = (bf16[64,4096]{1,0:T(8,128)(2,1)S(1)}, bf16[64,4096]{1,0:T(8,128)(2,1)S(1)}, u32[]{:S(2)}, u32[]{:S(2)}) collective-permute-start(bf16[64,4096]{1,0:T(8,128)(2,1)S(1)} %collective-permute-done), channel_id=1, source_target_pairs={{0,4},{1,3},{2,6},{3,1},{4,0},{5,7},{6,2},{7,5},{8,12},{9,11},{10,... | collective-permute-start | bytes 1572872 | tf_op jit(solution)/shard_map/ppermute | solution.py:24
  57.0 3.4 %collective-permute-start.6 = (bf16[64,4096]{1,0:T(8,128)(2,1)S(1)}, bf16[64,4096]{1,0:T(8,128)(2,1)S(1)}, u32[]{:S(2)}, u32[]{:S(2)}) collective-permute-start(bf16[64,4096]{1,0:T(8,128)(2,1)S(1)} %collective-permute-done.2), channel_id=1, source_target_pairs={{0,1},{1,0},{2,3},{3,2},{4,5},{5,4},{6,7},{7,6},{8,9},{9,8},{10,11... | collective-permute-start | bytes 1572872 | tf_op jit(solution)/shard_map/ppermute | solution.py:28
  67.3 4.6 %copy-start = (bf16[512,4096]{1,0:T(8,128)(2,1)S(1)}, bf16[512,4096]{1,0:T(8,128)(2,1)}, u32[]{:S(2)}) copy-start(bf16[512,4096]{1,0:T(8,128)(2,1)} %constant_dynamic-update-slice_fusion) | copy-start | bytes 12582916
  70.4 7.9 %collective-permute-start.7 = (bf16[16,4096]{1,0:T(8,128)(2,1)S(1)}, bf16[16,4096]{1,0:T(8,128)(2,1)S(1)}, u32[]{:S(2)}, u32[]{:S(2)}) collective-permute-start(bf16[16,4096]{1,0:T(8,128)(2,1)S(1)} %convolution_convert_fusion), channel_id=1, source_target_pairs={{0,8},{8,16},{16,24},{24,0},{1,9},{9,17},{17,25},{25,1},{2,10},{10... | collective-permute-start | bytes 393224 | tf_op jit(solution)/shard_map/ppermute | solution.py:77
  72.8 13.7 %collective-permute-start.9 = (bf16[16,4096]{1,0:T(8,128)(2,1)S(1)}, bf16[16,4096]{1,0:T(8,128)(2,1)S(1)}, u32[]{:S(2)}, u32[]{:S(2)}) collective-permute-start(bf16[16,4096]{1,0:T(8,128)(2,1)S(1)} %convolution_convert_fusion), channel_id=1, source_target_pairs={{0,24},{8,0},{16,8},{24,16},{1,25},{9,1},{17,9},{25,17},{2,26},{10... | collective-permute-start | bytes 393224 | tf_op jit(solution)/shard_map/ppermute | solution.py:77
  75.5 11.1 %collective-permute-start.8 = (bf16[16,4096]{1,0:T(8,128)(2,1)S(1)}, bf16[16,4096]{1,0:T(8,128)(2,1)S(1)}, u32[]{:S(2)}, u32[]{:S(2)}) collective-permute-start(bf16[16,4096]{1,0:T(8,128)(2,1)S(1)} %convolution_convert_fusion), channel_id=1, source_target_pairs={{0,16},{8,24},{16,0},{24,8},{1,17},{9,25},{17,1},{25,9},{2,18},{10... | collective-permute-start | bytes 393224 | tf_op jit(solution)/shard_map/ppermute | solution.py:77
  86.6 22.0 %slice-start = ((s8[8388608]{0:T(1024)(128)(4,1)}), s8[4194304]{0:T(1024)(128)(4,1)S(1)}, s32[]{:S(2)}) async-start(s8[8388608]{0:T(1024)(128)(4,1)} %bitcast.20), calls=%async_computation | async-start | bytes 8388608
  86.6 21.9 %slice-start.1 = ((s8[8388608]{0:T(1024)(128)(4,1)}), s8[4194304]{0:T(1024)(128)(4,1)S(1)}, s32[]{:S(2)}) async-start(s8[8388608]{0:T(1024)(128)(4,1)} %bitcast.20), calls=%async_computation.1 | async-start | bytes 8388608
  86.6 12.9 %collective-permute-start.11 = (bf16[48,4096]{1,0:T(8,128)(2,1)S(1)}, bf16[48,4096]{1,0:T(8,128)(2,1)S(1)}, u32[]{:S(2)}, u32[]{:S(2)}) collective-permute-start(bf16[48,4096]{1,0:T(8,128)(2,1)S(1)} %get-tuple-element.6), channel_id=1, source_target_pairs={{0,4},{1,3},{2,6},{3,1},{4,0},{5,7},{6,2},{7,5},{8,12},{9,11},{10,... | collective-permute-start | bytes 1179656 | tf_op jit(solution)/shard_map/ppermute | solution.py:24
  88.2 9.6 %collective-permute-start.10 = (bf16[48,4096]{1,0:T(8,128)(2,1)S(1)}, bf16[48,4096]{1,0:T(8,128)(2,1)S(1)}, u32[]{:S(2)}, u32[]{:S(2)}) collective-permute-start(bf16[48,4096]{1,0:T(8,128)(2,1)S(1)} %get-tuple-element.6), channel_id=1, source_target_pairs={{0,2},{1,5},{2,0},{3,7},{4,6},{5,1},{6,4},{7,3},{8,10},{9,13},{10,... | collective-permute-start | bytes 1179656 | tf_op jit(solution)/shard_map/ppermute | solution.py:24
  97.8 8.3 %collective-permute-start.13 = (bf16[48,4096]{1,0:T(8,128)(2,1)S(1)}, bf16[48,4096]{1,0:T(8,128)(2,1)S(1)}, u32[]{:S(2)}, u32[]{:S(2)}) collective-permute-start(bf16[48,4096]{1,0:T(8,128)(2,1)S(1)} %get-tuple-element.6), channel_id=1, source_target_pairs={{0,1},{1,0},{2,3},{3,2},{4,5},{5,4},{6,7},{7,6},{8,9},{9,8},{10,11... | collective-permute-start | bytes 1179656 | tf_op jit(solution)/shard_map/ppermute | solution.py:28
  97.8 8.4 %collective-permute-start.14 = (bf16[48,4096]{1,0:T(8,128)(2,1)S(1)}, bf16[48,4096]{1,0:T(8,128)(2,1)S(1)}, u32[]{:S(2)}, u32[]{:S(2)}) collective-permute-start(bf16[48,4096]{1,0:T(8,128)(2,1)S(1)} %collective-permute-done.10), channel_id=1, source_target_pairs={{0,1},{1,0},{2,3},{3,2},{4,5},{5,4},{6,7},{7,6},{8,9},{9,8},{10,11... | collective-permute-start | bytes 1179656 | tf_op jit(solution)/shard_map/ppermute | solution.py:28
  98.3 7.8 %collective-permute-start.12 = (bf16[48,4096]{1,0:T(8,128)(2,1)S(1)}, bf16[48,4096]{1,0:T(8,128)(2,1)S(1)}, u32[]{:S(2)}, u32[]{:S(2)}) collective-permute-start(bf16[48,4096]{1,0:T(8,128)(2,1)S(1)} %collective-permute-done.10), channel_id=1, source_target_pairs={{0,4},{1,3},{2,6},{3,1},{4,0},{5,7},{6,2},{7,5},{8,12},{9,11},{10,... | collective-permute-start | bytes 1179656 | tf_op jit(solution)/shard_map/ppermute | solution.py:24
  99.5 6.7 %collective-permute-start.15 = (bf16[48,4096]{1,0:T(8,128)(2,1)S(1)}, bf16[48,4096]{1,0:T(8,128)(2,1)S(1)}, u32[]{:S(2)}, u32[]{:S(2)}) collective-permute-start(bf16[48,4096]{1,0:T(8,128)(2,1)S(1)} %collective-permute-done.11), channel_id=1, source_target_pairs={{0,1},{1,0},{2,3},{3,2},{4,5},{5,4},{6,7},{7,6},{8,9},{9,8},{10,11... | collective-permute-start | bytes 1179656 | tf_op jit(solution)/shard_map/ppermute | solution.py:28
  106.1 1.7 %collective-permute-start.16 = (bf16[48,4096]{1,0:T(8,128)(2,1)S(1)}, bf16[48,4096]{1,0:T(8,128)(2,1)S(1)}, u32[]{:S(2)}, u32[]{:S(2)}) collective-permute-start(bf16[48,4096]{1,0:T(8,128)(2,1)S(1)} %collective-permute-done.12), channel_id=1, source_target_pairs={{0,1},{1,0},{2,3},{3,2},{4,5},{5,4},{6,7},{7,6},{8,9},{9,8},{10,11... | collective-permute-start | bytes 1179656 | tf_op jit(solution)/shard_map/ppermute | solution.py:28

commit v2 on v0

v2 whole, which is shorter than its diff:
```python
import functools

import jax
import jax.numpy as jnp
from jax import lax
from jax.experimental import pallas as pl
from jax.experimental.pallas import tpu as pltpu
from jax.sharding import PartitionSpec as P


def sq_norms(matrix):
    return jnp.sum(jnp.square(matrix.astype(jnp.float32)), axis=1)


def chip_bits(size):
    return [1 << b for b in range(1, size.bit_length() - 1)]


def xor_permute(block, size, flip):
    return lax.ppermute(block, "mem", [(m, m ^ flip) for m in range(size)])


def mixed_permute(block, size, stage):
    bits = chip_bits(size)
    even, odd = bits[stage], bits[len(bits) - 1 - stage]
    return lax.ppermute(block, "mem", [(m, m ^ (odd if m & 1 else even)) for m in range(size)])


def gather_chips(block, size):
    held = [block]
    for stage in range(len(chip_bits(size))):
        held = held + [mixed_permute(b, size, stage) for b in held]
    return held


def sibling_place(index, stages):
    place = 0
    for s in range(stages):
        if index >> s & 1:
            place |= 1 << (stages - 1 - s)
    return place


def join_cores(held, size):
    stages = len(chip_bits(size))
    other = [None] * len(held)
    for i, block in enumerate(held):
        other[sibling_place(i, stages)] = xor_permute(block, size, 1)
    return jnp.concatenate(
        [jnp.concatenate(held, axis=0), jnp.concatenate(other, axis=0)], axis=1
    )


def dense_kernel(size, picks_chip, rest_chip, counts_ref, chosen_ref, own_ref, sib_ref, *rest):
    outs, raw, sems = rest[:-2], rest[-2], rest[-1]
    me = lax.axis_index("mem")
    chip, core = me // 2, me % 2
    slots, half = own_ref.shape[0], raw.shape[1]
    columns = pl.ds(pl.multiple_of(core * half, half), half)
    copies = [
        pltpu.make_async_copy(ref.at[:, columns], raw.at[pl.ds(i * slots, slots), :], sems.at[i])
        for i, ref in enumerate((own_ref, sib_ref))
    ]
    for copy in copies:
        copy.start()

    offset_own, offset_sib = jnp.int32(0), jnp.int32(0)
    for d in range(size):
        origin, count = lax.bitwise_xor(me, d), counts_ref[0, d]
        offset_own += jnp.where(origin < me, count, 0)
        offset_sib += jnp.where(origin < lax.bitwise_xor(me, 1), count, 0)
    lane = lax.broadcasted_iota(jnp.int32, (1, 2 * slots), 1)
    first = lane < slots
    within = jnp.where(first, lane, lane - slots)
    live = within < jnp.where(first, counts_ref[0, 0], counts_ref[0, 1])
    position = jnp.where(live, within + jnp.where(first, offset_own, offset_sib), -1)
    chosen = chosen_ref[...]
    below = jnp.sum((chosen < position).astype(jnp.int32), axis=0, keepdims=True)
    taken = jnp.sum((chosen == position).astype(jnp.int32), axis=0, keepdims=True)
    rank = jnp.where(live & (taken == 0), position - below, -1)

    for copy in copies:
        copy.wait()
    rows = raw[...]
    place = lax.broadcasted_iota(jnp.int32, (rest_chip, 1), 0)
    for d, out in enumerate(outs):
        target = lax.bitwise_xor(chip, d)
        ids = chosen_ref[pl.ds(pl.multiple_of(target * picks_chip, picks_chip), picks_chip), :]
        for select, at in (
            (ids == position, pl.ds(0, picks_chip)),
            (place + target * rest_chip == rank, pl.ds(picks_chip, rest_chip)),
        ):
            one_hot = select.astype(jnp.float32).astype(jnp.bfloat16)
            out[at, :] = jnp.dot(one_hot, rows, preferred_element_type=jnp.float32).astype(
                jnp.bfloat16
            )


def dense_parts(size, picks_chip, rest_chip, counts, chosen, own, sib):
    slots, width = own.shape
    chips, half = size // 2, width // 2
    rows = picks_chip + rest_chip
    return pl.pallas_call(
        functools.partial(dense_kernel, size, picks_chip, rest_chip),
        out_shape=[jax.ShapeDtypeStruct((rows, half), jnp.bfloat16)] * chips,
        in_specs=[
            pl.BlockSpec(memory_space=pltpu.SMEM),
            pl.BlockSpec(memory_space=pltpu.VMEM),
            pl.BlockSpec(memory_space=pl.ANY),
            pl.BlockSpec(memory_space=pl.ANY),
        ],
        out_specs=[pl.BlockSpec(memory_space=pltpu.VMEM)] * chips,
        scratch_shapes=[
            pltpu.VMEM((2 * slots, half), jnp.bfloat16),
            pltpu.SemaphoreType.DMA((2,)),
        ],
        cost_estimate=pl.CostEstimate(
            flops=2 * chips * rows * 2 * slots * half,
            bytes_accessed=2 * (2 * slots + chips * rows) * half,
            transcendentals=0,
        ),
        name="dense_parts",
    )(counts, chosen, own, sib)


def body(candidates, round_one, counts, chosen):
    mem_size = lax.axis_size("mem")
    grp_size = lax.axis_size("grp")
    me = lax.axis_index("mem")
    slot_max, width = round_one.shape
    half, chips = width // 2, mem_size // 2
    picks_total = chosen.shape[1]
    live_total = mem_size * slot_max * 3 // 8
    picks_chip = picks_total // chips
    rest_chip = (live_total - picks_total) // chips
    rows_chip = picks_chip + rest_chip

    group_counts = jnp.concatenate(
        [counts] + [xor_permute(counts, mem_size, d) for d in range(1, mem_size)], axis=1
    )
    sib_rows = xor_permute(round_one, mem_size, 1)
    parts = dense_parts(
        mem_size, picks_chip, rest_chip, group_counts, chosen.reshape(-1, 1), round_one, sib_rows
    )
    own = parts[0]
    for d in range(1, chips):
        own = own + xor_permute(parts[d], mem_size, 2 * d)

    start = (me % 2) * half
    cand = jnp.concatenate(
        [
            lax.dynamic_slice_in_dim(candidates, start, half, 1),
            lax.dynamic_slice_in_dim(candidates, half - start, half, 1),
        ],
        axis=1,
    )
    cand_norm = sq_norms(candidates)

    picks = own[:picks_chip]
    far = [
        lax.ppermute(picks, "grp", [(g, (g + k) % grp_size) for g in range(grp_size)])
        for k in range(1, grp_size)
    ]

    def gaps_to(rows):
        inner = lax.dot_general(
            cand, rows, (((1,), (1,)), ((), ())), preferred_element_type=jnp.float32
        )
        return cand_norm[:, None] + sq_norms(rows)[None, :] - 2.0 * inner

    own_gaps = gaps_to(join_cores(gather_chips(own, mem_size), mem_size))
    nearest = jnp.min(own_gaps, axis=1)
    is_pick = jnp.arange(chips * rows_chip) % rows_chip < picks_chip
    final = jnp.min(jnp.where(is_pick[None, :], own_gaps, jnp.inf), axis=1)
    far_rows = [join_cores(gather_chips(block, mem_size), mem_size) for block in far]
    for rows in (jnp.concatenate(far_rows[:-1], axis=0), far_rows[-1]):
        final = jnp.minimum(final, jnp.min(gaps_to(rows), axis=1))
    return nearest, final


def solution(mesh):
    in_specs = (P(("grp", "mem"), None), P(("grp", "mem"), None), P("grp", "mem"), P("grp", None))
    out_specs = (P(("grp", "mem")), P(("grp", "mem")))
    return jax.shard_map(body, mesh=mesh, in_specs=in_specs, out_specs=out_specs, check_vma=False)
```

time: 134 us -> 103 us (0.77)
  waiting for transfers between devices: 79.6 us -> 23.4 us
  starting transfers between devices: 0.08 us -> 30.4 us
  other arithmetic: 9.64 us -> 23.7 us
  between operations: 14.7 us -> 1.51 us
  blocking collectives: 9.48 us -> 0 us
  local copies, waits for them, and re-layouts: 3.72 us -> 11.6 us
  matrix products: 16.7 us -> 9.19 us
  Pallas kernels: 0 us -> 3.31 us
    all_gather x2 -> x0, waiting for transfers between devices: 78.9 us -> none  [the longest x1 49.9 us: body(): lax.all_gather(my_share, ('grp', 'mem'), axis=0, tiled=True)]
    ppermute x0 -> x42, starting transfers between devices: none -> 30.4 us  [the longest x27 15.5 us: xor_permute(): return lax.ppermute(block, 'mem', [(m, m ^ flip) for m in range(size)])]
    ppermute x0 -> x42, waiting for transfers between devices: none -> 23.4 us  [the longest x27 12.4 us: xor_permute(): return lax.ppermute(block, 'mem', [(m, m ^ flip) for m in range(size)])]
    reduce_sum x3 -> x4, other arithmetic: 9.35 us -> 22.1 us  [sq_norms(): return jnp.sum(jnp.square(matrix.astype(jnp.float32)), axis=1)]
    unnamed x1 -> x0, blocking collectives: 9.48 us -> none
    dot_general x3, matrix products: 16.7 us -> 9.19 us  [gaps_to(): lax.dot_general(cand, rows, (((1,), (1,)), ((), ())), preferred_element_t...]
    concatenate x0 -> x1, local copies, waits for them, and re-layouts: none -> 5.1 us  [body(): jnp.concatenate([counts] + [xor_permute(counts, mem_size, d) for d in ran...]
    dynamic_slice x0 -> x1, local copies, waits for them, and re-layouts: none -> 4.31 us  [body(): lax.dynamic_slice_in_dim(candidates, start, half, 1)]
  transfers between devices with their start and end apart: 2 -> 42, of which waited for: 2 -> 11; matrix products, arithmetic and copies ran while one was open for 10% -> 31% of each run, Pallas kernels for 0% -> 0%
where the time goes in v2:
time: 103 us
  starting transfers between devices  30.4 us (30%)
  other arithmetic  23.7 us (23%)
  waiting for transfers between devices  23.4 us (23%)
  local copies, waits for them, and re-layouts  11.6 us (11%)
  matrix products  9.19 us (9%)
  Pallas kernels  3.31 us (3%)
  between operations  1.51 us (1%)
    reduce_sum x4, other arithmetic, sq_norms(): return jnp.sum(jnp.square(matrix.astype(jnp.float32)), axis=1)  22.1 us
    ppermute x27, starting transfers between devices, xor_permute(): return lax.ppermute(block, 'mem', [(m, m ^ flip) for m in range(size)])  15.5 us
    ppermute x27, waiting for transfers between devices, xor_permute(): return lax.ppermute(block, 'mem', [(m, m ^ flip) for m in range(size)])  12.4 us
    ppermute x12, starting transfers between devices, mixed_permute(): lax.ppermute(block, 'mem', [(m, m ^ (odd if m & 1 else even)) for m in ra...  10.2 us
    dot_general x3, matrix products, gaps_to(): lax.dot_general(cand, rows, (((1,), (1,)), ((), ())), preferred_element_t...  9.19 us
    ppermute x3, waiting for transfers between devices, body(): lax.ppermute(picks, 'grp', [(g, (g + k) % grp_size) for g in range(grp_si...  8.59 us
    concatenate x1, local copies, waits for them, and re-layouts, body(): jnp.concatenate([counts] + [xor_permute(counts, mem_size, d) for d in ran...  5.1 us
    ppermute x3, starting transfers between devices, body(): lax.ppermute(picks, 'grp', [(g, (g + k) % grp_size) for g in range(grp_si...  4.67 us
  transfers between devices with their start and end apart: 42, of which 11 were waited for; matrix products, arithmetic and copies ran while one was open for 31% of the time, Pallas kernels for 0%

profile of v2, /device:TPU:0, one launch (start us, length us, event | category | flops | bytes accessed | tf_op | source)
XLA Modules:
  0.0 103.1 jit_solution(10629476162289200840)
XLA Ops:
  1.2 2.9 %collective-permute-start.1 = (s32[1,1]{1,0:T(1,128)}, s32[1,1]{1,0:T(1,128)}, u32[]{:S(2)}, u32[]{:S(2)}) collective-permute-start(s32[1,1]{1,0:T(1,128)} %param.6), channel_id=1, source_target_pairs={{0,2},{1,3},{2,0},{3,1},{4,6},{5,7},{6,4},{7,5},{8,10},{9,11},{10,... | collective-permute-start | bytes 20 | tf_op jit(solution)/shard_map/ppermute | solution.py:20
  4.1 1.5 %collective-permute-start.3 = (s32[1,1]{1,0:T(1,128)}, s32[1,1]{1,0:T(1,128)}, u32[]{:S(2)}, u32[]{:S(2)}) collective-permute-start(s32[1,1]{1,0:T(1,128)} %param.6), channel_id=1, source_target_pairs={{0,4},{1,5},{2,6},{3,7},{4,0},{5,1},{6,2},{7,3},{8,12},{9,13},{10,... | collective-permute-start | bytes 20 | tf_op jit(solution)/shard_map/ppermute | solution.py:20
  8.0 2.7 %collective-permute-start.5 = (s32[1,1]{1,0:T(1,128)}, s32[1,1]{1,0:T(1,128)}, u32[]{:S(2)}, u32[]{:S(2)}) collective-permute-start(s32[1,1]{1,0:T(1,128)} %param.6), channel_id=1, source_target_pairs={{0,6},{1,7},{2,4},{3,5},{4,2},{5,3},{6,0},{7,1},{8,14},{9,15},{10,... | collective-permute-start | bytes 20 | tf_op jit(solution)/shard_map/ppermute | solution.py:20
  10.8 1.8 %collective-permute-done.5 = s32[1,1]{1,0:T(1,128)} collective-permute-done((s32[1,1]{1,0:T(1,128)}, s32[1,1]{1,0:T(1,128)}, u32[]{:S(2)}, u32[]{:S(2)}) %collective-permute-start.5) | collective-permute-done | bytes 36 | tf_op jit(solution)/shard_map/ppermute | solution.py:20
  12.6 2.2 %collective-permute-done.6 = s32[1,1]{1,0:T(1,128)} collective-permute-done((s32[1,1]{1,0:T(1,128)}, s32[1,1]{1,0:T(1,128)}, u32[]{:S(2)}, u32[]{:S(2)}) %collective-permute-start.6) | collective-permute-done | bytes 36 | tf_op jit(solution)/shard_map/ppermute | solution.py:20
  14.8 5.1 %concatenate.45.counts_ref = s32[1,8]{1,0:T(1,128)} concatenate(s32[1,1]{1,0:T(1,128)S(6)} %copy.7, s32[1,1]{1,0:T(1,128)} %collective-permute-done, s32[1,1]{1,0:T(1,128)} %collective-permute-done.1, s32[1,1]{1,0:T(1,128)} %collective-permute-done.2, s32[1,1]{1,0:T(1,128)} %collective-permute-done.3, s32[1,1]{1,0:T(1,128)} %collective-permute-done.4, ...), dimensions={1} | concatenate | bytes 64 | tf_op jit(solution)/shard_map/concatenate | solution.py:138
  20.7 3.3 %dense_parts.1 = (bf16[48,2048]{1,0:T(8,128)(2,1)}, bf16[48,2048]{1,0:T(8,128)(2,1)}, bf16[48,2048]{1,0:T(8,128)(2,1)}, bf16[48,2048]{1,0:T(8,128)(2,1)}) custom-call(s32[1,8]{1,0:T(1,128)} %concatenate.45.counts_ref, s32[128,1]{1,0:T(8,128)} %copy.6.chosen_ref, bf16[64,4096]{1,0:T(8,128)(2,1)} %own_ref.1, bf16[64,4096]{1,0:T(8,128)(2,1)} %copy-done), custom_call_target="tpu_custom_call" | custom-call | flops 100663296 | bytes 1310720 | tf_op jit(solution)/shard_map/dense_parts/pallas_call | solution.py:103
  24.5 1.5 %collective-permute-start.8 = (bf16[48,2048]{1,0:T(8,128)(2,1)}, bf16[48,2048]{1,0:T(8,128)(2,1)S(1)}, u32[]{:S(2)}, u32[]{:S(2)}) collective-permute-start(bf16[48,2048]{1,0:T(8,128)(2,1)} %get-tuple-element.7), channel_id=1, source_target_pairs={{0,2},{1,3},{2,0},{3,1},{4,6},{5,7},{6,4},{7,5},{8,10},{9,11},{10,... | collective-permute-start | bytes 589832 | tf_op jit(solution)/shard_map/ppermute | solution.py:20
  26.0 1.5 %collective-permute-start.9 = (bf16[48,2048]{1,0:T(8,128)(2,1)}, bf16[48,2048]{1,0:T(8,128)(2,1)S(1)}, u32[]{:S(2)}, u32[]{:S(2)}) collective-permute-start(bf16[48,2048]{1,0:T(8,128)(2,1)} %get-tuple-element.8), channel_id=1, source_target_pairs={{0,4},{1,5},{2,6},{3,7},{4,0},{5,1},{6,2},{7,3},{8,12},{9,13},{10,... | collective-permute-start | bytes 589832 | tf_op jit(solution)/shard_map/ppermute | solution.py:20
  27.6 5.5 %collective-permute-done.10 = bf16[48,2048]{1,0:T(8,128)(2,1)S(1)} collective-permute-done((bf16[48,2048]{1,0:T(8,128)(2,1)}, bf16[48,2048]{1,0:T(8,128)(2,1)S(1)}, u32[]{:S(2)}, u32[]{:S(2)}) %collective-permute-start.10) | collective-permute-done | bytes 196640 | tf_op jit(solution)/shard_map/ppermute | solution.py:20
  33.0 1.8 %collective-permute-done.8 = bf16[48,2048]{1,0:T(8,128)(2,1)S(1)} collective-permute-done((bf16[48,2048]{1,0:T(8,128)(2,1)}, bf16[48,2048]{1,0:T(8,128)(2,1)S(1)}, u32[]{:S(2)}, u32[]{:S(2)}) %collective-permute-start.8) | collective-permute-done | bytes 196640 | tf_op jit(solution)/shard_map/ppermute | solution.py:20
  36.8 1.6 %collective-permute-start.18 = (bf16[32,2048]{1,0:T(8,128)(2,1)S(1)}, bf16[32,2048]{1,0:T(8,128)(2,1)S(1)}, u32[]{:S(2)}, u32[]{:S(2)}) collective-permute-start(bf16[32,2048]{1,0:T(8,128)(2,1)S(1)} %slice.4), channel_id=1, source_target_pairs={{0,8},{8,16},{16,24},{24,0},{1,9},{9,17},{17,25},{25,1},{2,10},{10... | collective-permute-start | bytes 393224 | tf_op jit(solution)/shard_map/ppermute | solution.py:161
  38.5 2.2 %collective-permute-start.34 = (bf16[32,2048]{1,0:T(8,128)(2,1)S(1)}, bf16[32,2048]{1,0:T(8,128)(2,1)S(1)}, u32[]{:S(2)}, u32[]{:S(2)}) collective-permute-start(bf16[32,2048]{1,0:T(8,128)(2,1)S(1)} %slice.4), channel_id=1, source_target_pairs={{0,24},{8,0},{16,8},{24,16},{1,25},{9,1},{17,9},{25,17},{2,26},{10... | collective-permute-start | bytes 393224 | tf_op jit(solution)/shard_map/ppermute | solution.py:161
  42.7 2.3 %collective-permute-done.18 = bf16[32,2048]{1,0:T(8,128)(2,1)S(1)} collective-permute-done((bf16[32,2048]{1,0:T(8,128)(2,1)S(1)}, bf16[32,2048]{1,0:T(8,128)(2,1)S(1)}, u32[]{:S(2)}, u32[]{:S(2)}) %collective-permute-start.18) | collective-permute-done | bytes 131104 | tf_op jit(solution)/shard_map/ppermute | solution.py:161
  47.1 5.5 %collective-permute-done.26 = bf16[32,2048]{1,0:T(8,128)(2,1)S(1)} collective-permute-done((bf16[32,2048]{1,0:T(8,128)(2,1)S(1)}, bf16[32,2048]{1,0:T(8,128)(2,1)S(1)}, u32[]{:S(2)}, u32[]{:S(2)}) %collective-permute-start.26) | collective-permute-done | bytes 131104 | tf_op jit(solution)/shard_map/ppermute | solution.py:161
  55.8 1.5 %collective-permute-start.37 = (bf16[32,2048]{1,0:T(8,128)(2,1)S(1)}, bf16[32,2048]{1,0:T(8,128)(2,1)S(1)}, u32[]{:S(2)}, u32[]{:S(2)}) collective-permute-start(bf16[32,2048]{1,0:T(8,128)(2,1)S(1)} %collective-permute-done.35), channel_id=1, source_target_pairs={{0,4},{1,3},{2,6},{3,1},{4,0},{5,7},{6,2},{7,5},{8,12},{9,11},{10,... | collective-permute-start | bytes 393224 | tf_op jit(solution)/shard_map/ppermute | solution.py:26
  57.3 5.1 %multiply_reduce_fusion = f32[1024]{0:T(1024)S(1)} fusion(bf16[1024,4096]{1,0:T(8,128)(2,1)} %param.4), kind=kLoop, calls=%fused_computation | loop fusion | flops 12581888 | bytes 8392704 | tf_op jit(solution)/shard_map/reduce_sum | solution.py:12
  63.6 4.3 %constant_dynamic-slice_fusion.1 = (bf16[1024,2048]{1,0:T(8,128)(2,1)S(1)}, bf16[1024,2048]{1,0:T(8,128)(2,1)S(1)}) fusion(bf16[1024,4096]{1,0:T(8,128)(2,1)} %param.4, s32[]{:T(128)S(6)} %select_n.28, s32[]{:T(128)S(6)} %select_n.29), kind=kLoop, calls=%fused_computation.25 | loop fusion | bytes 16777224 | tf_op jit(solution)/shard_map/dynamic_slice | solution.py:152
  70.8 1.6 %collective-permute-start.13 = (bf16[48,2048]{1,0:T(8,128)(2,1)S(1)}, bf16[48,2048]{1,0:T(8,128)(2,1)S(1)}, u32[]{:S(2)}, u32[]{:S(2)}) collective-permute-start(bf16[48,2048]{1,0:T(8,128)(2,1)S(1)} %collective-permute-done.11), channel_id=1, source_target_pairs={{0,4},{1,3},{2,6},{3,1},{4,0},{5,7},{6,2},{7,5},{8,12},{9,11},{10,... | collective-permute-start | bytes 589832 | tf_op jit(solution)/shard_map/ppermute | solution.py:26
  75.4 2.9 %fusion.7 = f32[1024]{0:T(1024)S(1)} fusion(bf16[1024,2048]{1,0:T(8,128)(2,1)S(1)} %get-tuple-element.15, bf16[1024,2048]{1,0:T(8,128)(2,1)S(1)} %get-tuple-element.14, f32[128]{0:T(128)S(1)} %multiply_reduce_fusion.3, f32[1024]{0:T(1024)S(1)} %multiply_reduce_fusion, bf16[32,2048]{1,0:T(8,128)(2,1)S(1)} %collective-permute-done.41, ...), kind=kOutput, calls=%fused_computation.14 | convolution fusion | flops 1099430912 | bytes 9445888 | tf_op jit(solution)/shard_map/dot_general | solution.py:166
  79.4 9.7 %multiply_reduce_fusion.1 = (f32[256]{0:T(256)S(1)}, bf16[256,4096]{1,0:T(8,128)(2,1)S(1)}) fusion(bf16[32,2048]{1,0:T(8,128)(2,1)S(1)} %collective-permute-done.33, bf16[32,2048]{1,0:T(8,128)(2,1)S(1)} %collective-permute-done.32, bf16[32,2048]{1,0:T(8,128)(2,1)S(1)} %collective-permute-done.31, bf16[32,2048]{1,0:T(8,128)(2,1)S(1)} %collective-permute-done.30, ...), kind=kLoop, calls=%fused_computation.2 | loop fusion | flops 36699904 | bytes 4195328 | tf_op jit(solution)/shard_map/reduce_sum | solution.py:12
  89.1 2.7 %subtract_reduce_fusion = f32[1024]{0:T(1024)S(1)} fusion(bf16[256,4096]{1,0:T(8,128)(2,1)S(1)} %get-tuple-element.13, bf16[1024,2048]{1,0:T(8,128)(2,1)S(1)} %get-tuple-element.15, bf16[1024,2048]{1,0:T(8,128)(2,1)S(1)} %get-tuple-element.14, f32[256]{0:T(256)S(1)} %get-tuple-element.12, f32[1024]{0:T(1024)S(1)} %multiply_reduce_fusion), kind=kOutput, calls=%fused_computation.16 | convolution fusion | flops 2165308416 | bytes 10494976 | tf_op jit(solution)/shard_map/dot_general | solution.py:166
  91.9 7.0 %multiply_reduce_fusion.2 = f32[192]{0:T(256)S(1)} fusion(bf16[48,2048]{1,0:T(8,128)(2,1)S(1)} %collective-permute-done.17, bf16[48,2048]{1,0:T(8,128)(2,1)S(1)} %collective-permute-done.16, bf16[48,2048]{1,0:T(8,128)(2,1)S(1)} %collective-permute-done.15, bf16[48,2048]{1,0:T(8,128)(2,1)S(1)} %collective-permute-done.14, ...), kind=kLoop, calls=%fused_computation.3 | loop fusion | flops 14155584 | bytes 1573632 | tf_op jit(solution)/shard_map/reduce_sum | solution.py:12
  98.9 3.6 %select_reduce_fusion = (f32[1024]{0:T(1024)S(1)}, f32[1024]{0:T(1024)}) fusion(f32[192]{0:T(256)S(1)} %multiply_reduce_fusion.2, f32[1024]{0:T(1024)S(1)} %multiply_reduce_fusion, pred[192]{0:T(512)(128)(4,1)S(1)} %fusion.9, bf16[48,2048]{1,0:T(8,128)(2,1)S(1)} %collective-permute-done.17, bf16[48,2048]{1,0:T(8,128)(2,1)S(1)} %collective-permute-done.16, ...), kind=kOutput, calls=%fused_computation.17 | convolution fusion | flops 1641150464 | bytes 9974720 | tf_op jit(solution)/shard_map/dot_general | solution.py:166
  (77 shorter events, 21.6 us)
Async XLA Ops:
  0.6 19.3 %collective-permute-start.7 = (bf16[64,4096]{1,0:T(8,128)(2,1)}, bf16[64,4096]{1,0:T(8,128)(2,1)S(1)}, u32[]{:S(2)}, u32[]{:S(2)}) collective-permute-start(bf16[64,4096]{1,0:T(8,128)(2,1)} %own_ref.1), channel_id=1, source_target_pairs={{0,1},{1,0},{2,3},{3,2},{4,5},{5,4},{6,7},{7,6},{8,9},{9,8},{10,11... | collective-permute-start | bytes 1572872 | tf_op jit(solution)/shard_map/ppermute | solution.py:20
  1.1 6.6 %collective-permute-start = (s32[1,1]{1,0:T(1,128)}, s32[1,1]{1,0:T(1,128)}, u32[]{:S(2)}, u32[]{:S(2)}) collective-permute-start(s32[1,1]{1,0:T(1,128)} %param.6), channel_id=1, source_target_pairs={{0,1},{1,0},{2,3},{3,2},{4,5},{5,4},{6,7},{7,6},{8,9},{9,8},{10,11... | collective-permute-start | bytes 20 | tf_op jit(solution)/shard_map/ppermute | solution.py:20
  1.2 6.8 %collective-permute-start.1 = (s32[1,1]{1,0:T(1,128)}, s32[1,1]{1,0:T(1,128)}, u32[]{:S(2)}, u32[]{:S(2)}) collective-permute-start(s32[1,1]{1,0:T(1,128)} %param.6), channel_id=1, source_target_pairs={{0,2},{1,3},{2,0},{3,1},{4,6},{5,7},{6,4},{7,5},{8,10},{9,11},{10,... | collective-permute-start | bytes 20 | tf_op jit(solution)/shard_map/ppermute | solution.py:20
  24.0 9.0 %collective-permute-start.10 = (bf16[48,2048]{1,0:T(8,128)(2,1)}, bf16[48,2048]{1,0:T(8,128)(2,1)S(1)}, u32[]{:S(2)}, u32[]{:S(2)}) collective-permute-start(bf16[48,2048]{1,0:T(8,128)(2,1)} %get-tuple-element.9), channel_id=1, source_target_pairs={{0,6},{1,7},{2,4},{3,5},{4,2},{5,3},{6,0},{7,1},{8,14},{9,15},{10,... | collective-permute-start | bytes 589832 | tf_op jit(solution)/shard_map/ppermute | solution.py:20
  24.5 10.4 %collective-permute-start.8 = (bf16[48,2048]{1,0:T(8,128)(2,1)}, bf16[48,2048]{1,0:T(8,128)(2,1)S(1)}, u32[]{:S(2)}, u32[]{:S(2)}) collective-permute-start(bf16[48,2048]{1,0:T(8,128)(2,1)} %get-tuple-element.7), channel_id=1, source_target_pairs={{0,2},{1,3},{2,0},{3,1},{4,6},{5,7},{6,4},{7,5},{8,10},{9,11},{10,... | collective-permute-start | bytes 589832 | tf_op jit(solution)/shard_map/ppermute | solution.py:20
  26.0 9.8 %collective-permute-start.9 = (bf16[48,2048]{1,0:T(8,128)(2,1)}, bf16[48,2048]{1,0:T(8,128)(2,1)S(1)}, u32[]{:S(2)}, u32[]{:S(2)}) collective-permute-start(bf16[48,2048]{1,0:T(8,128)(2,1)} %get-tuple-element.8), channel_id=1, source_target_pairs={{0,4},{1,5},{2,6},{3,7},{4,0},{5,1},{6,2},{7,3},{8,12},{9,13},{10,... | collective-permute-start | bytes 589832 | tf_op jit(solution)/shard_map/ppermute | solution.py:20
  36.8 8.2 %collective-permute-start.18 = (bf16[32,2048]{1,0:T(8,128)(2,1)S(1)}, bf16[32,2048]{1,0:T(8,128)(2,1)S(1)}, u32[]{:S(2)}, u32[]{:S(2)}) collective-permute-start(bf16[32,2048]{1,0:T(8,128)(2,1)S(1)} %slice.4), channel_id=1, source_target_pairs={{0,8},{8,16},{16,24},{24,0},{1,9},{9,17},{17,25},{25,1},{2,10},{10... | collective-permute-start | bytes 393224 | tf_op jit(solution)/shard_map/ppermute | solution.py:161
  38.5 7.9 %collective-permute-start.34 = (bf16[32,2048]{1,0:T(8,128)(2,1)S(1)}, bf16[32,2048]{1,0:T(8,128)(2,1)S(1)}, u32[]{:S(2)}, u32[]{:S(2)}) collective-permute-start(bf16[32,2048]{1,0:T(8,128)(2,1)S(1)} %slice.4), channel_id=1, source_target_pairs={{0,24},{8,0},{16,8},{24,16},{1,25},{9,1},{17,9},{25,17},{2,26},{10... | collective-permute-start | bytes 393224 | tf_op jit(solution)/shard_map/ppermute | solution.py:161
  40.7 12.2 %collective-permute-start.11 = (bf16[48,2048]{1,0:T(8,128)(2,1)S(1)}, bf16[48,2048]{1,0:T(8,128)(2,1)S(1)}, u32[]{:S(2)}, u32[]{:S(2)}) collective-permute-start(bf16[48,2048]{1,0:T(8,128)(2,1)S(1)} %add_add_fusion), channel_id=1, source_target_pairs={{0,2},{1,5},{2,0},{3,7},{4,6},{5,1},{6,4},{7,3},{8,10},{9,13},{10,... | collective-permute-start | bytes 589832 | tf_op jit(solution)/shard_map/ppermute | solution.py:26
  41.3 12.5 %collective-permute-start.12 = (bf16[48,2048]{1,0:T(8,128)(2,1)S(1)}, bf16[48,2048]{1,0:T(8,128)(2,1)S(1)}, u32[]{:S(2)}, u32[]{:S(2)}) collective-permute-start(bf16[48,2048]{1,0:T(8,128)(2,1)S(1)} %add_add_fusion), channel_id=1, source_target_pairs={{0,4},{1,3},{2,6},{3,1},{4,0},{5,7},{6,2},{7,5},{8,12},{9,11},{10,... | collective-permute-start | bytes 589832 | tf_op jit(solution)/shard_map/ppermute | solution.py:26
  41.9 10.7 %collective-permute-start.26 = (bf16[32,2048]{1,0:T(8,128)(2,1)S(1)}, bf16[32,2048]{1,0:T(8,128)(2,1)S(1)}, u32[]{:S(2)}, u32[]{:S(2)}) collective-permute-start(bf16[32,2048]{1,0:T(8,128)(2,1)S(1)} %slice.4), channel_id=1, source_target_pairs={{0,16},{8,24},{16,0},{24,8},{1,17},{9,25},{17,1},{25,9},{2,18},{10... | collective-permute-start | bytes 393224 | tf_op jit(solution)/shard_map/ppermute | solution.py:161
  45.0 10.2 %collective-permute-start.19 = (bf16[32,2048]{1,0:T(8,128)(2,1)S(1)}, bf16[32,2048]{1,0:T(8,128)(2,1)S(1)}, u32[]{:S(2)}, u32[]{:S(2)}) collective-permute-start(bf16[32,2048]{1,0:T(8,128)(2,1)S(1)} %collective-permute-done.18), channel_id=1, source_target_pairs={{0,2},{1,5},{2,0},{3,7},{4,6},{5,1},{6,4},{7,3},{8,10},{9,13},{10,... | collective-permute-start | bytes 393224 | tf_op jit(solution)/shard_map/ppermute | solution.py:26
  46.4 9.4 %collective-permute-start.35 = (bf16[32,2048]{1,0:T(8,128)(2,1)S(1)}, bf16[32,2048]{1,0:T(8,128)(2,1)S(1)}, u32[]{:S(2)}, u32[]{:S(2)}) collective-permute-start(bf16[32,2048]{1,0:T(8,128)(2,1)S(1)} %collective-permute-done.34), channel_id=1, source_target_pairs={{0,2},{1,5},{2,0},{3,7},{4,6},{5,1},{6,4},{7,3},{8,10},{9,13},{10,... | collective-permute-start | bytes 393224 | tf_op jit(solution)/shard_map/ppermute | solution.py:26
  52.6 9.9 %collective-permute-start.20 = (bf16[32,2048]{1,0:T(8,128)(2,1)S(1)}, bf16[32,2048]{1,0:T(8,128)(2,1)S(1)}, u32[]{:S(2)}, u32[]{:S(2)}) collective-permute-start(bf16[32,2048]{1,0:T(8,128)(2,1)S(1)} %collective-permute-done.18), channel_id=1, source_target_pairs={{0,4},{1,3},{2,6},{3,1},{4,0},{5,7},{6,2},{7,5},{8,12},{9,11},{10,... | collective-permute-start | bytes 393224 | tf_op jit(solution)/shard_map/ppermute | solution.py:26
  52.9 9.5 %collective-permute-start.27 = (bf16[32,2048]{1,0:T(8,128)(2,1)S(1)}, bf16[32,2048]{1,0:T(8,128)(2,1)S(1)}, u32[]{:S(2)}, u32[]{:S(2)}) collective-permute-start(bf16[32,2048]{1,0:T(8,128)(2,1)S(1)} %collective-permute-done.26), channel_id=1, source_target_pairs={{0,2},{1,5},{2,0},{3,7},{4,6},{5,1},{6,4},{7,3},{8,10},{9,13},{10,... | collective-permute-start | bytes 393224 | tf_op jit(solution)/shard_map/ppermute | solution.py:26
  53.8 9.2 %collective-permute-start.28 = (bf16[32,2048]{1,0:T(8,128)(2,1)S(1)}, bf16[32,2048]{1,0:T(8,128)(2,1)S(1)}, u32[]{:S(2)}, u32[]{:S(2)}) collective-permute-start(bf16[32,2048]{1,0:T(8,128)(2,1)S(1)} %collective-permute-done.26), channel_id=1, source_target_pairs={{0,4},{1,3},{2,6},{3,1},{4,0},{5,7},{6,2},{7,5},{8,12},{9,11},{10,... | collective-permute-start | bytes 393224 | tf_op jit(solution)/shard_map/ppermute | solution.py:26
  55.2 7.8 %collective-permute-start.36 = (bf16[32,2048]{1,0:T(8,128)(2,1)S(1)}, bf16[32,2048]{1,0:T(8,128)(2,1)S(1)}, u32[]{:S(2)}, u32[]{:S(2)}) collective-permute-start(bf16[32,2048]{1,0:T(8,128)(2,1)S(1)} %collective-permute-done.34), channel_id=1, source_target_pairs={{0,4},{1,3},{2,6},{3,1},{4,0},{5,7},{6,2},{7,5},{8,12},{9,11},{10,... | collective-permute-start | bytes 393224 | tf_op jit(solution)/shard_map/ppermute | solution.py:26
  55.8 7.7 %collective-permute-start.37 = (bf16[32,2048]{1,0:T(8,128)(2,1)S(1)}, bf16[32,2048]{1,0:T(8,128)(2,1)S(1)}, u32[]{:S(2)}, u32[]{:S(2)}) collective-permute-start(bf16[32,2048]{1,0:T(8,128)(2,1)S(1)} %collective-permute-done.35), channel_id=1, source_target_pairs={{0,4},{1,3},{2,6},{3,1},{4,0},{5,7},{6,2},{7,5},{8,12},{9,11},{10,... | collective-permute-start | bytes 393224 | tf_op jit(solution)/shard_map/ppermute | solution.py:26
  63.5 7.0 %collective-permute-start.41 = (bf16[32,2048]{1,0:T(8,128)(2,1)S(1)}, bf16[32,2048]{1,0:T(8,128)(2,1)S(1)}, u32[]{:S(2)}, u32[]{:S(2)}) collective-permute-start(bf16[32,2048]{1,0:T(8,128)(2,1)S(1)} %collective-permute-done.37), channel_id=1, source_target_pairs={{0,1},{1,0},{2,3},{3,2},{4,5},{5,4},{6,7},{7,6},{8,9},{9,8},{10,11... | collective-permute-start | bytes 393224 | tf_op jit(solution)/shard_map/ppermute | solution.py:20
  70.8 8.1 %collective-permute-start.13 = (bf16[48,2048]{1,0:T(8,128)(2,1)S(1)}, bf16[48,2048]{1,0:T(8,128)(2,1)S(1)}, u32[]{:S(2)}, u32[]{:S(2)}) collective-permute-start(bf16[48,2048]{1,0:T(8,128)(2,1)S(1)} %collective-permute-done.11), channel_id=1, source_target_pairs={{0,4},{1,3},{2,6},{3,1},{4,0},{5,7},{6,2},{7,5},{8,12},{9,11},{10,... | collective-permute-start | bytes 589832 | tf_op jit(solution)/shard_map/ppermute | solution.py:26
  78.3 13.6 %collective-permute-start.14 = (bf16[48,2048]{1,0:T(8,128)(2,1)S(1)}, bf16[48,2048]{1,0:T(8,128)(2,1)S(1)}, u32[]{:S(2)}, u32[]{:S(2)}) collective-permute-start(bf16[48,2048]{1,0:T(8,128)(2,1)S(1)} %add_add_fusion), channel_id=1, source_target_pairs={{0,1},{1,0},{2,3},{3,2},{4,5},{5,4},{6,7},{7,6},{8,9},{9,8},{10,11... | collective-permute-start | bytes 589832 | tf_op jit(solution)/shard_map/ppermute | solution.py:20
  78.8 13.1 %collective-permute-start.16 = (bf16[48,2048]{1,0:T(8,128)(2,1)S(1)}, bf16[48,2048]{1,0:T(8,128)(2,1)S(1)}, u32[]{:S(2)}, u32[]{:S(2)}) collective-permute-start(bf16[48,2048]{1,0:T(8,128)(2,1)S(1)} %collective-permute-done.11), channel_id=1, source_target_pairs={{0,1},{1,0},{2,3},{3,2},{4,5},{5,4},{6,7},{7,6},{8,9},{9,8},{10,11... | collective-permute-start | bytes 589832 | tf_op jit(solution)/shard_map/ppermute | solution.py:20
  78.9 13.0 %collective-permute-start.15 = (bf16[48,2048]{1,0:T(8,128)(2,1)S(1)}, bf16[48,2048]{1,0:T(8,128)(2,1)S(1)}, u32[]{:S(2)}, u32[]{:S(2)}) collective-permute-start(bf16[48,2048]{1,0:T(8,128)(2,1)S(1)} %collective-permute-done.12), channel_id=1, source_target_pairs={{0,1},{1,0},{2,3},{3,2},{4,5},{5,4},{6,7},{7,6},{8,9},{9,8},{10,11... | collective-permute-start | bytes 589832 | tf_op jit(solution)/shard_map/ppermute | solution.py:20
  79.3 12.6 %collective-permute-start.17 = (bf16[48,2048]{1,0:T(8,128)(2,1)S(1)}, bf16[48,2048]{1,0:T(8,128)(2,1)S(1)}, u32[]{:S(2)}, u32[]{:S(2)}) collective-permute-start(bf16[48,2048]{1,0:T(8,128)(2,1)S(1)} %collective-permute-done.13), channel_id=1, source_target_pairs={{0,1},{1,0},{2,3},{3,2},{4,5},{5,4},{6,7},{7,6},{8,9},{9,8},{10,11... | collective-permute-start | bytes 589832 | tf_op jit(solution)/shard_map/ppermute | solution.py:20
  (19 other events, 90.8 us)

commit v3 on v0

v3 whole, which is shorter than its diff:
```python
import functools

import jax
import jax.numpy as jnp
from jax import lax
from jax.experimental import pallas as pl
from jax.experimental.pallas import tpu as pltpu
from jax.sharding import PartitionSpec as P

CHUNKS = 2
TILE = 256
MARK = 2.0
VMEM_LIMIT = 28 * 1024 * 1024
LOAD_VMEM_LIMIT = 42 * 1024 * 1024
F32, BF16 = jnp.float32, jnp.bfloat16


def chip_bits(size):
    return [1 << b for b in range(1, size.bit_length() - 1)]


def crossing(size, odd):
    return chip_bits(size)[::-1] if odd else chip_bits(size)


def mixed_permute(block, size, stage):
    even, odd = crossing(size, False)[stage], crossing(size, True)[stage]
    return lax.ppermute(block, "mem", [(m, m ^ (odd if m & 1 else even)) for m in range(size)])


def core_permute(block, size):
    return lax.ppermute(block, "mem", [(m, m ^ 1) for m in range(size)])


def gather_mem(block, size):
    held = [block]
    for stage in range(len(chip_bits(size))):
        held = held + [mixed_permute(b, size, stage) for b in held]
    return held + [core_permute(b, size) for b in held]


def block_flips(size, odd):
    flips = [0]
    for bit in crossing(size, odd):
        flips = flips + [f ^ bit for f in flips]
    return flips


def block_origins(me, size):
    odd_core = lax.rem(me, 2) == 1
    even, odd = block_flips(size, False), block_flips(size, True)
    own = [lax.bitwise_xor(me, jnp.where(odd_core, o, e)) for e, o in zip(even, odd)]
    sib = [lax.bitwise_xor(me, jnp.where(odd_core, e, o) + 1) for e, o in zip(even, odd)]
    return own + sib


def vmem_specs(count):
    return [pl.BlockSpec(memory_space=pltpu.VMEM)] * count


def call(kernel, name, out_shape, operands, flops, specs=None, scratch=(), after=(), limit=VMEM_LIMIT):
    shapes = jax.tree.leaves(out_shape)
    moved = sum(a.size * a.dtype.itemsize for a in list(operands) + shapes)
    count = len(operands)

    def run(*refs):
        kernel(*refs[:count], *refs[count + len(after) :])

    return pl.pallas_call(
        run,
        out_shape=out_shape,
        in_specs=(specs or vmem_specs(count)) + [pl.BlockSpec(memory_space=pl.ANY)] * len(after),
        out_specs=jax.tree.map(lambda _: pl.BlockSpec(memory_space=pltpu.VMEM), out_shape),
        scratch_shapes=scratch,
        compiler_params=pltpu.CompilerParams(vmem_limit_bytes=limit),
        cost_estimate=pl.CostEstimate(flops=flops, bytes_accessed=moved, transcendentals=0),
        name=name,
    )(*operands, *after)


def split_kernel(chunk, count_ref, rows_ref, out):
    slots, part = out.shape
    out[...] = rows_ref[:, chunk * part : (chunk + 1) * part]
    if chunk:
        return
    lane = lax.broadcasted_iota(jnp.int32, (slots, 128), 1)
    row = lax.broadcasted_iota(jnp.int32, (slots, 128), 0)
    dead = (lane == 0) & (row >= count_ref[0, 0])
    out[:, :128] = jnp.where(dead, MARK, rows_ref[:, :128].astype(F32)).astype(BF16)


def load_kernel(cand_hbm, cand_ref, norm_ref, sems):
    tiles = cand_ref.shape[0] // TILE
    copies = [
        pltpu.make_async_copy(
            cand_hbm.at[pl.ds(t * TILE, TILE), :], cand_ref.at[pl.ds(t * TILE, TILE), :], sems.at[t]
        )
        for t in range(tiles)
    ]
    for copy in copies:
        copy.start()
    for t, copy in enumerate(copies):
        copy.wait()
        squares = jnp.zeros((TILE, 128), F32)
        for k in range(0, cand_ref.shape[1], 128):
            entries = cand_ref[t * TILE : (t + 1) * TILE, k : k + 128].astype(F32)
            squares += entries * entries
        norm_ref[:, t * TILE : (t + 1) * TILE] = jnp.sum(squares.T, axis=0, keepdims=True)


def join_kernel(*refs):
    blocks, out = refs[:-1], refs[-1]
    out[...] = jnp.concatenate([b[...] for b in blocks], axis=0)


def select_rows(select, blocks, out):
    slots = blocks[0].shape[0]

    @pl.loop(0, out.shape[1] // TILE)
    def _(t):
        at = pl.ds(pl.multiple_of(t * TILE, TILE), TILE)
        rows = jnp.concatenate([b[:, at] for b in blocks], axis=0)
        out[:, at] = jnp.dot(select, rows, preferred_element_type=F32).astype(BF16)


def first_pick_kernel(size, chosen_ref, *refs):
    blocks, (out, select_ref, live_ref, pick_ref) = refs[:size], refs[size:]
    slots, share = blocks[0].shape[0], out.shape[0]
    picks = chosen_ref.shape[1]
    me = lax.axis_index("mem")
    origins = block_origins(me, size)
    counts = [
        jnp.sum((b[:, :1].astype(F32) < 1.5).astype(jnp.int32), axis=0, keepdims=True)
        for b in blocks
    ]
    chosen = chosen_ref[...]
    row = lax.broadcasted_iota(jnp.int32, (share, picks), 0)
    lane = lax.broadcasted_iota(jnp.int32, (share, picks), 1)
    ids = jnp.sum(jnp.where(lane == me * share + row, chosen, 0), axis=1, keepdims=True)
    across = lax.broadcasted_iota(jnp.int32, (1, slots), 1)
    down = lax.broadcasted_iota(jnp.int32, (slots, 1), 0)
    for i, count in enumerate(counts):
        offset = jnp.zeros((1, 1), jnp.int32)
        for other, origin in zip(counts, origins):
            offset += other * (origin < origins[i]).astype(jnp.int32)
        at = slice(i * slots, (i + 1) * slots)
        position = jnp.where(across < count, across + offset, -1)
        select_ref[:, at] = (ids == position).astype(F32).astype(BF16)
        live = down < count
        hit = jnp.max((chosen == down + offset).astype(F32), axis=1, keepdims=True) > 0.5
        live_ref[at, :] = jnp.where(live, 0.0, jnp.inf)
        pick_ref[at, :] = jnp.where(live & hit, 0.0, jnp.inf)
    select_rows(select_ref[...], blocks, out)


def next_pick_kernel(size, select_ref, *refs):
    select_rows(select_ref[...], refs[:size], refs[size])


def row_norms(ref):
    rows = ref[...].astype(F32)
    return jnp.sum(rows * rows, axis=1, keepdims=True)


def group_kernel(size, cand_ref, norm_ref, live_ref, pick_ref, *refs):
    blocks, (near_ref, own_ref, rows_ref, cn_ref) = refs[:-4], refs[-4:]
    slots, part = blocks[0].shape
    for i in range(size):
        at = slice(i * slots, (i + 1) * slots)
        norm = jnp.zeros((slots, 1), F32)
        for c in range(CHUNKS):
            block = blocks[c * size + i]
            rows_ref[at, c * part : (c + 1) * part] = block[...]
            norm += row_norms(block)
        cn_ref[at, :] = norm

    @pl.loop(0, cand_ref.shape[0] // TILE)
    def _(t):
        at = pl.ds(pl.multiple_of(t * TILE, TILE), TILE)
        inner = lax.dot_general(
            rows_ref[...], cand_ref[at, :], (((1,), (1,)), ((), ())), preferred_element_type=F32
        )
        gaps = cn_ref[...] - 2.0 * inner
        nearest = jnp.min(gaps + live_ref[...], axis=0, keepdims=True)
        near_ref[:, at] = nearest + norm_ref[:, at]
        own_ref[:, at] = jnp.min(gaps + pick_ref[...], axis=0, keepdims=True)


def far_gaps(chunk, cand_ref, blocks, rows_ref, cn_ref, emit):
    count, part = blocks[0].shape
    for i, block in enumerate(blocks):
        at = slice(i * count, (i + 1) * count)
        rows_ref[at, :] = block[...]
        cn_ref[at, :] = row_norms(block)

    @pl.loop(0, cand_ref.shape[0] // TILE)
    def _(t):
        at = pl.ds(pl.multiple_of(t * TILE, TILE), TILE)
        inner = lax.dot_general(
            rows_ref[...],
            cand_ref[at, chunk * part : (chunk + 1) * part],
            (((1,), (1,)), ((), ())),
            preferred_element_type=F32,
        )
        emit(at, cn_ref[...] - 2.0 * inner)


def far_kernel(chunk, cand_ref, *refs):
    blocks, (part_ref, rows_ref, cn_ref) = refs[:-3], refs[-3:]
    before = None
    if chunk:
        before, blocks = blocks[0], blocks[1:]

    def emit(at, gaps):
        part_ref[:, at] = gaps + before[:, at] if chunk else gaps

    far_gaps(chunk, cand_ref, blocks, rows_ref, cn_ref, emit)


def last_kernel(chunk, cand_ref, own_ref, norm_ref, before, *refs):
    blocks, (out, rows_ref, cn_ref) = refs[:-3], refs[-3:]

    def emit(at, gaps):
        nearest = jnp.min(gaps + before[:, at], axis=0, keepdims=True)
        out[:, at] = jnp.minimum(nearest, own_ref[:, at]) + norm_ref[:, at]

    far_gaps(chunk, cand_ref, blocks, rows_ref, cn_ref, emit)


def body(candidates, round_one, counts, chosen):
    size, groups = lax.axis_size("mem"), lax.axis_size("grp")
    slots, width = round_one.shape
    part = width // CHUNKS
    picks, rows = chosen.shape[1], candidates.shape[0]
    share = picks // size
    shape = jax.ShapeDtypeStruct
    line = shape((1, rows), F32)

    def split(chunk, *after):
        return call(
            functools.partial(split_kernel, chunk), "split", shape((slots, part), BF16),
            (counts, round_one), 0, after=after,
            specs=[pl.BlockSpec(memory_space=pltpu.SMEM)] + vmem_specs(1),
        )

    tiles = rows // TILE
    cand, norm = call(
        load_kernel, "load", [shape(candidates.shape, BF16), line], (candidates,), 0,
        specs=[pl.BlockSpec(memory_space=pltpu.HBM)], scratch=[pltpu.SemaphoreType.DMA((tiles,))],
        limit=LOAD_VMEM_LIMIT,
    )
    raw, far, shifted, near = [], [], [], None
    flops = 2 * share * size * slots * part
    out, mask = shape((share, part), BF16), shape((size * slots, 1), F32)
    for c in range(CHUNKS):
        raw.append(gather_mem(split(c, *[blocks[1] for blocks in raw[-1:]], *[norm][: len(raw)]), size))
    for c in range(CHUNKS):
        if c == 0:
            picked, select, live, pick = call(
                functools.partial(first_pick_kernel, size), "pick_first",
                [out, shape((share, size * slots), BF16), mask, mask], (chosen, *raw[c]), flops,
                after=(raw[-1][1], raw[-1][2], raw[-1][size // 2]),
            )
        else:
            picked = call(
                functools.partial(next_pick_kernel, size), "pick_next", out, (select, *raw[c]),
                flops, after=shifted,
            )
        if c == CHUNKS - 1:
            near, own = call(
                functools.partial(group_kernel, size), "group", [line] * 2,
                (cand, norm, live, pick, *sum(raw, [])), 2 * rows * size * slots * width,
                scratch=[pltpu.VMEM((size * slots, width), BF16), pltpu.VMEM((size * slots, 1), F32)],
                after=(picked,),
            )
        shifted = [
            lax.ppermute(picked, "grp", [(g, (g + k) % groups) for g in range(groups)])
            for k in range(1, groups)
        ]
        if share % 16:
            block = jnp.concatenate(shifted, axis=0)
        else:
            block = call(
                join_kernel, "join", shape(((groups - 1) * share, part), BF16), shifted, 0,
                after=() if near is None else (near,),
            )
        blocks = gather_mem(block, size)
        if blocks[0].shape[0] % 16:
            blocks = [jnp.concatenate(blocks, axis=0)]
        far.append(blocks)

    centers = (groups - 1) * picks
    scratch = [pltpu.VMEM((centers, part), BF16), pltpu.VMEM((centers, 1), F32)]
    flops = 2 * rows * centers * part
    before = ()
    for c in range(CHUNKS - 1):
        before = (
            call(
                functools.partial(far_kernel, c), "far", shape((centers, rows), F32),
                (cand, *before, *far[c]), flops, scratch=scratch,
            ),
        )
    final = call(
        functools.partial(last_kernel, CHUNKS - 1), "far_last", line,
        (cand, own, norm, *before, *far[-1]), flops, scratch=scratch,
    )
    return near.reshape(-1), final.reshape(-1)


def solution(mesh):
    in_specs = (P(("grp", "mem"), None), P(("grp", "mem"), None), P("grp", "mem"), P("grp", None))
    out_specs = (P(("grp", "mem")), P(("grp", "mem")))
    return jax.shard_map(body, mesh=mesh, in_specs=in_specs, out_specs=out_specs, check_vma=False)
```

time: 134 us -> 77.9 us (0.58)
  waiting for transfers between devices: 79.6 us -> 26.7 us
  starting transfers between devices: 0.08 us -> 25.9 us
  Pallas kernels: 0 us -> 21 us
  matrix products: 16.7 us -> 0 us
  between operations: 14.7 us -> 1.46 us
  other arithmetic: 9.64 us -> 0 us
  blocking collectives: 9.48 us -> 0 us
  local copies, waits for them, and re-layouts: 3.72 us -> 1.73 us
    all_gather x2 -> x0, waiting for transfers between devices: 78.9 us -> none  [the longest x1 49.9 us: body(): lax.all_gather(my_share, ('grp', 'mem'), axis=0, tiled=True)]
    ppermute x0 -> x34, waiting for transfers between devices: none -> 26.7 us  [the longest x12 17.6 us: mixed_permute(): lax.ppermute(block, 'mem', [(m, m ^ (odd if m & 1 else even)) for m in ra...]
    ppermute x0 -> x34, starting transfers between devices: none -> 25.9 us  [the longest x12 16.9 us: mixed_permute(): lax.ppermute(block, 'mem', [(m, m ^ (odd if m & 1 else even)) for m in ra...]
    pallas_call x0 -> x10, Pallas kernels: none -> 21 us  [call(): pl.pallas_call(run, out_shape=out_shape, in_specs=(specs or vmem_specs(co...]
    dot_general x3 -> x0, matrix products: 16.7 us -> none  [the longest x2 13.8 us: distances(): lax.dot_general(cand_rows, center_rows, (((1,), (1,)), ((), ())), preferr...]
    unnamed x1 -> x0, blocking collectives: 9.48 us -> none
    reduce_sum x4 -> x0, other arithmetic: 9.44 us -> none  [the longest x3 9.35 us: sq_norms(): return jnp.sum(jnp.square(matrix.astype(jnp.float32)), axis=1)]
    unnamed x9 -> x8, local copies, waits for them, and re-layouts: 3.05 us -> 1.73 us
  transfers between devices with their start and end apart: 2 -> 34, of which waited for: 2 -> 9; matrix products, arithmetic and copies ran while one was open for 10% -> 0% of each run, Pallas kernels for 0% -> 23%
where the time goes in v3:
time: 77.9 us; the launch traced here: 76.8 us
  waiting for transfers between devices  26.7 us (34%)
  starting transfers between devices  25.9 us (33%)
  Pallas kernels  21 us (27%)
  local copies, waits for them, and re-layouts  1.73 us (2%)
  between operations  1.46 us (2%)
    pallas_call x10, Pallas kernels, call(): pl.pallas_call(run, out_shape=out_shape, in_specs=(specs or vmem_specs(co...  21 us
    ppermute x12, waiting for transfers between devices, mixed_permute(): lax.ppermute(block, 'mem', [(m, m ^ (odd if m & 1 else even)) for m in ra...  17.6 us
    ppermute x12, starting transfers between devices, mixed_permute(): lax.ppermute(block, 'mem', [(m, m ^ (odd if m & 1 else even)) for m in ra...  16.9 us
    ppermute x6, waiting for transfers between devices, body(): lax.ppermute(picked, 'grp', [(g, (g + k) % groups) for g in range(groups)])  9.05 us
    ppermute x6, starting transfers between devices, body(): lax.ppermute(picked, 'grp', [(g, (g + k) % groups) for g in range(groups)])  6.33 us
    ppermute x16, starting transfers between devices, core_permute(): return lax.ppermute(block, 'mem', [(m, m ^ 1) for m in range(size)])  2.73 us
    unnamed x8, local copies, waits for them, and re-layouts  1.73 us
  transfers between devices with their start and end apart: 34, of which 9 were waited for; matrix products, arithmetic and copies ran while one was open for 0% of the time, Pallas kernels for 23%

profile of v3, /device:TPU:0, one launch (start us, length us, event | category | flops | bytes accessed | tf_op | source)
XLA Modules:
  0.0 76.8 jit_solution(16993636185230489506)
XLA Ops:
  2.4 3.0 %collective-permute-start = (bf16[64,2048]{1,0:T(8,128)(2,1)S(1)}, bf16[64,2048]{1,0:T(8,128)(2,1)S(1)}, u32[]{:S(2)}, u32[]{:S(2)}) collective-permute-start(bf16[64,2048]{1,0:T(8,128)(2,1)S(1)} %split.2.refs_1_.refs_4_), channel_id=1, source_target_pairs={{0,2},{1,5},{2,0},{3,7},{4,6},{5,1},{6,4},{7,3},{8,10},{9,13},{10,... | collective-permute-start | bytes 786440 | tf_op jit(solution)/shard_map/ppermute | solution.py:28
  5.4 1.5 %collective-permute-start.1 = (bf16[64,2048]{1,0:T(8,128)(2,1)S(1)}, bf16[64,2048]{1,0:T(8,128)(2,1)S(1)}, u32[]{:S(2)}, u32[]{:S(2)}) collective-permute-start(bf16[64,2048]{1,0:T(8,128)(2,1)S(1)} %split.2.refs_1_.refs_4_), channel_id=1, source_target_pairs={{0,4},{1,3},{2,6},{3,1},{4,0},{5,7},{6,2},{7,5},{8,12},{9,11},{10,... | collective-permute-start | bytes 786440 | tf_op jit(solution)/shard_map/ppermute | solution.py:28
  6.9 4.0 %load.1 = (bf16[1024,4096]{1,0:T(8,128)(2,1)S(1)}, f32[1,1024]{1,0:T(1,128)S(1)}) custom-call(bf16[1024,4096]{1,0:T(8,128)(2,1)} %refs_0_.4), custom_call_target="tpu_custom_call" | custom-call | bytes 16781312 | tf_op jit(solution)/shard_map/load/pallas_call | solution.py:69
  10.9 1.1 %collective-permute-done.refs_2_.refs_5_ = bf16[64,2048]{1,0:T(8,128)(2,1)S(1)} collective-permute-done((bf16[64,2048]{1,0:T(8,128)(2,1)S(1)}, bf16[64,2048]{1,0:T(8,128)(2,1)S(1)}, u32[]{:S(2)}, u32[]{:S(2)}) %collective-permute-start) | collective-permute-done | bytes 262176 | tf_op jit(solution)/shard_map/ppermute | solution.py:28
  12.0 2.5 %collective-permute-start.7 = (bf16[64,2048]{1,0:T(8,128)(2,1)S(1)}, bf16[64,2048]{1,0:T(8,128)(2,1)S(1)}, u32[]{:S(2)}, u32[]{:S(2)}) collective-permute-start(bf16[64,2048]{1,0:T(8,128)(2,1)S(1)} %split.3.refs_1_.refs_12_), channel_id=1, source_target_pairs={{0,2},{1,5},{2,0},{3,7},{4,6},{5,1},{6,4},{7,3},{8,10},{9,13},{10,... | collective-permute-start | bytes 786440 | tf_op jit(solution)/shard_map/ppermute | solution.py:28
  15.3 1.3 %collective-permute-start.8 = (bf16[64,2048]{1,0:T(8,128)(2,1)S(1)}, bf16[64,2048]{1,0:T(8,128)(2,1)S(1)}, u32[]{:S(2)}, u32[]{:S(2)}) collective-permute-start(bf16[64,2048]{1,0:T(8,128)(2,1)S(1)} %split.3.refs_1_.refs_12_), channel_id=1, source_target_pairs={{0,4},{1,3},{2,6},{3,1},{4,0},{5,7},{6,2},{7,5},{8,12},{9,11},{10,... | collective-permute-start | bytes 786440 | tf_op jit(solution)/shard_map/ppermute | solution.py:28
  16.6 4.7 %collective-permute-done.7.refs_9_.refs_2_.refs_13_ = bf16[64,2048]{1,0:T(8,128)(2,1)S(1)} collective-permute-done((bf16[64,2048]{1,0:T(8,128)(2,1)S(1)}, bf16[64,2048]{1,0:T(8,128)(2,1)S(1)}, u32[]{:S(2)}, u32[]{:S(2)}) %collective-permute-start.7) | collective-permute-done | bytes 262176 | tf_op jit(solution)/shard_map/ppermute | solution.py:28
  22.5 1.2 %collective-permute-done.8.refs_10_.refs_3_.refs_14_ = bf16[64,2048]{1,0:T(8,128)(2,1)S(1)} collective-permute-done((bf16[64,2048]{1,0:T(8,128)(2,1)S(1)}, bf16[64,2048]{1,0:T(8,128)(2,1)S(1)}, u32[]{:S(2)}, u32[]{:S(2)}) %collective-permute-start.8) | collective-permute-done | bytes 262176 | tf_op jit(solution)/shard_map/ppermute | solution.py:28
  24.3 3.3 %collective-permute-done.10.refs_4_.refs_15_ = bf16[64,2048]{1,0:T(8,128)(2,1)S(1)} collective-permute-done((bf16[64,2048]{1,0:T(8,128)(2,1)S(1)}, bf16[64,2048]{1,0:T(8,128)(2,1)S(1)}, u32[]{:S(2)}, u32[]{:S(2)}) %collective-permute-start.10) | collective-permute-done | bytes 262176 | tf_op jit(solution)/shard_map/ppermute | solution.py:28
  27.6 2.5 %pick_first.1 = (bf16[16,2048]{1,0:T(8,128)(2,1)S(1)}, bf16[16,512]{1,0:T(8,128)(2,1)S(1)}, f32[512,1]{1,0:T(8,128)S(1)}, f32[512,1]{1,0:T(8,128)S(1)}) custom-call(s32[1,128]{1,0:T(1,128)S(1)} %copy-done.3, bf16[64,2048]{1,0:T(8,128)(2,1)S(1)} %split.2.refs_1_.refs_4_, bf16[64,2048]{1,0:T(8,128)(2,1)S(1)} %collective-permute-done.refs_2_.refs_5_, ...), custom_call_target="tpu_custom_call" | custom-call | flops 33554432 | bytes 2183680 | tf_op jit(solution)/shard_map/pick_first/pallas_call | solution.py:69
  30.1 3.7 %collective-permute-start.16 = (bf16[16,2048]{1,0:T(8,128)(2,1)S(1)}, bf16[16,2048]{1,0:T(8,128)(2,1)S(1)}, u32[]{:S(2)}, u32[]{:S(2)}) collective-permute-start(bf16[16,2048]{1,0:T(8,128)(2,1)S(1)} %get-tuple-element.15), channel_id=1, source_target_pairs={{0,24},{8,0},{16,8},{24,16},{1,25},{9,1},{17,9},{25,17},{2,26},{10... | collective-permute-start | bytes 196616 | tf_op jit(solution)/shard_map/ppermute | solution.py:277
  33.8 2.5 %collective-permute-done.16.refs_11_.refs_2_ = bf16[16,2048]{1,0:T(8,128)(2,1)S(1)} collective-permute-done((bf16[16,2048]{1,0:T(8,128)(2,1)S(1)}, bf16[16,2048]{1,0:T(8,128)(2,1)S(1)}, u32[]{:S(2)}, u32[]{:S(2)}) %collective-permute-start.16) | collective-permute-done | bytes 65568 | tf_op jit(solution)/shard_map/ppermute | solution.py:277
  36.3 3.1 %collective-permute-done.15.refs_10_.refs_1_ = bf16[16,2048]{1,0:T(8,128)(2,1)S(1)} collective-permute-done((bf16[16,2048]{1,0:T(8,128)(2,1)S(1)}, bf16[16,2048]{1,0:T(8,128)(2,1)S(1)}, u32[]{:S(2)}, u32[]{:S(2)}) %collective-permute-start.15) | collective-permute-done | bytes 65568 | tf_op jit(solution)/shard_map/ppermute | solution.py:277
  39.4 3.5 %collective-permute-done.14.refs_9_.refs_0_ = bf16[16,2048]{1,0:T(8,128)(2,1)S(1)} collective-permute-done((bf16[16,2048]{1,0:T(8,128)(2,1)S(1)}, bf16[16,2048]{1,0:T(8,128)(2,1)S(1)}, u32[]{:S(2)}, u32[]{:S(2)}) %collective-permute-start.14) | collective-permute-done | bytes 65568 | tf_op jit(solution)/shard_map/ppermute | solution.py:277
  43.7 2.3 %collective-permute-start.17 = (bf16[48,2048]{1,0:T(8,128)(2,1)S(1)}, bf16[48,2048]{1,0:T(8,128)(2,1)S(1)}, u32[]{:S(2)}, u32[]{:S(2)}) collective-permute-start(bf16[48,2048]{1,0:T(8,128)(2,1)S(1)} %join.2.refs_1_), channel_id=1, source_target_pairs={{0,2},{1,5},{2,0},{3,7},{4,6},{5,1},{6,4},{7,3},{8,10},{9,13},{10,... | collective-permute-start | bytes 589832 | tf_op jit(solution)/shard_map/ppermute | solution.py:28
  46.0 1.2 %pick_next.1.refs_20_ = bf16[16,2048]{1,0:T(8,128)(2,1)S(1)} custom-call(bf16[16,512]{1,0:T(8,128)(2,1)S(1)} %get-tuple-element.14.refs_0_, bf16[64,2048]{1,0:T(8,128)(2,1)S(1)} %split.3.refs_1_.refs_12_, bf16[64,2048]{1,0:T(8,128)(2,1)S(1)} %collective-permute-done.7.refs_9_.refs_2_.refs_13_, ...), custom_call_target="tpu_custom_call" | custom-call | flops 33554432 | bytes 2179072 | tf_op jit(solution)/shard_map/pick_next/pallas_call | solution.py:69
  47.2 2.0 %collective-permute-start.26 = (bf16[16,2048]{1,0:T(8,128)(2,1)S(1)}, bf16[16,2048]{1,0:T(8,128)(2,1)S(1)}, u32[]{:S(2)}, u32[]{:S(2)}) collective-permute-start(bf16[16,2048]{1,0:T(8,128)(2,1)S(1)} %pick_next.1.refs_20_), channel_id=1, source_target_pairs={{0,24},{8,0},{16,8},{24,16},{1,25},{9,1},{17,9},{25,17},{2,26},{10... | collective-permute-start | bytes 196616 | tf_op jit(solution)/shard_map/ppermute | solution.py:277
  49.8 6.9 %group.1 = (f32[1,1024]{1,0:T(1,128)}, f32[1,1024]{1,0:T(1,128)S(1)}) custom-call(bf16[1024,4096]{1,0:T(8,128)(2,1)S(1)} %get-tuple-element.10.refs_0_, f32[1,1024]{1,0:T(1,128)S(1)} %get-tuple-element.11.refs_3_.refs_1_.refs_2_, f32[512,1]{1,0:T(8,128)S(1)} %get-tuple-element.12.refs_2_, f32[512,1]{1,0:T(8,128)S(1)} %get-tuple-element.13.refs_3_, ...), custom_call_target="tpu_custom_call" | custom-call | flops 4294967296 | bytes 12599296 | tf_op jit(solution)/shard_map/group/pallas_call | solution.py:69
  57.5 1.4 %collective-permute-start.19 = (bf16[48,2048]{1,0:T(8,128)(2,1)S(1)}, bf16[48,2048]{1,0:T(8,128)(2,1)S(1)}, u32[]{:S(2)}, u32[]{:S(2)}) collective-permute-start(bf16[48,2048]{1,0:T(8,128)(2,1)S(1)} %collective-permute-done.17.refs_2_), channel_id=1, source_target_pairs={{0,4},{1,3},{2,6},{3,1},{4,0},{5,7},{6,2},{7,5},{8,12},{9,11},{10,... | collective-permute-start | bytes 589832 | tf_op jit(solution)/shard_map/ppermute | solution.py:28
  60.2 4.6 %collective-permute-done.27.refs_5_ = bf16[48,2048]{1,0:T(8,128)(2,1)S(1)} collective-permute-done((bf16[48,2048]{1,0:T(8,128)(2,1)S(1)}, bf16[48,2048]{1,0:T(8,128)(2,1)S(1)}, u32[]{:S(2)}, u32[]{:S(2)}) %collective-permute-start.27) | collective-permute-done | bytes 196640 | tf_op jit(solution)/shard_map/ppermute | solution.py:28
  64.8 1.8 %collective-permute-start.29 = (bf16[48,2048]{1,0:T(8,128)(2,1)S(1)}, bf16[48,2048]{1,0:T(8,128)(2,1)S(1)}, u32[]{:S(2)}, u32[]{:S(2)}) collective-permute-start(bf16[48,2048]{1,0:T(8,128)(2,1)S(1)} %collective-permute-done.27.refs_5_), channel_id=1, source_target_pairs={{0,4},{1,3},{2,6},{3,1},{4,0},{5,7},{6,2},{7,5},{8,12},{9,11},{10,... | collective-permute-start | bytes 589832 | tf_op jit(solution)/shard_map/ppermute | solution.py:28
  67.6 2.8 %collective-permute-done.29.refs_7_ = bf16[48,2048]{1,0:T(8,128)(2,1)S(1)} collective-permute-done((bf16[48,2048]{1,0:T(8,128)(2,1)S(1)}, bf16[48,2048]{1,0:T(8,128)(2,1)S(1)}, u32[]{:S(2)}, u32[]{:S(2)}) %collective-permute-start.29) | collective-permute-done | bytes 196640 | tf_op jit(solution)/shard_map/ppermute | solution.py:28
  70.5 2.8 %far.1.refs_3_ = f32[384,1024]{1,0:T(8,128)S(1)} custom-call(bf16[1024,4096]{1,0:T(8,128)(2,1)S(1)} %get-tuple-element.10.refs_0_, bf16[48,2048]{1,0:T(8,128)(2,1)S(1)} %join.2.refs_1_, bf16[48,2048]{1,0:T(8,128)(2,1)S(1)} %collective-permute-done.17.refs_2_, bf16[48,2048]{1,0:T(8,128)(2,1)S(1)} %collective-permute-done.18.refs_3_, ...), custom_call_target="tpu_custom_call" | custom-call | flops 1610612736 | bytes 11534336 | tf_op jit(solution)/shard_map/far/pallas_call | solution.py:69
  73.3 3.5 %far_last.1 = f32[1,1024]{1,0:T(1,128)} custom-call(bf16[1024,4096]{1,0:T(8,128)(2,1)S(1)} %get-tuple-element.10.refs_0_, f32[1,1024]{1,0:T(1,128)S(1)} %get-tuple-element.17.refs_1_, f32[1,1024]{1,0:T(1,128)S(1)} %get-tuple-element.11.refs_3_.refs_1_.refs_2_, f32[384,1024]{1,0:T(8,128)S(1)} %far.1.refs_3_, bf16[48,2048]{1,0:T(8,128)(2,1)S(1)} %join.3.refs_4_, ...), custom_call_target="tpu_custom_call" | custom-call | flops 1610612736 | bytes 11546624 | tf_op jit(solution)/shard_map/far_last/pallas_call | solution.py:69
  (62 shorter events, 8.2 us)
Async XLA Ops:
  2.4 9.6 %collective-permute-start = (bf16[64,2048]{1,0:T(8,128)(2,1)S(1)}, bf16[64,2048]{1,0:T(8,128)(2,1)S(1)}, u32[]{:S(2)}, u32[]{:S(2)}) collective-permute-start(bf16[64,2048]{1,0:T(8,128)(2,1)S(1)} %split.2.refs_1_.refs_4_), channel_id=1, source_target_pairs={{0,2},{1,5},{2,0},{3,7},{4,6},{5,1},{6,4},{7,3},{8,10},{9,13},{10,... | collective-permute-start | bytes 786440 | tf_op jit(solution)/shard_map/ppermute | solution.py:28
  5.4 9.2 %collective-permute-start.1 = (bf16[64,2048]{1,0:T(8,128)(2,1)S(1)}, bf16[64,2048]{1,0:T(8,128)(2,1)S(1)}, u32[]{:S(2)}, u32[]{:S(2)}) collective-permute-start(bf16[64,2048]{1,0:T(8,128)(2,1)S(1)} %split.2.refs_1_.refs_4_), channel_id=1, source_target_pairs={{0,4},{1,3},{2,6},{3,1},{4,0},{5,7},{6,2},{7,5},{8,12},{9,11},{10,... | collective-permute-start | bytes 786440 | tf_op jit(solution)/shard_map/ppermute | solution.py:28
  6.9 8.4 %collective-permute-start.3 = (bf16[64,2048]{1,0:T(8,128)(2,1)S(1)}, bf16[64,2048]{1,0:T(8,128)(2,1)S(1)}, u32[]{:S(2)}, u32[]{:S(2)}) collective-permute-start(bf16[64,2048]{1,0:T(8,128)(2,1)S(1)} %split.2.refs_1_.refs_4_), channel_id=1, source_target_pairs={{0,1},{1,0},{2,3},{3,2},{4,5},{5,4},{6,7},{7,6},{8,9},{9,8},{10,11... | collective-permute-start | bytes 786440 | tf_op jit(solution)/shard_map/ppermute | solution.py:32
  12.0 9.2 %collective-permute-start.7 = (bf16[64,2048]{1,0:T(8,128)(2,1)S(1)}, bf16[64,2048]{1,0:T(8,128)(2,1)S(1)}, u32[]{:S(2)}, u32[]{:S(2)}) collective-permute-start(bf16[64,2048]{1,0:T(8,128)(2,1)S(1)} %split.3.refs_1_.refs_12_), channel_id=1, source_target_pairs={{0,2},{1,5},{2,0},{3,7},{4,6},{5,1},{6,4},{7,3},{8,10},{9,13},{10,... | collective-permute-start | bytes 786440 | tf_op jit(solution)/shard_map/ppermute | solution.py:28
  14.5 7.4 %collective-permute-start.5 = (bf16[64,2048]{1,0:T(8,128)(2,1)S(1)}, bf16[64,2048]{1,0:T(8,128)(2,1)S(1)}, u32[]{:S(2)}, u32[]{:S(2)}) collective-permute-start(bf16[64,2048]{1,0:T(8,128)(2,1)S(1)} %collective-permute-done.1.refs_3_.refs_6_), channel_id=1, source_target_pairs={{0,1},{1,0},{2,3},{3,2},{4,5},{5,4},{6,7},{7,6},{8,9},{9,8},{10,11... | collective-permute-start | bytes 786440 | tf_op jit(solution)/shard_map/ppermute | solution.py:32
  14.5 7.4 %collective-permute-start.2 = (bf16[64,2048]{1,0:T(8,128)(2,1)S(1)}, bf16[64,2048]{1,0:T(8,128)(2,1)S(1)}, u32[]{:S(2)}, u32[]{:S(2)}) collective-permute-start(bf16[64,2048]{1,0:T(8,128)(2,1)S(1)} %collective-permute-done.refs_2_.refs_5_), channel_id=1, source_target_pairs={{0,4},{1,3},{2,6},{3,1},{4,0},{5,7},{6,2},{7,5},{8,12},{9,11},{10,... | collective-permute-start | bytes 786440 | tf_op jit(solution)/shard_map/ppermute | solution.py:28
  15.3 7.2 %collective-permute-start.4 = (bf16[64,2048]{1,0:T(8,128)(2,1)S(1)}, bf16[64,2048]{1,0:T(8,128)(2,1)S(1)}, u32[]{:S(2)}, u32[]{:S(2)}) collective-permute-start(bf16[64,2048]{1,0:T(8,128)(2,1)S(1)} %collective-permute-done.refs_2_.refs_5_), channel_id=1, source_target_pairs={{0,1},{1,0},{2,3},{3,2},{4,5},{5,4},{6,7},{7,6},{8,9},{9,8},{10,11... | collective-permute-start | bytes 786440 | tf_op jit(solution)/shard_map/ppermute | solution.py:32
  15.3 8.5 %collective-permute-start.8 = (bf16[64,2048]{1,0:T(8,128)(2,1)S(1)}, bf16[64,2048]{1,0:T(8,128)(2,1)S(1)}, u32[]{:S(2)}, u32[]{:S(2)}) collective-permute-start(bf16[64,2048]{1,0:T(8,128)(2,1)S(1)} %split.3.refs_1_.refs_12_), channel_id=1, source_target_pairs={{0,4},{1,3},{2,6},{3,1},{4,0},{5,7},{6,2},{7,5},{8,12},{9,11},{10,... | collective-permute-start | bytes 786440 | tf_op jit(solution)/shard_map/ppermute | solution.py:28
  21.2 6.4 %collective-permute-start.10 = (bf16[64,2048]{1,0:T(8,128)(2,1)S(1)}, bf16[64,2048]{1,0:T(8,128)(2,1)S(1)}, u32[]{:S(2)}, u32[]{:S(2)}) collective-permute-start(bf16[64,2048]{1,0:T(8,128)(2,1)S(1)} %collective-permute-done.7.refs_9_.refs_2_.refs_13_), channel_id=1, source_target_pairs={{0,4},{1,3},{2,6},{3,1},{4,0},{5,7},{6,2},{7,5},{8,12},{9,11},{10,... | collective-permute-start | bytes 786440 | tf_op jit(solution)/shard_map/ppermute | solution.py:28
  22.5 23.5 %collective-permute-start.11 = (bf16[64,2048]{1,0:T(8,128)(2,1)S(1)}, bf16[64,2048]{1,0:T(8,128)(2,1)S(1)}, u32[]{:S(2)}, u32[]{:S(2)}) collective-permute-start(bf16[64,2048]{1,0:T(8,128)(2,1)S(1)} %collective-permute-done.7.refs_9_.refs_2_.refs_13_), channel_id=1, source_target_pairs={{0,1},{1,0},{2,3},{3,2},{4,5},{5,4},{6,7},{7,6},{8,9},{9,8},{10,11... | collective-permute-start | bytes 786440 | tf_op jit(solution)/shard_map/ppermute | solution.py:32
  23.7 22.2 %collective-permute-start.12 = (bf16[64,2048]{1,0:T(8,128)(2,1)S(1)}, bf16[64,2048]{1,0:T(8,128)(2,1)S(1)}, u32[]{:S(2)}, u32[]{:S(2)}) collective-permute-start(bf16[64,2048]{1,0:T(8,128)(2,1)S(1)} %collective-permute-done.8.refs_10_.refs_3_.refs_14_), channel_id=1, source_target_pairs={{0,1},{1,0},{2,3},{3,2},{4,5},{5,4},{6,7},{7,6},{8,9},{9,8},{10,11... | collective-permute-start | bytes 786440 | tf_op jit(solution)/shard_map/ppermute | solution.py:32
  27.6 18.3 %collective-permute-start.13 = (bf16[64,2048]{1,0:T(8,128)(2,1)S(1)}, bf16[64,2048]{1,0:T(8,128)(2,1)S(1)}, u32[]{:S(2)}, u32[]{:S(2)}) collective-permute-start(bf16[64,2048]{1,0:T(8,128)(2,1)S(1)} %collective-permute-done.10.refs_4_.refs_15_), channel_id=1, source_target_pairs={{0,1},{1,0},{2,3},{3,2},{4,5},{5,4},{6,7},{7,6},{8,9},{9,8},{10,11... | collective-permute-start | bytes 786440 | tf_op jit(solution)/shard_map/ppermute | solution.py:32
  36.3 6.6 %collective-permute-start.14 = (bf16[16,2048]{1,0:T(8,128)(2,1)S(1)}, bf16[16,2048]{1,0:T(8,128)(2,1)S(1)}, u32[]{:S(2)}, u32[]{:S(2)}) collective-permute-start(bf16[16,2048]{1,0:T(8,128)(2,1)S(1)} %get-tuple-element.15), channel_id=1, source_target_pairs={{0,8},{8,16},{16,24},{24,0},{1,9},{9,17},{17,25},{25,1},{2,10},{10... | collective-permute-start | bytes 196616 | tf_op jit(solution)/shard_map/ppermute | solution.py:277
  42.9 16.0 %collective-permute-start.18 = (bf16[48,2048]{1,0:T(8,128)(2,1)S(1)}, bf16[48,2048]{1,0:T(8,128)(2,1)S(1)}, u32[]{:S(2)}, u32[]{:S(2)}) collective-permute-start(bf16[48,2048]{1,0:T(8,128)(2,1)S(1)} %join.2.refs_1_), channel_id=1, source_target_pairs={{0,4},{1,3},{2,6},{3,1},{4,0},{5,7},{6,2},{7,5},{8,12},{9,11},{10,... | collective-permute-start | bytes 589832 | tf_op jit(solution)/shard_map/ppermute | solution.py:28
  43.7 13.9 %collective-permute-start.17 = (bf16[48,2048]{1,0:T(8,128)(2,1)S(1)}, bf16[48,2048]{1,0:T(8,128)(2,1)S(1)}, u32[]{:S(2)}, u32[]{:S(2)}) collective-permute-start(bf16[48,2048]{1,0:T(8,128)(2,1)S(1)} %join.2.refs_1_), channel_id=1, source_target_pairs={{0,2},{1,5},{2,0},{3,7},{4,6},{5,1},{6,4},{7,3},{8,10},{9,13},{10,... | collective-permute-start | bytes 589832 | tf_op jit(solution)/shard_map/ppermute | solution.py:28
  47.2 9.5 %collective-permute-start.26 = (bf16[16,2048]{1,0:T(8,128)(2,1)S(1)}, bf16[16,2048]{1,0:T(8,128)(2,1)S(1)}, u32[]{:S(2)}, u32[]{:S(2)}) collective-permute-start(bf16[16,2048]{1,0:T(8,128)(2,1)S(1)} %pick_next.1.refs_20_), channel_id=1, source_target_pairs={{0,24},{8,0},{16,8},{24,16},{1,25},{9,1},{17,9},{25,17},{2,26},{10... | collective-permute-start | bytes 196616 | tf_op jit(solution)/shard_map/ppermute | solution.py:277
  49.2 7.5 %collective-permute-start.25 = (bf16[16,2048]{1,0:T(8,128)(2,1)S(1)}, bf16[16,2048]{1,0:T(8,128)(2,1)S(1)}, u32[]{:S(2)}, u32[]{:S(2)}) collective-permute-start(bf16[16,2048]{1,0:T(8,128)(2,1)S(1)} %pick_next.1.refs_20_), channel_id=1, source_target_pairs={{0,16},{8,24},{16,0},{24,8},{1,17},{9,25},{17,1},{25,9},{2,18},{10... | collective-permute-start | bytes 196616 | tf_op jit(solution)/shard_map/ppermute | solution.py:277
  49.2 7.5 %collective-permute-start.24 = (bf16[16,2048]{1,0:T(8,128)(2,1)S(1)}, bf16[16,2048]{1,0:T(8,128)(2,1)S(1)}, u32[]{:S(2)}, u32[]{:S(2)}) collective-permute-start(bf16[16,2048]{1,0:T(8,128)(2,1)S(1)} %pick_next.1.refs_20_), channel_id=1, source_target_pairs={{0,8},{8,16},{16,24},{24,0},{1,9},{9,17},{17,25},{25,1},{2,10},{10... | collective-permute-start | bytes 196616 | tf_op jit(solution)/shard_map/ppermute | solution.py:277
  57.5 7.3 %collective-permute-start.27 = (bf16[48,2048]{1,0:T(8,128)(2,1)S(1)}, bf16[48,2048]{1,0:T(8,128)(2,1)S(1)}, u32[]{:S(2)}, u32[]{:S(2)}) collective-permute-start(bf16[48,2048]{1,0:T(8,128)(2,1)S(1)} %join.3.refs_4_), channel_id=1, source_target_pairs={{0,2},{1,5},{2,0},{3,7},{4,6},{5,1},{6,4},{7,3},{8,10},{9,13},{10,... | collective-permute-start | bytes 589832 | tf_op jit(solution)/shard_map/ppermute | solution.py:28
  57.5 9.1 %collective-permute-start.19 = (bf16[48,2048]{1,0:T(8,128)(2,1)S(1)}, bf16[48,2048]{1,0:T(8,128)(2,1)S(1)}, u32[]{:S(2)}, u32[]{:S(2)}) collective-permute-start(bf16[48,2048]{1,0:T(8,128)(2,1)S(1)} %collective-permute-done.17.refs_2_), channel_id=1, source_target_pairs={{0,4},{1,3},{2,6},{3,1},{4,0},{5,7},{6,2},{7,5},{8,12},{9,11},{10,... | collective-permute-start | bytes 589832 | tf_op jit(solution)/shard_map/ppermute | solution.py:28
  58.9 7.7 %collective-permute-start.22 = (bf16[48,2048]{1,0:T(8,128)(2,1)S(1)}, bf16[48,2048]{1,0:T(8,128)(2,1)S(1)}, u32[]{:S(2)}, u32[]{:S(2)}) collective-permute-start(bf16[48,2048]{1,0:T(8,128)(2,1)S(1)} %collective-permute-done.18.refs_3_), channel_id=1, source_target_pairs={{0,1},{1,0},{2,3},{3,2},{4,5},{5,4},{6,7},{7,6},{8,9},{9,8},{10,11... | collective-permute-start | bytes 589832 | tf_op jit(solution)/shard_map/ppermute | solution.py:32
  59.1 8.0 %collective-permute-start.21 = (bf16[48,2048]{1,0:T(8,128)(2,1)S(1)}, bf16[48,2048]{1,0:T(8,128)(2,1)S(1)}, u32[]{:S(2)}, u32[]{:S(2)}) collective-permute-start(bf16[48,2048]{1,0:T(8,128)(2,1)S(1)} %collective-permute-done.17.refs_2_), channel_id=1, source_target_pairs={{0,1},{1,0},{2,3},{3,2},{4,5},{5,4},{6,7},{7,6},{8,9},{9,8},{10,11... | collective-permute-start | bytes 589832 | tf_op jit(solution)/shard_map/ppermute | solution.py:32
  59.4 7.8 %collective-permute-start.28 = (bf16[48,2048]{1,0:T(8,128)(2,1)S(1)}, bf16[48,2048]{1,0:T(8,128)(2,1)S(1)}, u32[]{:S(2)}, u32[]{:S(2)}) collective-permute-start(bf16[48,2048]{1,0:T(8,128)(2,1)S(1)} %join.3.refs_4_), channel_id=1, source_target_pairs={{0,4},{1,3},{2,6},{3,1},{4,0},{5,7},{6,2},{7,5},{8,12},{9,11},{10,... | collective-permute-start | bytes 589832 | tf_op jit(solution)/shard_map/ppermute | solution.py:28
  66.6 6.7 %collective-permute-start.30 = (bf16[48,2048]{1,0:T(8,128)(2,1)S(1)}, bf16[48,2048]{1,0:T(8,128)(2,1)S(1)}, u32[]{:S(2)}, u32[]{:S(2)}) collective-permute-start(bf16[48,2048]{1,0:T(8,128)(2,1)S(1)} %join.3.refs_4_), channel_id=1, source_target_pairs={{0,1},{1,0},{2,3},{3,2},{4,5},{5,4},{6,7},{7,6},{8,9},{9,8},{10,11... | collective-permute-start | bytes 589832 | tf_op jit(solution)/shard_map/ppermute | solution.py:32
  (14 other events, 88.8 us)

commit v4 on v0

v4 whole, which is shorter than its diff:
```python
import functools

import jax
import jax.numpy as jnp
from jax import lax
from jax.experimental import pallas as pl
from jax.experimental.pallas import tpu as pltpu
from jax.sharding import PartitionSpec as P

CHUNKS = 2
TILE = 256
MARK = 2.0
MIB = 1024 * 1024
F32, BF16 = jnp.float32, jnp.bfloat16


def chip_bits(size):
    return [1 << b for b in range(1, size.bit_length() - 1)]


def crossing(size, odd):
    return chip_bits(size)[::-1] if odd else chip_bits(size)


def mixed_permute(block, size, stage):
    even, odd = crossing(size, False)[stage], crossing(size, True)[stage]
    return lax.ppermute(block, "mem", [(m, m ^ (odd if m & 1 else even)) for m in range(size)])


def core_permute(block, size):
    return lax.ppermute(block, "mem", [(m, m ^ 1) for m in range(size)])


def gather_chips(block, size):
    held = [block]
    for stage in range(len(chip_bits(size))):
        held = held + [mixed_permute(b, size, stage) for b in held]
    return held


def block_flips(size, odd):
    flips = [0]
    for bit in crossing(size, odd):
        flips = flips + [f ^ bit for f in flips]
    return flips


def sibling_place(index, size):
    return block_flips(size, True).index(block_flips(size, False)[index])


def vmem_specs(count):
    return [pl.BlockSpec(memory_space=pltpu.VMEM)] * count


def call(
    kernel, name, out_shape, operands, flops=0, specs=None, scratch=(), after=(), limit=28 * MIB
):
    shapes = jax.tree.leaves(out_shape)
    moved = sum(a.size * a.dtype.itemsize for a in list(operands) + shapes)
    count = len(operands)

    def run(*refs):
        kernel(*refs[:count], *refs[count + len(after) :])

    return pl.pallas_call(
        run,
        out_shape=out_shape,
        in_specs=(specs or vmem_specs(count)) + [pl.BlockSpec(memory_space=pl.ANY)] * len(after),
        out_specs=jax.tree.map(lambda _: pl.BlockSpec(memory_space=pltpu.VMEM), out_shape),
        scratch_shapes=scratch,
        compiler_params=pltpu.CompilerParams(vmem_limit_bytes=limit),
        cost_estimate=pl.CostEstimate(flops=flops, bytes_accessed=moved, transcendentals=0),
        name=name,
    )(*operands, *after)


def mark_kernel(count_ref, rows_ref, keep_ref, send_ref):
    slots, half = keep_ref.shape
    core = lax.rem(lax.axis_index("mem"), 2)
    lane = lax.broadcasted_iota(jnp.int32, (slots, 128), 1)
    row = lax.broadcasted_iota(jnp.int32, (slots, 128), 0)
    dead = (lane == 0) & (row >= count_ref[0, 0])
    for out, start in ((keep_ref, core * half), (send_ref, (1 - core) * half)):
        start = pl.multiple_of(start, half)
        first = rows_ref[:, pl.ds(start, 128)].astype(F32)
        out[...] = rows_ref[:, pl.ds(start, half)]
        out[:, :128] = jnp.where(dead, MARK, first).astype(BF16)


def load_kernel(cand_hbm, cand_ref, norm_ref, sems):
    half = cand_ref.shape[1] // 2
    part = half // CHUNKS
    core = lax.rem(lax.axis_index("mem"), 2)
    tiles = cand_ref.shape[0] // TILE
    copies = []
    for t in range(tiles):
        at = pl.ds(t * TILE, TILE)
        for p in range(2 * CHUNKS):
            own = core if p % 2 == 0 else 1 - core
            start = pl.multiple_of(own * half + p // 2 * part, part)
            copies.append(
                pltpu.make_async_copy(
                    cand_hbm.at[at, pl.ds(start, part)],
                    cand_ref.at[at, pl.ds(p * part, part)],
                    sems.at[len(copies)],
                )
            )
    for copy in copies:
        copy.start()
    for t in range(tiles):
        for copy in copies[t * 2 * CHUNKS : (t + 1) * 2 * CHUNKS]:
            copy.wait()
        squares = jnp.zeros((TILE, 128), F32)
        for k in range(0, cand_ref.shape[1], 128):
            entries = cand_ref[t * TILE : (t + 1) * TILE, k : k + 128].astype(F32)
            squares += entries * entries
        norm_ref[:, t * TILE : (t + 1) * TILE] = jnp.sum(squares.T, axis=0, keepdims=True)


def join_kernel(count, start, *refs):
    blocks, out = refs[:count], refs[count]
    rows = blocks[0].shape[0]
    for i, block in enumerate(blocks):
        out[i * rows : (i + 1) * rows, :] = block[:, start : start + out.shape[1]]


def beside_kernel(*refs):
    blocks, out = refs[:-1], refs[-1]
    part = blocks[0].shape[1]
    for i, block in enumerate(blocks):
        out[:, i * part : (i + 1) * part] = block[...]


def select_rows(select, blocks, outs):
    @pl.loop(0, outs[0].shape[1] // TILE)
    def _(t):
        at = pl.ds(pl.multiple_of(t * TILE, TILE), TILE)
        rows = jnp.concatenate([b[:, at] for b in blocks], axis=0)
        found = jnp.dot(select, rows, preferred_element_type=F32).astype(BF16)
        top = 0
        for out in outs:
            out[:, at] = found[top : top + out.shape[0], :]
            top += out.shape[0]


def first_pick_kernel(size, chosen_ref, *refs):
    blocks, (share_ref, dense_ref, select_ref) = refs[:-3], refs[-3:]
    slots, share, live = blocks[0].shape[0] // 2, share_ref.shape[0], dense_ref.shape[0]
    picks = chosen_ref.shape[1]
    me = lax.axis_index("mem")
    odd_core = lax.rem(me, 2) == 1
    origins, counts = [], []
    for e, o, block in zip(block_flips(size, False), block_flips(size, True), blocks):
        origin = lax.bitwise_xor(me, jnp.where(odd_core, o, e))
        alive = (block[:, :1].astype(F32) < 1.5).astype(jnp.int32)
        for h in range(2):
            origins.append(lax.bitwise_xor(origin, h))
            counts.append(jnp.sum(alive[h * slots : (h + 1) * slots], axis=0, keepdims=True))
    chosen = chosen_ref[...]
    row = lax.broadcasted_iota(jnp.int32, (share, picks), 0)
    lane = lax.broadcasted_iota(jnp.int32, (share, picks), 1)
    mine = lane == (me // 2) * share + row
    ids = jnp.sum(jnp.where(mine, chosen, 0), axis=1, keepdims=True)
    wanted = jnp.concatenate([ids, lax.broadcasted_iota(jnp.int32, (live, 1), 0)], axis=0)
    across = lax.broadcasted_iota(jnp.int32, (1, 2 * slots), 1)
    for i in range(0, size, 2):
        offsets = []
        for mine in origins[i : i + 2]:
            offset = jnp.zeros((1, 1), jnp.int32)
            for count, origin in zip(counts, origins):
                offset += count * (origin < mine).astype(jnp.int32)
            offsets.append(offset)
        first = across < slots
        within = jnp.where(first, across, across - slots)
        position = within + jnp.where(first, offsets[0], offsets[1])
        alive = within < jnp.where(first, counts[i], counts[i + 1])
        position = jnp.where(alive, position, -1)
        select_ref[:, i * slots : (i + 2) * slots] = (wanted == position).astype(F32).astype(BF16)
    select_rows(select_ref[...], blocks, (share_ref, dense_ref))


def next_pick_kernel(select_ref, *refs):
    select_rows(select_ref[...], refs[:-2], refs[-2:])


def row_norms(rows):
    rows = rows.astype(F32)
    return jnp.sum(rows * rows, axis=1, keepdims=True)


def product(rows, cand):
    return lax.dot_general(rows, cand, (((1,), (1,)), ((), ())), preferred_element_type=F32)


def group_kernel(picks, cand_ref, norm_ref, chosen_ref, own, sib, near_ref, best_ref, rows_ref, cn_ref):
    live, part = own.shape[0], own.shape[1] // CHUNKS
    for c in range(CHUNKS):
        at = slice(c * part, (c + 1) * part)
        rows_ref[:, 2 * c * part : (2 * c + 1) * part] = own[:, at]
        rows_ref[:, (2 * c + 1) * part : (2 * c + 2) * part] = sib[:, at]
    norm = row_norms(own[...]) + row_norms(sib[...])
    cn_ref[...] = norm
    down = lax.broadcasted_iota(jnp.int32, (live, 1), 0)
    hit = jnp.max((chosen_ref[...] == down).astype(F32), axis=1, keepdims=True) > 0.5
    outside = jnp.where(hit, 0.0, jnp.inf)

    @pl.loop(0, cand_ref.shape[0] // TILE)
    def _(t):
        at = pl.ds(pl.multiple_of(t * TILE, TILE), TILE)
        gaps = cn_ref[...] - 2.0 * product(rows_ref[...], cand_ref[at, :])
        near_ref[:, at] = jnp.min(gaps, axis=0, keepdims=True) + norm_ref[:, at]
        best_ref[:, at] = jnp.min(gaps + outside, axis=0, keepdims=True)


def far_rows(size, blocks, early, late, rows_ref):
    rows, part = blocks[0].shape
    last = len(blocks) - 1
    for i, block in enumerate(blocks):
        rows_ref[i * rows : (i + 1) * rows, :part] = block[...]
        top = sibling_place(i, size) * rows
        other = late[...] if i == last else early[i * rows : (i + 1) * rows, :]
        rows_ref[top : top + rows, part:] = other


def far_kernel(size, chunk, cand_ref, *refs):
    before = refs[:1] if chunk else ()
    *blocks, early, late, out, rows_ref = refs[len(before) :]
    far_rows(size, blocks, early, late, rows_ref)
    width = rows_ref.shape[1]
    norm = row_norms(rows_ref[...])

    @pl.loop(0, cand_ref.shape[0] // TILE)
    def _(t):
        at = pl.ds(pl.multiple_of(t * TILE, TILE), TILE)
        inner = product(rows_ref[...], cand_ref[at, chunk * width : (chunk + 1) * width])
        gaps = norm - 2.0 * inner
        for ref in before:
            gaps += ref[:, at]
        out[:, at] = gaps


def last_kernel(size, chunk, cand_ref, best_ref, norm_ref, *refs):
    before = refs[:1] if chunk else ()
    *blocks, early, late, out, rows_ref = refs[len(before) :]
    far_rows(size, blocks, early, late, rows_ref)
    width = rows_ref.shape[1]
    norm = row_norms(rows_ref[...])

    @pl.loop(0, cand_ref.shape[0] // TILE)
    def _(t):
        at = pl.ds(pl.multiple_of(t * TILE, TILE), TILE)
        inner = product(rows_ref[...], cand_ref[at, chunk * width : (chunk + 1) * width])
        gaps = norm - 2.0 * inner
        for ref in before:
            gaps += ref[:, at]
        nearest = jnp.minimum(jnp.min(gaps, axis=0, keepdims=True), best_ref[:, at])
        out[:, at] = nearest + norm_ref[:, at]


def body(candidates, round_one, counts, chosen):
    size, groups = lax.axis_size("mem"), lax.axis_size("grp")
    slots, width = round_one.shape
    half, chips = width // 2, size // 2
    part = half // CHUNKS
    picks, rows = chosen.shape[1], candidates.shape[0]
    share, live = picks // chips, size * slots * 3 // 8
    centers = (groups - 1) * picks

    def bf16(*dims):
        return jax.ShapeDtypeStruct(dims, BF16)

    line = jax.ShapeDtypeStruct((1, rows), F32)
    keep, send = call(
        mark_kernel, "mark", [bf16(slots, half)] * 2, (counts, round_one),
        specs=[pl.BlockSpec(memory_space=pltpu.SMEM)] + vmem_specs(1),
    )
    other = core_permute(send, size)
    cand, norm = call(
        load_kernel, "load", [bf16(rows, width), line], (candidates,),
        specs=[pl.BlockSpec(memory_space=pltpu.HBM)],
        scratch=[pltpu.SemaphoreType.DMA((rows // TILE * 2 * CHUNKS,))], limit=42 * MIB,
    )

    def join(blocks, columns, start=0, after=()):
        count = blocks[0].shape[0] * len(blocks)
        return call(
            functools.partial(join_kernel, len(blocks), start), "join", bf16(count, columns),
            blocks, after=after,
        )

    raw = []
    for c in range(CHUNKS):
        after = (*raw[-1][1:3], norm) if c else ()
        raw.append(gather_chips(join((keep, other), part, c * part, after), size))

    dense, shifted, select = [], [], None
    for c in range(CHUNKS):
        outs = [bf16(share, part), bf16(live, part)]
        flops = 2 * (share + live) * size * slots * part
        if c == 0:
            picked, found, select = call(
                functools.partial(first_pick_kernel, size), "pick_first",
                outs + [bf16(share + live, size * slots)], (chosen, *raw[c]), flops,
            )
        else:
            picked, found = call(
                next_pick_kernel, "pick_next", outs, (select, *raw[c]), flops, after=shifted[-1]
            )
        dense.append(found)
        shifted.append(
            [
                lax.ppermute(picked, "grp", [(g, (g + k) % groups) for g in range(groups)])
                for k in range(1, groups)
            ]
        )

    far, held = [], ()
    for c in range(CHUNKS):
        if c == CHUNKS - 1:
            own = call(
                beside_kernel, "beside", bf16(live, half), dense, after=(*shifted[c], *held[1:3])
            )
            near, best = call(
                functools.partial(group_kernel, picks), "group", [line] * 2,
                (cand, norm, chosen, own, core_permute(own, size)), 2 * rows * live * width,
                scratch=[pltpu.VMEM((live, width), BF16), pltpu.VMEM((live, 1), F32)],
            )
        held = gather_chips(join(shifted[c], part, after=() if c else (picked,)), size)
        early = join(held[:-1], part, after=(best,) if c == CHUNKS - 1 else ())
        far.append((*held, core_permute(early, size), core_permute(held[-1], size)))

    scratch = [pltpu.VMEM((centers, 2 * part), BF16)]
    flops = 2 * rows * centers * 2 * part
    before = ()
    for c in range(CHUNKS - 1):
        before = (
            call(
                functools.partial(far_kernel, size, c), "far",
                jax.ShapeDtypeStruct((centers, rows), F32), (cand, *before, *far[c]), flops,
                scratch=scratch,
            ),
        )
    final = call(
        functools.partial(last_kernel, size, CHUNKS - 1), "far_last", line,
        (cand, best, norm, *before, *far[-1]), flops, scratch=scratch,
    )
    return near.reshape(-1), final.reshape(-1)


def solution(mesh):
    in_specs = (P(("grp", "mem"), None), P(("grp", "mem"), None), P("grp", "mem"), P("grp", None))
    out_specs = (P(("grp", "mem")), P(("grp", "mem")))
    return jax.shard_map(body, mesh=mesh, in_specs=in_specs, out_specs=out_specs, check_vma=False)
```

time: 134 us -> 68.4 us (0.51)
  waiting for transfers between devices: 79.6 us -> 21.3 us
  starting transfers between devices: 0.08 us -> 27.2 us
  Pallas kernels: 0 us -> 17.2 us
  matrix products: 16.7 us -> 0 us
  between operations: 14.7 us -> 1.44 us
  other arithmetic: 9.64 us -> 0 us
  blocking collectives: 9.48 us -> 0 us
  local copies, waits for them, and re-layouts: 3.72 us -> 1.04 us
    all_gather x2 -> x0, waiting for transfers between devices: 78.9 us -> none  [the longest x1 49.9 us: body(): lax.all_gather(my_share, ('grp', 'mem'), axis=0, tiled=True)]
    ppermute x0 -> x24, starting transfers between devices: none -> 27.2 us  [the longest x12 16.7 us: mixed_permute(): lax.ppermute(block, 'mem', [(m, m ^ (odd if m & 1 else even)) for m in ra...]
    ppermute x0 -> x24, waiting for transfers between devices: none -> 21.3 us  [the longest x12 12.8 us: mixed_permute(): lax.ppermute(block, 'mem', [(m, m ^ (odd if m & 1 else even)) for m in ra...]
    pallas_call x0 -> x14, Pallas kernels: none -> 17.2 us  [call(): pl.pallas_call(run, out_shape=out_shape, in_specs=(specs or vmem_specs(co...]
    dot_general x3 -> x0, matrix products: 16.7 us -> none  [the longest x2 13.8 us: distances(): lax.dot_general(cand_rows, center_rows, (((1,), (1,)), ((), ())), preferr...]
    unnamed x1 -> x0, blocking collectives: 9.48 us -> none
    reduce_sum x4 -> x0, other arithmetic: 9.44 us -> none  [the longest x3 9.35 us: sq_norms(): return jnp.sum(jnp.square(matrix.astype(jnp.float32)), axis=1)]
    unnamed x9 -> x4, local copies, waits for them, and re-layouts: 3.05 us -> 1.04 us
  transfers between devices with their start and end apart: 2 -> 24, of which waited for: 2 -> 14; matrix products, arithmetic and copies ran while one was open for 10% -> 0% of each run, Pallas kernels for 0% -> 18%
where the time goes in v4:
time: 68.4 us; the launch traced here: 68.1 us
  starting transfers between devices  27.2 us (40%)
  waiting for transfers between devices  21.3 us (31%)
  Pallas kernels  17.2 us (25%)
  between operations  1.44 us (2%)
  local copies, waits for them, and re-layouts  1.04 us (2%)
    pallas_call x14, Pallas kernels, call(): pl.pallas_call(run, out_shape=out_shape, in_specs=(specs or vmem_specs(co...  17.2 us
    ppermute x12, starting transfers between devices, mixed_permute(): lax.ppermute(block, 'mem', [(m, m ^ (odd if m & 1 else even)) for m in ra...  16.7 us
    ppermute x12, waiting for transfers between devices, mixed_permute(): lax.ppermute(block, 'mem', [(m, m ^ (odd if m & 1 else even)) for m in ra...  12.8 us
    ppermute x6, starting transfers between devices, body(): lax.ppermute(picked, 'grp', [(g, (g + k) % groups) for g in range(groups)])  9.62 us
    ppermute x6, waiting for transfers between devices, body(): lax.ppermute(picked, 'grp', [(g, (g + k) % groups) for g in range(groups)])  6.95 us
    ppermute x6, waiting for transfers between devices, core_permute(): return lax.ppermute(block, 'mem', [(m, m ^ 1) for m in range(size)])  1.56 us
  transfers between devices with their start and end apart: 24, of which 14 were waited for; matrix products, arithmetic and copies ran while one was open for 0% of the time, Pallas kernels for 18%

profile of v4, /device:TPU:0, one launch (start us, length us, event | category | flops | bytes accessed | tf_op | source)
XLA Modules:
  0.0 68.1 jit_solution(13498898453635858771)
XLA Ops:
  2.9 1.2 %collective-permute-done.refs_1_ = bf16[64,2048]{1,0:T(8,128)(2,1)S(1)} collective-permute-done((bf16[64,2048]{1,0:T(8,128)(2,1)S(1)}, bf16[64,2048]{1,0:T(8,128)(2,1)S(1)}, u32[]{:S(2)}, u32[]{:S(2)}) %collective-permute-start) | collective-permute-done | bytes 262176 | tf_op jit(solution)/shard_map/ppermute | solution.py:31
  4.1 2.9 %collective-permute-start.1 = (bf16[128,1024]{1,0:T(8,128)(2,1)S(1)}, bf16[128,1024]{1,0:T(8,128)(2,1)S(1)}, u32[]{:S(2)}, u32[]{:S(2)}) collective-permute-start(bf16[128,1024]{1,0:T(8,128)(2,1)S(1)} %join.6.refs_1_), channel_id=1, source_target_pairs={{0,2},{1,5},{2,0},{3,7},{4,6},{5,1},{6,4},{7,3},{8,10},{9,13},{10,... | collective-permute-start | bytes 786440 | tf_op jit(solution)/shard_map/ppermute | solution.py:27
  7.0 1.5 %collective-permute-start.2 = (bf16[128,1024]{1,0:T(8,128)(2,1)S(1)}, bf16[128,1024]{1,0:T(8,128)(2,1)S(1)}, u32[]{:S(2)}, u32[]{:S(2)}) collective-permute-start(bf16[128,1024]{1,0:T(8,128)(2,1)S(1)} %join.6.refs_1_), channel_id=1, source_target_pairs={{0,4},{1,3},{2,6},{3,1},{4,0},{5,7},{6,2},{7,5},{8,12},{9,11},{10,... | collective-permute-start | bytes 786440 | tf_op jit(solution)/shard_map/ppermute | solution.py:27
  8.6 4.0 %load.1 = (bf16[1024,4096]{1,0:T(8,128)(2,1)S(1)}, f32[1,1024]{1,0:T(1,128)S(1)}) custom-call(bf16[1024,4096]{1,0:T(8,128)(2,1)} %refs_0_.3), custom_call_target="tpu_custom_call" | custom-call | bytes 16781312 | tf_op jit(solution)/shard_map/load/pallas_call | solution.py:66
  13.7 2.3 %collective-permute-start.4 = (bf16[128,1024]{1,0:T(8,128)(2,1)S(1)}, bf16[128,1024]{1,0:T(8,128)(2,1)S(1)}, u32[]{:S(2)}, u32[]{:S(2)}) collective-permute-start(bf16[128,1024]{1,0:T(8,128)(2,1)S(1)} %join.7.refs_1_), channel_id=1, source_target_pairs={{0,2},{1,5},{2,0},{3,7},{4,6},{5,1},{6,4},{7,3},{8,10},{9,13},{10,... | collective-permute-start | bytes 786440 | tf_op jit(solution)/shard_map/ppermute | solution.py:27
  16.0 1.2 %collective-permute-start.3 = (bf16[128,1024]{1,0:T(8,128)(2,1)S(1)}, bf16[128,1024]{1,0:T(8,128)(2,1)S(1)}, u32[]{:S(2)}, u32[]{:S(2)}) collective-permute-start(bf16[128,1024]{1,0:T(8,128)(2,1)S(1)} %collective-permute-done.1.refs_2_), channel_id=1, source_target_pairs={{0,4},{1,3},{2,6},{3,1},{4,0},{5,7},{6,2},{7,5},{8,12},{9,11},{10,... | collective-permute-start | bytes 786440 | tf_op jit(solution)/shard_map/ppermute | solution.py:27
  18.0 5.1 %collective-permute-done.4.refs_2_ = bf16[128,1024]{1,0:T(8,128)(2,1)S(1)} collective-permute-done((bf16[128,1024]{1,0:T(8,128)(2,1)S(1)}, bf16[128,1024]{1,0:T(8,128)(2,1)S(1)}, u32[]{:S(2)}, u32[]{:S(2)}) %collective-permute-start.4) | collective-permute-done | bytes 262176 | tf_op jit(solution)/shard_map/ppermute | solution.py:27
  23.1 1.5 %collective-permute-start.6 = (bf16[128,1024]{1,0:T(8,128)(2,1)S(1)}, bf16[128,1024]{1,0:T(8,128)(2,1)S(1)}, u32[]{:S(2)}, u32[]{:S(2)}) collective-permute-start(bf16[128,1024]{1,0:T(8,128)(2,1)S(1)} %collective-permute-done.4.refs_2_), channel_id=1, source_target_pairs={{0,4},{1,3},{2,6},{3,1},{4,0},{5,7},{6,2},{7,5},{8,12},{9,11},{10,... | collective-permute-start | bytes 786440 | tf_op jit(solution)/shard_map/ppermute | solution.py:27
  24.7 1.1 %pick_first.1 = (bf16[32,1024]{1,0:T(8,128)(2,1)S(1)}, bf16[192,1024]{1,0:T(8,128)(2,1)S(1)}, bf16[224,512]{1,0:T(8,128)(2,1)S(1)}) custom-call(s32[1,128]{1,0:T(1,128)S(1)} %copy-done.1, bf16[128,1024]{1,0:T(8,128)(2,1)S(1)} %join.6.refs_1_, bf16[128,1024]{1,0:T(8,128)(2,1)S(1)} %collective-permute-done.1.refs_2_, ...), custom_call_target="tpu_custom_call" | custom-call | flops 234881024 | bytes 1737216 | tf_op jit(solution)/shard_map/pick_first/pallas_call | solution.py:66
  25.8 1.9 %collective-permute-start.7 = (bf16[32,1024]{1,0:T(8,128)(2,1)S(1)}, bf16[32,1024]{1,0:T(8,128)(2,1)S(1)}, u32[]{:S(2)}, u32[]{:S(2)}) collective-permute-start(bf16[32,1024]{1,0:T(8,128)(2,1)S(1)} %get-tuple-element.19), channel_id=1, source_target_pairs={{0,8},{8,16},{16,24},{24,0},{1,9},{9,17},{17,25},{25,1},{2,10},{10... | collective-permute-start | bytes 196616 | tf_op jit(solution)/shard_map/ppermute | solution.py:313
  27.7 2.6 %collective-permute-start.8 = (bf16[32,1024]{1,0:T(8,128)(2,1)S(1)}, bf16[32,1024]{1,0:T(8,128)(2,1)S(1)}, u32[]{:S(2)}, u32[]{:S(2)}) collective-permute-start(bf16[32,1024]{1,0:T(8,128)(2,1)S(1)} %get-tuple-element.19), channel_id=1, source_target_pairs={{0,16},{8,24},{16,0},{24,8},{1,17},{9,25},{17,1},{25,9},{2,18},{10... | collective-permute-start | bytes 196616 | tf_op jit(solution)/shard_map/ppermute | solution.py:313
  30.3 1.3 %collective-permute-start.9 = (bf16[32,1024]{1,0:T(8,128)(2,1)S(1)}, bf16[32,1024]{1,0:T(8,128)(2,1)S(1)}, u32[]{:S(2)}, u32[]{:S(2)}) collective-permute-start(bf16[32,1024]{1,0:T(8,128)(2,1)S(1)} %get-tuple-element.19), channel_id=1, source_target_pairs={{0,24},{8,0},{16,8},{24,16},{1,25},{9,1},{17,9},{25,17},{2,26},{10... | collective-permute-start | bytes 196616 | tf_op jit(solution)/shard_map/ppermute | solution.py:313
  33.1 1.5 %collective-permute-done.9.refs_7_.refs_2_ = bf16[32,1024]{1,0:T(8,128)(2,1)S(1)} collective-permute-done((bf16[32,1024]{1,0:T(8,128)(2,1)S(1)}, bf16[32,1024]{1,0:T(8,128)(2,1)S(1)}, u32[]{:S(2)}, u32[]{:S(2)}) %collective-permute-start.9) | collective-permute-done | bytes 65568 | tf_op jit(solution)/shard_map/ppermute | solution.py:313
  35.5 1.6 %collective-permute-start.13 = (bf16[96,1024]{1,0:T(8,128)(2,1)S(1)}, bf16[96,1024]{1,0:T(8,128)(2,1)S(1)}, u32[]{:S(2)}, u32[]{:S(2)}) collective-permute-start(bf16[96,1024]{1,0:T(8,128)(2,1)S(1)} %join.8.refs_0_.refs_1_), channel_id=1, source_target_pairs={{0,2},{1,5},{2,0},{3,7},{4,6},{5,1},{6,4},{7,3},{8,10},{9,13},{10,... | collective-permute-start | bytes 589832 | tf_op jit(solution)/shard_map/ppermute | solution.py:27
  37.0 1.1 %collective-permute-start.14 = (bf16[96,1024]{1,0:T(8,128)(2,1)S(1)}, bf16[96,1024]{1,0:T(8,128)(2,1)S(1)}, u32[]{:S(2)}, u32[]{:S(2)}) collective-permute-start(bf16[96,1024]{1,0:T(8,128)(2,1)S(1)} %join.8.refs_0_.refs_1_), channel_id=1, source_target_pairs={{0,4},{1,3},{2,6},{3,1},{4,0},{5,7},{6,2},{7,5},{8,12},{9,11},{10,... | collective-permute-start | bytes 589832 | tf_op jit(solution)/shard_map/ppermute | solution.py:27
  38.7 2.8 %collective-permute-start.11 = (bf16[32,1024]{1,0:T(8,128)(2,1)S(1)}, bf16[32,1024]{1,0:T(8,128)(2,1)S(1)}, u32[]{:S(2)}, u32[]{:S(2)}) collective-permute-start(bf16[32,1024]{1,0:T(8,128)(2,1)S(1)} %get-tuple-element.21.refs_3_), channel_id=1, source_target_pairs={{0,16},{8,24},{16,0},{24,8},{1,17},{9,25},{17,1},{25,9},{2,18},{10... | collective-permute-start | bytes 196616 | tf_op jit(solution)/shard_map/ppermute | solution.py:313
  41.9 2.3 %collective-permute-done.10.refs_2_.refs_0_ = bf16[32,1024]{1,0:T(8,128)(2,1)S(1)} collective-permute-done((bf16[32,1024]{1,0:T(8,128)(2,1)S(1)}, bf16[32,1024]{1,0:T(8,128)(2,1)S(1)}, u32[]{:S(2)}, u32[]{:S(2)}) %collective-permute-start.10) | collective-permute-done | bytes 65568 | tf_op jit(solution)/shard_map/ppermute | solution.py:313
  46.7 1.1 %collective-permute-start.20 = (bf16[96,1024]{1,0:T(8,128)(2,1)S(1)}, bf16[96,1024]{1,0:T(8,128)(2,1)S(1)}, u32[]{:S(2)}, u32[]{:S(2)}) collective-permute-start(bf16[96,1024]{1,0:T(8,128)(2,1)S(1)} %join.10.refs_0_.refs_4_), channel_id=1, source_target_pairs={{0,4},{1,3},{2,6},{3,1},{4,0},{5,7},{6,2},{7,5},{8,12},{9,11},{10,... | collective-permute-start | bytes 589832 | tf_op jit(solution)/shard_map/ppermute | solution.py:27
  48.4 4.4 %group.1 = (f32[1,1024]{1,0:T(1,128)}, f32[1,1024]{1,0:T(1,128)S(1)}) custom-call(bf16[1024,4096]{1,0:T(8,128)(2,1)S(1)} %get-tuple-element.13.refs_0_, f32[1,1024]{1,0:T(1,128)S(1)} %get-tuple-element.14.refs_4_.refs_1_.refs_2_, s32[1,128]{1,0:T(1,128)S(1)} %copy-done.1, bf16[192,2048]{1,0:T(8,128)(2,1)S(1)} %beside.1.refs_3_, ...), custom_call_target="tpu_custom_call" | custom-call | flops 1610612736 | bytes 9974272 | tf_op jit(solution)/shard_map/group/pallas_call | solution.py:66
  53.9 1.3 %collective-permute-start.16 = (bf16[96,1024]{1,0:T(8,128)(2,1)S(1)}, bf16[96,1024]{1,0:T(8,128)(2,1)S(1)}, u32[]{:S(2)}, u32[]{:S(2)}) collective-permute-start(bf16[96,1024]{1,0:T(8,128)(2,1)S(1)} %collective-permute-done.13.refs_5_.refs_1_.refs_2_), channel_id=1, source_target_pairs={{0,4},{1,3},{2,6},{3,1},{4,0},{5,7},{6,2},{7,5},{8,12},{9,11},{10,... | collective-permute-start | bytes 589832 | tf_op jit(solution)/shard_map/ppermute | solution.py:27
  55.9 3.6 %collective-permute-done.16.refs_4_ = bf16[96,1024]{1,0:T(8,128)(2,1)S(1)} collective-permute-done((bf16[96,1024]{1,0:T(8,128)(2,1)S(1)}, bf16[96,1024]{1,0:T(8,128)(2,1)S(1)}, u32[]{:S(2)}, u32[]{:S(2)}) %collective-permute-start.16) | collective-permute-done | bytes 196640 | tf_op jit(solution)/shard_map/ppermute | solution.py:27
  59.6 2.1 %collective-permute-done.21.refs_7_ = bf16[96,1024]{1,0:T(8,128)(2,1)S(1)} collective-permute-done((bf16[96,1024]{1,0:T(8,128)(2,1)S(1)}, bf16[96,1024]{1,0:T(8,128)(2,1)S(1)}, u32[]{:S(2)}, u32[]{:S(2)}) %collective-permute-start.21) | collective-permute-done | bytes 196640 | tf_op jit(solution)/shard_map/ppermute | solution.py:27
  61.7 2.9 %far.1.refs_3_ = f32[384,1024]{1,0:T(8,128)S(1)} custom-call(bf16[1024,4096]{1,0:T(8,128)(2,1)S(1)} %get-tuple-element.13.refs_0_, bf16[96,1024]{1,0:T(8,128)(2,1)S(1)} %join.8.refs_0_.refs_1_, bf16[96,1024]{1,0:T(8,128)(2,1)S(1)} %collective-permute-done.13.refs_5_.refs_1_.refs_2_, bf16[96,1024]{1,0:T(8,128)(2,1)S(1)} %collective-permute-done.14.refs_6_.refs_2_.refs_3_, ...), custom_call_target="tpu_custom_call" | custom-call | flops 1610612736 | bytes 11534336 | tf_op jit(solution)/shard_map/far/pallas_call | solution.py:66
  64.6 3.5 %far_last.1 = f32[1,1024]{1,0:T(1,128)} custom-call(bf16[1024,4096]{1,0:T(8,128)(2,1)S(1)} %get-tuple-element.13.refs_0_, f32[1,1024]{1,0:T(1,128)S(1)} %get-tuple-element.23.refs_3_.refs_1_, f32[1,1024]{1,0:T(1,128)S(1)} %get-tuple-element.14.refs_4_.refs_1_.refs_2_, f32[384,1024]{1,0:T(8,128)S(1)} %far.1.refs_3_, ...), custom_call_target="tpu_custom_call" | custom-call | flops 1610612736 | bytes 11546624 | tf_op jit(solution)/shard_map/far_last/pallas_call | solution.py:66
  (42 shorter events, 11.7 us)
Async XLA Ops:
  2.4 1.7 %collective-permute-start = (bf16[64,2048]{1,0:T(8,128)(2,1)S(1)}, bf16[64,2048]{1,0:T(8,128)(2,1)S(1)}, u32[]{:S(2)}, u32[]{:S(2)}) collective-permute-start(bf16[64,2048]{1,0:T(8,128)(2,1)S(1)} %get-tuple-element.16), channel_id=1, source_target_pairs={{0,1},{1,0},{2,3},{3,2},{4,5},{5,4},{6,7},{7,6},{8,9},{9,8},{10,11... | collective-permute-start | bytes 786440 | tf_op jit(solution)/shard_map/ppermute | solution.py:31
  4.1 9.3 %collective-permute-start.1 = (bf16[128,1024]{1,0:T(8,128)(2,1)S(1)}, bf16[128,1024]{1,0:T(8,128)(2,1)S(1)}, u32[]{:S(2)}, u32[]{:S(2)}) collective-permute-start(bf16[128,1024]{1,0:T(8,128)(2,1)S(1)} %join.6.refs_1_), channel_id=1, source_target_pairs={{0,2},{1,5},{2,0},{3,7},{4,6},{5,1},{6,4},{7,3},{8,10},{9,13},{10,... | collective-permute-start | bytes 786440 | tf_op jit(solution)/shard_map/ppermute | solution.py:27
  7.0 6.6 %collective-permute-start.2 = (bf16[128,1024]{1,0:T(8,128)(2,1)S(1)}, bf16[128,1024]{1,0:T(8,128)(2,1)S(1)}, u32[]{:S(2)}, u32[]{:S(2)}) collective-permute-start(bf16[128,1024]{1,0:T(8,128)(2,1)S(1)} %join.6.refs_1_), channel_id=1, source_target_pairs={{0,4},{1,3},{2,6},{3,1},{4,0},{5,7},{6,2},{7,5},{8,12},{9,11},{10,... | collective-permute-start | bytes 786440 | tf_op jit(solution)/shard_map/ppermute | solution.py:27
  13.7 9.4 %collective-permute-start.4 = (bf16[128,1024]{1,0:T(8,128)(2,1)S(1)}, bf16[128,1024]{1,0:T(8,128)(2,1)S(1)}, u32[]{:S(2)}, u32[]{:S(2)}) collective-permute-start(bf16[128,1024]{1,0:T(8,128)(2,1)S(1)} %join.7.refs_1_), channel_id=1, source_target_pairs={{0,2},{1,5},{2,0},{3,7},{4,6},{5,1},{6,4},{7,3},{8,10},{9,13},{10,... | collective-permute-start | bytes 786440 | tf_op jit(solution)/shard_map/ppermute | solution.py:27
  16.0 8.7 %collective-permute-start.3 = (bf16[128,1024]{1,0:T(8,128)(2,1)S(1)}, bf16[128,1024]{1,0:T(8,128)(2,1)S(1)}, u32[]{:S(2)}, u32[]{:S(2)}) collective-permute-start(bf16[128,1024]{1,0:T(8,128)(2,1)S(1)} %collective-permute-done.1.refs_2_), channel_id=1, source_target_pairs={{0,4},{1,3},{2,6},{3,1},{4,0},{5,7},{6,2},{7,5},{8,12},{9,11},{10,... | collective-permute-start | bytes 786440 | tf_op jit(solution)/shard_map/ppermute | solution.py:27
  17.2 14.4 %collective-permute-start.5 = (bf16[128,1024]{1,0:T(8,128)(2,1)S(1)}, bf16[128,1024]{1,0:T(8,128)(2,1)S(1)}, u32[]{:S(2)}, u32[]{:S(2)}) collective-permute-start(bf16[128,1024]{1,0:T(8,128)(2,1)S(1)} %join.7.refs_1_), channel_id=1, source_target_pairs={{0,4},{1,3},{2,6},{3,1},{4,0},{5,7},{6,2},{7,5},{8,12},{9,11},{10,... | collective-permute-start | bytes 786440 | tf_op jit(solution)/shard_map/ppermute | solution.py:27
  23.1 11.4 %collective-permute-start.6 = (bf16[128,1024]{1,0:T(8,128)(2,1)S(1)}, bf16[128,1024]{1,0:T(8,128)(2,1)S(1)}, u32[]{:S(2)}, u32[]{:S(2)}) collective-permute-start(bf16[128,1024]{1,0:T(8,128)(2,1)S(1)} %collective-permute-done.4.refs_2_), channel_id=1, source_target_pairs={{0,4},{1,3},{2,6},{3,1},{4,0},{5,7},{6,2},{7,5},{8,12},{9,11},{10,... | collective-permute-start | bytes 786440 | tf_op jit(solution)/shard_map/ppermute | solution.py:27
  25.8 6.3 %collective-permute-start.7 = (bf16[32,1024]{1,0:T(8,128)(2,1)S(1)}, bf16[32,1024]{1,0:T(8,128)(2,1)S(1)}, u32[]{:S(2)}, u32[]{:S(2)}) collective-permute-start(bf16[32,1024]{1,0:T(8,128)(2,1)S(1)} %get-tuple-element.19), channel_id=1, source_target_pairs={{0,8},{8,16},{16,24},{24,0},{1,9},{9,17},{17,25},{25,1},{2,10},{10... | collective-permute-start | bytes 196616 | tf_op jit(solution)/shard_map/ppermute | solution.py:313
  27.7 5.4 %collective-permute-start.8 = (bf16[32,1024]{1,0:T(8,128)(2,1)S(1)}, bf16[32,1024]{1,0:T(8,128)(2,1)S(1)}, u32[]{:S(2)}, u32[]{:S(2)}) collective-permute-start(bf16[32,1024]{1,0:T(8,128)(2,1)S(1)} %get-tuple-element.19), channel_id=1, source_target_pairs={{0,16},{8,24},{16,0},{24,8},{1,17},{9,25},{17,1},{25,9},{2,18},{10... | collective-permute-start | bytes 196616 | tf_op jit(solution)/shard_map/ppermute | solution.py:313
  30.3 4.3 %collective-permute-start.9 = (bf16[32,1024]{1,0:T(8,128)(2,1)S(1)}, bf16[32,1024]{1,0:T(8,128)(2,1)S(1)}, u32[]{:S(2)}, u32[]{:S(2)}) collective-permute-start(bf16[32,1024]{1,0:T(8,128)(2,1)S(1)} %get-tuple-element.19), channel_id=1, source_target_pairs={{0,24},{8,0},{16,8},{24,16},{1,25},{9,1},{17,9},{25,17},{2,26},{10... | collective-permute-start | bytes 196616 | tf_op jit(solution)/shard_map/ppermute | solution.py:313
  35.5 10.5 %collective-permute-start.13 = (bf16[96,1024]{1,0:T(8,128)(2,1)S(1)}, bf16[96,1024]{1,0:T(8,128)(2,1)S(1)}, u32[]{:S(2)}, u32[]{:S(2)}) collective-permute-start(bf16[96,1024]{1,0:T(8,128)(2,1)S(1)} %join.8.refs_0_.refs_1_), channel_id=1, source_target_pairs={{0,2},{1,5},{2,0},{3,7},{4,6},{5,1},{6,4},{7,3},{8,10},{9,13},{10,... | collective-permute-start | bytes 589832 | tf_op jit(solution)/shard_map/ppermute | solution.py:27
  37.0 9.0 %collective-permute-start.14 = (bf16[96,1024]{1,0:T(8,128)(2,1)S(1)}, bf16[96,1024]{1,0:T(8,128)(2,1)S(1)}, u32[]{:S(2)}, u32[]{:S(2)}) collective-permute-start(bf16[96,1024]{1,0:T(8,128)(2,1)S(1)} %join.8.refs_0_.refs_1_), channel_id=1, source_target_pairs={{0,4},{1,3},{2,6},{3,1},{4,0},{5,7},{6,2},{7,5},{8,12},{9,11},{10,... | collective-permute-start | bytes 589832 | tf_op jit(solution)/shard_map/ppermute | solution.py:27
  38.1 6.2 %collective-permute-start.10 = (bf16[32,1024]{1,0:T(8,128)(2,1)S(1)}, bf16[32,1024]{1,0:T(8,128)(2,1)S(1)}, u32[]{:S(2)}, u32[]{:S(2)}) collective-permute-start(bf16[32,1024]{1,0:T(8,128)(2,1)S(1)} %get-tuple-element.21.refs_3_), channel_id=1, source_target_pairs={{0,8},{8,16},{16,24},{24,0},{1,9},{9,17},{17,25},{25,1},{2,10},{10... | collective-permute-start | bytes 196616 | tf_op jit(solution)/shard_map/ppermute | solution.py:313
  38.7 6.6 %collective-permute-start.11 = (bf16[32,1024]{1,0:T(8,128)(2,1)S(1)}, bf16[32,1024]{1,0:T(8,128)(2,1)S(1)}, u32[]{:S(2)}, u32[]{:S(2)}) collective-permute-start(bf16[32,1024]{1,0:T(8,128)(2,1)S(1)} %get-tuple-element.21.refs_3_), channel_id=1, source_target_pairs={{0,16},{8,24},{16,0},{24,8},{1,17},{9,25},{17,1},{25,9},{2,18},{10... | collective-permute-start | bytes 196616 | tf_op jit(solution)/shard_map/ppermute | solution.py:313
  41.5 4.5 %collective-permute-start.12 = (bf16[32,1024]{1,0:T(8,128)(2,1)S(1)}, bf16[32,1024]{1,0:T(8,128)(2,1)S(1)}, u32[]{:S(2)}, u32[]{:S(2)}) collective-permute-start(bf16[32,1024]{1,0:T(8,128)(2,1)S(1)} %get-tuple-element.21.refs_3_), channel_id=1, source_target_pairs={{0,24},{8,0},{16,8},{24,16},{1,25},{9,1},{17,9},{25,17},{2,26},{10... | collective-permute-start | bytes 196616 | tf_op jit(solution)/shard_map/ppermute | solution.py:313
  46.0 2.4 %collective-permute-start.15 = (bf16[192,2048]{1,0:T(8,128)(2,1)S(1)}, bf16[192,2048]{1,0:T(8,128)(2,1)S(1)}, u32[]{:S(2)}, u32[]{:S(2)}) collective-permute-start(bf16[192,2048]{1,0:T(8,128)(2,1)S(1)} %beside.1.refs_3_), channel_id=1, source_target_pairs={{0,1},{1,0},{2,3},{3,2},{4,5},{5,4},{6,7},{7,6},{8,9},{9,8},{10,11... | collective-permute-start | bytes 2359304 | tf_op jit(solution)/shard_map/ppermute | solution.py:31
  46.1 7.5 %collective-permute-start.19 = (bf16[96,1024]{1,0:T(8,128)(2,1)S(1)}, bf16[96,1024]{1,0:T(8,128)(2,1)S(1)}, u32[]{:S(2)}, u32[]{:S(2)}) collective-permute-start(bf16[96,1024]{1,0:T(8,128)(2,1)S(1)} %join.10.refs_0_.refs_4_), channel_id=1, source_target_pairs={{0,2},{1,5},{2,0},{3,7},{4,6},{5,1},{6,4},{7,3},{8,10},{9,13},{10,... | collective-permute-start | bytes 589832 | tf_op jit(solution)/shard_map/ppermute | solution.py:27
  46.7 6.9 %collective-permute-start.20 = (bf16[96,1024]{1,0:T(8,128)(2,1)S(1)}, bf16[96,1024]{1,0:T(8,128)(2,1)S(1)}, u32[]{:S(2)}, u32[]{:S(2)}) collective-permute-start(bf16[96,1024]{1,0:T(8,128)(2,1)S(1)} %join.10.refs_0_.refs_4_), channel_id=1, source_target_pairs={{0,4},{1,3},{2,6},{3,1},{4,0},{5,7},{6,2},{7,5},{8,12},{9,11},{10,... | collective-permute-start | bytes 589832 | tf_op jit(solution)/shard_map/ppermute | solution.py:27
  47.9 13.8 %collective-permute-start.17 = (bf16[288,1024]{1,0:T(8,128)(2,1)S(1)}, bf16[288,1024]{1,0:T(8,128)(2,1)S(1)}, u32[]{:S(2)}, u32[]{:S(2)}) collective-permute-start(bf16[288,1024]{1,0:T(8,128)(2,1)S(1)} %join.9), channel_id=1, source_target_pairs={{0,1},{1,0},{2,3},{3,2},{4,5},{5,4},{6,7},{7,6},{8,9},{9,8},{10,11... | collective-permute-start | bytes 1769480 | tf_op jit(solution)/shard_map/ppermute | solution.py:31
  53.7 10.9 %collective-permute-start.22 = (bf16[288,1024]{1,0:T(8,128)(2,1)S(1)}, bf16[288,1024]{1,0:T(8,128)(2,1)S(1)}, u32[]{:S(2)}, u32[]{:S(2)}) collective-permute-start(bf16[288,1024]{1,0:T(8,128)(2,1)S(1)} %join.11), channel_id=1, source_target_pairs={{0,1},{1,0},{2,3},{3,2},{4,5},{5,4},{6,7},{7,6},{8,9},{9,8},{10,11... | collective-permute-start | bytes 1769480 | tf_op jit(solution)/shard_map/ppermute | solution.py:31
  53.9 5.7 %collective-permute-start.16 = (bf16[96,1024]{1,0:T(8,128)(2,1)S(1)}, bf16[96,1024]{1,0:T(8,128)(2,1)S(1)}, u32[]{:S(2)}, u32[]{:S(2)}) collective-permute-start(bf16[96,1024]{1,0:T(8,128)(2,1)S(1)} %collective-permute-done.13.refs_5_.refs_1_.refs_2_), channel_id=1, source_target_pairs={{0,4},{1,3},{2,6},{3,1},{4,0},{5,7},{6,2},{7,5},{8,12},{9,11},{10,... | collective-permute-start | bytes 589832 | tf_op jit(solution)/shard_map/ppermute | solution.py:27
  55.2 6.5 %collective-permute-start.21 = (bf16[96,1024]{1,0:T(8,128)(2,1)S(1)}, bf16[96,1024]{1,0:T(8,128)(2,1)S(1)}, u32[]{:S(2)}, u32[]{:S(2)}) collective-permute-start(bf16[96,1024]{1,0:T(8,128)(2,1)S(1)} %collective-permute-done.19.refs_1_.refs_5_), channel_id=1, source_target_pairs={{0,4},{1,3},{2,6},{3,1},{4,0},{5,7},{6,2},{7,5},{8,12},{9,11},{10,... | collective-permute-start | bytes 589832 | tf_op jit(solution)/shard_map/ppermute | solution.py:27
  59.6 2.1 %collective-permute-start.18 = (bf16[96,1024]{1,0:T(8,128)(2,1)S(1)}, bf16[96,1024]{1,0:T(8,128)(2,1)S(1)}, u32[]{:S(2)}, u32[]{:S(2)}) collective-permute-start(bf16[96,1024]{1,0:T(8,128)(2,1)S(1)} %collective-permute-done.16.refs_4_), channel_id=1, source_target_pairs={{0,1},{1,0},{2,3},{3,2},{4,5},{5,4},{6,7},{7,6},{8,9},{9,8},{10,11... | collective-permute-start | bytes 589832 | tf_op jit(solution)/shard_map/ppermute | solution.py:31
  61.7 2.9 %collective-permute-start.23 = (bf16[96,1024]{1,0:T(8,128)(2,1)S(1)}, bf16[96,1024]{1,0:T(8,128)(2,1)S(1)}, u32[]{:S(2)}, u32[]{:S(2)}) collective-permute-start(bf16[96,1024]{1,0:T(8,128)(2,1)S(1)} %collective-permute-done.21.refs_7_), channel_id=1, source_target_pairs={{0,1},{1,0},{2,3},{3,2},{4,5},{5,4},{6,7},{7,6},{8,9},{9,8},{10,11... | collective-permute-start | bytes 589832 | tf_op jit(solution)/shard_map/ppermute | solution.py:31
  (2 other events, 25.1 us)

commit v5 on v4

--- a/solution.py
+++ b/solution.py
@@ -7,7 +7,7 @@
 from jax.experimental.pallas import tpu as pltpu
 from jax.sharding import PartitionSpec as P
 
-CHUNKS = 2
+CHUNKS = 1
 TILE = 256
 MARK = 2.0
 MIB = 1024 * 1024
@@ -301,7 +301,7 @@
         if c == 0:
             picked, found, select = call(
                 functools.partial(first_pick_kernel, size), "pick_first",
-                outs + [bf16(share + live, size * slots)], (chosen, *raw[c]), flops,
+                outs + [bf16(share + live, size * slots)], (chosen, *raw[c]), flops, after=(norm,),
             )
         else:
             picked, found = call(
@@ -318,15 +318,17 @@
     far, held = [], ()
     for c in range(CHUNKS):
         if c == CHUNKS - 1:
-            own = call(
-                beside_kernel, "beside", bf16(live, half), dense, after=(*shifted[c], *held[1:3])
-            )
+            own = dense[0]
+            if c:
+                after = (*shifted[c], *held[1:3])
+                own = call(beside_kernel, "beside", bf16(live, half), dense, after=after)
             near, best = call(
                 functools.partial(group_kernel, picks), "group", [line] * 2,
                 (cand, norm, chosen, own, core_permute(own, size)), 2 * rows * live * width,
                 scratch=[pltpu.VMEM((live, width), BF16), pltpu.VMEM((live, 1), F32)],
             )
-        held = gather_chips(join(shifted[c], part, after=() if c else (picked,)), size)
+        after = (best,) if CHUNKS == 1 else () if c else (picked,)
+        held = gather_chips(join(shifted[c], part, after=after), size)
         early = join(held[:-1], part, after=(best,) if c == CHUNKS - 1 else ())
         far.append((*held, core_permute(early, size), core_permute(held[-1], size)))
 

time: 68.4 us -> 73.3 us (1.072)
  waiting for transfers between devices: 21.3 us -> 36.2 us
  starting transfers between devices: 27.2 us -> 17.2 us
    ppermute x12 -> x6, waiting for transfers between devices: 12.8 us -> 29.9 us  [mixed_permute(): lax.ppermute(block, 'mem', [(m, m ^ (odd if m & 1 else even)) for m in ra...]
    ppermute x12 -> x6, starting transfers between devices: 16.7 us -> 10.1 us  [mixed_permute(): lax.ppermute(block, 'mem', [(m, m ^ (odd if m & 1 else even)) for m in ra...]
    ppermute x6 -> x3, waiting for transfers between devices: 6.95 us -> 3.5 us  [body(): lax.ppermute(picked, 'grp', [(g, (g + k) % groups) for g in range(groups)])]
    ppermute x6 -> x3, starting transfers between devices: 9.62 us -> 6.44 us  [body(): lax.ppermute(picked, 'grp', [(g, (g + k) % groups) for g in range(groups)])]
    ppermute x6 -> x4, waiting for transfers between devices: 1.56 us -> 2.89 us  [core_permute(): return lax.ppermute(block, 'mem', [(m, m ^ 1) for m in range(size)])]
    pallas_call x14 -> x8, Pallas kernels: 17.2 us -> 16.6 us  [call(): pl.pallas_call(run, out_shape=out_shape, in_specs=(specs or vmem_specs(co...]
  transfers between devices with their start and end apart: 24 -> 13, of which waited for: 14 -> 7; matrix products, arithmetic and copies ran while one was open for 0% -> 0% of each run, Pallas kernels for 18% -> 12%
where the time goes in v5:
time: 73.3 us; the launch traced here: 72.5 us
  waiting for transfers between devices  36.2 us (49%)
  starting transfers between devices  17.2 us (23%)
  Pallas kernels  16.6 us (23%)
  between operations  1.36 us (2%)
  local copies, waits for them, and re-layouts  1.04 us (1%)
    ppermute x6, waiting for transfers between devices, mixed_permute(): lax.ppermute(block, 'mem', [(m, m ^ (odd if m & 1 else even)) for m in ra...  29.9 us
    pallas_call x8, Pallas kernels, call(): pl.pallas_call(run, out_shape=out_shape, in_specs=(specs or vmem_specs(co...  16.6 us
    ppermute x6, starting transfers between devices, mixed_permute(): lax.ppermute(block, 'mem', [(m, m ^ (odd if m & 1 else even)) for m in ra...  10.1 us
    ppermute x3, starting transfers between devices, body(): lax.ppermute(picked, 'grp', [(g, (g + k) % groups) for g in range(groups)])  6.44 us
    ppermute x3, waiting for transfers between devices, body(): lax.ppermute(picked, 'grp', [(g, (g + k) % groups) for g in range(groups)])  3.5 us
    ppermute x4, waiting for transfers between devices, core_permute(): return lax.ppermute(block, 'mem', [(m, m ^ 1) for m in range(size)])  2.89 us
  transfers between devices with their start and end apart: 13, of which 7 were waited for; matrix products, arithmetic and copies ran while one was open for 0% of the time, Pallas kernels for 12%

profile of v5, /device:TPU:0, one launch (start us, length us, event | category | flops | bytes accessed | tf_op | source)
XLA Modules:
  0.0 72.5 jit_solution(5880356269611263051)
XLA Ops:
  1.3 1.0 %copy-done = bf16[64,4096]{1,0:T(8,128)(2,1)S(1)} copy-done((bf16[64,4096]{1,0:T(8,128)(2,1)S(1)}, bf16[64,4096]{1,0:T(8,128)(2,1)}, u32[]{:S(2)}) %copy-start) | copy-done | bytes 524312
  2.4 0.5 collective-permute-start
  2.9 1.2 %collective-permute-done.refs_1_ = bf16[64,2048]{1,0:T(8,128)(2,1)S(1)} collective-permute-done((bf16[64,2048]{1,0:T(8,128)(2,1)S(1)}, bf16[64,2048]{1,0:T(8,128)(2,1)S(1)}, u32[]{:S(2)}, u32[]{:S(2)}) %collective-permute-start) | collective-permute-done | bytes 262176 | tf_op jit(solution)/shard_map/ppermute | solution.py:31
  4.1 2.9 %collective-permute-start.1 = (bf16[128,2048]{1,0:T(8,128)(2,1)S(1)}, bf16[128,2048]{1,0:T(8,128)(2,1)S(1)}, u32[]{:S(2)}, u32[]{:S(2)}) collective-permute-start(bf16[128,2048]{1,0:T(8,128)(2,1)S(1)} %join.3.refs_1_), channel_id=1, source_target_pairs={{0,2},{1,5},{2,0},{3,7},{4,6},{5,1},{6,4},{7,3},{8,10},{9,13},{10,... | collective-permute-start | bytes 1572872 | tf_op jit(solution)/shard_map/ppermute | solution.py:27
  7.0 1.5 %collective-permute-start.2 = (bf16[128,2048]{1,0:T(8,128)(2,1)S(1)}, bf16[128,2048]{1,0:T(8,128)(2,1)S(1)}, u32[]{:S(2)}, u32[]{:S(2)}) collective-permute-start(bf16[128,2048]{1,0:T(8,128)(2,1)S(1)} %join.3.refs_1_), channel_id=1, source_target_pairs={{0,4},{1,3},{2,6},{3,1},{4,0},{5,7},{6,2},{7,5},{8,12},{9,11},{10,... | collective-permute-start | bytes 1572872 | tf_op jit(solution)/shard_map/ppermute | solution.py:27
  8.6 10.5 %collective-permute-done.1.refs_2_ = bf16[128,2048]{1,0:T(8,128)(2,1)S(1)} collective-permute-done((bf16[128,2048]{1,0:T(8,128)(2,1)S(1)}, bf16[128,2048]{1,0:T(8,128)(2,1)S(1)}, u32[]{:S(2)}, u32[]{:S(2)}) %collective-permute-start.1) | collective-permute-done | bytes 524320 | tf_op jit(solution)/shard_map/ppermute | solution.py:27
  19.0 2.1 %collective-permute-start.3 = (bf16[128,2048]{1,0:T(8,128)(2,1)S(1)}, bf16[128,2048]{1,0:T(8,128)(2,1)S(1)}, u32[]{:S(2)}, u32[]{:S(2)}) collective-permute-start(bf16[128,2048]{1,0:T(8,128)(2,1)S(1)} %collective-permute-done.1.refs_2_), channel_id=1, source_target_pairs={{0,4},{1,3},{2,6},{3,1},{4,0},{5,7},{6,2},{7,5},{8,12},{9,11},{10,... | collective-permute-start | bytes 1572872 | tf_op jit(solution)/shard_map/ppermute | solution.py:27
  21.1 4.0 %load.1 = (bf16[1024,4096]{1,0:T(8,128)(2,1)S(1)}, f32[1,1024]{1,0:T(1,128)S(1)}) custom-call(bf16[1024,4096]{1,0:T(8,128)(2,1)} %refs_0_.3), custom_call_target="tpu_custom_call" | custom-call | bytes 16781312 | tf_op jit(solution)/shard_map/load/pallas_call | solution.py:66
  25.1 3.2 %collective-permute-done.3.refs_4_ = bf16[128,2048]{1,0:T(8,128)(2,1)S(1)} collective-permute-done((bf16[128,2048]{1,0:T(8,128)(2,1)S(1)}, bf16[128,2048]{1,0:T(8,128)(2,1)S(1)}, u32[]{:S(2)}, u32[]{:S(2)}) %collective-permute-start.3) | collective-permute-done | bytes 524320 | tf_op jit(solution)/shard_map/ppermute | solution.py:27
  28.3 2.5 %pick_first.1 = (bf16[32,2048]{1,0:T(8,128)(2,1)S(1)}, bf16[192,2048]{1,0:T(8,128)(2,1)S(1)}, bf16[224,512]{1,0:T(8,128)(2,1)}) custom-call(s32[1,128]{1,0:T(1,128)S(1)} %copy-done.1, bf16[128,2048]{1,0:T(8,128)(2,1)S(1)} %join.3.refs_1_, bf16[128,2048]{1,0:T(8,128)(2,1)S(1)} %collective-permute-done.1.refs_2_, ...), custom_call_target="tpu_custom_call" | custom-call | flops 469762048 | bytes 3244544 | tf_op jit(solution)/shard_map/pick_first/pallas_call | solution.py:66
  30.8 2.5 %collective-permute-start.5 = (bf16[32,2048]{1,0:T(8,128)(2,1)S(1)}, bf16[32,2048]{1,0:T(8,128)(2,1)S(1)}, u32[]{:S(2)}, u32[]{:S(2)}) collective-permute-start(bf16[32,2048]{1,0:T(8,128)(2,1)S(1)} %get-tuple-element.17), channel_id=1, source_target_pairs={{0,8},{8,16},{16,24},{24,0},{1,9},{9,17},{17,25},{25,1},{2,10},{10... | collective-permute-start | bytes 393224 | tf_op jit(solution)/shard_map/ppermute | solution.py:313
  33.3 2.6 %collective-permute-start.6 = (bf16[32,2048]{1,0:T(8,128)(2,1)S(1)}, bf16[32,2048]{1,0:T(8,128)(2,1)S(1)}, u32[]{:S(2)}, u32[]{:S(2)}) collective-permute-start(bf16[32,2048]{1,0:T(8,128)(2,1)S(1)} %get-tuple-element.17), channel_id=1, source_target_pairs={{0,16},{8,24},{16,0},{24,8},{1,17},{9,25},{17,1},{25,9},{2,18},{10... | collective-permute-start | bytes 393224 | tf_op jit(solution)/shard_map/ppermute | solution.py:313
  35.9 1.3 %collective-permute-start.7 = (bf16[32,2048]{1,0:T(8,128)(2,1)S(1)}, bf16[32,2048]{1,0:T(8,128)(2,1)S(1)}, u32[]{:S(2)}, u32[]{:S(2)}) collective-permute-start(bf16[32,2048]{1,0:T(8,128)(2,1)S(1)} %get-tuple-element.17), channel_id=1, source_target_pairs={{0,24},{8,0},{16,8},{24,16},{1,25},{9,1},{17,9},{25,17},{2,26},{10... | collective-permute-start | bytes 393224 | tf_op jit(solution)/shard_map/ppermute | solution.py:313
  37.3 4.4 %group.1 = (f32[1,1024]{1,0:T(1,128)}, f32[1,1024]{1,0:T(1,128)S(1)}) custom-call(bf16[1024,4096]{1,0:T(8,128)(2,1)S(1)} %get-tuple-element.10.refs_0_, f32[1,1024]{1,0:T(1,128)S(1)} %get-tuple-element.11.refs_5_.refs_1_.refs_2_, s32[1,128]{1,0:T(1,128)S(1)} %copy-done.1, bf16[192,2048]{1,0:T(8,128)(2,1)S(1)} %get-tuple-element.14.refs_3_, ...), custom_call_target="tpu_custom_call" | custom-call | flops 1610612736 | bytes 9974272 | tf_op jit(solution)/shard_map/group/pallas_call | solution.py:66
  41.7 3.5 %collective-permute-done.6.refs_1_ = bf16[32,2048]{1,0:T(8,128)(2,1)S(1)} collective-permute-done((bf16[32,2048]{1,0:T(8,128)(2,1)S(1)}, bf16[32,2048]{1,0:T(8,128)(2,1)S(1)}, u32[]{:S(2)}, u32[]{:S(2)}) %collective-permute-start.6) | collective-permute-done | bytes 131104 | tf_op jit(solution)/shard_map/ppermute | solution.py:313
  45.2 1.6 %collective-permute-start.8 = (bf16[96,2048]{1,0:T(8,128)(2,1)S(1)}, bf16[96,2048]{1,0:T(8,128)(2,1)S(1)}, u32[]{:S(2)}, u32[]{:S(2)}) collective-permute-start(bf16[96,2048]{1,0:T(8,128)(2,1)S(1)} %join.4.refs_0_.refs_3_), channel_id=1, source_target_pairs={{0,2},{1,5},{2,0},{3,7},{4,6},{5,1},{6,4},{7,3},{8,10},{9,13},{10,... | collective-permute-start | bytes 1179656 | tf_op jit(solution)/shard_map/ppermute | solution.py:27
  46.8 1.2 %collective-permute-start.9 = (bf16[96,2048]{1,0:T(8,128)(2,1)S(1)}, bf16[96,2048]{1,0:T(8,128)(2,1)S(1)}, u32[]{:S(2)}, u32[]{:S(2)}) collective-permute-start(bf16[96,2048]{1,0:T(8,128)(2,1)S(1)} %join.4.refs_0_.refs_3_), channel_id=1, source_target_pairs={{0,4},{1,3},{2,6},{3,1},{4,0},{5,7},{6,2},{7,5},{8,12},{9,11},{10,... | collective-permute-start | bytes 1179656 | tf_op jit(solution)/shard_map/ppermute | solution.py:27
  48.0 9.2 %collective-permute-done.8.refs_1_.refs_4_ = bf16[96,2048]{1,0:T(8,128)(2,1)S(1)} collective-permute-done((bf16[96,2048]{1,0:T(8,128)(2,1)S(1)}, bf16[96,2048]{1,0:T(8,128)(2,1)S(1)}, u32[]{:S(2)}, u32[]{:S(2)}) %collective-permute-start.8) | collective-permute-done | bytes 393248 | tf_op jit(solution)/shard_map/ppermute | solution.py:27
  57.3 0.1 join.5
  57.4 0.1 collective-permute-start.11
  57.5 0.8 %collective-permute-start.10 = (bf16[96,2048]{1,0:T(8,128)(2,1)S(1)}, bf16[96,2048]{1,0:T(8,128)(2,1)S(1)}, u32[]{:S(2)}, u32[]{:S(2)}) collective-permute-start(bf16[96,2048]{1,0:T(8,128)(2,1)S(1)} %collective-permute-done.8.refs_1_.refs_4_), channel_id=1, source_target_pairs={{0,4},{1,3},{2,6},{3,1},{4,0},{5,7},{6,2},{7,5},{8,12},{9,11},{10,... | collective-permute-start | bytes 1179656 | tf_op jit(solution)/shard_map/ppermute | solution.py:27
  58.3 7.0 %collective-permute-done.10.refs_6_ = bf16[96,2048]{1,0:T(8,128)(2,1)S(1)} collective-permute-done((bf16[96,2048]{1,0:T(8,128)(2,1)S(1)}, bf16[96,2048]{1,0:T(8,128)(2,1)S(1)}, u32[]{:S(2)}, u32[]{:S(2)}) %collective-permute-start.10) | collective-permute-done | bytes 393248 | tf_op jit(solution)/shard_map/ppermute | solution.py:27
  65.3 1.7 %collective-permute-done.12.refs_8_ = bf16[96,2048]{1,0:T(8,128)(2,1)S(1)} collective-permute-done((bf16[96,2048]{1,0:T(8,128)(2,1)S(1)}, bf16[96,2048]{1,0:T(8,128)(2,1)S(1)}, u32[]{:S(2)}, u32[]{:S(2)}) %collective-permute-start.12) | collective-permute-done | bytes 393248 | tf_op jit(solution)/shard_map/ppermute | solution.py:31
  67.0 5.5 %far_last.1 = f32[1,1024]{1,0:T(1,128)} custom-call(bf16[1024,4096]{1,0:T(8,128)(2,1)S(1)} %get-tuple-element.10.refs_0_, f32[1,1024]{1,0:T(1,128)S(1)} %get-tuple-element.16.refs_3_.refs_1_, f32[1,1024]{1,0:T(1,128)S(1)} %get-tuple-element.11.refs_5_.refs_1_.refs_2_, bf16[96,2048]{1,0:T(8,128)(2,1)S(1)} %join.4.refs_0_.refs_3_, ...), custom_call_target="tpu_custom_call" | custom-call | flops 3221225472 | bytes 11546624 | tf_op jit(solution)/shard_map/far_last/pallas_call | solution.py:66
  (14 shorter events, 0.1 us)
Async XLA Ops:
  0.6 27.6 %copy-start.1 = (s32[1,128]{1,0:T(1,128)S(1)}, s32[1,128]{1,0:T(1,128)}, u32[]{:S(2)}) copy-start(s32[1,128]{1,0:T(1,128)} %refs_2_.1) | copy-start | bytes 1540
  1.3 1.0 %copy-start = (bf16[64,4096]{1,0:T(8,128)(2,1)S(1)}, bf16[64,4096]{1,0:T(8,128)(2,1)}, u32[]{:S(2)}) copy-start(bf16[64,4096]{1,0:T(8,128)(2,1)} %refs_1_.1) | copy-start | bytes 1572868
  2.4 1.7 %collective-permute-start = (bf16[64,2048]{1,0:T(8,128)(2,1)S(1)}, bf16[64,2048]{1,0:T(8,128)(2,1)S(1)}, u32[]{:S(2)}, u32[]{:S(2)}) collective-permute-start(bf16[64,2048]{1,0:T(8,128)(2,1)S(1)} %get-tuple-element.13), channel_id=1, source_target_pairs={{0,1},{1,0},{2,3},{3,2},{4,5},{5,4},{6,7},{7,6},{8,9},{9,8},{10,11... | collective-permute-start | bytes 786440 | tf_op jit(solution)/shard_map/ppermute | solution.py:31
  4.1 14.9 %collective-permute-start.1 = (bf16[128,2048]{1,0:T(8,128)(2,1)S(1)}, bf16[128,2048]{1,0:T(8,128)(2,1)S(1)}, u32[]{:S(2)}, u32[]{:S(2)}) collective-permute-start(bf16[128,2048]{1,0:T(8,128)(2,1)S(1)} %join.3.refs_1_), channel_id=1, source_target_pairs={{0,2},{1,5},{2,0},{3,7},{4,6},{5,1},{6,4},{7,3},{8,10},{9,13},{10,... | collective-permute-start | bytes 1572872 | tf_op jit(solution)/shard_map/ppermute | solution.py:27
  7.0 18.0 %collective-permute-start.2 = (bf16[128,2048]{1,0:T(8,128)(2,1)S(1)}, bf16[128,2048]{1,0:T(8,128)(2,1)S(1)}, u32[]{:S(2)}, u32[]{:S(2)}) collective-permute-start(bf16[128,2048]{1,0:T(8,128)(2,1)S(1)} %join.3.refs_1_), channel_id=1, source_target_pairs={{0,4},{1,3},{2,6},{3,1},{4,0},{5,7},{6,2},{7,5},{8,12},{9,11},{10,... | collective-permute-start | bytes 1572872 | tf_op jit(solution)/shard_map/ppermute | solution.py:27
  19.0 9.2 %collective-permute-start.3 = (bf16[128,2048]{1,0:T(8,128)(2,1)S(1)}, bf16[128,2048]{1,0:T(8,128)(2,1)S(1)}, u32[]{:S(2)}, u32[]{:S(2)}) collective-permute-start(bf16[128,2048]{1,0:T(8,128)(2,1)S(1)} %collective-permute-done.1.refs_2_), channel_id=1, source_target_pairs={{0,4},{1,3},{2,6},{3,1},{4,0},{5,7},{6,2},{7,5},{8,12},{9,11},{10,... | collective-permute-start | bytes 1572872 | tf_op jit(solution)/shard_map/ppermute | solution.py:27
  30.8 6.4 %collective-permute-start.4 = (bf16[192,2048]{1,0:T(8,128)(2,1)S(1)}, bf16[192,2048]{1,0:T(8,128)(2,1)S(1)}, u32[]{:S(2)}, u32[]{:S(2)}) collective-permute-start(bf16[192,2048]{1,0:T(8,128)(2,1)S(1)} %get-tuple-element.14.refs_3_), channel_id=1, source_target_pairs={{0,1},{1,0},{2,3},{3,2},{4,5},{5,4},{6,7},{7,6},{8,9},{9,8},{10,11... | collective-permute-start | bytes 2359304 | tf_op jit(solution)/shard_map/ppermute | solution.py:31
  30.8 10.9 %collective-permute-start.5 = (bf16[32,2048]{1,0:T(8,128)(2,1)S(1)}, bf16[32,2048]{1,0:T(8,128)(2,1)S(1)}, u32[]{:S(2)}, u32[]{:S(2)}) collective-permute-start(bf16[32,2048]{1,0:T(8,128)(2,1)S(1)} %get-tuple-element.17), channel_id=1, source_target_pairs={{0,8},{8,16},{16,24},{24,0},{1,9},{9,17},{17,25},{25,1},{2,10},{10... | collective-permute-start | bytes 393224 | tf_op jit(solution)/shard_map/ppermute | solution.py:313
  33.3 11.9 %collective-permute-start.6 = (bf16[32,2048]{1,0:T(8,128)(2,1)S(1)}, bf16[32,2048]{1,0:T(8,128)(2,1)S(1)}, u32[]{:S(2)}, u32[]{:S(2)}) collective-permute-start(bf16[32,2048]{1,0:T(8,128)(2,1)S(1)} %get-tuple-element.17), channel_id=1, source_target_pairs={{0,16},{8,24},{16,0},{24,8},{1,17},{9,25},{17,1},{25,9},{2,18},{10... | collective-permute-start | bytes 393224 | tf_op jit(solution)/shard_map/ppermute | solution.py:313
  35.9 9.3 %collective-permute-start.7 = (bf16[32,2048]{1,0:T(8,128)(2,1)S(1)}, bf16[32,2048]{1,0:T(8,128)(2,1)S(1)}, u32[]{:S(2)}, u32[]{:S(2)}) collective-permute-start(bf16[32,2048]{1,0:T(8,128)(2,1)S(1)} %get-tuple-element.17), channel_id=1, source_target_pairs={{0,24},{8,0},{16,8},{24,16},{1,25},{9,1},{17,9},{25,17},{2,26},{10... | collective-permute-start | bytes 393224 | tf_op jit(solution)/shard_map/ppermute | solution.py:313
  45.2 12.0 %collective-permute-start.8 = (bf16[96,2048]{1,0:T(8,128)(2,1)S(1)}, bf16[96,2048]{1,0:T(8,128)(2,1)S(1)}, u32[]{:S(2)}, u32[]{:S(2)}) collective-permute-start(bf16[96,2048]{1,0:T(8,128)(2,1)S(1)} %join.4.refs_0_.refs_3_), channel_id=1, source_target_pairs={{0,2},{1,5},{2,0},{3,7},{4,6},{5,1},{6,4},{7,3},{8,10},{9,13},{10,... | collective-permute-start | bytes 1179656 | tf_op jit(solution)/shard_map/ppermute | solution.py:27
  46.8 10.5 %collective-permute-start.9 = (bf16[96,2048]{1,0:T(8,128)(2,1)S(1)}, bf16[96,2048]{1,0:T(8,128)(2,1)S(1)}, u32[]{:S(2)}, u32[]{:S(2)}) collective-permute-start(bf16[96,2048]{1,0:T(8,128)(2,1)S(1)} %join.4.refs_0_.refs_3_), channel_id=1, source_target_pairs={{0,4},{1,3},{2,6},{3,1},{4,0},{5,7},{6,2},{7,5},{8,12},{9,11},{10,... | collective-permute-start | bytes 1179656 | tf_op jit(solution)/shard_map/ppermute | solution.py:27
  57.4 9.6 %collective-permute-start.11 = (bf16[288,2048]{1,0:T(8,128)(2,1)S(1)}, bf16[288,2048]{1,0:T(8,128)(2,1)S(1)}, u32[]{:S(2)}, u32[]{:S(2)}) collective-permute-start(bf16[288,2048]{1,0:T(8,128)(2,1)S(1)} %join.5), channel_id=1, source_target_pairs={{0,1},{1,0},{2,3},{3,2},{4,5},{5,4},{6,7},{7,6},{8,9},{9,8},{10,11... | collective-permute-start | bytes 3538952 | tf_op jit(solution)/shard_map/ppermute | solution.py:31
  57.5 7.8 %collective-permute-start.10 = (bf16[96,2048]{1,0:T(8,128)(2,1)S(1)}, bf16[96,2048]{1,0:T(8,128)(2,1)S(1)}, u32[]{:S(2)}, u32[]{:S(2)}) collective-permute-start(bf16[96,2048]{1,0:T(8,128)(2,1)S(1)} %collective-permute-done.8.refs_1_.refs_4_), channel_id=1, source_target_pairs={{0,4},{1,3},{2,6},{3,1},{4,0},{5,7},{6,2},{7,5},{8,12},{9,11},{10,... | collective-permute-start | bytes 1179656 | tf_op jit(solution)/shard_map/ppermute | solution.py:27
  65.3 1.7 %collective-permute-start.12 = (bf16[96,2048]{1,0:T(8,128)(2,1)S(1)}, bf16[96,2048]{1,0:T(8,128)(2,1)S(1)}, u32[]{:S(2)}, u32[]{:S(2)}) collective-permute-start(bf16[96,2048]{1,0:T(8,128)(2,1)S(1)} %collective-permute-done.10.refs_6_), channel_id=1, source_target_pairs={{0,1},{1,0},{2,3},{3,2},{4,5},{5,4},{6,7},{7,6},{8,9},{9,8},{10,11... | collective-permute-start | bytes 1179656 | tf_op jit(solution)/shard_map/ppermute | solution.py:31

commit v6 on v4

--- a/solution.py
+++ b/solution.py
@@ -10,6 +10,7 @@
 CHUNKS = 2
 TILE = 256
 MARK = 2.0
+WEIGHT = 10**10
 MIB = 1024 * 1024
 F32, BF16 = jnp.float32, jnp.bfloat16
 
@@ -29,13 +30,6 @@
 
 def core_permute(block, size):
     return lax.ppermute(block, "mem", [(m, m ^ 1) for m in range(size)])
-
-
-def gather_chips(block, size):
-    held = [block]
-    for stage in range(len(chip_bits(size))):
-        held = held + [mixed_permute(b, size, stage) for b in held]
-    return held
 
 
 def block_flips(size, odd):
@@ -146,17 +140,18 @@
 
 def first_pick_kernel(size, chosen_ref, *refs):
     blocks, (share_ref, dense_ref, select_ref) = refs[:-3], refs[-3:]
-    slots, share, live = blocks[0].shape[0] // 2, share_ref.shape[0], dense_ref.shape[0]
+    slots, share, live = blocks[0].shape[0] * 2 // size, share_ref.shape[0], dense_ref.shape[0]
     picks = chosen_ref.shape[1]
     me = lax.axis_index("mem")
     odd_core = lax.rem(me, 2) == 1
     origins, counts = [], []
-    for e, o, block in zip(block_flips(size, False), block_flips(size, True), blocks):
+    for e, o in zip(block_flips(size, False), block_flips(size, True)):
         origin = lax.bitwise_xor(me, jnp.where(odd_core, o, e))
+        origins += [origin, lax.bitwise_xor(origin, 1)]
+    for block in blocks:
         alive = (block[:, :1].astype(F32) < 1.5).astype(jnp.int32)
-        for h in range(2):
-            origins.append(lax.bitwise_xor(origin, h))
-            counts.append(jnp.sum(alive[h * slots : (h + 1) * slots], axis=0, keepdims=True))
+        for top in range(0, block.shape[0], slots):
+            counts.append(jnp.sum(alive[top : top + slots], axis=0, keepdims=True))
     chosen = chosen_ref[...]
     row = lax.broadcasted_iota(jnp.int32, (share, picks), 0)
     lane = lax.broadcasted_iota(jnp.int32, (share, picks), 1)
@@ -184,78 +179,96 @@
     select_rows(select_ref[...], refs[:-2], refs[-2:])
 
 
-def row_norms(rows):
-    rows = rows.astype(F32)
-    return jnp.sum(rows * rows, axis=1, keepdims=True)
-
-
-def product(rows, cand):
-    return lax.dot_general(rows, cand, (((1,), (1,)), ((), ())), preferred_element_type=F32)
-
-
-def group_kernel(picks, cand_ref, norm_ref, chosen_ref, own, sib, near_ref, best_ref, rows_ref, cn_ref):
+def lane_norms(rows_ref, width):
+    squares = jnp.zeros((rows_ref.shape[0], 128), F32)
+    for k in range(0, width, 128):
+        entries = rows_ref[:, k : k + 128].astype(F32)
+        squares += entries * entries
+    return jnp.sum(squares.T, axis=0, keepdims=True)
+
+
+def gaps_to(cand, rows_ref, norms):
+    inner = lax.dot_general(
+        cand, rows_ref[...], (((1,), (1,)), ((), ())), preferred_element_type=F32
+    )
+    return norms - 2.0 * inner
+
+
+def nearest(gaps):
+    least = gaps[:, :128]
+    for k in range(128, gaps.shape[1], 128):
+        least = jnp.minimum(least, gaps[:, k : k + 128])
+    return jnp.min(least.T, axis=0, keepdims=True)
+
+
+def group_kernel(picks, cand_ref, norm_ref, chosen_ref, own, sib, near_ref, best_ref, rows_ref):
     live, part = own.shape[0], own.shape[1] // CHUNKS
     for c in range(CHUNKS):
         at = slice(c * part, (c + 1) * part)
-        rows_ref[:, 2 * c * part : (2 * c + 1) * part] = own[:, at]
-        rows_ref[:, (2 * c + 1) * part : (2 * c + 2) * part] = sib[:, at]
-    norm = row_norms(own[...]) + row_norms(sib[...])
-    cn_ref[...] = norm
-    down = lax.broadcasted_iota(jnp.int32, (live, 1), 0)
-    hit = jnp.max((chosen_ref[...] == down).astype(F32), axis=1, keepdims=True) > 0.5
-    outside = jnp.where(hit, 0.0, jnp.inf)
+        rows_ref[:live, 2 * c * part : (2 * c + 1) * part] = own[:, at]
+        rows_ref[:live, (2 * c + 1) * part : (2 * c + 2) * part] = sib[:, at]
+    padded = rows_ref.shape[0]
+    if padded > live:
+        rows_ref[live:, :] = jnp.zeros((padded - live, rows_ref.shape[1]), BF16)
+    lane = lax.broadcasted_iota(jnp.int32, (1, padded), 1)
+    norms = jnp.where(lane < live, lane_norms(rows_ref, rows_ref.shape[1]), jnp.inf)
+    row = lax.broadcasted_iota(jnp.int32, (padded, picks), 0)
+    hit = (chosen_ref[...] == row).astype(F32)
+    hits = jnp.zeros((1, padded), F32)
+    for k in range(0, picks, 128):
+        hits += jnp.sum(hit[:, k : k + 128].T, axis=0, keepdims=True)
+    outside = jnp.where(hits > 0.5, 0.0, jnp.inf)
 
     @pl.loop(0, cand_ref.shape[0] // TILE)
     def _(t):
         at = pl.ds(pl.multiple_of(t * TILE, TILE), TILE)
-        gaps = cn_ref[...] - 2.0 * product(rows_ref[...], cand_ref[at, :])
-        near_ref[:, at] = jnp.min(gaps, axis=0, keepdims=True) + norm_ref[:, at]
-        best_ref[:, at] = jnp.min(gaps + outside, axis=0, keepdims=True)
-
-
-def far_rows(size, blocks, early, late, rows_ref):
-    rows, part = blocks[0].shape
-    last = len(blocks) - 1
-    for i, block in enumerate(blocks):
-        rows_ref[i * rows : (i + 1) * rows, :part] = block[...]
-        top = sibling_place(i, size) * rows
-        other = late[...] if i == last else early[i * rows : (i + 1) * rows, :]
-        rows_ref[top : top + rows, part:] = other
+        gaps = gaps_to(cand_ref[at, :], rows_ref, norms)
+        near_ref[:, at] = nearest(gaps) + norm_ref[:, at]
+        best_ref[:, at] = nearest(gaps + outside)
+
+
+def far_rows(size, held, sibs, rows_ref):
+    rows, part = rows_ref.shape[0] // (size // 2), held[0].shape[1]
+    for i, block in enumerate(held):
+        top = i * block.shape[0]
+        rows_ref[top : top + block.shape[0], :part] = block[...]
+    for i in range(size // 2):
+        block = sibs[i * rows // sibs[0].shape[0]]
+        top = i * rows % sibs[0].shape[0]
+        to = sibling_place(i, size) * rows
+        rows_ref[to : to + rows, part:] = block[top : top + rows, :]
 
 
 def far_kernel(size, chunk, cand_ref, *refs):
     before = refs[:1] if chunk else ()
-    *blocks, early, late, out, rows_ref = refs[len(before) :]
-    far_rows(size, blocks, early, late, rows_ref)
+    *blocks, out, rows_ref = refs[len(before) :]
+    far_rows(size, blocks[:2], blocks[2:], rows_ref)
     width = rows_ref.shape[1]
-    norm = row_norms(rows_ref[...])
+    norms = lane_norms(rows_ref, width)
 
     @pl.loop(0, cand_ref.shape[0] // TILE)
     def _(t):
         at = pl.ds(pl.multiple_of(t * TILE, TILE), TILE)
-        inner = product(rows_ref[...], cand_ref[at, chunk * width : (chunk + 1) * width])
-        gaps = norm - 2.0 * inner
+        gaps = gaps_to(cand_ref[at, chunk * width : (chunk + 1) * width], rows_ref, norms)
         for ref in before:
-            gaps += ref[:, at]
-        out[:, at] = gaps
+            gaps += ref[at, :]
+        out[at, :] = gaps
 
 
 def last_kernel(size, chunk, cand_ref, best_ref, norm_ref, *refs):
     before = refs[:1] if chunk else ()
-    *blocks, early, late, out, rows_ref = refs[len(before) :]
-    far_rows(size, blocks, early, late, rows_ref)
+    *blocks, out, rows_ref = refs[len(before) :]
+    far_rows(size, blocks[:2], blocks[2:], rows_ref)
     width = rows_ref.shape[1]
-    norm = row_norms(rows_ref[...])
+    norms = lane_norms(rows_ref, width)
 
     @pl.loop(0, cand_ref.shape[0] // TILE)
     def _(t):
         at = pl.ds(pl.multiple_of(t * TILE, TILE), TILE)
-        inner = product(rows_ref[...], cand_ref[at, chunk * width : (chunk + 1) * width])
-        gaps = norm - 2.0 * inner
+        gaps = gaps_to(cand_ref[at, chunk * width : (chunk + 1) * width], rows_ref, norms)
         for ref in before:
-            gaps += ref[:, at]
-        nearest = jnp.minimum(jnp.min(gaps, axis=0, keepdims=True), best_ref[:, at])
-        out[:, at] = nearest + norm_ref[:, at]
+            gaps += ref[at, :]
+        out[:, at] = jnp.minimum(nearest(gaps), best_ref[:, at]) + norm_ref[:, at]
 
 
 def body(candidates, round_one, counts, chosen):
@@ -276,23 +289,30 @@
         specs=[pl.BlockSpec(memory_space=pltpu.SMEM)] + vmem_specs(1),
     )
     other = core_permute(send, size)
-    cand, norm = call(
-        load_kernel, "load", [bf16(rows, width), line], (candidates,),
-        specs=[pl.BlockSpec(memory_space=pltpu.HBM)],
-        scratch=[pltpu.SemaphoreType.DMA((rows // TILE * 2 * CHUNKS,))], limit=42 * MIB,
-    )
-
-    def join(blocks, columns, start=0, after=()):
+
+    def join(blocks, columns, start=0, after=(), weight=0):
         count = blocks[0].shape[0] * len(blocks)
         return call(
             functools.partial(join_kernel, len(blocks), start), "join", bf16(count, columns),
-            blocks, after=after,
+            blocks, weight, after=after,
         )
 
-    raw = []
-    for c in range(CHUNKS):
-        after = (*raw[-1][1:3], norm) if c else ()
-        raw.append(gather_chips(join((keep, other), part, c * part, after), size))
+    def double(block, got, stages, after=(), weight=0):
+        for stage in stages:
+            block = join((block, got), block.shape[1], after=after, weight=weight)
+            got = mixed_permute(block, size, stage)
+        return block, got
+
+    stages = range(1, len(chip_bits(size)))
+    first = [join((keep, other), part, c * part) for c in range(CHUNKS)]
+    got = [mixed_permute(block, size, 0) for block in first]
+    raw = [double(first[0], got[0], stages)]
+    cand, norm = call(
+        load_kernel, "load", [bf16(rows, width), line], (candidates,),
+        specs=[pl.BlockSpec(memory_space=pltpu.HBM)], after=raw[0][:1],
+        scratch=[pltpu.SemaphoreType.DMA((rows // TILE * 2 * CHUNKS,))], limit=42 * MIB,
+    )
+    raw += [double(f, g, stages, after=(norm,)) for f, g in zip(first[1:], got[1:])]
 
     dense, shifted, select = [], [], None
     for c in range(CHUNKS):
@@ -302,6 +322,7 @@
             picked, found, select = call(
                 functools.partial(first_pick_kernel, size), "pick_first",
                 outs + [bf16(share + live, size * slots)], (chosen, *raw[c]), flops,
+                after=(norm,),
             )
         else:
             picked, found = call(
@@ -315,36 +336,36 @@
             ]
         )
 
-    far, held = [], ()
+    scratch = [pltpu.VMEM((centers, 2 * part), BF16)]
+    flops = 2 * rows * centers * 2 * part
+    before, best, final = (), None, None
     for c in range(CHUNKS):
+        block = join(shifted[c], part, after=() if c else (picked,))
+        got = mixed_permute(block, size, 0)
         if c == CHUNKS - 1:
-            own = call(
-                beside_kernel, "beside", bf16(live, half), dense, after=(*shifted[c], *held[1:3])
-            )
+            own = call(beside_kernel, "beside", bf16(live, half), dense)
             near, best = call(
                 functools.partial(group_kernel, picks), "group", [line] * 2,
                 (cand, norm, chosen, own, core_permute(own, size)), 2 * rows * live * width,
-                scratch=[pltpu.VMEM((live, width), BF16), pltpu.VMEM((live, 1), F32)],
-            )
-        held = gather_chips(join(shifted[c], part, after=() if c else (picked,)), size)
-        early = join(held[:-1], part, after=(best,) if c == CHUNKS - 1 else ())
-        far.append((*held, core_permute(early, size), core_permute(held[-1], size)))
-
-    scratch = [pltpu.VMEM((centers, 2 * part), BF16)]
-    flops = 2 * rows * centers * 2 * part
-    before = ()
-    for c in range(CHUNKS - 1):
-        before = (
-            call(
-                functools.partial(far_kernel, size, c), "far",
-                jax.ShapeDtypeStruct((centers, rows), F32), (cand, *before, *far[c]), flops,
-                scratch=scratch,
-            ),
-        )
-    final = call(
-        functools.partial(last_kernel, size, CHUNKS - 1), "far_last", line,
-        (cand, best, norm, *before, *far[-1]), flops, scratch=scratch,
-    )
+                scratch=[pltpu.VMEM((-(-live // 128) * 128, width), BF16)], after=(block,),
+            )
+        weight = WEIGHT if c < CHUNKS - 1 else 0
+        mine, got = double(block, got, stages, after=(best,) if best is not None else (), weight=weight)
+        sent = join((got,), part, after=before) if before else got
+        blocks = (mine, got, core_permute(mine, size), core_permute(sent, size))
+        if c < CHUNKS - 1:
+            before = (
+                call(
+                    functools.partial(far_kernel, size, c), "far",
+                    jax.ShapeDtypeStruct((rows, centers), F32), (cand, *before, *blocks), flops,
+                    scratch=scratch,
+                ),
+            )
+        else:
+            final = call(
+                functools.partial(last_kernel, size, c), "far_last", line,
+                (cand, best, norm, *before, *blocks), flops, scratch=scratch,
+            )
     return near.reshape(-1), final.reshape(-1)
 
 

time: 68.4 us -> 68.8 us (level)
  starting transfers between devices: 27.2 us -> 21.9 us
  waiting for transfers between devices: 21.3 us -> 25.6 us
  Pallas kernels: 17.2 us -> 18.6 us
    ppermute x12 -> x8, starting transfers between devices: 16.7 us -> 10.5 us  [mixed_permute(): lax.ppermute(block, 'mem', [(m, m ^ (odd if m & 1 else even)) for m in ra...]
    ppermute x12 -> x8, waiting for transfers between devices: 12.8 us -> 15.3 us  [mixed_permute(): lax.ppermute(block, 'mem', [(m, m ^ (odd if m & 1 else even)) for m in ra...]
    pallas_call x14 -> x17, Pallas kernels: 17.2 us -> 18.6 us  [call(): pl.pallas_call(run, out_shape=out_shape, in_specs=(specs or vmem_specs(co...]
    ppermute x6, waiting for transfers between devices: 1.56 us -> 2.87 us  [core_permute(): return lax.ppermute(block, 'mem', [(m, m ^ 1) for m in range(size)])]
  transfers between devices with their start and end apart: 24 -> 20, of which waited for: 14 -> 11; matrix products, arithmetic and copies ran while one was open for 0% -> 0% of each run, Pallas kernels for 18% -> 19%
where the time goes in v6:
time: 68.8 us; the launch traced here: 68.6 us
  waiting for transfers between devices  25.6 us (37%)
  starting transfers between devices  21.9 us (32%)
  Pallas kernels  18.6 us (27%)
  between operations  1.44 us (2%)
  local copies, waits for them, and re-layouts  1.04 us (2%)
    pallas_call x17, Pallas kernels, call(): pl.pallas_call(run, out_shape=out_shape, in_specs=(specs or vmem_specs(co...  18.6 us
    ppermute x8, waiting for transfers between devices, mixed_permute(): lax.ppermute(block, 'mem', [(m, m ^ (odd if m & 1 else even)) for m in ra...  15.3 us
    ppermute x8, starting transfers between devices, mixed_permute(): lax.ppermute(block, 'mem', [(m, m ^ (odd if m & 1 else even)) for m in ra...  10.5 us
    ppermute x6, starting transfers between devices, body(): lax.ppermute(picked, 'grp', [(g, (g + k) % groups) for g in range(groups)])  10.2 us
    ppermute x6, waiting for transfers between devices, body(): lax.ppermute(picked, 'grp', [(g, (g + k) % groups) for g in range(groups)])  7.51 us
    ppermute x6, waiting for transfers between devices, core_permute(): return lax.ppermute(block, 'mem', [(m, m ^ 1) for m in range(size)])  2.87 us
  transfers between devices with their start and end apart: 20, of which 11 were waited for; matrix products, arithmetic and copies ran while one was open for 0% of the time, Pallas kernels for 19%

profile of v6, /device:TPU:0, one launch (start us, length us, event | category | flops | bytes accessed | tf_op | source)
XLA Modules:
  0.0 68.6 jit_solution(12485772503810077394)
XLA Ops:
  2.9 1.2 %collective-permute-done.refs_1_ = bf16[64,2048]{1,0:T(8,128)(2,1)S(1)} collective-permute-done((bf16[64,2048]{1,0:T(8,128)(2,1)S(1)}, bf16[64,2048]{1,0:T(8,128)(2,1)S(1)}, u32[]{:S(2)}, u32[]{:S(2)}) %collective-permute-start) | collective-permute-done | bytes 262176 | tf_op jit(solution)/shard_map/ppermute | solution.py:32
  4.1 2.9 %collective-permute-start.1 = (bf16[128,1024]{1,0:T(8,128)(2,1)S(1)}, bf16[128,1024]{1,0:T(8,128)(2,1)S(1)}, u32[]{:S(2)}, u32[]{:S(2)}) collective-permute-start(bf16[128,1024]{1,0:T(8,128)(2,1)S(1)} %join.9.refs_0_), channel_id=1, source_target_pairs={{0,2},{1,5},{2,0},{3,7},{4,6},{5,1},{6,4},{7,3},{8,10},{9,13},{10,... | collective-permute-start | bytes 786440 | tf_op jit(solution)/shard_map/ppermute | solution.py:28
  7.1 4.2 %collective-permute-done.1.refs_1_ = bf16[128,1024]{1,0:T(8,128)(2,1)S(1)} collective-permute-done((bf16[128,1024]{1,0:T(8,128)(2,1)S(1)}, bf16[128,1024]{1,0:T(8,128)(2,1)S(1)}, u32[]{:S(2)}, u32[]{:S(2)}) %collective-permute-start.1) | collective-permute-done | bytes 262176 | tf_op jit(solution)/shard_map/ppermute | solution.py:28
  11.4 2.1 %collective-permute-start.2 = (bf16[256,1024]{1,0:T(8,128)(2,1)S(1)}, bf16[256,1024]{1,0:T(8,128)(2,1)S(1)}, u32[]{:S(2)}, u32[]{:S(2)}) collective-permute-start(bf16[256,1024]{1,0:T(8,128)(2,1)S(1)} %join.10.refs_1_), channel_id=1, source_target_pairs={{0,4},{1,3},{2,6},{3,1},{4,0},{5,7},{6,2},{7,5},{8,12},{9,11},{10,... | collective-permute-start | bytes 1572872 | tf_op jit(solution)/shard_map/ppermute | solution.py:28
  13.5 4.0 %load.1 = (bf16[1024,4096]{1,0:T(8,128)(2,1)S(1)}, f32[1,1024]{1,0:T(1,128)S(1)}) custom-call(bf16[1024,4096]{1,0:T(8,128)(2,1)} %refs_0_.3, bf16[256,1024]{1,0:T(8,128)(2,1)S(1)} %join.10.refs_1_), custom_call_target="tpu_custom_call" | custom-call | bytes 16781312 | tf_op jit(solution)/shard_map/load/pallas_call | solution.py:60
  17.7 3.0 %collective-permute-done.2.refs_2_ = bf16[256,1024]{1,0:T(8,128)(2,1)S(1)} collective-permute-done((bf16[256,1024]{1,0:T(8,128)(2,1)S(1)}, bf16[256,1024]{1,0:T(8,128)(2,1)S(1)}, u32[]{:S(2)}, u32[]{:S(2)}) %collective-permute-start.2) | collective-permute-done | bytes 524320 | tf_op jit(solution)/shard_map/ppermute | solution.py:28
  20.7 1.1 %pick_first.1 = (bf16[32,1024]{1,0:T(8,128)(2,1)S(1)}, bf16[192,1024]{1,0:T(8,128)(2,1)S(1)}, bf16[224,512]{1,0:T(8,128)(2,1)S(1)}) custom-call(s32[1,128]{1,0:T(1,128)S(1)} %copy-done.1, bf16[256,1024]{1,0:T(8,128)(2,1)S(1)} %join.10.refs_1_, bf16[256,1024]{1,0:T(8,128)(2,1)S(1)} %collective-permute-done.2.refs_2_, ...), custom_call_target="tpu_custom_call" | custom-call | flops 234881024 | bytes 1737216 | tf_op jit(solution)/shard_map/pick_first/pallas_call | solution.py:60
  21.8 2.1 %collective-permute-start.5 = (bf16[32,1024]{1,0:T(8,128)(2,1)S(1)}, bf16[32,1024]{1,0:T(8,128)(2,1)S(1)}, u32[]{:S(2)}, u32[]{:S(2)}) collective-permute-start(bf16[32,1024]{1,0:T(8,128)(2,1)S(1)} %get-tuple-element.19), channel_id=1, source_target_pairs={{0,8},{8,16},{16,24},{24,0},{1,9},{9,17},{17,25},{25,1},{2,10},{10... | collective-permute-start | bytes 196616 | tf_op jit(solution)/shard_map/ppermute | solution.py:334
  24.0 2.6 %collective-permute-start.6 = (bf16[32,1024]{1,0:T(8,128)(2,1)S(1)}, bf16[32,1024]{1,0:T(8,128)(2,1)S(1)}, u32[]{:S(2)}, u32[]{:S(2)}) collective-permute-start(bf16[32,1024]{1,0:T(8,128)(2,1)S(1)} %get-tuple-element.19), channel_id=1, source_target_pairs={{0,16},{8,24},{16,0},{24,8},{1,17},{9,25},{17,1},{25,9},{2,18},{10... | collective-permute-start | bytes 196616 | tf_op jit(solution)/shard_map/ppermute | solution.py:334
  26.6 1.3 %collective-permute-start.7 = (bf16[32,1024]{1,0:T(8,128)(2,1)S(1)}, bf16[32,1024]{1,0:T(8,128)(2,1)S(1)}, u32[]{:S(2)}, u32[]{:S(2)}) collective-permute-start(bf16[32,1024]{1,0:T(8,128)(2,1)S(1)} %get-tuple-element.19), channel_id=1, source_target_pairs={{0,24},{8,0},{16,8},{24,16},{1,25},{9,1},{17,9},{25,17},{2,26},{10... | collective-permute-start | bytes 196616 | tf_op jit(solution)/shard_map/ppermute | solution.py:334
  27.9 1.2 %collective-permute-done.5.refs_3_.refs_0_ = bf16[32,1024]{1,0:T(8,128)(2,1)S(1)} collective-permute-done((bf16[32,1024]{1,0:T(8,128)(2,1)S(1)}, bf16[32,1024]{1,0:T(8,128)(2,1)S(1)}, u32[]{:S(2)}, u32[]{:S(2)}) %collective-permute-start.5) | collective-permute-done | bytes 65568 | tf_op jit(solution)/shard_map/ppermute | solution.py:334
  29.1 2.1 %collective-permute-done.6.refs_4_.refs_1_ = bf16[32,1024]{1,0:T(8,128)(2,1)S(1)} collective-permute-done((bf16[32,1024]{1,0:T(8,128)(2,1)S(1)}, bf16[32,1024]{1,0:T(8,128)(2,1)S(1)}, u32[]{:S(2)}, u32[]{:S(2)}) %collective-permute-start.6) | collective-permute-done | bytes 65568 | tf_op jit(solution)/shard_map/ppermute | solution.py:334
  32.1 1.6 %collective-permute-start.12 = (bf16[96,1024]{1,0:T(8,128)(2,1)S(1)}, bf16[96,1024]{1,0:T(8,128)(2,1)S(1)}, u32[]{:S(2)}, u32[]{:S(2)}) collective-permute-start(bf16[96,1024]{1,0:T(8,128)(2,1)S(1)} %join.14.refs_0_), channel_id=1, source_target_pairs={{0,2},{1,5},{2,0},{3,7},{4,6},{5,1},{6,4},{7,3},{8,10},{9,13},{10,... | collective-permute-start | bytes 589832 | tf_op jit(solution)/shard_map/ppermute | solution.py:28
  33.9 4.1 %collective-permute-done.12.refs_1_ = bf16[96,1024]{1,0:T(8,128)(2,1)S(1)} collective-permute-done((bf16[96,1024]{1,0:T(8,128)(2,1)S(1)}, bf16[96,1024]{1,0:T(8,128)(2,1)S(1)}, u32[]{:S(2)}, u32[]{:S(2)}) %collective-permute-start.12) | collective-permute-done | bytes 196640 | tf_op jit(solution)/shard_map/ppermute | solution.py:28
  38.0 1.5 %collective-permute-start.13 = (bf16[192,1024]{1,0:T(8,128)(2,1)S(1)}, bf16[192,1024]{1,0:T(8,128)(2,1)S(1)}, u32[]{:S(2)}, u32[]{:S(2)}) collective-permute-start(bf16[192,1024]{1,0:T(8,128)(2,1)S(1)} %join.15.refs_1_), channel_id=1, source_target_pairs={{0,4},{1,3},{2,6},{3,1},{4,0},{5,7},{6,2},{7,5},{8,12},{9,11},{10,... | collective-permute-start | bytes 1179656 | tf_op jit(solution)/shard_map/ppermute | solution.py:28
  40.6 3.1 %collective-permute-start.10 = (bf16[32,1024]{1,0:T(8,128)(2,1)S(1)}, bf16[32,1024]{1,0:T(8,128)(2,1)S(1)}, u32[]{:S(2)}, u32[]{:S(2)}) collective-permute-start(bf16[32,1024]{1,0:T(8,128)(2,1)S(1)} %get-tuple-element.21.refs_3_), channel_id=1, source_target_pairs={{0,16},{8,24},{16,0},{24,8},{1,17},{9,25},{17,1},{25,9},{2,18},{10... | collective-permute-start | bytes 196616 | tf_op jit(solution)/shard_map/ppermute | solution.py:334
  43.7 2.0 %collective-permute-done.9.refs_0_ = bf16[32,1024]{1,0:T(8,128)(2,1)S(1)} collective-permute-done((bf16[32,1024]{1,0:T(8,128)(2,1)S(1)}, bf16[32,1024]{1,0:T(8,128)(2,1)S(1)}, u32[]{:S(2)}, u32[]{:S(2)}) %collective-permute-start.9) | collective-permute-done | bytes 65568 | tf_op jit(solution)/shard_map/ppermute | solution.py:334
  45.6 1.4 %collective-permute-done.10.refs_1_ = bf16[32,1024]{1,0:T(8,128)(2,1)S(1)} collective-permute-done((bf16[32,1024]{1,0:T(8,128)(2,1)S(1)}, bf16[32,1024]{1,0:T(8,128)(2,1)S(1)}, u32[]{:S(2)}, u32[]{:S(2)}) %collective-permute-start.10) | collective-permute-done | bytes 65568 | tf_op jit(solution)/shard_map/ppermute | solution.py:334
  47.9 1.6 %collective-permute-start.16 = (bf16[96,1024]{1,0:T(8,128)(2,1)S(1)}, bf16[96,1024]{1,0:T(8,128)(2,1)S(1)}, u32[]{:S(2)}, u32[]{:S(2)}) collective-permute-start(bf16[96,1024]{1,0:T(8,128)(2,1)S(1)} %join.13.refs_5_.refs_0_), channel_id=1, source_target_pairs={{0,2},{1,5},{2,0},{3,7},{4,6},{5,1},{6,4},{7,3},{8,10},{9,13},{10,... | collective-permute-start | bytes 589832 | tf_op jit(solution)/shard_map/ppermute | solution.py:28
  50.1 4.6 %group.1 = (f32[1,1024]{1,0:T(1,128)}, f32[1,1024]{1,0:T(1,128)S(1)}) custom-call(bf16[1024,4096]{1,0:T(8,128)(2,1)S(1)} %get-tuple-element.15.refs_0_, f32[1,1024]{1,0:T(1,128)S(1)} %get-tuple-element.16.refs_3_.refs_2_.refs_1_, s32[1,128]{1,0:T(1,128)S(1)} %copy-done.1, bf16[192,2048]{1,0:T(8,128)(2,1)S(1)} %beside.1.refs_3_, ...), custom_call_target="tpu_custom_call" | custom-call | flops 1610612736 | bytes 9974272 | tf_op jit(solution)/shard_map/group/pallas_call | solution.py:60
  55.3 3.4 %far.1.refs_1_.refs_3_ = f32[1024,384]{1,0:T(8,128)S(1)} custom-call(bf16[1024,4096]{1,0:T(8,128)(2,1)S(1)} %get-tuple-element.15.refs_0_, bf16[192,1024]{1,0:T(8,128)(2,1)S(1)} %join.15.refs_1_, bf16[192,1024]{1,0:T(8,128)(2,1)S(1)} %collective-permute-done.13.refs_2_, bf16[192,1024]{1,0:T(8,128)(2,1)S(1)} %collective-permute-done.14.refs_3_, ...), custom_call_target="tpu_custom_call" | custom-call | flops 1610612736 | bytes 11534336 | tf_op jit(solution)/shard_map/far/pallas_call | solution.py:60
  58.6 3.9 %collective-permute-done.17.refs_0_.refs_5_ = bf16[192,1024]{1,0:T(8,128)(2,1)S(1)} collective-permute-done((bf16[192,1024]{1,0:T(8,128)(2,1)S(1)}, bf16[192,1024]{1,0:T(8,128)(2,1)S(1)}, u32[]{:S(2)}, u32[]{:S(2)}) %collective-permute-start.17) | collective-permute-done | bytes 393248 | tf_op jit(solution)/shard_map/ppermute | solution.py:28
  62.7 1.7 %collective-permute-done.19.refs_7_ = bf16[192,1024]{1,0:T(8,128)(2,1)S(1)} collective-permute-done((bf16[192,1024]{1,0:T(8,128)(2,1)S(1)}, bf16[192,1024]{1,0:T(8,128)(2,1)S(1)}, u32[]{:S(2)}, u32[]{:S(2)}) %collective-permute-start.19) | collective-permute-done | bytes 393248 | tf_op jit(solution)/shard_map/ppermute | solution.py:32
  64.4 4.3 %far_last.1 = f32[1,1024]{1,0:T(1,128)} custom-call(bf16[1024,4096]{1,0:T(8,128)(2,1)S(1)} %get-tuple-element.15.refs_0_, f32[1,1024]{1,0:T(1,128)S(1)} %get-tuple-element.23.refs_2_.refs_1_, f32[1,1024]{1,0:T(1,128)S(1)} %get-tuple-element.16.refs_3_.refs_2_.refs_1_, f32[1024,384]{1,0:T(8,128)S(1)} %far.1.refs_1_.refs_3_, ...), custom_call_target="tpu_custom_call" | custom-call | flops 1610612736 | bytes 11546624 | tf_op jit(solution)/shard_map/far_last/pallas_call | solution.py:60
  (37 shorter events, 6.2 us)
Async XLA Ops:
  0.6 20.1 %copy-start.1 = (s32[1,128]{1,0:T(1,128)S(1)}, s32[1,128]{1,0:T(1,128)}, u32[]{:S(2)}) copy-start(s32[1,128]{1,0:T(1,128)} %refs_2_.1) | copy-start | bytes 1540
  1.3 1.0 %copy-start = (bf16[64,4096]{1,0:T(8,128)(2,1)S(1)}, bf16[64,4096]{1,0:T(8,128)(2,1)}, u32[]{:S(2)}) copy-start(bf16[64,4096]{1,0:T(8,128)(2,1)} %refs_1_.1) | copy-start | bytes 1572868
  2.4 1.7 %collective-permute-start = (bf16[64,2048]{1,0:T(8,128)(2,1)S(1)}, bf16[64,2048]{1,0:T(8,128)(2,1)S(1)}, u32[]{:S(2)}, u32[]{:S(2)}) collective-permute-start(bf16[64,2048]{1,0:T(8,128)(2,1)S(1)} %get-tuple-element.14), channel_id=1, source_target_pairs={{0,1},{1,0},{2,3},{3,2},{4,5},{5,4},{6,7},{7,6},{8,9},{9,8},{10,11... | collective-permute-start | bytes 786440 | tf_op jit(solution)/shard_map/ppermute | solution.py:32
  4.1 7.3 %collective-permute-start.1 = (bf16[128,1024]{1,0:T(8,128)(2,1)S(1)}, bf16[128,1024]{1,0:T(8,128)(2,1)S(1)}, u32[]{:S(2)}, u32[]{:S(2)}) collective-permute-start(bf16[128,1024]{1,0:T(8,128)(2,1)S(1)} %join.9.refs_0_), channel_id=1, source_target_pairs={{0,2},{1,5},{2,0},{3,7},{4,6},{5,1},{6,4},{7,3},{8,10},{9,13},{10,... | collective-permute-start | bytes 786440 | tf_op jit(solution)/shard_map/ppermute | solution.py:28
  7.0 10.5 %collective-permute-start.3 = (bf16[128,1024]{1,0:T(8,128)(2,1)S(1)}, bf16[128,1024]{1,0:T(8,128)(2,1)S(1)}, u32[]{:S(2)}, u32[]{:S(2)}) collective-permute-start(bf16[128,1024]{1,0:T(8,128)(2,1)S(1)} %join.11.refs_0_), channel_id=1, source_target_pairs={{0,2},{1,5},{2,0},{3,7},{4,6},{5,1},{6,4},{7,3},{8,10},{9,13},{10,... | collective-permute-start | bytes 786440 | tf_op jit(solution)/shard_map/ppermute | solution.py:28
  11.4 9.3 %collective-permute-start.2 = (bf16[256,1024]{1,0:T(8,128)(2,1)S(1)}, bf16[256,1024]{1,0:T(8,128)(2,1)S(1)}, u32[]{:S(2)}, u32[]{:S(2)}) collective-permute-start(bf16[256,1024]{1,0:T(8,128)(2,1)S(1)} %join.10.refs_1_), channel_id=1, source_target_pairs={{0,4},{1,3},{2,6},{3,1},{4,0},{5,7},{6,2},{7,5},{8,12},{9,11},{10,... | collective-permute-start | bytes 1572872 | tf_op jit(solution)/shard_map/ppermute | solution.py:28
  17.6 10.3 %collective-permute-start.4 = (bf16[256,1024]{1,0:T(8,128)(2,1)S(1)}, bf16[256,1024]{1,0:T(8,128)(2,1)S(1)}, u32[]{:S(2)}, u32[]{:S(2)}) collective-permute-start(bf16[256,1024]{1,0:T(8,128)(2,1)S(1)} %join.12.refs_1_), channel_id=1, source_target_pairs={{0,4},{1,3},{2,6},{3,1},{4,0},{5,7},{6,2},{7,5},{8,12},{9,11},{10,... | collective-permute-start | bytes 1572872 | tf_op jit(solution)/shard_map/ppermute | solution.py:28
  21.8 7.2 %collective-permute-start.5 = (bf16[32,1024]{1,0:T(8,128)(2,1)S(1)}, bf16[32,1024]{1,0:T(8,128)(2,1)S(1)}, u32[]{:S(2)}, u32[]{:S(2)}) collective-permute-start(bf16[32,1024]{1,0:T(8,128)(2,1)S(1)} %get-tuple-element.19), channel_id=1, source_target_pairs={{0,8},{8,16},{16,24},{24,0},{1,9},{9,17},{17,25},{25,1},{2,10},{10... | collective-permute-start | bytes 196616 | tf_op jit(solution)/shard_map/ppermute | solution.py:334
  24.0 7.2 %collective-permute-start.6 = (bf16[32,1024]{1,0:T(8,128)(2,1)S(1)}, bf16[32,1024]{1,0:T(8,128)(2,1)S(1)}, u32[]{:S(2)}, u32[]{:S(2)}) collective-permute-start(bf16[32,1024]{1,0:T(8,128)(2,1)S(1)} %get-tuple-element.19), channel_id=1, source_target_pairs={{0,16},{8,24},{16,0},{24,8},{1,17},{9,25},{17,1},{25,9},{2,18},{10... | collective-permute-start | bytes 196616 | tf_op jit(solution)/shard_map/ppermute | solution.py:334
  26.6 4.6 %collective-permute-start.7 = (bf16[32,1024]{1,0:T(8,128)(2,1)S(1)}, bf16[32,1024]{1,0:T(8,128)(2,1)S(1)}, u32[]{:S(2)}, u32[]{:S(2)}) collective-permute-start(bf16[32,1024]{1,0:T(8,128)(2,1)S(1)} %get-tuple-element.19), channel_id=1, source_target_pairs={{0,24},{8,0},{16,8},{24,16},{1,25},{9,1},{17,9},{25,17},{2,26},{10... | collective-permute-start | bytes 196616 | tf_op jit(solution)/shard_map/ppermute | solution.py:334
  32.1 5.9 %collective-permute-start.12 = (bf16[96,1024]{1,0:T(8,128)(2,1)S(1)}, bf16[96,1024]{1,0:T(8,128)(2,1)S(1)}, u32[]{:S(2)}, u32[]{:S(2)}) collective-permute-start(bf16[96,1024]{1,0:T(8,128)(2,1)S(1)} %join.14.refs_0_), channel_id=1, source_target_pairs={{0,2},{1,5},{2,0},{3,7},{4,6},{5,1},{6,4},{7,3},{8,10},{9,13},{10,... | collective-permute-start | bytes 589832 | tf_op jit(solution)/shard_map/ppermute | solution.py:28
  33.8 16.3 %collective-permute-start.8 = (bf16[192,2048]{1,0:T(8,128)(2,1)S(1)}, bf16[192,2048]{1,0:T(8,128)(2,1)S(1)}, u32[]{:S(2)}, u32[]{:S(2)}) collective-permute-start(bf16[192,2048]{1,0:T(8,128)(2,1)S(1)} %beside.1.refs_3_), channel_id=1, source_target_pairs={{0,1},{1,0},{2,3},{3,2},{4,5},{5,4},{6,7},{7,6},{8,9},{9,8},{10,11... | collective-permute-start | bytes 2359304 | tf_op jit(solution)/shard_map/ppermute | solution.py:32
  38.0 11.6 %collective-permute-start.13 = (bf16[192,1024]{1,0:T(8,128)(2,1)S(1)}, bf16[192,1024]{1,0:T(8,128)(2,1)S(1)}, u32[]{:S(2)}, u32[]{:S(2)}) collective-permute-start(bf16[192,1024]{1,0:T(8,128)(2,1)S(1)} %join.15.refs_1_), channel_id=1, source_target_pairs={{0,4},{1,3},{2,6},{3,1},{4,0},{5,7},{6,2},{7,5},{8,12},{9,11},{10,... | collective-permute-start | bytes 1179656 | tf_op jit(solution)/shard_map/ppermute | solution.py:28
  39.5 6.1 %collective-permute-start.9 = (bf16[32,1024]{1,0:T(8,128)(2,1)S(1)}, bf16[32,1024]{1,0:T(8,128)(2,1)S(1)}, u32[]{:S(2)}, u32[]{:S(2)}) collective-permute-start(bf16[32,1024]{1,0:T(8,128)(2,1)S(1)} %get-tuple-element.21.refs_3_), channel_id=1, source_target_pairs={{0,8},{8,16},{16,24},{24,0},{1,9},{9,17},{17,25},{25,1},{2,10},{10... | collective-permute-start | bytes 196616 | tf_op jit(solution)/shard_map/ppermute | solution.py:334
  40.6 6.4 %collective-permute-start.10 = (bf16[32,1024]{1,0:T(8,128)(2,1)S(1)}, bf16[32,1024]{1,0:T(8,128)(2,1)S(1)}, u32[]{:S(2)}, u32[]{:S(2)}) collective-permute-start(bf16[32,1024]{1,0:T(8,128)(2,1)S(1)} %get-tuple-element.21.refs_3_), channel_id=1, source_target_pairs={{0,16},{8,24},{16,0},{24,8},{1,17},{9,25},{17,1},{25,9},{2,18},{10... | collective-permute-start | bytes 196616 | tf_op jit(solution)/shard_map/ppermute | solution.py:334
  43.7 4.3 %collective-permute-start.11 = (bf16[32,1024]{1,0:T(8,128)(2,1)S(1)}, bf16[32,1024]{1,0:T(8,128)(2,1)S(1)}, u32[]{:S(2)}, u32[]{:S(2)}) collective-permute-start(bf16[32,1024]{1,0:T(8,128)(2,1)S(1)} %get-tuple-element.21.refs_3_), channel_id=1, source_target_pairs={{0,24},{8,0},{16,8},{24,16},{1,25},{9,1},{17,9},{25,17},{2,26},{10... | collective-permute-start | bytes 196616 | tf_op jit(solution)/shard_map/ppermute | solution.py:334
  47.9 6.7 %collective-permute-start.16 = (bf16[96,1024]{1,0:T(8,128)(2,1)S(1)}, bf16[96,1024]{1,0:T(8,128)(2,1)S(1)}, u32[]{:S(2)}, u32[]{:S(2)}) collective-permute-start(bf16[96,1024]{1,0:T(8,128)(2,1)S(1)} %join.13.refs_5_.refs_0_), channel_id=1, source_target_pairs={{0,2},{1,5},{2,0},{3,7},{4,6},{5,1},{6,4},{7,3},{8,10},{9,13},{10,... | collective-permute-start | bytes 589832 | tf_op jit(solution)/shard_map/ppermute | solution.py:28
  49.6 5.7 %collective-permute-start.14 = (bf16[192,1024]{1,0:T(8,128)(2,1)S(1)}, bf16[192,1024]{1,0:T(8,128)(2,1)S(1)}, u32[]{:S(2)}, u32[]{:S(2)}) collective-permute-start(bf16[192,1024]{1,0:T(8,128)(2,1)S(1)} %join.15.refs_1_), channel_id=1, source_target_pairs={{0,1},{1,0},{2,3},{3,2},{4,5},{5,4},{6,7},{7,6},{8,9},{9,8},{10,11... | collective-permute-start | bytes 1179656 | tf_op jit(solution)/shard_map/ppermute | solution.py:32
  49.6 5.7 %collective-permute-start.15 = (bf16[192,1024]{1,0:T(8,128)(2,1)S(1)}, bf16[192,1024]{1,0:T(8,128)(2,1)S(1)}, u32[]{:S(2)}, u32[]{:S(2)}) collective-permute-start(bf16[192,1024]{1,0:T(8,128)(2,1)S(1)} %collective-permute-done.13.refs_2_), channel_id=1, source_target_pairs={{0,1},{1,0},{2,3},{3,2},{4,5},{5,4},{6,7},{7,6},{8,9},{9,8},{10,11... | collective-permute-start | bytes 1179656 | tf_op jit(solution)/shard_map/ppermute | solution.py:32
  54.7 7.8 %collective-permute-start.17 = (bf16[192,1024]{1,0:T(8,128)(2,1)S(1)}, bf16[192,1024]{1,0:T(8,128)(2,1)S(1)}, u32[]{:S(2)}, u32[]{:S(2)}) collective-permute-start(bf16[192,1024]{1,0:T(8,128)(2,1)S(1)} %join.16.refs_4_), channel_id=1, source_target_pairs={{0,4},{1,3},{2,6},{3,1},{4,0},{5,7},{6,2},{7,5},{8,12},{9,11},{10,... | collective-permute-start | bytes 1179656 | tf_op jit(solution)/shard_map/ppermute | solution.py:28
  55.3 7.4 %collective-permute-start.18 = (bf16[192,1024]{1,0:T(8,128)(2,1)S(1)}, bf16[192,1024]{1,0:T(8,128)(2,1)S(1)}, u32[]{:S(2)}, u32[]{:S(2)}) collective-permute-start(bf16[192,1024]{1,0:T(8,128)(2,1)S(1)} %join.16.refs_4_), channel_id=1, source_target_pairs={{0,1},{1,0},{2,3},{3,2},{4,5},{5,4},{6,7},{7,6},{8,9},{9,8},{10,11... | collective-permute-start | bytes 1179656 | tf_op jit(solution)/shard_map/ppermute | solution.py:32
  62.6 1.8 %collective-permute-start.19 = (bf16[192,1024]{1,0:T(8,128)(2,1)S(1)}, bf16[192,1024]{1,0:T(8,128)(2,1)S(1)}, u32[]{:S(2)}, u32[]{:S(2)}) collective-permute-start(bf16[192,1024]{1,0:T(8,128)(2,1)S(1)} %join.17), channel_id=1, source_target_pairs={{0,1},{1,0},{2,3},{3,2},{4,5},{5,4},{6,7},{7,6},{8,9},{9,8},{10,11... | collective-permute-start | bytes 1179656 | tf_op jit(solution)/shard_map/ppermute | solution.py:32

commit v7 on v6

--- a/solution.py
+++ b/solution.py
@@ -10,8 +10,8 @@
 CHUNKS = 2
 TILE = 256
 MARK = 2.0
+MIB = 1024 * 1024
 WEIGHT = 10**10
-MIB = 1024 * 1024
 F32, BF16 = jnp.float32, jnp.bfloat16
 
 
@@ -64,7 +64,7 @@
         out_specs=jax.tree.map(lambda _: pl.BlockSpec(memory_space=pltpu.VMEM), out_shape),
         scratch_shapes=scratch,
         compiler_params=pltpu.CompilerParams(vmem_limit_bytes=limit),
-        cost_estimate=pl.CostEstimate(flops=flops, bytes_accessed=moved, transcendentals=0),
+        cost_estimate=pl.CostEstimate(flops=WEIGHT, bytes_accessed=moved, transcendentals=0),
         name=name,
     )(*operands, *after)
 
@@ -74,7 +74,7 @@
     core = lax.rem(lax.axis_index("mem"), 2)
     lane = lax.broadcasted_iota(jnp.int32, (slots, 128), 1)
     row = lax.broadcasted_iota(jnp.int32, (slots, 128), 0)
-    dead = (lane == 0) & (row >= count_ref[0, 0])
+    dead = (lane == 0) & (row >= count_ref[...])
     for out, start in ((keep_ref, core * half), (send_ref, (1 - core) * half)):
         start = pl.multiple_of(start, half)
         first = rows_ref[:, pl.ds(start, 128)].astype(F32)
@@ -82,34 +82,37 @@
         out[:, :128] = jnp.where(dead, MARK, first).astype(BF16)
 
 
-def load_kernel(cand_hbm, cand_ref, norm_ref, sems):
-    half = cand_ref.shape[1] // 2
-    part = half // CHUNKS
+def load_kernel(cand_hbm, cand_ref, norm_ref, tile_ref, sems):
+    width, rows = cand_ref.shape
+    half, part = width // 2, width // (2 * CHUNKS)
     core = lax.rem(lax.axis_index("mem"), 2)
-    tiles = cand_ref.shape[0] // TILE
     copies = []
-    for t in range(tiles):
-        at = pl.ds(t * TILE, TILE)
+    for t in range(rows // TILE):
         for p in range(2 * CHUNKS):
             own = core if p % 2 == 0 else 1 - core
             start = pl.multiple_of(own * half + p // 2 * part, part)
             copies.append(
                 pltpu.make_async_copy(
-                    cand_hbm.at[at, pl.ds(start, part)],
-                    cand_ref.at[at, pl.ds(p * part, part)],
+                    cand_hbm.at[pl.ds(t * TILE, TILE), pl.ds(start, part)],
+                    tile_ref.at[pl.ds(t * TILE, TILE), pl.ds(p * part, part)],
                     sems.at[len(copies)],
                 )
             )
     for copy in copies:
         copy.start()
-    for t in range(tiles):
+    for t in range(rows // TILE):
+        at = slice(t * TILE, (t + 1) * TILE)
         for copy in copies[t * 2 * CHUNKS : (t + 1) * 2 * CHUNKS]:
             copy.wait()
-        squares = jnp.zeros((TILE, 128), F32)
-        for k in range(0, cand_ref.shape[1], 128):
-            entries = cand_ref[t * TILE : (t + 1) * TILE, k : k + 128].astype(F32)
-            squares += entries * entries
-        norm_ref[:, t * TILE : (t + 1) * TILE] = jnp.sum(squares.T, axis=0, keepdims=True)
+
+        def turn(k, squares, at=at):
+            columns = pl.ds(pl.multiple_of(k * TILE, TILE), TILE)
+            turned = tile_ref[at, columns].T
+            cand_ref[columns, at] = turned
+            entries = turned.astype(F32)
+            return squares + jnp.sum(entries * entries, axis=0, keepdims=True)
+
+        norm_ref[:, at] = lax.fori_loop(0, width // TILE, turn, jnp.zeros((1, TILE), F32))
 
 
 def join_kernel(count, start, *refs):
@@ -179,52 +182,32 @@
     select_rows(select_ref[...], refs[:-2], refs[-2:])
 
 
-def lane_norms(rows_ref, width):
-    squares = jnp.zeros((rows_ref.shape[0], 128), F32)
-    for k in range(0, width, 128):
-        entries = rows_ref[:, k : k + 128].astype(F32)
-        squares += entries * entries
-    return jnp.sum(squares.T, axis=0, keepdims=True)
-
-
-def gaps_to(cand, rows_ref, norms):
-    inner = lax.dot_general(
-        cand, rows_ref[...], (((1,), (1,)), ((), ())), preferred_element_type=F32
-    )
-    return norms - 2.0 * inner
-
-
-def nearest(gaps):
-    least = gaps[:, :128]
-    for k in range(128, gaps.shape[1], 128):
-        least = jnp.minimum(least, gaps[:, k : k + 128])
-    return jnp.min(least.T, axis=0, keepdims=True)
+def row_norms(rows):
+    rows = rows.astype(F32)
+    return jnp.sum(rows * rows, axis=1, keepdims=True)
+
+
+def product(rows, cand):
+    return jnp.dot(rows, cand, preferred_element_type=F32)
 
 
 def group_kernel(picks, cand_ref, norm_ref, chosen_ref, own, sib, near_ref, best_ref, rows_ref):
     live, part = own.shape[0], own.shape[1] // CHUNKS
     for c in range(CHUNKS):
         at = slice(c * part, (c + 1) * part)
-        rows_ref[:live, 2 * c * part : (2 * c + 1) * part] = own[:, at]
-        rows_ref[:live, (2 * c + 1) * part : (2 * c + 2) * part] = sib[:, at]
-    padded = rows_ref.shape[0]
-    if padded > live:
-        rows_ref[live:, :] = jnp.zeros((padded - live, rows_ref.shape[1]), BF16)
-    lane = lax.broadcasted_iota(jnp.int32, (1, padded), 1)
-    norms = jnp.where(lane < live, lane_norms(rows_ref, rows_ref.shape[1]), jnp.inf)
-    row = lax.broadcasted_iota(jnp.int32, (padded, picks), 0)
-    hit = (chosen_ref[...] == row).astype(F32)
-    hits = jnp.zeros((1, padded), F32)
-    for k in range(0, picks, 128):
-        hits += jnp.sum(hit[:, k : k + 128].T, axis=0, keepdims=True)
-    outside = jnp.where(hits > 0.5, 0.0, jnp.inf)
-
-    @pl.loop(0, cand_ref.shape[0] // TILE)
+        rows_ref[:, 2 * c * part : (2 * c + 1) * part] = own[:, at]
+        rows_ref[:, (2 * c + 1) * part : (2 * c + 2) * part] = sib[:, at]
+    norms = row_norms(rows_ref[...])
+    down = lax.broadcasted_iota(jnp.int32, (live, 1), 0)
+    hit = jnp.max((chosen_ref[...] == down).astype(F32), axis=1, keepdims=True) > 0.5
+    outside = jnp.where(hit, 0.0, jnp.inf)
+
+    @pl.loop(0, cand_ref.shape[1] // TILE)
     def _(t):
         at = pl.ds(pl.multiple_of(t * TILE, TILE), TILE)
-        gaps = gaps_to(cand_ref[at, :], rows_ref, norms)
-        near_ref[:, at] = nearest(gaps) + norm_ref[:, at]
-        best_ref[:, at] = nearest(gaps + outside)
+        gaps = norms - 2.0 * product(rows_ref[...], cand_ref[:, at])
+        near_ref[:, at] = jnp.min(gaps, axis=0, keepdims=True) + norm_ref[:, at]
+        best_ref[:, at] = jnp.min(gaps + outside, axis=0, keepdims=True)
 
 
 def far_rows(size, held, sibs, rows_ref):
@@ -239,36 +222,39 @@
         rows_ref[to : to + rows, part:] = block[top : top + rows, :]
 
 
-def far_kernel(size, chunk, cand_ref, *refs):
-    before = refs[:1] if chunk else ()
-    *blocks, out, rows_ref = refs[len(before) :]
+def far_gaps(size, chunk, cand_ref, before, blocks, rows_ref, emit):
     far_rows(size, blocks[:2], blocks[2:], rows_ref)
     width = rows_ref.shape[1]
-    norms = lane_norms(rows_ref, width)
-
-    @pl.loop(0, cand_ref.shape[0] // TILE)
+    norms = row_norms(rows_ref[...])
+
+    @pl.loop(0, cand_ref.shape[1] // TILE)
     def _(t):
         at = pl.ds(pl.multiple_of(t * TILE, TILE), TILE)
-        gaps = gaps_to(cand_ref[at, chunk * width : (chunk + 1) * width], rows_ref, norms)
+        gaps = norms - 2.0 * product(
+            rows_ref[...], cand_ref[chunk * width : (chunk + 1) * width, at]
+        )
         for ref in before:
-            gaps += ref[at, :]
-        out[at, :] = gaps
+            gaps += ref[:, at]
+        emit(at, gaps)
+
+
+def far_kernel(size, chunk, cand_ref, *refs):
+    *before, mine, got, sib_mine, sib_got, out, rows_ref = refs
+
+    def emit(at, gaps):
+        out[:, at] = gaps
+
+    far_gaps(size, chunk, cand_ref, before, (mine, got, sib_mine, sib_got), rows_ref, emit)
 
 
 def last_kernel(size, chunk, cand_ref, best_ref, norm_ref, *refs):
-    before = refs[:1] if chunk else ()
-    *blocks, out, rows_ref = refs[len(before) :]
-    far_rows(size, blocks[:2], blocks[2:], rows_ref)
-    width = rows_ref.shape[1]
-    norms = lane_norms(rows_ref, width)
-
-    @pl.loop(0, cand_ref.shape[0] // TILE)
-    def _(t):
-        at = pl.ds(pl.multiple_of(t * TILE, TILE), TILE)
-        gaps = gaps_to(cand_ref[at, chunk * width : (chunk + 1) * width], rows_ref, norms)
-        for ref in before:
-            gaps += ref[at, :]
-        out[:, at] = jnp.minimum(nearest(gaps), best_ref[:, at]) + norm_ref[:, at]
+    *before, mine, got, sib_mine, sib_got, out, rows_ref = refs
+
+    def emit(at, gaps):
+        least = jnp.minimum(jnp.min(gaps, axis=0, keepdims=True), best_ref[:, at])
+        out[:, at] = least + norm_ref[:, at]
+
+    far_gaps(size, chunk, cand_ref, before, (mine, got, sib_mine, sib_got), rows_ref, emit)
 
 
 def body(candidates, round_one, counts, chosen):
@@ -285,21 +271,20 @@
 
     line = jax.ShapeDtypeStruct((1, rows), F32)
     keep, send = call(
-        mark_kernel, "mark", [bf16(slots, half)] * 2, (counts, round_one),
-        specs=[pl.BlockSpec(memory_space=pltpu.SMEM)] + vmem_specs(1),
+        mark_kernel, "mark", [bf16(slots, half)] * 2, (counts, round_one)
     )
     other = core_permute(send, size)
 
-    def join(blocks, columns, start=0, after=(), weight=0):
+    def join(blocks, columns, start=0, after=()):
         count = blocks[0].shape[0] * len(blocks)
         return call(
             functools.partial(join_kernel, len(blocks), start), "join", bf16(count, columns),
-            blocks, weight, after=after,
+            blocks, after=after,
         )
 
-    def double(block, got, stages, after=(), weight=0):
+    def double(block, got, stages, after=()):
         for stage in stages:
-            block = join((block, got), block.shape[1], after=after, weight=weight)
+            block = join((block, got), block.shape[1], after=after)
             got = mixed_permute(block, size, stage)
         return block, got
 
@@ -308,9 +293,13 @@
     got = [mixed_permute(block, size, 0) for block in first]
     raw = [double(first[0], got[0], stages)]
     cand, norm = call(
-        load_kernel, "load", [bf16(rows, width), line], (candidates,),
+        load_kernel, "load", [bf16(width, rows), line], (candidates,),
         specs=[pl.BlockSpec(memory_space=pltpu.HBM)], after=raw[0][:1],
-        scratch=[pltpu.SemaphoreType.DMA((rows // TILE * 2 * CHUNKS,))], limit=42 * MIB,
+        scratch=[
+            pltpu.VMEM((rows, width), BF16),
+            pltpu.SemaphoreType.DMA((rows // TILE * 2 * CHUNKS,)),
+        ],
+        limit=42 * MIB,
     )
     raw += [double(f, g, stages, after=(norm,)) for f, g in zip(first[1:], got[1:])]
 
@@ -343,21 +332,21 @@
         block = join(shifted[c], part, after=() if c else (picked,))
         got = mixed_permute(block, size, 0)
         if c == CHUNKS - 1:
-            own = call(beside_kernel, "beside", bf16(live, half), dense)
+            own = call(beside_kernel, "beside", bf16(live, half), dense, after=(block,))
             near, best = call(
                 functools.partial(group_kernel, picks), "group", [line] * 2,
                 (cand, norm, chosen, own, core_permute(own, size)), 2 * rows * live * width,
-                scratch=[pltpu.VMEM((-(-live // 128) * 128, width), BF16)], after=(block,),
-            )
-        weight = WEIGHT if c < CHUNKS - 1 else 0
-        mine, got = double(block, got, stages, after=(best,) if best is not None else (), weight=weight)
+                scratch=[pltpu.VMEM((live, width), BF16)],
+            )
+        after = (best,) if c == CHUNKS - 1 else shifted[c + 1]
+        mine, got = double(block, got, stages, after=after)
         sent = join((got,), part, after=before) if before else got
         blocks = (mine, got, core_permute(mine, size), core_permute(sent, size))
         if c < CHUNKS - 1:
             before = (
                 call(
                     functools.partial(far_kernel, size, c), "far",
-                    jax.ShapeDtypeStruct((rows, centers), F32), (cand, *before, *blocks), flops,
+                    jax.ShapeDtypeStruct((centers, rows), F32), (cand, *before, *blocks), flops,
                     scratch=scratch,
                 ),
             )

time: 68.8 us -> 69 us (level)
  Pallas kernels: 18.6 us -> 20.5 us
  waiting for transfers between devices: 25.6 us -> 23.9 us
    ppermute x6, waiting for transfers between devices: 7.51 us -> 3.72 us  [body(): lax.ppermute(picked, 'grp', [(g, (g + k) % groups) for g in range(groups)])]
    ppermute x8, waiting for transfers between devices: 15.3 us -> 17.3 us  [mixed_permute(): lax.ppermute(block, 'mem', [(m, m ^ (odd if m & 1 else even)) for m in ra...]
    pallas_call x17, Pallas kernels: 18.6 us -> 20.5 us  [call(): pl.pallas_call(run, out_shape=out_shape, in_specs=(specs or vmem_specs(co...]
  transfers between devices with their start and end apart: 20 -> 20, of which waited for: 11 -> 12; matrix products, arithmetic and copies ran while one was open for 0% -> 0% of each run, Pallas kernels for 19% -> 23%
where the time goes in v7:
time: 69 us; the launch traced here: 68.8 us
  waiting for transfers between devices  23.9 us (35%)
  starting transfers between devices  21.5 us (31%)
  Pallas kernels  20.5 us (30%)
  local copies, waits for them, and re-layouts  1.55 us (2%)
  between operations  1.42 us (2%)
    pallas_call x17, Pallas kernels, call(): pl.pallas_call(run, out_shape=out_shape, in_specs=(specs or vmem_specs(co...  20.5 us
    ppermute x8, waiting for transfers between devices, mixed_permute(): lax.ppermute(block, 'mem', [(m, m ^ (odd if m & 1 else even)) for m in ra...  17.3 us
    ppermute x8, starting transfers between devices, mixed_permute(): lax.ppermute(block, 'mem', [(m, m ^ (odd if m & 1 else even)) for m in ra...  11 us
    ppermute x6, starting transfers between devices, body(): lax.ppermute(picked, 'grp', [(g, (g + k) % groups) for g in range(groups)])  9.79 us
    ppermute x6, waiting for transfers between devices, body(): lax.ppermute(picked, 'grp', [(g, (g + k) % groups) for g in range(groups)])  3.72 us
    ppermute x6, waiting for transfers between devices, core_permute(): return lax.ppermute(block, 'mem', [(m, m ^ 1) for m in range(size)])  2.87 us
    unnamed x4, local copies, waits for them, and re-layouts  1.55 us
  transfers between devices with their start and end apart: 20, of which 12 were waited for; matrix products, arithmetic and copies ran while one was open for 0% of the time, Pallas kernels for 23%

profile of v7, /device:TPU:0, one launch (start us, length us, event | category | flops | bytes accessed | tf_op | source)
XLA Modules:
  0.0 68.8 jit_solution(17700334686650966411)
XLA Ops:
  1.3 1.0 %copy-done = bf16[64,4096]{1,0:T(8,128)(2,1)S(1)} copy-done((bf16[64,4096]{1,0:T(8,128)(2,1)S(1)}, bf16[64,4096]{1,0:T(8,128)(2,1)}, u32[]{:S(2)}) %copy-start) | copy-done | bytes 524312
  2.9 1.2 %collective-permute-done.refs_1_ = bf16[64,2048]{1,0:T(8,128)(2,1)S(1)} collective-permute-done((bf16[64,2048]{1,0:T(8,128)(2,1)S(1)}, bf16[64,2048]{1,0:T(8,128)(2,1)S(1)}, u32[]{:S(2)}, u32[]{:S(2)}) %collective-permute-start) | collective-permute-done | bytes 262176 | tf_op jit(solution)/shard_map/ppermute | solution.py:32
  4.1 2.9 %collective-permute-start.1 = (bf16[128,1024]{1,0:T(8,128)(2,1)S(1)}, bf16[128,1024]{1,0:T(8,128)(2,1)S(1)}, u32[]{:S(2)}, u32[]{:S(2)}) collective-permute-start(bf16[128,1024]{1,0:T(8,128)(2,1)S(1)} %join.9.refs_0_), channel_id=1, source_target_pairs={{0,2},{1,5},{2,0},{3,7},{4,6},{5,1},{6,4},{7,3},{8,10},{9,13},{10,... | collective-permute-start | bytes 786440 | tf_op jit(solution)/shard_map/ppermute | solution.py:28
  7.1 4.2 %collective-permute-done.1.refs_1_ = bf16[128,1024]{1,0:T(8,128)(2,1)S(1)} collective-permute-done((bf16[128,1024]{1,0:T(8,128)(2,1)S(1)}, bf16[128,1024]{1,0:T(8,128)(2,1)S(1)}, u32[]{:S(2)}, u32[]{:S(2)}) %collective-permute-start.1) | collective-permute-done | bytes 262176 | tf_op jit(solution)/shard_map/ppermute | solution.py:28
  11.4 2.1 %collective-permute-start.2 = (bf16[256,1024]{1,0:T(8,128)(2,1)S(1)}, bf16[256,1024]{1,0:T(8,128)(2,1)S(1)}, u32[]{:S(2)}, u32[]{:S(2)}) collective-permute-start(bf16[256,1024]{1,0:T(8,128)(2,1)S(1)} %join.10.refs_1_), channel_id=1, source_target_pairs={{0,4},{1,3},{2,6},{3,1},{4,0},{5,7},{6,2},{7,5},{8,12},{9,11},{10,... | collective-permute-start | bytes 1572872 | tf_op jit(solution)/shard_map/ppermute | solution.py:28
  13.5 8.1 %load.1 = (bf16[4096,1024]{1,0:T(8,128)(2,1)S(1)}, f32[1,1024]{1,0:T(1,128)S(1)}) custom-call(bf16[1024,4096]{1,0:T(8,128)(2,1)} %refs_0_.3, bf16[256,1024]{1,0:T(8,128)(2,1)S(1)} %join.10.refs_1_), custom_call_target="tpu_custom_call" | custom-call | flops 10000000000 | bytes 16781312 | tf_op jit(solution)/shard_map/load/pallas_call | solution.py:60
  22.3 1.1 %pick_first.1 = (bf16[32,1024]{1,0:T(8,128)(2,1)S(1)}, bf16[192,1024]{1,0:T(8,128)(2,1)S(1)}, bf16[224,512]{1,0:T(8,128)(2,1)S(1)}) custom-call(s32[1,128]{1,0:T(1,128)S(1)} %copy-done.1, bf16[256,1024]{1,0:T(8,128)(2,1)S(1)} %join.10.refs_1_, bf16[256,1024]{1,0:T(8,128)(2,1)S(1)} %collective-permute-done.2.refs_2_, ...), custom_call_target="tpu_custom_call" | custom-call | flops 10000000000 | bytes 1737216 | tf_op jit(solution)/shard_map/pick_first/pallas_call | solution.py:60
  23.5 1.6 %collective-permute-start.5 = (bf16[32,1024]{1,0:T(8,128)(2,1)S(1)}, bf16[32,1024]{1,0:T(8,128)(2,1)S(1)}, u32[]{:S(2)}, u32[]{:S(2)}) collective-permute-start(bf16[32,1024]{1,0:T(8,128)(2,1)S(1)} %get-tuple-element.19), channel_id=1, source_target_pairs={{0,8},{8,16},{16,24},{24,0},{1,9},{9,17},{17,25},{25,1},{2,10},{10... | collective-permute-start | bytes 196616 | tf_op jit(solution)/shard_map/ppermute | solution.py:323
  25.1 2.6 %collective-permute-start.6 = (bf16[32,1024]{1,0:T(8,128)(2,1)S(1)}, bf16[32,1024]{1,0:T(8,128)(2,1)S(1)}, u32[]{:S(2)}, u32[]{:S(2)}) collective-permute-start(bf16[32,1024]{1,0:T(8,128)(2,1)S(1)} %get-tuple-element.19), channel_id=1, source_target_pairs={{0,16},{8,24},{16,0},{24,8},{1,17},{9,25},{17,1},{25,9},{2,18},{10... | collective-permute-start | bytes 196616 | tf_op jit(solution)/shard_map/ppermute | solution.py:323
  27.7 1.3 %collective-permute-start.7 = (bf16[32,1024]{1,0:T(8,128)(2,1)S(1)}, bf16[32,1024]{1,0:T(8,128)(2,1)S(1)}, u32[]{:S(2)}, u32[]{:S(2)}) collective-permute-start(bf16[32,1024]{1,0:T(8,128)(2,1)S(1)} %get-tuple-element.19), channel_id=1, source_target_pairs={{0,24},{8,0},{16,8},{24,16},{1,25},{9,1},{17,9},{25,17},{2,26},{10... | collective-permute-start | bytes 196616 | tf_op jit(solution)/shard_map/ppermute | solution.py:323
  29.0 1.9 %collective-permute-done.4.refs_2_ = bf16[256,1024]{1,0:T(8,128)(2,1)S(1)} collective-permute-done((bf16[256,1024]{1,0:T(8,128)(2,1)S(1)}, bf16[256,1024]{1,0:T(8,128)(2,1)S(1)}, u32[]{:S(2)}, u32[]{:S(2)}) %collective-permute-start.4) | collective-permute-done | bytes 524320 | tf_op jit(solution)/shard_map/ppermute | solution.py:28
  34.1 2.5 %collective-permute-start.9 = (bf16[32,1024]{1,0:T(8,128)(2,1)S(1)}, bf16[32,1024]{1,0:T(8,128)(2,1)S(1)}, u32[]{:S(2)}, u32[]{:S(2)}) collective-permute-start(bf16[32,1024]{1,0:T(8,128)(2,1)S(1)} %get-tuple-element.21.refs_3_), channel_id=1, source_target_pairs={{0,16},{8,24},{16,0},{24,8},{1,17},{9,25},{17,1},{25,9},{2,18},{10... | collective-permute-start | bytes 196616 | tf_op jit(solution)/shard_map/ppermute | solution.py:323
  37.5 1.6 %collective-permute-start.12 = (bf16[96,1024]{1,0:T(8,128)(2,1)S(1)}, bf16[96,1024]{1,0:T(8,128)(2,1)S(1)}, u32[]{:S(2)}, u32[]{:S(2)}) collective-permute-start(bf16[96,1024]{1,0:T(8,128)(2,1)S(1)} %join.14.refs_0_), channel_id=1, source_target_pairs={{0,2},{1,5},{2,0},{3,7},{4,6},{5,1},{6,4},{7,3},{8,10},{9,13},{10,... | collective-permute-start | bytes 589832 | tf_op jit(solution)/shard_map/ppermute | solution.py:28
  39.5 1.3 %collective-permute-done.9.refs_1_.refs_3_ = bf16[32,1024]{1,0:T(8,128)(2,1)S(1)} collective-permute-done((bf16[32,1024]{1,0:T(8,128)(2,1)S(1)}, bf16[32,1024]{1,0:T(8,128)(2,1)S(1)}, u32[]{:S(2)}, u32[]{:S(2)}) %collective-permute-start.9) | collective-permute-done | bytes 65568 | tf_op jit(solution)/shard_map/ppermute | solution.py:323
  41.6 1.7 %collective-permute-done.12.refs_1_ = bf16[96,1024]{1,0:T(8,128)(2,1)S(1)} collective-permute-done((bf16[96,1024]{1,0:T(8,128)(2,1)S(1)}, bf16[96,1024]{1,0:T(8,128)(2,1)S(1)}, u32[]{:S(2)}, u32[]{:S(2)}) %collective-permute-start.12) | collective-permute-done | bytes 196640 | tf_op jit(solution)/shard_map/ppermute | solution.py:28
  43.3 1.2 %collective-permute-start.13 = (bf16[192,1024]{1,0:T(8,128)(2,1)S(1)}, bf16[192,1024]{1,0:T(8,128)(2,1)S(1)}, u32[]{:S(2)}, u32[]{:S(2)}) collective-permute-start(bf16[192,1024]{1,0:T(8,128)(2,1)S(1)} %join.15.refs_1_), channel_id=1, source_target_pairs={{0,4},{1,3},{2,6},{3,1},{4,0},{5,7},{6,2},{7,5},{8,12},{9,11},{10,... | collective-permute-start | bytes 1179656 | tf_op jit(solution)/shard_map/ppermute | solution.py:28
  44.5 1.5 %collective-permute-start.16 = (bf16[96,1024]{1,0:T(8,128)(2,1)S(1)}, bf16[96,1024]{1,0:T(8,128)(2,1)S(1)}, u32[]{:S(2)}, u32[]{:S(2)}) collective-permute-start(bf16[96,1024]{1,0:T(8,128)(2,1)S(1)} %join.13.refs_2_.refs_0_), channel_id=1, source_target_pairs={{0,2},{1,5},{2,0},{3,7},{4,6},{5,1},{6,4},{7,3},{8,10},{9,13},{10,... | collective-permute-start | bytes 589832 | tf_op jit(solution)/shard_map/ppermute | solution.py:28
  45.9 6.0 %collective-permute-done.13.refs_2_ = bf16[192,1024]{1,0:T(8,128)(2,1)S(1)} collective-permute-done((bf16[192,1024]{1,0:T(8,128)(2,1)S(1)}, bf16[192,1024]{1,0:T(8,128)(2,1)S(1)}, u32[]{:S(2)}, u32[]{:S(2)}) %collective-permute-start.13) | collective-permute-done | bytes 393248 | tf_op jit(solution)/shard_map/ppermute | solution.py:28
  52.0 3.6 %group.1 = (f32[1,1024]{1,0:T(1,128)}, f32[1,1024]{1,0:T(1,128)S(1)}) custom-call(bf16[4096,1024]{1,0:T(8,128)(2,1)S(1)} %get-tuple-element.15.refs_0_, f32[1,1024]{1,0:T(1,128)S(1)} %get-tuple-element.16.refs_3_.refs_2_.refs_1_, s32[1,128]{1,0:T(1,128)S(1)} %copy-done.1, bf16[192,2048]{1,0:T(8,128)(2,1)S(1)} %beside.1.refs_3_, ...), custom_call_target="tpu_custom_call" | custom-call | flops 10000000000 | bytes 9974272 | tf_op jit(solution)/shard_map/group/pallas_call | solution.py:60
  55.6 1.6 %collective-permute-start.17 = (bf16[192,1024]{1,0:T(8,128)(2,1)S(1)}, bf16[192,1024]{1,0:T(8,128)(2,1)S(1)}, u32[]{:S(2)}, u32[]{:S(2)}) collective-permute-start(bf16[192,1024]{1,0:T(8,128)(2,1)S(1)} %join.16.refs_4_), channel_id=1, source_target_pairs={{0,4},{1,3},{2,6},{3,1},{4,0},{5,7},{6,2},{7,5},{8,12},{9,11},{10,... | collective-permute-start | bytes 1179656 | tf_op jit(solution)/shard_map/ppermute | solution.py:28
  57.2 2.8 %far.1.refs_1_.refs_3_ = f32[384,1024]{1,0:T(8,128)S(1)} custom-call(bf16[4096,1024]{1,0:T(8,128)(2,1)S(1)} %get-tuple-element.15.refs_0_, bf16[192,1024]{1,0:T(8,128)(2,1)S(1)} %join.15.refs_1_, bf16[192,1024]{1,0:T(8,128)(2,1)S(1)} %collective-permute-done.13.refs_2_, bf16[192,1024]{1,0:T(8,128)(2,1)S(1)} %collective-permute-done.14.refs_3_, ...), custom_call_target="tpu_custom_call" | custom-call | flops 10000000000 | bytes 11534336 | tf_op jit(solution)/shard_map/far/pallas_call | solution.py:60
  60.1 3.4 %collective-permute-done.17.refs_0_.refs_5_ = bf16[192,1024]{1,0:T(8,128)(2,1)S(1)} collective-permute-done((bf16[192,1024]{1,0:T(8,128)(2,1)S(1)}, bf16[192,1024]{1,0:T(8,128)(2,1)S(1)}, u32[]{:S(2)}, u32[]{:S(2)}) %collective-permute-start.17) | collective-permute-done | bytes 393248 | tf_op jit(solution)/shard_map/ppermute | solution.py:28
  63.6 1.7 %collective-permute-done.19.refs_7_ = bf16[192,1024]{1,0:T(8,128)(2,1)S(1)} collective-permute-done((bf16[192,1024]{1,0:T(8,128)(2,1)S(1)}, bf16[192,1024]{1,0:T(8,128)(2,1)S(1)}, u32[]{:S(2)}, u32[]{:S(2)}) %collective-permute-start.19) | collective-permute-done | bytes 393248 | tf_op jit(solution)/shard_map/ppermute | solution.py:32
  65.3 3.5 %far_last.1 = f32[1,1024]{1,0:T(1,128)} custom-call(bf16[4096,1024]{1,0:T(8,128)(2,1)S(1)} %get-tuple-element.15.refs_0_, f32[1,1024]{1,0:T(1,128)S(1)} %get-tuple-element.23.refs_2_.refs_1_, f32[1,1024]{1,0:T(1,128)S(1)} %get-tuple-element.16.refs_3_.refs_2_.refs_1_, f32[384,1024]{1,0:T(8,128)S(1)} %far.1.refs_1_.refs_3_, ...), custom_call_target="tpu_custom_call" | custom-call | flops 10000000000 | bytes 11546624 | tf_op jit(solution)/shard_map/far_last/pallas_call | solution.py:60
  (37 shorter events, 6.7 us)
Async XLA Ops:
  1.3 1.0 %copy-start = (bf16[64,4096]{1,0:T(8,128)(2,1)S(1)}, bf16[64,4096]{1,0:T(8,128)(2,1)}, u32[]{:S(2)}) copy-start(bf16[64,4096]{1,0:T(8,128)(2,1)} %refs_1_.1) | copy-start | bytes 1572868
  2.4 1.7 %collective-permute-start = (bf16[64,2048]{1,0:T(8,128)(2,1)S(1)}, bf16[64,2048]{1,0:T(8,128)(2,1)S(1)}, u32[]{:S(2)}, u32[]{:S(2)}) collective-permute-start(bf16[64,2048]{1,0:T(8,128)(2,1)S(1)} %get-tuple-element.14), channel_id=1, source_target_pairs={{0,1},{1,0},{2,3},{3,2},{4,5},{5,4},{6,7},{7,6},{8,9},{9,8},{10,11... | collective-permute-start | bytes 786440 | tf_op jit(solution)/shard_map/ppermute | solution.py:32
  4.1 7.3 %collective-permute-start.1 = (bf16[128,1024]{1,0:T(8,128)(2,1)S(1)}, bf16[128,1024]{1,0:T(8,128)(2,1)S(1)}, u32[]{:S(2)}, u32[]{:S(2)}) collective-permute-start(bf16[128,1024]{1,0:T(8,128)(2,1)S(1)} %join.9.refs_0_), channel_id=1, source_target_pairs={{0,2},{1,5},{2,0},{3,7},{4,6},{5,1},{6,4},{7,3},{8,10},{9,13},{10,... | collective-permute-start | bytes 786440 | tf_op jit(solution)/shard_map/ppermute | solution.py:28
  7.0 14.6 %collective-permute-start.3 = (bf16[128,1024]{1,0:T(8,128)(2,1)S(1)}, bf16[128,1024]{1,0:T(8,128)(2,1)S(1)}, u32[]{:S(2)}, u32[]{:S(2)}) collective-permute-start(bf16[128,1024]{1,0:T(8,128)(2,1)S(1)} %join.11.refs_0_), channel_id=1, source_target_pairs={{0,2},{1,5},{2,0},{3,7},{4,6},{5,1},{6,4},{7,3},{8,10},{9,13},{10,... | collective-permute-start | bytes 786440 | tf_op jit(solution)/shard_map/ppermute | solution.py:28
  11.4 10.4 %collective-permute-start.2 = (bf16[256,1024]{1,0:T(8,128)(2,1)S(1)}, bf16[256,1024]{1,0:T(8,128)(2,1)S(1)}, u32[]{:S(2)}, u32[]{:S(2)}) collective-permute-start(bf16[256,1024]{1,0:T(8,128)(2,1)S(1)} %join.10.refs_1_), channel_id=1, source_target_pairs={{0,4},{1,3},{2,6},{3,1},{4,0},{5,7},{6,2},{7,5},{8,12},{9,11},{10,... | collective-permute-start | bytes 1572872 | tf_op jit(solution)/shard_map/ppermute | solution.py:28
  21.7 0.7 copy-start.1
  21.7 9.2 %collective-permute-start.4 = (bf16[256,1024]{1,0:T(8,128)(2,1)S(1)}, bf16[256,1024]{1,0:T(8,128)(2,1)S(1)}, u32[]{:S(2)}, u32[]{:S(2)}) collective-permute-start(bf16[256,1024]{1,0:T(8,128)(2,1)S(1)} %join.12.refs_1_), channel_id=1, source_target_pairs={{0,4},{1,3},{2,6},{3,1},{4,0},{5,7},{6,2},{7,5},{8,12},{9,11},{10,... | collective-permute-start | bytes 1572872 | tf_op jit(solution)/shard_map/ppermute | solution.py:28
  23.5 7.5 %collective-permute-start.5 = (bf16[32,1024]{1,0:T(8,128)(2,1)S(1)}, bf16[32,1024]{1,0:T(8,128)(2,1)S(1)}, u32[]{:S(2)}, u32[]{:S(2)}) collective-permute-start(bf16[32,1024]{1,0:T(8,128)(2,1)S(1)} %get-tuple-element.19), channel_id=1, source_target_pairs={{0,8},{8,16},{16,24},{24,0},{1,9},{9,17},{17,25},{25,1},{2,10},{10... | collective-permute-start | bytes 196616 | tf_op jit(solution)/shard_map/ppermute | solution.py:323
  25.1 6.9 %collective-permute-start.6 = (bf16[32,1024]{1,0:T(8,128)(2,1)S(1)}, bf16[32,1024]{1,0:T(8,128)(2,1)S(1)}, u32[]{:S(2)}, u32[]{:S(2)}) collective-permute-start(bf16[32,1024]{1,0:T(8,128)(2,1)S(1)} %get-tuple-element.19), channel_id=1, source_target_pairs={{0,16},{8,24},{16,0},{24,8},{1,17},{9,25},{17,1},{25,9},{2,18},{10... | collective-permute-start | bytes 196616 | tf_op jit(solution)/shard_map/ppermute | solution.py:323
  27.7 4.6 %collective-permute-start.7 = (bf16[32,1024]{1,0:T(8,128)(2,1)S(1)}, bf16[32,1024]{1,0:T(8,128)(2,1)S(1)}, u32[]{:S(2)}, u32[]{:S(2)}) collective-permute-start(bf16[32,1024]{1,0:T(8,128)(2,1)S(1)} %get-tuple-element.19), channel_id=1, source_target_pairs={{0,24},{8,0},{16,8},{24,16},{1,25},{9,1},{17,9},{25,17},{2,26},{10... | collective-permute-start | bytes 196616 | tf_op jit(solution)/shard_map/ppermute | solution.py:323
  33.2 6.2 %collective-permute-start.8 = (bf16[32,1024]{1,0:T(8,128)(2,1)S(1)}, bf16[32,1024]{1,0:T(8,128)(2,1)S(1)}, u32[]{:S(2)}, u32[]{:S(2)}) collective-permute-start(bf16[32,1024]{1,0:T(8,128)(2,1)S(1)} %get-tuple-element.21.refs_3_), channel_id=1, source_target_pairs={{0,8},{8,16},{16,24},{24,0},{1,9},{9,17},{17,25},{25,1},{2,10},{10... | collective-permute-start | bytes 196616 | tf_op jit(solution)/shard_map/ppermute | solution.py:323
  34.1 6.6 %collective-permute-start.9 = (bf16[32,1024]{1,0:T(8,128)(2,1)S(1)}, bf16[32,1024]{1,0:T(8,128)(2,1)S(1)}, u32[]{:S(2)}, u32[]{:S(2)}) collective-permute-start(bf16[32,1024]{1,0:T(8,128)(2,1)S(1)} %get-tuple-element.21.refs_3_), channel_id=1, source_target_pairs={{0,16},{8,24},{16,0},{24,8},{1,17},{9,25},{17,1},{25,9},{2,18},{10... | collective-permute-start | bytes 196616 | tf_op jit(solution)/shard_map/ppermute | solution.py:323
  36.7 4.8 %collective-permute-start.10 = (bf16[32,1024]{1,0:T(8,128)(2,1)S(1)}, bf16[32,1024]{1,0:T(8,128)(2,1)S(1)}, u32[]{:S(2)}, u32[]{:S(2)}) collective-permute-start(bf16[32,1024]{1,0:T(8,128)(2,1)S(1)} %get-tuple-element.21.refs_3_), channel_id=1, source_target_pairs={{0,24},{8,0},{16,8},{24,16},{1,25},{9,1},{17,9},{25,17},{2,26},{10... | collective-permute-start | bytes 196616 | tf_op jit(solution)/shard_map/ppermute | solution.py:323
  37.5 5.7 %collective-permute-start.12 = (bf16[96,1024]{1,0:T(8,128)(2,1)S(1)}, bf16[96,1024]{1,0:T(8,128)(2,1)S(1)}, u32[]{:S(2)}, u32[]{:S(2)}) collective-permute-start(bf16[96,1024]{1,0:T(8,128)(2,1)S(1)} %join.14.refs_0_), channel_id=1, source_target_pairs={{0,2},{1,5},{2,0},{3,7},{4,6},{5,1},{6,4},{7,3},{8,10},{9,13},{10,... | collective-permute-start | bytes 589832 | tf_op jit(solution)/shard_map/ppermute | solution.py:28
  41.5 10.5 %collective-permute-start.11 = (bf16[192,2048]{1,0:T(8,128)(2,1)S(1)}, bf16[192,2048]{1,0:T(8,128)(2,1)S(1)}, u32[]{:S(2)}, u32[]{:S(2)}) collective-permute-start(bf16[192,2048]{1,0:T(8,128)(2,1)S(1)} %beside.1.refs_3_), channel_id=1, source_target_pairs={{0,1},{1,0},{2,3},{3,2},{4,5},{5,4},{6,7},{7,6},{8,9},{9,8},{10,11... | collective-permute-start | bytes 2359304 | tf_op jit(solution)/shard_map/ppermute | solution.py:32
  43.3 8.7 %collective-permute-start.13 = (bf16[192,1024]{1,0:T(8,128)(2,1)S(1)}, bf16[192,1024]{1,0:T(8,128)(2,1)S(1)}, u32[]{:S(2)}, u32[]{:S(2)}) collective-permute-start(bf16[192,1024]{1,0:T(8,128)(2,1)S(1)} %join.15.refs_1_), channel_id=1, source_target_pairs={{0,4},{1,3},{2,6},{3,1},{4,0},{5,7},{6,2},{7,5},{8,12},{9,11},{10,... | collective-permute-start | bytes 1179656 | tf_op jit(solution)/shard_map/ppermute | solution.py:28
  44.5 11.1 %collective-permute-start.16 = (bf16[96,1024]{1,0:T(8,128)(2,1)S(1)}, bf16[96,1024]{1,0:T(8,128)(2,1)S(1)}, u32[]{:S(2)}, u32[]{:S(2)}) collective-permute-start(bf16[96,1024]{1,0:T(8,128)(2,1)S(1)} %join.13.refs_2_.refs_0_), channel_id=1, source_target_pairs={{0,2},{1,5},{2,0},{3,7},{4,6},{5,1},{6,4},{7,3},{8,10},{9,13},{10,... | collective-permute-start | bytes 589832 | tf_op jit(solution)/shard_map/ppermute | solution.py:28
  45.9 11.3 %collective-permute-start.14 = (bf16[192,1024]{1,0:T(8,128)(2,1)S(1)}, bf16[192,1024]{1,0:T(8,128)(2,1)S(1)}, u32[]{:S(2)}, u32[]{:S(2)}) collective-permute-start(bf16[192,1024]{1,0:T(8,128)(2,1)S(1)} %join.15.refs_1_), channel_id=1, source_target_pairs={{0,1},{1,0},{2,3},{3,2},{4,5},{5,4},{6,7},{7,6},{8,9},{9,8},{10,11... | collective-permute-start | bytes 1179656 | tf_op jit(solution)/shard_map/ppermute | solution.py:32
  52.0 5.2 %collective-permute-start.15 = (bf16[192,1024]{1,0:T(8,128)(2,1)S(1)}, bf16[192,1024]{1,0:T(8,128)(2,1)S(1)}, u32[]{:S(2)}, u32[]{:S(2)}) collective-permute-start(bf16[192,1024]{1,0:T(8,128)(2,1)S(1)} %collective-permute-done.13.refs_2_), channel_id=1, source_target_pairs={{0,1},{1,0},{2,3},{3,2},{4,5},{5,4},{6,7},{7,6},{8,9},{9,8},{10,11... | collective-permute-start | bytes 1179656 | tf_op jit(solution)/shard_map/ppermute | solution.py:32
  55.6 7.8 %collective-permute-start.17 = (bf16[192,1024]{1,0:T(8,128)(2,1)S(1)}, bf16[192,1024]{1,0:T(8,128)(2,1)S(1)}, u32[]{:S(2)}, u32[]{:S(2)}) collective-permute-start(bf16[192,1024]{1,0:T(8,128)(2,1)S(1)} %join.16.refs_4_), channel_id=1, source_target_pairs={{0,4},{1,3},{2,6},{3,1},{4,0},{5,7},{6,2},{7,5},{8,12},{9,11},{10,... | collective-permute-start | bytes 1179656 | tf_op jit(solution)/shard_map/ppermute | solution.py:28
  57.2 6.4 %collective-permute-start.18 = (bf16[192,1024]{1,0:T(8,128)(2,1)S(1)}, bf16[192,1024]{1,0:T(8,128)(2,1)S(1)}, u32[]{:S(2)}, u32[]{:S(2)}) collective-permute-start(bf16[192,1024]{1,0:T(8,128)(2,1)S(1)} %join.16.refs_4_), channel_id=1, source_target_pairs={{0,1},{1,0},{2,3},{3,2},{4,5},{5,4},{6,7},{7,6},{8,9},{9,8},{10,11... | collective-permute-start | bytes 1179656 | tf_op jit(solution)/shard_map/ppermute | solution.py:32
  63.5 1.8 %collective-permute-start.19 = (bf16[192,1024]{1,0:T(8,128)(2,1)S(1)}, bf16[192,1024]{1,0:T(8,128)(2,1)S(1)}, u32[]{:S(2)}, u32[]{:S(2)}) collective-permute-start(bf16[192,1024]{1,0:T(8,128)(2,1)S(1)} %join.17), channel_id=1, source_target_pairs={{0,1},{1,0},{2,3},{3,2},{4,5},{5,4},{6,7},{7,6},{8,9},{9,8},{10,11... | collective-permute-start | bytes 1179656 | tf_op jit(solution)/shard_map/ppermute | solution.py:32

commit v8 on v7

v8 whole, which is shorter than its diff:
```python
import functools

import jax
import jax.numpy as jnp
from jax import lax
from jax.experimental import pallas as pl
from jax.experimental.pallas import tpu as pltpu
from jax.sharding import PartitionSpec as P

CHUNKS = 2
TILE = 256
MIB = 1024 * 1024
WEIGHT = 10**10
F32, BF16 = jnp.float32, jnp.bfloat16


def chip_bits(size):
    return [1 << b for b in range(1, size.bit_length() - 1)]


def crossing(size, odd):
    return chip_bits(size)[::-1] if odd else chip_bits(size)


def mixed_permute(block, size, stage):
    even, odd = crossing(size, False)[stage], crossing(size, True)[stage]
    return lax.ppermute(block, "mem", [(m, m ^ (odd if m & 1 else even)) for m in range(size)])


def core_permute(block, size):
    return lax.ppermute(block, "mem", [(m, m ^ 1) for m in range(size)])


def block_flips(size, odd):
    flips = [0]
    for bit in crossing(size, odd):
        flips = flips + [f ^ bit for f in flips]
    return flips


def sibling_place(index, size):
    return block_flips(size, True).index(block_flips(size, False)[index])


def vmem_specs(count):
    return [pl.BlockSpec(memory_space=pltpu.VMEM)] * count


def call(kernel, name, out_shape, operands, specs=None, scratch=(), after=(), limit=28 * MIB, weight=WEIGHT):
    shapes = jax.tree.leaves(out_shape)
    moved = sum(a.size * a.dtype.itemsize for a in list(operands) + shapes)
    count = len(operands)

    def run(*refs):
        kernel(*refs[:count], *refs[count + len(after) :])

    return pl.pallas_call(
        run,
        out_shape=out_shape,
        in_specs=(specs or vmem_specs(count)) + [pl.BlockSpec(memory_space=pl.ANY)] * len(after),
        out_specs=jax.tree.map(lambda _: pl.BlockSpec(memory_space=pltpu.VMEM), out_shape),
        scratch_shapes=scratch,
        compiler_params=pltpu.CompilerParams(vmem_limit_bytes=limit),
        cost_estimate=pl.CostEstimate(flops=weight, bytes_accessed=moved, transcendentals=0),
        name=name,
    )(*operands, *after)


def spread_kernel(count_ref, out):
    out[...] = jnp.broadcast_to(count_ref[0, 0], out.shape)


def pair_kernel(own, sib, out):
    lane = lax.broadcasted_iota(jnp.int32, out.shape, 1)
    out[...] = jnp.where(lane == 0, own[...], sib[...])


def split_kernel(rows_ref, keep_ref, send_ref):
    half = keep_ref.shape[1]
    core = lax.rem(lax.axis_index("mem"), 2)
    keep_ref[...] = rows_ref[:, pl.ds(pl.multiple_of(core * half, half), half)]
    send_ref[...] = rows_ref[:, pl.ds(pl.multiple_of((1 - core) * half, half), half)]


def load_kernel(cand_hbm, cand_ref, norm_ref, sems):
    half = cand_ref.shape[1] // 2
    part = half // CHUNKS
    core = lax.rem(lax.axis_index("mem"), 2)
    tiles = cand_ref.shape[0] // TILE
    copies = []
    for t in range(tiles):
        at = pl.ds(t * TILE, TILE)
        for p in range(2 * CHUNKS):
            own = core if p % 2 == 0 else 1 - core
            start = pl.multiple_of(own * half + p // 2 * part, part)
            copies.append(
                pltpu.make_async_copy(
                    cand_hbm.at[at, pl.ds(start, part)],
                    cand_ref.at[at, pl.ds(p * part, part)],
                    sems.at[len(copies)],
                )
            )
    for copy in copies:
        copy.start()
    for t in range(tiles):
        for copy in copies[t * 2 * CHUNKS : (t + 1) * 2 * CHUNKS]:
            copy.wait()
        squares = jnp.zeros((TILE, 128), F32)
        for k in range(0, cand_ref.shape[1], 128):
            entries = cand_ref[t * TILE : (t + 1) * TILE, k : k + 128].astype(F32)
            squares += entries * entries
        norm_ref[:, t * TILE : (t + 1) * TILE] = jnp.sum(squares.T, axis=0, keepdims=True)


def join_kernel(count, start, *refs):
    blocks, out = refs[:count], refs[count]
    rows = blocks[0].shape[0]
    for i, block in enumerate(blocks):
        out[i * rows : (i + 1) * rows, :] = block[:, start : start + out.shape[1]]


def owner_flips(size, odd):
    flips = [0]
    for bit in crossing(size, odd)[::-1]:
        flips = flips + [f ^ bit for f in flips]
    return flips


def dense_kernel(size, picks_chip, rest_chip, chosen_ref, *refs):
    counts, (own, sib, keep_ref, send_ref, select_ref) = refs[:-5], refs[-5:]
    slots, picks = own.shape[0], chosen_ref.shape[1]
    rows_chip = picks_chip + rest_chip
    me = lax.axis_index("mem")
    odd_core = lax.rem(me, 2) == 1
    offsets = [jnp.zeros((1, 1), jnp.int32) for _ in range(2)]
    for d, ref in enumerate(counts):
        for h in range(2):
            origin = lax.bitwise_xor(me, 2 * d + h)
            for k in range(2):
                before = (origin < lax.bitwise_xor(me, k)).astype(jnp.int32)
                offsets[k] += ref[:1, h : h + 1] * before
    lane = lax.broadcasted_iota(jnp.int32, (1, 2 * slots), 1)
    first = lane < slots
    within = jnp.where(first, lane, lane - slots)
    alive = within < jnp.where(first, counts[0][:1, :1], counts[0][:1, 1:2])
    position = jnp.where(alive, within + jnp.where(first, offsets[0], offsets[1]), -1)

    chosen = chosen_ref[...]

    def column(start, length):
        row = lax.broadcasted_iota(jnp.int32, (length, picks), 0)
        across = lax.broadcasted_iota(jnp.int32, (length, picks), 1)
        return jnp.sum(jnp.where(across == row + start, chosen, 0), axis=1, keepdims=True)

    ids = column(0, picks)
    below = jnp.sum((ids < position).astype(jnp.int32), axis=0, keepdims=True)
    taken = jnp.sum((ids == position).astype(jnp.int32), axis=0, keepdims=True)
    rank = jnp.where(alive & (taken == 0), position - below, -1)
    place = lax.broadcasted_iota(jnp.int32, (rest_chip, 1), 0)
    for n, (e, o) in enumerate(zip(owner_flips(size, False), owner_flips(size, True))):
        owner = lax.bitwise_xor(me, jnp.where(odd_core, o, e)) // 2
        top = n * rows_chip
        hit = column(owner * picks_chip, picks_chip) == position
        select_ref[top : top + picks_chip, :] = hit.astype(F32).astype(BF16)
        hit = place + owner * rest_chip == rank
        select_ref[top + picks_chip : top + rows_chip, :] = hit.astype(F32).astype(BF16)

    half_rows = keep_ref.shape[0]

    @pl.loop(0, keep_ref.shape[1] // TILE)
    def _(t):
        at = pl.ds(pl.multiple_of(t * TILE, TILE), TILE)
        rows = jnp.concatenate([own[:, at], sib[:, at]], axis=0)
        found = jnp.dot(select_ref[...], rows, preferred_element_type=F32).astype(BF16)
        keep_ref[:, at] = found[:half_rows]
        send_ref[:, at] = found[half_rows:]


def add_kernel(keep, got, *outs):
    top = 0
    for out in outs:
        rows = out.shape[0]
        out[...] = keep[top : top + rows, :] + got[top : top + rows, :]
        top += rows


def owned_kernel(keep, got, out, picks_ref):
    out[...] = keep[...] + got[...]
    picks_ref[...] = out[: picks_ref.shape[0], :]


def row_norms(rows):
    rows = rows.astype(F32)
    return jnp.sum(rows * rows, axis=1, keepdims=True)


def gaps_to(rows_ref, norms, cand):
    inner = lax.dot_general(
        rows_ref[...], cand, (((1,), (1,)), ((), ())), preferred_element_type=F32
    )
    return norms - 2.0 * inner


def group_kernel(size, picks_chip, cand_ref, norm_ref, own, sib, near_ref, best_ref, rows_ref):
    chips, half = size // 2, own.shape[1]
    part, rows_chip = half // CHUNKS, own.shape[0] // chips
    for c in range(CHUNKS):
        at = slice(c * part, (c + 1) * part)
        rows_ref[:, 2 * c * part : (2 * c + 1) * part] = own[:, at]
        for i in range(chips):
            to = sibling_place(i, size) * rows_chip
            rows_ref[to : to + rows_chip, (2 * c + 1) * part : (2 * c + 2) * part] = sib[
                i * rows_chip : (i + 1) * rows_chip, at
            ]
    norms = row_norms(rows_ref[...])
    down = lax.broadcasted_iota(jnp.int32, norms.shape, 0)
    outside = jnp.where(lax.rem(down, rows_chip) < picks_chip, 0.0, jnp.inf)

    @pl.loop(0, cand_ref.shape[0] // TILE)
    def _(t):
        at = pl.ds(pl.multiple_of(t * TILE, TILE), TILE)
        gaps = gaps_to(rows_ref, norms, cand_ref[at, :])
        near_ref[:, at] = jnp.min(gaps, axis=0, keepdims=True) + norm_ref[:, at]
        best_ref[:, at] = jnp.min(gaps + outside, axis=0, keepdims=True)


def far_rows(size, held, sibs, rows_ref):
    rows, part = rows_ref.shape[0] // (size // 2), held[0].shape[1]
    for i, block in enumerate(held):
        top = i * block.shape[0]
        rows_ref[top : top + block.shape[0], :part] = block[...]
    for i in range(size // 2):
        block = sibs[i * rows // sibs[0].shape[0]]
        top = i * rows % sibs[0].shape[0]
        to = sibling_place(i, size) * rows
        rows_ref[to : to + rows, part:] = block[top : top + rows, :]


def far_gaps(size, chunk, cand_ref, before, blocks, rows_ref, emit):
    far_rows(size, blocks[:2], blocks[2:], rows_ref)
    width = rows_ref.shape[1]
    norms = row_norms(rows_ref[...])

    @pl.loop(0, cand_ref.shape[0] // TILE)
    def _(t):
        at = pl.ds(pl.multiple_of(t * TILE, TILE), TILE)
        gaps = gaps_to(rows_ref, norms, cand_ref[at, chunk * width : (chunk + 1) * width])
        for ref in before:
            gaps += ref[:, at]
        emit(at, gaps)


def far_kernel(size, chunk, cand_ref, *refs):
    *before, mine, got, sib_mine, sib_got, out, rows_ref = refs

    def emit(at, gaps):
        out[:, at] = gaps

    far_gaps(size, chunk, cand_ref, before, (mine, got, sib_mine, sib_got), rows_ref, emit)


def last_kernel(size, chunk, cand_ref, best_ref, norm_ref, *refs):
    *before, mine, got, sib_mine, sib_got, out, rows_ref = refs

    def emit(at, gaps):
        least = jnp.minimum(jnp.min(gaps, axis=0, keepdims=True), best_ref[:, at])
        out[:, at] = least + norm_ref[:, at]

    far_gaps(size, chunk, cand_ref, before, (mine, got, sib_mine, sib_got), rows_ref, emit)


def body(candidates, round_one, counts, chosen):
    size, groups = lax.axis_size("mem"), lax.axis_size("grp")
    slots, width = round_one.shape
    half, chips = width // 2, size // 2
    part = half // CHUNKS
    picks, rows = chosen.shape[1], candidates.shape[0]
    picks_chip = picks // chips
    rest_chip = (size * slots * 3 // 8 - picks) // chips
    rows_chip = picks_chip + rest_chip
    live, centers = chips * rows_chip, (groups - 1) * picks
    stages = len(chip_bits(size))

    def bf16(*dims):
        return jax.ShapeDtypeStruct(dims, BF16)

    def join(blocks, columns, start=0, after=(), weight=WEIGHT):
        count = blocks[0].shape[0] * len(blocks)
        return call(
            functools.partial(join_kernel, len(blocks), start), "join", bf16(count, columns),
            blocks, after=after, weight=weight,
        )

    line = jax.ShapeDtypeStruct((1, rows), F32)
    tile = jax.ShapeDtypeStruct((8, 128), jnp.int32)
    count = call(
        spread_kernel, "spread", tile, (counts,), specs=[pl.BlockSpec(memory_space=pltpu.SMEM)]
    )
    pair = call(pair_kernel, "pair", tile, (count, core_permute(count, size)))
    pairs = [pair] + [
        lax.ppermute(pair, "mem", [(m, m ^ (2 * d)) for m in range(size)]) for d in range(1, chips)
    ]
    own, send = call(split_kernel, "split", [bf16(slots, half)] * 2, (round_one,))
    sib = core_permute(send, size)

    held = live // 2
    keep, send = call(
        functools.partial(dense_kernel, size, picks_chip, rest_chip), "dense",
        [bf16(held, half)] * 2, (chosen, *pairs, own, sib),
        scratch=[pltpu.VMEM((live, 2 * slots), BF16)],
    )
    cand, norm = call(
        load_kernel, "load", [bf16(rows, width), line], (candidates,),
        specs=[pl.BlockSpec(memory_space=pltpu.HBM)], after=(keep,),
        scratch=[pltpu.SemaphoreType.DMA((rows // TILE * 2 * CHUNKS,))], limit=42 * MIB,
    )
    for stage in range(stages - 1):
        held //= 2
        got = mixed_permute(send, size, stage)
        keep, send = call(
            add_kernel, "add", [bf16(held, half)] * 2, (keep, got), after=(norm,)
        )
    got = mixed_permute(send, size, stages - 1)
    owned, picked = call(
        owned_kernel, "owned", [bf16(rows_chip, half), bf16(picks_chip, half)], (keep, got)
    )

    shifted = [
        lax.ppermute(picked, "grp", [(g, (g + k) % groups) for g in range(groups)])
        for k in range(1, groups)
    ]
    dense = owned
    for stage in range(stages):
        dense = join((dense, mixed_permute(dense, size, stage)), half, weight=0)
    near, best = call(
        functools.partial(group_kernel, size, picks_chip), "group", [line] * 2,
        (cand, norm, dense, core_permute(dense, size)),
        scratch=[pltpu.VMEM((live, width), BF16)],
    )
    block = join(shifted, half, after=(best,))

    got = mixed_permute(block, size, 0)
    for stage in range(1, stages - 1):
        block = join((block, got), half)
        got = mixed_permute(block, size, stage)
    scratch = [pltpu.VMEM((centers, 2 * part), BF16)]
    mine = [join((block, got), part, c * part) for c in range(CHUNKS)]
    got = [mixed_permute(m, size, stages - 1) for m in mine]
    before, final = (), None
    for c in range(CHUNKS):
        sent = join((got[c],), part, after=before) if before else got[c]
        blocks = (mine[c], got[c], core_permute(mine[c], size), core_permute(sent, size))
        if c < CHUNKS - 1:
            before = (
                call(
                    functools.partial(far_kernel, size, c), "far",
                    jax.ShapeDtypeStruct((centers, rows), F32), (cand, *before, *blocks),
                    scratch=scratch,
                ),
            )
        else:
            final = call(
                functools.partial(last_kernel, size, c), "far_last", line,
                (cand, best, norm, *before, *blocks), scratch=scratch,
            )
    return near.reshape(-1), final.reshape(-1)


def solution(mesh):
    in_specs = (P(("grp", "mem"), None), P(("grp", "mem"), None), P("grp", "mem"), P("grp", None))
    out_specs = (P(("grp", "mem")), P(("grp", "mem")))
    return jax.shard_map(body, mesh=mesh, in_specs=in_specs, out_specs=out_specs, check_vma=False)
```

time: 69 us -> 87.2 us (1.26)
  waiting for transfers between devices: 23.9 us -> 51.1 us
  starting transfers between devices: 21.5 us -> 17.2 us
  Pallas kernels: 20.5 us -> 16.8 us
  local copies, waits for them, and re-layouts: 1.55 us -> 0.51 us
    ppermute x8 -> x7, waiting for transfers between devices: 17.3 us -> 39.3 us  [mixed_permute(): lax.ppermute(block, 'mem', [(m, m ^ (odd if m & 1 else even)) for m in ra...]
    ppermute x6 -> x3, starting transfers between devices: 9.79 us -> 4.67 us  [body(): lax.ppermute(picked, 'grp', [(g, (g + k) % groups) for g in range(groups)])]
    ppermute x8 -> x7, starting transfers between devices: 11 us -> 6.63 us  [mixed_permute(): lax.ppermute(block, 'mem', [(m, m ^ (odd if m & 1 else even)) for m in ra...]
    ppermute x0 -> x3, starting transfers between devices: none -> 4.18 us  [body(): lax.ppermute(pair, 'mem', [(m, m ^ 2 * d) for m in range(size)])]
    pallas_call x17 -> x16, Pallas kernels: 20.5 us -> 16.8 us  [call(): pl.pallas_call(run, out_shape=out_shape, in_specs=(specs or vmem_specs(co...]
    ppermute x0 -> x3, waiting for transfers between devices: none -> 3.47 us  [body(): lax.ppermute(pair, 'mem', [(m, m ^ 2 * d) for m in range(size)])]
    ppermute x6 -> x3, waiting for transfers between devices: 3.72 us -> 6.57 us  [body(): lax.ppermute(picked, 'grp', [(g, (g + k) % groups) for g in range(groups)])]
    ppermute x6 -> x7, waiting for transfers between devices: 2.87 us -> 1.71 us  [core_permute(): return lax.ppermute(block, 'mem', [(m, m ^ 1) for m in range(size)])]
  transfers between devices with their start and end apart: 20 -> 20, of which waited for: 12 -> 12; matrix products, arithmetic and copies ran while one was open for 0% -> 0% of each run, Pallas kernels for 23% -> 13%
where the time goes in v8:
time: 87.2 us; the launch traced here: 87 us
  waiting for transfers between devices  51.1 us (59%)
  starting transfers between devices  17.2 us (20%)
  Pallas kernels  16.8 us (19%)
  between operations  1.42 us (2%)
    ppermute x7, waiting for transfers between devices, mixed_permute(): lax.ppermute(block, 'mem', [(m, m ^ (odd if m & 1 else even)) for m in ra...  39.3 us
    pallas_call x16, Pallas kernels, call(): pl.pallas_call(run, out_shape=out_shape, in_specs=(specs or vmem_specs(co...  16.8 us
    ppermute x7, starting transfers between devices, mixed_permute(): lax.ppermute(block, 'mem', [(m, m ^ (odd if m & 1 else even)) for m in ra...  6.63 us
    ppermute x3, waiting for transfers between devices, body(): lax.ppermute(picked, 'grp', [(g, (g + k) % groups) for g in range(groups)])  6.57 us
    ppermute x3, starting transfers between devices, body(): lax.ppermute(picked, 'grp', [(g, (g + k) % groups) for g in range(groups)])  4.67 us
    ppermute x3, starting transfers between devices, body(): lax.ppermute(pair, 'mem', [(m, m ^ 2 * d) for m in range(size)])  4.18 us
    ppermute x3, waiting for transfers between devices, body(): lax.ppermute(pair, 'mem', [(m, m ^ 2 * d) for m in range(size)])  3.47 us
    ppermute x7, starting transfers between devices, core_permute(): return lax.ppermute(block, 'mem', [(m, m ^ 1) for m in range(size)])  1.75 us
  transfers between devices with their start and end apart: 20, of which 12 were waited for; matrix products, arithmetic and copies ran while one was open for 0% of the time, Pallas kernels for 13%

profile of v8, /device:TPU:0, one launch (start us, length us, event | category | flops | bytes accessed | tf_op | source)
XLA Modules:
  0.0 87.0 jit_solution(14029139479431893226)
XLA Ops:
  2.9 3.5 %collective-permute-start.3 = (s32[8,128]{1,0:T(8,128)S(1)}, s32[8,128]{1,0:T(8,128)S(1)}, u32[]{:S(2)}, u32[]{:S(2)}) collective-permute-start(s32[8,128]{1,0:T(8,128)S(1)} %pair.1.refs_1_), channel_id=1, source_target_pairs={{0,6},{1,7},{2,4},{3,5},{4,2},{5,3},{6,0},{7,1},{8,14},{9,15},{10,... | collective-permute-start | bytes 12296 | tf_op jit(solution)/shard_map/ppermute | solution.py:301
  7.1 0.9 %collective-permute-done.3.refs_4_ = s32[8,128]{1,0:T(8,128)S(1)} collective-permute-done((s32[8,128]{1,0:T(8,128)S(1)}, s32[8,128]{1,0:T(8,128)S(1)}, u32[]{:S(2)}, u32[]{:S(2)}) %collective-permute-start.3) | collective-permute-done | bytes 4128 | tf_op jit(solution)/shard_map/ppermute | solution.py:301
  8.0 2.0 %collective-permute-done.2.refs_3_ = s32[8,128]{1,0:T(8,128)S(1)} collective-permute-done((s32[8,128]{1,0:T(8,128)S(1)}, s32[8,128]{1,0:T(8,128)S(1)}, u32[]{:S(2)}, u32[]{:S(2)}) %collective-permute-start.2) | collective-permute-done | bytes 4128 | tf_op jit(solution)/shard_map/ppermute | solution.py:301
  10.6 1.5 %dense.1 = (bf16[96,2048]{1,0:T(8,128)(2,1)S(1)}, bf16[96,2048]{1,0:T(8,128)(2,1)S(1)}) custom-call(s32[1,128]{1,0:T(1,128)S(1)} %copy-done.1, s32[8,128]{1,0:T(8,128)S(1)} %pair.1.refs_1_, s32[8,128]{1,0:T(8,128)S(1)} %collective-permute-done.1.refs_2_, s32[8,128]{1,0:T(8,128)S(1)} %collective-permute-done.2.refs_3_, ...), custom_call_target="tpu_custom_call" | custom-call | flops 10000000000 | bytes 1327616 | tf_op jit(solution)/shard_map/dense/pallas_call | solution.py:57
  12.3 4.0 %load.1 = (bf16[1024,4096]{1,0:T(8,128)(2,1)S(1)}, f32[1,1024]{1,0:T(1,128)S(1)}) custom-call(bf16[1024,4096]{1,0:T(8,128)(2,1)} %refs_0_.6, bf16[96,2048]{1,0:T(8,128)(2,1)S(1)} %get-tuple-element.16.refs_1_.refs_0_), custom_call_target="tpu_custom_call" | custom-call | flops 10000000000 | bytes 16781312 | tf_op jit(solution)/shard_map/load/pallas_call | solution.py:57
  16.3 3.6 %collective-permute-done.5.refs_1_ = bf16[96,2048]{1,0:T(8,128)(2,1)S(1)} collective-permute-done((bf16[96,2048]{1,0:T(8,128)(2,1)S(1)}, bf16[96,2048]{1,0:T(8,128)(2,1)S(1)}, u32[]{:S(2)}, u32[]{:S(2)}) %collective-permute-start.5) | collective-permute-done | bytes 393248 | tf_op jit(solution)/shard_map/ppermute | solution.py:27
  20.0 1.6 %collective-permute-start.6 = (bf16[48,2048]{1,0:T(8,128)(2,1)S(1)}, bf16[48,2048]{1,0:T(8,128)(2,1)S(1)}, u32[]{:S(2)}, u32[]{:S(2)}) collective-permute-start(bf16[48,2048]{1,0:T(8,128)(2,1)S(1)} %get-tuple-element.21), channel_id=1, source_target_pairs={{0,4},{1,3},{2,6},{3,1},{4,0},{5,7},{6,2},{7,5},{8,12},{9,11},{10,... | collective-permute-start | bytes 589832 | tf_op jit(solution)/shard_map/ppermute | solution.py:27
  21.6 4.7 %collective-permute-done.6.refs_1_ = bf16[48,2048]{1,0:T(8,128)(2,1)S(1)} collective-permute-done((bf16[48,2048]{1,0:T(8,128)(2,1)S(1)}, bf16[48,2048]{1,0:T(8,128)(2,1)S(1)}, u32[]{:S(2)}, u32[]{:S(2)}) %collective-permute-start.6) | collective-permute-done | bytes 196640 | tf_op jit(solution)/shard_map/ppermute | solution.py:27
  26.4 7.4 %collective-permute-done.7.refs_1_ = bf16[48,2048]{1,0:T(8,128)(2,1)S(1)} collective-permute-done((bf16[48,2048]{1,0:T(8,128)(2,1)S(1)}, bf16[48,2048]{1,0:T(8,128)(2,1)S(1)}, u32[]{:S(2)}, u32[]{:S(2)}) %collective-permute-start.7) | collective-permute-done | bytes 196640 | tf_op jit(solution)/shard_map/ppermute | solution.py:27
  33.8 1.6 %collective-permute-start.8 = (bf16[96,2048]{1,0:T(8,128)(2,1)S(1)}, bf16[96,2048]{1,0:T(8,128)(2,1)S(1)}, u32[]{:S(2)}, u32[]{:S(2)}) collective-permute-start(bf16[96,2048]{1,0:T(8,128)(2,1)S(1)} %join.6.refs_0_), channel_id=1, source_target_pairs={{0,4},{1,3},{2,6},{3,1},{4,0},{5,7},{6,2},{7,5},{8,12},{9,11},{10,... | collective-permute-start | bytes 1179656 | tf_op jit(solution)/shard_map/ppermute | solution.py:27
  35.4 6.3 %collective-permute-done.8.refs_1_ = bf16[96,2048]{1,0:T(8,128)(2,1)S(1)} collective-permute-done((bf16[96,2048]{1,0:T(8,128)(2,1)S(1)}, bf16[96,2048]{1,0:T(8,128)(2,1)S(1)}, u32[]{:S(2)}, u32[]{:S(2)}) %collective-permute-start.8) | collective-permute-done | bytes 393248 | tf_op jit(solution)/shard_map/ppermute | solution.py:27
  41.8 3.6 %collective-permute-start.12 = (bf16[32,2048]{1,0:T(8,128)(2,1)S(1)}, bf16[32,2048]{1,0:T(8,128)(2,1)S(1)}, u32[]{:S(2)}, u32[]{:S(2)}) collective-permute-start(bf16[32,2048]{1,0:T(8,128)(2,1)S(1)} %get-tuple-element.25), channel_id=1, source_target_pairs={{0,24},{8,0},{16,8},{24,16},{1,25},{9,1},{17,9},{25,17},{2,26},{10... | collective-permute-start | bytes 393224 | tf_op jit(solution)/shard_map/ppermute | solution.py:329
  45.4 1.0 %collective-permute-start.10 = (bf16[32,2048]{1,0:T(8,128)(2,1)S(1)}, bf16[32,2048]{1,0:T(8,128)(2,1)S(1)}, u32[]{:S(2)}, u32[]{:S(2)}) collective-permute-start(bf16[32,2048]{1,0:T(8,128)(2,1)S(1)} %get-tuple-element.25), channel_id=1, source_target_pairs={{0,8},{8,16},{16,24},{24,0},{1,9},{9,17},{17,25},{25,1},{2,10},{10... | collective-permute-start | bytes 393224 | tf_op jit(solution)/shard_map/ppermute | solution.py:329
  46.5 4.5 %group.1 = (f32[1,1024]{1,0:T(1,128)}, f32[1,1024]{1,0:T(1,128)S(1)}) custom-call(bf16[1024,4096]{1,0:T(8,128)(2,1)S(1)} %get-tuple-element.17.refs_0_, f32[1,1024]{1,0:T(1,128)S(1)} %get-tuple-element.18.refs_2_.refs_1_, bf16[192,2048]{1,0:T(8,128)(2,1)S(1)} %join.7.refs_2_, bf16[192,2048]{1,0:T(8,128)(2,1)S(1)} %collective-permute-done.9.refs_3_), custom_call_target="tpu_custom_call" | custom-call | flops 10000000000 | bytes 9973760 | tf_op jit(solution)/shard_map/group/pallas_call | solution.py:57
  51.0 6.6 %collective-permute-done.11.refs_1_ = bf16[32,2048]{1,0:T(8,128)(2,1)S(1)} collective-permute-done((bf16[32,2048]{1,0:T(8,128)(2,1)S(1)}, bf16[32,2048]{1,0:T(8,128)(2,1)S(1)}, u32[]{:S(2)}, u32[]{:S(2)}) %collective-permute-start.11) | collective-permute-done | bytes 131104 | tf_op jit(solution)/shard_map/ppermute | solution.py:329
  57.6 7.8 %collective-permute-done.13.refs_1_ = bf16[96,2048]{1,0:T(8,128)(2,1)S(1)} collective-permute-done((bf16[96,2048]{1,0:T(8,128)(2,1)S(1)}, bf16[96,2048]{1,0:T(8,128)(2,1)S(1)}, u32[]{:S(2)}, u32[]{:S(2)}) %collective-permute-start.13) | collective-permute-done | bytes 393248 | tf_op jit(solution)/shard_map/ppermute | solution.py:27
  65.4 1.6 %collective-permute-start.14 = (bf16[192,1024]{1,0:T(8,128)(2,1)S(1)}, bf16[192,1024]{1,0:T(8,128)(2,1)S(1)}, u32[]{:S(2)}, u32[]{:S(2)}) collective-permute-start(bf16[192,1024]{1,0:T(8,128)(2,1)S(1)} %join.9.refs_1_), channel_id=1, source_target_pairs={{0,4},{1,3},{2,6},{3,1},{4,0},{5,7},{6,2},{7,5},{8,12},{9,11},{10,... | collective-permute-start | bytes 1179656 | tf_op jit(solution)/shard_map/ppermute | solution.py:27
  67.0 6.2 %collective-permute-done.14.refs_2_ = bf16[192,1024]{1,0:T(8,128)(2,1)S(1)} collective-permute-done((bf16[192,1024]{1,0:T(8,128)(2,1)S(1)}, bf16[192,1024]{1,0:T(8,128)(2,1)S(1)}, u32[]{:S(2)}, u32[]{:S(2)}) %collective-permute-start.14) | collective-permute-done | bytes 393248 | tf_op jit(solution)/shard_map/ppermute | solution.py:27
  73.3 0.6 collective-permute-start.18
  73.9 1.5 %collective-permute-start.17 = (bf16[192,1024]{1,0:T(8,128)(2,1)S(1)}, bf16[192,1024]{1,0:T(8,128)(2,1)S(1)}, u32[]{:S(2)}, u32[]{:S(2)}) collective-permute-start(bf16[192,1024]{1,0:T(8,128)(2,1)S(1)} %join.10.refs_4_), channel_id=1, source_target_pairs={{0,4},{1,3},{2,6},{3,1},{4,0},{5,7},{6,2},{7,5},{8,12},{9,11},{10,... | collective-permute-start | bytes 1179656 | tf_op jit(solution)/shard_map/ppermute | solution.py:27
  75.4 2.9 %far.1.refs_1_.refs_3_ = f32[384,1024]{1,0:T(8,128)S(1)} custom-call(bf16[1024,4096]{1,0:T(8,128)(2,1)S(1)} %get-tuple-element.17.refs_0_, bf16[192,1024]{1,0:T(8,128)(2,1)S(1)} %join.9.refs_1_, bf16[192,1024]{1,0:T(8,128)(2,1)S(1)} %collective-permute-done.14.refs_2_, bf16[192,1024]{1,0:T(8,128)(2,1)S(1)} %collective-permute-done.15.refs_3_, ...), custom_call_target="tpu_custom_call" | custom-call | flops 10000000000 | bytes 11534336 | tf_op jit(solution)/shard_map/far/pallas_call | solution.py:57
  78.3 3.4 %collective-permute-done.17.refs_0_.refs_5_ = bf16[192,1024]{1,0:T(8,128)(2,1)S(1)} collective-permute-done((bf16[192,1024]{1,0:T(8,128)(2,1)S(1)}, bf16[192,1024]{1,0:T(8,128)(2,1)S(1)}, u32[]{:S(2)}, u32[]{:S(2)}) %collective-permute-start.17) | collective-permute-done | bytes 393248 | tf_op jit(solution)/shard_map/ppermute | solution.py:27
  81.8 1.7 %collective-permute-done.19.refs_7_ = bf16[192,1024]{1,0:T(8,128)(2,1)S(1)} collective-permute-done((bf16[192,1024]{1,0:T(8,128)(2,1)S(1)}, bf16[192,1024]{1,0:T(8,128)(2,1)S(1)}, u32[]{:S(2)}, u32[]{:S(2)}) %collective-permute-start.19) | collective-permute-done | bytes 393248 | tf_op jit(solution)/shard_map/ppermute | solution.py:31
  83.5 3.5 %far_last.1 = f32[1,1024]{1,0:T(1,128)} custom-call(bf16[1024,4096]{1,0:T(8,128)(2,1)S(1)} %get-tuple-element.17.refs_0_, f32[1,1024]{1,0:T(1,128)S(1)} %get-tuple-element.24.refs_3_.refs_1_, f32[1,1024]{1,0:T(1,128)S(1)} %get-tuple-element.18.refs_2_.refs_1_, f32[384,1024]{1,0:T(8,128)S(1)} %far.1.refs_1_.refs_3_, bf16[192,1024]{1,0:T(8,128)(2,1)S(1)} %join.10.refs_4_, ...), custom_call_target="tpu_custom_call" | custom-call | flops 10000000000 | bytes 11546624 | tf_op jit(solution)/shard_map/far_last/pallas_call | solution.py:57
  (36 shorter events, 3.5 us)
Async XLA Ops:
  1.3 1.0 %copy-start = (bf16[64,4096]{1,0:T(8,128)(2,1)S(1)}, bf16[64,4096]{1,0:T(8,128)(2,1)}, u32[]{:S(2)}) copy-start(bf16[64,4096]{1,0:T(8,128)(2,1)} %refs_0_.4) | copy-start | bytes 1572868
  1.3 1.6 %collective-permute-start = (s32[8,128]{1,0:T(8,128)S(1)}, s32[8,128]{1,0:T(8,128)S(1)}, u32[]{:S(2)}, u32[]{:S(2)}) collective-permute-start(s32[8,128]{1,0:T(8,128)S(1)} %spread.1.refs_0_), channel_id=1, source_target_pairs={{0,1},{1,0},{2,3},{3,2},{4,5},{5,4},{6,7},{7,6},{8,9},{9,8},{10,11... | collective-permute-start | bytes 12296 | tf_op jit(solution)/shard_map/ppermute | solution.py:31
  2.4 8.2 %copy-start.1 = (s32[1,128]{1,0:T(1,128)S(1)}, s32[1,128]{1,0:T(1,128)}, u32[]{:S(2)}) copy-start(s32[1,128]{1,0:T(1,128)} %refs_0_.5) | copy-start | bytes 1540
  2.4 8.2 %collective-permute-start.4 = (bf16[64,2048]{1,0:T(8,128)(2,1)S(1)}, bf16[64,2048]{1,0:T(8,128)(2,1)S(1)}, u32[]{:S(2)}, u32[]{:S(2)}) collective-permute-start(bf16[64,2048]{1,0:T(8,128)(2,1)S(1)} %get-tuple-element.15), channel_id=1, source_target_pairs={{0,1},{1,0},{2,3},{3,2},{4,5},{5,4},{6,7},{7,6},{8,9},{9,8},{10,11... | collective-permute-start | bytes 786440 | tf_op jit(solution)/shard_map/ppermute | solution.py:31
  2.9 5.1 %collective-permute-start.3 = (s32[8,128]{1,0:T(8,128)S(1)}, s32[8,128]{1,0:T(8,128)S(1)}, u32[]{:S(2)}, u32[]{:S(2)}) collective-permute-start(s32[8,128]{1,0:T(8,128)S(1)} %pair.1.refs_1_), channel_id=1, source_target_pairs={{0,6},{1,7},{2,4},{3,5},{4,2},{5,3},{6,0},{7,1},{8,14},{9,15},{10,... | collective-permute-start | bytes 12296 | tf_op jit(solution)/shard_map/ppermute | solution.py:301
  6.4 3.6 %collective-permute-start.2 = (s32[8,128]{1,0:T(8,128)S(1)}, s32[8,128]{1,0:T(8,128)S(1)}, u32[]{:S(2)}, u32[]{:S(2)}) collective-permute-start(s32[8,128]{1,0:T(8,128)S(1)} %pair.1.refs_1_), channel_id=1, source_target_pairs={{0,4},{1,5},{2,6},{3,7},{4,0},{5,1},{6,2},{7,3},{8,12},{9,13},{10,... | collective-permute-start | bytes 12296 | tf_op jit(solution)/shard_map/ppermute | solution.py:301
  6.9 3.6 %collective-permute-start.1 = (s32[8,128]{1,0:T(8,128)S(1)}, s32[8,128]{1,0:T(8,128)S(1)}, u32[]{:S(2)}, u32[]{:S(2)}) collective-permute-start(s32[8,128]{1,0:T(8,128)S(1)} %pair.1.refs_1_), channel_id=1, source_target_pairs={{0,2},{1,3},{2,0},{3,1},{4,6},{5,7},{6,4},{7,5},{8,10},{9,11},{10,... | collective-permute-start | bytes 12296 | tf_op jit(solution)/shard_map/ppermute | solution.py:301
  12.1 7.8 %collective-permute-start.5 = (bf16[96,2048]{1,0:T(8,128)(2,1)S(1)}, bf16[96,2048]{1,0:T(8,128)(2,1)S(1)}, u32[]{:S(2)}, u32[]{:S(2)}) collective-permute-start(bf16[96,2048]{1,0:T(8,128)(2,1)S(1)} %get-tuple-element.19), channel_id=1, source_target_pairs={{0,2},{1,5},{2,0},{3,7},{4,6},{5,1},{6,4},{7,3},{8,10},{9,13},{10,... | collective-permute-start | bytes 1179656 | tf_op jit(solution)/shard_map/ppermute | solution.py:27
  20.0 6.3 %collective-permute-start.6 = (bf16[48,2048]{1,0:T(8,128)(2,1)S(1)}, bf16[48,2048]{1,0:T(8,128)(2,1)S(1)}, u32[]{:S(2)}, u32[]{:S(2)}) collective-permute-start(bf16[48,2048]{1,0:T(8,128)(2,1)S(1)} %get-tuple-element.21), channel_id=1, source_target_pairs={{0,4},{1,3},{2,6},{3,1},{4,0},{5,7},{6,2},{7,5},{8,12},{9,11},{10,... | collective-permute-start | bytes 589832 | tf_op jit(solution)/shard_map/ppermute | solution.py:27
  26.3 7.5 %collective-permute-start.7 = (bf16[48,2048]{1,0:T(8,128)(2,1)S(1)}, bf16[48,2048]{1,0:T(8,128)(2,1)S(1)}, u32[]{:S(2)}, u32[]{:S(2)}) collective-permute-start(bf16[48,2048]{1,0:T(8,128)(2,1)S(1)} %get-tuple-element.22.refs_0_), channel_id=1, source_target_pairs={{0,2},{1,5},{2,0},{3,7},{4,6},{5,1},{6,4},{7,3},{8,10},{9,13},{10,... | collective-permute-start | bytes 589832 | tf_op jit(solution)/shard_map/ppermute | solution.py:27
  33.8 7.8 %collective-permute-start.8 = (bf16[96,2048]{1,0:T(8,128)(2,1)S(1)}, bf16[96,2048]{1,0:T(8,128)(2,1)S(1)}, u32[]{:S(2)}, u32[]{:S(2)}) collective-permute-start(bf16[96,2048]{1,0:T(8,128)(2,1)S(1)} %join.6.refs_0_), channel_id=1, source_target_pairs={{0,4},{1,3},{2,6},{3,1},{4,0},{5,7},{6,2},{7,5},{8,12},{9,11},{10,... | collective-permute-start | bytes 1179656 | tf_op jit(solution)/shard_map/ppermute | solution.py:27
  41.7 4.8 %collective-permute-start.9 = (bf16[192,2048]{1,0:T(8,128)(2,1)S(1)}, bf16[192,2048]{1,0:T(8,128)(2,1)S(1)}, u32[]{:S(2)}, u32[]{:S(2)}) collective-permute-start(bf16[192,2048]{1,0:T(8,128)(2,1)S(1)} %join.7.refs_2_), channel_id=1, source_target_pairs={{0,1},{1,0},{2,3},{3,2},{4,5},{5,4},{6,7},{7,6},{8,9},{9,8},{10,11... | collective-permute-start | bytes 2359304 | tf_op jit(solution)/shard_map/ppermute | solution.py:31
  41.8 9.2 %collective-permute-start.12 = (bf16[32,2048]{1,0:T(8,128)(2,1)S(1)}, bf16[32,2048]{1,0:T(8,128)(2,1)S(1)}, u32[]{:S(2)}, u32[]{:S(2)}) collective-permute-start(bf16[32,2048]{1,0:T(8,128)(2,1)S(1)} %get-tuple-element.25), channel_id=1, source_target_pairs={{0,24},{8,0},{16,8},{24,16},{1,25},{9,1},{17,9},{25,17},{2,26},{10... | collective-permute-start | bytes 393224 | tf_op jit(solution)/shard_map/ppermute | solution.py:329
  45.4 12.1 %collective-permute-start.11 = (bf16[32,2048]{1,0:T(8,128)(2,1)S(1)}, bf16[32,2048]{1,0:T(8,128)(2,1)S(1)}, u32[]{:S(2)}, u32[]{:S(2)}) collective-permute-start(bf16[32,2048]{1,0:T(8,128)(2,1)S(1)} %get-tuple-element.25), channel_id=1, source_target_pairs={{0,16},{8,24},{16,0},{24,8},{1,17},{9,25},{17,1},{25,9},{2,18},{10... | collective-permute-start | bytes 393224 | tf_op jit(solution)/shard_map/ppermute | solution.py:329
  45.4 12.1 %collective-permute-start.10 = (bf16[32,2048]{1,0:T(8,128)(2,1)S(1)}, bf16[32,2048]{1,0:T(8,128)(2,1)S(1)}, u32[]{:S(2)}, u32[]{:S(2)}) collective-permute-start(bf16[32,2048]{1,0:T(8,128)(2,1)S(1)} %get-tuple-element.25), channel_id=1, source_target_pairs={{0,8},{8,16},{16,24},{24,0},{1,9},{9,17},{17,25},{25,1},{2,10},{10... | collective-permute-start | bytes 393224 | tf_op jit(solution)/shard_map/ppermute | solution.py:329
  57.6 7.8 %collective-permute-start.13 = (bf16[96,2048]{1,0:T(8,128)(2,1)S(1)}, bf16[96,2048]{1,0:T(8,128)(2,1)S(1)}, u32[]{:S(2)}, u32[]{:S(2)}) collective-permute-start(bf16[96,2048]{1,0:T(8,128)(2,1)S(1)} %join.8.refs_0_), channel_id=1, source_target_pairs={{0,2},{1,5},{2,0},{3,7},{4,6},{5,1},{6,4},{7,3},{8,10},{9,13},{10,... | collective-permute-start | bytes 1179656 | tf_op jit(solution)/shard_map/ppermute | solution.py:27
  65.4 7.8 %collective-permute-start.14 = (bf16[192,1024]{1,0:T(8,128)(2,1)S(1)}, bf16[192,1024]{1,0:T(8,128)(2,1)S(1)}, u32[]{:S(2)}, u32[]{:S(2)}) collective-permute-start(bf16[192,1024]{1,0:T(8,128)(2,1)S(1)} %join.9.refs_1_), channel_id=1, source_target_pairs={{0,4},{1,3},{2,6},{3,1},{4,0},{5,7},{6,2},{7,5},{8,12},{9,11},{10,... | collective-permute-start | bytes 1179656 | tf_op jit(solution)/shard_map/ppermute | solution.py:27
  67.0 8.4 %collective-permute-start.15 = (bf16[192,1024]{1,0:T(8,128)(2,1)S(1)}, bf16[192,1024]{1,0:T(8,128)(2,1)S(1)}, u32[]{:S(2)}, u32[]{:S(2)}) collective-permute-start(bf16[192,1024]{1,0:T(8,128)(2,1)S(1)} %join.9.refs_1_), channel_id=1, source_target_pairs={{0,1},{1,0},{2,3},{3,2},{4,5},{5,4},{6,7},{7,6},{8,9},{9,8},{10,11... | collective-permute-start | bytes 1179656 | tf_op jit(solution)/shard_map/ppermute | solution.py:31
  73.3 2.1 %collective-permute-start.16 = (bf16[192,1024]{1,0:T(8,128)(2,1)S(1)}, bf16[192,1024]{1,0:T(8,128)(2,1)S(1)}, u32[]{:S(2)}, u32[]{:S(2)}) collective-permute-start(bf16[192,1024]{1,0:T(8,128)(2,1)S(1)} %collective-permute-done.14.refs_2_), channel_id=1, source_target_pairs={{0,1},{1,0},{2,3},{3,2},{4,5},{5,4},{6,7},{7,6},{8,9},{9,8},{10,11... | collective-permute-start | bytes 1179656 | tf_op jit(solution)/shard_map/ppermute | solution.py:31
  73.3 8.5 %collective-permute-start.18 = (bf16[192,1024]{1,0:T(8,128)(2,1)S(1)}, bf16[192,1024]{1,0:T(8,128)(2,1)S(1)}, u32[]{:S(2)}, u32[]{:S(2)}) collective-permute-start(bf16[192,1024]{1,0:T(8,128)(2,1)S(1)} %join.10.refs_4_), channel_id=1, source_target_pairs={{0,1},{1,0},{2,3},{3,2},{4,5},{5,4},{6,7},{7,6},{8,9},{9,8},{10,11... | collective-permute-start | bytes 1179656 | tf_op jit(solution)/shard_map/ppermute | solution.py:31
  73.9 7.8 %collective-permute-start.17 = (bf16[192,1024]{1,0:T(8,128)(2,1)S(1)}, bf16[192,1024]{1,0:T(8,128)(2,1)S(1)}, u32[]{:S(2)}, u32[]{:S(2)}) collective-permute-start(bf16[192,1024]{1,0:T(8,128)(2,1)S(1)} %join.10.refs_4_), channel_id=1, source_target_pairs={{0,4},{1,3},{2,6},{3,1},{4,0},{5,7},{6,2},{7,5},{8,12},{9,11},{10,... | collective-permute-start | bytes 1179656 | tf_op jit(solution)/shard_map/ppermute | solution.py:27
  81.7 1.8 %collective-permute-start.19 = (bf16[192,1024]{1,0:T(8,128)(2,1)S(1)}, bf16[192,1024]{1,0:T(8,128)(2,1)S(1)}, u32[]{:S(2)}, u32[]{:S(2)}) collective-permute-start(bf16[192,1024]{1,0:T(8,128)(2,1)S(1)} %join.11), channel_id=1, source_target_pairs={{0,1},{1,0},{2,3},{3,2},{4,5},{5,4},{6,7},{7,6},{8,9},{9,8},{10,11... | collective-permute-start | bytes 1179656 | tf_op jit(solution)/shard_map/ppermute | solution.py:31

commit v9 on v8

v9 whole, which is shorter than its diff:
```python
import functools

import jax
import jax.numpy as jnp
from jax import lax
from jax.experimental import pallas as pl
from jax.experimental.pallas import tpu as pltpu
from jax.sharding import PartitionSpec as P

CHUNKS = (6, 2)
TILE = 256
MIB = 1024 * 1024
WEIGHT = 10**10
F32, BF16 = jnp.float32, jnp.bfloat16


def flip_permute(block, size, flip):
    return lax.ppermute(block, "mem", [(m, m ^ flip) for m in range(size)])


def to_chips(block, size):
    return [block] + [flip_permute(block, size, 2 * d) for d in range(1, size // 2)]


def vmem_specs(count):
    return [pl.BlockSpec(memory_space=pltpu.VMEM)] * count


def call(kernel, name, out_shape, operands, specs=None, scratch=(), after=(), limit=28 * MIB, weight=WEIGHT):
    shapes = jax.tree.leaves(out_shape)
    moved = sum(a.size * a.dtype.itemsize for a in list(operands) + shapes)
    count = len(operands)

    def run(*refs):
        kernel(*refs[:count], *refs[count + len(after) :])

    return pl.pallas_call(
        run,
        out_shape=out_shape,
        in_specs=(specs or vmem_specs(count)) + [pl.BlockSpec(memory_space=pl.ANY)] * len(after),
        out_specs=jax.tree.map(lambda _: pl.BlockSpec(memory_space=pltpu.VMEM), out_shape),
        scratch_shapes=scratch,
        compiler_params=pltpu.CompilerParams(vmem_limit_bytes=limit),
        cost_estimate=pl.CostEstimate(flops=weight, bytes_accessed=moved, transcendentals=0),
        name=name,
    )(*operands, *after)


def spread_kernel(count_ref, out):
    out[...] = jnp.broadcast_to(count_ref[0, 0], out.shape)


def pair_kernel(own, sib, out):
    lane = lax.broadcasted_iota(jnp.int32, out.shape, 1)
    out[...] = jnp.where(lane == 0, own[...], sib[...])


def split_kernel(rows_ref, keep_ref, send_ref):
    half = keep_ref.shape[1]
    core = lax.rem(lax.axis_index("mem"), 2)
    keep_ref[...] = rows_ref[:, pl.ds(pl.multiple_of(core * half, half), half)]
    send_ref[...] = rows_ref[:, pl.ds(pl.multiple_of((1 - core) * half, half), half)]


def chunk_bounds(half):
    bounds, start = [], 0
    for eighths in CHUNKS:
        bounds.append((start, half * eighths // 8))
        start += bounds[-1][1]
    return bounds


def load_kernel(cand_hbm, cand_ref, norm_ref, sems):
    half = cand_ref.shape[1] // 2
    core = lax.rem(lax.axis_index("mem"), 2)
    tiles, copies = cand_ref.shape[0] // TILE, []
    for t in range(tiles):
        at = pl.ds(t * TILE, TILE)
        for start, width in chunk_bounds(half):
            for k, own in enumerate((core, 1 - core)):
                origin = pl.multiple_of(own * half + start, 128)
                copies.append(
                    pltpu.make_async_copy(
                        cand_hbm.at[at, pl.ds(origin, width)],
                        cand_ref.at[at, pl.ds(2 * start + k * width, width)],
                        sems.at[len(copies)],
                    )
                )
    for copy in copies:
        copy.start()
    each = len(copies) // tiles
    for t in range(tiles):
        for copy in copies[t * each : (t + 1) * each]:
            copy.wait()
        squares = jnp.zeros((TILE, 128), F32)
        for k in range(0, cand_ref.shape[1], 128):
            entries = cand_ref[t * TILE : (t + 1) * TILE, k : k + 128].astype(F32)
            squares += entries * entries
        norm_ref[:, t * TILE : (t + 1) * TILE] = jnp.sum(squares.T, axis=0, keepdims=True)


def join_kernel(count, start, *refs):
    blocks, out = refs[:count], refs[count]
    rows = blocks[0].shape[0]
    for i, block in enumerate(blocks):
        out[i * rows : (i + 1) * rows, :] = block[:, start : start + out.shape[1]]


def dense_kernel(size, picks_chip, rest_chip, chosen_ref, *refs):
    chips = size // 2
    counts, (own, sib, *outs, select_ref) = refs[:chips], refs[chips:]
    slots, picks = own.shape[0], chosen_ref.shape[1]
    rows_chip = picks_chip + rest_chip
    me = lax.axis_index("mem")
    offsets = [jnp.zeros((1, 1), jnp.int32) for _ in range(2)]
    for d, ref in enumerate(counts):
        for h in range(2):
            origin = lax.bitwise_xor(me, 2 * d + h)
            for k in range(2):
                before = (origin < lax.bitwise_xor(me, k)).astype(jnp.int32)
                offsets[k] += ref[:1, h : h + 1] * before
    lane = lax.broadcasted_iota(jnp.int32, (1, 2 * slots), 1)
    first = lane < slots
    within = jnp.where(first, lane, lane - slots)
    alive = within < jnp.where(first, counts[0][:1, :1], counts[0][:1, 1:2])
    position = jnp.where(alive, within + jnp.where(first, offsets[0], offsets[1]), -1)

    chosen = chosen_ref[...]

    def column(start, length):
        row = lax.broadcasted_iota(jnp.int32, (length, picks), 0)
        across = lax.broadcasted_iota(jnp.int32, (length, picks), 1)
        return jnp.sum(jnp.where(across == row + start, chosen, 0), axis=1, keepdims=True)

    ids = column(0, picks)
    below = jnp.sum((ids < position).astype(jnp.int32), axis=0, keepdims=True)
    taken = jnp.sum((ids == position).astype(jnp.int32), axis=0, keepdims=True)
    rank = jnp.where(alive & (taken == 0), position - below, -1)
    place = lax.broadcasted_iota(jnp.int32, (rest_chip, 1), 0)
    for d in range(chips):
        owner = lax.bitwise_xor(me // 2, d)
        top = d * rows_chip
        hit = column(owner * picks_chip, picks_chip) == position
        select_ref[top : top + picks_chip, :] = hit.astype(F32).astype(BF16)
        hit = place + owner * rest_chip == rank
        select_ref[top + picks_chip : top + rows_chip, :] = hit.astype(F32).astype(BF16)

    @pl.loop(0, own.shape[1] // TILE)
    def _(t):
        at = pl.ds(pl.multiple_of(t * TILE, TILE), TILE)
        rows = jnp.concatenate([own[:, at], sib[:, at]], axis=0)
        found = jnp.dot(select_ref[...], rows, preferred_element_type=F32).astype(BF16)
        for d, out in enumerate(outs):
            out[:, at] = found[d * rows_chip : (d + 1) * rows_chip]


def sum_kernel(*refs):
    *parts, out, picks_ref = refs
    total = parts[0][...]
    for ref in parts[1:]:
        total += ref[...]
    out[...] = total
    picks_ref[...] = total[: picks_ref.shape[0], :]


def square_kernel(own, first, second, left, right, out):
    rows, part = left.shape
    for i, block in enumerate((own, first, second)):
        out[i * rows : (i + 1) * rows, :] = block[...]
    out[3 * rows :, :part] = left[...]
    out[3 * rows :, part:] = right[...]


def row_norms(rows):
    rows = rows.astype(F32)
    return jnp.sum(rows * rows, axis=1, keepdims=True)


def gaps_to(rows_ref, norms, cand):
    inner = lax.dot_general(
        rows_ref[...], cand, (((1,), (1,)), ((), ())), preferred_element_type=F32
    )
    return norms - 2.0 * inner


def group_kernel(rows_chip, picks_chip, cand_ref, norm_ref, own, sib, near_ref, best_ref, rows_ref):
    for start, width in chunk_bounds(own.shape[1]):
        at = slice(start, start + width)
        rows_ref[:, 2 * start : 2 * start + width] = own[:, at]
        rows_ref[:, 2 * start + width : 2 * (start + width)] = sib[:, at]
    norms = row_norms(rows_ref[...])
    down = lax.broadcasted_iota(jnp.int32, norms.shape, 0)
    outside = jnp.where(lax.rem(down, rows_chip) < picks_chip, 0.0, jnp.inf)

    @pl.loop(0, cand_ref.shape[0] // TILE)
    def _(t):
        at = pl.ds(pl.multiple_of(t * TILE, TILE), TILE)
        gaps = gaps_to(rows_ref, norms, cand_ref[at, :])
        near_ref[:, at] = jnp.min(gaps, axis=0, keepdims=True) + norm_ref[:, at]
        best_ref[:, at] = jnp.min(gaps + outside, axis=0, keepdims=True)


def far_gaps(start, cand_ref, before, blocks, rows_ref, emit):
    own, sib = blocks
    part = own.shape[1]
    rows_ref[:, :part] = own[...]
    rows_ref[:, part:] = sib[...]
    norms = row_norms(rows_ref[...])

    @pl.loop(0, cand_ref.shape[0] // TILE)
    def _(t):
        at = pl.ds(pl.multiple_of(t * TILE, TILE), TILE)
        gaps = gaps_to(rows_ref, norms, cand_ref[at, 2 * start : 2 * (start + part)])
        for ref in before:
            gaps += ref[:, at]
        emit(at, gaps)


def far_kernel(start, cand_ref, *refs):
    *before, own, sib, out, rows_ref = refs

    def emit(at, gaps):
        out[:, at] = gaps

    far_gaps(start, cand_ref, before, (own, sib), rows_ref, emit)


def last_kernel(start, cand_ref, best_ref, norm_ref, *refs):
    *before, own, sib, out, rows_ref = refs

    def emit(at, gaps):
        least = jnp.minimum(jnp.min(gaps, axis=0, keepdims=True), best_ref[:, at])
        out[:, at] = least + norm_ref[:, at]

    far_gaps(start, cand_ref, before, (own, sib), rows_ref, emit)


def body(candidates, round_one, counts, chosen):
    size, groups = lax.axis_size("mem"), lax.axis_size("grp")
    slots, width = round_one.shape
    half, chips = width // 2, size // 2
    picks, rows = chosen.shape[1], candidates.shape[0]
    picks_chip = picks // chips
    rest_chip = (size * slots * 3 // 8 - picks) // chips
    rows_chip = picks_chip + rest_chip
    live, centers = chips * rows_chip, (groups - 1) * picks

    def bf16(*dims):
        return jax.ShapeDtypeStruct(dims, BF16)

    def join(blocks, columns, start=0, after=(), weight=WEIGHT):
        count = blocks[0].shape[0] * len(blocks)
        return call(
            functools.partial(join_kernel, len(blocks), start), "join", bf16(count, columns),
            blocks, after=after, weight=weight,
        )

    line = jax.ShapeDtypeStruct((1, rows), F32)
    tile = jax.ShapeDtypeStruct((8, 128), jnp.int32)
    count = call(
        spread_kernel, "spread", tile, (counts,), specs=[pl.BlockSpec(memory_space=pltpu.SMEM)]
    )
    pair = call(pair_kernel, "pair", tile, (count, flip_permute(count, size, 1)))
    pairs = to_chips(pair, size)
    own, send = call(split_kernel, "split", [bf16(slots, half)] * 2, (round_one,))
    sib = flip_permute(send, size, 1)

    parts = call(
        functools.partial(dense_kernel, size, picks_chip, rest_chip), "dense",
        [bf16(rows_chip, half)] * chips, (chosen, *pairs, own, sib),
        scratch=[pltpu.VMEM((live, 2 * slots), BF16)],
    )
    copies = rows // TILE * 2 * len(CHUNKS)
    cand, norm = call(
        load_kernel, "load", [bf16(rows, width), line], (candidates,),
        specs=[pl.BlockSpec(memory_space=pltpu.HBM)], after=parts[:1],
        scratch=[pltpu.SemaphoreType.DMA((copies,))], limit=42 * MIB,
    )
    got = [flip_permute(parts[d], size, 2 * d) for d in range(1, chips)]
    owned, picked = call(
        sum_kernel, "owned", [bf16(rows_chip, half), bf16(picks_chip, half)], (parts[0], *got),
        after=(norm,),
    )

    shifted = [
        lax.ppermute(picked, "grp", [(g, (g + k) % groups) for g in range(groups)])
        for k in range(1, groups)
    ]
    if chips == 4:
        first, second = (flip_permute(owned, size, flip) for flip in (2, 4))
        left = flip_permute(join((first,), half // 2, weight=0), size, 4)
        right = flip_permute(join((second,), half // 2, half // 2, weight=0), size, 2)
        dense = call(
            square_kernel, "square", bf16(live, half), (owned, first, second, left, right), weight=0
        )
    else:
        dense = join(to_chips(owned, size), half)
    near, best = call(
        functools.partial(group_kernel, rows_chip, picks_chip), "group", [line] * 2,
        (cand, norm, dense, flip_permute(dense, size, 1)),
        scratch=[pltpu.VMEM((live, width), BF16)],
    )

    bounds = chunk_bounds(half)
    far = [to_chips(join(shifted, part, start, after=(dense,)), size) for start, part in bounds]
    before, final = (), None
    for c, (start, part) in enumerate(bounds):
        block = join(far[c], part, after=before or (best,))
        operands = (*before, block, flip_permute(block, size, 1))
        scratch = [pltpu.VMEM((centers, 2 * part), BF16)]
        if c < len(bounds) - 1:
            before = (
                call(
                    functools.partial(far_kernel, start), "far",
                    jax.ShapeDtypeStruct((centers, rows), F32), (cand, *operands), scratch=scratch,
                ),
            )
        else:
            final = call(
                functools.partial(last_kernel, start), "far_last", line,
                (cand, best, norm, *operands), scratch=scratch,
            )
    return near.reshape(-1), final.reshape(-1)


def solution(mesh):
    in_specs = (P(("grp", "mem"), None), P(("grp", "mem"), None), P("grp", "mem"), P("grp", None))
    out_specs = (P(("grp", "mem")), P(("grp", "mem")))
    return jax.shard_map(body, mesh=mesh, in_specs=in_specs, out_specs=out_specs, check_vma=False)
```

time: 87.2 us -> 65.6 us (0.75)
  waiting for transfers between devices: 51.1 us -> 21.9 us
  starting transfers between devices: 17.2 us -> 25 us
    ppermute x17 -> x21, waiting for transfers between devices: 44.5 us -> 20.1 us  [flip_permute(): return lax.ppermute(block, 'mem', [(m, m ^ flip) for m in range(size)])]
    ppermute x17 -> x21, starting transfers between devices: 12.6 us -> 20.3 us  [flip_permute(): return lax.ppermute(block, 'mem', [(m, m ^ flip) for m in range(size)])]
    ppermute x3, waiting for transfers between devices: 6.57 us -> 1.78 us  [body(): lax.ppermute(picked, 'grp', [(g, (g + k) % groups) for g in range(groups)])]
  transfers between devices with their start and end apart: 20 -> 24, of which waited for: 12 -> 13; matrix products, arithmetic and copies ran while one was open for 0% -> 0% of each run, Pallas kernels for 13% -> 19%
where the time goes in v9:
time: 65.6 us; the launch traced here: 65.4 us
  starting transfers between devices  25 us (38%)
  waiting for transfers between devices  21.9 us (33%)
  Pallas kernels  16.7 us (25%)
  between operations  1.42 us (2%)
    ppermute x21, starting transfers between devices, flip_permute(): return lax.ppermute(block, 'mem', [(m, m ^ flip) for m in range(size)])  20.3 us
    ppermute x21, waiting for transfers between devices, flip_permute(): return lax.ppermute(block, 'mem', [(m, m ^ flip) for m in range(size)])  20.1 us
    pallas_call x16, Pallas kernels, call(): pl.pallas_call(run, out_shape=out_shape, in_specs=(specs or vmem_specs(co...  16.7 us
    ppermute x3, starting transfers between devices, body(): lax.ppermute(picked, 'grp', [(g, (g + k) % groups) for g in range(groups)])  4.7 us
    ppermute x3, waiting for transfers between devices, body(): lax.ppermute(picked, 'grp', [(g, (g + k) % groups) for g in range(groups)])  1.78 us
  transfers between devices with their start and end apart: 24, of which 13 were waited for; matrix products, arithmetic and copies ran while one was open for 0% of the time, Pallas kernels for 19%

profile of v9, /device:TPU:0, one launch (start us, length us, event | category | flops | bytes accessed | tf_op | source)
XLA Modules:
  0.0 65.4 jit_solution(9383719459943590192)
XLA Ops:
  2.9 3.5 %collective-permute-start.3 = (s32[8,128]{1,0:T(8,128)S(1)}, s32[8,128]{1,0:T(8,128)S(1)}, u32[]{:S(2)}, u32[]{:S(2)}) collective-permute-start(s32[8,128]{1,0:T(8,128)S(1)} %pair.1.refs_1_), channel_id=1, source_target_pairs={{0,6},{1,7},{2,4},{3,5},{4,2},{5,3},{6,0},{7,1},{8,14},{9,15},{10,... | collective-permute-start | bytes 12296 | tf_op jit(solution)/shard_map/ppermute | solution.py:18
  8.0 2.0 %collective-permute-done.2.refs_3_ = s32[8,128]{1,0:T(8,128)S(1)} collective-permute-done((s32[8,128]{1,0:T(8,128)S(1)}, s32[8,128]{1,0:T(8,128)S(1)}, u32[]{:S(2)}, u32[]{:S(2)}) %collective-permute-start.2) | collective-permute-done | bytes 4128 | tf_op jit(solution)/shard_map/ppermute | solution.py:18
  10.6 1.6 %dense.1 = (bf16[48,2048]{1,0:T(8,128)(2,1)S(1)}, bf16[48,2048]{1,0:T(8,128)(2,1)S(1)}, bf16[48,2048]{1,0:T(8,128)(2,1)S(1)}, bf16[48,2048]{1,0:T(8,128)(2,1)S(1)}) custom-call(s32[1,128]{1,0:T(1,128)S(1)} %copy-done.1, s32[8,128]{1,0:T(8,128)S(1)} %pair.1.refs_1_, s32[8,128]{1,0:T(8,128)S(1)} %collective-permute-done.1.refs_2_, ...), custom_call_target="tpu_custom_call" | custom-call | flops 10000000000 | bytes 1327616 | tf_op jit(solution)/shard_map/dense/pallas_call | solution.py:37
  12.3 1.9 %collective-permute-start.6 = (bf16[48,2048]{1,0:T(8,128)(2,1)S(1)}, bf16[48,2048]{1,0:T(8,128)(2,1)S(1)}, u32[]{:S(2)}, u32[]{:S(2)}) collective-permute-start(bf16[48,2048]{1,0:T(8,128)(2,1)S(1)} %get-tuple-element.20), channel_id=1, source_target_pairs={{0,4},{1,5},{2,6},{3,7},{4,0},{5,1},{6,2},{7,3},{8,12},{9,13},{10,... | collective-permute-start | bytes 589832 | tf_op jit(solution)/shard_map/ppermute | solution.py:18
  14.2 1.4 %collective-permute-start.7 = (bf16[48,2048]{1,0:T(8,128)(2,1)S(1)}, bf16[48,2048]{1,0:T(8,128)(2,1)S(1)}, u32[]{:S(2)}, u32[]{:S(2)}) collective-permute-start(bf16[48,2048]{1,0:T(8,128)(2,1)S(1)} %get-tuple-element.21), channel_id=1, source_target_pairs={{0,6},{1,7},{2,4},{3,5},{4,2},{5,3},{6,0},{7,1},{8,14},{9,15},{10,... | collective-permute-start | bytes 589832 | tf_op jit(solution)/shard_map/ppermute | solution.py:18
  15.7 4.0 %load.1 = (bf16[1024,4096]{1,0:T(8,128)(2,1)S(1)}, f32[1,1024]{1,0:T(1,128)S(1)}) custom-call(bf16[1024,4096]{1,0:T(8,128)(2,1)} %refs_0_.6, bf16[48,2048]{1,0:T(8,128)(2,1)S(1)} %get-tuple-element.16.refs_1_.refs_0_), custom_call_target="tpu_custom_call" | custom-call | flops 10000000000 | bytes 16781312 | tf_op jit(solution)/shard_map/load/pallas_call | solution.py:37
  19.8 2.0 %collective-permute-done.6.refs_2_ = bf16[48,2048]{1,0:T(8,128)(2,1)S(1)} collective-permute-done((bf16[48,2048]{1,0:T(8,128)(2,1)S(1)}, bf16[48,2048]{1,0:T(8,128)(2,1)S(1)}, u32[]{:S(2)}, u32[]{:S(2)}) %collective-permute-start.6) | collective-permute-done | bytes 196640 | tf_op jit(solution)/shard_map/ppermute | solution.py:18
  21.8 1.1 %collective-permute-done.7.refs_3_ = bf16[48,2048]{1,0:T(8,128)(2,1)S(1)} collective-permute-done((bf16[48,2048]{1,0:T(8,128)(2,1)S(1)}, bf16[48,2048]{1,0:T(8,128)(2,1)S(1)}, u32[]{:S(2)}, u32[]{:S(2)}) %collective-permute-start.7) | collective-permute-done | bytes 196640 | tf_op jit(solution)/shard_map/ppermute | solution.py:18
  22.9 1.5 %collective-permute-start.9 = (bf16[48,2048]{1,0:T(8,128)(2,1)S(1)}, bf16[48,2048]{1,0:T(8,128)(2,1)S(1)}, u32[]{:S(2)}, u32[]{:S(2)}) collective-permute-start(bf16[48,2048]{1,0:T(8,128)(2,1)S(1)} %get-tuple-element.22.refs_0_), channel_id=1, source_target_pairs={{0,4},{1,5},{2,6},{3,7},{4,0},{5,1},{6,2},{7,3},{8,12},{9,13},{10,... | collective-permute-start | bytes 589832 | tf_op jit(solution)/shard_map/ppermute | solution.py:18
  25.3 3.7 %collective-permute-start.15 = (bf16[32,2048]{1,0:T(8,128)(2,1)S(1)}, bf16[32,2048]{1,0:T(8,128)(2,1)S(1)}, u32[]{:S(2)}, u32[]{:S(2)}) collective-permute-start(bf16[32,2048]{1,0:T(8,128)(2,1)S(1)} %get-tuple-element.25), channel_id=1, source_target_pairs={{0,24},{8,0},{16,8},{24,16},{1,25},{9,1},{17,9},{25,17},{2,26},{10... | collective-permute-start | bytes 393224 | tf_op jit(solution)/shard_map/ppermute | solution.py:286
  30.0 1.1 %collective-permute-start.11 = (bf16[48,1024]{1,0:T(8,128)(2,1)S(1)}, bf16[48,1024]{1,0:T(8,128)(2,1)S(1)}, u32[]{:S(2)}, u32[]{:S(2)}) collective-permute-start(bf16[48,1024]{1,0:T(8,128)(2,1)S(1)} %join.7), channel_id=1, source_target_pairs={{0,2},{1,3},{2,0},{3,1},{4,6},{5,7},{6,4},{7,5},{8,10},{9,11},{10,... | collective-permute-start | bytes 294920 | tf_op jit(solution)/shard_map/ppermute | solution.py:18
  31.8 2.9 %collective-permute-done.11.refs_4_ = bf16[48,1024]{1,0:T(8,128)(2,1)S(1)} collective-permute-done((bf16[48,1024]{1,0:T(8,128)(2,1)S(1)}, bf16[48,1024]{1,0:T(8,128)(2,1)S(1)}, u32[]{:S(2)}, u32[]{:S(2)}) %collective-permute-start.11) | collective-permute-done | bytes 98336 | tf_op jit(solution)/shard_map/ppermute | solution.py:18
  34.7 1.1 %collective-permute-done.10.refs_3_ = bf16[48,1024]{1,0:T(8,128)(2,1)S(1)} collective-permute-done((bf16[48,1024]{1,0:T(8,128)(2,1)S(1)}, bf16[48,1024]{1,0:T(8,128)(2,1)S(1)}, u32[]{:S(2)}, u32[]{:S(2)}) %collective-permute-start.10) | collective-permute-done | bytes 98336 | tf_op jit(solution)/shard_map/ppermute | solution.py:18
  36.0 1.8 %collective-permute-done.14.refs_1_ = bf16[32,2048]{1,0:T(8,128)(2,1)S(1)} collective-permute-done((bf16[32,2048]{1,0:T(8,128)(2,1)S(1)}, bf16[32,2048]{1,0:T(8,128)(2,1)S(1)}, u32[]{:S(2)}, u32[]{:S(2)}) %collective-permute-start.14) | collective-permute-done | bytes 131104 | tf_op jit(solution)/shard_map/ppermute | solution.py:286
  37.8 1.6 %collective-permute-start.18 = (bf16[96,1536]{1,0:T(8,128)(2,1)S(1)}, bf16[96,1536]{1,0:T(8,128)(2,1)S(1)}, u32[]{:S(2)}, u32[]{:S(2)}) collective-permute-start(bf16[96,1536]{1,0:T(8,128)(2,1)S(1)} %join.8.refs_0_), channel_id=1, source_target_pairs={{0,6},{1,7},{2,4},{3,5},{4,2},{5,3},{6,0},{7,1},{8,14},{9,15},{10,... | collective-permute-start | bytes 884744 | tf_op jit(solution)/shard_map/ppermute | solution.py:18
  39.9 1.5 %collective-permute-start.16 = (bf16[96,1536]{1,0:T(8,128)(2,1)S(1)}, bf16[96,1536]{1,0:T(8,128)(2,1)S(1)}, u32[]{:S(2)}, u32[]{:S(2)}) collective-permute-start(bf16[96,1536]{1,0:T(8,128)(2,1)S(1)} %join.8.refs_0_), channel_id=1, source_target_pairs={{0,2},{1,3},{2,0},{3,1},{4,6},{5,7},{6,4},{7,5},{8,10},{9,11},{10,... | collective-permute-start | bytes 884744 | tf_op jit(solution)/shard_map/ppermute | solution.py:18
  41.4 4.5 %group.1 = (f32[1,1024]{1,0:T(1,128)}, f32[1,1024]{1,0:T(1,128)S(1)}) custom-call(bf16[1024,4096]{1,0:T(8,128)(2,1)S(1)} %get-tuple-element.17.refs_0_, f32[1,1024]{1,0:T(1,128)S(1)} %get-tuple-element.18.refs_4_.refs_1_.refs_2_, bf16[192,2048]{1,0:T(8,128)(2,1)S(1)} %square.1.refs_2_.refs_3_, bf16[192,2048]{1,0:T(8,128)(2,1)S(1)} %collective-permute-done.12.refs_3_), custom_call_target="tpu_custom_call" | custom-call | flops 10000000000 | bytes 9973760 | tf_op jit(solution)/shard_map/group/pallas_call | solution.py:37
  45.8 2.9 %collective-permute-done.18.refs_3_ = bf16[96,1536]{1,0:T(8,128)(2,1)S(1)} collective-permute-done((bf16[96,1536]{1,0:T(8,128)(2,1)S(1)}, bf16[96,1536]{1,0:T(8,128)(2,1)S(1)}, u32[]{:S(2)}, u32[]{:S(2)}) %collective-permute-start.18) | collective-permute-done | bytes 294944 | tf_op jit(solution)/shard_map/ppermute | solution.py:18
  48.7 3.9 %collective-permute-done.17.refs_2_ = bf16[96,1536]{1,0:T(8,128)(2,1)S(1)} collective-permute-done((bf16[96,1536]{1,0:T(8,128)(2,1)S(1)}, bf16[96,1536]{1,0:T(8,128)(2,1)S(1)}, u32[]{:S(2)}, u32[]{:S(2)}) %collective-permute-start.17) | collective-permute-done | bytes 294944 | tf_op jit(solution)/shard_map/ppermute | solution.py:18
  52.8 1.2 %collective-permute-start.22 = (bf16[96,512]{1,0:T(8,128)(2,1)S(1)}, bf16[96,512]{1,0:T(8,128)(2,1)S(1)}, u32[]{:S(2)}, u32[]{:S(2)}) collective-permute-start(bf16[96,512]{1,0:T(8,128)(2,1)S(1)} %join.10.refs_0_), channel_id=1, source_target_pairs={{0,6},{1,7},{2,4},{3,5},{4,2},{5,3},{6,0},{7,1},{8,14},{9,15},{10,... | collective-permute-start | bytes 294920 | tf_op jit(solution)/shard_map/ppermute | solution.py:18
  54.1 1.3 %collective-permute-start.21 = (bf16[96,512]{1,0:T(8,128)(2,1)S(1)}, bf16[96,512]{1,0:T(8,128)(2,1)S(1)}, u32[]{:S(2)}, u32[]{:S(2)}) collective-permute-start(bf16[96,512]{1,0:T(8,128)(2,1)S(1)} %join.10.refs_0_), channel_id=1, source_target_pairs={{0,4},{1,5},{2,6},{3,7},{4,0},{5,1},{6,2},{7,3},{8,12},{9,13},{10,... | collective-permute-start | bytes 294920 | tf_op jit(solution)/shard_map/ppermute | solution.py:18
  56.4 3.8 %far.1.refs_4_.refs_3_ = f32[384,1024]{1,0:T(8,128)S(1)} custom-call(bf16[1024,4096]{1,0:T(8,128)(2,1)S(1)} %get-tuple-element.17.refs_0_, bf16[384,1536]{1,0:T(8,128)(2,1)S(1)} %join.9.refs_1_, bf16[384,1536]{1,0:T(8,128)(2,1)S(1)} %collective-permute-done.19.refs_2_), custom_call_target="tpu_custom_call" | custom-call | flops 10000000000 | bytes 12320768 | tf_op jit(solution)/shard_map/far/pallas_call | solution.py:37
  61.2 1.7 %collective-permute-done.23.refs_5_ = bf16[384,512]{1,0:T(8,128)(2,1)S(1)} collective-permute-done((bf16[384,512]{1,0:T(8,128)(2,1)S(1)}, bf16[384,512]{1,0:T(8,128)(2,1)S(1)}, u32[]{:S(2)}, u32[]{:S(2)}) %collective-permute-start.23) | collective-permute-done | bytes 393248 | tf_op jit(solution)/shard_map/ppermute | solution.py:18
  62.9 2.5 %far_last.1 = f32[1,1024]{1,0:T(1,128)} custom-call(bf16[1024,4096]{1,0:T(8,128)(2,1)S(1)} %get-tuple-element.17.refs_0_, f32[1,1024]{1,0:T(1,128)S(1)} %get-tuple-element.24.refs_4_.refs_1_, f32[1,1024]{1,0:T(1,128)S(1)} %get-tuple-element.18.refs_4_.refs_1_.refs_2_, f32[384,1024]{1,0:T(8,128)S(1)} %far.1.refs_4_.refs_3_, ...), custom_call_target="tpu_custom_call" | custom-call | flops 10000000000 | bytes 10760192 | tf_op jit(solution)/shard_map/far_last/pallas_call | solution.py:37
  (44 shorter events, 9.5 us)
Async XLA Ops:
  1.3 1.6 %collective-permute-start = (s32[8,128]{1,0:T(8,128)S(1)}, s32[8,128]{1,0:T(8,128)S(1)}, u32[]{:S(2)}, u32[]{:S(2)}) collective-permute-start(s32[8,128]{1,0:T(8,128)S(1)} %spread.1.refs_0_), channel_id=1, source_target_pairs={{0,1},{1,0},{2,3},{3,2},{4,5},{5,4},{6,7},{7,6},{8,9},{9,8},{10,11... | collective-permute-start | bytes 12296 | tf_op jit(solution)/shard_map/ppermute | solution.py:18
  2.4 8.2 %collective-permute-start.4 = (bf16[64,2048]{1,0:T(8,128)(2,1)S(1)}, bf16[64,2048]{1,0:T(8,128)(2,1)S(1)}, u32[]{:S(2)}, u32[]{:S(2)}) collective-permute-start(bf16[64,2048]{1,0:T(8,128)(2,1)S(1)} %get-tuple-element.15), channel_id=1, source_target_pairs={{0,1},{1,0},{2,3},{3,2},{4,5},{5,4},{6,7},{7,6},{8,9},{9,8},{10,11... | collective-permute-start | bytes 786440 | tf_op jit(solution)/shard_map/ppermute | solution.py:18
  2.9 5.1 %collective-permute-start.3 = (s32[8,128]{1,0:T(8,128)S(1)}, s32[8,128]{1,0:T(8,128)S(1)}, u32[]{:S(2)}, u32[]{:S(2)}) collective-permute-start(s32[8,128]{1,0:T(8,128)S(1)} %pair.1.refs_1_), channel_id=1, source_target_pairs={{0,6},{1,7},{2,4},{3,5},{4,2},{5,3},{6,0},{7,1},{8,14},{9,15},{10,... | collective-permute-start | bytes 12296 | tf_op jit(solution)/shard_map/ppermute | solution.py:18
  6.4 3.6 %collective-permute-start.2 = (s32[8,128]{1,0:T(8,128)S(1)}, s32[8,128]{1,0:T(8,128)S(1)}, u32[]{:S(2)}, u32[]{:S(2)}) collective-permute-start(s32[8,128]{1,0:T(8,128)S(1)} %pair.1.refs_1_), channel_id=1, source_target_pairs={{0,4},{1,5},{2,6},{3,7},{4,0},{5,1},{6,2},{7,3},{8,12},{9,13},{10,... | collective-permute-start | bytes 12296 | tf_op jit(solution)/shard_map/ppermute | solution.py:18
  6.9 3.6 %collective-permute-start.1 = (s32[8,128]{1,0:T(8,128)S(1)}, s32[8,128]{1,0:T(8,128)S(1)}, u32[]{:S(2)}, u32[]{:S(2)}) collective-permute-start(s32[8,128]{1,0:T(8,128)S(1)} %pair.1.refs_1_), channel_id=1, source_target_pairs={{0,2},{1,3},{2,0},{3,1},{4,6},{5,7},{6,4},{7,5},{8,10},{9,11},{10,... | collective-permute-start | bytes 12296 | tf_op jit(solution)/shard_map/ppermute | solution.py:18
  12.1 7.7 %collective-permute-start.5 = (bf16[48,2048]{1,0:T(8,128)(2,1)S(1)}, bf16[48,2048]{1,0:T(8,128)(2,1)S(1)}, u32[]{:S(2)}, u32[]{:S(2)}) collective-permute-start(bf16[48,2048]{1,0:T(8,128)(2,1)S(1)} %get-tuple-element.19), channel_id=1, source_target_pairs={{0,2},{1,3},{2,0},{3,1},{4,6},{5,7},{6,4},{7,5},{8,10},{9,11},{10,... | collective-permute-start | bytes 589832 | tf_op jit(solution)/shard_map/ppermute | solution.py:18
  12.3 9.5 %collective-permute-start.6 = (bf16[48,2048]{1,0:T(8,128)(2,1)S(1)}, bf16[48,2048]{1,0:T(8,128)(2,1)S(1)}, u32[]{:S(2)}, u32[]{:S(2)}) collective-permute-start(bf16[48,2048]{1,0:T(8,128)(2,1)S(1)} %get-tuple-element.20), channel_id=1, source_target_pairs={{0,4},{1,5},{2,6},{3,7},{4,0},{5,1},{6,2},{7,3},{8,12},{9,13},{10,... | collective-permute-start | bytes 589832 | tf_op jit(solution)/shard_map/ppermute | solution.py:18
  14.2 8.6 %collective-permute-start.7 = (bf16[48,2048]{1,0:T(8,128)(2,1)S(1)}, bf16[48,2048]{1,0:T(8,128)(2,1)S(1)}, u32[]{:S(2)}, u32[]{:S(2)}) collective-permute-start(bf16[48,2048]{1,0:T(8,128)(2,1)S(1)} %get-tuple-element.21), channel_id=1, source_target_pairs={{0,6},{1,7},{2,4},{3,5},{4,2},{5,3},{6,0},{7,1},{8,14},{9,15},{10,... | collective-permute-start | bytes 589832 | tf_op jit(solution)/shard_map/ppermute | solution.py:18
  22.9 7.1 %collective-permute-start.9 = (bf16[48,2048]{1,0:T(8,128)(2,1)S(1)}, bf16[48,2048]{1,0:T(8,128)(2,1)S(1)}, u32[]{:S(2)}, u32[]{:S(2)}) collective-permute-start(bf16[48,2048]{1,0:T(8,128)(2,1)S(1)} %get-tuple-element.22.refs_0_), channel_id=1, source_target_pairs={{0,4},{1,5},{2,6},{3,7},{4,0},{5,1},{6,2},{7,3},{8,12},{9,13},{10,... | collective-permute-start | bytes 589832 | tf_op jit(solution)/shard_map/ppermute | solution.py:18
  24.4 6.7 %collective-permute-start.8 = (bf16[48,2048]{1,0:T(8,128)(2,1)S(1)}, bf16[48,2048]{1,0:T(8,128)(2,1)S(1)}, u32[]{:S(2)}, u32[]{:S(2)}) collective-permute-start(bf16[48,2048]{1,0:T(8,128)(2,1)S(1)} %get-tuple-element.22.refs_0_), channel_id=1, source_target_pairs={{0,2},{1,3},{2,0},{3,1},{4,6},{5,7},{6,4},{7,5},{8,10},{9,11},{10,... | collective-permute-start | bytes 589832 | tf_op jit(solution)/shard_map/ppermute | solution.py:18
  25.3 10.7 %collective-permute-start.15 = (bf16[32,2048]{1,0:T(8,128)(2,1)S(1)}, bf16[32,2048]{1,0:T(8,128)(2,1)S(1)}, u32[]{:S(2)}, u32[]{:S(2)}) collective-permute-start(bf16[32,2048]{1,0:T(8,128)(2,1)S(1)} %get-tuple-element.25), channel_id=1, source_target_pairs={{0,24},{8,0},{16,8},{24,16},{1,25},{9,1},{17,9},{25,17},{2,26},{10... | collective-permute-start | bytes 393224 | tf_op jit(solution)/shard_map/ppermute | solution.py:286
  29.0 8.8 %collective-permute-start.14 = (bf16[32,2048]{1,0:T(8,128)(2,1)S(1)}, bf16[32,2048]{1,0:T(8,128)(2,1)S(1)}, u32[]{:S(2)}, u32[]{:S(2)}) collective-permute-start(bf16[32,2048]{1,0:T(8,128)(2,1)S(1)} %get-tuple-element.25), channel_id=1, source_target_pairs={{0,16},{8,24},{16,0},{24,8},{1,17},{9,25},{17,1},{25,9},{2,18},{10... | collective-permute-start | bytes 393224 | tf_op jit(solution)/shard_map/ppermute | solution.py:286
  29.0 8.8 %collective-permute-start.13 = (bf16[32,2048]{1,0:T(8,128)(2,1)S(1)}, bf16[32,2048]{1,0:T(8,128)(2,1)S(1)}, u32[]{:S(2)}, u32[]{:S(2)}) collective-permute-start(bf16[32,2048]{1,0:T(8,128)(2,1)S(1)} %get-tuple-element.25), channel_id=1, source_target_pairs={{0,8},{8,16},{16,24},{24,0},{1,9},{9,17},{17,25},{25,1},{2,10},{10... | collective-permute-start | bytes 393224 | tf_op jit(solution)/shard_map/ppermute | solution.py:286
  30.0 4.7 %collective-permute-start.11 = (bf16[48,1024]{1,0:T(8,128)(2,1)S(1)}, bf16[48,1024]{1,0:T(8,128)(2,1)S(1)}, u32[]{:S(2)}, u32[]{:S(2)}) collective-permute-start(bf16[48,1024]{1,0:T(8,128)(2,1)S(1)} %join.7), channel_id=1, source_target_pairs={{0,2},{1,3},{2,0},{3,1},{4,6},{5,7},{6,4},{7,5},{8,10},{9,11},{10,... | collective-permute-start | bytes 294920 | tf_op jit(solution)/shard_map/ppermute | solution.py:18
  31.2 4.7 %collective-permute-start.10 = (bf16[48,1024]{1,0:T(8,128)(2,1)S(1)}, bf16[48,1024]{1,0:T(8,128)(2,1)S(1)}, u32[]{:S(2)}, u32[]{:S(2)}) collective-permute-start(bf16[48,1024]{1,0:T(8,128)(2,1)S(1)} %join.6), channel_id=1, source_target_pairs={{0,4},{1,5},{2,6},{3,7},{4,0},{5,1},{6,2},{7,3},{8,12},{9,13},{10,... | collective-permute-start | bytes 294920 | tf_op jit(solution)/shard_map/ppermute | solution.py:18
  35.9 5.4 %collective-permute-start.12 = (bf16[192,2048]{1,0:T(8,128)(2,1)S(1)}, bf16[192,2048]{1,0:T(8,128)(2,1)S(1)}, u32[]{:S(2)}, u32[]{:S(2)}) collective-permute-start(bf16[192,2048]{1,0:T(8,128)(2,1)S(1)} %square.1.refs_2_.refs_3_), channel_id=1, source_target_pairs={{0,1},{1,0},{2,3},{3,2},{4,5},{5,4},{6,7},{7,6},{8,9},{9,8},{10,11... | collective-permute-start | bytes 2359304 | tf_op jit(solution)/shard_map/ppermute | solution.py:18
  37.8 10.9 %collective-permute-start.18 = (bf16[96,1536]{1,0:T(8,128)(2,1)S(1)}, bf16[96,1536]{1,0:T(8,128)(2,1)S(1)}, u32[]{:S(2)}, u32[]{:S(2)}) collective-permute-start(bf16[96,1536]{1,0:T(8,128)(2,1)S(1)} %join.8.refs_0_), channel_id=1, source_target_pairs={{0,6},{1,7},{2,4},{3,5},{4,2},{5,3},{6,0},{7,1},{8,14},{9,15},{10,... | collective-permute-start | bytes 884744 | tf_op jit(solution)/shard_map/ppermute | solution.py:18
  39.4 13.3 %collective-permute-start.17 = (bf16[96,1536]{1,0:T(8,128)(2,1)S(1)}, bf16[96,1536]{1,0:T(8,128)(2,1)S(1)}, u32[]{:S(2)}, u32[]{:S(2)}) collective-permute-start(bf16[96,1536]{1,0:T(8,128)(2,1)S(1)} %join.8.refs_0_), channel_id=1, source_target_pairs={{0,4},{1,5},{2,6},{3,7},{4,0},{5,1},{6,2},{7,3},{8,12},{9,13},{10,... | collective-permute-start | bytes 884744 | tf_op jit(solution)/shard_map/ppermute | solution.py:18
  39.9 12.8 %collective-permute-start.16 = (bf16[96,1536]{1,0:T(8,128)(2,1)S(1)}, bf16[96,1536]{1,0:T(8,128)(2,1)S(1)}, u32[]{:S(2)}, u32[]{:S(2)}) collective-permute-start(bf16[96,1536]{1,0:T(8,128)(2,1)S(1)} %join.8.refs_0_), channel_id=1, source_target_pairs={{0,2},{1,3},{2,0},{3,1},{4,6},{5,7},{6,4},{7,5},{8,10},{9,11},{10,... | collective-permute-start | bytes 884744 | tf_op jit(solution)/shard_map/ppermute | solution.py:18
  52.7 3.7 %collective-permute-start.19 = (bf16[384,1536]{1,0:T(8,128)(2,1)S(1)}, bf16[384,1536]{1,0:T(8,128)(2,1)S(1)}, u32[]{:S(2)}, u32[]{:S(2)}) collective-permute-start(bf16[384,1536]{1,0:T(8,128)(2,1)S(1)} %join.9.refs_1_), channel_id=1, source_target_pairs={{0,1},{1,0},{2,3},{3,2},{4,5},{5,4},{6,7},{7,6},{8,9},{9,8},{10,11... | collective-permute-start | bytes 3538952 | tf_op jit(solution)/shard_map/ppermute | solution.py:18
  52.8 7.4 %collective-permute-start.22 = (bf16[96,512]{1,0:T(8,128)(2,1)S(1)}, bf16[96,512]{1,0:T(8,128)(2,1)S(1)}, u32[]{:S(2)}, u32[]{:S(2)}) collective-permute-start(bf16[96,512]{1,0:T(8,128)(2,1)S(1)} %join.10.refs_0_), channel_id=1, source_target_pairs={{0,6},{1,7},{2,4},{3,5},{4,2},{5,3},{6,0},{7,1},{8,14},{9,15},{10,... | collective-permute-start | bytes 294920 | tf_op jit(solution)/shard_map/ppermute | solution.py:18
  54.1 7.0 %collective-permute-start.21 = (bf16[96,512]{1,0:T(8,128)(2,1)S(1)}, bf16[96,512]{1,0:T(8,128)(2,1)S(1)}, u32[]{:S(2)}, u32[]{:S(2)}) collective-permute-start(bf16[96,512]{1,0:T(8,128)(2,1)S(1)} %join.10.refs_0_), channel_id=1, source_target_pairs={{0,4},{1,5},{2,6},{3,7},{4,0},{5,1},{6,2},{7,3},{8,12},{9,13},{10,... | collective-permute-start | bytes 294920 | tf_op jit(solution)/shard_map/ppermute | solution.py:18
  55.4 5.7 %collective-permute-start.20 = (bf16[96,512]{1,0:T(8,128)(2,1)S(1)}, bf16[96,512]{1,0:T(8,128)(2,1)S(1)}, u32[]{:S(2)}, u32[]{:S(2)}) collective-permute-start(bf16[96,512]{1,0:T(8,128)(2,1)S(1)} %join.10.refs_0_), channel_id=1, source_target_pairs={{0,2},{1,3},{2,0},{3,1},{4,6},{5,7},{6,4},{7,5},{8,10},{9,11},{10,... | collective-permute-start | bytes 294920 | tf_op jit(solution)/shard_map/ppermute | solution.py:18
  61.1 1.8 %collective-permute-start.23 = (bf16[384,512]{1,0:T(8,128)(2,1)S(1)}, bf16[384,512]{1,0:T(8,128)(2,1)S(1)}, u32[]{:S(2)}, u32[]{:S(2)}) collective-permute-start(bf16[384,512]{1,0:T(8,128)(2,1)S(1)} %join.11.refs_4_), channel_id=1, source_target_pairs={{0,1},{1,0},{2,3},{3,2},{4,5},{5,4},{6,7},{7,6},{8,9},{9,8},{10,11... | collective-permute-start | bytes 1179656 | tf_op jit(solution)/shard_map/ppermute | solution.py:18
  (2 other events, 9.2 us)

commit v10 on v9

--- a/solution.py
+++ b/solution.py
@@ -7,7 +7,6 @@
 from jax.experimental.pallas import tpu as pltpu
 from jax.sharding import PartitionSpec as P
 
-CHUNKS = (6, 2)
 TILE = 256
 MIB = 1024 * 1024
 WEIGHT = 10**10
@@ -50,9 +49,13 @@
     out[...] = jnp.broadcast_to(count_ref[0, 0], out.shape)
 
 
-def pair_kernel(own, sib, out):
+def pack_kernel(*refs):
+    *counts, out = refs
     lane = lax.broadcasted_iota(jnp.int32, out.shape, 1)
-    out[...] = jnp.where(lane == 0, own[...], sib[...])
+    total = counts[0][...]
+    for d, ref in enumerate(counts):
+        total = jnp.where(lane == d, ref[...], total)
+    out[...] = total
 
 
 def split_kernel(rows_ref, keep_ref, send_ref):
@@ -60,14 +63,6 @@
     core = lax.rem(lax.axis_index("mem"), 2)
     keep_ref[...] = rows_ref[:, pl.ds(pl.multiple_of(core * half, half), half)]
     send_ref[...] = rows_ref[:, pl.ds(pl.multiple_of((1 - core) * half, half), half)]
-
-
-def chunk_bounds(half):
-    bounds, start = [], 0
-    for eighths in CHUNKS:
-        bounds.append((start, half * eighths // 8))
-        start += bounds[-1][1]
-    return bounds
 
 
 def load_kernel(cand_hbm, cand_ref, norm_ref, sems):
@@ -76,21 +71,18 @@
     tiles, copies = cand_ref.shape[0] // TILE, []
     for t in range(tiles):
         at = pl.ds(t * TILE, TILE)
-        for start, width in chunk_bounds(half):
-            for k, own in enumerate((core, 1 - core)):
-                origin = pl.multiple_of(own * half + start, 128)
-                copies.append(
-                    pltpu.make_async_copy(
-                        cand_hbm.at[at, pl.ds(origin, width)],
-                        cand_ref.at[at, pl.ds(2 * start + k * width, width)],
-                        sems.at[len(copies)],
-                    )
+        for k, own in enumerate((core, 1 - core)):
+            copies.append(
+                pltpu.make_async_copy(
+                    cand_hbm.at[at, pl.ds(pl.multiple_of(own * half, half), half)],
+                    cand_ref.at[at, pl.ds(k * half, half)],
+                    sems.at[len(copies)],
                 )
+            )
     for copy in copies:
         copy.start()
-    each = len(copies) // tiles
     for t in range(tiles):
-        for copy in copies[t * each : (t + 1) * each]:
+        for copy in copies[2 * t : 2 * t + 2]:
             copy.wait()
         squares = jnp.zeros((TILE, 128), F32)
         for k in range(0, cand_ref.shape[1], 128):
@@ -108,21 +100,22 @@
 
 def dense_kernel(size, picks_chip, rest_chip, chosen_ref, *refs):
     chips = size // 2
-    counts, (own, sib, *outs, select_ref) = refs[:chips], refs[chips:]
+    *counts, own, sib = refs[:4]
+    outs, select_ref = refs[4:-1], refs[-1]
     slots, picks = own.shape[0], chosen_ref.shape[1]
     rows_chip = picks_chip + rest_chip
     me = lax.axis_index("mem")
     offsets = [jnp.zeros((1, 1), jnp.int32) for _ in range(2)]
-    for d, ref in enumerate(counts):
-        for h in range(2):
+    for d in range(chips):
+        for h, ref in enumerate(counts):
             origin = lax.bitwise_xor(me, 2 * d + h)
             for k in range(2):
                 before = (origin < lax.bitwise_xor(me, k)).astype(jnp.int32)
-                offsets[k] += ref[:1, h : h + 1] * before
+                offsets[k] += ref[:1, d : d + 1] * before
     lane = lax.broadcasted_iota(jnp.int32, (1, 2 * slots), 1)
     first = lane < slots
     within = jnp.where(first, lane, lane - slots)
-    alive = within < jnp.where(first, counts[0][:1, :1], counts[0][:1, 1:2])
+    alive = within < jnp.where(first, counts[0][:1, :1], counts[1][:1, :1])
     position = jnp.where(alive, within + jnp.where(first, offsets[0], offsets[1]), -1)
 
     chosen = chosen_ref[...]
@@ -183,56 +176,44 @@
     return norms - 2.0 * inner
 
 
+def tiles_of(cand_ref):
+    return [slice(t, t + TILE) for t in range(0, cand_ref.shape[0], TILE)]
+
+
 def group_kernel(rows_chip, picks_chip, cand_ref, norm_ref, own, sib, near_ref, best_ref, rows_ref):
-    for start, width in chunk_bounds(own.shape[1]):
-        at = slice(start, start + width)
-        rows_ref[:, 2 * start : 2 * start + width] = own[:, at]
-        rows_ref[:, 2 * start + width : 2 * (start + width)] = sib[:, at]
+    half = own.shape[1]
+    rows_ref[:, :half] = own[...]
+    rows_ref[:, half:] = sib[...]
     norms = row_norms(rows_ref[...])
     down = lax.broadcasted_iota(jnp.int32, norms.shape, 0)
     outside = jnp.where(lax.rem(down, rows_chip) < picks_chip, 0.0, jnp.inf)
-
-    @pl.loop(0, cand_ref.shape[0] // TILE)
-    def _(t):
-        at = pl.ds(pl.multiple_of(t * TILE, TILE), TILE)
+    for at in tiles_of(cand_ref):
         gaps = gaps_to(rows_ref, norms, cand_ref[at, :])
         near_ref[:, at] = jnp.min(gaps, axis=0, keepdims=True) + norm_ref[:, at]
         best_ref[:, at] = jnp.min(gaps + outside, axis=0, keepdims=True)
 
 
-def far_gaps(start, cand_ref, before, blocks, rows_ref, emit):
-    own, sib = blocks
-    part = own.shape[1]
-    rows_ref[:, :part] = own[...]
-    rows_ref[:, part:] = sib[...]
+def far_kernel(cand_ref, best_ref, own, sib, out, rows_ref):
+    half = own.shape[1]
+    rows_ref[:, :half] = own[...]
+    rows_ref[:, half:] = sib[...]
     norms = row_norms(rows_ref[...])
-
-    @pl.loop(0, cand_ref.shape[0] // TILE)
-    def _(t):
-        at = pl.ds(pl.multiple_of(t * TILE, TILE), TILE)
-        gaps = gaps_to(rows_ref, norms, cand_ref[at, 2 * start : 2 * (start + part)])
-        for ref in before:
-            gaps += ref[:, at]
-        emit(at, gaps)
-
-
-def far_kernel(start, cand_ref, *refs):
-    *before, own, sib, out, rows_ref = refs
-
-    def emit(at, gaps):
-        out[:, at] = gaps
-
-    far_gaps(start, cand_ref, before, (own, sib), rows_ref, emit)
-
-
-def last_kernel(start, cand_ref, best_ref, norm_ref, *refs):
-    *before, own, sib, out, rows_ref = refs
-
-    def emit(at, gaps):
+    for at in tiles_of(cand_ref):
+        gaps = gaps_to(rows_ref, norms, cand_ref[at, :])
+        out[:, at] = jnp.minimum(jnp.min(gaps, axis=0, keepdims=True), best_ref[:, at])
+
+
+def last_kernel(cand_ref, best_ref, norm_ref, *refs):
+    *parts, out, rows_ref = refs
+    start = 0
+    for part in parts:
+        rows_ref[:, start : start + part.shape[1]] = part[...]
+        start += part.shape[1]
+    norms = row_norms(rows_ref[...])
+    for at in tiles_of(cand_ref):
+        gaps = gaps_to(rows_ref, norms, cand_ref[at, :])
         least = jnp.minimum(jnp.min(gaps, axis=0, keepdims=True), best_ref[:, at])
         out[:, at] = least + norm_ref[:, at]
-
-    far_gaps(start, cand_ref, before, (own, sib), rows_ref, emit)
 
 
 def body(candidates, round_one, counts, chosen):
@@ -243,7 +224,7 @@
     picks_chip = picks // chips
     rest_chip = (size * slots * 3 // 8 - picks) // chips
     rows_chip = picks_chip + rest_chip
-    live, centers = chips * rows_chip, (groups - 1) * picks
+    live = chips * rows_chip
 
     def bf16(*dims):
         return jax.ShapeDtypeStruct(dims, BF16)
@@ -260,21 +241,20 @@
     count = call(
         spread_kernel, "spread", tile, (counts,), specs=[pl.BlockSpec(memory_space=pltpu.SMEM)]
     )
-    pair = call(pair_kernel, "pair", tile, (count, flip_permute(count, size, 1)))
-    pairs = to_chips(pair, size)
+    mine = call(pack_kernel, "pack", tile, to_chips(count, size), weight=0)
+    theirs = flip_permute(mine, size, 1)
     own, send = call(split_kernel, "split", [bf16(slots, half)] * 2, (round_one,))
     sib = flip_permute(send, size, 1)
 
     parts = call(
         functools.partial(dense_kernel, size, picks_chip, rest_chip), "dense",
-        [bf16(rows_chip, half)] * chips, (chosen, *pairs, own, sib),
+        [bf16(rows_chip, half)] * chips, (chosen, mine, theirs, own, sib),
         scratch=[pltpu.VMEM((live, 2 * slots), BF16)],
     )
-    copies = rows // TILE * 2 * len(CHUNKS)
     cand, norm = call(
         load_kernel, "load", [bf16(rows, width), line], (candidates,),
         specs=[pl.BlockSpec(memory_space=pltpu.HBM)], after=parts[:1],
-        scratch=[pltpu.SemaphoreType.DMA((copies,))], limit=42 * MIB,
+        scratch=[pltpu.SemaphoreType.DMA((rows // TILE * 2,))], limit=42 * MIB,
     )
     got = [flip_permute(parts[d], size, 2 * d) for d in range(1, chips)]
     owned, picked = call(
@@ -286,12 +266,16 @@
         lax.ppermute(picked, "grp", [(g, (g + k) % groups) for g in range(groups)])
         for k in range(1, groups)
     ]
+    def corner(first, second, weight):
+        left = flip_permute(join((first,), half // 2, weight=weight), size, 4)
+        right = flip_permute(join((second,), half // 2, half // 2, weight=weight), size, 2)
+        return left, right
+
     if chips == 4:
         first, second = (flip_permute(owned, size, flip) for flip in (2, 4))
-        left = flip_permute(join((first,), half // 2, weight=0), size, 4)
-        right = flip_permute(join((second,), half // 2, half // 2, weight=0), size, 2)
         dense = call(
-            square_kernel, "square", bf16(live, half), (owned, first, second, left, right), weight=0
+            square_kernel, "square", bf16(live, half),
+            (owned, first, second, *corner(first, second, 0)), weight=0,
         )
     else:
         dense = join(to_chips(owned, size), half)
@@ -301,25 +285,24 @@
         scratch=[pltpu.VMEM((live, width), BF16)],
     )
 
-    bounds = chunk_bounds(half)
-    far = [to_chips(join(shifted, part, start, after=(dense,)), size) for start, part in bounds]
-    before, final = (), None
-    for c, (start, part) in enumerate(bounds):
-        block = join(far[c], part, after=before or (best,))
-        operands = (*before, block, flip_permute(block, size, 1))
-        scratch = [pltpu.VMEM((centers, 2 * part), BF16)]
-        if c < len(bounds) - 1:
-            before = (
-                call(
-                    functools.partial(far_kernel, start), "far",
-                    jax.ShapeDtypeStruct((centers, rows), F32), (cand, *operands), scratch=scratch,
-                ),
-            )
-        else:
-            final = call(
-                functools.partial(last_kernel, start), "far_last", line,
-                (cand, best, norm, *operands), scratch=scratch,
-            )
+    block = join(shifted, half, after=(dense,))
+    if chips == 4:
+        first, second = (flip_permute(block, size, flip) for flip in (2, 4))
+        blocks, last = (block, first, second), corner(first, second, 0)
+    else:
+        *blocks, end = to_chips(block, size)
+        last = (end,)
+    early = join(blocks, half, after=(best,))
+    best = call(
+        far_kernel, "far", line, (cand, best, early, flip_permute(early, size, 1)),
+        scratch=[pltpu.VMEM((early.shape[0], width), BF16)],
+    )
+    sent = [join((part,), part.shape[1], after=(best,), weight=0) for part in last]
+    final = call(
+        last_kernel, "far_last", line,
+        (cand, best, norm, *last, *[flip_permute(part, size, 1) for part in sent]),
+        scratch=[pltpu.VMEM((block.shape[0], width), BF16)],
+    )
     return near.reshape(-1), final.reshape(-1)
 
 

time: 65.6 us -> 66.5 us (1.014)
  waiting for transfers between devices: 21.9 us -> 26.7 us
  starting transfers between devices: 25 us -> 21.8 us
  Pallas kernels: 16.7 us -> 15.4 us
    ppermute x21 -> x20, starting transfers between devices: 20.3 us -> 17.2 us  [flip_permute(): return lax.ppermute(block, 'mem', [(m, m ^ flip) for m in range(size)])]
    ppermute x3, waiting for transfers between devices: 1.78 us -> 4.25 us  [body(): lax.ppermute(picked, 'grp', [(g, (g + k) % groups) for g in range(groups)])]
    ppermute x21 -> x20, waiting for transfers between devices: 20.1 us -> 22.4 us  [flip_permute(): return lax.ppermute(block, 'mem', [(m, m ^ flip) for m in range(size)])]
    pallas_call x16 -> x18, Pallas kernels: 16.7 us -> 15.4 us  [call(): pl.pallas_call(run, out_shape=out_shape, in_specs=(specs or vmem_specs(co...]
  transfers between devices with their start and end apart: 24 -> 23, of which waited for: 13 -> 16; matrix products, arithmetic and copies ran while one was open for 0% -> 0% of each run, Pallas kernels for 19% -> 16%
where the time goes in v10:
time: 66.5 us; the launch traced here: 66.4 us
  waiting for transfers between devices  26.7 us (40%)
  starting transfers between devices  21.8 us (33%)
  Pallas kernels  15.4 us (23%)
  between operations  1.43 us (2%)
  local copies, waits for them, and re-layouts  1.04 us (2%)
    ppermute x20, waiting for transfers between devices, flip_permute(): return lax.ppermute(block, 'mem', [(m, m ^ flip) for m in range(size)])  22.4 us
    ppermute x20, starting transfers between devices, flip_permute(): return lax.ppermute(block, 'mem', [(m, m ^ flip) for m in range(size)])  17.2 us
    pallas_call x18, Pallas kernels, call(): pl.pallas_call(run, out_shape=out_shape, in_specs=(specs or vmem_specs(co...  15.4 us
    ppermute x3, starting transfers between devices, body(): lax.ppermute(picked, 'grp', [(g, (g + k) % groups) for g in range(groups)])  4.62 us
    ppermute x3, waiting for transfers between devices, body(): lax.ppermute(picked, 'grp', [(g, (g + k) % groups) for g in range(groups)])  4.25 us
  transfers between devices with their start and end apart: 23, of which 16 were waited for; matrix products, arithmetic and copies ran while one was open for 0% of the time, Pallas kernels for 16%

profile of v10, /device:TPU:0, one launch (start us, length us, event | category | flops | bytes accessed | tf_op | source)
XLA Modules:
  0.0 66.4 jit_solution(9182673507302231180)
XLA Ops:
  0.6 1.0 %copy-done = bf16[64,4096]{1,0:T(8,128)(2,1)S(1)} copy-done((bf16[64,4096]{1,0:T(8,128)(2,1)S(1)}, bf16[64,4096]{1,0:T(8,128)(2,1)}, u32[]{:S(2)}) %copy-start) | copy-done | bytes 524312
  2.9 3.5 %collective-permute-start.2 = (s32[8,128]{1,0:T(8,128)S(1)}, s32[8,128]{1,0:T(8,128)S(1)}, u32[]{:S(2)}, u32[]{:S(2)}) collective-permute-start(s32[8,128]{1,0:T(8,128)S(1)} %spread.1.refs_0_), channel_id=1, source_target_pairs={{0,6},{1,7},{2,4},{3,5},{4,2},{5,3},{6,0},{7,1},{8,14},{9,15},{10,... | collective-permute-start | bytes 12296 | tf_op jit(solution)/shard_map/ppermute | solution.py:17
  7.1 0.9 %collective-permute-done.2.refs_3_ = s32[8,128]{1,0:T(8,128)S(1)} collective-permute-done((s32[8,128]{1,0:T(8,128)S(1)}, s32[8,128]{1,0:T(8,128)S(1)}, u32[]{:S(2)}, u32[]{:S(2)}) %collective-permute-start.2) | collective-permute-done | bytes 4128 | tf_op jit(solution)/shard_map/ppermute | solution.py:17
  8.0 2.0 %collective-permute-done.1.refs_2_ = s32[8,128]{1,0:T(8,128)S(1)} collective-permute-done((s32[8,128]{1,0:T(8,128)S(1)}, s32[8,128]{1,0:T(8,128)S(1)}, u32[]{:S(2)}, u32[]{:S(2)}) %collective-permute-start.1) | collective-permute-done | bytes 4128 | tf_op jit(solution)/shard_map/ppermute | solution.py:17
  10.5 1.2 %collective-permute-done.3.refs_2_ = s32[8,128]{1,0:T(8,128)S(1)} collective-permute-done((s32[8,128]{1,0:T(8,128)S(1)}, s32[8,128]{1,0:T(8,128)S(1)}, u32[]{:S(2)}, u32[]{:S(2)}) %collective-permute-start.3) | collective-permute-done | bytes 4128 | tf_op jit(solution)/shard_map/ppermute | solution.py:17
  11.7 1.6 %dense.1 = (bf16[48,2048]{1,0:T(8,128)(2,1)S(1)}, bf16[48,2048]{1,0:T(8,128)(2,1)S(1)}, bf16[48,2048]{1,0:T(8,128)(2,1)S(1)}, bf16[48,2048]{1,0:T(8,128)(2,1)S(1)}) custom-call(s32[1,128]{1,0:T(1,128)S(1)} %copy-done.1, s32[8,128]{1,0:T(8,128)S(1)} %pack.1.refs_1_, s32[8,128]{1,0:T(8,128)S(1)} %collective-permute-done.3.refs_2_, ...), custom_call_target="tpu_custom_call" | custom-call | flops 10000000000 | bytes 1319424 | tf_op jit(solution)/shard_map/dense/pallas_call | solution.py:36
  13.5 1.9 %collective-permute-start.6 = (bf16[48,2048]{1,0:T(8,128)(2,1)S(1)}, bf16[48,2048]{1,0:T(8,128)(2,1)S(1)}, u32[]{:S(2)}, u32[]{:S(2)}) collective-permute-start(bf16[48,2048]{1,0:T(8,128)(2,1)S(1)} %get-tuple-element.20), channel_id=1, source_target_pairs={{0,4},{1,5},{2,6},{3,7},{4,0},{5,1},{6,2},{7,3},{8,12},{9,13},{10,... | collective-permute-start | bytes 589832 | tf_op jit(solution)/shard_map/ppermute | solution.py:17
  15.4 1.4 %collective-permute-start.7 = (bf16[48,2048]{1,0:T(8,128)(2,1)S(1)}, bf16[48,2048]{1,0:T(8,128)(2,1)S(1)}, u32[]{:S(2)}, u32[]{:S(2)}) collective-permute-start(bf16[48,2048]{1,0:T(8,128)(2,1)S(1)} %get-tuple-element.21), channel_id=1, source_target_pairs={{0,6},{1,7},{2,4},{3,5},{4,2},{5,3},{6,0},{7,1},{8,14},{9,15},{10,... | collective-permute-start | bytes 589832 | tf_op jit(solution)/shard_map/ppermute | solution.py:17
  16.8 4.0 %load.1 = (bf16[1024,4096]{1,0:T(8,128)(2,1)S(1)}, f32[1,1024]{1,0:T(1,128)S(1)}) custom-call(bf16[1024,4096]{1,0:T(8,128)(2,1)} %refs_0_.6, bf16[48,2048]{1,0:T(8,128)(2,1)S(1)} %get-tuple-element.16.refs_1_.refs_0_), custom_call_target="tpu_custom_call" | custom-call | flops 10000000000 | bytes 16781312 | tf_op jit(solution)/shard_map/load/pallas_call | solution.py:36
  21.1 2.8 %collective-permute-done.6.refs_2_ = bf16[48,2048]{1,0:T(8,128)(2,1)S(1)} collective-permute-done((bf16[48,2048]{1,0:T(8,128)(2,1)S(1)}, bf16[48,2048]{1,0:T(8,128)(2,1)S(1)}, u32[]{:S(2)}, u32[]{:S(2)}) %collective-permute-start.6) | collective-permute-done | bytes 196640 | tf_op jit(solution)/shard_map/ppermute | solution.py:17
  23.8 1.6 %collective-permute-done.7.refs_3_ = bf16[48,2048]{1,0:T(8,128)(2,1)S(1)} collective-permute-done((bf16[48,2048]{1,0:T(8,128)(2,1)S(1)}, bf16[48,2048]{1,0:T(8,128)(2,1)S(1)}, u32[]{:S(2)}, u32[]{:S(2)}) %collective-permute-start.7) | collective-permute-done | bytes 196640 | tf_op jit(solution)/shard_map/ppermute | solution.py:17
  26.4 1.5 %collective-permute-start.8 = (bf16[48,2048]{1,0:T(8,128)(2,1)S(1)}, bf16[48,2048]{1,0:T(8,128)(2,1)S(1)}, u32[]{:S(2)}, u32[]{:S(2)}) collective-permute-start(bf16[48,2048]{1,0:T(8,128)(2,1)S(1)} %get-tuple-element.22.refs_0_), channel_id=1, source_target_pairs={{0,2},{1,3},{2,0},{3,1},{4,6},{5,7},{6,4},{7,5},{8,10},{9,11},{10,... | collective-permute-start | bytes 589832 | tf_op jit(solution)/shard_map/ppermute | solution.py:17
  27.9 3.6 %collective-permute-start.15 = (bf16[32,2048]{1,0:T(8,128)(2,1)S(1)}, bf16[32,2048]{1,0:T(8,128)(2,1)S(1)}, u32[]{:S(2)}, u32[]{:S(2)}) collective-permute-start(bf16[32,2048]{1,0:T(8,128)(2,1)S(1)} %get-tuple-element.25), channel_id=1, source_target_pairs={{0,24},{8,0},{16,8},{24,16},{1,25},{9,1},{17,9},{25,17},{2,26},{10... | collective-permute-start | bytes 393224 | tf_op jit(solution)/shard_map/ppermute | solution.py:266
  31.5 1.0 %collective-permute-start.13 = (bf16[32,2048]{1,0:T(8,128)(2,1)S(1)}, bf16[32,2048]{1,0:T(8,128)(2,1)S(1)}, u32[]{:S(2)}, u32[]{:S(2)}) collective-permute-start(bf16[32,2048]{1,0:T(8,128)(2,1)S(1)} %get-tuple-element.25), channel_id=1, source_target_pairs={{0,8},{8,16},{16,24},{24,0},{1,9},{9,17},{17,25},{25,1},{2,10},{10... | collective-permute-start | bytes 393224 | tf_op jit(solution)/shard_map/ppermute | solution.py:266
  33.2 1.3 %collective-permute-start.10 = (bf16[48,1024]{1,0:T(8,128)(2,1)S(1)}, bf16[48,1024]{1,0:T(8,128)(2,1)S(1)}, u32[]{:S(2)}, u32[]{:S(2)}) collective-permute-start(bf16[48,1024]{1,0:T(8,128)(2,1)S(1)} %join.8), channel_id=1, source_target_pairs={{0,4},{1,5},{2,6},{3,7},{4,0},{5,1},{6,2},{7,3},{8,12},{9,13},{10,... | collective-permute-start | bytes 294920 | tf_op jit(solution)/shard_map/ppermute | solution.py:17
  34.4 2.8 %collective-permute-done.11.refs_4_ = bf16[48,1024]{1,0:T(8,128)(2,1)S(1)} collective-permute-done((bf16[48,1024]{1,0:T(8,128)(2,1)S(1)}, bf16[48,1024]{1,0:T(8,128)(2,1)S(1)}, u32[]{:S(2)}, u32[]{:S(2)}) %collective-permute-start.11) | collective-permute-done | bytes 98336 | tf_op jit(solution)/shard_map/ppermute | solution.py:17
  38.0 4.2 %collective-permute-done.14.refs_1_ = bf16[32,2048]{1,0:T(8,128)(2,1)S(1)} collective-permute-done((bf16[32,2048]{1,0:T(8,128)(2,1)S(1)}, bf16[32,2048]{1,0:T(8,128)(2,1)S(1)}, u32[]{:S(2)}, u32[]{:S(2)}) %collective-permute-start.14) | collective-permute-done | bytes 131104 | tf_op jit(solution)/shard_map/ppermute | solution.py:266
  42.9 1.2 %collective-permute-start.16 = (bf16[96,2048]{1,0:T(8,128)(2,1)S(1)}, bf16[96,2048]{1,0:T(8,128)(2,1)S(1)}, u32[]{:S(2)}, u32[]{:S(2)}) collective-permute-start(bf16[96,2048]{1,0:T(8,128)(2,1)S(1)} %join.10.refs_0_), channel_id=1, source_target_pairs={{0,2},{1,3},{2,0},{3,1},{4,6},{5,7},{6,4},{7,5},{8,10},{9,11},{10,... | collective-permute-start | bytes 1179656 | tf_op jit(solution)/shard_map/ppermute | solution.py:17
  44.2 3.6 %group.1 = (f32[1,1024]{1,0:T(1,128)}, f32[1,1024]{1,0:T(1,128)S(1)}) custom-call(bf16[1024,4096]{1,0:T(8,128)(2,1)S(1)} %get-tuple-element.17.refs_0_, f32[1,1024]{1,0:T(1,128)S(1)} %get-tuple-element.18.refs_4_.refs_1_.refs_2_, bf16[192,2048]{1,0:T(8,128)(2,1)S(1)} %square.1.refs_2_.refs_3_, bf16[192,2048]{1,0:T(8,128)(2,1)S(1)} %collective-permute-done.12.refs_3_), custom_call_target="tpu_custom_call" | custom-call | flops 10000000000 | bytes 9973760 | tf_op jit(solution)/shard_map/group/pallas_call | solution.py:36
  47.7 4.4 %collective-permute-done.17.refs_2_.refs_0_ = bf16[96,2048]{1,0:T(8,128)(2,1)S(1)} collective-permute-done((bf16[96,2048]{1,0:T(8,128)(2,1)S(1)}, bf16[96,2048]{1,0:T(8,128)(2,1)S(1)}, u32[]{:S(2)}, u32[]{:S(2)}) %collective-permute-start.17) | collective-permute-done | bytes 393248 | tf_op jit(solution)/shard_map/ppermute | solution.py:17
  52.7 1.5 %collective-permute-start.20 = (bf16[96,1024]{1,0:T(8,128)(2,1)S(1)}, bf16[96,1024]{1,0:T(8,128)(2,1)S(1)}, u32[]{:S(2)}, u32[]{:S(2)}) collective-permute-start(bf16[96,1024]{1,0:T(8,128)(2,1)S(1)} %join.13), channel_id=1, source_target_pairs={{0,2},{1,3},{2,0},{3,1},{4,6},{5,7},{6,4},{7,5},{8,10},{9,11},{10,... | collective-permute-start | bytes 589832 | tf_op jit(solution)/shard_map/ppermute | solution.py:17
  55.5 2.7 %far.1.refs_1_ = f32[1,1024]{1,0:T(1,128)S(1)} custom-call(bf16[1024,4096]{1,0:T(8,128)(2,1)S(1)} %get-tuple-element.17.refs_0_, f32[1,1024]{1,0:T(1,128)S(1)} %get-tuple-element.24.refs_3_.refs_1_, bf16[288,2048]{1,0:T(8,128)(2,1)S(1)} %join.11.refs_2_, bf16[288,2048]{1,0:T(8,128)(2,1)S(1)} %collective-permute-done.18.refs_3_), custom_call_target="tpu_custom_call" | custom-call | flops 10000000000 | bytes 10756096 | tf_op jit(solution)/shard_map/far/pallas_call | solution.py:36
  58.2 3.1 %collective-permute-done.19.refs_0_.refs_3_ = bf16[96,1024]{1,0:T(8,128)(2,1)S(1)} collective-permute-done((bf16[96,1024]{1,0:T(8,128)(2,1)S(1)}, bf16[96,1024]{1,0:T(8,128)(2,1)S(1)}, u32[]{:S(2)}, u32[]{:S(2)}) %collective-permute-start.19) | collective-permute-done | bytes 196640 | tf_op jit(solution)/shard_map/ppermute | solution.py:17
  63.1 3.3 %far_last.1 = f32[1,1024]{1,0:T(1,128)} custom-call(bf16[1024,4096]{1,0:T(8,128)(2,1)S(1)} %get-tuple-element.17.refs_0_, f32[1,1024]{1,0:T(1,128)S(1)} %far.1.refs_1_, f32[1,1024]{1,0:T(1,128)S(1)} %get-tuple-element.18.refs_4_.refs_1_.refs_2_, bf16[96,1024]{1,0:T(8,128)(2,1)S(1)} %collective-permute-done.19.refs_0_.refs_3_, ...), custom_call_target="tpu_custom_call" | custom-call | flops 10000000000 | bytes 9187328 | tf_op jit(solution)/shard_map/far_last/pallas_call | solution.py:36
  (44 shorter events, 8.8 us)
Async XLA Ops:
  1.7 10.0 %collective-permute-start.4 = (bf16[64,2048]{1,0:T(8,128)(2,1)S(1)}, bf16[64,2048]{1,0:T(8,128)(2,1)S(1)}, u32[]{:S(2)}, u32[]{:S(2)}) collective-permute-start(bf16[64,2048]{1,0:T(8,128)(2,1)S(1)} %get-tuple-element.15), channel_id=1, source_target_pairs={{0,1},{1,0},{2,3},{3,2},{4,5},{5,4},{6,7},{7,6},{8,9},{9,8},{10,11... | collective-permute-start | bytes 786440 | tf_op jit(solution)/shard_map/ppermute | solution.py:17
  2.9 8.8 %copy-start.1 = (s32[1,128]{1,0:T(1,128)S(1)}, s32[1,128]{1,0:T(1,128)}, u32[]{:S(2)}) copy-start(s32[1,128]{1,0:T(1,128)} %refs_0_.5) | copy-start | bytes 1540
  2.9 5.1 %collective-permute-start.2 = (s32[8,128]{1,0:T(8,128)S(1)}, s32[8,128]{1,0:T(8,128)S(1)}, u32[]{:S(2)}, u32[]{:S(2)}) collective-permute-start(s32[8,128]{1,0:T(8,128)S(1)} %spread.1.refs_0_), channel_id=1, source_target_pairs={{0,6},{1,7},{2,4},{3,5},{4,2},{5,3},{6,0},{7,1},{8,14},{9,15},{10,... | collective-permute-start | bytes 12296 | tf_op jit(solution)/shard_map/ppermute | solution.py:17
  6.4 3.6 %collective-permute-start.1 = (s32[8,128]{1,0:T(8,128)S(1)}, s32[8,128]{1,0:T(8,128)S(1)}, u32[]{:S(2)}, u32[]{:S(2)}) collective-permute-start(s32[8,128]{1,0:T(8,128)S(1)} %spread.1.refs_0_), channel_id=1, source_target_pairs={{0,4},{1,5},{2,6},{3,7},{4,0},{5,1},{6,2},{7,3},{8,12},{9,13},{10,... | collective-permute-start | bytes 12296 | tf_op jit(solution)/shard_map/ppermute | solution.py:17
  6.9 3.6 %collective-permute-start = (s32[8,128]{1,0:T(8,128)S(1)}, s32[8,128]{1,0:T(8,128)S(1)}, u32[]{:S(2)}, u32[]{:S(2)}) collective-permute-start(s32[8,128]{1,0:T(8,128)S(1)} %spread.1.refs_0_), channel_id=1, source_target_pairs={{0,2},{1,3},{2,0},{3,1},{4,6},{5,7},{6,4},{7,5},{8,10},{9,11},{10,... | collective-permute-start | bytes 12296 | tf_op jit(solution)/shard_map/ppermute | solution.py:17
  10.5 1.2 %collective-permute-start.3 = (s32[8,128]{1,0:T(8,128)S(1)}, s32[8,128]{1,0:T(8,128)S(1)}, u32[]{:S(2)}, u32[]{:S(2)}) collective-permute-start(s32[8,128]{1,0:T(8,128)S(1)} %pack.1.refs_1_), channel_id=1, source_target_pairs={{0,1},{1,0},{2,3},{3,2},{4,5},{5,4},{6,7},{7,6},{8,9},{9,8},{10,11... | collective-permute-start | bytes 12296 | tf_op jit(solution)/shard_map/ppermute | solution.py:17
  13.3 7.8 %collective-permute-start.5 = (bf16[48,2048]{1,0:T(8,128)(2,1)S(1)}, bf16[48,2048]{1,0:T(8,128)(2,1)S(1)}, u32[]{:S(2)}, u32[]{:S(2)}) collective-permute-start(bf16[48,2048]{1,0:T(8,128)(2,1)S(1)} %get-tuple-element.19), channel_id=1, source_target_pairs={{0,2},{1,3},{2,0},{3,1},{4,6},{5,7},{6,4},{7,5},{8,10},{9,11},{10,... | collective-permute-start | bytes 589832 | tf_op jit(solution)/shard_map/ppermute | solution.py:17
  13.5 10.4 %collective-permute-start.6 = (bf16[48,2048]{1,0:T(8,128)(2,1)S(1)}, bf16[48,2048]{1,0:T(8,128)(2,1)S(1)}, u32[]{:S(2)}, u32[]{:S(2)}) collective-permute-start(bf16[48,2048]{1,0:T(8,128)(2,1)S(1)} %get-tuple-element.20), channel_id=1, source_target_pairs={{0,4},{1,5},{2,6},{3,7},{4,0},{5,1},{6,2},{7,3},{8,12},{9,13},{10,... | collective-permute-start | bytes 589832 | tf_op jit(solution)/shard_map/ppermute | solution.py:17
  15.4 10.1 %collective-permute-start.7 = (bf16[48,2048]{1,0:T(8,128)(2,1)S(1)}, bf16[48,2048]{1,0:T(8,128)(2,1)S(1)}, u32[]{:S(2)}, u32[]{:S(2)}) collective-permute-start(bf16[48,2048]{1,0:T(8,128)(2,1)S(1)} %get-tuple-element.21), channel_id=1, source_target_pairs={{0,6},{1,7},{2,4},{3,5},{4,2},{5,3},{6,0},{7,1},{8,14},{9,15},{10,... | collective-permute-start | bytes 589832 | tf_op jit(solution)/shard_map/ppermute | solution.py:17
  25.5 7.0 %collective-permute-start.9 = (bf16[48,2048]{1,0:T(8,128)(2,1)S(1)}, bf16[48,2048]{1,0:T(8,128)(2,1)S(1)}, u32[]{:S(2)}, u32[]{:S(2)}) collective-permute-start(bf16[48,2048]{1,0:T(8,128)(2,1)S(1)} %get-tuple-element.22.refs_0_), channel_id=1, source_target_pairs={{0,4},{1,5},{2,6},{3,7},{4,0},{5,1},{6,2},{7,3},{8,12},{9,13},{10,... | collective-permute-start | bytes 589832 | tf_op jit(solution)/shard_map/ppermute | solution.py:17
  26.4 6.7 %collective-permute-start.8 = (bf16[48,2048]{1,0:T(8,128)(2,1)S(1)}, bf16[48,2048]{1,0:T(8,128)(2,1)S(1)}, u32[]{:S(2)}, u32[]{:S(2)}) collective-permute-start(bf16[48,2048]{1,0:T(8,128)(2,1)S(1)} %get-tuple-element.22.refs_0_), channel_id=1, source_target_pairs={{0,2},{1,3},{2,0},{3,1},{4,6},{5,7},{6,4},{7,5},{8,10},{9,11},{10,... | collective-permute-start | bytes 589832 | tf_op jit(solution)/shard_map/ppermute | solution.py:17
  27.9 10.1 %collective-permute-start.15 = (bf16[32,2048]{1,0:T(8,128)(2,1)S(1)}, bf16[32,2048]{1,0:T(8,128)(2,1)S(1)}, u32[]{:S(2)}, u32[]{:S(2)}) collective-permute-start(bf16[32,2048]{1,0:T(8,128)(2,1)S(1)} %get-tuple-element.25), channel_id=1, source_target_pairs={{0,24},{8,0},{16,8},{24,16},{1,25},{9,1},{17,9},{25,17},{2,26},{10... | collective-permute-start | bytes 393224 | tf_op jit(solution)/shard_map/ppermute | solution.py:266
  31.5 10.7 %collective-permute-start.14 = (bf16[32,2048]{1,0:T(8,128)(2,1)S(1)}, bf16[32,2048]{1,0:T(8,128)(2,1)S(1)}, u32[]{:S(2)}, u32[]{:S(2)}) collective-permute-start(bf16[32,2048]{1,0:T(8,128)(2,1)S(1)} %get-tuple-element.25), channel_id=1, source_target_pairs={{0,16},{8,24},{16,0},{24,8},{1,17},{9,25},{17,1},{25,9},{2,18},{10... | collective-permute-start | bytes 393224 | tf_op jit(solution)/shard_map/ppermute | solution.py:266
  31.5 10.7 %collective-permute-start.13 = (bf16[32,2048]{1,0:T(8,128)(2,1)S(1)}, bf16[32,2048]{1,0:T(8,128)(2,1)S(1)}, u32[]{:S(2)}, u32[]{:S(2)}) collective-permute-start(bf16[32,2048]{1,0:T(8,128)(2,1)S(1)} %get-tuple-element.25), channel_id=1, source_target_pairs={{0,8},{8,16},{16,24},{24,0},{1,9},{9,17},{17,25},{25,1},{2,10},{10... | collective-permute-start | bytes 393224 | tf_op jit(solution)/shard_map/ppermute | solution.py:266
  32.5 4.7 %collective-permute-start.11 = (bf16[48,1024]{1,0:T(8,128)(2,1)S(1)}, bf16[48,1024]{1,0:T(8,128)(2,1)S(1)}, u32[]{:S(2)}, u32[]{:S(2)}) collective-permute-start(bf16[48,1024]{1,0:T(8,128)(2,1)S(1)} %join.9), channel_id=1, source_target_pairs={{0,2},{1,3},{2,0},{3,1},{4,6},{5,7},{6,4},{7,5},{8,10},{9,11},{10,... | collective-permute-start | bytes 294920 | tf_op jit(solution)/shard_map/ppermute | solution.py:17
  33.2 4.7 %collective-permute-start.10 = (bf16[48,1024]{1,0:T(8,128)(2,1)S(1)}, bf16[48,1024]{1,0:T(8,128)(2,1)S(1)}, u32[]{:S(2)}, u32[]{:S(2)}) collective-permute-start(bf16[48,1024]{1,0:T(8,128)(2,1)S(1)} %join.8), channel_id=1, source_target_pairs={{0,4},{1,5},{2,6},{3,7},{4,0},{5,1},{6,2},{7,3},{8,12},{9,13},{10,... | collective-permute-start | bytes 294920 | tf_op jit(solution)/shard_map/ppermute | solution.py:17
  37.9 6.3 %collective-permute-start.12 = (bf16[192,2048]{1,0:T(8,128)(2,1)S(1)}, bf16[192,2048]{1,0:T(8,128)(2,1)S(1)}, u32[]{:S(2)}, u32[]{:S(2)}) collective-permute-start(bf16[192,2048]{1,0:T(8,128)(2,1)S(1)} %square.1.refs_2_.refs_3_), channel_id=1, source_target_pairs={{0,1},{1,0},{2,3},{3,2},{4,5},{5,4},{6,7},{7,6},{8,9},{9,8},{10,11... | collective-permute-start | bytes 2359304 | tf_op jit(solution)/shard_map/ppermute | solution.py:17
  42.3 9.9 %collective-permute-start.17 = (bf16[96,2048]{1,0:T(8,128)(2,1)S(1)}, bf16[96,2048]{1,0:T(8,128)(2,1)S(1)}, u32[]{:S(2)}, u32[]{:S(2)}) collective-permute-start(bf16[96,2048]{1,0:T(8,128)(2,1)S(1)} %join.10.refs_0_), channel_id=1, source_target_pairs={{0,4},{1,5},{2,6},{3,7},{4,0},{5,1},{6,2},{7,3},{8,12},{9,13},{10,... | collective-permute-start | bytes 1179656 | tf_op jit(solution)/shard_map/ppermute | solution.py:17
  42.9 9.6 %collective-permute-start.16 = (bf16[96,2048]{1,0:T(8,128)(2,1)S(1)}, bf16[96,2048]{1,0:T(8,128)(2,1)S(1)}, u32[]{:S(2)}, u32[]{:S(2)}) collective-permute-start(bf16[96,2048]{1,0:T(8,128)(2,1)S(1)} %join.10.refs_0_), channel_id=1, source_target_pairs={{0,2},{1,3},{2,0},{3,1},{4,6},{5,7},{6,4},{7,5},{8,10},{9,11},{10,... | collective-permute-start | bytes 1179656 | tf_op jit(solution)/shard_map/ppermute | solution.py:17
  52.6 2.9 %collective-permute-start.18 = (bf16[288,2048]{1,0:T(8,128)(2,1)S(1)}, bf16[288,2048]{1,0:T(8,128)(2,1)S(1)}, u32[]{:S(2)}, u32[]{:S(2)}) collective-permute-start(bf16[288,2048]{1,0:T(8,128)(2,1)S(1)} %join.11.refs_2_), channel_id=1, source_target_pairs={{0,1},{1,0},{2,3},{3,2},{4,5},{5,4},{6,7},{7,6},{8,9},{9,8},{10,11... | collective-permute-start | bytes 3538952 | tf_op jit(solution)/shard_map/ppermute | solution.py:17
  52.7 8.7 %collective-permute-start.20 = (bf16[96,1024]{1,0:T(8,128)(2,1)S(1)}, bf16[96,1024]{1,0:T(8,128)(2,1)S(1)}, u32[]{:S(2)}, u32[]{:S(2)}) collective-permute-start(bf16[96,1024]{1,0:T(8,128)(2,1)S(1)} %join.13), channel_id=1, source_target_pairs={{0,2},{1,3},{2,0},{3,1},{4,6},{5,7},{6,4},{7,5},{8,10},{9,11},{10,... | collective-permute-start | bytes 589832 | tf_op jit(solution)/shard_map/ppermute | solution.py:17
  54.2 7.1 %collective-permute-start.19 = (bf16[96,1024]{1,0:T(8,128)(2,1)S(1)}, bf16[96,1024]{1,0:T(8,128)(2,1)S(1)}, u32[]{:S(2)}, u32[]{:S(2)}) collective-permute-start(bf16[96,1024]{1,0:T(8,128)(2,1)S(1)} %join.12), channel_id=1, source_target_pairs={{0,4},{1,5},{2,6},{3,7},{4,0},{5,1},{6,2},{7,3},{8,12},{9,13},{10,... | collective-permute-start | bytes 589832 | tf_op jit(solution)/shard_map/ppermute | solution.py:17
  61.3 1.5 %collective-permute-start.21 = (bf16[96,1024]{1,0:T(8,128)(2,1)S(1)}, bf16[96,1024]{1,0:T(8,128)(2,1)S(1)}, u32[]{:S(2)}, u32[]{:S(2)}) collective-permute-start(bf16[96,1024]{1,0:T(8,128)(2,1)S(1)} %join.14), channel_id=1, source_target_pairs={{0,1},{1,0},{2,3},{3,2},{4,5},{5,4},{6,7},{7,6},{8,9},{9,8},{10,11... | collective-permute-start | bytes 589832 | tf_op jit(solution)/shard_map/ppermute | solution.py:17
  61.4 1.7 %collective-permute-start.22 = (bf16[96,1024]{1,0:T(8,128)(2,1)S(1)}, bf16[96,1024]{1,0:T(8,128)(2,1)S(1)}, u32[]{:S(2)}, u32[]{:S(2)}) collective-permute-start(bf16[96,1024]{1,0:T(8,128)(2,1)S(1)} %join.15), channel_id=1, source_target_pairs={{0,1},{1,0},{2,3},{3,2},{4,5},{5,4},{6,7},{7,6},{8,9},{9,8},{10,11... | collective-permute-start | bytes 589832 | tf_op jit(solution)/shard_map/ppermute | solution.py:17
  (1 other events, 1.0 us)

commit v11 on v10

--- a/solution.py
+++ b/solution.py
@@ -49,13 +49,9 @@
     out[...] = jnp.broadcast_to(count_ref[0, 0], out.shape)
 
 
-def pack_kernel(*refs):
-    *counts, out = refs
+def pair_kernel(own, sib, out):
     lane = lax.broadcasted_iota(jnp.int32, out.shape, 1)
-    total = counts[0][...]
-    for d, ref in enumerate(counts):
-        total = jnp.where(lane == d, ref[...], total)
-    out[...] = total
+    out[...] = jnp.where(lane == 0, own[...], sib[...])
 
 
 def split_kernel(rows_ref, keep_ref, send_ref):
@@ -91,31 +87,32 @@
         norm_ref[:, t * TILE : (t + 1) * TILE] = jnp.sum(squares.T, axis=0, keepdims=True)
 
 
-def join_kernel(count, start, *refs):
-    blocks, out = refs[:count], refs[count]
-    rows = blocks[0].shape[0]
-    for i, block in enumerate(blocks):
-        out[i * rows : (i + 1) * rows, :] = block[:, start : start + out.shape[1]]
+def stack_kernel(start, *refs):
+    *blocks, out = refs
+    top = 0
+    for block in blocks:
+        rows = block.shape[0]
+        out[top : top + rows, :] = block[:, start : start + out.shape[1]]
+        top += rows
 
 
 def dense_kernel(size, picks_chip, rest_chip, chosen_ref, *refs):
     chips = size // 2
-    *counts, own, sib = refs[:4]
-    outs, select_ref = refs[4:-1], refs[-1]
+    counts, (own, sib, *outs, select_ref) = refs[:chips], refs[chips:]
     slots, picks = own.shape[0], chosen_ref.shape[1]
     rows_chip = picks_chip + rest_chip
     me = lax.axis_index("mem")
     offsets = [jnp.zeros((1, 1), jnp.int32) for _ in range(2)]
-    for d in range(chips):
-        for h, ref in enumerate(counts):
+    for d, ref in enumerate(counts):
+        for h in range(2):
             origin = lax.bitwise_xor(me, 2 * d + h)
             for k in range(2):
                 before = (origin < lax.bitwise_xor(me, k)).astype(jnp.int32)
-                offsets[k] += ref[:1, d : d + 1] * before
+                offsets[k] += ref[:1, h : h + 1] * before
     lane = lax.broadcasted_iota(jnp.int32, (1, 2 * slots), 1)
     first = lane < slots
     within = jnp.where(first, lane, lane - slots)
-    alive = within < jnp.where(first, counts[0][:1, :1], counts[1][:1, :1])
+    alive = within < jnp.where(first, counts[0][:1, :1], counts[0][:1, 1:2])
     position = jnp.where(alive, within + jnp.where(first, offsets[0], offsets[1]), -1)
 
     chosen = chosen_ref[...]
@@ -156,14 +153,6 @@
     picks_ref[...] = total[: picks_ref.shape[0], :]
 
 
-def square_kernel(own, first, second, left, right, out):
-    rows, part = left.shape
-    for i, block in enumerate((own, first, second)):
-        out[i * rows : (i + 1) * rows, :] = block[...]
-    out[3 * rows :, :part] = left[...]
-    out[3 * rows :, part:] = right[...]
-
-
 def row_norms(rows):
     rows = rows.astype(F32)
     return jnp.sum(rows * rows, axis=1, keepdims=True)
@@ -180,40 +169,48 @@
     return [slice(t, t + TILE) for t in range(0, cand_ref.shape[0], TILE)]
 
 
-def group_kernel(rows_chip, picks_chip, cand_ref, norm_ref, own, sib, near_ref, best_ref, rows_ref):
-    half = own.shape[1]
-    rows_ref[:, :half] = own[...]
-    rows_ref[:, half:] = sib[...]
-    norms = row_norms(rows_ref[...])
-    down = lax.broadcasted_iota(jnp.int32, norms.shape, 0)
-    outside = jnp.where(lax.rem(down, rows_chip) < picks_chip, 0.0, jnp.inf)
+def lay_out(row_blocks, rows_ref):
+    top = 0
+    for parts in row_blocks:
+        left, rows = 0, parts[0].shape[0]
+        for part in parts:
+            rows_ref[top : top + rows, left : left + part.shape[1]] = part[...]
+            left += part.shape[1]
+        top += rows
+    return row_norms(rows_ref[...])
+
+
+def row_masks(picks_chip, rows_chip, mixed_chip, mixed, rows):
+    row = lax.broadcasted_iota(jnp.int32, (rows, 1), 0)
+    place = lax.rem(row, mixed_chip)
+    own = (row < mixed) & (place < rows_chip)
+    pick = (row >= mixed) | (place < picks_chip) | (place >= rows_chip)
+    return jnp.where(own, 0.0, jnp.inf), jnp.where(pick, 0.0, jnp.inf)
+
+
+def least(gaps):
+    return jnp.min(gaps, axis=0, keepdims=True)
+
+
+def first_kernel(chip_rows, cand_ref, own, sib, near_ref, best_ref, rows_ref):
+    norms = lay_out([(own, sib)], rows_ref)
+    no_row, no_pick = row_masks(*chip_rows, norms.shape[0], norms.shape[0])
     for at in tiles_of(cand_ref):
         gaps = gaps_to(rows_ref, norms, cand_ref[at, :])
-        near_ref[:, at] = jnp.min(gaps, axis=0, keepdims=True) + norm_ref[:, at]
-        best_ref[:, at] = jnp.min(gaps + outside, axis=0, keepdims=True)
-
-
-def far_kernel(cand_ref, best_ref, own, sib, out, rows_ref):
-    half = own.shape[1]
-    rows_ref[:, :half] = own[...]
-    rows_ref[:, half:] = sib[...]
-    norms = row_norms(rows_ref[...])
+        near_ref[:, at] = least(gaps + no_row)
+        best_ref[:, at] = least(gaps + no_pick)
+
+
+def last_kernel(
+    chip_rows, cand_ref, norm_ref, near_ref, best_ref, mid, mid_sib, *refs
+):
+    *corner, near_out, best_out, rows_ref = refs
+    norms = lay_out([corner, (mid, mid_sib)], rows_ref)
+    no_row, no_pick = row_masks(*chip_rows, corner[0].shape[0], norms.shape[0])
     for at in tiles_of(cand_ref):
         gaps = gaps_to(rows_ref, norms, cand_ref[at, :])
-        out[:, at] = jnp.minimum(jnp.min(gaps, axis=0, keepdims=True), best_ref[:, at])
-
-
-def last_kernel(cand_ref, best_ref, norm_ref, *refs):
-    *parts, out, rows_ref = refs
-    start = 0
-    for part in parts:
-        rows_ref[:, start : start + part.shape[1]] = part[...]
-        start += part.shape[1]
-    norms = row_norms(rows_ref[...])
-    for at in tiles_of(cand_ref):
-        gaps = gaps_to(rows_ref, norms, cand_ref[at, :])
-        least = jnp.minimum(jnp.min(gaps, axis=0, keepdims=True), best_ref[:, at])
-        out[:, at] = least + norm_ref[:, at]
+        near_out[:, at] = jnp.minimum(least(gaps + no_row), near_ref[:, at]) + norm_ref[:, at]
+        best_out[:, at] = jnp.minimum(least(gaps + no_pick), best_ref[:, at]) + norm_ref[:, at]
 
 
 def body(candidates, round_one, counts, chosen):
@@ -229,11 +226,10 @@
     def bf16(*dims):
         return jax.ShapeDtypeStruct(dims, BF16)
 
-    def join(blocks, columns, start=0, after=(), weight=WEIGHT):
-        count = blocks[0].shape[0] * len(blocks)
+    def stack(blocks, columns=half, start=0, after=()):
         return call(
-            functools.partial(join_kernel, len(blocks), start), "join", bf16(count, columns),
-            blocks, after=after, weight=weight,
+            functools.partial(stack_kernel, start), "stack",
+            bf16(sum(b.shape[0] for b in blocks), columns), blocks, after=after, weight=0,
         )
 
     line = jax.ShapeDtypeStruct((1, rows), F32)
@@ -241,14 +237,14 @@
     count = call(
         spread_kernel, "spread", tile, (counts,), specs=[pl.BlockSpec(memory_space=pltpu.SMEM)]
     )
-    mine = call(pack_kernel, "pack", tile, to_chips(count, size), weight=0)
-    theirs = flip_permute(mine, size, 1)
+    pair = call(pair_kernel, "pair", tile, (count, flip_permute(count, size, 1)))
+    pairs = to_chips(pair, size)
     own, send = call(split_kernel, "split", [bf16(slots, half)] * 2, (round_one,))
     sib = flip_permute(send, size, 1)
 
     parts = call(
         functools.partial(dense_kernel, size, picks_chip, rest_chip), "dense",
-        [bf16(rows_chip, half)] * chips, (chosen, mine, theirs, own, sib),
+        [bf16(rows_chip, half)] * chips, (chosen, *pairs, own, sib),
         scratch=[pltpu.VMEM((live, 2 * slots), BF16)],
     )
     cand, norm = call(
@@ -262,46 +258,42 @@
         after=(norm,),
     )
 
+    middle = groups // 2
     shifted = [
         lax.ppermute(picked, "grp", [(g, (g + k) % groups) for g in range(groups)])
         for k in range(1, groups)
     ]
-    def corner(first, second, weight):
-        left = flip_permute(join((first,), half // 2, weight=weight), size, 4)
-        right = flip_permute(join((second,), half // 2, half // 2, weight=weight), size, 2)
-        return left, right
+    far = [shifted[k - 1] for k in range(1, groups) if k != middle]
 
     if chips == 4:
-        first, second = (flip_permute(owned, size, flip) for flip in (2, 4))
-        dense = call(
-            square_kernel, "square", bf16(live, half),
-            (owned, first, second, *corner(first, second, 0)), weight=0,
-        )
+        own_x, own_y = (flip_permute(owned, size, flip) for flip in (2, 4))
+        close = stack(far, after=(own_x, own_y))
+        close_x, close_y = (flip_permute(close, size, flip) for flip in (2, 4))
+        early = stack((owned, close, own_x, close_x, own_y, close_y), after=shifted[middle - 1 : middle])
+        left = stack((own_x, close_x), half // 2)
+        right = stack((own_y, close_y), half // 2, half // 2)
+        corner = (flip_permute(left, size, 4), flip_permute(right, size, 2))
     else:
-        dense = join(to_chips(owned, size), half)
+        close = stack(far)
+        *early, end = to_chips(stack((owned, close)), size)
+        early, corner = stack(early), (end,)
+    mid = to_chips(shifted[middle - 1], size)
+
+    chip_rows = (picks_chip, rows_chip, owned.shape[0] + close.shape[0])
     near, best = call(
-        functools.partial(group_kernel, rows_chip, picks_chip), "group", [line] * 2,
-        (cand, norm, dense, flip_permute(dense, size, 1)),
-        scratch=[pltpu.VMEM((live, width), BF16)],
-    )
-
-    block = join(shifted, half, after=(dense,))
-    if chips == 4:
-        first, second = (flip_permute(block, size, flip) for flip in (2, 4))
-        blocks, last = (block, first, second), corner(first, second, 0)
-    else:
-        *blocks, end = to_chips(block, size)
-        last = (end,)
-    early = join(blocks, half, after=(best,))
-    best = call(
-        far_kernel, "far", line, (cand, best, early, flip_permute(early, size, 1)),
-        scratch=[pltpu.VMEM((early.shape[0], width), BF16)],
-    )
-    sent = [join((part,), part.shape[1], after=(best,), weight=0) for part in last]
-    final = call(
-        last_kernel, "far_last", line,
-        (cand, best, norm, *last, *[flip_permute(part, size, 1) for part in sent]),
-        scratch=[pltpu.VMEM((block.shape[0], width), BF16)],
+        functools.partial(first_kernel, chip_rows), "products", [line] * 2,
+        (cand, early, flip_permute(early, size, 1)),
+        scratch=[pltpu.VMEM((early.shape[0], width), BF16)], weight=WEIGHT // 3,
+    )
+    mid = stack(mid, after=(best,))
+    sent = [stack((part,), part.shape[1], after=(best,)) for part in corner]
+    near, final = call(
+        functools.partial(last_kernel, chip_rows), "products_last", [line] * 2,
+        (
+            cand, norm, near, best, mid, flip_permute(mid, size, 1),
+            *corner, *[flip_permute(part, size, 1) for part in sent],
+        ),
+        scratch=[pltpu.VMEM((corner[0].shape[0] + mid.shape[0], width), BF16)],
     )
     return near.reshape(-1), final.reshape(-1)
 

time: 66.5 us -> 66.1 us (level)
  Pallas kernels: 15.4 us -> 12.1 us
  starting transfers between devices: 21.8 us -> 23.9 us
  waiting for transfers between devices: 26.7 us -> 28.1 us
    ppermute x3, waiting for transfers between devices: 4.25 us -> 10.2 us  [body(): lax.ppermute(picked, 'grp', [(g, (g + k) % groups) for g in range(groups)])]
    ppermute x20 -> x21, waiting for transfers between devices: 22.4 us -> 17.9 us  [flip_permute(): return lax.ppermute(block, 'mem', [(m, m ^ flip) for m in range(size)])]
    pallas_call x18 -> x15, Pallas kernels: 15.4 us -> 12.1 us  [call(): pl.pallas_call(run, out_shape=out_shape, in_specs=(specs or vmem_specs(co...]
    ppermute x20 -> x21, starting transfers between devices: 17.2 us -> 18.9 us  [flip_permute(): return lax.ppermute(block, 'mem', [(m, m ^ flip) for m in range(size)])]
  transfers between devices with their start and end apart: 23 -> 24, of which waited for: 16 -> 12; matrix products, arithmetic and copies ran while one was open for 0% -> 0% of each run, Pallas kernels for 16% -> 11%
where the time goes in v11:
time: 66.1 us; the launch traced here: 66 us
  waiting for transfers between devices  28.1 us (43%)
  starting transfers between devices  23.9 us (36%)
  Pallas kernels  12.1 us (18%)
  between operations  1.41 us (2%)
    ppermute x21, starting transfers between devices, flip_permute(): return lax.ppermute(block, 'mem', [(m, m ^ flip) for m in range(size)])  18.9 us
    ppermute x21, waiting for transfers between devices, flip_permute(): return lax.ppermute(block, 'mem', [(m, m ^ flip) for m in range(size)])  17.9 us
    pallas_call x15, Pallas kernels, call(): pl.pallas_call(run, out_shape=out_shape, in_specs=(specs or vmem_specs(co...  12.1 us
    ppermute x3, waiting for transfers between devices, body(): lax.ppermute(picked, 'grp', [(g, (g + k) % groups) for g in range(groups)])  10.2 us
    ppermute x3, starting transfers between devices, body(): lax.ppermute(picked, 'grp', [(g, (g + k) % groups) for g in range(groups)])  5 us
  transfers between devices with their start and end apart: 24, of which 12 were waited for; matrix products, arithmetic and copies ran while one was open for 0% of the time, Pallas kernels for 11%

profile of v11, /device:TPU:0, one launch (start us, length us, event | category | flops | bytes accessed | tf_op | source)
XLA Modules:
  0.0 66.0 jit_solution(9128499849660572825)
XLA Ops:
  2.9 2.6 %collective-permute-start.1 = (s32[8,128]{1,0:T(8,128)S(1)}, s32[8,128]{1,0:T(8,128)S(1)}, u32[]{:S(2)}, u32[]{:S(2)}) collective-permute-start(s32[8,128]{1,0:T(8,128)S(1)} %pair.1.refs_1_), channel_id=1, source_target_pairs={{0,2},{1,3},{2,0},{3,1},{4,6},{5,7},{6,4},{7,5},{8,10},{9,11},{10,... | collective-permute-start | bytes 12296 | tf_op jit(solution)/shard_map/ppermute | solution.py:17
  5.5 1.5 %collective-permute-start.2 = (s32[8,128]{1,0:T(8,128)S(1)}, s32[8,128]{1,0:T(8,128)S(1)}, u32[]{:S(2)}, u32[]{:S(2)}) collective-permute-start(s32[8,128]{1,0:T(8,128)S(1)} %pair.1.refs_1_), channel_id=1, source_target_pairs={{0,4},{1,5},{2,6},{3,7},{4,0},{5,1},{6,2},{7,3},{8,12},{9,13},{10,... | collective-permute-start | bytes 12296 | tf_op jit(solution)/shard_map/ppermute | solution.py:17
  7.1 2.0 %collective-permute-done.2.refs_3_ = s32[8,128]{1,0:T(8,128)S(1)} collective-permute-done((s32[8,128]{1,0:T(8,128)S(1)}, s32[8,128]{1,0:T(8,128)S(1)}, u32[]{:S(2)}, u32[]{:S(2)}) %collective-permute-start.2) | collective-permute-done | bytes 4128 | tf_op jit(solution)/shard_map/ppermute | solution.py:17
  9.1 2.4 %collective-permute-done.3.refs_4_ = s32[8,128]{1,0:T(8,128)S(1)} collective-permute-done((s32[8,128]{1,0:T(8,128)S(1)}, s32[8,128]{1,0:T(8,128)S(1)}, u32[]{:S(2)}, u32[]{:S(2)}) %collective-permute-start.3) | collective-permute-done | bytes 4128 | tf_op jit(solution)/shard_map/ppermute | solution.py:17
  11.5 1.6 %dense.1 = (bf16[48,2048]{1,0:T(8,128)(2,1)S(1)}, bf16[48,2048]{1,0:T(8,128)(2,1)S(1)}, bf16[48,2048]{1,0:T(8,128)(2,1)S(1)}, bf16[48,2048]{1,0:T(8,128)(2,1)S(1)}) custom-call(s32[1,128]{1,0:T(1,128)S(1)} %copy-done.1, s32[8,128]{1,0:T(8,128)S(1)} %pair.1.refs_1_, s32[8,128]{1,0:T(8,128)S(1)} %collective-permute-done.1.refs_2_, ...), custom_call_target="tpu_custom_call" | custom-call | flops 10000000000 | bytes 1327616 | tf_op jit(solution)/shard_map/dense/pallas_call | solution.py:36
  13.7 2.9 %collective-permute-start.7 = (bf16[48,2048]{1,0:T(8,128)(2,1)S(1)}, bf16[48,2048]{1,0:T(8,128)(2,1)S(1)}, u32[]{:S(2)}, u32[]{:S(2)}) collective-permute-start(bf16[48,2048]{1,0:T(8,128)(2,1)S(1)} %get-tuple-element.23), channel_id=1, source_target_pairs={{0,6},{1,7},{2,4},{3,5},{4,2},{5,3},{6,0},{7,1},{8,14},{9,15},{10,... | collective-permute-start | bytes 589832 | tf_op jit(solution)/shard_map/ppermute | solution.py:17
  16.6 4.0 %load.1 = (bf16[1024,4096]{1,0:T(8,128)(2,1)S(1)}, f32[1,1024]{1,0:T(1,128)S(1)}) custom-call(bf16[1024,4096]{1,0:T(8,128)(2,1)} %refs_0_.6, bf16[48,2048]{1,0:T(8,128)(2,1)S(1)} %get-tuple-element.18.refs_1_.refs_0_), custom_call_target="tpu_custom_call" | custom-call | flops 10000000000 | bytes 16781312 | tf_op jit(solution)/shard_map/load/pallas_call | solution.py:36
  20.8 2.4 %collective-permute-done.6.refs_2_ = bf16[48,2048]{1,0:T(8,128)(2,1)S(1)} collective-permute-done((bf16[48,2048]{1,0:T(8,128)(2,1)S(1)}, bf16[48,2048]{1,0:T(8,128)(2,1)S(1)}, u32[]{:S(2)}, u32[]{:S(2)}) %collective-permute-start.6) | collective-permute-done | bytes 196640 | tf_op jit(solution)/shard_map/ppermute | solution.py:17
  23.2 1.6 %collective-permute-start.10 = (bf16[48,2048]{1,0:T(8,128)(2,1)S(1)}, bf16[48,2048]{1,0:T(8,128)(2,1)S(1)}, u32[]{:S(2)}, u32[]{:S(2)}) collective-permute-start(bf16[48,2048]{1,0:T(8,128)(2,1)S(1)} %get-tuple-element.24.refs_0_), channel_id=1, source_target_pairs={{0,2},{1,3},{2,0},{3,1},{4,6},{5,7},{6,4},{7,5},{8,10},{9,11},{10,... | collective-permute-start | bytes 589832 | tf_op jit(solution)/shard_map/ppermute | solution.py:17
  25.5 1.6 %collective-permute-start.8 = (bf16[32,2048]{1,0:T(8,128)(2,1)S(1)}, bf16[32,2048]{1,0:T(8,128)(2,1)S(1)}, u32[]{:S(2)}, u32[]{:S(2)}) collective-permute-start(bf16[32,2048]{1,0:T(8,128)(2,1)S(1)} %get-tuple-element.25), channel_id=1, source_target_pairs={{0,8},{8,16},{16,24},{24,0},{1,9},{9,17},{17,25},{25,1},{2,10},{10... | collective-permute-start | bytes 393224 | tf_op jit(solution)/shard_map/ppermute | solution.py:263
  27.1 2.2 %collective-permute-start.9 = (bf16[32,2048]{1,0:T(8,128)(2,1)S(1)}, bf16[32,2048]{1,0:T(8,128)(2,1)S(1)}, u32[]{:S(2)}, u32[]{:S(2)}) collective-permute-start(bf16[32,2048]{1,0:T(8,128)(2,1)S(1)} %get-tuple-element.25), channel_id=1, source_target_pairs={{0,24},{8,0},{16,8},{24,16},{1,25},{9,1},{17,9},{25,17},{2,26},{10... | collective-permute-start | bytes 393224 | tf_op jit(solution)/shard_map/ppermute | solution.py:263
  29.3 3.1 %collective-permute-done.8.refs_0_ = bf16[32,2048]{1,0:T(8,128)(2,1)S(1)} collective-permute-done((bf16[32,2048]{1,0:T(8,128)(2,1)S(1)}, bf16[32,2048]{1,0:T(8,128)(2,1)S(1)}, u32[]{:S(2)}, u32[]{:S(2)}) %collective-permute-start.8) | collective-permute-done | bytes 131104 | tf_op jit(solution)/shard_map/ppermute | solution.py:263
  32.4 1.0 %collective-permute-done.9.refs_1_ = bf16[32,2048]{1,0:T(8,128)(2,1)S(1)} collective-permute-done((bf16[32,2048]{1,0:T(8,128)(2,1)S(1)}, bf16[32,2048]{1,0:T(8,128)(2,1)S(1)}, u32[]{:S(2)}, u32[]{:S(2)}) %collective-permute-start.9) | collective-permute-done | bytes 131104 | tf_op jit(solution)/shard_map/ppermute | solution.py:263
  33.5 1.4 %collective-permute-start.13 = (bf16[64,2048]{1,0:T(8,128)(2,1)S(1)}, bf16[64,2048]{1,0:T(8,128)(2,1)S(1)}, u32[]{:S(2)}, u32[]{:S(2)}) collective-permute-start(bf16[64,2048]{1,0:T(8,128)(2,1)S(1)} %stack.7.refs_1_), channel_id=1, source_target_pairs={{0,4},{1,5},{2,6},{3,7},{4,0},{5,1},{6,2},{7,3},{8,12},{9,13},{10,... | collective-permute-start | bytes 786440 | tf_op jit(solution)/shard_map/ppermute | solution.py:17
  35.4 1.2 %collective-permute-start.14 = (bf16[32,2048]{1,0:T(8,128)(2,1)S(1)}, bf16[32,2048]{1,0:T(8,128)(2,1)S(1)}, u32[]{:S(2)}, u32[]{:S(2)}) collective-permute-start(bf16[32,2048]{1,0:T(8,128)(2,1)S(1)} %get-tuple-element.25), channel_id=1, source_target_pairs={{0,16},{8,24},{16,0},{24,8},{1,17},{9,25},{17,1},{25,9},{2,18},{10... | collective-permute-start | bytes 393224 | tf_op jit(solution)/shard_map/ppermute | solution.py:263
  36.5 6.1 %collective-permute-done.14.refs_6_.refs_0_ = bf16[32,2048]{1,0:T(8,128)(2,1)S(1)} collective-permute-done((bf16[32,2048]{1,0:T(8,128)(2,1)S(1)}, bf16[32,2048]{1,0:T(8,128)(2,1)S(1)}, u32[]{:S(2)}, u32[]{:S(2)}) %collective-permute-start.14) | collective-permute-done | bytes 131104 | tf_op jit(solution)/shard_map/ppermute | solution.py:263
  42.8 1.6 %collective-permute-start.16 = (bf16[32,2048]{1,0:T(8,128)(2,1)S(1)}, bf16[32,2048]{1,0:T(8,128)(2,1)S(1)}, u32[]{:S(2)}, u32[]{:S(2)}) collective-permute-start(bf16[32,2048]{1,0:T(8,128)(2,1)S(1)} %collective-permute-done.14.refs_6_.refs_0_), channel_id=1, source_target_pairs={{0,2},{1,3},{2,0},{3,1},{4,6},{5,7},{6,4},{7,5},{8,10},{9,11},{10,... | collective-permute-start | bytes 393224 | tf_op jit(solution)/shard_map/ppermute | solution.py:17
  45.1 1.3 %collective-permute-start.18 = (bf16[32,2048]{1,0:T(8,128)(2,1)S(1)}, bf16[32,2048]{1,0:T(8,128)(2,1)S(1)}, u32[]{:S(2)}, u32[]{:S(2)}) collective-permute-start(bf16[32,2048]{1,0:T(8,128)(2,1)S(1)} %collective-permute-done.14.refs_6_.refs_0_), channel_id=1, source_target_pairs={{0,6},{1,7},{2,4},{3,5},{4,2},{5,3},{6,0},{7,1},{8,14},{9,15},{10,... | collective-permute-start | bytes 393224 | tf_op jit(solution)/shard_map/ppermute | solution.py:17
  46.4 3.2 %products.1 = (f32[1,1024]{1,0:T(1,128)S(1)}, f32[1,1024]{1,0:T(1,128)S(1)}) custom-call(bf16[1024,4096]{1,0:T(8,128)(2,1)S(1)} %get-tuple-element.19.refs_0_, bf16[336,2048]{1,0:T(8,128)(2,1)S(1)} %stack.8.refs_1_, bf16[336,2048]{1,0:T(8,128)(2,1)S(1)} %collective-permute-done.15.refs_2_), custom_call_target="tpu_custom_call" | custom-call | flops 3333333248 | bytes 11149312 | tf_op jit(solution)/shard_map/products/pallas_call | solution.py:36
  49.6 3.2 %collective-permute-done.17.refs_2_ = bf16[32,2048]{1,0:T(8,128)(2,1)S(1)} collective-permute-done((bf16[32,2048]{1,0:T(8,128)(2,1)S(1)}, bf16[32,2048]{1,0:T(8,128)(2,1)S(1)}, u32[]{:S(2)}, u32[]{:S(2)}) %collective-permute-start.17) | collective-permute-done | bytes 131104 | tf_op jit(solution)/shard_map/ppermute | solution.py:17
  53.5 1.3 %collective-permute-start.20 = (bf16[112,1024]{1,0:T(8,128)(2,1)S(1)}, bf16[112,1024]{1,0:T(8,128)(2,1)S(1)}, u32[]{:S(2)}, u32[]{:S(2)}) collective-permute-start(bf16[112,1024]{1,0:T(8,128)(2,1)S(1)} %stack.10), channel_id=1, source_target_pairs={{0,4},{1,5},{2,6},{3,7},{4,0},{5,1},{6,2},{7,3},{8,12},{9,13},{10,... | collective-permute-start | bytes 688136 | tf_op jit(solution)/shard_map/ppermute | solution.py:17
  54.8 6.2 %collective-permute-done.21.refs_0_.refs_7_ = bf16[112,1024]{1,0:T(8,128)(2,1)S(1)} collective-permute-done((bf16[112,1024]{1,0:T(8,128)(2,1)S(1)}, bf16[112,1024]{1,0:T(8,128)(2,1)S(1)}, u32[]{:S(2)}, u32[]{:S(2)}) %collective-permute-start.21) | collective-permute-done | bytes 229408 | tf_op jit(solution)/shard_map/ppermute | solution.py:17
  61.6 0.9 %collective-permute-done.23.refs_9_ = bf16[112,1024]{1,0:T(8,128)(2,1)S(1)} collective-permute-done((bf16[112,1024]{1,0:T(8,128)(2,1)S(1)}, bf16[112,1024]{1,0:T(8,128)(2,1)S(1)}, u32[]{:S(2)}, u32[]{:S(2)}) %collective-permute-start.23) | collective-permute-done | bytes 229408 | tf_op jit(solution)/shard_map/ppermute | solution.py:17
  62.9 3.1 %products_last.1 = (f32[1,1024]{1,0:T(1,128)}, f32[1,1024]{1,0:T(1,128)}) custom-call(bf16[1024,4096]{1,0:T(8,128)(2,1)S(1)} %get-tuple-element.19.refs_0_, f32[1,1024]{1,0:T(1,128)S(1)} %get-tuple-element.20.refs_4_.refs_1_, f32[1,1024]{1,0:T(1,128)S(1)} %get-tuple-element.26.refs_2_, f32[1,1024]{1,0:T(1,128)S(1)} %get-tuple-element.27.refs_4_.refs_1_.refs_3_, ...), custom_call_target="tpu_custom_call" | custom-call | flops 10000000000 | bytes 10375168 | tf_op jit(solution)/shard_map/products_last/pallas_call | solution.py:36
  (43 shorter events, 6.5 us)
Async XLA Ops:
  1.3 1.6 %collective-permute-start = (s32[8,128]{1,0:T(8,128)S(1)}, s32[8,128]{1,0:T(8,128)S(1)}, u32[]{:S(2)}, u32[]{:S(2)}) collective-permute-start(s32[8,128]{1,0:T(8,128)S(1)} %spread.1.refs_0_), channel_id=1, source_target_pairs={{0,1},{1,0},{2,3},{3,2},{4,5},{5,4},{6,7},{7,6},{8,9},{9,8},{10,11... | collective-permute-start | bytes 12296 | tf_op jit(solution)/shard_map/ppermute | solution.py:17
  2.4 9.1 %collective-permute-start.4 = (bf16[64,2048]{1,0:T(8,128)(2,1)S(1)}, bf16[64,2048]{1,0:T(8,128)(2,1)S(1)}, u32[]{:S(2)}, u32[]{:S(2)}) collective-permute-start(bf16[64,2048]{1,0:T(8,128)(2,1)S(1)} %get-tuple-element.17), channel_id=1, source_target_pairs={{0,1},{1,0},{2,3},{3,2},{4,5},{5,4},{6,7},{7,6},{8,9},{9,8},{10,11... | collective-permute-start | bytes 786440 | tf_op jit(solution)/shard_map/ppermute | solution.py:17
  2.9 4.2 %collective-permute-start.1 = (s32[8,128]{1,0:T(8,128)S(1)}, s32[8,128]{1,0:T(8,128)S(1)}, u32[]{:S(2)}, u32[]{:S(2)}) collective-permute-start(s32[8,128]{1,0:T(8,128)S(1)} %pair.1.refs_1_), channel_id=1, source_target_pairs={{0,2},{1,3},{2,0},{3,1},{4,6},{5,7},{6,4},{7,5},{8,10},{9,11},{10,... | collective-permute-start | bytes 12296 | tf_op jit(solution)/shard_map/ppermute | solution.py:17
  5.5 3.6 %collective-permute-start.2 = (s32[8,128]{1,0:T(8,128)S(1)}, s32[8,128]{1,0:T(8,128)S(1)}, u32[]{:S(2)}, u32[]{:S(2)}) collective-permute-start(s32[8,128]{1,0:T(8,128)S(1)} %pair.1.refs_1_), channel_id=1, source_target_pairs={{0,4},{1,5},{2,6},{3,7},{4,0},{5,1},{6,2},{7,3},{8,12},{9,13},{10,... | collective-permute-start | bytes 12296 | tf_op jit(solution)/shard_map/ppermute | solution.py:17
  7.0 4.5 %collective-permute-start.3 = (s32[8,128]{1,0:T(8,128)S(1)}, s32[8,128]{1,0:T(8,128)S(1)}, u32[]{:S(2)}, u32[]{:S(2)}) collective-permute-start(s32[8,128]{1,0:T(8,128)S(1)} %pair.1.refs_1_), channel_id=1, source_target_pairs={{0,6},{1,7},{2,4},{3,5},{4,2},{5,3},{6,0},{7,1},{8,14},{9,15},{10,... | collective-permute-start | bytes 12296 | tf_op jit(solution)/shard_map/ppermute | solution.py:17
  13.1 7.7 %collective-permute-start.5 = (bf16[48,2048]{1,0:T(8,128)(2,1)S(1)}, bf16[48,2048]{1,0:T(8,128)(2,1)S(1)}, u32[]{:S(2)}, u32[]{:S(2)}) collective-permute-start(bf16[48,2048]{1,0:T(8,128)(2,1)S(1)} %get-tuple-element.21), channel_id=1, source_target_pairs={{0,2},{1,3},{2,0},{3,1},{4,6},{5,7},{6,4},{7,5},{8,10},{9,11},{10,... | collective-permute-start | bytes 589832 | tf_op jit(solution)/shard_map/ppermute | solution.py:17
  13.7 9.5 %collective-permute-start.6 = (bf16[48,2048]{1,0:T(8,128)(2,1)S(1)}, bf16[48,2048]{1,0:T(8,128)(2,1)S(1)}, u32[]{:S(2)}, u32[]{:S(2)}) collective-permute-start(bf16[48,2048]{1,0:T(8,128)(2,1)S(1)} %get-tuple-element.22), channel_id=1, source_target_pairs={{0,4},{1,5},{2,6},{3,7},{4,0},{5,1},{6,2},{7,3},{8,12},{9,13},{10,... | collective-permute-start | bytes 589832 | tf_op jit(solution)/shard_map/ppermute | solution.py:17
  13.7 9.4 %collective-permute-start.7 = (bf16[48,2048]{1,0:T(8,128)(2,1)S(1)}, bf16[48,2048]{1,0:T(8,128)(2,1)S(1)}, u32[]{:S(2)}, u32[]{:S(2)}) collective-permute-start(bf16[48,2048]{1,0:T(8,128)(2,1)S(1)} %get-tuple-element.23), channel_id=1, source_target_pairs={{0,6},{1,7},{2,4},{3,5},{4,2},{5,3},{6,0},{7,1},{8,14},{9,15},{10,... | collective-permute-start | bytes 589832 | tf_op jit(solution)/shard_map/ppermute | solution.py:17
  23.2 10.2 %collective-permute-start.10 = (bf16[48,2048]{1,0:T(8,128)(2,1)S(1)}, bf16[48,2048]{1,0:T(8,128)(2,1)S(1)}, u32[]{:S(2)}, u32[]{:S(2)}) collective-permute-start(bf16[48,2048]{1,0:T(8,128)(2,1)S(1)} %get-tuple-element.24.refs_0_), channel_id=1, source_target_pairs={{0,2},{1,3},{2,0},{3,1},{4,6},{5,7},{6,4},{7,5},{8,10},{9,11},{10,... | collective-permute-start | bytes 589832 | tf_op jit(solution)/shard_map/ppermute | solution.py:17
  24.7 8.7 %collective-permute-start.11 = (bf16[48,2048]{1,0:T(8,128)(2,1)S(1)}, bf16[48,2048]{1,0:T(8,128)(2,1)S(1)}, u32[]{:S(2)}, u32[]{:S(2)}) collective-permute-start(bf16[48,2048]{1,0:T(8,128)(2,1)S(1)} %get-tuple-element.24.refs_0_), channel_id=1, source_target_pairs={{0,4},{1,5},{2,6},{3,7},{4,0},{5,1},{6,2},{7,3},{8,12},{9,13},{10,... | collective-permute-start | bytes 589832 | tf_op jit(solution)/shard_map/ppermute | solution.py:17
  25.5 6.9 %collective-permute-start.8 = (bf16[32,2048]{1,0:T(8,128)(2,1)S(1)}, bf16[32,2048]{1,0:T(8,128)(2,1)S(1)}, u32[]{:S(2)}, u32[]{:S(2)}) collective-permute-start(bf16[32,2048]{1,0:T(8,128)(2,1)S(1)} %get-tuple-element.25), channel_id=1, source_target_pairs={{0,8},{8,16},{16,24},{24,0},{1,9},{9,17},{17,25},{25,1},{2,10},{10... | collective-permute-start | bytes 393224 | tf_op jit(solution)/shard_map/ppermute | solution.py:263
  27.1 6.4 %collective-permute-start.9 = (bf16[32,2048]{1,0:T(8,128)(2,1)S(1)}, bf16[32,2048]{1,0:T(8,128)(2,1)S(1)}, u32[]{:S(2)}, u32[]{:S(2)}) collective-permute-start(bf16[32,2048]{1,0:T(8,128)(2,1)S(1)} %get-tuple-element.25), channel_id=1, source_target_pairs={{0,24},{8,0},{16,8},{24,16},{1,25},{9,1},{17,9},{25,17},{2,26},{10... | collective-permute-start | bytes 393224 | tf_op jit(solution)/shard_map/ppermute | solution.py:263
  33.5 9.2 %collective-permute-start.13 = (bf16[64,2048]{1,0:T(8,128)(2,1)S(1)}, bf16[64,2048]{1,0:T(8,128)(2,1)S(1)}, u32[]{:S(2)}, u32[]{:S(2)}) collective-permute-start(bf16[64,2048]{1,0:T(8,128)(2,1)S(1)} %stack.7.refs_1_), channel_id=1, source_target_pairs={{0,4},{1,5},{2,6},{3,7},{4,0},{5,1},{6,2},{7,3},{8,12},{9,13},{10,... | collective-permute-start | bytes 786440 | tf_op jit(solution)/shard_map/ppermute | solution.py:17
  34.8 7.8 %collective-permute-start.12 = (bf16[64,2048]{1,0:T(8,128)(2,1)S(1)}, bf16[64,2048]{1,0:T(8,128)(2,1)S(1)}, u32[]{:S(2)}, u32[]{:S(2)}) collective-permute-start(bf16[64,2048]{1,0:T(8,128)(2,1)S(1)} %stack.7.refs_1_), channel_id=1, source_target_pairs={{0,2},{1,3},{2,0},{3,1},{4,6},{5,7},{6,4},{7,5},{8,10},{9,11},{10,... | collective-permute-start | bytes 786440 | tf_op jit(solution)/shard_map/ppermute | solution.py:17
  35.4 7.3 %collective-permute-start.14 = (bf16[32,2048]{1,0:T(8,128)(2,1)S(1)}, bf16[32,2048]{1,0:T(8,128)(2,1)S(1)}, u32[]{:S(2)}, u32[]{:S(2)}) collective-permute-start(bf16[32,2048]{1,0:T(8,128)(2,1)S(1)} %get-tuple-element.25), channel_id=1, source_target_pairs={{0,16},{8,24},{16,0},{24,8},{1,17},{9,25},{17,1},{25,9},{2,18},{10... | collective-permute-start | bytes 393224 | tf_op jit(solution)/shard_map/ppermute | solution.py:263
  42.7 3.6 %collective-permute-start.15 = (bf16[336,2048]{1,0:T(8,128)(2,1)S(1)}, bf16[336,2048]{1,0:T(8,128)(2,1)S(1)}, u32[]{:S(2)}, u32[]{:S(2)}) collective-permute-start(bf16[336,2048]{1,0:T(8,128)(2,1)S(1)} %stack.8.refs_1_), channel_id=1, source_target_pairs={{0,1},{1,0},{2,3},{3,2},{4,5},{5,4},{6,7},{7,6},{8,9},{9,8},{10,11... | collective-permute-start | bytes 4128776 | tf_op jit(solution)/shard_map/ppermute | solution.py:17
  42.8 6.8 %collective-permute-start.16 = (bf16[32,2048]{1,0:T(8,128)(2,1)S(1)}, bf16[32,2048]{1,0:T(8,128)(2,1)S(1)}, u32[]{:S(2)}, u32[]{:S(2)}) collective-permute-start(bf16[32,2048]{1,0:T(8,128)(2,1)S(1)} %collective-permute-done.14.refs_6_.refs_0_), channel_id=1, source_target_pairs={{0,2},{1,3},{2,0},{3,1},{4,6},{5,7},{6,4},{7,5},{8,10},{9,11},{10,... | collective-permute-start | bytes 393224 | tf_op jit(solution)/shard_map/ppermute | solution.py:17
  44.4 8.4 %collective-permute-start.17 = (bf16[32,2048]{1,0:T(8,128)(2,1)S(1)}, bf16[32,2048]{1,0:T(8,128)(2,1)S(1)}, u32[]{:S(2)}, u32[]{:S(2)}) collective-permute-start(bf16[32,2048]{1,0:T(8,128)(2,1)S(1)} %collective-permute-done.14.refs_6_.refs_0_), channel_id=1, source_target_pairs={{0,4},{1,5},{2,6},{3,7},{4,0},{5,1},{6,2},{7,3},{8,12},{9,13},{10,... | collective-permute-start | bytes 393224 | tf_op jit(solution)/shard_map/ppermute | solution.py:17
  45.1 7.6 %collective-permute-start.18 = (bf16[32,2048]{1,0:T(8,128)(2,1)S(1)}, bf16[32,2048]{1,0:T(8,128)(2,1)S(1)}, u32[]{:S(2)}, u32[]{:S(2)}) collective-permute-start(bf16[32,2048]{1,0:T(8,128)(2,1)S(1)} %collective-permute-done.14.refs_6_.refs_0_), channel_id=1, source_target_pairs={{0,6},{1,7},{2,4},{3,5},{4,2},{5,3},{6,0},{7,1},{8,14},{9,15},{10,... | collective-permute-start | bytes 393224 | tf_op jit(solution)/shard_map/ppermute | solution.py:17
  52.8 10.1 %collective-permute-start.19 = (bf16[128,2048]{1,0:T(8,128)(2,1)S(1)}, bf16[128,2048]{1,0:T(8,128)(2,1)S(1)}, u32[]{:S(2)}, u32[]{:S(2)}) collective-permute-start(bf16[128,2048]{1,0:T(8,128)(2,1)S(1)} %stack.9.refs_4_), channel_id=1, source_target_pairs={{0,1},{1,0},{2,3},{3,2},{4,5},{5,4},{6,7},{7,6},{8,9},{9,8},{10,11... | collective-permute-start | bytes 1572872 | tf_op jit(solution)/shard_map/ppermute | solution.py:17
  52.9 8.1 %collective-permute-start.21 = (bf16[112,1024]{1,0:T(8,128)(2,1)S(1)}, bf16[112,1024]{1,0:T(8,128)(2,1)S(1)}, u32[]{:S(2)}, u32[]{:S(2)}) collective-permute-start(bf16[112,1024]{1,0:T(8,128)(2,1)S(1)} %stack.11), channel_id=1, source_target_pairs={{0,2},{1,3},{2,0},{3,1},{4,6},{5,7},{6,4},{7,5},{8,10},{9,11},{10,... | collective-permute-start | bytes 688136 | tf_op jit(solution)/shard_map/ppermute | solution.py:17
  53.5 7.8 %collective-permute-start.20 = (bf16[112,1024]{1,0:T(8,128)(2,1)S(1)}, bf16[112,1024]{1,0:T(8,128)(2,1)S(1)}, u32[]{:S(2)}, u32[]{:S(2)}) collective-permute-start(bf16[112,1024]{1,0:T(8,128)(2,1)S(1)} %stack.10), channel_id=1, source_target_pairs={{0,4},{1,5},{2,6},{3,7},{4,0},{5,1},{6,2},{7,3},{8,12},{9,13},{10,... | collective-permute-start | bytes 688136 | tf_op jit(solution)/shard_map/ppermute | solution.py:17
  61.0 1.6 %collective-permute-start.23 = (bf16[112,1024]{1,0:T(8,128)(2,1)S(1)}, bf16[112,1024]{1,0:T(8,128)(2,1)S(1)}, u32[]{:S(2)}, u32[]{:S(2)}) collective-permute-start(bf16[112,1024]{1,0:T(8,128)(2,1)S(1)} %stack.13), channel_id=1, source_target_pairs={{0,1},{1,0},{2,3},{3,2},{4,5},{5,4},{6,7},{7,6},{8,9},{9,8},{10,11... | collective-permute-start | bytes 688136 | tf_op jit(solution)/shard_map/ppermute | solution.py:17
  61.3 1.6 %collective-permute-start.22 = (bf16[112,1024]{1,0:T(8,128)(2,1)S(1)}, bf16[112,1024]{1,0:T(8,128)(2,1)S(1)}, u32[]{:S(2)}, u32[]{:S(2)}) collective-permute-start(bf16[112,1024]{1,0:T(8,128)(2,1)S(1)} %stack.12), channel_id=1, source_target_pairs={{0,1},{1,0},{2,3},{3,2},{4,5},{5,4},{6,7},{7,6},{8,9},{9,8},{10,11... | collective-permute-start | bytes 688136 | tf_op jit(solution)/shard_map/ppermute | solution.py:17
  (2 other events, 10.2 us)

commit v12 on v11

--- a/solution.py
+++ b/solution.py
@@ -285,7 +285,7 @@
         (cand, early, flip_permute(early, size, 1)),
         scratch=[pltpu.VMEM((early.shape[0], width), BF16)], weight=WEIGHT // 3,
     )
-    mid = stack(mid, after=(best,))
+    mid = stack(mid, after=(best, *corner))
     sent = [stack((part,), part.shape[1], after=(best,)) for part in corner]
     near, final = call(
         functools.partial(last_kernel, chip_rows), "products_last", [line] * 2,

time: 66.1 us -> 63.6 us (0.962)
  waiting for transfers between devices: 28.1 us -> 24.8 us
  starting transfers between devices: 23.9 us -> 24.6 us
    ppermute x21, waiting for transfers between devices: 17.9 us -> 14.6 us  [flip_permute(): return lax.ppermute(block, 'mem', [(m, m ^ flip) for m in range(size)])]
    ppermute x21, starting transfers between devices: 18.9 us -> 19.6 us  [flip_permute(): return lax.ppermute(block, 'mem', [(m, m ^ flip) for m in range(size)])]
where the time goes in v12:
time: 63.6 us; the launch traced here: 63.4 us
  waiting for transfers between devices  24.8 us (39%)
  starting transfers between devices  24.6 us (39%)
  Pallas kernels  12.1 us (19%)
  between operations  1.41 us (2%)
    ppermute x21, starting transfers between devices, flip_permute(): return lax.ppermute(block, 'mem', [(m, m ^ flip) for m in range(size)])  19.6 us
    ppermute x21, waiting for transfers between devices, flip_permute(): return lax.ppermute(block, 'mem', [(m, m ^ flip) for m in range(size)])  14.6 us
    pallas_call x15, Pallas kernels, call(): pl.pallas_call(run, out_shape=out_shape, in_specs=(specs or vmem_specs(co...  12.1 us
    ppermute x3, waiting for transfers between devices, body(): lax.ppermute(picked, 'grp', [(g, (g + k) % groups) for g in range(groups)])  10.2 us
    ppermute x3, starting transfers between devices, body(): lax.ppermute(picked, 'grp', [(g, (g + k) % groups) for g in range(groups)])  5 us
  transfers between devices with their start and end apart: 24, of which 12 were waited for; matrix products, arithmetic and copies ran while one was open for 0% of the time, Pallas kernels for 11%

profile of v12, /device:TPU:0, one launch (start us, length us, event | category | flops | bytes accessed | tf_op | source)
XLA Modules:
  0.0 63.4 jit_solution(16715379333168010445)
XLA Ops:
  2.9 2.6 %collective-permute-start.1 = (s32[8,128]{1,0:T(8,128)S(1)}, s32[8,128]{1,0:T(8,128)S(1)}, u32[]{:S(2)}, u32[]{:S(2)}) collective-permute-start(s32[8,128]{1,0:T(8,128)S(1)} %pair.1.refs_1_), channel_id=1, source_target_pairs={{0,2},{1,3},{2,0},{3,1},{4,6},{5,7},{6,4},{7,5},{8,10},{9,11},{10,... | collective-permute-start | bytes 12296 | tf_op jit(solution)/shard_map/ppermute | solution.py:17
  5.5 1.5 %collective-permute-start.2 = (s32[8,128]{1,0:T(8,128)S(1)}, s32[8,128]{1,0:T(8,128)S(1)}, u32[]{:S(2)}, u32[]{:S(2)}) collective-permute-start(s32[8,128]{1,0:T(8,128)S(1)} %pair.1.refs_1_), channel_id=1, source_target_pairs={{0,4},{1,5},{2,6},{3,7},{4,0},{5,1},{6,2},{7,3},{8,12},{9,13},{10,... | collective-permute-start | bytes 12296 | tf_op jit(solution)/shard_map/ppermute | solution.py:17
  7.1 2.0 %collective-permute-done.2.refs_3_ = s32[8,128]{1,0:T(8,128)S(1)} collective-permute-done((s32[8,128]{1,0:T(8,128)S(1)}, s32[8,128]{1,0:T(8,128)S(1)}, u32[]{:S(2)}, u32[]{:S(2)}) %collective-permute-start.2) | collective-permute-done | bytes 4128 | tf_op jit(solution)/shard_map/ppermute | solution.py:17
  9.1 2.4 %collective-permute-done.3.refs_4_ = s32[8,128]{1,0:T(8,128)S(1)} collective-permute-done((s32[8,128]{1,0:T(8,128)S(1)}, s32[8,128]{1,0:T(8,128)S(1)}, u32[]{:S(2)}, u32[]{:S(2)}) %collective-permute-start.3) | collective-permute-done | bytes 4128 | tf_op jit(solution)/shard_map/ppermute | solution.py:17
  11.5 1.6 %dense.1 = (bf16[48,2048]{1,0:T(8,128)(2,1)S(1)}, bf16[48,2048]{1,0:T(8,128)(2,1)S(1)}, bf16[48,2048]{1,0:T(8,128)(2,1)S(1)}, bf16[48,2048]{1,0:T(8,128)(2,1)S(1)}) custom-call(s32[1,128]{1,0:T(1,128)S(1)} %copy-done.1, s32[8,128]{1,0:T(8,128)S(1)} %pair.1.refs_1_, s32[8,128]{1,0:T(8,128)S(1)} %collective-permute-done.1.refs_2_, ...), custom_call_target="tpu_custom_call" | custom-call | flops 10000000000 | bytes 1327616 | tf_op jit(solution)/shard_map/dense/pallas_call | solution.py:36
  13.7 2.9 %collective-permute-start.7 = (bf16[48,2048]{1,0:T(8,128)(2,1)S(1)}, bf16[48,2048]{1,0:T(8,128)(2,1)S(1)}, u32[]{:S(2)}, u32[]{:S(2)}) collective-permute-start(bf16[48,2048]{1,0:T(8,128)(2,1)S(1)} %get-tuple-element.23), channel_id=1, source_target_pairs={{0,6},{1,7},{2,4},{3,5},{4,2},{5,3},{6,0},{7,1},{8,14},{9,15},{10,... | collective-permute-start | bytes 589832 | tf_op jit(solution)/shard_map/ppermute | solution.py:17
  16.6 4.0 %load.1 = (bf16[1024,4096]{1,0:T(8,128)(2,1)S(1)}, f32[1,1024]{1,0:T(1,128)S(1)}) custom-call(bf16[1024,4096]{1,0:T(8,128)(2,1)} %refs_0_.6, bf16[48,2048]{1,0:T(8,128)(2,1)S(1)} %get-tuple-element.18.refs_1_.refs_0_), custom_call_target="tpu_custom_call" | custom-call | flops 10000000000 | bytes 16781312 | tf_op jit(solution)/shard_map/load/pallas_call | solution.py:36
  20.8 2.4 %collective-permute-done.6.refs_2_ = bf16[48,2048]{1,0:T(8,128)(2,1)S(1)} collective-permute-done((bf16[48,2048]{1,0:T(8,128)(2,1)S(1)}, bf16[48,2048]{1,0:T(8,128)(2,1)S(1)}, u32[]{:S(2)}, u32[]{:S(2)}) %collective-permute-start.6) | collective-permute-done | bytes 196640 | tf_op jit(solution)/shard_map/ppermute | solution.py:17
  23.2 1.6 %collective-permute-start.10 = (bf16[48,2048]{1,0:T(8,128)(2,1)S(1)}, bf16[48,2048]{1,0:T(8,128)(2,1)S(1)}, u32[]{:S(2)}, u32[]{:S(2)}) collective-permute-start(bf16[48,2048]{1,0:T(8,128)(2,1)S(1)} %get-tuple-element.24.refs_0_), channel_id=1, source_target_pairs={{0,2},{1,3},{2,0},{3,1},{4,6},{5,7},{6,4},{7,5},{8,10},{9,11},{10,... | collective-permute-start | bytes 589832 | tf_op jit(solution)/shard_map/ppermute | solution.py:17
  25.5 1.6 %collective-permute-start.8 = (bf16[32,2048]{1,0:T(8,128)(2,1)S(1)}, bf16[32,2048]{1,0:T(8,128)(2,1)S(1)}, u32[]{:S(2)}, u32[]{:S(2)}) collective-permute-start(bf16[32,2048]{1,0:T(8,128)(2,1)S(1)} %get-tuple-element.25), channel_id=1, source_target_pairs={{0,8},{8,16},{16,24},{24,0},{1,9},{9,17},{17,25},{25,1},{2,10},{10... | collective-permute-start | bytes 393224 | tf_op jit(solution)/shard_map/ppermute | solution.py:263
  27.1 2.2 %collective-permute-start.9 = (bf16[32,2048]{1,0:T(8,128)(2,1)S(1)}, bf16[32,2048]{1,0:T(8,128)(2,1)S(1)}, u32[]{:S(2)}, u32[]{:S(2)}) collective-permute-start(bf16[32,2048]{1,0:T(8,128)(2,1)S(1)} %get-tuple-element.25), channel_id=1, source_target_pairs={{0,24},{8,0},{16,8},{24,16},{1,25},{9,1},{17,9},{25,17},{2,26},{10... | collective-permute-start | bytes 393224 | tf_op jit(solution)/shard_map/ppermute | solution.py:263
  29.3 3.1 %collective-permute-done.8.refs_0_ = bf16[32,2048]{1,0:T(8,128)(2,1)S(1)} collective-permute-done((bf16[32,2048]{1,0:T(8,128)(2,1)S(1)}, bf16[32,2048]{1,0:T(8,128)(2,1)S(1)}, u32[]{:S(2)}, u32[]{:S(2)}) %collective-permute-start.8) | collective-permute-done | bytes 131104 | tf_op jit(solution)/shard_map/ppermute | solution.py:263
  33.5 1.4 %collective-permute-start.13 = (bf16[64,2048]{1,0:T(8,128)(2,1)S(1)}, bf16[64,2048]{1,0:T(8,128)(2,1)S(1)}, u32[]{:S(2)}, u32[]{:S(2)}) collective-permute-start(bf16[64,2048]{1,0:T(8,128)(2,1)S(1)} %stack.7.refs_1_), channel_id=1, source_target_pairs={{0,4},{1,5},{2,6},{3,7},{4,0},{5,1},{6,2},{7,3},{8,12},{9,13},{10,... | collective-permute-start | bytes 786440 | tf_op jit(solution)/shard_map/ppermute | solution.py:17
  35.4 1.2 %collective-permute-start.14 = (bf16[32,2048]{1,0:T(8,128)(2,1)S(1)}, bf16[32,2048]{1,0:T(8,128)(2,1)S(1)}, u32[]{:S(2)}, u32[]{:S(2)}) collective-permute-start(bf16[32,2048]{1,0:T(8,128)(2,1)S(1)} %get-tuple-element.25), channel_id=1, source_target_pairs={{0,16},{8,24},{16,0},{24,8},{1,17},{9,25},{17,1},{25,9},{2,18},{10... | collective-permute-start | bytes 393224 | tf_op jit(solution)/shard_map/ppermute | solution.py:263
  36.5 6.1 %collective-permute-done.14.refs_6_.refs_0_ = bf16[32,2048]{1,0:T(8,128)(2,1)S(1)} collective-permute-done((bf16[32,2048]{1,0:T(8,128)(2,1)S(1)}, bf16[32,2048]{1,0:T(8,128)(2,1)S(1)}, u32[]{:S(2)}, u32[]{:S(2)}) %collective-permute-start.14) | collective-permute-done | bytes 131104 | tf_op jit(solution)/shard_map/ppermute | solution.py:263
  42.8 1.6 %collective-permute-start.16 = (bf16[32,2048]{1,0:T(8,128)(2,1)S(1)}, bf16[32,2048]{1,0:T(8,128)(2,1)S(1)}, u32[]{:S(2)}, u32[]{:S(2)}) collective-permute-start(bf16[32,2048]{1,0:T(8,128)(2,1)S(1)} %collective-permute-done.14.refs_6_.refs_0_), channel_id=1, source_target_pairs={{0,2},{1,3},{2,0},{3,1},{4,6},{5,7},{6,4},{7,5},{8,10},{9,11},{10,... | collective-permute-start | bytes 393224 | tf_op jit(solution)/shard_map/ppermute | solution.py:17
  45.1 1.3 %collective-permute-start.18 = (bf16[32,2048]{1,0:T(8,128)(2,1)S(1)}, bf16[32,2048]{1,0:T(8,128)(2,1)S(1)}, u32[]{:S(2)}, u32[]{:S(2)}) collective-permute-start(bf16[32,2048]{1,0:T(8,128)(2,1)S(1)} %collective-permute-done.14.refs_6_.refs_0_), channel_id=1, source_target_pairs={{0,6},{1,7},{2,4},{3,5},{4,2},{5,3},{6,0},{7,1},{8,14},{9,15},{10,... | collective-permute-start | bytes 393224 | tf_op jit(solution)/shard_map/ppermute | solution.py:17
  46.4 1.6 %collective-permute-start.20 = (bf16[112,1024]{1,0:T(8,128)(2,1)S(1)}, bf16[112,1024]{1,0:T(8,128)(2,1)S(1)}, u32[]{:S(2)}, u32[]{:S(2)}) collective-permute-start(bf16[112,1024]{1,0:T(8,128)(2,1)S(1)} %stack.10), channel_id=1, source_target_pairs={{0,2},{1,3},{2,0},{3,1},{4,6},{5,7},{6,4},{7,5},{8,10},{9,11},{10,... | collective-permute-start | bytes 688136 | tf_op jit(solution)/shard_map/ppermute | solution.py:17
  48.8 3.2 %products.1 = (f32[1,1024]{1,0:T(1,128)S(1)}, f32[1,1024]{1,0:T(1,128)S(1)}) custom-call(bf16[1024,4096]{1,0:T(8,128)(2,1)S(1)} %get-tuple-element.19.refs_0_, bf16[336,2048]{1,0:T(8,128)(2,1)S(1)} %stack.8.refs_1_, bf16[336,2048]{1,0:T(8,128)(2,1)S(1)} %collective-permute-done.15.refs_2_), custom_call_target="tpu_custom_call" | custom-call | flops 3333333248 | bytes 11149312 | tf_op jit(solution)/shard_map/products/pallas_call | solution.py:36
  52.0 1.2 %collective-permute-done.17.refs_2_ = bf16[32,2048]{1,0:T(8,128)(2,1)S(1)} collective-permute-done((bf16[32,2048]{1,0:T(8,128)(2,1)S(1)}, bf16[32,2048]{1,0:T(8,128)(2,1)S(1)}, u32[]{:S(2)}, u32[]{:S(2)}) %collective-permute-start.17) | collective-permute-done | bytes 131104 | tf_op jit(solution)/shard_map/ppermute | solution.py:17
  53.2 3.3 %collective-permute-done.20.refs_6_.refs_0_.refs_7_ = bf16[112,1024]{1,0:T(8,128)(2,1)S(1)} collective-permute-done((bf16[112,1024]{1,0:T(8,128)(2,1)S(1)}, bf16[112,1024]{1,0:T(8,128)(2,1)S(1)}, u32[]{:S(2)}, u32[]{:S(2)}) %collective-permute-start.20) | collective-permute-done | bytes 229408 | tf_op jit(solution)/shard_map/ppermute | solution.py:17
  56.5 1.2 %collective-permute-done.19.refs_5_.refs_0_.refs_6_ = bf16[112,1024]{1,0:T(8,128)(2,1)S(1)} collective-permute-done((bf16[112,1024]{1,0:T(8,128)(2,1)S(1)}, bf16[112,1024]{1,0:T(8,128)(2,1)S(1)}, u32[]{:S(2)}, u32[]{:S(2)}) %collective-permute-start.19) | collective-permute-done | bytes 229408 | tf_op jit(solution)/shard_map/ppermute | solution.py:17
  58.5 1.5 %collective-permute-done.23.refs_9_ = bf16[112,1024]{1,0:T(8,128)(2,1)S(1)} collective-permute-done((bf16[112,1024]{1,0:T(8,128)(2,1)S(1)}, bf16[112,1024]{1,0:T(8,128)(2,1)S(1)}, u32[]{:S(2)}, u32[]{:S(2)}) %collective-permute-start.23) | collective-permute-done | bytes 229408 | tf_op jit(solution)/shard_map/ppermute | solution.py:17
  60.3 3.1 %products_last.1 = (f32[1,1024]{1,0:T(1,128)}, f32[1,1024]{1,0:T(1,128)}) custom-call(bf16[1024,4096]{1,0:T(8,128)(2,1)S(1)} %get-tuple-element.19.refs_0_, f32[1,1024]{1,0:T(1,128)S(1)} %get-tuple-element.20.refs_4_.refs_1_, f32[1,1024]{1,0:T(1,128)S(1)} %get-tuple-element.26.refs_2_, f32[1,1024]{1,0:T(1,128)S(1)} %get-tuple-element.27.refs_4_.refs_1_.refs_3_, ...), custom_call_target="tpu_custom_call" | custom-call | flops 10000000000 | bytes 10375168 | tf_op jit(solution)/shard_map/products_last/pallas_call | solution.py:36
  (43 shorter events, 7.7 us)
Async XLA Ops:
  1.3 1.6 %collective-permute-start = (s32[8,128]{1,0:T(8,128)S(1)}, s32[8,128]{1,0:T(8,128)S(1)}, u32[]{:S(2)}, u32[]{:S(2)}) collective-permute-start(s32[8,128]{1,0:T(8,128)S(1)} %spread.1.refs_0_), channel_id=1, source_target_pairs={{0,1},{1,0},{2,3},{3,2},{4,5},{5,4},{6,7},{7,6},{8,9},{9,8},{10,11... | collective-permute-start | bytes 12296 | tf_op jit(solution)/shard_map/ppermute | solution.py:17
  2.4 9.1 %collective-permute-start.4 = (bf16[64,2048]{1,0:T(8,128)(2,1)S(1)}, bf16[64,2048]{1,0:T(8,128)(2,1)S(1)}, u32[]{:S(2)}, u32[]{:S(2)}) collective-permute-start(bf16[64,2048]{1,0:T(8,128)(2,1)S(1)} %get-tuple-element.17), channel_id=1, source_target_pairs={{0,1},{1,0},{2,3},{3,2},{4,5},{5,4},{6,7},{7,6},{8,9},{9,8},{10,11... | collective-permute-start | bytes 786440 | tf_op jit(solution)/shard_map/ppermute | solution.py:17
  2.9 4.2 %collective-permute-start.1 = (s32[8,128]{1,0:T(8,128)S(1)}, s32[8,128]{1,0:T(8,128)S(1)}, u32[]{:S(2)}, u32[]{:S(2)}) collective-permute-start(s32[8,128]{1,0:T(8,128)S(1)} %pair.1.refs_1_), channel_id=1, source_target_pairs={{0,2},{1,3},{2,0},{3,1},{4,6},{5,7},{6,4},{7,5},{8,10},{9,11},{10,... | collective-permute-start | bytes 12296 | tf_op jit(solution)/shard_map/ppermute | solution.py:17
  5.5 3.6 %collective-permute-start.2 = (s32[8,128]{1,0:T(8,128)S(1)}, s32[8,128]{1,0:T(8,128)S(1)}, u32[]{:S(2)}, u32[]{:S(2)}) collective-permute-start(s32[8,128]{1,0:T(8,128)S(1)} %pair.1.refs_1_), channel_id=1, source_target_pairs={{0,4},{1,5},{2,6},{3,7},{4,0},{5,1},{6,2},{7,3},{8,12},{9,13},{10,... | collective-permute-start | bytes 12296 | tf_op jit(solution)/shard_map/ppermute | solution.py:17
  7.0 4.5 %collective-permute-start.3 = (s32[8,128]{1,0:T(8,128)S(1)}, s32[8,128]{1,0:T(8,128)S(1)}, u32[]{:S(2)}, u32[]{:S(2)}) collective-permute-start(s32[8,128]{1,0:T(8,128)S(1)} %pair.1.refs_1_), channel_id=1, source_target_pairs={{0,6},{1,7},{2,4},{3,5},{4,2},{5,3},{6,0},{7,1},{8,14},{9,15},{10,... | collective-permute-start | bytes 12296 | tf_op jit(solution)/shard_map/ppermute | solution.py:17
  13.1 7.7 %collective-permute-start.5 = (bf16[48,2048]{1,0:T(8,128)(2,1)S(1)}, bf16[48,2048]{1,0:T(8,128)(2,1)S(1)}, u32[]{:S(2)}, u32[]{:S(2)}) collective-permute-start(bf16[48,2048]{1,0:T(8,128)(2,1)S(1)} %get-tuple-element.21), channel_id=1, source_target_pairs={{0,2},{1,3},{2,0},{3,1},{4,6},{5,7},{6,4},{7,5},{8,10},{9,11},{10,... | collective-permute-start | bytes 589832 | tf_op jit(solution)/shard_map/ppermute | solution.py:17
  13.7 9.5 %collective-permute-start.6 = (bf16[48,2048]{1,0:T(8,128)(2,1)S(1)}, bf16[48,2048]{1,0:T(8,128)(2,1)S(1)}, u32[]{:S(2)}, u32[]{:S(2)}) collective-permute-start(bf16[48,2048]{1,0:T(8,128)(2,1)S(1)} %get-tuple-element.22), channel_id=1, source_target_pairs={{0,4},{1,5},{2,6},{3,7},{4,0},{5,1},{6,2},{7,3},{8,12},{9,13},{10,... | collective-permute-start | bytes 589832 | tf_op jit(solution)/shard_map/ppermute | solution.py:17
  13.7 9.4 %collective-permute-start.7 = (bf16[48,2048]{1,0:T(8,128)(2,1)S(1)}, bf16[48,2048]{1,0:T(8,128)(2,1)S(1)}, u32[]{:S(2)}, u32[]{:S(2)}) collective-permute-start(bf16[48,2048]{1,0:T(8,128)(2,1)S(1)} %get-tuple-element.23), channel_id=1, source_target_pairs={{0,6},{1,7},{2,4},{3,5},{4,2},{5,3},{6,0},{7,1},{8,14},{9,15},{10,... | collective-permute-start | bytes 589832 | tf_op jit(solution)/shard_map/ppermute | solution.py:17
  23.2 10.2 %collective-permute-start.10 = (bf16[48,2048]{1,0:T(8,128)(2,1)S(1)}, bf16[48,2048]{1,0:T(8,128)(2,1)S(1)}, u32[]{:S(2)}, u32[]{:S(2)}) collective-permute-start(bf16[48,2048]{1,0:T(8,128)(2,1)S(1)} %get-tuple-element.24.refs_0_), channel_id=1, source_target_pairs={{0,2},{1,3},{2,0},{3,1},{4,6},{5,7},{6,4},{7,5},{8,10},{9,11},{10,... | collective-permute-start | bytes 589832 | tf_op jit(solution)/shard_map/ppermute | solution.py:17
  24.7 8.7 %collective-permute-start.11 = (bf16[48,2048]{1,0:T(8,128)(2,1)S(1)}, bf16[48,2048]{1,0:T(8,128)(2,1)S(1)}, u32[]{:S(2)}, u32[]{:S(2)}) collective-permute-start(bf16[48,2048]{1,0:T(8,128)(2,1)S(1)} %get-tuple-element.24.refs_0_), channel_id=1, source_target_pairs={{0,4},{1,5},{2,6},{3,7},{4,0},{5,1},{6,2},{7,3},{8,12},{9,13},{10,... | collective-permute-start | bytes 589832 | tf_op jit(solution)/shard_map/ppermute | solution.py:17
  25.5 6.9 %collective-permute-start.8 = (bf16[32,2048]{1,0:T(8,128)(2,1)S(1)}, bf16[32,2048]{1,0:T(8,128)(2,1)S(1)}, u32[]{:S(2)}, u32[]{:S(2)}) collective-permute-start(bf16[32,2048]{1,0:T(8,128)(2,1)S(1)} %get-tuple-element.25), channel_id=1, source_target_pairs={{0,8},{8,16},{16,24},{24,0},{1,9},{9,17},{17,25},{25,1},{2,10},{10... | collective-permute-start | bytes 393224 | tf_op jit(solution)/shard_map/ppermute | solution.py:263
  27.1 6.4 %collective-permute-start.9 = (bf16[32,2048]{1,0:T(8,128)(2,1)S(1)}, bf16[32,2048]{1,0:T(8,128)(2,1)S(1)}, u32[]{:S(2)}, u32[]{:S(2)}) collective-permute-start(bf16[32,2048]{1,0:T(8,128)(2,1)S(1)} %get-tuple-element.25), channel_id=1, source_target_pairs={{0,24},{8,0},{16,8},{24,16},{1,25},{9,1},{17,9},{25,17},{2,26},{10... | collective-permute-start | bytes 393224 | tf_op jit(solution)/shard_map/ppermute | solution.py:263
  33.5 9.2 %collective-permute-start.13 = (bf16[64,2048]{1,0:T(8,128)(2,1)S(1)}, bf16[64,2048]{1,0:T(8,128)(2,1)S(1)}, u32[]{:S(2)}, u32[]{:S(2)}) collective-permute-start(bf16[64,2048]{1,0:T(8,128)(2,1)S(1)} %stack.7.refs_1_), channel_id=1, source_target_pairs={{0,4},{1,5},{2,6},{3,7},{4,0},{5,1},{6,2},{7,3},{8,12},{9,13},{10,... | collective-permute-start | bytes 786440 | tf_op jit(solution)/shard_map/ppermute | solution.py:17
  34.8 7.8 %collective-permute-start.12 = (bf16[64,2048]{1,0:T(8,128)(2,1)S(1)}, bf16[64,2048]{1,0:T(8,128)(2,1)S(1)}, u32[]{:S(2)}, u32[]{:S(2)}) collective-permute-start(bf16[64,2048]{1,0:T(8,128)(2,1)S(1)} %stack.7.refs_1_), channel_id=1, source_target_pairs={{0,2},{1,3},{2,0},{3,1},{4,6},{5,7},{6,4},{7,5},{8,10},{9,11},{10,... | collective-permute-start | bytes 786440 | tf_op jit(solution)/shard_map/ppermute | solution.py:17
  35.4 7.3 %collective-permute-start.14 = (bf16[32,2048]{1,0:T(8,128)(2,1)S(1)}, bf16[32,2048]{1,0:T(8,128)(2,1)S(1)}, u32[]{:S(2)}, u32[]{:S(2)}) collective-permute-start(bf16[32,2048]{1,0:T(8,128)(2,1)S(1)} %get-tuple-element.25), channel_id=1, source_target_pairs={{0,16},{8,24},{16,0},{24,8},{1,17},{9,25},{17,1},{25,9},{2,18},{10... | collective-permute-start | bytes 393224 | tf_op jit(solution)/shard_map/ppermute | solution.py:263
  42.7 5.2 %collective-permute-start.15 = (bf16[336,2048]{1,0:T(8,128)(2,1)S(1)}, bf16[336,2048]{1,0:T(8,128)(2,1)S(1)}, u32[]{:S(2)}, u32[]{:S(2)}) collective-permute-start(bf16[336,2048]{1,0:T(8,128)(2,1)S(1)} %stack.8.refs_1_), channel_id=1, source_target_pairs={{0,1},{1,0},{2,3},{3,2},{4,5},{5,4},{6,7},{7,6},{8,9},{9,8},{10,11... | collective-permute-start | bytes 4128776 | tf_op jit(solution)/shard_map/ppermute | solution.py:17
  42.8 9.2 %collective-permute-start.16 = (bf16[32,2048]{1,0:T(8,128)(2,1)S(1)}, bf16[32,2048]{1,0:T(8,128)(2,1)S(1)}, u32[]{:S(2)}, u32[]{:S(2)}) collective-permute-start(bf16[32,2048]{1,0:T(8,128)(2,1)S(1)} %collective-permute-done.14.refs_6_.refs_0_), channel_id=1, source_target_pairs={{0,2},{1,3},{2,0},{3,1},{4,6},{5,7},{6,4},{7,5},{8,10},{9,11},{10,... | collective-permute-start | bytes 393224 | tf_op jit(solution)/shard_map/ppermute | solution.py:17
  44.4 8.8 %collective-permute-start.17 = (bf16[32,2048]{1,0:T(8,128)(2,1)S(1)}, bf16[32,2048]{1,0:T(8,128)(2,1)S(1)}, u32[]{:S(2)}, u32[]{:S(2)}) collective-permute-start(bf16[32,2048]{1,0:T(8,128)(2,1)S(1)} %collective-permute-done.14.refs_6_.refs_0_), channel_id=1, source_target_pairs={{0,4},{1,5},{2,6},{3,7},{4,0},{5,1},{6,2},{7,3},{8,12},{9,13},{10,... | collective-permute-start | bytes 393224 | tf_op jit(solution)/shard_map/ppermute | solution.py:17
  45.1 8.1 %collective-permute-start.18 = (bf16[32,2048]{1,0:T(8,128)(2,1)S(1)}, bf16[32,2048]{1,0:T(8,128)(2,1)S(1)}, u32[]{:S(2)}, u32[]{:S(2)}) collective-permute-start(bf16[32,2048]{1,0:T(8,128)(2,1)S(1)} %collective-permute-done.14.refs_6_.refs_0_), channel_id=1, source_target_pairs={{0,6},{1,7},{2,4},{3,5},{4,2},{5,3},{6,0},{7,1},{8,14},{9,15},{10,... | collective-permute-start | bytes 393224 | tf_op jit(solution)/shard_map/ppermute | solution.py:17
  46.4 10.1 %collective-permute-start.20 = (bf16[112,1024]{1,0:T(8,128)(2,1)S(1)}, bf16[112,1024]{1,0:T(8,128)(2,1)S(1)}, u32[]{:S(2)}, u32[]{:S(2)}) collective-permute-start(bf16[112,1024]{1,0:T(8,128)(2,1)S(1)} %stack.10), channel_id=1, source_target_pairs={{0,2},{1,3},{2,0},{3,1},{4,6},{5,7},{6,4},{7,5},{8,10},{9,11},{10,... | collective-permute-start | bytes 688136 | tf_op jit(solution)/shard_map/ppermute | solution.py:17
  48.0 9.7 %collective-permute-start.19 = (bf16[112,1024]{1,0:T(8,128)(2,1)S(1)}, bf16[112,1024]{1,0:T(8,128)(2,1)S(1)}, u32[]{:S(2)}, u32[]{:S(2)}) collective-permute-start(bf16[112,1024]{1,0:T(8,128)(2,1)S(1)} %stack.9), channel_id=1, source_target_pairs={{0,4},{1,5},{2,6},{3,7},{4,0},{5,1},{6,2},{7,3},{8,12},{9,13},{10,... | collective-permute-start | bytes 688136 | tf_op jit(solution)/shard_map/ppermute | solution.py:17
  57.7 2.6 %collective-permute-start.21 = (bf16[128,2048]{1,0:T(8,128)(2,1)S(1)}, bf16[128,2048]{1,0:T(8,128)(2,1)S(1)}, u32[]{:S(2)}, u32[]{:S(2)}) collective-permute-start(bf16[128,2048]{1,0:T(8,128)(2,1)S(1)} %stack.11.refs_4_), channel_id=1, source_target_pairs={{0,1},{1,0},{2,3},{3,2},{4,5},{5,4},{6,7},{7,6},{8,9},{9,8},{10,11... | collective-permute-start | bytes 1572872 | tf_op jit(solution)/shard_map/ppermute | solution.py:17
  57.8 2.2 %collective-permute-start.23 = (bf16[112,1024]{1,0:T(8,128)(2,1)S(1)}, bf16[112,1024]{1,0:T(8,128)(2,1)S(1)}, u32[]{:S(2)}, u32[]{:S(2)}) collective-permute-start(bf16[112,1024]{1,0:T(8,128)(2,1)S(1)} %stack.13), channel_id=1, source_target_pairs={{0,1},{1,0},{2,3},{3,2},{4,5},{5,4},{6,7},{7,6},{8,9},{9,8},{10,11... | collective-permute-start | bytes 688136 | tf_op jit(solution)/shard_map/ppermute | solution.py:17
  58.4 2.0 %collective-permute-start.22 = (bf16[112,1024]{1,0:T(8,128)(2,1)S(1)}, bf16[112,1024]{1,0:T(8,128)(2,1)S(1)}, u32[]{:S(2)}, u32[]{:S(2)}) collective-permute-start(bf16[112,1024]{1,0:T(8,128)(2,1)S(1)} %stack.12), channel_id=1, source_target_pairs={{0,1},{1,0},{2,3},{3,2},{4,5},{5,4},{6,7},{7,6},{8,9},{9,8},{10,11... | collective-permute-start | bytes 688136 | tf_op jit(solution)/shard_map/ppermute | solution.py:17
  (2 other events, 10.2 us)

commit v13 on v12

--- a/solution.py
+++ b/solution.py
@@ -180,11 +180,10 @@
     return row_norms(rows_ref[...])
 
 
-def row_masks(picks_chip, rows_chip, mixed_chip, mixed, rows):
-    row = lax.broadcasted_iota(jnp.int32, (rows, 1), 0)
-    place = lax.rem(row, mixed_chip)
-    own = (row < mixed) & (place < rows_chip)
-    pick = (row >= mixed) | (place < picks_chip) | (place >= rows_chip)
+def row_masks(picks_chip, rows_chip, all_chip, rows):
+    place = lax.rem(lax.broadcasted_iota(jnp.int32, (rows, 1), 0), all_chip)
+    own = place < rows_chip
+    pick = (place < picks_chip) | ~own
     return jnp.where(own, 0.0, jnp.inf), jnp.where(pick, 0.0, jnp.inf)
 
 
@@ -194,21 +193,26 @@
 
 def first_kernel(chip_rows, cand_ref, own, sib, near_ref, best_ref, rows_ref):
     norms = lay_out([(own, sib)], rows_ref)
-    no_row, no_pick = row_masks(*chip_rows, norms.shape[0], norms.shape[0])
+    no_row, no_pick = row_masks(*chip_rows, norms.shape[0])
     for at in tiles_of(cand_ref):
         gaps = gaps_to(rows_ref, norms, cand_ref[at, :])
         near_ref[:, at] = least(gaps + no_row)
         best_ref[:, at] = least(gaps + no_pick)
 
 
-def last_kernel(
-    chip_rows, cand_ref, norm_ref, near_ref, best_ref, mid, mid_sib, *refs
-):
+def half_kernel(cand_ref, *refs):
+    *corner, out, rows_ref = refs
+    norms = lay_out([corner], rows_ref)
+    for at in tiles_of(cand_ref):
+        out[:, at] = gaps_to(rows_ref, norms, cand_ref[at, : rows_ref.shape[1]])
+
+
+def last_kernel(chip_rows, cand_ref, norm_ref, near_ref, best_ref, part_ref, *refs):
     *corner, near_out, best_out, rows_ref = refs
-    norms = lay_out([corner, (mid, mid_sib)], rows_ref)
-    no_row, no_pick = row_masks(*chip_rows, corner[0].shape[0], norms.shape[0])
+    norms = lay_out([corner], rows_ref)
+    no_row, no_pick = row_masks(*chip_rows, norms.shape[0])
     for at in tiles_of(cand_ref):
-        gaps = gaps_to(rows_ref, norms, cand_ref[at, :])
+        gaps = part_ref[:, at] + gaps_to(rows_ref, norms, cand_ref[at, rows_ref.shape[1] :])
         near_out[:, at] = jnp.minimum(least(gaps + no_row), near_ref[:, at]) + norm_ref[:, at]
         best_out[:, at] = jnp.minimum(least(gaps + no_pick), best_ref[:, at]) + norm_ref[:, at]
 
@@ -258,42 +262,41 @@
         after=(norm,),
     )
 
-    middle = groups // 2
     shifted = [
         lax.ppermute(picked, "grp", [(g, (g + k) % groups) for g in range(groups)])
         for k in range(1, groups)
     ]
-    far = [shifted[k - 1] for k in range(1, groups) if k != middle]
 
     if chips == 4:
         own_x, own_y = (flip_permute(owned, size, flip) for flip in (2, 4))
-        close = stack(far, after=(own_x, own_y))
-        close_x, close_y = (flip_permute(close, size, flip) for flip in (2, 4))
-        early = stack((owned, close, own_x, close_x, own_y, close_y), after=shifted[middle - 1 : middle])
-        left = stack((own_x, close_x), half // 2)
-        right = stack((own_y, close_y), half // 2, half // 2)
+        far = stack(shifted, after=(own_x, own_y))
+        far_x, far_y = (flip_permute(far, size, flip) for flip in (2, 4))
+        left = stack((own_x, far_x), half // 2)
+        right = stack((own_y, far_y), half // 2, half // 2)
+        early = stack((owned, far, own_x, far_x, own_y, far_y))
         corner = (flip_permute(left, size, 4), flip_permute(right, size, 2))
     else:
-        close = stack(far)
-        *early, end = to_chips(stack((owned, close)), size)
+        far = stack(shifted)
+        *early, end = to_chips(stack((owned, far)), size)
         early, corner = stack(early), (end,)
-    mid = to_chips(shifted[middle - 1], size)
-
-    chip_rows = (picks_chip, rows_chip, owned.shape[0] + close.shape[0])
+
+    chip_rows = (picks_chip, rows_chip, owned.shape[0] + far.shape[0])
     near, best = call(
         functools.partial(first_kernel, chip_rows), "products", [line] * 2,
         (cand, early, flip_permute(early, size, 1)),
         scratch=[pltpu.VMEM((early.shape[0], width), BF16)], weight=WEIGHT // 3,
     )
-    mid = stack(mid, after=(best, *corner))
     sent = [stack((part,), part.shape[1], after=(best,)) for part in corner]
+    swapped = [flip_permute(part, size, 1) for part in sent]
+    rows_end = corner[0].shape[0]
+    scratch = [pltpu.VMEM((rows_end, half), BF16)]
+    part = call(
+        half_kernel, "products_half", jax.ShapeDtypeStruct((rows_end, rows), F32), (cand, *corner),
+        scratch=scratch, after=(best,),
+    )
     near, final = call(
         functools.partial(last_kernel, chip_rows), "products_last", [line] * 2,
-        (
-            cand, norm, near, best, mid, flip_permute(mid, size, 1),
-            *corner, *[flip_permute(part, size, 1) for part in sent],
-        ),
-        scratch=[pltpu.VMEM((corner[0].shape[0] + mid.shape[0], width), BF16)],
+        (cand, norm, near, best, part, *swapped), scratch=scratch,
     )
     return near.reshape(-1), final.reshape(-1)
 

time: 63.6 us -> 63 us (level)
  starting transfers between devices: 24.6 us -> 19.6 us
  waiting for transfers between devices: 24.8 us -> 27.6 us
  Pallas kernels: 12.1 us -> 13.7 us
    ppermute x21 -> x17, waiting for transfers between devices: 14.6 us -> 19.8 us  [flip_permute(): return lax.ppermute(block, 'mem', [(m, m ^ flip) for m in range(size)])]
    ppermute x21 -> x17, starting transfers between devices: 19.6 us -> 14.9 us  [flip_permute(): return lax.ppermute(block, 'mem', [(m, m ^ flip) for m in range(size)])]
    ppermute x3, waiting for transfers between devices: 10.2 us -> 7.76 us  [body(): lax.ppermute(picked, 'grp', [(g, (g + k) % groups) for g in range(groups)])]
    pallas_call x15, Pallas kernels: 12.1 us -> 13.7 us  [call(): pl.pallas_call(run, out_shape=out_shape, in_specs=(specs or vmem_specs(co...]
  transfers between devices with their start and end apart: 24 -> 20, of which waited for: 12 -> 12; matrix products, arithmetic and copies ran while one was open for 0% -> 0% of each run, Pallas kernels for 11% -> 16%
where the time goes in v13:
time: 63 us; the launch traced here: 62.8 us
  waiting for transfers between devices  27.6 us (44%)
  starting transfers between devices  19.6 us (31%)
  Pallas kernels  13.7 us (22%)
  between operations  1.43 us (2%)
    ppermute x17, waiting for transfers between devices, flip_permute(): return lax.ppermute(block, 'mem', [(m, m ^ flip) for m in range(size)])  19.8 us
    ppermute x17, starting transfers between devices, flip_permute(): return lax.ppermute(block, 'mem', [(m, m ^ flip) for m in range(size)])  14.9 us
    pallas_call x15, Pallas kernels, call(): pl.pallas_call(run, out_shape=out_shape, in_specs=(specs or vmem_specs(co...  13.7 us
    ppermute x3, waiting for transfers between devices, body(): lax.ppermute(picked, 'grp', [(g, (g + k) % groups) for g in range(groups)])  7.76 us
    ppermute x3, starting transfers between devices, body(): lax.ppermute(picked, 'grp', [(g, (g + k) % groups) for g in range(groups)])  4.7 us
  transfers between devices with their start and end apart: 20, of which 12 were waited for; matrix products, arithmetic and copies ran while one was open for 0% of the time, Pallas kernels for 16%

profile of v13, /device:TPU:0, one launch (start us, length us, event | category | flops | bytes accessed | tf_op | source)
XLA Modules:
  0.0 62.8 jit_solution(3686528670901801764)
XLA Ops:
  2.9 3.5 %collective-permute-start.3 = (s32[8,128]{1,0:T(8,128)S(1)}, s32[8,128]{1,0:T(8,128)S(1)}, u32[]{:S(2)}, u32[]{:S(2)}) collective-permute-start(s32[8,128]{1,0:T(8,128)S(1)} %pair.1.refs_1_), channel_id=1, source_target_pairs={{0,6},{1,7},{2,4},{3,5},{4,2},{5,3},{6,0},{7,1},{8,14},{9,15},{10,... | collective-permute-start | bytes 12296 | tf_op jit(solution)/shard_map/ppermute | solution.py:17
  7.1 0.9 %collective-permute-done.3.refs_4_ = s32[8,128]{1,0:T(8,128)S(1)} collective-permute-done((s32[8,128]{1,0:T(8,128)S(1)}, s32[8,128]{1,0:T(8,128)S(1)}, u32[]{:S(2)}, u32[]{:S(2)}) %collective-permute-start.3) | collective-permute-done | bytes 4128 | tf_op jit(solution)/shard_map/ppermute | solution.py:17
  8.0 2.0 %collective-permute-done.2.refs_3_ = s32[8,128]{1,0:T(8,128)S(1)} collective-permute-done((s32[8,128]{1,0:T(8,128)S(1)}, s32[8,128]{1,0:T(8,128)S(1)}, u32[]{:S(2)}, u32[]{:S(2)}) %collective-permute-start.2) | collective-permute-done | bytes 4128 | tf_op jit(solution)/shard_map/ppermute | solution.py:17
  10.6 1.6 %dense.1 = (bf16[48,2048]{1,0:T(8,128)(2,1)S(1)}, bf16[48,2048]{1,0:T(8,128)(2,1)S(1)}, bf16[48,2048]{1,0:T(8,128)(2,1)S(1)}, bf16[48,2048]{1,0:T(8,128)(2,1)S(1)}) custom-call(s32[1,128]{1,0:T(1,128)S(1)} %copy-done.1, s32[8,128]{1,0:T(8,128)S(1)} %pair.1.refs_1_, s32[8,128]{1,0:T(8,128)S(1)} %collective-permute-done.1.refs_2_, ...), custom_call_target="tpu_custom_call" | custom-call | flops 10000000000 | bytes 1327616 | tf_op jit(solution)/shard_map/dense/pallas_call | solution.py:36
  12.3 1.9 %collective-permute-start.6 = (bf16[48,2048]{1,0:T(8,128)(2,1)S(1)}, bf16[48,2048]{1,0:T(8,128)(2,1)S(1)}, u32[]{:S(2)}, u32[]{:S(2)}) collective-permute-start(bf16[48,2048]{1,0:T(8,128)(2,1)S(1)} %get-tuple-element.22), channel_id=1, source_target_pairs={{0,4},{1,5},{2,6},{3,7},{4,0},{5,1},{6,2},{7,3},{8,12},{9,13},{10,... | collective-permute-start | bytes 589832 | tf_op jit(solution)/shard_map/ppermute | solution.py:17
  14.2 1.4 %collective-permute-start.7 = (bf16[48,2048]{1,0:T(8,128)(2,1)S(1)}, bf16[48,2048]{1,0:T(8,128)(2,1)S(1)}, u32[]{:S(2)}, u32[]{:S(2)}) collective-permute-start(bf16[48,2048]{1,0:T(8,128)(2,1)S(1)} %get-tuple-element.23), channel_id=1, source_target_pairs={{0,6},{1,7},{2,4},{3,5},{4,2},{5,3},{6,0},{7,1},{8,14},{9,15},{10,... | collective-permute-start | bytes 589832 | tf_op jit(solution)/shard_map/ppermute | solution.py:17
  15.7 4.0 %load.1 = (bf16[1024,4096]{1,0:T(8,128)(2,1)S(1)}, f32[1,1024]{1,0:T(1,128)S(1)}) custom-call(bf16[1024,4096]{1,0:T(8,128)(2,1)} %refs_0_.6, bf16[48,2048]{1,0:T(8,128)(2,1)S(1)} %get-tuple-element.18.refs_1_.refs_0_), custom_call_target="tpu_custom_call" | custom-call | flops 10000000000 | bytes 16781312 | tf_op jit(solution)/shard_map/load/pallas_call | solution.py:36
  19.8 2.0 %collective-permute-done.6.refs_2_ = bf16[48,2048]{1,0:T(8,128)(2,1)S(1)} collective-permute-done((bf16[48,2048]{1,0:T(8,128)(2,1)S(1)}, bf16[48,2048]{1,0:T(8,128)(2,1)S(1)}, u32[]{:S(2)}, u32[]{:S(2)}) %collective-permute-start.6) | collective-permute-done | bytes 196640 | tf_op jit(solution)/shard_map/ppermute | solution.py:17
  21.8 1.1 %collective-permute-done.7.refs_3_ = bf16[48,2048]{1,0:T(8,128)(2,1)S(1)} collective-permute-done((bf16[48,2048]{1,0:T(8,128)(2,1)S(1)}, bf16[48,2048]{1,0:T(8,128)(2,1)S(1)}, u32[]{:S(2)}, u32[]{:S(2)}) %collective-permute-start.7) | collective-permute-done | bytes 196640 | tf_op jit(solution)/shard_map/ppermute | solution.py:17
  22.9 1.5 %collective-permute-start.12 = (bf16[48,2048]{1,0:T(8,128)(2,1)S(1)}, bf16[48,2048]{1,0:T(8,128)(2,1)S(1)}, u32[]{:S(2)}, u32[]{:S(2)}) collective-permute-start(bf16[48,2048]{1,0:T(8,128)(2,1)S(1)} %get-tuple-element.24.refs_0_), channel_id=1, source_target_pairs={{0,4},{1,5},{2,6},{3,7},{4,0},{5,1},{6,2},{7,3},{8,12},{9,13},{10,... | collective-permute-start | bytes 589832 | tf_op jit(solution)/shard_map/ppermute | solution.py:17
  24.4 0.9 %collective-permute-start.11 = (bf16[48,2048]{1,0:T(8,128)(2,1)S(1)}, bf16[48,2048]{1,0:T(8,128)(2,1)S(1)}, u32[]{:S(2)}, u32[]{:S(2)}) collective-permute-start(bf16[48,2048]{1,0:T(8,128)(2,1)S(1)} %get-tuple-element.24.refs_0_), channel_id=1, source_target_pairs={{0,2},{1,3},{2,0},{3,1},{4,6},{5,7},{6,4},{7,5},{8,10},{9,11},{10,... | collective-permute-start | bytes 589832 | tf_op jit(solution)/shard_map/ppermute | solution.py:17
  25.3 3.7 %collective-permute-start.10 = (bf16[32,2048]{1,0:T(8,128)(2,1)S(1)}, bf16[32,2048]{1,0:T(8,128)(2,1)S(1)}, u32[]{:S(2)}, u32[]{:S(2)}) collective-permute-start(bf16[32,2048]{1,0:T(8,128)(2,1)S(1)} %get-tuple-element.25), channel_id=1, source_target_pairs={{0,24},{8,0},{16,8},{24,16},{1,25},{9,1},{17,9},{25,17},{2,26},{10... | collective-permute-start | bytes 393224 | tf_op jit(solution)/shard_map/ppermute | solution.py:266
  29.0 1.0 %collective-permute-start.8 = (bf16[32,2048]{1,0:T(8,128)(2,1)S(1)}, bf16[32,2048]{1,0:T(8,128)(2,1)S(1)}, u32[]{:S(2)}, u32[]{:S(2)}) collective-permute-start(bf16[32,2048]{1,0:T(8,128)(2,1)S(1)} %get-tuple-element.25), channel_id=1, source_target_pairs={{0,8},{8,16},{16,24},{24,0},{1,9},{9,17},{17,25},{25,1},{2,10},{10... | collective-permute-start | bytes 393224 | tf_op jit(solution)/shard_map/ppermute | solution.py:266
  30.0 2.7 %collective-permute-done.10.refs_2_ = bf16[32,2048]{1,0:T(8,128)(2,1)S(1)} collective-permute-done((bf16[32,2048]{1,0:T(8,128)(2,1)S(1)}, bf16[32,2048]{1,0:T(8,128)(2,1)S(1)}, u32[]{:S(2)}, u32[]{:S(2)}) %collective-permute-start.10) | collective-permute-done | bytes 131104 | tf_op jit(solution)/shard_map/ppermute | solution.py:266
  32.7 5.1 %collective-permute-done.9.refs_1_ = bf16[32,2048]{1,0:T(8,128)(2,1)S(1)} collective-permute-done((bf16[32,2048]{1,0:T(8,128)(2,1)S(1)}, bf16[32,2048]{1,0:T(8,128)(2,1)S(1)}, u32[]{:S(2)}, u32[]{:S(2)}) %collective-permute-start.9) | collective-permute-done | bytes 131104 | tf_op jit(solution)/shard_map/ppermute | solution.py:266
  37.8 1.5 %collective-permute-start.14 = (bf16[96,2048]{1,0:T(8,128)(2,1)S(1)}, bf16[96,2048]{1,0:T(8,128)(2,1)S(1)}, u32[]{:S(2)}, u32[]{:S(2)}) collective-permute-start(bf16[96,2048]{1,0:T(8,128)(2,1)S(1)} %stack.6.refs_1_), channel_id=1, source_target_pairs={{0,4},{1,5},{2,6},{3,7},{4,0},{5,1},{6,2},{7,3},{8,12},{9,13},{10,... | collective-permute-start | bytes 1179656 | tf_op jit(solution)/shard_map/ppermute | solution.py:17
  39.4 0.6 collective-permute-start.13
  40.0 7.1 %collective-permute-done.14.refs_5_.refs_1_ = bf16[96,2048]{1,0:T(8,128)(2,1)S(1)} collective-permute-done((bf16[96,2048]{1,0:T(8,128)(2,1)S(1)}, bf16[96,2048]{1,0:T(8,128)(2,1)S(1)}, u32[]{:S(2)}, u32[]{:S(2)}) %collective-permute-start.14) | collective-permute-done | bytes 393248 | tf_op jit(solution)/shard_map/ppermute | solution.py:17
  47.1 1.4 %collective-permute-done.13.refs_3_.refs_1_ = bf16[96,2048]{1,0:T(8,128)(2,1)S(1)} collective-permute-done((bf16[96,2048]{1,0:T(8,128)(2,1)S(1)}, bf16[96,2048]{1,0:T(8,128)(2,1)S(1)}, u32[]{:S(2)}, u32[]{:S(2)}) %collective-permute-start.13) | collective-permute-done | bytes 393248 | tf_op jit(solution)/shard_map/ppermute | solution.py:17
  49.7 2.7 %collective-permute-done.15.refs_2_ = bf16[432,2048]{1,0:T(8,128)(2,1)S(1)} collective-permute-done((bf16[432,2048]{1,0:T(8,128)(2,1)S(1)}, bf16[432,2048]{1,0:T(8,128)(2,1)S(1)}, u32[]{:S(2)}, u32[]{:S(2)}) %collective-permute-start.15) | collective-permute-done | bytes 1769504 | tf_op jit(solution)/shard_map/ppermute | solution.py:17
  52.3 4.2 %products.1 = (f32[1,1024]{1,0:T(1,128)S(1)}, f32[1,1024]{1,0:T(1,128)S(1)}) custom-call(bf16[1024,4096]{1,0:T(8,128)(2,1)S(1)} %get-tuple-element.19.refs_0_, bf16[432,2048]{1,0:T(8,128)(2,1)S(1)} %stack.7.refs_1_, bf16[432,2048]{1,0:T(8,128)(2,1)S(1)} %collective-permute-done.15.refs_2_), custom_call_target="tpu_custom_call" | custom-call | flops 3333333248 | bytes 11935744 | tf_op jit(solution)/shard_map/products/pallas_call | solution.py:36
  56.5 1.9 %collective-permute-done.16.refs_1_.refs_0_ = bf16[144,1024]{1,0:T(8,128)(2,1)S(1)} collective-permute-done((bf16[144,1024]{1,0:T(8,128)(2,1)S(1)}, bf16[144,1024]{1,0:T(8,128)(2,1)S(1)}, u32[]{:S(2)}, u32[]{:S(2)}) %collective-permute-start.16) | collective-permute-done | bytes 294944 | tf_op jit(solution)/shard_map/ppermute | solution.py:17
  59.1 1.5 %products_half.1.refs_4_ = f32[144,1024]{1,0:T(8,128)S(1)} custom-call(bf16[1024,4096]{1,0:T(8,128)(2,1)S(1)} %get-tuple-element.19.refs_0_, bf16[144,1024]{1,0:T(8,128)(2,1)S(1)} %collective-permute-done.16.refs_1_.refs_0_, bf16[144,1024]{1,0:T(8,128)(2,1)S(1)} %collective-permute-done.17.refs_2_.refs_0_, f32[1,1024]{1,0:T(1,128)S(1)} %get-tuple-element.27.refs_3_.refs_1_), custom_call_target="tpu_custom_call" | custom-call | flops 10000000000 | bytes 9568256 | tf_op jit(solution)/shard_map/products_half/pallas_call | solution.py:36
  60.7 2.2 %products_last.1 = (f32[1,1024]{1,0:T(1,128)}, f32[1,1024]{1,0:T(1,128)}) custom-call(bf16[1024,4096]{1,0:T(8,128)(2,1)S(1)} %get-tuple-element.19.refs_0_, f32[1,1024]{1,0:T(1,128)S(1)} %get-tuple-element.20.refs_4_.refs_1_, f32[1,1024]{1,0:T(1,128)S(1)} %get-tuple-element.26.refs_2_, f32[1,1024]{1,0:T(1,128)S(1)} %get-tuple-element.27.refs_3_.refs_1_, ...), custom_call_target="tpu_custom_call" | custom-call | flops 10000000000 | bytes 9588736 | tf_op jit(solution)/shard_map/products_last/pallas_call | solution.py:36
  (35 shorter events, 5.0 us)
Async XLA Ops:
  1.3 1.0 %copy-start = (bf16[64,4096]{1,0:T(8,128)(2,1)S(1)}, bf16[64,4096]{1,0:T(8,128)(2,1)}, u32[]{:S(2)}) copy-start(bf16[64,4096]{1,0:T(8,128)(2,1)} %refs_0_.4) | copy-start | bytes 1572868
  1.3 1.6 %collective-permute-start = (s32[8,128]{1,0:T(8,128)S(1)}, s32[8,128]{1,0:T(8,128)S(1)}, u32[]{:S(2)}, u32[]{:S(2)}) collective-permute-start(s32[8,128]{1,0:T(8,128)S(1)} %spread.1.refs_0_), channel_id=1, source_target_pairs={{0,1},{1,0},{2,3},{3,2},{4,5},{5,4},{6,7},{7,6},{8,9},{9,8},{10,11... | collective-permute-start | bytes 12296 | tf_op jit(solution)/shard_map/ppermute | solution.py:17
  2.4 8.2 %copy-start.1 = (s32[1,128]{1,0:T(1,128)S(1)}, s32[1,128]{1,0:T(1,128)}, u32[]{:S(2)}) copy-start(s32[1,128]{1,0:T(1,128)} %refs_0_.5) | copy-start | bytes 1540
  2.4 8.2 %collective-permute-start.4 = (bf16[64,2048]{1,0:T(8,128)(2,1)S(1)}, bf16[64,2048]{1,0:T(8,128)(2,1)S(1)}, u32[]{:S(2)}, u32[]{:S(2)}) collective-permute-start(bf16[64,2048]{1,0:T(8,128)(2,1)S(1)} %get-tuple-element.17), channel_id=1, source_target_pairs={{0,1},{1,0},{2,3},{3,2},{4,5},{5,4},{6,7},{7,6},{8,9},{9,8},{10,11... | collective-permute-start | bytes 786440 | tf_op jit(solution)/shard_map/ppermute | solution.py:17
  2.9 5.1 %collective-permute-start.3 = (s32[8,128]{1,0:T(8,128)S(1)}, s32[8,128]{1,0:T(8,128)S(1)}, u32[]{:S(2)}, u32[]{:S(2)}) collective-permute-start(s32[8,128]{1,0:T(8,128)S(1)} %pair.1.refs_1_), channel_id=1, source_target_pairs={{0,6},{1,7},{2,4},{3,5},{4,2},{5,3},{6,0},{7,1},{8,14},{9,15},{10,... | collective-permute-start | bytes 12296 | tf_op jit(solution)/shard_map/ppermute | solution.py:17
  6.4 3.6 %collective-permute-start.2 = (s32[8,128]{1,0:T(8,128)S(1)}, s32[8,128]{1,0:T(8,128)S(1)}, u32[]{:S(2)}, u32[]{:S(2)}) collective-permute-start(s32[8,128]{1,0:T(8,128)S(1)} %pair.1.refs_1_), channel_id=1, source_target_pairs={{0,4},{1,5},{2,6},{3,7},{4,0},{5,1},{6,2},{7,3},{8,12},{9,13},{10,... | collective-permute-start | bytes 12296 | tf_op jit(solution)/shard_map/ppermute | solution.py:17
  6.9 3.6 %collective-permute-start.1 = (s32[8,128]{1,0:T(8,128)S(1)}, s32[8,128]{1,0:T(8,128)S(1)}, u32[]{:S(2)}, u32[]{:S(2)}) collective-permute-start(s32[8,128]{1,0:T(8,128)S(1)} %pair.1.refs_1_), channel_id=1, source_target_pairs={{0,2},{1,3},{2,0},{3,1},{4,6},{5,7},{6,4},{7,5},{8,10},{9,11},{10,... | collective-permute-start | bytes 12296 | tf_op jit(solution)/shard_map/ppermute | solution.py:17
  12.1 7.7 %collective-permute-start.5 = (bf16[48,2048]{1,0:T(8,128)(2,1)S(1)}, bf16[48,2048]{1,0:T(8,128)(2,1)S(1)}, u32[]{:S(2)}, u32[]{:S(2)}) collective-permute-start(bf16[48,2048]{1,0:T(8,128)(2,1)S(1)} %get-tuple-element.21), channel_id=1, source_target_pairs={{0,2},{1,3},{2,0},{3,1},{4,6},{5,7},{6,4},{7,5},{8,10},{9,11},{10,... | collective-permute-start | bytes 589832 | tf_op jit(solution)/shard_map/ppermute | solution.py:17
  12.3 9.5 %collective-permute-start.6 = (bf16[48,2048]{1,0:T(8,128)(2,1)S(1)}, bf16[48,2048]{1,0:T(8,128)(2,1)S(1)}, u32[]{:S(2)}, u32[]{:S(2)}) collective-permute-start(bf16[48,2048]{1,0:T(8,128)(2,1)S(1)} %get-tuple-element.22), channel_id=1, source_target_pairs={{0,4},{1,5},{2,6},{3,7},{4,0},{5,1},{6,2},{7,3},{8,12},{9,13},{10,... | collective-permute-start | bytes 589832 | tf_op jit(solution)/shard_map/ppermute | solution.py:17
  14.2 8.6 %collective-permute-start.7 = (bf16[48,2048]{1,0:T(8,128)(2,1)S(1)}, bf16[48,2048]{1,0:T(8,128)(2,1)S(1)}, u32[]{:S(2)}, u32[]{:S(2)}) collective-permute-start(bf16[48,2048]{1,0:T(8,128)(2,1)S(1)} %get-tuple-element.23), channel_id=1, source_target_pairs={{0,6},{1,7},{2,4},{3,5},{4,2},{5,3},{6,0},{7,1},{8,14},{9,15},{10,... | collective-permute-start | bytes 589832 | tf_op jit(solution)/shard_map/ppermute | solution.py:17
  22.9 14.8 %collective-permute-start.12 = (bf16[48,2048]{1,0:T(8,128)(2,1)S(1)}, bf16[48,2048]{1,0:T(8,128)(2,1)S(1)}, u32[]{:S(2)}, u32[]{:S(2)}) collective-permute-start(bf16[48,2048]{1,0:T(8,128)(2,1)S(1)} %get-tuple-element.24.refs_0_), channel_id=1, source_target_pairs={{0,4},{1,5},{2,6},{3,7},{4,0},{5,1},{6,2},{7,3},{8,12},{9,13},{10,... | collective-permute-start | bytes 589832 | tf_op jit(solution)/shard_map/ppermute | solution.py:17
  24.4 13.3 %collective-permute-start.11 = (bf16[48,2048]{1,0:T(8,128)(2,1)S(1)}, bf16[48,2048]{1,0:T(8,128)(2,1)S(1)}, u32[]{:S(2)}, u32[]{:S(2)}) collective-permute-start(bf16[48,2048]{1,0:T(8,128)(2,1)S(1)} %get-tuple-element.24.refs_0_), channel_id=1, source_target_pairs={{0,2},{1,3},{2,0},{3,1},{4,6},{5,7},{6,4},{7,5},{8,10},{9,11},{10,... | collective-permute-start | bytes 589832 | tf_op jit(solution)/shard_map/ppermute | solution.py:17
  25.3 7.4 %collective-permute-start.10 = (bf16[32,2048]{1,0:T(8,128)(2,1)S(1)}, bf16[32,2048]{1,0:T(8,128)(2,1)S(1)}, u32[]{:S(2)}, u32[]{:S(2)}) collective-permute-start(bf16[32,2048]{1,0:T(8,128)(2,1)S(1)} %get-tuple-element.25), channel_id=1, source_target_pairs={{0,24},{8,0},{16,8},{24,16},{1,25},{9,1},{17,9},{25,17},{2,26},{10... | collective-permute-start | bytes 393224 | tf_op jit(solution)/shard_map/ppermute | solution.py:266
  29.0 8.8 %collective-permute-start.9 = (bf16[32,2048]{1,0:T(8,128)(2,1)S(1)}, bf16[32,2048]{1,0:T(8,128)(2,1)S(1)}, u32[]{:S(2)}, u32[]{:S(2)}) collective-permute-start(bf16[32,2048]{1,0:T(8,128)(2,1)S(1)} %get-tuple-element.25), channel_id=1, source_target_pairs={{0,16},{8,24},{16,0},{24,8},{1,17},{9,25},{17,1},{25,9},{2,18},{10... | collective-permute-start | bytes 393224 | tf_op jit(solution)/shard_map/ppermute | solution.py:266
  29.0 8.8 %collective-permute-start.8 = (bf16[32,2048]{1,0:T(8,128)(2,1)S(1)}, bf16[32,2048]{1,0:T(8,128)(2,1)S(1)}, u32[]{:S(2)}, u32[]{:S(2)}) collective-permute-start(bf16[32,2048]{1,0:T(8,128)(2,1)S(1)} %get-tuple-element.25), channel_id=1, source_target_pairs={{0,8},{8,16},{16,24},{24,0},{1,9},{9,17},{17,25},{25,1},{2,10},{10... | collective-permute-start | bytes 393224 | tf_op jit(solution)/shard_map/ppermute | solution.py:266
  37.8 9.2 %collective-permute-start.14 = (bf16[96,2048]{1,0:T(8,128)(2,1)S(1)}, bf16[96,2048]{1,0:T(8,128)(2,1)S(1)}, u32[]{:S(2)}, u32[]{:S(2)}) collective-permute-start(bf16[96,2048]{1,0:T(8,128)(2,1)S(1)} %stack.6.refs_1_), channel_id=1, source_target_pairs={{0,4},{1,5},{2,6},{3,7},{4,0},{5,1},{6,2},{7,3},{8,12},{9,13},{10,... | collective-permute-start | bytes 1179656 | tf_op jit(solution)/shard_map/ppermute | solution.py:17
  39.4 9.1 %collective-permute-start.13 = (bf16[96,2048]{1,0:T(8,128)(2,1)S(1)}, bf16[96,2048]{1,0:T(8,128)(2,1)S(1)}, u32[]{:S(2)}, u32[]{:S(2)}) collective-permute-start(bf16[96,2048]{1,0:T(8,128)(2,1)S(1)} %stack.6.refs_1_), channel_id=1, source_target_pairs={{0,2},{1,3},{2,0},{3,1},{4,6},{5,7},{6,4},{7,5},{8,10},{9,11},{10,... | collective-permute-start | bytes 1179656 | tf_op jit(solution)/shard_map/ppermute | solution.py:17
  48.6 3.8 %collective-permute-start.15 = (bf16[432,2048]{1,0:T(8,128)(2,1)S(1)}, bf16[432,2048]{1,0:T(8,128)(2,1)S(1)}, u32[]{:S(2)}, u32[]{:S(2)}) collective-permute-start(bf16[432,2048]{1,0:T(8,128)(2,1)S(1)} %stack.7.refs_1_), channel_id=1, source_target_pairs={{0,1},{1,0},{2,3},{3,2},{4,5},{5,4},{6,7},{7,6},{8,9},{9,8},{10,11... | collective-permute-start | bytes 5308424 | tf_op jit(solution)/shard_map/ppermute | solution.py:17
  48.7 9.8 %collective-permute-start.17 = (bf16[144,1024]{1,0:T(8,128)(2,1)S(1)}, bf16[144,1024]{1,0:T(8,128)(2,1)S(1)}, u32[]{:S(2)}, u32[]{:S(2)}) collective-permute-start(bf16[144,1024]{1,0:T(8,128)(2,1)S(1)} %stack.9), channel_id=1, source_target_pairs={{0,2},{1,3},{2,0},{3,1},{4,6},{5,7},{6,4},{7,5},{8,10},{9,11},{10,... | collective-permute-start | bytes 884744 | tf_op jit(solution)/shard_map/ppermute | solution.py:17
  49.2 9.2 %collective-permute-start.16 = (bf16[144,1024]{1,0:T(8,128)(2,1)S(1)}, bf16[144,1024]{1,0:T(8,128)(2,1)S(1)}, u32[]{:S(2)}, u32[]{:S(2)}) collective-permute-start(bf16[144,1024]{1,0:T(8,128)(2,1)S(1)} %stack.8), channel_id=1, source_target_pairs={{0,4},{1,5},{2,6},{3,7},{4,0},{5,1},{6,2},{7,3},{8,12},{9,13},{10,... | collective-permute-start | bytes 884744 | tf_op jit(solution)/shard_map/ppermute | solution.py:17
  58.4 2.2 %collective-permute-start.18 = (bf16[144,1024]{1,0:T(8,128)(2,1)S(1)}, bf16[144,1024]{1,0:T(8,128)(2,1)S(1)}, u32[]{:S(2)}, u32[]{:S(2)}) collective-permute-start(bf16[144,1024]{1,0:T(8,128)(2,1)S(1)} %stack.10), channel_id=1, source_target_pairs={{0,1},{1,0},{2,3},{3,2},{4,5},{5,4},{6,7},{7,6},{8,9},{9,8},{10,11... | collective-permute-start | bytes 884744 | tf_op jit(solution)/shard_map/ppermute | solution.py:17
  58.6 2.1 %collective-permute-start.19 = (bf16[144,1024]{1,0:T(8,128)(2,1)S(1)}, bf16[144,1024]{1,0:T(8,128)(2,1)S(1)}, u32[]{:S(2)}, u32[]{:S(2)}) collective-permute-start(bf16[144,1024]{1,0:T(8,128)(2,1)S(1)} %stack.11), channel_id=1, source_target_pairs={{0,1},{1,0},{2,3},{3,2},{4,5},{5,4},{6,7},{7,6},{8,9},{9,8},{10,11... | collective-permute-start | bytes 884744 | tf_op jit(solution)/shard_map/ppermute | solution.py:17

commit v14 on v13

--- a/solution.py
+++ b/solution.py
@@ -87,12 +87,13 @@
         norm_ref[:, t * TILE : (t + 1) * TILE] = jnp.sum(squares.T, axis=0, keepdims=True)
 
 
-def stack_kernel(start, *refs):
-    *blocks, out = refs
-    top = 0
-    for block in blocks:
-        rows = block.shape[0]
-        out[top : top + rows, :] = block[:, start : start + out.shape[1]]
+def stack_kernel(layout, *refs):
+    out, top = refs[-1], 0
+    for parts in layout:
+        left, rows = 0, refs[parts[0][0]].shape[0]
+        for index, start, columns in parts:
+            out[top : top + rows, left : left + columns] = refs[index][:, start : start + columns]
+            left += columns
         top += rows
 
 
@@ -169,21 +170,18 @@
     return [slice(t, t + TILE) for t in range(0, cand_ref.shape[0], TILE)]
 
 
-def lay_out(row_blocks, rows_ref):
-    top = 0
-    for parts in row_blocks:
-        left, rows = 0, parts[0].shape[0]
-        for part in parts:
-            rows_ref[top : top + rows, left : left + part.shape[1]] = part[...]
-            left += part.shape[1]
-        top += rows
+def lay_out(parts, rows_ref):
+    left = 0
+    for part in parts:
+        rows_ref[:, left : left + part.shape[1]] = part[...]
+        left += part.shape[1]
     return row_norms(rows_ref[...])
 
 
-def row_masks(picks_chip, rows_chip, all_chip, rows):
-    place = lax.rem(lax.broadcasted_iota(jnp.int32, (rows, 1), 0), all_chip)
-    own = place < rows_chip
-    pick = (place < picks_chip) | ~own
+def row_masks(picks_chip, rows_chip, own_rows, rows):
+    row = lax.broadcasted_iota(jnp.int32, (rows, 1), 0)
+    own = row < own_rows
+    pick = (lax.rem(row, rows_chip) < picks_chip) | ~own
     return jnp.where(own, 0.0, jnp.inf), jnp.where(pick, 0.0, jnp.inf)
 
 
@@ -192,7 +190,7 @@
 
 
 def first_kernel(chip_rows, cand_ref, own, sib, near_ref, best_ref, rows_ref):
-    norms = lay_out([(own, sib)], rows_ref)
+    norms = lay_out((own, sib), rows_ref)
     no_row, no_pick = row_masks(*chip_rows, norms.shape[0])
     for at in tiles_of(cand_ref):
         gaps = gaps_to(rows_ref, norms, cand_ref[at, :])
@@ -200,16 +198,28 @@
         best_ref[:, at] = least(gaps + no_pick)
 
 
+def next_kernel(blocks, cand_ref, best_ref, *refs):
+    *parts, out, rows_ref = refs
+    norms, count, rows = [], len(parts) // blocks, rows_ref.shape[0] // blocks
+    for b in range(blocks):
+        block = rows_ref.at[b * rows : (b + 1) * rows, :]
+        norms.append(lay_out(parts[b * count : (b + 1) * count], block))
+    norms = jnp.concatenate(norms, axis=0)
+    for at in tiles_of(cand_ref):
+        gaps = gaps_to(rows_ref, norms, cand_ref[at, :])
+        out[:, at] = jnp.minimum(least(gaps), best_ref[:, at])
+
+
 def half_kernel(cand_ref, *refs):
     *corner, out, rows_ref = refs
-    norms = lay_out([corner], rows_ref)
+    norms = lay_out(corner, rows_ref)
     for at in tiles_of(cand_ref):
         out[:, at] = gaps_to(rows_ref, norms, cand_ref[at, : rows_ref.shape[1]])
 
 
 def last_kernel(chip_rows, cand_ref, norm_ref, near_ref, best_ref, part_ref, *refs):
     *corner, near_out, best_out, rows_ref = refs
-    norms = lay_out([corner], rows_ref)
+    norms = lay_out(corner, rows_ref)
     no_row, no_pick = row_masks(*chip_rows, norms.shape[0])
     for at in tiles_of(cand_ref):
         gaps = part_ref[:, at] + gaps_to(rows_ref, norms, cand_ref[at, rows_ref.shape[1] :])
@@ -230,10 +240,17 @@
     def bf16(*dims):
         return jax.ShapeDtypeStruct(dims, BF16)
 
-    def stack(blocks, columns=half, start=0, after=()):
+    def stack(*blocks, after=()):
+        operands, layout = [], []
+        for block in blocks:
+            parts = [p if isinstance(p, tuple) else (p, 0, p.shape[1]) for p in block]
+            layout.append([(len(operands) + i, *p[1:]) for i, p in enumerate(parts)])
+            operands += [p[0] for p in parts]
+        shape = bf16(
+            sum(operands[parts[0][0]].shape[0] for parts in layout), sum(p[2] for p in layout[0])
+        )
         return call(
-            functools.partial(stack_kernel, start), "stack",
-            bf16(sum(b.shape[0] for b in blocks), columns), blocks, after=after, weight=0,
+            functools.partial(stack_kernel, layout), "stack", shape, operands, after=after, weight=0
         )
 
     line = jax.ShapeDtypeStruct((1, rows), F32)
@@ -268,25 +285,40 @@
     ]
 
     if chips == 4:
+        quarter = half // 2
         own_x, own_y = (flip_permute(owned, size, flip) for flip in (2, 4))
-        far = stack(shifted, after=(own_x, own_y))
-        far_x, far_y = (flip_permute(far, size, flip) for flip in (2, 4))
-        left = stack((own_x, far_x), half // 2)
-        right = stack((own_y, far_y), half // 2, half // 2)
-        early = stack((owned, far, own_x, far_x, own_y, far_y))
+        wait = (own_x, own_y)
+        low = stack(*[[(b, 0, quarter)] for b in shifted], after=wait)
+        high = stack(*[[(b, quarter, quarter)] for b in shifted], after=wait)
+        low_x, high_y = flip_permute(low, size, 2), flip_permute(high, size, 4)
+        high_x, low_y = flip_permute(high, size, 2), flip_permute(low, size, 4)
+        first, chips_first = stack([owned], [own_x], [own_y], [low, high]), chips - 1
+        others = ([low_x, high_x], [low_y, high_y])
+    else:
+        far = to_chips(stack(*[[b] for b in shifted]), size)
+        *own_blocks, own_end = to_chips(owned, size)
+        first, chips_first = stack(*[[b] for b in own_blocks], [far[0]]), chips - 1
+        others = [[b] for b in far[1:-1]]
+
+    near, best = call(
+        functools.partial(first_kernel, (picks_chip, rows_chip, chips_first * rows_chip)),
+        "products", [line] * 2, (cand, first, flip_permute(first, size, 1)),
+        scratch=[pltpu.VMEM((first.shape[0], width), BF16)], weight=WEIGHT // 10,
+    )
+    if chips == 4:
+        left = stack([(own_x, 0, quarter)], [low_x], after=(best,))
+        right = stack([(own_y, quarter, quarter)], [high_y], after=(best,))
         corner = (flip_permute(left, size, 4), flip_permute(right, size, 2))
     else:
-        far = stack(shifted)
-        *early, end = to_chips(stack((owned, far)), size)
-        early, corner = stack(early), (end,)
-
-    chip_rows = (picks_chip, rows_chip, owned.shape[0] + far.shape[0])
-    near, best = call(
-        functools.partial(first_kernel, chip_rows), "products", [line] * 2,
-        (cand, early, flip_permute(early, size, 1)),
-        scratch=[pltpu.VMEM((early.shape[0], width), BF16)], weight=WEIGHT // 3,
-    )
-    sent = [stack((part,), part.shape[1], after=(best,)) for part in corner]
+        corner = (stack([own_end], [far[-1]]),)
+    operands = []
+    for block in others:
+        operands += [*block, *[flip_permute(stack([b], after=(best,)), size, 1) for b in block]]
+    best = call(
+        functools.partial(next_kernel, len(others)), "products_next", line, (cand, best, *operands),
+        scratch=[pltpu.VMEM((len(others) * others[0][0].shape[0], width), BF16)], weight=0,
+    )
+    sent = [stack([part], after=(best,)) for part in corner]
     swapped = [flip_permute(part, size, 1) for part in sent]
     rows_end = corner[0].shape[0]
     scratch = [pltpu.VMEM((rows_end, half), BF16)]
@@ -295,8 +327,8 @@
         scratch=scratch, after=(best,),
     )
     near, final = call(
-        functools.partial(last_kernel, chip_rows), "products_last", [line] * 2,
-        (cand, norm, near, best, part, *swapped), scratch=scratch,
+        functools.partial(last_kernel, (picks_chip, rows_chip, rows_chip)), "products_last",
+        [line] * 2, (cand, norm, near, best, part, *swapped), scratch=scratch,
     )
     return near.reshape(-1), final.reshape(-1)
 

time: 63 us -> 60.1 us (0.954)
  waiting for transfers between devices: 27.6 us -> 18.9 us
  starting transfers between devices: 19.6 us -> 24 us
  Pallas kernels: 13.7 us -> 15 us
    ppermute x17 -> x23, waiting for transfers between devices: 19.8 us -> 13 us  [flip_permute(): return lax.ppermute(block, 'mem', [(m, m ^ flip) for m in range(size)])]
    ppermute x17 -> x23, starting transfers between devices: 14.9 us -> 18.5 us  [flip_permute(): return lax.ppermute(block, 'mem', [(m, m ^ flip) for m in range(size)])]
    ppermute x3, waiting for transfers between devices: 7.76 us -> 5.9 us  [body(): lax.ppermute(picked, 'grp', [(g, (g + k) % groups) for g in range(groups)])]
    pallas_call x15 -> x21, Pallas kernels: 13.7 us -> 15 us  [call(): pl.pallas_call(run, out_shape=out_shape, in_specs=(specs or vmem_specs(co...]
    ppermute x3, starting transfers between devices: 4.7 us -> 5.52 us  [body(): lax.ppermute(picked, 'grp', [(g, (g + k) % groups) for g in range(groups)])]
  transfers between devices with their start and end apart: 20 -> 26, of which waited for: 12 -> 13; matrix products, arithmetic and copies ran while one was open for 0% -> 0% of each run, Pallas kernels for 16% -> 19%
where the time goes in v14:
time: 60.1 us; the launch traced here: 60 us
  starting transfers between devices  24 us (40%)
  waiting for transfers between devices  18.9 us (31%)
  Pallas kernels  15 us (25%)
  between operations  1.5 us (2%)
    ppermute x23, starting transfers between devices, flip_permute(): return lax.ppermute(block, 'mem', [(m, m ^ flip) for m in range(size)])  18.5 us
    pallas_call x21, Pallas kernels, call(): pl.pallas_call(run, out_shape=out_shape, in_specs=(specs or vmem_specs(co...  15 us
    ppermute x23, waiting for transfers between devices, flip_permute(): return lax.ppermute(block, 'mem', [(m, m ^ flip) for m in range(size)])  13 us
    ppermute x3, waiting for transfers between devices, body(): lax.ppermute(picked, 'grp', [(g, (g + k) % groups) for g in range(groups)])  5.9 us
    ppermute x3, starting transfers between devices, body(): lax.ppermute(picked, 'grp', [(g, (g + k) % groups) for g in range(groups)])  5.52 us
  transfers between devices with their start and end apart: 26, of which 13 were waited for; matrix products, arithmetic and copies ran while one was open for 0% of the time, Pallas kernels for 19%

profile of v14, /device:TPU:0, one launch (start us, length us, event | category | flops | bytes accessed | tf_op | source)
XLA Modules:
  0.0 60.0 jit_solution(4081493321270499168)
XLA Ops:
  2.9 2.6 %collective-permute-start.1 = (s32[8,128]{1,0:T(8,128)S(1)}, s32[8,128]{1,0:T(8,128)S(1)}, u32[]{:S(2)}, u32[]{:S(2)}) collective-permute-start(s32[8,128]{1,0:T(8,128)S(1)} %pair.1.refs_1_), channel_id=1, source_target_pairs={{0,2},{1,3},{2,0},{3,1},{4,6},{5,7},{6,4},{7,5},{8,10},{9,11},{10,... | collective-permute-start | bytes 12296 | tf_op jit(solution)/shard_map/ppermute | solution.py:17
  5.5 1.5 %collective-permute-start.2 = (s32[8,128]{1,0:T(8,128)S(1)}, s32[8,128]{1,0:T(8,128)S(1)}, u32[]{:S(2)}, u32[]{:S(2)}) collective-permute-start(s32[8,128]{1,0:T(8,128)S(1)} %pair.1.refs_1_), channel_id=1, source_target_pairs={{0,4},{1,5},{2,6},{3,7},{4,0},{5,1},{6,2},{7,3},{8,12},{9,13},{10,... | collective-permute-start | bytes 12296 | tf_op jit(solution)/shard_map/ppermute | solution.py:17
  7.1 2.0 %collective-permute-done.2.refs_3_ = s32[8,128]{1,0:T(8,128)S(1)} collective-permute-done((s32[8,128]{1,0:T(8,128)S(1)}, s32[8,128]{1,0:T(8,128)S(1)}, u32[]{:S(2)}, u32[]{:S(2)}) %collective-permute-start.2) | collective-permute-done | bytes 4128 | tf_op jit(solution)/shard_map/ppermute | solution.py:17
  9.1 2.4 %collective-permute-done.3.refs_4_ = s32[8,128]{1,0:T(8,128)S(1)} collective-permute-done((s32[8,128]{1,0:T(8,128)S(1)}, s32[8,128]{1,0:T(8,128)S(1)}, u32[]{:S(2)}, u32[]{:S(2)}) %collective-permute-start.3) | collective-permute-done | bytes 4128 | tf_op jit(solution)/shard_map/ppermute | solution.py:17
  11.5 1.6 %dense.1 = (bf16[48,2048]{1,0:T(8,128)(2,1)S(1)}, bf16[48,2048]{1,0:T(8,128)(2,1)S(1)}, bf16[48,2048]{1,0:T(8,128)(2,1)S(1)}, bf16[48,2048]{1,0:T(8,128)(2,1)S(1)}) custom-call(s32[1,128]{1,0:T(1,128)S(1)} %copy-done.1, s32[8,128]{1,0:T(8,128)S(1)} %pair.1.refs_1_, s32[8,128]{1,0:T(8,128)S(1)} %collective-permute-done.1.refs_2_, ...), custom_call_target="tpu_custom_call" | custom-call | flops 10000000000 | bytes 1327616 | tf_op jit(solution)/shard_map/dense/pallas_call | solution.py:36
  13.7 2.9 %collective-permute-start.7 = (bf16[48,2048]{1,0:T(8,128)(2,1)S(1)}, bf16[48,2048]{1,0:T(8,128)(2,1)S(1)}, u32[]{:S(2)}, u32[]{:S(2)}) collective-permute-start(bf16[48,2048]{1,0:T(8,128)(2,1)S(1)} %get-tuple-element.23), channel_id=1, source_target_pairs={{0,6},{1,7},{2,4},{3,5},{4,2},{5,3},{6,0},{7,1},{8,14},{9,15},{10,... | collective-permute-start | bytes 589832 | tf_op jit(solution)/shard_map/ppermute | solution.py:17
  16.6 4.0 %load.1 = (bf16[1024,4096]{1,0:T(8,128)(2,1)S(1)}, f32[1,1024]{1,0:T(1,128)S(1)}) custom-call(bf16[1024,4096]{1,0:T(8,128)(2,1)} %refs_0_.6, bf16[48,2048]{1,0:T(8,128)(2,1)S(1)} %get-tuple-element.18.refs_1_.refs_0_), custom_call_target="tpu_custom_call" | custom-call | flops 10000000000 | bytes 16781312 | tf_op jit(solution)/shard_map/load/pallas_call | solution.py:36
  20.8 2.4 %collective-permute-done.6.refs_2_ = bf16[48,2048]{1,0:T(8,128)(2,1)S(1)} collective-permute-done((bf16[48,2048]{1,0:T(8,128)(2,1)S(1)}, bf16[48,2048]{1,0:T(8,128)(2,1)S(1)}, u32[]{:S(2)}, u32[]{:S(2)}) %collective-permute-start.6) | collective-permute-done | bytes 196640 | tf_op jit(solution)/shard_map/ppermute | solution.py:17
  23.2 1.6 %collective-permute-start.8 = (bf16[48,2048]{1,0:T(8,128)(2,1)S(1)}, bf16[48,2048]{1,0:T(8,128)(2,1)S(1)}, u32[]{:S(2)}, u32[]{:S(2)}) collective-permute-start(bf16[48,2048]{1,0:T(8,128)(2,1)S(1)} %get-tuple-element.24.refs_0_), channel_id=1, source_target_pairs={{0,2},{1,3},{2,0},{3,1},{4,6},{5,7},{6,4},{7,5},{8,10},{9,11},{10,... | collective-permute-start | bytes 589832 | tf_op jit(solution)/shard_map/ppermute | solution.py:17
  25.5 1.6 %collective-permute-start.10 = (bf16[32,2048]{1,0:T(8,128)(2,1)S(1)}, bf16[32,2048]{1,0:T(8,128)(2,1)S(1)}, u32[]{:S(2)}, u32[]{:S(2)}) collective-permute-start(bf16[32,2048]{1,0:T(8,128)(2,1)S(1)} %get-tuple-element.25), channel_id=1, source_target_pairs={{0,8},{8,16},{16,24},{24,0},{1,9},{9,17},{17,25},{25,1},{2,10},{10... | collective-permute-start | bytes 393224 | tf_op jit(solution)/shard_map/ppermute | solution.py:283
  27.1 2.6 %collective-permute-start.11 = (bf16[32,2048]{1,0:T(8,128)(2,1)S(1)}, bf16[32,2048]{1,0:T(8,128)(2,1)S(1)}, u32[]{:S(2)}, u32[]{:S(2)}) collective-permute-start(bf16[32,2048]{1,0:T(8,128)(2,1)S(1)} %get-tuple-element.25), channel_id=1, source_target_pairs={{0,16},{8,24},{16,0},{24,8},{1,17},{9,25},{17,1},{25,9},{2,18},{10... | collective-permute-start | bytes 393224 | tf_op jit(solution)/shard_map/ppermute | solution.py:283
  29.7 1.3 %collective-permute-start.12 = (bf16[32,2048]{1,0:T(8,128)(2,1)S(1)}, bf16[32,2048]{1,0:T(8,128)(2,1)S(1)}, u32[]{:S(2)}, u32[]{:S(2)}) collective-permute-start(bf16[32,2048]{1,0:T(8,128)(2,1)S(1)} %get-tuple-element.25), channel_id=1, source_target_pairs={{0,24},{8,0},{16,8},{24,16},{1,25},{9,1},{17,9},{25,17},{2,26},{10... | collective-permute-start | bytes 393224 | tf_op jit(solution)/shard_map/ppermute | solution.py:283
  31.0 1.9 %collective-permute-done.10.refs_0_ = bf16[32,2048]{1,0:T(8,128)(2,1)S(1)} collective-permute-done((bf16[32,2048]{1,0:T(8,128)(2,1)S(1)}, bf16[32,2048]{1,0:T(8,128)(2,1)S(1)}, u32[]{:S(2)}, u32[]{:S(2)}) %collective-permute-start.10) | collective-permute-done | bytes 131104 | tf_op jit(solution)/shard_map/ppermute | solution.py:283
  32.9 4.0 %collective-permute-done.11.refs_1_ = bf16[32,2048]{1,0:T(8,128)(2,1)S(1)} collective-permute-done((bf16[32,2048]{1,0:T(8,128)(2,1)S(1)}, bf16[32,2048]{1,0:T(8,128)(2,1)S(1)}, u32[]{:S(2)}, u32[]{:S(2)}) %collective-permute-start.11) | collective-permute-done | bytes 131104 | tf_op jit(solution)/shard_map/ppermute | solution.py:283
  38.5 1.3 %collective-permute-start.15 = (bf16[96,1024]{1,0:T(8,128)(2,1)S(1)}, bf16[96,1024]{1,0:T(8,128)(2,1)S(1)}, u32[]{:S(2)}, u32[]{:S(2)}) collective-permute-start(bf16[96,1024]{1,0:T(8,128)(2,1)S(1)} %stack.12.refs_4_), channel_id=1, source_target_pairs={{0,2},{1,3},{2,0},{3,1},{4,6},{5,7},{6,4},{7,5},{8,10},{9,11},{10,... | collective-permute-start | bytes 589832 | tf_op jit(solution)/shard_map/ppermute | solution.py:17
  39.9 1.4 %collective-permute-start.18 = (bf16[96,1024]{1,0:T(8,128)(2,1)S(1)}, bf16[96,1024]{1,0:T(8,128)(2,1)S(1)}, u32[]{:S(2)}, u32[]{:S(2)}) collective-permute-start(bf16[96,1024]{1,0:T(8,128)(2,1)S(1)} %stack.11.refs_3_), channel_id=1, source_target_pairs={{0,4},{1,5},{2,6},{3,7},{4,0},{5,1},{6,2},{7,3},{8,12},{9,13},{10,... | collective-permute-start | bytes 589832 | tf_op jit(solution)/shard_map/ppermute | solution.py:17
  41.2 2.5 %products.1 = (f32[1,1024]{1,0:T(1,128)S(1)}, f32[1,1024]{1,0:T(1,128)S(1)}) custom-call(bf16[1024,4096]{1,0:T(8,128)(2,1)S(1)} %get-tuple-element.19.refs_0_, bf16[240,2048]{1,0:T(8,128)(2,1)S(1)} %stack.13.refs_1_, bf16[240,2048]{1,0:T(8,128)(2,1)S(1)} %collective-permute-done.13.refs_2_), custom_call_target="tpu_custom_call" | custom-call | flops 1000000000 | bytes 10362880 | tf_op jit(solution)/shard_map/products/pallas_call | solution.py:36
  43.7 1.1 %collective-permute-done.14.refs_0_.refs_2_.refs_1_ = bf16[96,1024]{1,0:T(8,128)(2,1)S(1)} collective-permute-done((bf16[96,1024]{1,0:T(8,128)(2,1)S(1)}, bf16[96,1024]{1,0:T(8,128)(2,1)S(1)}, u32[]{:S(2)}, u32[]{:S(2)}) %collective-permute-start.14) | collective-permute-done | bytes 196640 | tf_op jit(solution)/shard_map/ppermute | solution.py:17
  45.8 1.2 %collective-permute-start.23 = (bf16[144,1024]{1,0:T(8,128)(2,1)S(1)}, bf16[144,1024]{1,0:T(8,128)(2,1)S(1)}, u32[]{:S(2)}, u32[]{:S(2)}) collective-permute-start(bf16[144,1024]{1,0:T(8,128)(2,1)S(1)} %stack.19), channel_id=1, source_target_pairs={{0,2},{1,3},{2,0},{3,1},{4,6},{5,7},{6,4},{7,5},{8,10},{9,11},{10,... | collective-permute-start | bytes 884744 | tf_op jit(solution)/shard_map/ppermute | solution.py:17
  47.0 1.6 %collective-permute-done.15.refs_0_.refs_3_ = bf16[96,1024]{1,0:T(8,128)(2,1)S(1)} collective-permute-done((bf16[96,1024]{1,0:T(8,128)(2,1)S(1)}, bf16[96,1024]{1,0:T(8,128)(2,1)S(1)}, u32[]{:S(2)}, u32[]{:S(2)}) %collective-permute-start.15) | collective-permute-done | bytes 196640 | tf_op jit(solution)/shard_map/ppermute | solution.py:17
  48.7 1.3 %collective-permute-done.18.refs_0_.refs_6_ = bf16[96,1024]{1,0:T(8,128)(2,1)S(1)} collective-permute-done((bf16[96,1024]{1,0:T(8,128)(2,1)S(1)}, bf16[96,1024]{1,0:T(8,128)(2,1)S(1)}, u32[]{:S(2)}, u32[]{:S(2)}) %collective-permute-start.18) | collective-permute-done | bytes 196640 | tf_op jit(solution)/shard_map/ppermute | solution.py:17
  51.8 3.0 %products_next.1.refs_3_.refs_1_ = f32[1,1024]{1,0:T(1,128)S(1)} custom-call(bf16[1024,4096]{1,0:T(8,128)(2,1)S(1)} %get-tuple-element.19.refs_0_, f32[1,1024]{1,0:T(1,128)S(1)} %get-tuple-element.27.refs_1_.refs_2_, bf16[96,1024]{1,0:T(8,128)(2,1)S(1)} %collective-permute-done.14.refs_0_.refs_2_.refs_1_, ...), custom_call_target="tpu_custom_call" | custom-call | bytes 9969664 | tf_op jit(solution)/shard_map/products_next/pallas_call | solution.py:36
  56.2 1.5 %products_half.1.refs_4_ = f32[144,1024]{1,0:T(8,128)S(1)} custom-call(bf16[1024,4096]{1,0:T(8,128)(2,1)S(1)} %get-tuple-element.19.refs_0_, bf16[144,1024]{1,0:T(8,128)(2,1)S(1)} %collective-permute-done.22.refs_1_.refs_0_, bf16[144,1024]{1,0:T(8,128)(2,1)S(1)} %collective-permute-done.23.refs_2_.refs_0_, f32[1,1024]{1,0:T(1,128)S(1)} %products_next.1.refs_3_.refs_1_), custom_call_target="tpu_custom_call" | custom-call | flops 10000000000 | bytes 9568256 | tf_op jit(solution)/shard_map/products_half/pallas_call | solution.py:36
  57.8 2.2 %products_last.1 = (f32[1,1024]{1,0:T(1,128)}, f32[1,1024]{1,0:T(1,128)}) custom-call(bf16[1024,4096]{1,0:T(8,128)(2,1)S(1)} %get-tuple-element.19.refs_0_, f32[1,1024]{1,0:T(1,128)S(1)} %get-tuple-element.20.refs_4_.refs_1_, f32[1,1024]{1,0:T(1,128)S(1)} %get-tuple-element.26.refs_2_, f32[1,1024]{1,0:T(1,128)S(1)} %products_next.1.refs_3_.refs_1_, ...), custom_call_target="tpu_custom_call" | custom-call | flops 10000000000 | bytes 9588736 | tf_op jit(solution)/shard_map/products_last/pallas_call | solution.py:36
  (53 shorter events, 9.1 us)
Async XLA Ops:
  2.4 9.1 %collective-permute-start.4 = (bf16[64,2048]{1,0:T(8,128)(2,1)S(1)}, bf16[64,2048]{1,0:T(8,128)(2,1)S(1)}, u32[]{:S(2)}, u32[]{:S(2)}) collective-permute-start(bf16[64,2048]{1,0:T(8,128)(2,1)S(1)} %get-tuple-element.17), channel_id=1, source_target_pairs={{0,1},{1,0},{2,3},{3,2},{4,5},{5,4},{6,7},{7,6},{8,9},{9,8},{10,11... | collective-permute-start | bytes 786440 | tf_op jit(solution)/shard_map/ppermute | solution.py:17
  2.9 4.2 %collective-permute-start.1 = (s32[8,128]{1,0:T(8,128)S(1)}, s32[8,128]{1,0:T(8,128)S(1)}, u32[]{:S(2)}, u32[]{:S(2)}) collective-permute-start(s32[8,128]{1,0:T(8,128)S(1)} %pair.1.refs_1_), channel_id=1, source_target_pairs={{0,2},{1,3},{2,0},{3,1},{4,6},{5,7},{6,4},{7,5},{8,10},{9,11},{10,... | collective-permute-start | bytes 12296 | tf_op jit(solution)/shard_map/ppermute | solution.py:17
  5.5 3.6 %collective-permute-start.2 = (s32[8,128]{1,0:T(8,128)S(1)}, s32[8,128]{1,0:T(8,128)S(1)}, u32[]{:S(2)}, u32[]{:S(2)}) collective-permute-start(s32[8,128]{1,0:T(8,128)S(1)} %pair.1.refs_1_), channel_id=1, source_target_pairs={{0,4},{1,5},{2,6},{3,7},{4,0},{5,1},{6,2},{7,3},{8,12},{9,13},{10,... | collective-permute-start | bytes 12296 | tf_op jit(solution)/shard_map/ppermute | solution.py:17
  7.0 4.5 %collective-permute-start.3 = (s32[8,128]{1,0:T(8,128)S(1)}, s32[8,128]{1,0:T(8,128)S(1)}, u32[]{:S(2)}, u32[]{:S(2)}) collective-permute-start(s32[8,128]{1,0:T(8,128)S(1)} %pair.1.refs_1_), channel_id=1, source_target_pairs={{0,6},{1,7},{2,4},{3,5},{4,2},{5,3},{6,0},{7,1},{8,14},{9,15},{10,... | collective-permute-start | bytes 12296 | tf_op jit(solution)/shard_map/ppermute | solution.py:17
  13.1 7.7 %collective-permute-start.5 = (bf16[48,2048]{1,0:T(8,128)(2,1)S(1)}, bf16[48,2048]{1,0:T(8,128)(2,1)S(1)}, u32[]{:S(2)}, u32[]{:S(2)}) collective-permute-start(bf16[48,2048]{1,0:T(8,128)(2,1)S(1)} %get-tuple-element.21), channel_id=1, source_target_pairs={{0,2},{1,3},{2,0},{3,1},{4,6},{5,7},{6,4},{7,5},{8,10},{9,11},{10,... | collective-permute-start | bytes 589832 | tf_op jit(solution)/shard_map/ppermute | solution.py:17
  13.7 9.5 %collective-permute-start.6 = (bf16[48,2048]{1,0:T(8,128)(2,1)S(1)}, bf16[48,2048]{1,0:T(8,128)(2,1)S(1)}, u32[]{:S(2)}, u32[]{:S(2)}) collective-permute-start(bf16[48,2048]{1,0:T(8,128)(2,1)S(1)} %get-tuple-element.22), channel_id=1, source_target_pairs={{0,4},{1,5},{2,6},{3,7},{4,0},{5,1},{6,2},{7,3},{8,12},{9,13},{10,... | collective-permute-start | bytes 589832 | tf_op jit(solution)/shard_map/ppermute | solution.py:17
  13.7 9.4 %collective-permute-start.7 = (bf16[48,2048]{1,0:T(8,128)(2,1)S(1)}, bf16[48,2048]{1,0:T(8,128)(2,1)S(1)}, u32[]{:S(2)}, u32[]{:S(2)}) collective-permute-start(bf16[48,2048]{1,0:T(8,128)(2,1)S(1)} %get-tuple-element.23), channel_id=1, source_target_pairs={{0,6},{1,7},{2,4},{3,5},{4,2},{5,3},{6,0},{7,1},{8,14},{9,15},{10,... | collective-permute-start | bytes 589832 | tf_op jit(solution)/shard_map/ppermute | solution.py:17
  23.2 13.7 %collective-permute-start.8 = (bf16[48,2048]{1,0:T(8,128)(2,1)S(1)}, bf16[48,2048]{1,0:T(8,128)(2,1)S(1)}, u32[]{:S(2)}, u32[]{:S(2)}) collective-permute-start(bf16[48,2048]{1,0:T(8,128)(2,1)S(1)} %get-tuple-element.24.refs_0_), channel_id=1, source_target_pairs={{0,2},{1,3},{2,0},{3,1},{4,6},{5,7},{6,4},{7,5},{8,10},{9,11},{10,... | collective-permute-start | bytes 589832 | tf_op jit(solution)/shard_map/ppermute | solution.py:17
  24.7 12.2 %collective-permute-start.9 = (bf16[48,2048]{1,0:T(8,128)(2,1)S(1)}, bf16[48,2048]{1,0:T(8,128)(2,1)S(1)}, u32[]{:S(2)}, u32[]{:S(2)}) collective-permute-start(bf16[48,2048]{1,0:T(8,128)(2,1)S(1)} %get-tuple-element.24.refs_0_), channel_id=1, source_target_pairs={{0,4},{1,5},{2,6},{3,7},{4,0},{5,1},{6,2},{7,3},{8,12},{9,13},{10,... | collective-permute-start | bytes 589832 | tf_op jit(solution)/shard_map/ppermute | solution.py:17
  25.5 7.4 %collective-permute-start.10 = (bf16[32,2048]{1,0:T(8,128)(2,1)S(1)}, bf16[32,2048]{1,0:T(8,128)(2,1)S(1)}, u32[]{:S(2)}, u32[]{:S(2)}) collective-permute-start(bf16[32,2048]{1,0:T(8,128)(2,1)S(1)} %get-tuple-element.25), channel_id=1, source_target_pairs={{0,8},{8,16},{16,24},{24,0},{1,9},{9,17},{17,25},{25,1},{2,10},{10... | collective-permute-start | bytes 393224 | tf_op jit(solution)/shard_map/ppermute | solution.py:283
  27.1 9.8 %collective-permute-start.11 = (bf16[32,2048]{1,0:T(8,128)(2,1)S(1)}, bf16[32,2048]{1,0:T(8,128)(2,1)S(1)}, u32[]{:S(2)}, u32[]{:S(2)}) collective-permute-start(bf16[32,2048]{1,0:T(8,128)(2,1)S(1)} %get-tuple-element.25), channel_id=1, source_target_pairs={{0,16},{8,24},{16,0},{24,8},{1,17},{9,25},{17,1},{25,9},{2,18},{10... | collective-permute-start | bytes 393224 | tf_op jit(solution)/shard_map/ppermute | solution.py:283
  29.7 7.2 %collective-permute-start.12 = (bf16[32,2048]{1,0:T(8,128)(2,1)S(1)}, bf16[32,2048]{1,0:T(8,128)(2,1)S(1)}, u32[]{:S(2)}, u32[]{:S(2)}) collective-permute-start(bf16[32,2048]{1,0:T(8,128)(2,1)S(1)} %get-tuple-element.25), channel_id=1, source_target_pairs={{0,24},{8,0},{16,8},{24,16},{1,25},{9,1},{17,9},{25,17},{2,26},{10... | collective-permute-start | bytes 393224 | tf_op jit(solution)/shard_map/ppermute | solution.py:283
  37.0 4.2 %collective-permute-start.13 = (bf16[240,2048]{1,0:T(8,128)(2,1)S(1)}, bf16[240,2048]{1,0:T(8,128)(2,1)S(1)}, u32[]{:S(2)}, u32[]{:S(2)}) collective-permute-start(bf16[240,2048]{1,0:T(8,128)(2,1)S(1)} %stack.13.refs_1_), channel_id=1, source_target_pairs={{0,1},{1,0},{2,3},{3,2},{4,5},{5,4},{6,7},{7,6},{8,9},{9,8},{10,11... | collective-permute-start | bytes 2949128 | tf_op jit(solution)/shard_map/ppermute | solution.py:17
  37.1 7.8 %collective-permute-start.14 = (bf16[96,1024]{1,0:T(8,128)(2,1)S(1)}, bf16[96,1024]{1,0:T(8,128)(2,1)S(1)}, u32[]{:S(2)}, u32[]{:S(2)}) collective-permute-start(bf16[96,1024]{1,0:T(8,128)(2,1)S(1)} %stack.11.refs_3_), channel_id=1, source_target_pairs={{0,2},{1,3},{2,0},{3,1},{4,6},{5,7},{6,4},{7,5},{8,10},{9,11},{10,... | collective-permute-start | bytes 589832 | tf_op jit(solution)/shard_map/ppermute | solution.py:17
  38.0 7.7 %collective-permute-start.19 = (bf16[96,1024]{1,0:T(8,128)(2,1)S(1)}, bf16[96,1024]{1,0:T(8,128)(2,1)S(1)}, u32[]{:S(2)}, u32[]{:S(2)}) collective-permute-start(bf16[96,1024]{1,0:T(8,128)(2,1)S(1)} %stack.12.refs_4_), channel_id=1, source_target_pairs={{0,4},{1,5},{2,6},{3,7},{4,0},{5,1},{6,2},{7,3},{8,12},{9,13},{10,... | collective-permute-start | bytes 589832 | tf_op jit(solution)/shard_map/ppermute | solution.py:17
  38.5 10.1 %collective-permute-start.15 = (bf16[96,1024]{1,0:T(8,128)(2,1)S(1)}, bf16[96,1024]{1,0:T(8,128)(2,1)S(1)}, u32[]{:S(2)}, u32[]{:S(2)}) collective-permute-start(bf16[96,1024]{1,0:T(8,128)(2,1)S(1)} %stack.12.refs_4_), channel_id=1, source_target_pairs={{0,2},{1,3},{2,0},{3,1},{4,6},{5,7},{6,4},{7,5},{8,10},{9,11},{10,... | collective-permute-start | bytes 589832 | tf_op jit(solution)/shard_map/ppermute | solution.py:17
  39.9 10.1 %collective-permute-start.18 = (bf16[96,1024]{1,0:T(8,128)(2,1)S(1)}, bf16[96,1024]{1,0:T(8,128)(2,1)S(1)}, u32[]{:S(2)}, u32[]{:S(2)}) collective-permute-start(bf16[96,1024]{1,0:T(8,128)(2,1)S(1)} %stack.11.refs_3_), channel_id=1, source_target_pairs={{0,4},{1,5},{2,6},{3,7},{4,0},{5,1},{6,2},{7,3},{8,12},{9,13},{10,... | collective-permute-start | bytes 589832 | tf_op jit(solution)/shard_map/ppermute | solution.py:17
  44.9 5.2 %collective-permute-start.16 = (bf16[96,1024]{1,0:T(8,128)(2,1)S(1)}, bf16[96,1024]{1,0:T(8,128)(2,1)S(1)}, u32[]{:S(2)}, u32[]{:S(2)}) collective-permute-start(bf16[96,1024]{1,0:T(8,128)(2,1)S(1)} %stack.14), channel_id=1, source_target_pairs={{0,1},{1,0},{2,3},{3,2},{4,5},{5,4},{6,7},{7,6},{8,9},{9,8},{10,11... | collective-permute-start | bytes 589832 | tf_op jit(solution)/shard_map/ppermute | solution.py:17
  45.0 10.5 %collective-permute-start.22 = (bf16[144,1024]{1,0:T(8,128)(2,1)S(1)}, bf16[144,1024]{1,0:T(8,128)(2,1)S(1)}, u32[]{:S(2)}, u32[]{:S(2)}) collective-permute-start(bf16[144,1024]{1,0:T(8,128)(2,1)S(1)} %stack.18), channel_id=1, source_target_pairs={{0,4},{1,5},{2,6},{3,7},{4,0},{5,1},{6,2},{7,3},{8,12},{9,13},{10,... | collective-permute-start | bytes 884744 | tf_op jit(solution)/shard_map/ppermute | solution.py:17
  45.8 9.8 %collective-permute-start.23 = (bf16[144,1024]{1,0:T(8,128)(2,1)S(1)}, bf16[144,1024]{1,0:T(8,128)(2,1)S(1)}, u32[]{:S(2)}, u32[]{:S(2)}) collective-permute-start(bf16[144,1024]{1,0:T(8,128)(2,1)S(1)} %stack.19), channel_id=1, source_target_pairs={{0,2},{1,3},{2,0},{3,1},{4,6},{5,7},{6,4},{7,5},{8,10},{9,11},{10,... | collective-permute-start | bytes 884744 | tf_op jit(solution)/shard_map/ppermute | solution.py:17
  48.7 2.0 %collective-permute-start.17 = (bf16[96,1024]{1,0:T(8,128)(2,1)S(1)}, bf16[96,1024]{1,0:T(8,128)(2,1)S(1)}, u32[]{:S(2)}, u32[]{:S(2)}) collective-permute-start(bf16[96,1024]{1,0:T(8,128)(2,1)S(1)} %stack.15), channel_id=1, source_target_pairs={{0,1},{1,0},{2,3},{3,2},{4,5},{5,4},{6,7},{7,6},{8,9},{9,8},{10,11... | collective-permute-start | bytes 589832 | tf_op jit(solution)/shard_map/ppermute | solution.py:17
  50.1 1.7 %collective-permute-start.21 = (bf16[96,1024]{1,0:T(8,128)(2,1)S(1)}, bf16[96,1024]{1,0:T(8,128)(2,1)S(1)}, u32[]{:S(2)}, u32[]{:S(2)}) collective-permute-start(bf16[96,1024]{1,0:T(8,128)(2,1)S(1)} %stack.17), channel_id=1, source_target_pairs={{0,1},{1,0},{2,3},{3,2},{4,5},{5,4},{6,7},{7,6},{8,9},{9,8},{10,11... | collective-permute-start | bytes 589832 | tf_op jit(solution)/shard_map/ppermute | solution.py:17
  55.6 2.2 %collective-permute-start.24 = (bf16[144,1024]{1,0:T(8,128)(2,1)S(1)}, bf16[144,1024]{1,0:T(8,128)(2,1)S(1)}, u32[]{:S(2)}, u32[]{:S(2)}) collective-permute-start(bf16[144,1024]{1,0:T(8,128)(2,1)S(1)} %stack.20), channel_id=1, source_target_pairs={{0,1},{1,0},{2,3},{3,2},{4,5},{5,4},{6,7},{7,6},{8,9},{9,8},{10,11... | collective-permute-start | bytes 884744 | tf_op jit(solution)/shard_map/ppermute | solution.py:17
  55.7 2.1 %collective-permute-start.25 = (bf16[144,1024]{1,0:T(8,128)(2,1)S(1)}, bf16[144,1024]{1,0:T(8,128)(2,1)S(1)}, u32[]{:S(2)}, u32[]{:S(2)}) collective-permute-start(bf16[144,1024]{1,0:T(8,128)(2,1)S(1)} %stack.21), channel_id=1, source_target_pairs={{0,1},{1,0},{2,3},{3,2},{4,5},{5,4},{6,7},{7,6},{8,9},{9,8},{10,11... | collective-permute-start | bytes 884744 | tf_op jit(solution)/shard_map/ppermute | solution.py:17
  (4 other events, 13.3 us)

commit v15 on v14

--- a/solution.py
+++ b/solution.py
@@ -97,6 +97,13 @@
         top += rows
 
 
+def copy_kernel(block, out):
+    rows = min(block.shape[0], out.shape[0])
+    out[:rows, :] = block[:rows, :]
+    if out.shape[0] > rows:
+        out[rows:, :] = block[: out.shape[0] - rows, :]
+
+
 def dense_kernel(size, picks_chip, rest_chip, chosen_ref, *refs):
     chips = size // 2
     counts, (own, sib, *outs, select_ref) = refs[:chips], refs[chips:]
@@ -136,9 +143,8 @@
         hit = place + owner * rest_chip == rank
         select_ref[top + picks_chip : top + rows_chip, :] = hit.astype(F32).astype(BF16)
 
-    @pl.loop(0, own.shape[1] // TILE)
-    def _(t):
-        at = pl.ds(pl.multiple_of(t * TILE, TILE), TILE)
+    for t in range(0, own.shape[1], TILE):
+        at = slice(t, t + TILE)
         rows = jnp.concatenate([own[:, at], sib[:, at]], axis=0)
         found = jnp.dot(select_ref[...], rows, preferred_element_type=F32).astype(BF16)
         for d, out in enumerate(outs):
@@ -173,7 +179,7 @@
 def lay_out(parts, rows_ref):
     left = 0
     for part in parts:
-        rows_ref[:, left : left + part.shape[1]] = part[...]
+        rows_ref[:, left : left + part.shape[1]] = part[: rows_ref.shape[0], :]
         left += part.shape[1]
     return row_norms(rows_ref[...])
 
@@ -189,12 +195,12 @@
     return jnp.min(gaps, axis=0, keepdims=True)
 
 
-def first_kernel(chip_rows, cand_ref, own, sib, near_ref, best_ref, rows_ref):
+def first_kernel(chip_rows, cand_ref, norm_ref, own, sib, near_ref, best_ref, rows_ref):
     norms = lay_out((own, sib), rows_ref)
     no_row, no_pick = row_masks(*chip_rows, norms.shape[0])
     for at in tiles_of(cand_ref):
         gaps = gaps_to(rows_ref, norms, cand_ref[at, :])
-        near_ref[:, at] = least(gaps + no_row)
+        near_ref[:, at] = least(gaps + no_row) + norm_ref[:, at]
         best_ref[:, at] = least(gaps + no_pick)
 
 
@@ -217,14 +223,12 @@
         out[:, at] = gaps_to(rows_ref, norms, cand_ref[at, : rows_ref.shape[1]])
 
 
-def last_kernel(chip_rows, cand_ref, norm_ref, near_ref, best_ref, part_ref, *refs):
-    *corner, near_out, best_out, rows_ref = refs
+def last_kernel(cand_ref, norm_ref, best_ref, part_ref, *refs):
+    *corner, out, rows_ref = refs
     norms = lay_out(corner, rows_ref)
-    no_row, no_pick = row_masks(*chip_rows, norms.shape[0])
     for at in tiles_of(cand_ref):
         gaps = part_ref[:, at] + gaps_to(rows_ref, norms, cand_ref[at, rows_ref.shape[1] :])
-        near_out[:, at] = jnp.minimum(least(gaps + no_row), near_ref[:, at]) + norm_ref[:, at]
-        best_out[:, at] = jnp.minimum(least(gaps + no_pick), best_ref[:, at]) + norm_ref[:, at]
+        out[:, at] = jnp.minimum(least(gaps), best_ref[:, at]) + norm_ref[:, at]
 
 
 def body(candidates, round_one, counts, chosen):
@@ -253,6 +257,10 @@
             functools.partial(stack_kernel, layout), "stack", shape, operands, after=after, weight=0
         )
 
+    def copy(block, count, after):
+        shape = bf16(count, block.shape[1])
+        return call(copy_kernel, "copy", shape, (block,), after=after, weight=0)
+
     line = jax.ShapeDtypeStruct((1, rows), F32)
     tile = jax.ShapeDtypeStruct((8, 128), jnp.int32)
     count = call(
@@ -287,48 +295,51 @@
     if chips == 4:
         quarter = half // 2
         own_x, own_y = (flip_permute(owned, size, flip) for flip in (2, 4))
-        wait = (own_x, own_y)
+        own_left = flip_permute(stack([(own_x, 0, quarter)]), size, 4)
+        own_right = flip_permute(stack([(own_y, quarter, quarter)]), size, 2)
+        wait = (own_left, own_right)
         low = stack(*[[(b, 0, quarter)] for b in shifted], after=wait)
         high = stack(*[[(b, quarter, quarter)] for b in shifted], after=wait)
         low_x, high_y = flip_permute(low, size, 2), flip_permute(high, size, 4)
         high_x, low_y = flip_permute(high, size, 2), flip_permute(low, size, 4)
-        first, chips_first = stack([owned], [own_x], [own_y], [low, high]), chips - 1
+        first = stack([owned], [own_x], [own_y], [own_left, own_right], [low, high])
         others = ([low_x, high_x], [low_y, high_y])
     else:
         far = to_chips(stack(*[[b] for b in shifted]), size)
-        *own_blocks, own_end = to_chips(owned, size)
-        first, chips_first = stack(*[[b] for b in own_blocks], [far[0]]), chips - 1
+        first = stack(*[[b] for b in to_chips(owned, size)], [far[0]])
         others = [[b] for b in far[1:-1]]
 
     near, best = call(
-        functools.partial(first_kernel, (picks_chip, rows_chip, chips_first * rows_chip)),
-        "products", [line] * 2, (cand, first, flip_permute(first, size, 1)),
+        functools.partial(first_kernel, (picks_chip, rows_chip, live)),
+        "products", [line] * 2, (cand, norm, first, flip_permute(first, size, 1)),
         scratch=[pltpu.VMEM((first.shape[0], width), BF16)], weight=WEIGHT // 10,
     )
+    rows_end = (groups - 1) * picks_chip
     if chips == 4:
-        left = stack([(own_x, 0, quarter)], [low_x], after=(best,))
-        right = stack([(own_y, quarter, quarter)], [high_y], after=(best,))
+        left = copy(low_x, rows_end + 16, (best,))
+        right = copy(high_y, rows_end + 16, (best,))
         corner = (flip_permute(left, size, 4), flip_permute(right, size, 2))
     else:
-        corner = (stack([own_end], [far[-1]]),)
-    operands = []
+        corner = (far[-1],)
+    operands, handed = [], (left, right) if chips == 4 else ()
     for block in others:
-        operands += [*block, *[flip_permute(stack([b], after=(best,)), size, 1) for b in block]]
+        operands += block
+        for b in block:
+            after = (best, *handed) if chips == 4 and b is not low_x else (best,)
+            operands.append(flip_permute(stack([b], after=after), size, 1))
     best = call(
         functools.partial(next_kernel, len(others)), "products_next", line, (cand, best, *operands),
         scratch=[pltpu.VMEM((len(others) * others[0][0].shape[0], width), BF16)], weight=0,
     )
-    sent = [stack([part], after=(best,)) for part in corner]
+    sent = [copy(part, rows_end, (best,)) for part in corner]
     swapped = [flip_permute(part, size, 1) for part in sent]
-    rows_end = corner[0].shape[0]
     scratch = [pltpu.VMEM((rows_end, half), BF16)]
     part = call(
         half_kernel, "products_half", jax.ShapeDtypeStruct((rows_end, rows), F32), (cand, *corner),
         scratch=scratch, after=(best,),
     )
-    near, final = call(
-        functools.partial(last_kernel, (picks_chip, rows_chip, rows_chip)), "products_last",
-        [line] * 2, (cand, norm, near, best, part, *swapped), scratch=scratch,
+    final = call(
+        last_kernel, "products_last", line, (cand, norm, best, part, *swapped), scratch=scratch
     )
     return near.reshape(-1), final.reshape(-1)
 

time: 60.1 us -> 59.5 us (0.990)
  waiting for transfers between devices: 18.9 us -> 17.1 us
  starting transfers between devices: 24 us -> 25.6 us
    ppermute x3, waiting for transfers between devices: 5.9 us -> 3.91 us  [body(): lax.ppermute(picked, 'grp', [(g, (g + k) % groups) for g in range(groups)])]
    ppermute x23 -> x25, starting transfers between devices: 18.5 us -> 20.1 us  [flip_permute(): return lax.ppermute(block, 'mem', [(m, m ^ flip) for m in range(size)])]
    pallas_call x21 -> x23, Pallas kernels: 15 us -> 14.6 us  [call(): pl.pallas_call(run, out_shape=out_shape, in_specs=(specs or vmem_specs(co...]
    ppermute x23 -> x25, waiting for transfers between devices: 13 us -> 13.2 us  [flip_permute(): return lax.ppermute(block, 'mem', [(m, m ^ flip) for m in range(size)])]
  transfers between devices with their start and end apart: 26 -> 28, of which waited for: 13 -> 12; matrix products, arithmetic and copies ran while one was open for 0% -> 0% of each run, Pallas kernels for 19% -> 20%
where the time goes in v15:
time: 59.5 us; the launch traced here: 59.3 us
  starting transfers between devices  25.6 us (43%)
  waiting for transfers between devices  17.1 us (29%)
  Pallas kernels  14.6 us (25%)
  between operations  1.48 us (2%)
    ppermute x25, starting transfers between devices, flip_permute(): return lax.ppermute(block, 'mem', [(m, m ^ flip) for m in range(size)])  20.1 us
    pallas_call x23, Pallas kernels, call(): pl.pallas_call(run, out_shape=out_shape, in_specs=(specs or vmem_specs(co...  14.6 us
    ppermute x25, waiting for transfers between devices, flip_permute(): return lax.ppermute(block, 'mem', [(m, m ^ flip) for m in range(size)])  13.2 us
    ppermute x3, starting transfers between devices, body(): lax.ppermute(picked, 'grp', [(g, (g + k) % groups) for g in range(groups)])  5.51 us
    ppermute x3, waiting for transfers between devices, body(): lax.ppermute(picked, 'grp', [(g, (g + k) % groups) for g in range(groups)])  3.91 us
  transfers between devices with their start and end apart: 28, of which 12 were waited for; matrix products, arithmetic and copies ran while one was open for 0% of the time, Pallas kernels for 20%

profile of v15, /device:TPU:0, one launch (start us, length us, event | category | flops | bytes accessed | tf_op | source)
XLA Modules:
  0.0 59.3 jit_solution(17912762147856564614)
XLA Ops:
  2.9 2.6 %collective-permute-start.1 = (s32[8,128]{1,0:T(8,128)S(1)}, s32[8,128]{1,0:T(8,128)S(1)}, u32[]{:S(2)}, u32[]{:S(2)}) collective-permute-start(s32[8,128]{1,0:T(8,128)S(1)} %pair.1.refs_1_), channel_id=1, source_target_pairs={{0,2},{1,3},{2,0},{3,1},{4,6},{5,7},{6,4},{7,5},{8,10},{9,11},{10,... | collective-permute-start | bytes 12296 | tf_op jit(solution)/shard_map/ppermute | solution.py:17
  5.5 1.5 %collective-permute-start.2 = (s32[8,128]{1,0:T(8,128)S(1)}, s32[8,128]{1,0:T(8,128)S(1)}, u32[]{:S(2)}, u32[]{:S(2)}) collective-permute-start(s32[8,128]{1,0:T(8,128)S(1)} %pair.1.refs_1_), channel_id=1, source_target_pairs={{0,4},{1,5},{2,6},{3,7},{4,0},{5,1},{6,2},{7,3},{8,12},{9,13},{10,... | collective-permute-start | bytes 12296 | tf_op jit(solution)/shard_map/ppermute | solution.py:17
  7.1 2.0 %collective-permute-done.2.refs_3_ = s32[8,128]{1,0:T(8,128)S(1)} collective-permute-done((s32[8,128]{1,0:T(8,128)S(1)}, s32[8,128]{1,0:T(8,128)S(1)}, u32[]{:S(2)}, u32[]{:S(2)}) %collective-permute-start.2) | collective-permute-done | bytes 4128 | tf_op jit(solution)/shard_map/ppermute | solution.py:17
  9.1 2.4 %collective-permute-done.3.refs_4_ = s32[8,128]{1,0:T(8,128)S(1)} collective-permute-done((s32[8,128]{1,0:T(8,128)S(1)}, s32[8,128]{1,0:T(8,128)S(1)}, u32[]{:S(2)}, u32[]{:S(2)}) %collective-permute-start.3) | collective-permute-done | bytes 4128 | tf_op jit(solution)/shard_map/ppermute | solution.py:17
  12.7 2.9 %collective-permute-start.7 = (bf16[48,2048]{1,0:T(8,128)(2,1)S(1)}, bf16[48,2048]{1,0:T(8,128)(2,1)S(1)}, u32[]{:S(2)}, u32[]{:S(2)}) collective-permute-start(bf16[48,2048]{1,0:T(8,128)(2,1)S(1)} %get-tuple-element.21), channel_id=1, source_target_pairs={{0,6},{1,7},{2,4},{3,5},{4,2},{5,3},{6,0},{7,1},{8,14},{9,15},{10,... | collective-permute-start | bytes 589832 | tf_op jit(solution)/shard_map/ppermute | solution.py:17
  15.6 4.0 %load.1 = (bf16[1024,4096]{1,0:T(8,128)(2,1)S(1)}, f32[1,1024]{1,0:T(1,128)S(1)}) custom-call(bf16[1024,4096]{1,0:T(8,128)(2,1)} %refs_0_.6, bf16[48,2048]{1,0:T(8,128)(2,1)S(1)} %get-tuple-element.16.refs_1_.refs_0_), custom_call_target="tpu_custom_call" | custom-call | flops 10000000000 | bytes 16781312 | tf_op jit(solution)/shard_map/load/pallas_call | solution.py:36
  19.8 2.4 %collective-permute-done.6.refs_2_ = bf16[48,2048]{1,0:T(8,128)(2,1)S(1)} collective-permute-done((bf16[48,2048]{1,0:T(8,128)(2,1)S(1)}, bf16[48,2048]{1,0:T(8,128)(2,1)S(1)}, u32[]{:S(2)}, u32[]{:S(2)}) %collective-permute-start.6) | collective-permute-done | bytes 196640 | tf_op jit(solution)/shard_map/ppermute | solution.py:17
  22.2 1.6 %collective-permute-start.8 = (bf16[48,2048]{1,0:T(8,128)(2,1)S(1)}, bf16[48,2048]{1,0:T(8,128)(2,1)S(1)}, u32[]{:S(2)}, u32[]{:S(2)}) collective-permute-start(bf16[48,2048]{1,0:T(8,128)(2,1)S(1)} %get-tuple-element.22.refs_0_), channel_id=1, source_target_pairs={{0,2},{1,3},{2,0},{3,1},{4,6},{5,7},{6,4},{7,5},{8,10},{9,11},{10,... | collective-permute-start | bytes 589832 | tf_op jit(solution)/shard_map/ppermute | solution.py:17
  24.5 1.6 %collective-permute-start.12 = (bf16[32,2048]{1,0:T(8,128)(2,1)S(1)}, bf16[32,2048]{1,0:T(8,128)(2,1)S(1)}, u32[]{:S(2)}, u32[]{:S(2)}) collective-permute-start(bf16[32,2048]{1,0:T(8,128)(2,1)S(1)} %get-tuple-element.23), channel_id=1, source_target_pairs={{0,8},{8,16},{16,24},{24,0},{1,9},{9,17},{17,25},{25,1},{2,10},{10... | collective-permute-start | bytes 393224 | tf_op jit(solution)/shard_map/ppermute | solution.py:291
  26.1 2.6 %collective-permute-start.13 = (bf16[32,2048]{1,0:T(8,128)(2,1)S(1)}, bf16[32,2048]{1,0:T(8,128)(2,1)S(1)}, u32[]{:S(2)}, u32[]{:S(2)}) collective-permute-start(bf16[32,2048]{1,0:T(8,128)(2,1)S(1)} %get-tuple-element.23), channel_id=1, source_target_pairs={{0,16},{8,24},{16,0},{24,8},{1,17},{9,25},{17,1},{25,9},{2,18},{10... | collective-permute-start | bytes 393224 | tf_op jit(solution)/shard_map/ppermute | solution.py:291
  28.6 1.3 %collective-permute-start.14 = (bf16[32,2048]{1,0:T(8,128)(2,1)S(1)}, bf16[32,2048]{1,0:T(8,128)(2,1)S(1)}, u32[]{:S(2)}, u32[]{:S(2)}) collective-permute-start(bf16[32,2048]{1,0:T(8,128)(2,1)S(1)} %get-tuple-element.23), channel_id=1, source_target_pairs={{0,24},{8,0},{16,8},{24,16},{1,25},{9,1},{17,9},{25,17},{2,26},{10... | collective-permute-start | bytes 393224 | tf_op jit(solution)/shard_map/ppermute | solution.py:291
  30.0 1.4 %collective-permute-start.10 = (bf16[48,1024]{1,0:T(8,128)(2,1)S(1)}, bf16[48,1024]{1,0:T(8,128)(2,1)S(1)}, u32[]{:S(2)}, u32[]{:S(2)}) collective-permute-start(bf16[48,1024]{1,0:T(8,128)(2,1)S(1)} %stack.9), channel_id=1, source_target_pairs={{0,4},{1,5},{2,6},{3,7},{4,0},{5,1},{6,2},{7,3},{8,12},{9,13},{10,... | collective-permute-start | bytes 294920 | tf_op jit(solution)/shard_map/ppermute | solution.py:17
  32.0 3.9 %collective-permute-done.13.refs_1_ = bf16[32,2048]{1,0:T(8,128)(2,1)S(1)} collective-permute-done((bf16[32,2048]{1,0:T(8,128)(2,1)S(1)}, bf16[32,2048]{1,0:T(8,128)(2,1)S(1)}, u32[]{:S(2)}, u32[]{:S(2)}) %collective-permute-start.13) | collective-permute-done | bytes 131104 | tf_op jit(solution)/shard_map/ppermute | solution.py:291
  37.0 1.3 %collective-permute-start.17 = (bf16[96,1024]{1,0:T(8,128)(2,1)S(1)}, bf16[96,1024]{1,0:T(8,128)(2,1)S(1)}, u32[]{:S(2)}, u32[]{:S(2)}) collective-permute-start(bf16[96,1024]{1,0:T(8,128)(2,1)S(1)} %stack.12.refs_6_), channel_id=1, source_target_pairs={{0,2},{1,3},{2,0},{3,1},{4,6},{5,7},{6,4},{7,5},{8,10},{9,11},{10,... | collective-permute-start | bytes 589832 | tf_op jit(solution)/shard_map/ppermute | solution.py:17
  39.1 1.3 %collective-permute-start.21 = (bf16[96,1024]{1,0:T(8,128)(2,1)S(1)}, bf16[96,1024]{1,0:T(8,128)(2,1)S(1)}, u32[]{:S(2)}, u32[]{:S(2)}) collective-permute-start(bf16[96,1024]{1,0:T(8,128)(2,1)S(1)} %stack.11.refs_5_), channel_id=1, source_target_pairs={{0,4},{1,5},{2,6},{3,7},{4,0},{5,1},{6,2},{7,3},{8,12},{9,13},{10,... | collective-permute-start | bytes 589832 | tf_op jit(solution)/shard_map/ppermute | solution.py:17
  40.4 3.3 %products.1 = (f32[1,1024]{1,0:T(1,128)}, f32[1,1024]{1,0:T(1,128)S(1)}) custom-call(bf16[1024,4096]{1,0:T(8,128)(2,1)S(1)} %get-tuple-element.17.refs_0_, f32[1,1024]{1,0:T(1,128)S(1)} %get-tuple-element.18.refs_4_.refs_1_, bf16[288,2048]{1,0:T(8,128)(2,1)S(1)} %stack.13.refs_2_, bf16[288,2048]{1,0:T(8,128)(2,1)S(1)} %collective-permute-done.15.refs_3_), custom_call_target="tpu_custom_call" | custom-call | flops 1000000000 | bytes 10760192 | tf_op jit(solution)/shard_map/products/pallas_call | solution.py:36
  44.2 0.8 %collective-permute-start.24 = (bf16[112,1024]{1,0:T(8,128)(2,1)S(1)}, bf16[112,1024]{1,0:T(8,128)(2,1)S(1)}, u32[]{:S(2)}, u32[]{:S(2)}) collective-permute-start(bf16[112,1024]{1,0:T(8,128)(2,1)S(1)} %copy.11.refs_2_), channel_id=1, source_target_pairs={{0,4},{1,5},{2,6},{3,7},{4,0},{5,1},{6,2},{7,3},{8,12},{9,13},{10,... | collective-permute-start | bytes 688136 | tf_op jit(solution)/shard_map/ppermute | solution.py:17
  45.0 1.2 %collective-permute-done.19.refs_0_.refs_7_ = bf16[96,1024]{1,0:T(8,128)(2,1)S(1)} collective-permute-done((bf16[96,1024]{1,0:T(8,128)(2,1)S(1)}, bf16[96,1024]{1,0:T(8,128)(2,1)S(1)}, u32[]{:S(2)}, u32[]{:S(2)}) %collective-permute-start.19) | collective-permute-done | bytes 196640 | tf_op jit(solution)/shard_map/ppermute | solution.py:17
  46.9 0.9 %collective-permute-done.17.refs_0_.refs_3_ = bf16[96,1024]{1,0:T(8,128)(2,1)S(1)} collective-permute-done((bf16[96,1024]{1,0:T(8,128)(2,1)S(1)}, bf16[96,1024]{1,0:T(8,128)(2,1)S(1)}, u32[]{:S(2)}, u32[]{:S(2)}) %collective-permute-start.17) | collective-permute-done | bytes 196640 | tf_op jit(solution)/shard_map/ppermute | solution.py:17
  47.9 2.5 %collective-permute-done.21.refs_0_.refs_6_ = bf16[96,1024]{1,0:T(8,128)(2,1)S(1)} collective-permute-done((bf16[96,1024]{1,0:T(8,128)(2,1)S(1)}, bf16[96,1024]{1,0:T(8,128)(2,1)S(1)}, u32[]{:S(2)}, u32[]{:S(2)}) %collective-permute-start.21) | collective-permute-done | bytes 196640 | tf_op jit(solution)/shard_map/ppermute | solution.py:17
  51.0 0.8 %collective-permute-done.22.refs_8_ = bf16[96,1024]{1,0:T(8,128)(2,1)S(1)} collective-permute-done((bf16[96,1024]{1,0:T(8,128)(2,1)S(1)}, bf16[96,1024]{1,0:T(8,128)(2,1)S(1)}, u32[]{:S(2)}, u32[]{:S(2)}) %collective-permute-start.22) | collective-permute-done | bytes 196640 | tf_op jit(solution)/shard_map/ppermute | solution.py:17
  52.2 3.0 %products_next.1.refs_3_.refs_1_.refs_2_ = f32[1,1024]{1,0:T(1,128)S(1)} custom-call(bf16[1024,4096]{1,0:T(8,128)(2,1)S(1)} %get-tuple-element.17.refs_0_, f32[1,1024]{1,0:T(1,128)S(1)} %get-tuple-element.25.refs_1_, bf16[96,1024]{1,0:T(8,128)(2,1)S(1)} %collective-permute-done.16.refs_0_.refs_2_, ...), custom_call_target="tpu_custom_call" | custom-call | bytes 9969664 | tf_op jit(solution)/shard_map/products_next/pallas_call | solution.py:36
  55.8 1.4 %products_half.1.refs_3_ = f32[96,1024]{1,0:T(8,128)S(1)} custom-call(bf16[1024,4096]{1,0:T(8,128)(2,1)S(1)} %get-tuple-element.17.refs_0_, bf16[112,1024]{1,0:T(8,128)(2,1)S(1)} %collective-permute-done.24.refs_1_.refs_0_, bf16[112,1024]{1,0:T(8,128)(2,1)S(1)} %collective-permute-done.25.refs_2_.refs_0_, f32[1,1024]{1,0:T(1,128)S(1)} %products_next.1.refs_3_.refs_1_.refs_2_), custom_call_target="tpu_custom_call" | custom-call | flops 10000000000 | bytes 9240576 | tf_op jit(solution)/shard_map/products_half/pallas_call | solution.py:36
  57.3 2.0 %products_last.1 = f32[1,1024]{1,0:T(1,128)} custom-call(bf16[1024,4096]{1,0:T(8,128)(2,1)S(1)} %get-tuple-element.17.refs_0_, f32[1,1024]{1,0:T(1,128)S(1)} %get-tuple-element.18.refs_4_.refs_1_, f32[1,1024]{1,0:T(1,128)S(1)} %products_next.1.refs_3_.refs_1_.refs_2_, f32[96,1024]{1,0:T(8,128)S(1)} %products_half.1.refs_3_, ...), custom_call_target="tpu_custom_call" | custom-call | flops 10000000000 | bytes 9187328 | tf_op jit(solution)/shard_map/products_last/pallas_call | solution.py:36
  (59 shorter events, 9.2 us)
Async XLA Ops:
  2.4 9.1 %collective-permute-start.4 = (bf16[64,2048]{1,0:T(8,128)(2,1)S(1)}, bf16[64,2048]{1,0:T(8,128)(2,1)S(1)}, u32[]{:S(2)}, u32[]{:S(2)}) collective-permute-start(bf16[64,2048]{1,0:T(8,128)(2,1)S(1)} %get-tuple-element.15), channel_id=1, source_target_pairs={{0,1},{1,0},{2,3},{3,2},{4,5},{5,4},{6,7},{7,6},{8,9},{9,8},{10,11... | collective-permute-start | bytes 786440 | tf_op jit(solution)/shard_map/ppermute | solution.py:17
  2.9 4.2 %collective-permute-start.1 = (s32[8,128]{1,0:T(8,128)S(1)}, s32[8,128]{1,0:T(8,128)S(1)}, u32[]{:S(2)}, u32[]{:S(2)}) collective-permute-start(s32[8,128]{1,0:T(8,128)S(1)} %pair.1.refs_1_), channel_id=1, source_target_pairs={{0,2},{1,3},{2,0},{3,1},{4,6},{5,7},{6,4},{7,5},{8,10},{9,11},{10,... | collective-permute-start | bytes 12296 | tf_op jit(solution)/shard_map/ppermute | solution.py:17
  5.5 3.6 %collective-permute-start.2 = (s32[8,128]{1,0:T(8,128)S(1)}, s32[8,128]{1,0:T(8,128)S(1)}, u32[]{:S(2)}, u32[]{:S(2)}) collective-permute-start(s32[8,128]{1,0:T(8,128)S(1)} %pair.1.refs_1_), channel_id=1, source_target_pairs={{0,4},{1,5},{2,6},{3,7},{4,0},{5,1},{6,2},{7,3},{8,12},{9,13},{10,... | collective-permute-start | bytes 12296 | tf_op jit(solution)/shard_map/ppermute | solution.py:17
  7.0 4.5 %collective-permute-start.3 = (s32[8,128]{1,0:T(8,128)S(1)}, s32[8,128]{1,0:T(8,128)S(1)}, u32[]{:S(2)}, u32[]{:S(2)}) collective-permute-start(s32[8,128]{1,0:T(8,128)S(1)} %pair.1.refs_1_), channel_id=1, source_target_pairs={{0,6},{1,7},{2,4},{3,5},{4,2},{5,3},{6,0},{7,1},{8,14},{9,15},{10,... | collective-permute-start | bytes 12296 | tf_op jit(solution)/shard_map/ppermute | solution.py:17
  12.1 7.7 %collective-permute-start.5 = (bf16[48,2048]{1,0:T(8,128)(2,1)S(1)}, bf16[48,2048]{1,0:T(8,128)(2,1)S(1)}, u32[]{:S(2)}, u32[]{:S(2)}) collective-permute-start(bf16[48,2048]{1,0:T(8,128)(2,1)S(1)} %get-tuple-element.19), channel_id=1, source_target_pairs={{0,2},{1,3},{2,0},{3,1},{4,6},{5,7},{6,4},{7,5},{8,10},{9,11},{10,... | collective-permute-start | bytes 589832 | tf_op jit(solution)/shard_map/ppermute | solution.py:17
  12.7 9.5 %collective-permute-start.6 = (bf16[48,2048]{1,0:T(8,128)(2,1)S(1)}, bf16[48,2048]{1,0:T(8,128)(2,1)S(1)}, u32[]{:S(2)}, u32[]{:S(2)}) collective-permute-start(bf16[48,2048]{1,0:T(8,128)(2,1)S(1)} %get-tuple-element.20), channel_id=1, source_target_pairs={{0,4},{1,5},{2,6},{3,7},{4,0},{5,1},{6,2},{7,3},{8,12},{9,13},{10,... | collective-permute-start | bytes 589832 | tf_op jit(solution)/shard_map/ppermute | solution.py:17
  12.7 9.4 %collective-permute-start.7 = (bf16[48,2048]{1,0:T(8,128)(2,1)S(1)}, bf16[48,2048]{1,0:T(8,128)(2,1)S(1)}, u32[]{:S(2)}, u32[]{:S(2)}) collective-permute-start(bf16[48,2048]{1,0:T(8,128)(2,1)S(1)} %get-tuple-element.21), channel_id=1, source_target_pairs={{0,6},{1,7},{2,4},{3,5},{4,2},{5,3},{6,0},{7,1},{8,14},{9,15},{10,... | collective-permute-start | bytes 589832 | tf_op jit(solution)/shard_map/ppermute | solution.py:17
  22.2 7.8 %collective-permute-start.8 = (bf16[48,2048]{1,0:T(8,128)(2,1)S(1)}, bf16[48,2048]{1,0:T(8,128)(2,1)S(1)}, u32[]{:S(2)}, u32[]{:S(2)}) collective-permute-start(bf16[48,2048]{1,0:T(8,128)(2,1)S(1)} %get-tuple-element.22.refs_0_), channel_id=1, source_target_pairs={{0,2},{1,3},{2,0},{3,1},{4,6},{5,7},{6,4},{7,5},{8,10},{9,11},{10,... | collective-permute-start | bytes 589832 | tf_op jit(solution)/shard_map/ppermute | solution.py:17
  23.7 7.6 %collective-permute-start.9 = (bf16[48,2048]{1,0:T(8,128)(2,1)S(1)}, bf16[48,2048]{1,0:T(8,128)(2,1)S(1)}, u32[]{:S(2)}, u32[]{:S(2)}) collective-permute-start(bf16[48,2048]{1,0:T(8,128)(2,1)S(1)} %get-tuple-element.22.refs_0_), channel_id=1, source_target_pairs={{0,4},{1,5},{2,6},{3,7},{4,0},{5,1},{6,2},{7,3},{8,12},{9,13},{10,... | collective-permute-start | bytes 589832 | tf_op jit(solution)/shard_map/ppermute | solution.py:17
  24.5 7.5 %collective-permute-start.12 = (bf16[32,2048]{1,0:T(8,128)(2,1)S(1)}, bf16[32,2048]{1,0:T(8,128)(2,1)S(1)}, u32[]{:S(2)}, u32[]{:S(2)}) collective-permute-start(bf16[32,2048]{1,0:T(8,128)(2,1)S(1)} %get-tuple-element.23), channel_id=1, source_target_pairs={{0,8},{8,16},{16,24},{24,0},{1,9},{9,17},{17,25},{25,1},{2,10},{10... | collective-permute-start | bytes 393224 | tf_op jit(solution)/shard_map/ppermute | solution.py:291
  26.1 9.8 %collective-permute-start.13 = (bf16[32,2048]{1,0:T(8,128)(2,1)S(1)}, bf16[32,2048]{1,0:T(8,128)(2,1)S(1)}, u32[]{:S(2)}, u32[]{:S(2)}) collective-permute-start(bf16[32,2048]{1,0:T(8,128)(2,1)S(1)} %get-tuple-element.23), channel_id=1, source_target_pairs={{0,16},{8,24},{16,0},{24,8},{1,17},{9,25},{17,1},{25,9},{2,18},{10... | collective-permute-start | bytes 393224 | tf_op jit(solution)/shard_map/ppermute | solution.py:291
  28.6 7.2 %collective-permute-start.14 = (bf16[32,2048]{1,0:T(8,128)(2,1)S(1)}, bf16[32,2048]{1,0:T(8,128)(2,1)S(1)}, u32[]{:S(2)}, u32[]{:S(2)}) collective-permute-start(bf16[32,2048]{1,0:T(8,128)(2,1)S(1)} %get-tuple-element.23), channel_id=1, source_target_pairs={{0,24},{8,0},{16,8},{24,16},{1,25},{9,1},{17,9},{25,17},{2,26},{10... | collective-permute-start | bytes 393224 | tf_op jit(solution)/shard_map/ppermute | solution.py:291
  30.0 5.9 %collective-permute-start.10 = (bf16[48,1024]{1,0:T(8,128)(2,1)S(1)}, bf16[48,1024]{1,0:T(8,128)(2,1)S(1)}, u32[]{:S(2)}, u32[]{:S(2)}) collective-permute-start(bf16[48,1024]{1,0:T(8,128)(2,1)S(1)} %stack.9), channel_id=1, source_target_pairs={{0,4},{1,5},{2,6},{3,7},{4,0},{5,1},{6,2},{7,3},{8,12},{9,13},{10,... | collective-permute-start | bytes 294920 | tf_op jit(solution)/shard_map/ppermute | solution.py:17
  31.4 4.7 %collective-permute-start.11 = (bf16[48,1024]{1,0:T(8,128)(2,1)S(1)}, bf16[48,1024]{1,0:T(8,128)(2,1)S(1)}, u32[]{:S(2)}, u32[]{:S(2)}) collective-permute-start(bf16[48,1024]{1,0:T(8,128)(2,1)S(1)} %stack.10), channel_id=1, source_target_pairs={{0,2},{1,3},{2,0},{3,1},{4,6},{5,7},{6,4},{7,5},{8,10},{9,11},{10,... | collective-permute-start | bytes 294920 | tf_op jit(solution)/shard_map/ppermute | solution.py:17
  36.2 4.2 %collective-permute-start.15 = (bf16[288,2048]{1,0:T(8,128)(2,1)S(1)}, bf16[288,2048]{1,0:T(8,128)(2,1)S(1)}, u32[]{:S(2)}, u32[]{:S(2)}) collective-permute-start(bf16[288,2048]{1,0:T(8,128)(2,1)S(1)} %stack.13.refs_2_), channel_id=1, source_target_pairs={{0,1},{1,0},{2,3},{3,2},{4,5},{5,4},{6,7},{7,6},{8,9},{9,8},{10,11... | collective-permute-start | bytes 3538952 | tf_op jit(solution)/shard_map/ppermute | solution.py:17
  36.3 7.8 %collective-permute-start.16 = (bf16[96,1024]{1,0:T(8,128)(2,1)S(1)}, bf16[96,1024]{1,0:T(8,128)(2,1)S(1)}, u32[]{:S(2)}, u32[]{:S(2)}) collective-permute-start(bf16[96,1024]{1,0:T(8,128)(2,1)S(1)} %stack.11.refs_5_), channel_id=1, source_target_pairs={{0,2},{1,3},{2,0},{3,1},{4,6},{5,7},{6,4},{7,5},{8,10},{9,11},{10,... | collective-permute-start | bytes 589832 | tf_op jit(solution)/shard_map/ppermute | solution.py:17
  37.0 10.8 %collective-permute-start.17 = (bf16[96,1024]{1,0:T(8,128)(2,1)S(1)}, bf16[96,1024]{1,0:T(8,128)(2,1)S(1)}, u32[]{:S(2)}, u32[]{:S(2)}) collective-permute-start(bf16[96,1024]{1,0:T(8,128)(2,1)S(1)} %stack.12.refs_6_), channel_id=1, source_target_pairs={{0,2},{1,3},{2,0},{3,1},{4,6},{5,7},{6,4},{7,5},{8,10},{9,11},{10,... | collective-permute-start | bytes 589832 | tf_op jit(solution)/shard_map/ppermute | solution.py:17
  38.4 7.8 %collective-permute-start.19 = (bf16[96,1024]{1,0:T(8,128)(2,1)S(1)}, bf16[96,1024]{1,0:T(8,128)(2,1)S(1)}, u32[]{:S(2)}, u32[]{:S(2)}) collective-permute-start(bf16[96,1024]{1,0:T(8,128)(2,1)S(1)} %stack.12.refs_6_), channel_id=1, source_target_pairs={{0,4},{1,5},{2,6},{3,7},{4,0},{5,1},{6,2},{7,3},{8,12},{9,13},{10,... | collective-permute-start | bytes 589832 | tf_op jit(solution)/shard_map/ppermute | solution.py:17
  39.1 11.3 %collective-permute-start.21 = (bf16[96,1024]{1,0:T(8,128)(2,1)S(1)}, bf16[96,1024]{1,0:T(8,128)(2,1)S(1)}, u32[]{:S(2)}, u32[]{:S(2)}) collective-permute-start(bf16[96,1024]{1,0:T(8,128)(2,1)S(1)} %stack.11.refs_5_), channel_id=1, source_target_pairs={{0,4},{1,5},{2,6},{3,7},{4,0},{5,1},{6,2},{7,3},{8,12},{9,13},{10,... | collective-permute-start | bytes 589832 | tf_op jit(solution)/shard_map/ppermute | solution.py:17
  44.1 6.4 %collective-permute-start.18 = (bf16[96,1024]{1,0:T(8,128)(2,1)S(1)}, bf16[96,1024]{1,0:T(8,128)(2,1)S(1)}, u32[]{:S(2)}, u32[]{:S(2)}) collective-permute-start(bf16[96,1024]{1,0:T(8,128)(2,1)S(1)} %stack.14), channel_id=1, source_target_pairs={{0,1},{1,0},{2,3},{3,2},{4,5},{5,4},{6,7},{7,6},{8,9},{9,8},{10,11... | collective-permute-start | bytes 589832 | tf_op jit(solution)/shard_map/ppermute | solution.py:17
  44.2 11.0 %collective-permute-start.24 = (bf16[112,1024]{1,0:T(8,128)(2,1)S(1)}, bf16[112,1024]{1,0:T(8,128)(2,1)S(1)}, u32[]{:S(2)}, u32[]{:S(2)}) collective-permute-start(bf16[112,1024]{1,0:T(8,128)(2,1)S(1)} %copy.11.refs_2_), channel_id=1, source_target_pairs={{0,4},{1,5},{2,6},{3,7},{4,0},{5,1},{6,2},{7,3},{8,12},{9,13},{10,... | collective-permute-start | bytes 688136 | tf_op jit(solution)/shard_map/ppermute | solution.py:17
  46.2 9.4 %collective-permute-start.25 = (bf16[112,1024]{1,0:T(8,128)(2,1)S(1)}, bf16[112,1024]{1,0:T(8,128)(2,1)S(1)}, u32[]{:S(2)}, u32[]{:S(2)}) collective-permute-start(bf16[112,1024]{1,0:T(8,128)(2,1)S(1)} %copy.12.refs_3_), channel_id=1, source_target_pairs={{0,2},{1,3},{2,0},{3,1},{4,6},{5,7},{6,4},{7,5},{8,10},{9,11},{10,... | collective-permute-start | bytes 688136 | tf_op jit(solution)/shard_map/ppermute | solution.py:17
  47.8 3.2 %collective-permute-start.20 = (bf16[96,1024]{1,0:T(8,128)(2,1)S(1)}, bf16[96,1024]{1,0:T(8,128)(2,1)S(1)}, u32[]{:S(2)}, u32[]{:S(2)}) collective-permute-start(bf16[96,1024]{1,0:T(8,128)(2,1)S(1)} %stack.15), channel_id=1, source_target_pairs={{0,1},{1,0},{2,3},{3,2},{4,5},{5,4},{6,7},{7,6},{8,9},{9,8},{10,11... | collective-permute-start | bytes 589832 | tf_op jit(solution)/shard_map/ppermute | solution.py:17
  55.2 2.1 %collective-permute-start.26 = (bf16[96,1024]{1,0:T(8,128)(2,1)S(1)}, bf16[96,1024]{1,0:T(8,128)(2,1)S(1)}, u32[]{:S(2)}, u32[]{:S(2)}) collective-permute-start(bf16[96,1024]{1,0:T(8,128)(2,1)S(1)} %copy.13), channel_id=1, source_target_pairs={{0,1},{1,0},{2,3},{3,2},{4,5},{5,4},{6,7},{7,6},{8,9},{9,8},{10,11... | collective-permute-start | bytes 589832 | tf_op jit(solution)/shard_map/ppermute | solution.py:17
  (6 other events, 16.7 us)

commit v16 on v15

--- a/solution.py
+++ b/solution.py
@@ -204,23 +204,24 @@
         best_ref[:, at] = least(gaps + no_pick)
 
 
-def next_kernel(blocks, cand_ref, best_ref, *refs):
-    *parts, out, rows_ref = refs
-    norms, count, rows = [], len(parts) // blocks, rows_ref.shape[0] // blocks
+def next_kernel(blocks, count, cand_ref, best_ref, *refs):
+    *parts, out, part_ref, own_ref, sib_ref = refs
+    rows, half = sib_ref.shape
+    each = rows // blocks
+    own_norms, sib_norms = [], []
     for b in range(blocks):
-        block = rows_ref.at[b * rows : (b + 1) * rows, :]
-        norms.append(lay_out(parts[b * count : (b + 1) * count], block))
-    norms = jnp.concatenate(norms, axis=0)
+        at = slice(b * each, (b + 1) * each)
+        own_norms.append(lay_out(parts[:count], own_ref.at[at, :]))
+        sib_norms.append(lay_out(parts[count : 2 * count], sib_ref.at[at, :]))
+        parts = parts[2 * count :]
+    own_norms.append(lay_out(parts, own_ref.at[rows:, :]))
+    own_norms = jnp.concatenate(own_norms, axis=0)
+    sib_norms = jnp.concatenate(sib_norms, axis=0)
     for at in tiles_of(cand_ref):
-        gaps = gaps_to(rows_ref, norms, cand_ref[at, :])
+        gaps = gaps_to(own_ref, own_norms, cand_ref[at, :half])
+        part_ref[:, at] = gaps[rows:]
+        gaps = gaps[:rows] + gaps_to(sib_ref, sib_norms, cand_ref[at, half:])
         out[:, at] = jnp.minimum(least(gaps), best_ref[:, at])
-
-
-def half_kernel(cand_ref, *refs):
-    *corner, out, rows_ref = refs
-    norms = lay_out(corner, rows_ref)
-    for at in tiles_of(cand_ref):
-        out[:, at] = gaps_to(rows_ref, norms, cand_ref[at, : rows_ref.shape[1]])
 
 
 def last_kernel(cand_ref, norm_ref, best_ref, part_ref, *refs):
@@ -327,17 +328,17 @@
         for b in block:
             after = (best, *handed) if chips == 4 and b is not low_x else (best,)
             operands.append(flip_permute(stack([b], after=after), size, 1))
-    best = call(
-        functools.partial(next_kernel, len(others)), "products_next", line, (cand, best, *operands),
-        scratch=[pltpu.VMEM((len(others) * others[0][0].shape[0], width), BF16)], weight=0,
-    )
-    sent = [copy(part, rows_end, (best,)) for part in corner]
-    swapped = [flip_permute(part, size, 1) for part in sent]
+    swapped = [flip_permute(copy(part, rows_end, (operands[-1],)), size, 1) for part in corner]
+    rows_next = len(others) * rows_end
+    best, part = call(
+        functools.partial(next_kernel, len(others), len(others[0])), "products_next",
+        [line, jax.ShapeDtypeStruct((rows_end, rows), F32)], (cand, best, *operands, *corner),
+        scratch=[
+            pltpu.VMEM((rows_next + rows_end, half), BF16), pltpu.VMEM((rows_next, half), BF16)
+        ],
+        weight=WEIGHT // 3,
+    )
     scratch = [pltpu.VMEM((rows_end, half), BF16)]
-    part = call(
-        half_kernel, "products_half", jax.ShapeDtypeStruct((rows_end, rows), F32), (cand, *corner),
-        scratch=scratch, after=(best,),
-    )
     final = call(
         last_kernel, "products_last", line, (cand, norm, best, part, *swapped), scratch=scratch
     )

time: 59.5 us -> 58.9 us (0.990)
  Pallas kernels: 14.6 us -> 13 us
  waiting for transfers between devices: 17.1 us -> 18.1 us
    pallas_call x23 -> x22, Pallas kernels: 14.6 us -> 13 us  [call(): pl.pallas_call(run, out_shape=out_shape, in_specs=(specs or vmem_specs(co...]
    ppermute x25, waiting for transfers between devices: 13.2 us -> 14.2 us  [flip_permute(): return lax.ppermute(block, 'mem', [(m, m ^ flip) for m in range(size)])]
  transfers between devices with their start and end apart: 28 -> 28, of which waited for: 12 -> 12; matrix products, arithmetic and copies ran while one was open for 0% -> 0% of each run, Pallas kernels for 20% -> 18%
where the time goes in v16:
time: 58.9 us; the launch traced here: 58.7 us
  starting transfers between devices  25.6 us (43%)
  waiting for transfers between devices  18.1 us (31%)
  Pallas kernels  13 us (22%)
  between operations  1.46 us (2%)
    ppermute x25, starting transfers between devices, flip_permute(): return lax.ppermute(block, 'mem', [(m, m ^ flip) for m in range(size)])  20.1 us
    ppermute x25, waiting for transfers between devices, flip_permute(): return lax.ppermute(block, 'mem', [(m, m ^ flip) for m in range(size)])  14.2 us
    pallas_call x22, Pallas kernels, call(): pl.pallas_call(run, out_shape=out_shape, in_specs=(specs or vmem_specs(co...  13 us
    ppermute x3, starting transfers between devices, body(): lax.ppermute(picked, 'grp', [(g, (g + k) % groups) for g in range(groups)])  5.51 us
    ppermute x3, waiting for transfers between devices, body(): lax.ppermute(picked, 'grp', [(g, (g + k) % groups) for g in range(groups)])  3.91 us
  transfers between devices with their start and end apart: 28, of which 12 were waited for; matrix products, arithmetic and copies ran while one was open for 0% of the time, Pallas kernels for 18%

profile of v16, /device:TPU:0, one launch (start us, length us, event | category | flops | bytes accessed | tf_op | source)
XLA Modules:
  0.0 58.7 jit_solution(7235537243035945498)
XLA Ops:
  2.9 2.6 %collective-permute-start.1 = (s32[8,128]{1,0:T(8,128)S(1)}, s32[8,128]{1,0:T(8,128)S(1)}, u32[]{:S(2)}, u32[]{:S(2)}) collective-permute-start(s32[8,128]{1,0:T(8,128)S(1)} %pair.1.refs_1_), channel_id=1, source_target_pairs={{0,2},{1,3},{2,0},{3,1},{4,6},{5,7},{6,4},{7,5},{8,10},{9,11},{10,... | collective-permute-start | bytes 12296 | tf_op jit(solution)/shard_map/ppermute | solution.py:17
  5.5 1.5 %collective-permute-start.2 = (s32[8,128]{1,0:T(8,128)S(1)}, s32[8,128]{1,0:T(8,128)S(1)}, u32[]{:S(2)}, u32[]{:S(2)}) collective-permute-start(s32[8,128]{1,0:T(8,128)S(1)} %pair.1.refs_1_), channel_id=1, source_target_pairs={{0,4},{1,5},{2,6},{3,7},{4,0},{5,1},{6,2},{7,3},{8,12},{9,13},{10,... | collective-permute-start | bytes 12296 | tf_op jit(solution)/shard_map/ppermute | solution.py:17
  7.1 2.0 %collective-permute-done.2.refs_3_ = s32[8,128]{1,0:T(8,128)S(1)} collective-permute-done((s32[8,128]{1,0:T(8,128)S(1)}, s32[8,128]{1,0:T(8,128)S(1)}, u32[]{:S(2)}, u32[]{:S(2)}) %collective-permute-start.2) | collective-permute-done | bytes 4128 | tf_op jit(solution)/shard_map/ppermute | solution.py:17
  9.1 2.4 %collective-permute-done.3.refs_4_ = s32[8,128]{1,0:T(8,128)S(1)} collective-permute-done((s32[8,128]{1,0:T(8,128)S(1)}, s32[8,128]{1,0:T(8,128)S(1)}, u32[]{:S(2)}, u32[]{:S(2)}) %collective-permute-start.3) | collective-permute-done | bytes 4128 | tf_op jit(solution)/shard_map/ppermute | solution.py:17
  12.7 2.9 %collective-permute-start.7 = (bf16[48,2048]{1,0:T(8,128)(2,1)S(1)}, bf16[48,2048]{1,0:T(8,128)(2,1)S(1)}, u32[]{:S(2)}, u32[]{:S(2)}) collective-permute-start(bf16[48,2048]{1,0:T(8,128)(2,1)S(1)} %get-tuple-element.23), channel_id=1, source_target_pairs={{0,6},{1,7},{2,4},{3,5},{4,2},{5,3},{6,0},{7,1},{8,14},{9,15},{10,... | collective-permute-start | bytes 589832 | tf_op jit(solution)/shard_map/ppermute | solution.py:17
  15.6 4.0 %load.1 = (bf16[1024,4096]{1,0:T(8,128)(2,1)S(1)}, f32[1,1024]{1,0:T(1,128)S(1)}) custom-call(bf16[1024,4096]{1,0:T(8,128)(2,1)} %refs_0_.6, bf16[48,2048]{1,0:T(8,128)(2,1)S(1)} %get-tuple-element.18.refs_1_.refs_0_), custom_call_target="tpu_custom_call" | custom-call | flops 10000000000 | bytes 16781312 | tf_op jit(solution)/shard_map/load/pallas_call | solution.py:36
  19.8 2.4 %collective-permute-done.6.refs_2_ = bf16[48,2048]{1,0:T(8,128)(2,1)S(1)} collective-permute-done((bf16[48,2048]{1,0:T(8,128)(2,1)S(1)}, bf16[48,2048]{1,0:T(8,128)(2,1)S(1)}, u32[]{:S(2)}, u32[]{:S(2)}) %collective-permute-start.6) | collective-permute-done | bytes 196640 | tf_op jit(solution)/shard_map/ppermute | solution.py:17
  22.2 1.6 %collective-permute-start.8 = (bf16[48,2048]{1,0:T(8,128)(2,1)S(1)}, bf16[48,2048]{1,0:T(8,128)(2,1)S(1)}, u32[]{:S(2)}, u32[]{:S(2)}) collective-permute-start(bf16[48,2048]{1,0:T(8,128)(2,1)S(1)} %get-tuple-element.24.refs_0_), channel_id=1, source_target_pairs={{0,2},{1,3},{2,0},{3,1},{4,6},{5,7},{6,4},{7,5},{8,10},{9,11},{10,... | collective-permute-start | bytes 589832 | tf_op jit(solution)/shard_map/ppermute | solution.py:17
  24.5 1.6 %collective-permute-start.12 = (bf16[32,2048]{1,0:T(8,128)(2,1)S(1)}, bf16[32,2048]{1,0:T(8,128)(2,1)S(1)}, u32[]{:S(2)}, u32[]{:S(2)}) collective-permute-start(bf16[32,2048]{1,0:T(8,128)(2,1)S(1)} %get-tuple-element.25), channel_id=1, source_target_pairs={{0,8},{8,16},{16,24},{24,0},{1,9},{9,17},{17,25},{25,1},{2,10},{10... | collective-permute-start | bytes 393224 | tf_op jit(solution)/shard_map/ppermute | solution.py:292
  26.1 2.6 %collective-permute-start.13 = (bf16[32,2048]{1,0:T(8,128)(2,1)S(1)}, bf16[32,2048]{1,0:T(8,128)(2,1)S(1)}, u32[]{:S(2)}, u32[]{:S(2)}) collective-permute-start(bf16[32,2048]{1,0:T(8,128)(2,1)S(1)} %get-tuple-element.25), channel_id=1, source_target_pairs={{0,16},{8,24},{16,0},{24,8},{1,17},{9,25},{17,1},{25,9},{2,18},{10... | collective-permute-start | bytes 393224 | tf_op jit(solution)/shard_map/ppermute | solution.py:292
  28.6 1.3 %collective-permute-start.14 = (bf16[32,2048]{1,0:T(8,128)(2,1)S(1)}, bf16[32,2048]{1,0:T(8,128)(2,1)S(1)}, u32[]{:S(2)}, u32[]{:S(2)}) collective-permute-start(bf16[32,2048]{1,0:T(8,128)(2,1)S(1)} %get-tuple-element.25), channel_id=1, source_target_pairs={{0,24},{8,0},{16,8},{24,16},{1,25},{9,1},{17,9},{25,17},{2,26},{10... | collective-permute-start | bytes 393224 | tf_op jit(solution)/shard_map/ppermute | solution.py:292
  30.0 1.4 %collective-permute-start.10 = (bf16[48,1024]{1,0:T(8,128)(2,1)S(1)}, bf16[48,1024]{1,0:T(8,128)(2,1)S(1)}, u32[]{:S(2)}, u32[]{:S(2)}) collective-permute-start(bf16[48,1024]{1,0:T(8,128)(2,1)S(1)} %stack.9), channel_id=1, source_target_pairs={{0,4},{1,5},{2,6},{3,7},{4,0},{5,1},{6,2},{7,3},{8,12},{9,13},{10,... | collective-permute-start | bytes 294920 | tf_op jit(solution)/shard_map/ppermute | solution.py:17
  32.0 3.9 %collective-permute-done.13.refs_1_ = bf16[32,2048]{1,0:T(8,128)(2,1)S(1)} collective-permute-done((bf16[32,2048]{1,0:T(8,128)(2,1)S(1)}, bf16[32,2048]{1,0:T(8,128)(2,1)S(1)}, u32[]{:S(2)}, u32[]{:S(2)}) %collective-permute-start.13) | collective-permute-done | bytes 131104 | tf_op jit(solution)/shard_map/ppermute | solution.py:292
  36.3 0.8 %collective-permute-start.16 = (bf16[96,1024]{1,0:T(8,128)(2,1)S(1)}, bf16[96,1024]{1,0:T(8,128)(2,1)S(1)}, u32[]{:S(2)}, u32[]{:S(2)}) collective-permute-start(bf16[96,1024]{1,0:T(8,128)(2,1)S(1)} %stack.11.refs_5_), channel_id=1, source_target_pairs={{0,2},{1,3},{2,0},{3,1},{4,6},{5,7},{6,4},{7,5},{8,10},{9,11},{10,... | collective-permute-start | bytes 589832 | tf_op jit(solution)/shard_map/ppermute | solution.py:17
  37.0 1.0 %collective-permute-start.19 = (bf16[96,1024]{1,0:T(8,128)(2,1)S(1)}, bf16[96,1024]{1,0:T(8,128)(2,1)S(1)}, u32[]{:S(2)}, u32[]{:S(2)}) collective-permute-start(bf16[96,1024]{1,0:T(8,128)(2,1)S(1)} %stack.12.refs_6_), channel_id=1, source_target_pairs={{0,4},{1,5},{2,6},{3,7},{4,0},{5,1},{6,2},{7,3},{8,12},{9,13},{10,... | collective-permute-start | bytes 589832 | tf_op jit(solution)/shard_map/ppermute | solution.py:17
  38.1 1.0 %collective-permute-start.17 = (bf16[96,1024]{1,0:T(8,128)(2,1)S(1)}, bf16[96,1024]{1,0:T(8,128)(2,1)S(1)}, u32[]{:S(2)}, u32[]{:S(2)}) collective-permute-start(bf16[96,1024]{1,0:T(8,128)(2,1)S(1)} %stack.12.refs_6_), channel_id=1, source_target_pairs={{0,2},{1,3},{2,0},{3,1},{4,6},{5,7},{6,4},{7,5},{8,10},{9,11},{10,... | collective-permute-start | bytes 589832 | tf_op jit(solution)/shard_map/ppermute | solution.py:17
  39.1 1.3 %collective-permute-start.21 = (bf16[96,1024]{1,0:T(8,128)(2,1)S(1)}, bf16[96,1024]{1,0:T(8,128)(2,1)S(1)}, u32[]{:S(2)}, u32[]{:S(2)}) collective-permute-start(bf16[96,1024]{1,0:T(8,128)(2,1)S(1)} %stack.11.refs_5_), channel_id=1, source_target_pairs={{0,4},{1,5},{2,6},{3,7},{4,0},{5,1},{6,2},{7,3},{8,12},{9,13},{10,... | collective-permute-start | bytes 589832 | tf_op jit(solution)/shard_map/ppermute | solution.py:17
  40.4 3.3 %products.1 = (f32[1,1024]{1,0:T(1,128)}, f32[1,1024]{1,0:T(1,128)S(1)}) custom-call(bf16[1024,4096]{1,0:T(8,128)(2,1)S(1)} %get-tuple-element.19.refs_0_, f32[1,1024]{1,0:T(1,128)S(1)} %get-tuple-element.20.refs_4_.refs_1_, bf16[288,2048]{1,0:T(8,128)(2,1)S(1)} %stack.13.refs_2_, bf16[288,2048]{1,0:T(8,128)(2,1)S(1)} %collective-permute-done.15.refs_3_), custom_call_target="tpu_custom_call" | custom-call | flops 1000000000 | bytes 10760192 | tf_op jit(solution)/shard_map/products/pallas_call | solution.py:36
  44.9 1.1 %collective-permute-start.24 = (bf16[112,1024]{1,0:T(8,128)(2,1)S(1)}, bf16[112,1024]{1,0:T(8,128)(2,1)S(1)}, u32[]{:S(2)}, u32[]{:S(2)}) collective-permute-start(bf16[112,1024]{1,0:T(8,128)(2,1)S(1)} %copy.11.refs_2_), channel_id=1, source_target_pairs={{0,4},{1,5},{2,6},{3,7},{4,0},{5,1},{6,2},{7,3},{8,12},{9,13},{10,... | collective-permute-start | bytes 688136 | tf_op jit(solution)/shard_map/ppermute | solution.py:17
  46.0 1.0 %collective-permute-start.25 = (bf16[112,1024]{1,0:T(8,128)(2,1)S(1)}, bf16[112,1024]{1,0:T(8,128)(2,1)S(1)}, u32[]{:S(2)}, u32[]{:S(2)}) collective-permute-start(bf16[112,1024]{1,0:T(8,128)(2,1)S(1)} %copy.12.refs_3_), channel_id=1, source_target_pairs={{0,2},{1,3},{2,0},{3,1},{4,6},{5,7},{6,4},{7,5},{8,10},{9,11},{10,... | collective-permute-start | bytes 688136 | tf_op jit(solution)/shard_map/ppermute | solution.py:17
  47.0 0.8 %collective-permute-done.17.refs_0_.refs_3_ = bf16[96,1024]{1,0:T(8,128)(2,1)S(1)} collective-permute-done((bf16[96,1024]{1,0:T(8,128)(2,1)S(1)}, bf16[96,1024]{1,0:T(8,128)(2,1)S(1)}, u32[]{:S(2)}, u32[]{:S(2)}) %collective-permute-start.17) | collective-permute-done | bytes 196640 | tf_op jit(solution)/shard_map/ppermute | solution.py:17
  49.0 4.2 %collective-permute-done.24.refs_10_.refs_0_ = bf16[112,1024]{1,0:T(8,128)(2,1)S(1)} collective-permute-done((bf16[112,1024]{1,0:T(8,128)(2,1)S(1)}, bf16[112,1024]{1,0:T(8,128)(2,1)S(1)}, u32[]{:S(2)}, u32[]{:S(2)}) %collective-permute-start.24) | collective-permute-done | bytes 229408 | tf_op jit(solution)/shard_map/ppermute | solution.py:17
  53.8 2.8 %products_next.1 = (f32[1,1024]{1,0:T(1,128)S(1)}, f32[96,1024]{1,0:T(8,128)S(1)}) custom-call(bf16[1024,4096]{1,0:T(8,128)(2,1)S(1)} %get-tuple-element.19.refs_0_, f32[1,1024]{1,0:T(1,128)S(1)} %get-tuple-element.27.refs_1_, bf16[96,1024]{1,0:T(8,128)(2,1)S(1)} %collective-permute-done.16.refs_0_.refs_2_, ...), custom_call_target="tpu_custom_call" | custom-call | flops 3333333248 | bytes 10821632 | tf_op jit(solution)/shard_map/products_next/pallas_call | solution.py:36
  56.7 2.0 %products_last.1 = f32[1,1024]{1,0:T(1,128)} custom-call(bf16[1024,4096]{1,0:T(8,128)(2,1)S(1)} %get-tuple-element.19.refs_0_, f32[1,1024]{1,0:T(1,128)S(1)} %get-tuple-element.20.refs_4_.refs_1_, f32[1,1024]{1,0:T(1,128)S(1)} %get-tuple-element.28.refs_2_, f32[96,1024]{1,0:T(8,128)S(1)} %get-tuple-element.29.refs_3_, ...), custom_call_target="tpu_custom_call" | custom-call | flops 10000000000 | bytes 9187328 | tf_op jit(solution)/shard_map/products_last/pallas_call | solution.py:36
  (58 shorter events, 7.8 us)
Async XLA Ops:
  2.4 9.1 %collective-permute-start.4 = (bf16[64,2048]{1,0:T(8,128)(2,1)S(1)}, bf16[64,2048]{1,0:T(8,128)(2,1)S(1)}, u32[]{:S(2)}, u32[]{:S(2)}) collective-permute-start(bf16[64,2048]{1,0:T(8,128)(2,1)S(1)} %get-tuple-element.17), channel_id=1, source_target_pairs={{0,1},{1,0},{2,3},{3,2},{4,5},{5,4},{6,7},{7,6},{8,9},{9,8},{10,11... | collective-permute-start | bytes 786440 | tf_op jit(solution)/shard_map/ppermute | solution.py:17
  2.9 4.2 %collective-permute-start.1 = (s32[8,128]{1,0:T(8,128)S(1)}, s32[8,128]{1,0:T(8,128)S(1)}, u32[]{:S(2)}, u32[]{:S(2)}) collective-permute-start(s32[8,128]{1,0:T(8,128)S(1)} %pair.1.refs_1_), channel_id=1, source_target_pairs={{0,2},{1,3},{2,0},{3,1},{4,6},{5,7},{6,4},{7,5},{8,10},{9,11},{10,... | collective-permute-start | bytes 12296 | tf_op jit(solution)/shard_map/ppermute | solution.py:17
  5.5 3.6 %collective-permute-start.2 = (s32[8,128]{1,0:T(8,128)S(1)}, s32[8,128]{1,0:T(8,128)S(1)}, u32[]{:S(2)}, u32[]{:S(2)}) collective-permute-start(s32[8,128]{1,0:T(8,128)S(1)} %pair.1.refs_1_), channel_id=1, source_target_pairs={{0,4},{1,5},{2,6},{3,7},{4,0},{5,1},{6,2},{7,3},{8,12},{9,13},{10,... | collective-permute-start | bytes 12296 | tf_op jit(solution)/shard_map/ppermute | solution.py:17
  7.0 4.5 %collective-permute-start.3 = (s32[8,128]{1,0:T(8,128)S(1)}, s32[8,128]{1,0:T(8,128)S(1)}, u32[]{:S(2)}, u32[]{:S(2)}) collective-permute-start(s32[8,128]{1,0:T(8,128)S(1)} %pair.1.refs_1_), channel_id=1, source_target_pairs={{0,6},{1,7},{2,4},{3,5},{4,2},{5,3},{6,0},{7,1},{8,14},{9,15},{10,... | collective-permute-start | bytes 12296 | tf_op jit(solution)/shard_map/ppermute | solution.py:17
  12.1 7.7 %collective-permute-start.5 = (bf16[48,2048]{1,0:T(8,128)(2,1)S(1)}, bf16[48,2048]{1,0:T(8,128)(2,1)S(1)}, u32[]{:S(2)}, u32[]{:S(2)}) collective-permute-start(bf16[48,2048]{1,0:T(8,128)(2,1)S(1)} %get-tuple-element.21), channel_id=1, source_target_pairs={{0,2},{1,3},{2,0},{3,1},{4,6},{5,7},{6,4},{7,5},{8,10},{9,11},{10,... | collective-permute-start | bytes 589832 | tf_op jit(solution)/shard_map/ppermute | solution.py:17
  12.7 9.5 %collective-permute-start.6 = (bf16[48,2048]{1,0:T(8,128)(2,1)S(1)}, bf16[48,2048]{1,0:T(8,128)(2,1)S(1)}, u32[]{:S(2)}, u32[]{:S(2)}) collective-permute-start(bf16[48,2048]{1,0:T(8,128)(2,1)S(1)} %get-tuple-element.22), channel_id=1, source_target_pairs={{0,4},{1,5},{2,6},{3,7},{4,0},{5,1},{6,2},{7,3},{8,12},{9,13},{10,... | collective-permute-start | bytes 589832 | tf_op jit(solution)/shard_map/ppermute | solution.py:17
  12.7 9.4 %collective-permute-start.7 = (bf16[48,2048]{1,0:T(8,128)(2,1)S(1)}, bf16[48,2048]{1,0:T(8,128)(2,1)S(1)}, u32[]{:S(2)}, u32[]{:S(2)}) collective-permute-start(bf16[48,2048]{1,0:T(8,128)(2,1)S(1)} %get-tuple-element.23), channel_id=1, source_target_pairs={{0,6},{1,7},{2,4},{3,5},{4,2},{5,3},{6,0},{7,1},{8,14},{9,15},{10,... | collective-permute-start | bytes 589832 | tf_op jit(solution)/shard_map/ppermute | solution.py:17
  22.2 7.8 %collective-permute-start.8 = (bf16[48,2048]{1,0:T(8,128)(2,1)S(1)}, bf16[48,2048]{1,0:T(8,128)(2,1)S(1)}, u32[]{:S(2)}, u32[]{:S(2)}) collective-permute-start(bf16[48,2048]{1,0:T(8,128)(2,1)S(1)} %get-tuple-element.24.refs_0_), channel_id=1, source_target_pairs={{0,2},{1,3},{2,0},{3,1},{4,6},{5,7},{6,4},{7,5},{8,10},{9,11},{10,... | collective-permute-start | bytes 589832 | tf_op jit(solution)/shard_map/ppermute | solution.py:17
  23.7 7.6 %collective-permute-start.9 = (bf16[48,2048]{1,0:T(8,128)(2,1)S(1)}, bf16[48,2048]{1,0:T(8,128)(2,1)S(1)}, u32[]{:S(2)}, u32[]{:S(2)}) collective-permute-start(bf16[48,2048]{1,0:T(8,128)(2,1)S(1)} %get-tuple-element.24.refs_0_), channel_id=1, source_target_pairs={{0,4},{1,5},{2,6},{3,7},{4,0},{5,1},{6,2},{7,3},{8,12},{9,13},{10,... | collective-permute-start | bytes 589832 | tf_op jit(solution)/shard_map/ppermute | solution.py:17
  24.5 7.5 %collective-permute-start.12 = (bf16[32,2048]{1,0:T(8,128)(2,1)S(1)}, bf16[32,2048]{1,0:T(8,128)(2,1)S(1)}, u32[]{:S(2)}, u32[]{:S(2)}) collective-permute-start(bf16[32,2048]{1,0:T(8,128)(2,1)S(1)} %get-tuple-element.25), channel_id=1, source_target_pairs={{0,8},{8,16},{16,24},{24,0},{1,9},{9,17},{17,25},{25,1},{2,10},{10... | collective-permute-start | bytes 393224 | tf_op jit(solution)/shard_map/ppermute | solution.py:292
  26.1 9.8 %collective-permute-start.13 = (bf16[32,2048]{1,0:T(8,128)(2,1)S(1)}, bf16[32,2048]{1,0:T(8,128)(2,1)S(1)}, u32[]{:S(2)}, u32[]{:S(2)}) collective-permute-start(bf16[32,2048]{1,0:T(8,128)(2,1)S(1)} %get-tuple-element.25), channel_id=1, source_target_pairs={{0,16},{8,24},{16,0},{24,8},{1,17},{9,25},{17,1},{25,9},{2,18},{10... | collective-permute-start | bytes 393224 | tf_op jit(solution)/shard_map/ppermute | solution.py:292
  28.6 7.2 %collective-permute-start.14 = (bf16[32,2048]{1,0:T(8,128)(2,1)S(1)}, bf16[32,2048]{1,0:T(8,128)(2,1)S(1)}, u32[]{:S(2)}, u32[]{:S(2)}) collective-permute-start(bf16[32,2048]{1,0:T(8,128)(2,1)S(1)} %get-tuple-element.25), channel_id=1, source_target_pairs={{0,24},{8,0},{16,8},{24,16},{1,25},{9,1},{17,9},{25,17},{2,26},{10... | collective-permute-start | bytes 393224 | tf_op jit(solution)/shard_map/ppermute | solution.py:292
  30.0 5.9 %collective-permute-start.10 = (bf16[48,1024]{1,0:T(8,128)(2,1)S(1)}, bf16[48,1024]{1,0:T(8,128)(2,1)S(1)}, u32[]{:S(2)}, u32[]{:S(2)}) collective-permute-start(bf16[48,1024]{1,0:T(8,128)(2,1)S(1)} %stack.9), channel_id=1, source_target_pairs={{0,4},{1,5},{2,6},{3,7},{4,0},{5,1},{6,2},{7,3},{8,12},{9,13},{10,... | collective-permute-start | bytes 294920 | tf_op jit(solution)/shard_map/ppermute | solution.py:17
  31.4 4.7 %collective-permute-start.11 = (bf16[48,1024]{1,0:T(8,128)(2,1)S(1)}, bf16[48,1024]{1,0:T(8,128)(2,1)S(1)}, u32[]{:S(2)}, u32[]{:S(2)}) collective-permute-start(bf16[48,1024]{1,0:T(8,128)(2,1)S(1)} %stack.10), channel_id=1, source_target_pairs={{0,2},{1,3},{2,0},{3,1},{4,6},{5,7},{6,4},{7,5},{8,10},{9,11},{10,... | collective-permute-start | bytes 294920 | tf_op jit(solution)/shard_map/ppermute | solution.py:17
  36.2 4.2 %collective-permute-start.15 = (bf16[288,2048]{1,0:T(8,128)(2,1)S(1)}, bf16[288,2048]{1,0:T(8,128)(2,1)S(1)}, u32[]{:S(2)}, u32[]{:S(2)}) collective-permute-start(bf16[288,2048]{1,0:T(8,128)(2,1)S(1)} %stack.13.refs_2_), channel_id=1, source_target_pairs={{0,1},{1,0},{2,3},{3,2},{4,5},{5,4},{6,7},{7,6},{8,9},{9,8},{10,11... | collective-permute-start | bytes 3538952 | tf_op jit(solution)/shard_map/ppermute | solution.py:17
  36.3 7.8 %collective-permute-start.16 = (bf16[96,1024]{1,0:T(8,128)(2,1)S(1)}, bf16[96,1024]{1,0:T(8,128)(2,1)S(1)}, u32[]{:S(2)}, u32[]{:S(2)}) collective-permute-start(bf16[96,1024]{1,0:T(8,128)(2,1)S(1)} %stack.11.refs_5_), channel_id=1, source_target_pairs={{0,2},{1,3},{2,0},{3,1},{4,6},{5,7},{6,4},{7,5},{8,10},{9,11},{10,... | collective-permute-start | bytes 589832 | tf_op jit(solution)/shard_map/ppermute | solution.py:17
  37.0 7.7 %collective-permute-start.19 = (bf16[96,1024]{1,0:T(8,128)(2,1)S(1)}, bf16[96,1024]{1,0:T(8,128)(2,1)S(1)}, u32[]{:S(2)}, u32[]{:S(2)}) collective-permute-start(bf16[96,1024]{1,0:T(8,128)(2,1)S(1)} %stack.12.refs_6_), channel_id=1, source_target_pairs={{0,4},{1,5},{2,6},{3,7},{4,0},{5,1},{6,2},{7,3},{8,12},{9,13},{10,... | collective-permute-start | bytes 589832 | tf_op jit(solution)/shard_map/ppermute | solution.py:17
  38.1 9.7 %collective-permute-start.17 = (bf16[96,1024]{1,0:T(8,128)(2,1)S(1)}, bf16[96,1024]{1,0:T(8,128)(2,1)S(1)}, u32[]{:S(2)}, u32[]{:S(2)}) collective-permute-start(bf16[96,1024]{1,0:T(8,128)(2,1)S(1)} %stack.12.refs_6_), channel_id=1, source_target_pairs={{0,2},{1,3},{2,0},{3,1},{4,6},{5,7},{6,4},{7,5},{8,10},{9,11},{10,... | collective-permute-start | bytes 589832 | tf_op jit(solution)/shard_map/ppermute | solution.py:17
  39.1 9.3 %collective-permute-start.21 = (bf16[96,1024]{1,0:T(8,128)(2,1)S(1)}, bf16[96,1024]{1,0:T(8,128)(2,1)S(1)}, u32[]{:S(2)}, u32[]{:S(2)}) collective-permute-start(bf16[96,1024]{1,0:T(8,128)(2,1)S(1)} %stack.11.refs_5_), channel_id=1, source_target_pairs={{0,4},{1,5},{2,6},{3,7},{4,0},{5,1},{6,2},{7,3},{8,12},{9,13},{10,... | collective-permute-start | bytes 589832 | tf_op jit(solution)/shard_map/ppermute | solution.py:17
  44.9 8.2 %collective-permute-start.24 = (bf16[112,1024]{1,0:T(8,128)(2,1)S(1)}, bf16[112,1024]{1,0:T(8,128)(2,1)S(1)}, u32[]{:S(2)}, u32[]{:S(2)}) collective-permute-start(bf16[112,1024]{1,0:T(8,128)(2,1)S(1)} %copy.11.refs_2_), channel_id=1, source_target_pairs={{0,4},{1,5},{2,6},{3,7},{4,0},{5,1},{6,2},{7,3},{8,12},{9,13},{10,... | collective-permute-start | bytes 688136 | tf_op jit(solution)/shard_map/ppermute | solution.py:17
  46.0 7.7 %collective-permute-start.25 = (bf16[112,1024]{1,0:T(8,128)(2,1)S(1)}, bf16[112,1024]{1,0:T(8,128)(2,1)S(1)}, u32[]{:S(2)}, u32[]{:S(2)}) collective-permute-start(bf16[112,1024]{1,0:T(8,128)(2,1)S(1)} %copy.12.refs_3_), channel_id=1, source_target_pairs={{0,2},{1,3},{2,0},{3,1},{4,6},{5,7},{6,4},{7,5},{8,10},{9,11},{10,... | collective-permute-start | bytes 688136 | tf_op jit(solution)/shard_map/ppermute | solution.py:17
  47.8 6.0 %collective-permute-start.18 = (bf16[96,1024]{1,0:T(8,128)(2,1)S(1)}, bf16[96,1024]{1,0:T(8,128)(2,1)S(1)}, u32[]{:S(2)}, u32[]{:S(2)}) collective-permute-start(bf16[96,1024]{1,0:T(8,128)(2,1)S(1)} %stack.14), channel_id=1, source_target_pairs={{0,1},{1,0},{2,3},{3,2},{4,5},{5,4},{6,7},{7,6},{8,9},{9,8},{10,11... | collective-permute-start | bytes 589832 | tf_op jit(solution)/shard_map/ppermute | solution.py:17
  48.4 5.5 %collective-permute-start.20 = (bf16[96,1024]{1,0:T(8,128)(2,1)S(1)}, bf16[96,1024]{1,0:T(8,128)(2,1)S(1)}, u32[]{:S(2)}, u32[]{:S(2)}) collective-permute-start(bf16[96,1024]{1,0:T(8,128)(2,1)S(1)} %stack.15), channel_id=1, source_target_pairs={{0,1},{1,0},{2,3},{3,2},{4,5},{5,4},{6,7},{7,6},{8,9},{9,8},{10,11... | collective-permute-start | bytes 589832 | tf_op jit(solution)/shard_map/ppermute | solution.py:17
  48.4 5.4 %collective-permute-start.22 = (bf16[96,1024]{1,0:T(8,128)(2,1)S(1)}, bf16[96,1024]{1,0:T(8,128)(2,1)S(1)}, u32[]{:S(2)}, u32[]{:S(2)}) collective-permute-start(bf16[96,1024]{1,0:T(8,128)(2,1)S(1)} %stack.16), channel_id=1, source_target_pairs={{0,1},{1,0},{2,3},{3,2},{4,5},{5,4},{6,7},{7,6},{8,9},{9,8},{10,11... | collective-permute-start | bytes 589832 | tf_op jit(solution)/shard_map/ppermute | solution.py:17
  (6 other events, 21.8 us)

commit v17 on v15

--- a/solution.py
+++ b/solution.py
@@ -325,7 +325,7 @@
     for block in others:
         operands += block
         for b in block:
-            after = (best, *handed) if chips == 4 and b is not low_x else (best,)
+            after = (best, *handed)
             operands.append(flip_permute(stack([b], after=after), size, 1))
     best = call(
         functools.partial(next_kernel, len(others)), "products_next", line, (cand, best, *operands),

time: 59.5 us -> 57.5 us (0.966)
  waiting for transfers between devices: 17.1 us -> 14.7 us
    ppermute x25, waiting for transfers between devices: 13.2 us -> 10.7 us  [flip_permute(): return lax.ppermute(block, 'mem', [(m, m ^ flip) for m in range(size)])]
  transfers between devices with their start and end apart: 28 -> 28, of which waited for: 12 -> 14; matrix products, arithmetic and copies ran while one was open for 0% -> 0% of each run, Pallas kernels for 20% -> 21%
where the time goes in v17:
time: 57.5 us; the launch traced here: 57.3 us
  starting transfers between devices  26.1 us (45%)
  waiting for transfers between devices  14.7 us (26%)
  Pallas kernels  14.6 us (25%)
  between operations  1.48 us (3%)
    ppermute x25, starting transfers between devices, flip_permute(): return lax.ppermute(block, 'mem', [(m, m ^ flip) for m in range(size)])  20.6 us
    pallas_call x23, Pallas kernels, call(): pl.pallas_call(run, out_shape=out_shape, in_specs=(specs or vmem_specs(co...  14.6 us
    ppermute x25, waiting for transfers between devices, flip_permute(): return lax.ppermute(block, 'mem', [(m, m ^ flip) for m in range(size)])  10.7 us
    ppermute x3, starting transfers between devices, body(): lax.ppermute(picked, 'grp', [(g, (g + k) % groups) for g in range(groups)])  5.51 us
    ppermute x3, waiting for transfers between devices, body(): lax.ppermute(picked, 'grp', [(g, (g + k) % groups) for g in range(groups)])  3.91 us
  transfers between devices with their start and end apart: 28, of which 14 were waited for; matrix products, arithmetic and copies ran while one was open for 0% of the time, Pallas kernels for 21%

profile of v17, /device:TPU:0, one launch (start us, length us, event | category | flops | bytes accessed | tf_op | source)
XLA Modules:
  0.0 57.3 jit_solution(6521884674226910255)
XLA Ops:
  2.9 2.6 %collective-permute-start.1 = (s32[8,128]{1,0:T(8,128)S(1)}, s32[8,128]{1,0:T(8,128)S(1)}, u32[]{:S(2)}, u32[]{:S(2)}) collective-permute-start(s32[8,128]{1,0:T(8,128)S(1)} %pair.1.refs_1_), channel_id=1, source_target_pairs={{0,2},{1,3},{2,0},{3,1},{4,6},{5,7},{6,4},{7,5},{8,10},{9,11},{10,... | collective-permute-start | bytes 12296 | tf_op jit(solution)/shard_map/ppermute | solution.py:17
  5.5 1.5 %collective-permute-start.2 = (s32[8,128]{1,0:T(8,128)S(1)}, s32[8,128]{1,0:T(8,128)S(1)}, u32[]{:S(2)}, u32[]{:S(2)}) collective-permute-start(s32[8,128]{1,0:T(8,128)S(1)} %pair.1.refs_1_), channel_id=1, source_target_pairs={{0,4},{1,5},{2,6},{3,7},{4,0},{5,1},{6,2},{7,3},{8,12},{9,13},{10,... | collective-permute-start | bytes 12296 | tf_op jit(solution)/shard_map/ppermute | solution.py:17
  7.1 2.0 %collective-permute-done.2.refs_3_ = s32[8,128]{1,0:T(8,128)S(1)} collective-permute-done((s32[8,128]{1,0:T(8,128)S(1)}, s32[8,128]{1,0:T(8,128)S(1)}, u32[]{:S(2)}, u32[]{:S(2)}) %collective-permute-start.2) | collective-permute-done | bytes 4128 | tf_op jit(solution)/shard_map/ppermute | solution.py:17
  9.1 2.4 %collective-permute-done.3.refs_4_ = s32[8,128]{1,0:T(8,128)S(1)} collective-permute-done((s32[8,128]{1,0:T(8,128)S(1)}, s32[8,128]{1,0:T(8,128)S(1)}, u32[]{:S(2)}, u32[]{:S(2)}) %collective-permute-start.3) | collective-permute-done | bytes 4128 | tf_op jit(solution)/shard_map/ppermute | solution.py:17
  12.7 2.9 %collective-permute-start.7 = (bf16[48,2048]{1,0:T(8,128)(2,1)S(1)}, bf16[48,2048]{1,0:T(8,128)(2,1)S(1)}, u32[]{:S(2)}, u32[]{:S(2)}) collective-permute-start(bf16[48,2048]{1,0:T(8,128)(2,1)S(1)} %get-tuple-element.21), channel_id=1, source_target_pairs={{0,6},{1,7},{2,4},{3,5},{4,2},{5,3},{6,0},{7,1},{8,14},{9,15},{10,... | collective-permute-start | bytes 589832 | tf_op jit(solution)/shard_map/ppermute | solution.py:17
  15.6 4.0 %load.1 = (bf16[1024,4096]{1,0:T(8,128)(2,1)S(1)}, f32[1,1024]{1,0:T(1,128)S(1)}) custom-call(bf16[1024,4096]{1,0:T(8,128)(2,1)} %refs_0_.6, bf16[48,2048]{1,0:T(8,128)(2,1)S(1)} %get-tuple-element.16.refs_1_.refs_0_), custom_call_target="tpu_custom_call" | custom-call | flops 10000000000 | bytes 16781312 | tf_op jit(solution)/shard_map/load/pallas_call | solution.py:36
  19.8 2.4 %collective-permute-done.6.refs_2_ = bf16[48,2048]{1,0:T(8,128)(2,1)S(1)} collective-permute-done((bf16[48,2048]{1,0:T(8,128)(2,1)S(1)}, bf16[48,2048]{1,0:T(8,128)(2,1)S(1)}, u32[]{:S(2)}, u32[]{:S(2)}) %collective-permute-start.6) | collective-permute-done | bytes 196640 | tf_op jit(solution)/shard_map/ppermute | solution.py:17
  22.2 1.6 %collective-permute-start.8 = (bf16[48,2048]{1,0:T(8,128)(2,1)S(1)}, bf16[48,2048]{1,0:T(8,128)(2,1)S(1)}, u32[]{:S(2)}, u32[]{:S(2)}) collective-permute-start(bf16[48,2048]{1,0:T(8,128)(2,1)S(1)} %get-tuple-element.22.refs_0_), channel_id=1, source_target_pairs={{0,2},{1,3},{2,0},{3,1},{4,6},{5,7},{6,4},{7,5},{8,10},{9,11},{10,... | collective-permute-start | bytes 589832 | tf_op jit(solution)/shard_map/ppermute | solution.py:17
  24.5 1.6 %collective-permute-start.12 = (bf16[32,2048]{1,0:T(8,128)(2,1)S(1)}, bf16[32,2048]{1,0:T(8,128)(2,1)S(1)}, u32[]{:S(2)}, u32[]{:S(2)}) collective-permute-start(bf16[32,2048]{1,0:T(8,128)(2,1)S(1)} %get-tuple-element.23), channel_id=1, source_target_pairs={{0,8},{8,16},{16,24},{24,0},{1,9},{9,17},{17,25},{25,1},{2,10},{10... | collective-permute-start | bytes 393224 | tf_op jit(solution)/shard_map/ppermute | solution.py:291
  26.1 2.6 %collective-permute-start.13 = (bf16[32,2048]{1,0:T(8,128)(2,1)S(1)}, bf16[32,2048]{1,0:T(8,128)(2,1)S(1)}, u32[]{:S(2)}, u32[]{:S(2)}) collective-permute-start(bf16[32,2048]{1,0:T(8,128)(2,1)S(1)} %get-tuple-element.23), channel_id=1, source_target_pairs={{0,16},{8,24},{16,0},{24,8},{1,17},{9,25},{17,1},{25,9},{2,18},{10... | collective-permute-start | bytes 393224 | tf_op jit(solution)/shard_map/ppermute | solution.py:291
  28.6 1.3 %collective-permute-start.14 = (bf16[32,2048]{1,0:T(8,128)(2,1)S(1)}, bf16[32,2048]{1,0:T(8,128)(2,1)S(1)}, u32[]{:S(2)}, u32[]{:S(2)}) collective-permute-start(bf16[32,2048]{1,0:T(8,128)(2,1)S(1)} %get-tuple-element.23), channel_id=1, source_target_pairs={{0,24},{8,0},{16,8},{24,16},{1,25},{9,1},{17,9},{25,17},{2,26},{10... | collective-permute-start | bytes 393224 | tf_op jit(solution)/shard_map/ppermute | solution.py:291
  30.0 1.4 %collective-permute-start.10 = (bf16[48,1024]{1,0:T(8,128)(2,1)S(1)}, bf16[48,1024]{1,0:T(8,128)(2,1)S(1)}, u32[]{:S(2)}, u32[]{:S(2)}) collective-permute-start(bf16[48,1024]{1,0:T(8,128)(2,1)S(1)} %stack.9), channel_id=1, source_target_pairs={{0,4},{1,5},{2,6},{3,7},{4,0},{5,1},{6,2},{7,3},{8,12},{9,13},{10,... | collective-permute-start | bytes 294920 | tf_op jit(solution)/shard_map/ppermute | solution.py:17
  32.0 3.9 %collective-permute-done.13.refs_1_ = bf16[32,2048]{1,0:T(8,128)(2,1)S(1)} collective-permute-done((bf16[32,2048]{1,0:T(8,128)(2,1)S(1)}, bf16[32,2048]{1,0:T(8,128)(2,1)S(1)}, u32[]{:S(2)}, u32[]{:S(2)}) %collective-permute-start.13) | collective-permute-done | bytes 131104 | tf_op jit(solution)/shard_map/ppermute | solution.py:291
  36.3 0.8 %collective-permute-start.16 = (bf16[96,1024]{1,0:T(8,128)(2,1)S(1)}, bf16[96,1024]{1,0:T(8,128)(2,1)S(1)}, u32[]{:S(2)}, u32[]{:S(2)}) collective-permute-start(bf16[96,1024]{1,0:T(8,128)(2,1)S(1)} %stack.11.refs_5_), channel_id=1, source_target_pairs={{0,2},{1,3},{2,0},{3,1},{4,6},{5,7},{6,4},{7,5},{8,10},{9,11},{10,... | collective-permute-start | bytes 589832 | tf_op jit(solution)/shard_map/ppermute | solution.py:17
  37.0 1.0 %collective-permute-start.18 = (bf16[96,1024]{1,0:T(8,128)(2,1)S(1)}, bf16[96,1024]{1,0:T(8,128)(2,1)S(1)}, u32[]{:S(2)}, u32[]{:S(2)}) collective-permute-start(bf16[96,1024]{1,0:T(8,128)(2,1)S(1)} %stack.12.refs_6_), channel_id=1, source_target_pairs={{0,4},{1,5},{2,6},{3,7},{4,0},{5,1},{6,2},{7,3},{8,12},{9,13},{10,... | collective-permute-start | bytes 589832 | tf_op jit(solution)/shard_map/ppermute | solution.py:17
  38.1 1.0 %collective-permute-start.17 = (bf16[96,1024]{1,0:T(8,128)(2,1)S(1)}, bf16[96,1024]{1,0:T(8,128)(2,1)S(1)}, u32[]{:S(2)}, u32[]{:S(2)}) collective-permute-start(bf16[96,1024]{1,0:T(8,128)(2,1)S(1)} %stack.12.refs_6_), channel_id=1, source_target_pairs={{0,2},{1,3},{2,0},{3,1},{4,6},{5,7},{6,4},{7,5},{8,10},{9,11},{10,... | collective-permute-start | bytes 589832 | tf_op jit(solution)/shard_map/ppermute | solution.py:17
  39.1 1.3 %collective-permute-start.21 = (bf16[96,1024]{1,0:T(8,128)(2,1)S(1)}, bf16[96,1024]{1,0:T(8,128)(2,1)S(1)}, u32[]{:S(2)}, u32[]{:S(2)}) collective-permute-start(bf16[96,1024]{1,0:T(8,128)(2,1)S(1)} %stack.11.refs_5_), channel_id=1, source_target_pairs={{0,4},{1,5},{2,6},{3,7},{4,0},{5,1},{6,2},{7,3},{8,12},{9,13},{10,... | collective-permute-start | bytes 589832 | tf_op jit(solution)/shard_map/ppermute | solution.py:17
  40.4 3.3 %products.1 = (f32[1,1024]{1,0:T(1,128)}, f32[1,1024]{1,0:T(1,128)S(1)}) custom-call(bf16[1024,4096]{1,0:T(8,128)(2,1)S(1)} %get-tuple-element.17.refs_0_, f32[1,1024]{1,0:T(1,128)S(1)} %get-tuple-element.18.refs_4_.refs_1_, bf16[288,2048]{1,0:T(8,128)(2,1)S(1)} %stack.13.refs_2_, bf16[288,2048]{1,0:T(8,128)(2,1)S(1)} %collective-permute-done.15.refs_3_), custom_call_target="tpu_custom_call" | custom-call | flops 1000000000 | bytes 10760192 | tf_op jit(solution)/shard_map/products/pallas_call | solution.py:36
  44.9 1.1 %collective-permute-start.24 = (bf16[112,1024]{1,0:T(8,128)(2,1)S(1)}, bf16[112,1024]{1,0:T(8,128)(2,1)S(1)}, u32[]{:S(2)}, u32[]{:S(2)}) collective-permute-start(bf16[112,1024]{1,0:T(8,128)(2,1)S(1)} %copy.11.refs_2_), channel_id=1, source_target_pairs={{0,4},{1,5},{2,6},{3,7},{4,0},{5,1},{6,2},{7,3},{8,12},{9,13},{10,... | collective-permute-start | bytes 688136 | tf_op jit(solution)/shard_map/ppermute | solution.py:17
  46.0 1.0 %collective-permute-start.25 = (bf16[112,1024]{1,0:T(8,128)(2,1)S(1)}, bf16[112,1024]{1,0:T(8,128)(2,1)S(1)}, u32[]{:S(2)}, u32[]{:S(2)}) collective-permute-start(bf16[112,1024]{1,0:T(8,128)(2,1)S(1)} %copy.12.refs_3_), channel_id=1, source_target_pairs={{0,2},{1,3},{2,0},{3,1},{4,6},{5,7},{6,4},{7,5},{8,10},{9,11},{10,... | collective-permute-start | bytes 688136 | tf_op jit(solution)/shard_map/ppermute | solution.py:17
  47.0 0.8 %collective-permute-done.17.refs_0_.refs_3_ = bf16[96,1024]{1,0:T(8,128)(2,1)S(1)} collective-permute-done((bf16[96,1024]{1,0:T(8,128)(2,1)S(1)}, bf16[96,1024]{1,0:T(8,128)(2,1)S(1)}, u32[]{:S(2)}, u32[]{:S(2)}) %collective-permute-start.17) | collective-permute-done | bytes 196640 | tf_op jit(solution)/shard_map/ppermute | solution.py:17
  50.2 3.0 %products_next.1.refs_3_.refs_1_.refs_2_ = f32[1,1024]{1,0:T(1,128)S(1)} custom-call(bf16[1024,4096]{1,0:T(8,128)(2,1)S(1)} %get-tuple-element.17.refs_0_, f32[1,1024]{1,0:T(1,128)S(1)} %get-tuple-element.25.refs_1_, bf16[96,1024]{1,0:T(8,128)(2,1)S(1)} %collective-permute-done.16.refs_0_.refs_2_, ...), custom_call_target="tpu_custom_call" | custom-call | bytes 9969664 | tf_op jit(solution)/shard_map/products_next/pallas_call | solution.py:36
  53.8 1.4 %products_half.1.refs_3_ = f32[96,1024]{1,0:T(8,128)S(1)} custom-call(bf16[1024,4096]{1,0:T(8,128)(2,1)S(1)} %get-tuple-element.17.refs_0_, bf16[112,1024]{1,0:T(8,128)(2,1)S(1)} %collective-permute-done.24.refs_1_.refs_0_, bf16[112,1024]{1,0:T(8,128)(2,1)S(1)} %collective-permute-done.25.refs_2_.refs_0_, f32[1,1024]{1,0:T(1,128)S(1)} %products_next.1.refs_3_.refs_1_.refs_2_), custom_call_target="tpu_custom_call" | custom-call | flops 10000000000 | bytes 9240576 | tf_op jit(solution)/shard_map/products_half/pallas_call | solution.py:36
  55.3 2.0 %products_last.1 = f32[1,1024]{1,0:T(1,128)} custom-call(bf16[1024,4096]{1,0:T(8,128)(2,1)S(1)} %get-tuple-element.17.refs_0_, f32[1,1024]{1,0:T(1,128)S(1)} %get-tuple-element.18.refs_4_.refs_1_, f32[1,1024]{1,0:T(1,128)S(1)} %products_next.1.refs_3_.refs_1_.refs_2_, f32[96,1024]{1,0:T(8,128)S(1)} %products_half.1.refs_3_, ...), custom_call_target="tpu_custom_call" | custom-call | flops 10000000000 | bytes 9187328 | tf_op jit(solution)/shard_map/products_last/pallas_call | solution.py:36
  (59 shorter events, 9.0 us)
Async XLA Ops:
  2.4 9.1 %collective-permute-start.4 = (bf16[64,2048]{1,0:T(8,128)(2,1)S(1)}, bf16[64,2048]{1,0:T(8,128)(2,1)S(1)}, u32[]{:S(2)}, u32[]{:S(2)}) collective-permute-start(bf16[64,2048]{1,0:T(8,128)(2,1)S(1)} %get-tuple-element.15), channel_id=1, source_target_pairs={{0,1},{1,0},{2,3},{3,2},{4,5},{5,4},{6,7},{7,6},{8,9},{9,8},{10,11... | collective-permute-start | bytes 786440 | tf_op jit(solution)/shard_map/ppermute | solution.py:17
  2.9 4.2 %collective-permute-start.1 = (s32[8,128]{1,0:T(8,128)S(1)}, s32[8,128]{1,0:T(8,128)S(1)}, u32[]{:S(2)}, u32[]{:S(2)}) collective-permute-start(s32[8,128]{1,0:T(8,128)S(1)} %pair.1.refs_1_), channel_id=1, source_target_pairs={{0,2},{1,3},{2,0},{3,1},{4,6},{5,7},{6,4},{7,5},{8,10},{9,11},{10,... | collective-permute-start | bytes 12296 | tf_op jit(solution)/shard_map/ppermute | solution.py:17
  5.5 3.6 %collective-permute-start.2 = (s32[8,128]{1,0:T(8,128)S(1)}, s32[8,128]{1,0:T(8,128)S(1)}, u32[]{:S(2)}, u32[]{:S(2)}) collective-permute-start(s32[8,128]{1,0:T(8,128)S(1)} %pair.1.refs_1_), channel_id=1, source_target_pairs={{0,4},{1,5},{2,6},{3,7},{4,0},{5,1},{6,2},{7,3},{8,12},{9,13},{10,... | collective-permute-start | bytes 12296 | tf_op jit(solution)/shard_map/ppermute | solution.py:17
  7.0 4.5 %collective-permute-start.3 = (s32[8,128]{1,0:T(8,128)S(1)}, s32[8,128]{1,0:T(8,128)S(1)}, u32[]{:S(2)}, u32[]{:S(2)}) collective-permute-start(s32[8,128]{1,0:T(8,128)S(1)} %pair.1.refs_1_), channel_id=1, source_target_pairs={{0,6},{1,7},{2,4},{3,5},{4,2},{5,3},{6,0},{7,1},{8,14},{9,15},{10,... | collective-permute-start | bytes 12296 | tf_op jit(solution)/shard_map/ppermute | solution.py:17
  12.1 7.7 %collective-permute-start.5 = (bf16[48,2048]{1,0:T(8,128)(2,1)S(1)}, bf16[48,2048]{1,0:T(8,128)(2,1)S(1)}, u32[]{:S(2)}, u32[]{:S(2)}) collective-permute-start(bf16[48,2048]{1,0:T(8,128)(2,1)S(1)} %get-tuple-element.19), channel_id=1, source_target_pairs={{0,2},{1,3},{2,0},{3,1},{4,6},{5,7},{6,4},{7,5},{8,10},{9,11},{10,... | collective-permute-start | bytes 589832 | tf_op jit(solution)/shard_map/ppermute | solution.py:17
  12.7 9.5 %collective-permute-start.6 = (bf16[48,2048]{1,0:T(8,128)(2,1)S(1)}, bf16[48,2048]{1,0:T(8,128)(2,1)S(1)}, u32[]{:S(2)}, u32[]{:S(2)}) collective-permute-start(bf16[48,2048]{1,0:T(8,128)(2,1)S(1)} %get-tuple-element.20), channel_id=1, source_target_pairs={{0,4},{1,5},{2,6},{3,7},{4,0},{5,1},{6,2},{7,3},{8,12},{9,13},{10,... | collective-permute-start | bytes 589832 | tf_op jit(solution)/shard_map/ppermute | solution.py:17
  12.7 9.4 %collective-permute-start.7 = (bf16[48,2048]{1,0:T(8,128)(2,1)S(1)}, bf16[48,2048]{1,0:T(8,128)(2,1)S(1)}, u32[]{:S(2)}, u32[]{:S(2)}) collective-permute-start(bf16[48,2048]{1,0:T(8,128)(2,1)S(1)} %get-tuple-element.21), channel_id=1, source_target_pairs={{0,6},{1,7},{2,4},{3,5},{4,2},{5,3},{6,0},{7,1},{8,14},{9,15},{10,... | collective-permute-start | bytes 589832 | tf_op jit(solution)/shard_map/ppermute | solution.py:17
  22.2 7.8 %collective-permute-start.8 = (bf16[48,2048]{1,0:T(8,128)(2,1)S(1)}, bf16[48,2048]{1,0:T(8,128)(2,1)S(1)}, u32[]{:S(2)}, u32[]{:S(2)}) collective-permute-start(bf16[48,2048]{1,0:T(8,128)(2,1)S(1)} %get-tuple-element.22.refs_0_), channel_id=1, source_target_pairs={{0,2},{1,3},{2,0},{3,1},{4,6},{5,7},{6,4},{7,5},{8,10},{9,11},{10,... | collective-permute-start | bytes 589832 | tf_op jit(solution)/shard_map/ppermute | solution.py:17
  23.7 7.6 %collective-permute-start.9 = (bf16[48,2048]{1,0:T(8,128)(2,1)S(1)}, bf16[48,2048]{1,0:T(8,128)(2,1)S(1)}, u32[]{:S(2)}, u32[]{:S(2)}) collective-permute-start(bf16[48,2048]{1,0:T(8,128)(2,1)S(1)} %get-tuple-element.22.refs_0_), channel_id=1, source_target_pairs={{0,4},{1,5},{2,6},{3,7},{4,0},{5,1},{6,2},{7,3},{8,12},{9,13},{10,... | collective-permute-start | bytes 589832 | tf_op jit(solution)/shard_map/ppermute | solution.py:17
  24.5 7.5 %collective-permute-start.12 = (bf16[32,2048]{1,0:T(8,128)(2,1)S(1)}, bf16[32,2048]{1,0:T(8,128)(2,1)S(1)}, u32[]{:S(2)}, u32[]{:S(2)}) collective-permute-start(bf16[32,2048]{1,0:T(8,128)(2,1)S(1)} %get-tuple-element.23), channel_id=1, source_target_pairs={{0,8},{8,16},{16,24},{24,0},{1,9},{9,17},{17,25},{25,1},{2,10},{10... | collective-permute-start | bytes 393224 | tf_op jit(solution)/shard_map/ppermute | solution.py:291
  26.1 9.8 %collective-permute-start.13 = (bf16[32,2048]{1,0:T(8,128)(2,1)S(1)}, bf16[32,2048]{1,0:T(8,128)(2,1)S(1)}, u32[]{:S(2)}, u32[]{:S(2)}) collective-permute-start(bf16[32,2048]{1,0:T(8,128)(2,1)S(1)} %get-tuple-element.23), channel_id=1, source_target_pairs={{0,16},{8,24},{16,0},{24,8},{1,17},{9,25},{17,1},{25,9},{2,18},{10... | collective-permute-start | bytes 393224 | tf_op jit(solution)/shard_map/ppermute | solution.py:291
  28.6 7.2 %collective-permute-start.14 = (bf16[32,2048]{1,0:T(8,128)(2,1)S(1)}, bf16[32,2048]{1,0:T(8,128)(2,1)S(1)}, u32[]{:S(2)}, u32[]{:S(2)}) collective-permute-start(bf16[32,2048]{1,0:T(8,128)(2,1)S(1)} %get-tuple-element.23), channel_id=1, source_target_pairs={{0,24},{8,0},{16,8},{24,16},{1,25},{9,1},{17,9},{25,17},{2,26},{10... | collective-permute-start | bytes 393224 | tf_op jit(solution)/shard_map/ppermute | solution.py:291
  30.0 5.9 %collective-permute-start.10 = (bf16[48,1024]{1,0:T(8,128)(2,1)S(1)}, bf16[48,1024]{1,0:T(8,128)(2,1)S(1)}, u32[]{:S(2)}, u32[]{:S(2)}) collective-permute-start(bf16[48,1024]{1,0:T(8,128)(2,1)S(1)} %stack.9), channel_id=1, source_target_pairs={{0,4},{1,5},{2,6},{3,7},{4,0},{5,1},{6,2},{7,3},{8,12},{9,13},{10,... | collective-permute-start | bytes 294920 | tf_op jit(solution)/shard_map/ppermute | solution.py:17
  31.4 4.7 %collective-permute-start.11 = (bf16[48,1024]{1,0:T(8,128)(2,1)S(1)}, bf16[48,1024]{1,0:T(8,128)(2,1)S(1)}, u32[]{:S(2)}, u32[]{:S(2)}) collective-permute-start(bf16[48,1024]{1,0:T(8,128)(2,1)S(1)} %stack.10), channel_id=1, source_target_pairs={{0,2},{1,3},{2,0},{3,1},{4,6},{5,7},{6,4},{7,5},{8,10},{9,11},{10,... | collective-permute-start | bytes 294920 | tf_op jit(solution)/shard_map/ppermute | solution.py:17
  36.2 4.2 %collective-permute-start.15 = (bf16[288,2048]{1,0:T(8,128)(2,1)S(1)}, bf16[288,2048]{1,0:T(8,128)(2,1)S(1)}, u32[]{:S(2)}, u32[]{:S(2)}) collective-permute-start(bf16[288,2048]{1,0:T(8,128)(2,1)S(1)} %stack.13.refs_2_), channel_id=1, source_target_pairs={{0,1},{1,0},{2,3},{3,2},{4,5},{5,4},{6,7},{7,6},{8,9},{9,8},{10,11... | collective-permute-start | bytes 3538952 | tf_op jit(solution)/shard_map/ppermute | solution.py:17
  36.3 7.8 %collective-permute-start.16 = (bf16[96,1024]{1,0:T(8,128)(2,1)S(1)}, bf16[96,1024]{1,0:T(8,128)(2,1)S(1)}, u32[]{:S(2)}, u32[]{:S(2)}) collective-permute-start(bf16[96,1024]{1,0:T(8,128)(2,1)S(1)} %stack.11.refs_5_), channel_id=1, source_target_pairs={{0,2},{1,3},{2,0},{3,1},{4,6},{5,7},{6,4},{7,5},{8,10},{9,11},{10,... | collective-permute-start | bytes 589832 | tf_op jit(solution)/shard_map/ppermute | solution.py:17
  37.0 7.7 %collective-permute-start.18 = (bf16[96,1024]{1,0:T(8,128)(2,1)S(1)}, bf16[96,1024]{1,0:T(8,128)(2,1)S(1)}, u32[]{:S(2)}, u32[]{:S(2)}) collective-permute-start(bf16[96,1024]{1,0:T(8,128)(2,1)S(1)} %stack.12.refs_6_), channel_id=1, source_target_pairs={{0,4},{1,5},{2,6},{3,7},{4,0},{5,1},{6,2},{7,3},{8,12},{9,13},{10,... | collective-permute-start | bytes 589832 | tf_op jit(solution)/shard_map/ppermute | solution.py:17
  38.1 9.7 %collective-permute-start.17 = (bf16[96,1024]{1,0:T(8,128)(2,1)S(1)}, bf16[96,1024]{1,0:T(8,128)(2,1)S(1)}, u32[]{:S(2)}, u32[]{:S(2)}) collective-permute-start(bf16[96,1024]{1,0:T(8,128)(2,1)S(1)} %stack.12.refs_6_), channel_id=1, source_target_pairs={{0,2},{1,3},{2,0},{3,1},{4,6},{5,7},{6,4},{7,5},{8,10},{9,11},{10,... | collective-permute-start | bytes 589832 | tf_op jit(solution)/shard_map/ppermute | solution.py:17
  39.1 9.3 %collective-permute-start.21 = (bf16[96,1024]{1,0:T(8,128)(2,1)S(1)}, bf16[96,1024]{1,0:T(8,128)(2,1)S(1)}, u32[]{:S(2)}, u32[]{:S(2)}) collective-permute-start(bf16[96,1024]{1,0:T(8,128)(2,1)S(1)} %stack.11.refs_5_), channel_id=1, source_target_pairs={{0,4},{1,5},{2,6},{3,7},{4,0},{5,1},{6,2},{7,3},{8,12},{9,13},{10,... | collective-permute-start | bytes 589832 | tf_op jit(solution)/shard_map/ppermute | solution.py:17
  44.8 3.7 %collective-permute-start.19 = (bf16[96,1024]{1,0:T(8,128)(2,1)S(1)}, bf16[96,1024]{1,0:T(8,128)(2,1)S(1)}, u32[]{:S(2)}, u32[]{:S(2)}) collective-permute-start(bf16[96,1024]{1,0:T(8,128)(2,1)S(1)} %stack.14), channel_id=1, source_target_pairs={{0,1},{1,0},{2,3},{3,2},{4,5},{5,4},{6,7},{7,6},{8,9},{9,8},{10,11... | collective-permute-start | bytes 589832 | tf_op jit(solution)/shard_map/ppermute | solution.py:17
  44.9 8.2 %collective-permute-start.24 = (bf16[112,1024]{1,0:T(8,128)(2,1)S(1)}, bf16[112,1024]{1,0:T(8,128)(2,1)S(1)}, u32[]{:S(2)}, u32[]{:S(2)}) collective-permute-start(bf16[112,1024]{1,0:T(8,128)(2,1)S(1)} %copy.11.refs_2_), channel_id=1, source_target_pairs={{0,4},{1,5},{2,6},{3,7},{4,0},{5,1},{6,2},{7,3},{8,12},{9,13},{10,... | collective-permute-start | bytes 688136 | tf_op jit(solution)/shard_map/ppermute | solution.py:17
  46.0 7.7 %collective-permute-start.25 = (bf16[112,1024]{1,0:T(8,128)(2,1)S(1)}, bf16[112,1024]{1,0:T(8,128)(2,1)S(1)}, u32[]{:S(2)}, u32[]{:S(2)}) collective-permute-start(bf16[112,1024]{1,0:T(8,128)(2,1)S(1)} %copy.12.refs_3_), channel_id=1, source_target_pairs={{0,2},{1,3},{2,0},{3,1},{4,6},{5,7},{6,4},{7,5},{8,10},{9,11},{10,... | collective-permute-start | bytes 688136 | tf_op jit(solution)/shard_map/ppermute | solution.py:17
  48.5 1.7 %collective-permute-start.23 = (bf16[96,1024]{1,0:T(8,128)(2,1)S(1)}, bf16[96,1024]{1,0:T(8,128)(2,1)S(1)}, u32[]{:S(2)}, u32[]{:S(2)}) collective-permute-start(bf16[96,1024]{1,0:T(8,128)(2,1)S(1)} %stack.17), channel_id=1, source_target_pairs={{0,1},{1,0},{2,3},{3,2},{4,5},{5,4},{6,7},{7,6},{8,9},{9,8},{10,11... | collective-permute-start | bytes 589832 | tf_op jit(solution)/shard_map/ppermute | solution.py:17
  53.2 2.1 %collective-permute-start.26 = (bf16[96,1024]{1,0:T(8,128)(2,1)S(1)}, bf16[96,1024]{1,0:T(8,128)(2,1)S(1)}, u32[]{:S(2)}, u32[]{:S(2)}) collective-permute-start(bf16[96,1024]{1,0:T(8,128)(2,1)S(1)} %copy.13), channel_id=1, source_target_pairs={{0,1},{1,0},{2,3},{3,2},{4,5},{5,4},{6,7},{7,6},{8,9},{9,8},{10,11... | collective-permute-start | bytes 589832 | tf_op jit(solution)/shard_map/ppermute | solution.py:17
  (6 other events, 16.4 us)

commit v18 on v17

--- a/solution.py
+++ b/solution.py
@@ -52,6 +52,11 @@
 def pair_kernel(own, sib, out):
     lane = lax.broadcasted_iota(jnp.int32, out.shape, 1)
     out[...] = jnp.where(lane == 0, own[...], sib[...])
+
+
+def more_kernel(known, counts, got, out):
+    out[...] = counts[...]
+    out[known : 2 * known, :] = got[:known, :]
 
 
 def split_kernel(rows_ref, keep_ref, send_ref):
@@ -106,21 +111,21 @@
 
 def dense_kernel(size, picks_chip, rest_chip, chosen_ref, *refs):
     chips = size // 2
-    counts, (own, sib, *outs, select_ref) = refs[:chips], refs[chips:]
+    counts, own, sib, *outs, select_ref = refs
     slots, picks = own.shape[0], chosen_ref.shape[1]
     rows_chip = picks_chip + rest_chip
     me = lax.axis_index("mem")
     offsets = [jnp.zeros((1, 1), jnp.int32) for _ in range(2)]
-    for d, ref in enumerate(counts):
+    for d in range(chips):
         for h in range(2):
             origin = lax.bitwise_xor(me, 2 * d + h)
             for k in range(2):
                 before = (origin < lax.bitwise_xor(me, k)).astype(jnp.int32)
-                offsets[k] += ref[:1, h : h + 1] * before
+                offsets[k] += counts[d : d + 1, h : h + 1] * before
     lane = lax.broadcasted_iota(jnp.int32, (1, 2 * slots), 1)
     first = lane < slots
     within = jnp.where(first, lane, lane - slots)
-    alive = within < jnp.where(first, counts[0][:1, :1], counts[0][:1, 1:2])
+    alive = within < jnp.where(first, counts[:1, :1], counts[:1, 1:2])
     position = jnp.where(alive, within + jnp.where(first, offsets[0], offsets[1]), -1)
 
     chosen = chosen_ref[...]
@@ -267,13 +272,18 @@
         spread_kernel, "spread", tile, (counts,), specs=[pl.BlockSpec(memory_space=pltpu.SMEM)]
     )
     pair = call(pair_kernel, "pair", tile, (count, flip_permute(count, size, 1)))
-    pairs = to_chips(pair, size)
+    group_counts = pair
+    for stage in range(chips.bit_length() - 1):
+        group_counts = call(
+            functools.partial(more_kernel, 1 << stage), "more_counts", tile,
+            (group_counts, flip_permute(group_counts, size, 2 << stage)),
+        )
     own, send = call(split_kernel, "split", [bf16(slots, half)] * 2, (round_one,))
     sib = flip_permute(send, size, 1)
 
     parts = call(
         functools.partial(dense_kernel, size, picks_chip, rest_chip), "dense",
-        [bf16(rows_chip, half)] * chips, (chosen, *pairs, own, sib),
+        [bf16(rows_chip, half)] * chips, (chosen, group_counts, own, sib),
         scratch=[pltpu.VMEM((live, 2 * slots), BF16)],
     )
     cand, norm = call(

time: 57.5 us -> 59.2 us (1.030)
  waiting for transfers between devices: 14.7 us -> 16.8 us
    ppermute x25 -> x24, waiting for transfers between devices: 10.7 us -> 13.3 us  [flip_permute(): return lax.ppermute(block, 'mem', [(m, m ^ flip) for m in range(size)])]
    ppermute x25 -> x24, starting transfers between devices: 20.6 us -> 20.5 us  [flip_permute(): return lax.ppermute(block, 'mem', [(m, m ^ flip) for m in range(size)])]
    pallas_call x23 -> x25, Pallas kernels: 14.6 us -> 14.6 us  [call(): pl.pallas_call(run, out_shape=out_shape, in_specs=(specs or vmem_specs(co...]
  transfers between devices with their start and end apart: 28 -> 27, of which waited for: 14 -> 15; matrix products, arithmetic and copies ran while one was open for 0% -> 0% of each run, Pallas kernels for 21% -> 20%
where the time goes in v18:
time: 59.2 us; the launch traced here: 58.9 us
  starting transfers between devices  26 us (44%)
  waiting for transfers between devices  16.8 us (28%)
  Pallas kernels  14.6 us (25%)
  between operations  1.5 us (3%)
    ppermute x24, starting transfers between devices, flip_permute(): return lax.ppermute(block, 'mem', [(m, m ^ flip) for m in range(size)])  20.5 us
    pallas_call x25, Pallas kernels, call(): pl.pallas_call(run, out_shape=out_shape, in_specs=(specs or vmem_specs(co...  14.6 us
    ppermute x24, waiting for transfers between devices, flip_permute(): return lax.ppermute(block, 'mem', [(m, m ^ flip) for m in range(size)])  13.3 us
    ppermute x3, starting transfers between devices, body(): lax.ppermute(picked, 'grp', [(g, (g + k) % groups) for g in range(groups)])  5.52 us
    ppermute x3, waiting for transfers between devices, body(): lax.ppermute(picked, 'grp', [(g, (g + k) % groups) for g in range(groups)])  3.45 us
  transfers between devices with their start and end apart: 27, of which 15 were waited for; matrix products, arithmetic and copies ran while one was open for 0% of the time, Pallas kernels for 20%

profile of v18, /device:TPU:0, one launch (start us, length us, event | category | flops | bytes accessed | tf_op | source)
XLA Modules:
  0.0 58.9 jit_solution(16116104391306685911)
XLA Ops:
  2.6 2.8 %collective-permute-start.1 = (s32[8,128]{1,0:T(8,128)S(1)}, s32[8,128]{1,0:T(8,128)S(1)}, u32[]{:S(2)}, u32[]{:S(2)}) collective-permute-start(s32[8,128]{1,0:T(8,128)S(1)} %pair.1.refs_0_), channel_id=1, source_target_pairs={{0,2},{1,3},{2,0},{3,1},{4,6},{5,7},{6,4},{7,5},{8,10},{9,11},{10,... | collective-permute-start | bytes 12296 | tf_op jit(solution)/shard_map/ppermute | solution.py:17
  5.5 1.6 %collective-permute-done.1.refs_1_ = s32[8,128]{1,0:T(8,128)S(1)} collective-permute-done((s32[8,128]{1,0:T(8,128)S(1)}, s32[8,128]{1,0:T(8,128)S(1)}, u32[]{:S(2)}, u32[]{:S(2)}) %collective-permute-start.1) | collective-permute-done | bytes 4128 | tf_op jit(solution)/shard_map/ppermute | solution.py:17
  7.1 2.1 %collective-permute-start.2 = (s32[8,128]{1,0:T(8,128)S(1)}, s32[8,128]{1,0:T(8,128)S(1)}, u32[]{:S(2)}, u32[]{:S(2)}) collective-permute-start(s32[8,128]{1,0:T(8,128)S(1)} %more_counts.2.refs_0_), channel_id=1, source_target_pairs={{0,4},{1,5},{2,6},{3,7},{4,0},{5,1},{6,2},{7,3},{8,12},{9,13},{10,... | collective-permute-start | bytes 12296 | tf_op jit(solution)/shard_map/ppermute | solution.py:17
  9.2 1.5 %collective-permute-done.2.refs_1_ = s32[8,128]{1,0:T(8,128)S(1)} collective-permute-done((s32[8,128]{1,0:T(8,128)S(1)}, s32[8,128]{1,0:T(8,128)S(1)}, u32[]{:S(2)}, u32[]{:S(2)}) %collective-permute-start.2) | collective-permute-done | bytes 4128 | tf_op jit(solution)/shard_map/ppermute | solution.py:17
  11.3 2.0 %collective-permute-start.4 = (bf16[48,2048]{1,0:T(8,128)(2,1)S(1)}, bf16[48,2048]{1,0:T(8,128)(2,1)S(1)}, u32[]{:S(2)}, u32[]{:S(2)}) collective-permute-start(bf16[48,2048]{1,0:T(8,128)(2,1)S(1)} %get-tuple-element.19), channel_id=1, source_target_pairs={{0,2},{1,3},{2,0},{3,1},{4,6},{5,7},{6,4},{7,5},{8,10},{9,11},{10,... | collective-permute-start | bytes 589832 | tf_op jit(solution)/shard_map/ppermute | solution.py:17
  13.3 1.5 %collective-permute-start.5 = (bf16[48,2048]{1,0:T(8,128)(2,1)S(1)}, bf16[48,2048]{1,0:T(8,128)(2,1)S(1)}, u32[]{:S(2)}, u32[]{:S(2)}) collective-permute-start(bf16[48,2048]{1,0:T(8,128)(2,1)S(1)} %get-tuple-element.20), channel_id=1, source_target_pairs={{0,4},{1,5},{2,6},{3,7},{4,0},{5,1},{6,2},{7,3},{8,12},{9,13},{10,... | collective-permute-start | bytes 589832 | tf_op jit(solution)/shard_map/ppermute | solution.py:17
  14.9 4.0 %load.1 = (bf16[1024,4096]{1,0:T(8,128)(2,1)S(1)}, f32[1,1024]{1,0:T(1,128)S(1)}) custom-call(bf16[1024,4096]{1,0:T(8,128)(2,1)} %refs_0_.6, bf16[48,2048]{1,0:T(8,128)(2,1)S(1)} %get-tuple-element.16.refs_1_.refs_0_), custom_call_target="tpu_custom_call" | custom-call | flops 10000000000 | bytes 16781312 | tf_op jit(solution)/shard_map/load/pallas_call | solution.py:36
  19.1 4.6 %collective-permute-done.5.refs_2_ = bf16[48,2048]{1,0:T(8,128)(2,1)S(1)} collective-permute-done((bf16[48,2048]{1,0:T(8,128)(2,1)S(1)}, bf16[48,2048]{1,0:T(8,128)(2,1)S(1)}, u32[]{:S(2)}, u32[]{:S(2)}) %collective-permute-start.5) | collective-permute-done | bytes 196640 | tf_op jit(solution)/shard_map/ppermute | solution.py:17
  24.4 1.2 %collective-permute-start.8 = (bf16[48,2048]{1,0:T(8,128)(2,1)S(1)}, bf16[48,2048]{1,0:T(8,128)(2,1)S(1)}, u32[]{:S(2)}, u32[]{:S(2)}) collective-permute-start(bf16[48,2048]{1,0:T(8,128)(2,1)S(1)} %get-tuple-element.22.refs_0_), channel_id=1, source_target_pairs={{0,4},{1,5},{2,6},{3,7},{4,0},{5,1},{6,2},{7,3},{8,12},{9,13},{10,... | collective-permute-start | bytes 589832 | tf_op jit(solution)/shard_map/ppermute | solution.py:17
  25.6 1.6 %collective-permute-start.11 = (bf16[32,2048]{1,0:T(8,128)(2,1)S(1)}, bf16[32,2048]{1,0:T(8,128)(2,1)S(1)}, u32[]{:S(2)}, u32[]{:S(2)}) collective-permute-start(bf16[32,2048]{1,0:T(8,128)(2,1)S(1)} %get-tuple-element.23), channel_id=1, source_target_pairs={{0,8},{8,16},{16,24},{24,0},{1,9},{9,17},{17,25},{25,1},{2,10},{10... | collective-permute-start | bytes 393224 | tf_op jit(solution)/shard_map/ppermute | solution.py:301
  27.2 2.6 %collective-permute-start.12 = (bf16[32,2048]{1,0:T(8,128)(2,1)S(1)}, bf16[32,2048]{1,0:T(8,128)(2,1)S(1)}, u32[]{:S(2)}, u32[]{:S(2)}) collective-permute-start(bf16[32,2048]{1,0:T(8,128)(2,1)S(1)} %get-tuple-element.23), channel_id=1, source_target_pairs={{0,16},{8,24},{16,0},{24,8},{1,17},{9,25},{17,1},{25,9},{2,18},{10... | collective-permute-start | bytes 393224 | tf_op jit(solution)/shard_map/ppermute | solution.py:301
  29.8 1.3 %collective-permute-start.13 = (bf16[32,2048]{1,0:T(8,128)(2,1)S(1)}, bf16[32,2048]{1,0:T(8,128)(2,1)S(1)}, u32[]{:S(2)}, u32[]{:S(2)}) collective-permute-start(bf16[32,2048]{1,0:T(8,128)(2,1)S(1)} %get-tuple-element.23), channel_id=1, source_target_pairs={{0,24},{8,0},{16,8},{24,16},{1,25},{9,1},{17,9},{25,17},{2,26},{10... | collective-permute-start | bytes 393224 | tf_op jit(solution)/shard_map/ppermute | solution.py:301
  32.0 1.6 %collective-permute-start.10 = (bf16[48,1024]{1,0:T(8,128)(2,1)S(1)}, bf16[48,1024]{1,0:T(8,128)(2,1)S(1)}, u32[]{:S(2)}, u32[]{:S(2)}) collective-permute-start(bf16[48,1024]{1,0:T(8,128)(2,1)S(1)} %stack.10), channel_id=1, source_target_pairs={{0,2},{1,3},{2,0},{3,1},{4,6},{5,7},{6,4},{7,5},{8,10},{9,11},{10,... | collective-permute-start | bytes 294920 | tf_op jit(solution)/shard_map/ppermute | solution.py:17
  33.9 3.1 %collective-permute-done.12.refs_1_ = bf16[32,2048]{1,0:T(8,128)(2,1)S(1)} collective-permute-done((bf16[32,2048]{1,0:T(8,128)(2,1)S(1)}, bf16[32,2048]{1,0:T(8,128)(2,1)S(1)}, u32[]{:S(2)}, u32[]{:S(2)}) %collective-permute-start.12) | collective-permute-done | bytes 131104 | tf_op jit(solution)/shard_map/ppermute | solution.py:301
  37.3 1.3 %collective-permute-start.15 = (bf16[96,1024]{1,0:T(8,128)(2,1)S(1)}, bf16[96,1024]{1,0:T(8,128)(2,1)S(1)}, u32[]{:S(2)}, u32[]{:S(2)}) collective-permute-start(bf16[96,1024]{1,0:T(8,128)(2,1)S(1)} %stack.11.refs_5_), channel_id=1, source_target_pairs={{0,2},{1,3},{2,0},{3,1},{4,6},{5,7},{6,4},{7,5},{8,10},{9,11},{10,... | collective-permute-start | bytes 589832 | tf_op jit(solution)/shard_map/ppermute | solution.py:17
  38.6 1.0 %collective-permute-start.17 = (bf16[96,1024]{1,0:T(8,128)(2,1)S(1)}, bf16[96,1024]{1,0:T(8,128)(2,1)S(1)}, u32[]{:S(2)}, u32[]{:S(2)}) collective-permute-start(bf16[96,1024]{1,0:T(8,128)(2,1)S(1)} %stack.12.refs_6_), channel_id=1, source_target_pairs={{0,4},{1,5},{2,6},{3,7},{4,0},{5,1},{6,2},{7,3},{8,12},{9,13},{10,... | collective-permute-start | bytes 589832 | tf_op jit(solution)/shard_map/ppermute | solution.py:17
  40.2 1.2 %collective-permute-start.20 = (bf16[96,1024]{1,0:T(8,128)(2,1)S(1)}, bf16[96,1024]{1,0:T(8,128)(2,1)S(1)}, u32[]{:S(2)}, u32[]{:S(2)}) collective-permute-start(bf16[96,1024]{1,0:T(8,128)(2,1)S(1)} %stack.11.refs_5_), channel_id=1, source_target_pairs={{0,4},{1,5},{2,6},{3,7},{4,0},{5,1},{6,2},{7,3},{8,12},{9,13},{10,... | collective-permute-start | bytes 589832 | tf_op jit(solution)/shard_map/ppermute | solution.py:17
  41.4 3.3 %products.1 = (f32[1,1024]{1,0:T(1,128)}, f32[1,1024]{1,0:T(1,128)S(1)}) custom-call(bf16[1024,4096]{1,0:T(8,128)(2,1)S(1)} %get-tuple-element.17.refs_0_, f32[1,1024]{1,0:T(1,128)S(1)} %get-tuple-element.18.refs_4_.refs_1_, bf16[288,2048]{1,0:T(8,128)(2,1)S(1)} %stack.13.refs_2_, bf16[288,2048]{1,0:T(8,128)(2,1)S(1)} %collective-permute-done.14.refs_3_), custom_call_target="tpu_custom_call" | custom-call | flops 1000000000 | bytes 10760192 | tf_op jit(solution)/shard_map/products/pallas_call | solution.py:36
  45.1 1.3 %collective-permute-done.17.refs_0_.refs_7_ = bf16[96,1024]{1,0:T(8,128)(2,1)S(1)} collective-permute-done((bf16[96,1024]{1,0:T(8,128)(2,1)S(1)}, bf16[96,1024]{1,0:T(8,128)(2,1)S(1)}, u32[]{:S(2)}, u32[]{:S(2)}) %collective-permute-start.17) | collective-permute-done | bytes 196640 | tf_op jit(solution)/shard_map/ppermute | solution.py:17
  46.4 1.1 %collective-permute-start.23 = (bf16[112,1024]{1,0:T(8,128)(2,1)S(1)}, bf16[112,1024]{1,0:T(8,128)(2,1)S(1)}, u32[]{:S(2)}, u32[]{:S(2)}) collective-permute-start(bf16[112,1024]{1,0:T(8,128)(2,1)S(1)} %copy.11.refs_2_), channel_id=1, source_target_pairs={{0,4},{1,5},{2,6},{3,7},{4,0},{5,1},{6,2},{7,3},{8,12},{9,13},{10,... | collective-permute-start | bytes 688136 | tf_op jit(solution)/shard_map/ppermute | solution.py:17
  48.9 1.0 %collective-permute-done.20.refs_0_.refs_6_ = bf16[96,1024]{1,0:T(8,128)(2,1)S(1)} collective-permute-done((bf16[96,1024]{1,0:T(8,128)(2,1)S(1)}, bf16[96,1024]{1,0:T(8,128)(2,1)S(1)}, u32[]{:S(2)}, u32[]{:S(2)}) %collective-permute-start.20) | collective-permute-done | bytes 196640 | tf_op jit(solution)/shard_map/ppermute | solution.py:17
  51.7 3.0 %products_next.1.refs_3_.refs_1_.refs_2_ = f32[1,1024]{1,0:T(1,128)S(1)} custom-call(bf16[1024,4096]{1,0:T(8,128)(2,1)S(1)} %get-tuple-element.17.refs_0_, f32[1,1024]{1,0:T(1,128)S(1)} %get-tuple-element.25.refs_1_, bf16[96,1024]{1,0:T(8,128)(2,1)S(1)} %collective-permute-done.15.refs_0_.refs_2_, ...), custom_call_target="tpu_custom_call" | custom-call | bytes 9969664 | tf_op jit(solution)/shard_map/products_next/pallas_call | solution.py:36
  55.4 1.4 %products_half.1.refs_3_ = f32[96,1024]{1,0:T(8,128)S(1)} custom-call(bf16[1024,4096]{1,0:T(8,128)(2,1)S(1)} %get-tuple-element.17.refs_0_, bf16[112,1024]{1,0:T(8,128)(2,1)S(1)} %collective-permute-done.23.refs_1_.refs_0_, bf16[112,1024]{1,0:T(8,128)(2,1)S(1)} %collective-permute-done.24.refs_2_.refs_0_, f32[1,1024]{1,0:T(1,128)S(1)} %products_next.1.refs_3_.refs_1_.refs_2_), custom_call_target="tpu_custom_call" | custom-call | flops 10000000000 | bytes 9240576 | tf_op jit(solution)/shard_map/products_half/pallas_call | solution.py:36
  56.8 2.0 %products_last.1 = f32[1,1024]{1,0:T(1,128)} custom-call(bf16[1024,4096]{1,0:T(8,128)(2,1)S(1)} %get-tuple-element.17.refs_0_, f32[1,1024]{1,0:T(1,128)S(1)} %get-tuple-element.18.refs_4_.refs_1_, f32[1,1024]{1,0:T(1,128)S(1)} %products_next.1.refs_3_.refs_1_.refs_2_, f32[96,1024]{1,0:T(8,128)S(1)} %products_half.1.refs_3_, ...), custom_call_target="tpu_custom_call" | custom-call | flops 10000000000 | bytes 9187328 | tf_op jit(solution)/shard_map/products_last/pallas_call | solution.py:36
  (59 shorter events, 9.3 us)
Async XLA Ops:
  2.6 4.4 %collective-permute-start.1 = (s32[8,128]{1,0:T(8,128)S(1)}, s32[8,128]{1,0:T(8,128)S(1)}, u32[]{:S(2)}, u32[]{:S(2)}) collective-permute-start(s32[8,128]{1,0:T(8,128)S(1)} %pair.1.refs_0_), channel_id=1, source_target_pairs={{0,2},{1,3},{2,0},{3,1},{4,6},{5,7},{6,4},{7,5},{8,10},{9,11},{10,... | collective-permute-start | bytes 12296 | tf_op jit(solution)/shard_map/ppermute | solution.py:17
  7.1 3.6 %collective-permute-start.2 = (s32[8,128]{1,0:T(8,128)S(1)}, s32[8,128]{1,0:T(8,128)S(1)}, u32[]{:S(2)}, u32[]{:S(2)}) collective-permute-start(s32[8,128]{1,0:T(8,128)S(1)} %more_counts.2.refs_0_), channel_id=1, source_target_pairs={{0,4},{1,5},{2,6},{3,7},{4,0},{5,1},{6,2},{7,3},{8,12},{9,13},{10,... | collective-permute-start | bytes 12296 | tf_op jit(solution)/shard_map/ppermute | solution.py:17
  9.2 1.6 %collective-permute-start.3 = (bf16[64,2048]{1,0:T(8,128)(2,1)S(1)}, bf16[64,2048]{1,0:T(8,128)(2,1)S(1)}, u32[]{:S(2)}, u32[]{:S(2)}) collective-permute-start(bf16[64,2048]{1,0:T(8,128)(2,1)S(1)} %get-tuple-element.15), channel_id=1, source_target_pairs={{0,1},{1,0},{2,3},{3,2},{4,5},{5,4},{6,7},{7,6},{8,9},{9,8},{10,11... | collective-permute-start | bytes 786440 | tf_op jit(solution)/shard_map/ppermute | solution.py:17
  11.3 7.8 %collective-permute-start.4 = (bf16[48,2048]{1,0:T(8,128)(2,1)S(1)}, bf16[48,2048]{1,0:T(8,128)(2,1)S(1)}, u32[]{:S(2)}, u32[]{:S(2)}) collective-permute-start(bf16[48,2048]{1,0:T(8,128)(2,1)S(1)} %get-tuple-element.19), channel_id=1, source_target_pairs={{0,2},{1,3},{2,0},{3,1},{4,6},{5,7},{6,4},{7,5},{8,10},{9,11},{10,... | collective-permute-start | bytes 589832 | tf_op jit(solution)/shard_map/ppermute | solution.py:17
  13.3 10.4 %collective-permute-start.5 = (bf16[48,2048]{1,0:T(8,128)(2,1)S(1)}, bf16[48,2048]{1,0:T(8,128)(2,1)S(1)}, u32[]{:S(2)}, u32[]{:S(2)}) collective-permute-start(bf16[48,2048]{1,0:T(8,128)(2,1)S(1)} %get-tuple-element.20), channel_id=1, source_target_pairs={{0,4},{1,5},{2,6},{3,7},{4,0},{5,1},{6,2},{7,3},{8,12},{9,13},{10,... | collective-permute-start | bytes 589832 | tf_op jit(solution)/shard_map/ppermute | solution.py:17
  14.8 8.9 %collective-permute-start.6 = (bf16[48,2048]{1,0:T(8,128)(2,1)S(1)}, bf16[48,2048]{1,0:T(8,128)(2,1)S(1)}, u32[]{:S(2)}, u32[]{:S(2)}) collective-permute-start(bf16[48,2048]{1,0:T(8,128)(2,1)S(1)} %get-tuple-element.21), channel_id=1, source_target_pairs={{0,6},{1,7},{2,4},{3,5},{4,2},{5,3},{6,0},{7,1},{8,14},{9,15},{10,... | collective-permute-start | bytes 589832 | tf_op jit(solution)/shard_map/ppermute | solution.py:17
  23.8 7.3 %collective-permute-start.7 = (bf16[48,2048]{1,0:T(8,128)(2,1)S(1)}, bf16[48,2048]{1,0:T(8,128)(2,1)S(1)}, u32[]{:S(2)}, u32[]{:S(2)}) collective-permute-start(bf16[48,2048]{1,0:T(8,128)(2,1)S(1)} %get-tuple-element.22.refs_0_), channel_id=1, source_target_pairs={{0,2},{1,3},{2,0},{3,1},{4,6},{5,7},{6,4},{7,5},{8,10},{9,11},{10,... | collective-permute-start | bytes 589832 | tf_op jit(solution)/shard_map/ppermute | solution.py:17
  24.4 7.6 %collective-permute-start.8 = (bf16[48,2048]{1,0:T(8,128)(2,1)S(1)}, bf16[48,2048]{1,0:T(8,128)(2,1)S(1)}, u32[]{:S(2)}, u32[]{:S(2)}) collective-permute-start(bf16[48,2048]{1,0:T(8,128)(2,1)S(1)} %get-tuple-element.22.refs_0_), channel_id=1, source_target_pairs={{0,4},{1,5},{2,6},{3,7},{4,0},{5,1},{6,2},{7,3},{8,12},{9,13},{10,... | collective-permute-start | bytes 589832 | tf_op jit(solution)/shard_map/ppermute | solution.py:17
  25.6 8.3 %collective-permute-start.11 = (bf16[32,2048]{1,0:T(8,128)(2,1)S(1)}, bf16[32,2048]{1,0:T(8,128)(2,1)S(1)}, u32[]{:S(2)}, u32[]{:S(2)}) collective-permute-start(bf16[32,2048]{1,0:T(8,128)(2,1)S(1)} %get-tuple-element.23), channel_id=1, source_target_pairs={{0,8},{8,16},{16,24},{24,0},{1,9},{9,17},{17,25},{25,1},{2,10},{10... | collective-permute-start | bytes 393224 | tf_op jit(solution)/shard_map/ppermute | solution.py:301
  27.2 9.9 %collective-permute-start.12 = (bf16[32,2048]{1,0:T(8,128)(2,1)S(1)}, bf16[32,2048]{1,0:T(8,128)(2,1)S(1)}, u32[]{:S(2)}, u32[]{:S(2)}) collective-permute-start(bf16[32,2048]{1,0:T(8,128)(2,1)S(1)} %get-tuple-element.23), channel_id=1, source_target_pairs={{0,16},{8,24},{16,0},{24,8},{1,17},{9,25},{17,1},{25,9},{2,18},{10... | collective-permute-start | bytes 393224 | tf_op jit(solution)/shard_map/ppermute | solution.py:301
  29.8 7.3 %collective-permute-start.13 = (bf16[32,2048]{1,0:T(8,128)(2,1)S(1)}, bf16[32,2048]{1,0:T(8,128)(2,1)S(1)}, u32[]{:S(2)}, u32[]{:S(2)}) collective-permute-start(bf16[32,2048]{1,0:T(8,128)(2,1)S(1)} %get-tuple-element.23), channel_id=1, source_target_pairs={{0,24},{8,0},{16,8},{24,16},{1,25},{9,1},{17,9},{25,17},{2,26},{10... | collective-permute-start | bytes 393224 | tf_op jit(solution)/shard_map/ppermute | solution.py:301
  31.1 5.9 %collective-permute-start.9 = (bf16[48,1024]{1,0:T(8,128)(2,1)S(1)}, bf16[48,1024]{1,0:T(8,128)(2,1)S(1)}, u32[]{:S(2)}, u32[]{:S(2)}) collective-permute-start(bf16[48,1024]{1,0:T(8,128)(2,1)S(1)} %stack.9), channel_id=1, source_target_pairs={{0,4},{1,5},{2,6},{3,7},{4,0},{5,1},{6,2},{7,3},{8,12},{9,13},{10,... | collective-permute-start | bytes 294920 | tf_op jit(solution)/shard_map/ppermute | solution.py:17
  32.0 5.0 %collective-permute-start.10 = (bf16[48,1024]{1,0:T(8,128)(2,1)S(1)}, bf16[48,1024]{1,0:T(8,128)(2,1)S(1)}, u32[]{:S(2)}, u32[]{:S(2)}) collective-permute-start(bf16[48,1024]{1,0:T(8,128)(2,1)S(1)} %stack.10), channel_id=1, source_target_pairs={{0,2},{1,3},{2,0},{3,1},{4,6},{5,7},{6,4},{7,5},{8,10},{9,11},{10,... | collective-permute-start | bytes 294920 | tf_op jit(solution)/shard_map/ppermute | solution.py:17
  37.2 4.2 %collective-permute-start.14 = (bf16[288,2048]{1,0:T(8,128)(2,1)S(1)}, bf16[288,2048]{1,0:T(8,128)(2,1)S(1)}, u32[]{:S(2)}, u32[]{:S(2)}) collective-permute-start(bf16[288,2048]{1,0:T(8,128)(2,1)S(1)} %stack.13.refs_2_), channel_id=1, source_target_pairs={{0,1},{1,0},{2,3},{3,2},{4,5},{5,4},{6,7},{7,6},{8,9},{9,8},{10,11... | collective-permute-start | bytes 3538952 | tf_op jit(solution)/shard_map/ppermute | solution.py:17
  37.3 7.8 %collective-permute-start.15 = (bf16[96,1024]{1,0:T(8,128)(2,1)S(1)}, bf16[96,1024]{1,0:T(8,128)(2,1)S(1)}, u32[]{:S(2)}, u32[]{:S(2)}) collective-permute-start(bf16[96,1024]{1,0:T(8,128)(2,1)S(1)} %stack.11.refs_5_), channel_id=1, source_target_pairs={{0,2},{1,3},{2,0},{3,1},{4,6},{5,7},{6,4},{7,5},{8,10},{9,11},{10,... | collective-permute-start | bytes 589832 | tf_op jit(solution)/shard_map/ppermute | solution.py:17
  38.6 7.7 %collective-permute-start.17 = (bf16[96,1024]{1,0:T(8,128)(2,1)S(1)}, bf16[96,1024]{1,0:T(8,128)(2,1)S(1)}, u32[]{:S(2)}, u32[]{:S(2)}) collective-permute-start(bf16[96,1024]{1,0:T(8,128)(2,1)S(1)} %stack.12.refs_6_), channel_id=1, source_target_pairs={{0,4},{1,5},{2,6},{3,7},{4,0},{5,1},{6,2},{7,3},{8,12},{9,13},{10,... | collective-permute-start | bytes 589832 | tf_op jit(solution)/shard_map/ppermute | solution.py:17
  39.6 9.2 %collective-permute-start.16 = (bf16[96,1024]{1,0:T(8,128)(2,1)S(1)}, bf16[96,1024]{1,0:T(8,128)(2,1)S(1)}, u32[]{:S(2)}, u32[]{:S(2)}) collective-permute-start(bf16[96,1024]{1,0:T(8,128)(2,1)S(1)} %stack.12.refs_6_), channel_id=1, source_target_pairs={{0,2},{1,3},{2,0},{3,1},{4,6},{5,7},{6,4},{7,5},{8,10},{9,11},{10,... | collective-permute-start | bytes 589832 | tf_op jit(solution)/shard_map/ppermute | solution.py:17
  40.2 9.7 %collective-permute-start.20 = (bf16[96,1024]{1,0:T(8,128)(2,1)S(1)}, bf16[96,1024]{1,0:T(8,128)(2,1)S(1)}, u32[]{:S(2)}, u32[]{:S(2)}) collective-permute-start(bf16[96,1024]{1,0:T(8,128)(2,1)S(1)} %stack.11.refs_5_), channel_id=1, source_target_pairs={{0,4},{1,5},{2,6},{3,7},{4,0},{5,1},{6,2},{7,3},{8,12},{9,13},{10,... | collective-permute-start | bytes 589832 | tf_op jit(solution)/shard_map/ppermute | solution.py:17
  46.4 3.7 %collective-permute-start.18 = (bf16[96,1024]{1,0:T(8,128)(2,1)S(1)}, bf16[96,1024]{1,0:T(8,128)(2,1)S(1)}, u32[]{:S(2)}, u32[]{:S(2)}) collective-permute-start(bf16[96,1024]{1,0:T(8,128)(2,1)S(1)} %stack.14), channel_id=1, source_target_pairs={{0,1},{1,0},{2,3},{3,2},{4,5},{5,4},{6,7},{7,6},{8,9},{9,8},{10,11... | collective-permute-start | bytes 589832 | tf_op jit(solution)/shard_map/ppermute | solution.py:17
  46.4 8.2 %collective-permute-start.23 = (bf16[112,1024]{1,0:T(8,128)(2,1)S(1)}, bf16[112,1024]{1,0:T(8,128)(2,1)S(1)}, u32[]{:S(2)}, u32[]{:S(2)}) collective-permute-start(bf16[112,1024]{1,0:T(8,128)(2,1)S(1)} %copy.11.refs_2_), channel_id=1, source_target_pairs={{0,4},{1,5},{2,6},{3,7},{4,0},{5,1},{6,2},{7,3},{8,12},{9,13},{10,... | collective-permute-start | bytes 688136 | tf_op jit(solution)/shard_map/ppermute | solution.py:17
  47.6 7.7 %collective-permute-start.24 = (bf16[112,1024]{1,0:T(8,128)(2,1)S(1)}, bf16[112,1024]{1,0:T(8,128)(2,1)S(1)}, u32[]{:S(2)}, u32[]{:S(2)}) collective-permute-start(bf16[112,1024]{1,0:T(8,128)(2,1)S(1)} %copy.12.refs_3_), channel_id=1, source_target_pairs={{0,2},{1,3},{2,0},{3,1},{4,6},{5,7},{6,4},{7,5},{8,10},{9,11},{10,... | collective-permute-start | bytes 688136 | tf_op jit(solution)/shard_map/ppermute | solution.py:17
  48.8 1.8 %collective-permute-start.19 = (bf16[96,1024]{1,0:T(8,128)(2,1)S(1)}, bf16[96,1024]{1,0:T(8,128)(2,1)S(1)}, u32[]{:S(2)}, u32[]{:S(2)}) collective-permute-start(bf16[96,1024]{1,0:T(8,128)(2,1)S(1)} %stack.15), channel_id=1, source_target_pairs={{0,1},{1,0},{2,3},{3,2},{4,5},{5,4},{6,7},{7,6},{8,9},{9,8},{10,11... | collective-permute-start | bytes 589832 | tf_op jit(solution)/shard_map/ppermute | solution.py:17
  50.0 1.7 %collective-permute-start.22 = (bf16[96,1024]{1,0:T(8,128)(2,1)S(1)}, bf16[96,1024]{1,0:T(8,128)(2,1)S(1)}, u32[]{:S(2)}, u32[]{:S(2)}) collective-permute-start(bf16[96,1024]{1,0:T(8,128)(2,1)S(1)} %stack.17), channel_id=1, source_target_pairs={{0,1},{1,0},{2,3},{3,2},{4,5},{5,4},{6,7},{7,6},{8,9},{9,8},{10,11... | collective-permute-start | bytes 589832 | tf_op jit(solution)/shard_map/ppermute | solution.py:17
  54.7 2.1 %collective-permute-start.25 = (bf16[96,1024]{1,0:T(8,128)(2,1)S(1)}, bf16[96,1024]{1,0:T(8,128)(2,1)S(1)}, u32[]{:S(2)}, u32[]{:S(2)}) collective-permute-start(bf16[96,1024]{1,0:T(8,128)(2,1)S(1)} %copy.13), channel_id=1, source_target_pairs={{0,1},{1,0},{2,3},{3,2},{4,5},{5,4},{6,7},{7,6},{8,9},{9,8},{10,11... | collective-permute-start | bytes 589832 | tf_op jit(solution)/shard_map/ppermute | solution.py:17
  (5 other events, 12.5 us)

commit v19 on v17

--- a/solution.py
+++ b/solution.py
@@ -152,11 +152,12 @@
 
 
 def sum_kernel(*refs):
-    *parts, out, picks_ref = refs
+    *parts, low, high, picks_ref = refs
     total = parts[0][...]
     for ref in parts[1:]:
         total += ref[...]
-    out[...] = total
+    low[...] = total[:, : low.shape[1]]
+    high[...] = total[:, low.shape[1] :]
     picks_ref[...] = total[: picks_ref.shape[0], :]
 
 
@@ -282,8 +283,10 @@
         scratch=[pltpu.SemaphoreType.DMA((rows // TILE * 2,))], limit=42 * MIB,
     )
     got = [flip_permute(parts[d], size, 2 * d) for d in range(1, chips)]
-    owned, picked = call(
-        sum_kernel, "owned", [bf16(rows_chip, half), bf16(picks_chip, half)], (parts[0], *got),
+    quarter = half // 2
+    *owned, picked = call(
+        sum_kernel, "owned", [bf16(rows_chip, quarter)] * 2 + [bf16(picks_chip, half)],
+        (parts[0], *got),
         after=(norm,),
     )
 
@@ -293,20 +296,18 @@
     ]
 
     if chips == 4:
-        quarter = half // 2
-        own_x, own_y = (flip_permute(owned, size, flip) for flip in (2, 4))
-        own_left = flip_permute(stack([(own_x, 0, quarter)]), size, 4)
-        own_right = flip_permute(stack([(own_y, quarter, quarter)]), size, 2)
+        own_x, own_y = ([flip_permute(part, size, flip) for part in owned] for flip in (2, 4))
+        own_left, own_right = flip_permute(own_x[0], size, 4), flip_permute(own_y[1], size, 2)
         wait = (own_left, own_right)
         low = stack(*[[(b, 0, quarter)] for b in shifted], after=wait)
         high = stack(*[[(b, quarter, quarter)] for b in shifted], after=wait)
         low_x, high_y = flip_permute(low, size, 2), flip_permute(high, size, 4)
         high_x, low_y = flip_permute(high, size, 2), flip_permute(low, size, 4)
-        first = stack([owned], [own_x], [own_y], [own_left, own_right], [low, high])
+        first = stack(owned, own_x, own_y, [own_left, own_right], [low, high])
         others = ([low_x, high_x], [low_y, high_y])
     else:
         far = to_chips(stack(*[[b] for b in shifted]), size)
-        first = stack(*[[b] for b in to_chips(owned, size)], [far[0]])
+        first = stack(*[[b] for b in to_chips(stack(owned), size)], [far[0]])
         others = [[b] for b in far[1:-1]]
 
     near, best = call(

time: 57.5 us -> 61.7 us (1.073)
  waiting for transfers between devices: 14.7 us -> 17 us
  starting transfers between devices: 26.1 us -> 27.9 us
    ppermute x25 -> x27, waiting for transfers between devices: 10.7 us -> 17 us  [flip_permute(): return lax.ppermute(block, 'mem', [(m, m ^ flip) for m in range(size)])]
    ppermute x3, waiting for transfers between devices: 3.91 us -> 0.01 us  [body(): lax.ppermute(picked, 'grp', [(g, (g + k) % groups) for g in range(groups)])]
    ppermute x25 -> x27, starting transfers between devices: 20.6 us -> 22.3 us  [flip_permute(): return lax.ppermute(block, 'mem', [(m, m ^ flip) for m in range(size)])]
    pallas_call x23 -> x21, Pallas kernels: 14.6 us -> 14.6 us  [call(): pl.pallas_call(run, out_shape=out_shape, in_specs=(specs or vmem_specs(co...]
  transfers between devices with their start and end apart: 28 -> 30, of which waited for: 14 -> 16; matrix products, arithmetic and copies ran while one was open for 0% -> 0% of each run, Pallas kernels for 21% -> 19%
where the time goes in v19:
time: 61.7 us; the launch traced here: 61.5 us
  starting transfers between devices  27.9 us (45%)
  waiting for transfers between devices  17 us (28%)
  Pallas kernels  14.6 us (24%)
  between operations  1.49 us (2%)
    ppermute x27, starting transfers between devices, flip_permute(): return lax.ppermute(block, 'mem', [(m, m ^ flip) for m in range(size)])  22.3 us
    ppermute x27, waiting for transfers between devices, flip_permute(): return lax.ppermute(block, 'mem', [(m, m ^ flip) for m in range(size)])  17 us
    pallas_call x21, Pallas kernels, call(): pl.pallas_call(run, out_shape=out_shape, in_specs=(specs or vmem_specs(co...  14.6 us
    ppermute x3, starting transfers between devices, body(): lax.ppermute(picked, 'grp', [(g, (g + k) % groups) for g in range(groups)])  5.57 us
  transfers between devices with their start and end apart: 30, of which 16 were waited for; matrix products, arithmetic and copies ran while one was open for 0% of the time, Pallas kernels for 19%

profile of v19, /device:TPU:0, one launch (start us, length us, event | category | flops | bytes accessed | tf_op | source)
XLA Modules:
  0.0 61.5 jit_solution(11346188118773829044)
XLA Ops:
  2.9 2.6 %collective-permute-start.1 = (s32[8,128]{1,0:T(8,128)S(1)}, s32[8,128]{1,0:T(8,128)S(1)}, u32[]{:S(2)}, u32[]{:S(2)}) collective-permute-start(s32[8,128]{1,0:T(8,128)S(1)} %pair.1.refs_1_), channel_id=1, source_target_pairs={{0,2},{1,3},{2,0},{3,1},{4,6},{5,7},{6,4},{7,5},{8,10},{9,11},{10,... | collective-permute-start | bytes 12296 | tf_op jit(solution)/shard_map/ppermute | solution.py:17
  5.5 1.5 %collective-permute-start.2 = (s32[8,128]{1,0:T(8,128)S(1)}, s32[8,128]{1,0:T(8,128)S(1)}, u32[]{:S(2)}, u32[]{:S(2)}) collective-permute-start(s32[8,128]{1,0:T(8,128)S(1)} %pair.1.refs_1_), channel_id=1, source_target_pairs={{0,4},{1,5},{2,6},{3,7},{4,0},{5,1},{6,2},{7,3},{8,12},{9,13},{10,... | collective-permute-start | bytes 12296 | tf_op jit(solution)/shard_map/ppermute | solution.py:17
  7.1 2.0 %collective-permute-done.2.refs_3_ = s32[8,128]{1,0:T(8,128)S(1)} collective-permute-done((s32[8,128]{1,0:T(8,128)S(1)}, s32[8,128]{1,0:T(8,128)S(1)}, u32[]{:S(2)}, u32[]{:S(2)}) %collective-permute-start.2) | collective-permute-done | bytes 4128 | tf_op jit(solution)/shard_map/ppermute | solution.py:17
  9.1 2.4 %collective-permute-done.3.refs_4_ = s32[8,128]{1,0:T(8,128)S(1)} collective-permute-done((s32[8,128]{1,0:T(8,128)S(1)}, s32[8,128]{1,0:T(8,128)S(1)}, u32[]{:S(2)}, u32[]{:S(2)}) %collective-permute-start.3) | collective-permute-done | bytes 4128 | tf_op jit(solution)/shard_map/ppermute | solution.py:17
  12.7 2.9 %collective-permute-start.7 = (bf16[48,2048]{1,0:T(8,128)(2,1)S(1)}, bf16[48,2048]{1,0:T(8,128)(2,1)S(1)}, u32[]{:S(2)}, u32[]{:S(2)}) collective-permute-start(bf16[48,2048]{1,0:T(8,128)(2,1)S(1)} %get-tuple-element.22), channel_id=1, source_target_pairs={{0,6},{1,7},{2,4},{3,5},{4,2},{5,3},{6,0},{7,1},{8,14},{9,15},{10,... | collective-permute-start | bytes 589832 | tf_op jit(solution)/shard_map/ppermute | solution.py:17
  15.6 4.0 %load.1 = (bf16[1024,4096]{1,0:T(8,128)(2,1)S(1)}, f32[1,1024]{1,0:T(1,128)S(1)}) custom-call(bf16[1024,4096]{1,0:T(8,128)(2,1)} %refs_0_.6, bf16[48,2048]{1,0:T(8,128)(2,1)S(1)} %get-tuple-element.17.refs_1_.refs_0_), custom_call_target="tpu_custom_call" | custom-call | flops 10000000000 | bytes 16781312 | tf_op jit(solution)/shard_map/load/pallas_call | solution.py:36
  19.8 2.4 %collective-permute-done.6.refs_2_ = bf16[48,2048]{1,0:T(8,128)(2,1)S(1)} collective-permute-done((bf16[48,2048]{1,0:T(8,128)(2,1)S(1)}, bf16[48,2048]{1,0:T(8,128)(2,1)S(1)}, u32[]{:S(2)}, u32[]{:S(2)}) %collective-permute-start.6) | collective-permute-done | bytes 196640 | tf_op jit(solution)/shard_map/ppermute | solution.py:17
  22.2 1.6 %collective-permute-start.14 = (bf16[32,2048]{1,0:T(8,128)(2,1)S(1)}, bf16[32,2048]{1,0:T(8,128)(2,1)S(1)}, u32[]{:S(2)}, u32[]{:S(2)}) collective-permute-start(bf16[32,2048]{1,0:T(8,128)(2,1)S(1)} %get-tuple-element.25), channel_id=1, source_target_pairs={{0,8},{8,16},{16,24},{24,0},{1,9},{9,17},{17,25},{25,1},{2,10},{10... | collective-permute-start | bytes 393224 | tf_op jit(solution)/shard_map/ppermute | solution.py:294
  23.8 2.6 %collective-permute-start.15 = (bf16[32,2048]{1,0:T(8,128)(2,1)S(1)}, bf16[32,2048]{1,0:T(8,128)(2,1)S(1)}, u32[]{:S(2)}, u32[]{:S(2)}) collective-permute-start(bf16[32,2048]{1,0:T(8,128)(2,1)S(1)} %get-tuple-element.25), channel_id=1, source_target_pairs={{0,16},{8,24},{16,0},{24,8},{1,17},{9,25},{17,1},{25,9},{2,18},{10... | collective-permute-start | bytes 393224 | tf_op jit(solution)/shard_map/ppermute | solution.py:294
  26.4 1.5 %collective-permute-start.8 = (bf16[48,1024]{1,0:T(8,128)(2,1)S(1)}, bf16[48,1024]{1,0:T(8,128)(2,1)S(1)}, u32[]{:S(2)}, u32[]{:S(2)}) collective-permute-start(bf16[48,1024]{1,0:T(8,128)(2,1)S(1)} %get-tuple-element.23.refs_0_), channel_id=1, source_target_pairs={{0,2},{1,3},{2,0},{3,1},{4,6},{5,7},{6,4},{7,5},{8,10},{9,11},{10,... | collective-permute-start | bytes 294920 | tf_op jit(solution)/shard_map/ppermute | solution.py:17
  28.6 1.3 %collective-permute-start.16 = (bf16[32,2048]{1,0:T(8,128)(2,1)S(1)}, bf16[32,2048]{1,0:T(8,128)(2,1)S(1)}, u32[]{:S(2)}, u32[]{:S(2)}) collective-permute-start(bf16[32,2048]{1,0:T(8,128)(2,1)S(1)} %get-tuple-element.25), channel_id=1, source_target_pairs={{0,24},{8,0},{16,8},{24,16},{1,25},{9,1},{17,9},{25,17},{2,26},{10... | collective-permute-start | bytes 393224 | tf_op jit(solution)/shard_map/ppermute | solution.py:294
  30.0 1.7 %collective-permute-done.8.refs_2_ = bf16[48,1024]{1,0:T(8,128)(2,1)S(1)} collective-permute-done((bf16[48,1024]{1,0:T(8,128)(2,1)S(1)}, bf16[48,1024]{1,0:T(8,128)(2,1)S(1)}, u32[]{:S(2)}, u32[]{:S(2)}) %collective-permute-start.8) | collective-permute-done | bytes 98336 | tf_op jit(solution)/shard_map/ppermute | solution.py:17
  32.5 1.4 %collective-permute-start.13 = (bf16[48,1024]{1,0:T(8,128)(2,1)S(1)}, bf16[48,1024]{1,0:T(8,128)(2,1)S(1)}, u32[]{:S(2)}, u32[]{:S(2)}) collective-permute-start(bf16[48,1024]{1,0:T(8,128)(2,1)S(1)} %collective-permute-done.11.refs_5_), channel_id=1, source_target_pairs={{0,2},{1,3},{2,0},{3,1},{4,6},{5,7},{6,4},{7,5},{8,10},{9,11},{10,... | collective-permute-start | bytes 294920 | tf_op jit(solution)/shard_map/ppermute | solution.py:17
  34.6 1.2 %collective-permute-start.10 = (bf16[48,1024]{1,0:T(8,128)(2,1)S(1)}, bf16[48,1024]{1,0:T(8,128)(2,1)S(1)}, u32[]{:S(2)}, u32[]{:S(2)}) collective-permute-start(bf16[48,1024]{1,0:T(8,128)(2,1)S(1)} %get-tuple-element.23.refs_0_), channel_id=1, source_target_pairs={{0,4},{1,5},{2,6},{3,7},{4,0},{5,1},{6,2},{7,3},{8,12},{9,13},{10,... | collective-permute-start | bytes 294920 | tf_op jit(solution)/shard_map/ppermute | solution.py:17
  37.2 1.3 %collective-permute-done.9.refs_3_ = bf16[48,1024]{1,0:T(8,128)(2,1)S(1)} collective-permute-done((bf16[48,1024]{1,0:T(8,128)(2,1)S(1)}, bf16[48,1024]{1,0:T(8,128)(2,1)S(1)}, u32[]{:S(2)}, u32[]{:S(2)}) %collective-permute-start.9) | collective-permute-done | bytes 98336 | tf_op jit(solution)/shard_map/ppermute | solution.py:17
  39.3 1.4 %collective-permute-start.18 = (bf16[96,1024]{1,0:T(8,128)(2,1)S(1)}, bf16[96,1024]{1,0:T(8,128)(2,1)S(1)}, u32[]{:S(2)}, u32[]{:S(2)}) collective-permute-start(bf16[96,1024]{1,0:T(8,128)(2,1)S(1)} %stack.7.refs_8_), channel_id=1, source_target_pairs={{0,2},{1,3},{2,0},{3,1},{4,6},{5,7},{6,4},{7,5},{8,10},{9,11},{10,... | collective-permute-start | bytes 589832 | tf_op jit(solution)/shard_map/ppermute | solution.py:17
  40.8 1.5 %collective-permute-start.20 = (bf16[96,1024]{1,0:T(8,128)(2,1)S(1)}, bf16[96,1024]{1,0:T(8,128)(2,1)S(1)}, u32[]{:S(2)}, u32[]{:S(2)}) collective-permute-start(bf16[96,1024]{1,0:T(8,128)(2,1)S(1)} %stack.8.refs_9_), channel_id=1, source_target_pairs={{0,4},{1,5},{2,6},{3,7},{4,0},{5,1},{6,2},{7,3},{8,12},{9,13},{10,... | collective-permute-start | bytes 589832 | tf_op jit(solution)/shard_map/ppermute | solution.py:17
  43.5 3.3 %products.1 = (f32[1,1024]{1,0:T(1,128)}, f32[1,1024]{1,0:T(1,128)S(1)}) custom-call(bf16[1024,4096]{1,0:T(8,128)(2,1)S(1)} %get-tuple-element.18.refs_0_, f32[1,1024]{1,0:T(1,128)S(1)} %get-tuple-element.19.refs_4_.refs_1_, bf16[288,2048]{1,0:T(8,128)(2,1)S(1)} %stack.9.refs_2_, bf16[288,2048]{1,0:T(8,128)(2,1)S(1)} %collective-permute-done.17.refs_3_), custom_call_target="tpu_custom_call" | custom-call | flops 1000000000 | bytes 10760192 | tf_op jit(solution)/shard_map/products/pallas_call | solution.py:36
  47.1 1.4 %collective-permute-done.20.refs_0_.refs_7_ = bf16[96,1024]{1,0:T(8,128)(2,1)S(1)} collective-permute-done((bf16[96,1024]{1,0:T(8,128)(2,1)S(1)}, bf16[96,1024]{1,0:T(8,128)(2,1)S(1)}, u32[]{:S(2)}, u32[]{:S(2)}) %collective-permute-start.20) | collective-permute-done | bytes 196640 | tf_op jit(solution)/shard_map/ppermute | solution.py:17
  48.7 1.5 %collective-permute-start.26 = (bf16[112,1024]{1,0:T(8,128)(2,1)S(1)}, bf16[112,1024]{1,0:T(8,128)(2,1)S(1)}, u32[]{:S(2)}, u32[]{:S(2)}) collective-permute-start(bf16[112,1024]{1,0:T(8,128)(2,1)S(1)} %copy.11.refs_2_), channel_id=1, source_target_pairs={{0,4},{1,5},{2,6},{3,7},{4,0},{5,1},{6,2},{7,3},{8,12},{9,13},{10,... | collective-permute-start | bytes 688136 | tf_op jit(solution)/shard_map/ppermute | solution.py:17
  51.0 1.1 %collective-permute-done.23.refs_0_.refs_6_ = bf16[96,1024]{1,0:T(8,128)(2,1)S(1)} collective-permute-done((bf16[96,1024]{1,0:T(8,128)(2,1)S(1)}, bf16[96,1024]{1,0:T(8,128)(2,1)S(1)}, u32[]{:S(2)}, u32[]{:S(2)}) %collective-permute-start.23) | collective-permute-done | bytes 196640 | tf_op jit(solution)/shard_map/ppermute | solution.py:17
  53.9 3.0 %products_next.1.refs_3_.refs_1_.refs_2_ = f32[1,1024]{1,0:T(1,128)S(1)} custom-call(bf16[1024,4096]{1,0:T(8,128)(2,1)S(1)} %get-tuple-element.18.refs_0_, f32[1,1024]{1,0:T(1,128)S(1)} %get-tuple-element.27.refs_1_, bf16[96,1024]{1,0:T(8,128)(2,1)S(1)} %collective-permute-done.18.refs_0_.refs_2_, ...), custom_call_target="tpu_custom_call" | custom-call | bytes 9969664 | tf_op jit(solution)/shard_map/products_next/pallas_call | solution.py:36
  58.0 1.4 %products_half.1.refs_3_ = f32[96,1024]{1,0:T(8,128)S(1)} custom-call(bf16[1024,4096]{1,0:T(8,128)(2,1)S(1)} %get-tuple-element.18.refs_0_, bf16[112,1024]{1,0:T(8,128)(2,1)S(1)} %collective-permute-done.26.refs_1_.refs_0_, bf16[112,1024]{1,0:T(8,128)(2,1)S(1)} %collective-permute-done.27.refs_2_.refs_0_, f32[1,1024]{1,0:T(1,128)S(1)} %products_next.1.refs_3_.refs_1_.refs_2_), custom_call_target="tpu_custom_call" | custom-call | flops 10000000000 | bytes 9240576 | tf_op jit(solution)/shard_map/products_half/pallas_call | solution.py:36
  59.4 2.0 %products_last.1 = f32[1,1024]{1,0:T(1,128)} custom-call(bf16[1024,4096]{1,0:T(8,128)(2,1)S(1)} %get-tuple-element.18.refs_0_, f32[1,1024]{1,0:T(1,128)S(1)} %get-tuple-element.19.refs_4_.refs_1_, f32[1,1024]{1,0:T(1,128)S(1)} %products_next.1.refs_3_.refs_1_.refs_2_, f32[96,1024]{1,0:T(8,128)S(1)} %products_half.1.refs_3_, ...), custom_call_target="tpu_custom_call" | custom-call | flops 10000000000 | bytes 9187328 | tf_op jit(solution)/shard_map/products_last/pallas_call | solution.py:36
  (61 shorter events, 12.8 us)
Async XLA Ops:
  2.4 9.1 %collective-permute-start.4 = (bf16[64,2048]{1,0:T(8,128)(2,1)S(1)}, bf16[64,2048]{1,0:T(8,128)(2,1)S(1)}, u32[]{:S(2)}, u32[]{:S(2)}) collective-permute-start(bf16[64,2048]{1,0:T(8,128)(2,1)S(1)} %get-tuple-element.16), channel_id=1, source_target_pairs={{0,1},{1,0},{2,3},{3,2},{4,5},{5,4},{6,7},{7,6},{8,9},{9,8},{10,11... | collective-permute-start | bytes 786440 | tf_op jit(solution)/shard_map/ppermute | solution.py:17
  2.9 4.2 %collective-permute-start.1 = (s32[8,128]{1,0:T(8,128)S(1)}, s32[8,128]{1,0:T(8,128)S(1)}, u32[]{:S(2)}, u32[]{:S(2)}) collective-permute-start(s32[8,128]{1,0:T(8,128)S(1)} %pair.1.refs_1_), channel_id=1, source_target_pairs={{0,2},{1,3},{2,0},{3,1},{4,6},{5,7},{6,4},{7,5},{8,10},{9,11},{10,... | collective-permute-start | bytes 12296 | tf_op jit(solution)/shard_map/ppermute | solution.py:17
  5.5 3.6 %collective-permute-start.2 = (s32[8,128]{1,0:T(8,128)S(1)}, s32[8,128]{1,0:T(8,128)S(1)}, u32[]{:S(2)}, u32[]{:S(2)}) collective-permute-start(s32[8,128]{1,0:T(8,128)S(1)} %pair.1.refs_1_), channel_id=1, source_target_pairs={{0,4},{1,5},{2,6},{3,7},{4,0},{5,1},{6,2},{7,3},{8,12},{9,13},{10,... | collective-permute-start | bytes 12296 | tf_op jit(solution)/shard_map/ppermute | solution.py:17
  7.0 4.5 %collective-permute-start.3 = (s32[8,128]{1,0:T(8,128)S(1)}, s32[8,128]{1,0:T(8,128)S(1)}, u32[]{:S(2)}, u32[]{:S(2)}) collective-permute-start(s32[8,128]{1,0:T(8,128)S(1)} %pair.1.refs_1_), channel_id=1, source_target_pairs={{0,6},{1,7},{2,4},{3,5},{4,2},{5,3},{6,0},{7,1},{8,14},{9,15},{10,... | collective-permute-start | bytes 12296 | tf_op jit(solution)/shard_map/ppermute | solution.py:17
  12.1 7.7 %collective-permute-start.5 = (bf16[48,2048]{1,0:T(8,128)(2,1)S(1)}, bf16[48,2048]{1,0:T(8,128)(2,1)S(1)}, u32[]{:S(2)}, u32[]{:S(2)}) collective-permute-start(bf16[48,2048]{1,0:T(8,128)(2,1)S(1)} %get-tuple-element.20), channel_id=1, source_target_pairs={{0,2},{1,3},{2,0},{3,1},{4,6},{5,7},{6,4},{7,5},{8,10},{9,11},{10,... | collective-permute-start | bytes 589832 | tf_op jit(solution)/shard_map/ppermute | solution.py:17
  12.7 9.5 %collective-permute-start.6 = (bf16[48,2048]{1,0:T(8,128)(2,1)S(1)}, bf16[48,2048]{1,0:T(8,128)(2,1)S(1)}, u32[]{:S(2)}, u32[]{:S(2)}) collective-permute-start(bf16[48,2048]{1,0:T(8,128)(2,1)S(1)} %get-tuple-element.21), channel_id=1, source_target_pairs={{0,4},{1,5},{2,6},{3,7},{4,0},{5,1},{6,2},{7,3},{8,12},{9,13},{10,... | collective-permute-start | bytes 589832 | tf_op jit(solution)/shard_map/ppermute | solution.py:17
  12.7 9.4 %collective-permute-start.7 = (bf16[48,2048]{1,0:T(8,128)(2,1)S(1)}, bf16[48,2048]{1,0:T(8,128)(2,1)S(1)}, u32[]{:S(2)}, u32[]{:S(2)}) collective-permute-start(bf16[48,2048]{1,0:T(8,128)(2,1)S(1)} %get-tuple-element.22), channel_id=1, source_target_pairs={{0,6},{1,7},{2,4},{3,5},{4,2},{5,3},{6,0},{7,1},{8,14},{9,15},{10,... | collective-permute-start | bytes 589832 | tf_op jit(solution)/shard_map/ppermute | solution.py:17
  22.2 11.7 %collective-permute-start.14 = (bf16[32,2048]{1,0:T(8,128)(2,1)S(1)}, bf16[32,2048]{1,0:T(8,128)(2,1)S(1)}, u32[]{:S(2)}, u32[]{:S(2)}) collective-permute-start(bf16[32,2048]{1,0:T(8,128)(2,1)S(1)} %get-tuple-element.25), channel_id=1, source_target_pairs={{0,8},{8,16},{16,24},{24,0},{1,9},{9,17},{17,25},{25,1},{2,10},{10... | collective-permute-start | bytes 393224 | tf_op jit(solution)/shard_map/ppermute | solution.py:294
  23.8 10.7 %collective-permute-start.15 = (bf16[32,2048]{1,0:T(8,128)(2,1)S(1)}, bf16[32,2048]{1,0:T(8,128)(2,1)S(1)}, u32[]{:S(2)}, u32[]{:S(2)}) collective-permute-start(bf16[32,2048]{1,0:T(8,128)(2,1)S(1)} %get-tuple-element.25), channel_id=1, source_target_pairs={{0,16},{8,24},{16,0},{24,8},{1,17},{9,25},{17,1},{25,9},{2,18},{10... | collective-permute-start | bytes 393224 | tf_op jit(solution)/shard_map/ppermute | solution.py:294
  26.4 5.3 %collective-permute-start.8 = (bf16[48,1024]{1,0:T(8,128)(2,1)S(1)}, bf16[48,1024]{1,0:T(8,128)(2,1)S(1)}, u32[]{:S(2)}, u32[]{:S(2)}) collective-permute-start(bf16[48,1024]{1,0:T(8,128)(2,1)S(1)} %get-tuple-element.23.refs_0_), channel_id=1, source_target_pairs={{0,2},{1,3},{2,0},{3,1},{4,6},{5,7},{6,4},{7,5},{8,10},{9,11},{10,... | collective-permute-start | bytes 294920 | tf_op jit(solution)/shard_map/ppermute | solution.py:17
  27.9 4.6 %collective-permute-start.11 = (bf16[48,1024]{1,0:T(8,128)(2,1)S(1)}, bf16[48,1024]{1,0:T(8,128)(2,1)S(1)}, u32[]{:S(2)}, u32[]{:S(2)}) collective-permute-start(bf16[48,1024]{1,0:T(8,128)(2,1)S(1)} %get-tuple-element.24.refs_1_), channel_id=1, source_target_pairs={{0,4},{1,5},{2,6},{3,7},{4,0},{5,1},{6,2},{7,3},{8,12},{9,13},{10,... | collective-permute-start | bytes 294920 | tf_op jit(solution)/shard_map/ppermute | solution.py:17
  28.6 7.1 %collective-permute-start.16 = (bf16[32,2048]{1,0:T(8,128)(2,1)S(1)}, bf16[32,2048]{1,0:T(8,128)(2,1)S(1)}, u32[]{:S(2)}, u32[]{:S(2)}) collective-permute-start(bf16[32,2048]{1,0:T(8,128)(2,1)S(1)} %get-tuple-element.25), channel_id=1, source_target_pairs={{0,24},{8,0},{16,8},{24,16},{1,25},{9,1},{17,9},{25,17},{2,26},{10... | collective-permute-start | bytes 393224 | tf_op jit(solution)/shard_map/ppermute | solution.py:294
  31.7 4.6 %collective-permute-start.12 = (bf16[48,1024]{1,0:T(8,128)(2,1)S(1)}, bf16[48,1024]{1,0:T(8,128)(2,1)S(1)}, u32[]{:S(2)}, u32[]{:S(2)}) collective-permute-start(bf16[48,1024]{1,0:T(8,128)(2,1)S(1)} %collective-permute-done.8.refs_2_), channel_id=1, source_target_pairs={{0,4},{1,5},{2,6},{3,7},{4,0},{5,1},{6,2},{7,3},{8,12},{9,13},{10,... | collective-permute-start | bytes 294920 | tf_op jit(solution)/shard_map/ppermute | solution.py:17
  32.5 4.6 %collective-permute-start.13 = (bf16[48,1024]{1,0:T(8,128)(2,1)S(1)}, bf16[48,1024]{1,0:T(8,128)(2,1)S(1)}, u32[]{:S(2)}, u32[]{:S(2)}) collective-permute-start(bf16[48,1024]{1,0:T(8,128)(2,1)S(1)} %collective-permute-done.11.refs_5_), channel_id=1, source_target_pairs={{0,2},{1,3},{2,0},{3,1},{4,6},{5,7},{6,4},{7,5},{8,10},{9,11},{10,... | collective-permute-start | bytes 294920 | tf_op jit(solution)/shard_map/ppermute | solution.py:17
  33.9 4.6 %collective-permute-start.9 = (bf16[48,1024]{1,0:T(8,128)(2,1)S(1)}, bf16[48,1024]{1,0:T(8,128)(2,1)S(1)}, u32[]{:S(2)}, u32[]{:S(2)}) collective-permute-start(bf16[48,1024]{1,0:T(8,128)(2,1)S(1)} %get-tuple-element.24.refs_1_), channel_id=1, source_target_pairs={{0,2},{1,3},{2,0},{3,1},{4,6},{5,7},{6,4},{7,5},{8,10},{9,11},{10,... | collective-permute-start | bytes 294920 | tf_op jit(solution)/shard_map/ppermute | solution.py:17
  34.6 4.6 %collective-permute-start.10 = (bf16[48,1024]{1,0:T(8,128)(2,1)S(1)}, bf16[48,1024]{1,0:T(8,128)(2,1)S(1)}, u32[]{:S(2)}, u32[]{:S(2)}) collective-permute-start(bf16[48,1024]{1,0:T(8,128)(2,1)S(1)} %get-tuple-element.23.refs_0_), channel_id=1, source_target_pairs={{0,4},{1,5},{2,6},{3,7},{4,0},{5,1},{6,2},{7,3},{8,12},{9,13},{10,... | collective-permute-start | bytes 294920 | tf_op jit(solution)/shard_map/ppermute | solution.py:17
  39.3 4.2 %collective-permute-start.17 = (bf16[288,2048]{1,0:T(8,128)(2,1)S(1)}, bf16[288,2048]{1,0:T(8,128)(2,1)S(1)}, u32[]{:S(2)}, u32[]{:S(2)}) collective-permute-start(bf16[288,2048]{1,0:T(8,128)(2,1)S(1)} %stack.9.refs_2_), channel_id=1, source_target_pairs={{0,1},{1,0},{2,3},{3,2},{4,5},{5,4},{6,7},{7,6},{8,9},{9,8},{10,11... | collective-permute-start | bytes 3538952 | tf_op jit(solution)/shard_map/ppermute | solution.py:17
  39.3 7.8 %collective-permute-start.18 = (bf16[96,1024]{1,0:T(8,128)(2,1)S(1)}, bf16[96,1024]{1,0:T(8,128)(2,1)S(1)}, u32[]{:S(2)}, u32[]{:S(2)}) collective-permute-start(bf16[96,1024]{1,0:T(8,128)(2,1)S(1)} %stack.7.refs_8_), channel_id=1, source_target_pairs={{0,2},{1,3},{2,0},{3,1},{4,6},{5,7},{6,4},{7,5},{8,10},{9,11},{10,... | collective-permute-start | bytes 589832 | tf_op jit(solution)/shard_map/ppermute | solution.py:17
  40.8 7.7 %collective-permute-start.20 = (bf16[96,1024]{1,0:T(8,128)(2,1)S(1)}, bf16[96,1024]{1,0:T(8,128)(2,1)S(1)}, u32[]{:S(2)}, u32[]{:S(2)}) collective-permute-start(bf16[96,1024]{1,0:T(8,128)(2,1)S(1)} %stack.8.refs_9_), channel_id=1, source_target_pairs={{0,4},{1,5},{2,6},{3,7},{4,0},{5,1},{6,2},{7,3},{8,12},{9,13},{10,... | collective-permute-start | bytes 589832 | tf_op jit(solution)/shard_map/ppermute | solution.py:17
  42.3 8.6 %collective-permute-start.19 = (bf16[96,1024]{1,0:T(8,128)(2,1)S(1)}, bf16[96,1024]{1,0:T(8,128)(2,1)S(1)}, u32[]{:S(2)}, u32[]{:S(2)}) collective-permute-start(bf16[96,1024]{1,0:T(8,128)(2,1)S(1)} %stack.8.refs_9_), channel_id=1, source_target_pairs={{0,2},{1,3},{2,0},{3,1},{4,6},{5,7},{6,4},{7,5},{8,10},{9,11},{10,... | collective-permute-start | bytes 589832 | tf_op jit(solution)/shard_map/ppermute | solution.py:17
  42.6 9.5 %collective-permute-start.23 = (bf16[96,1024]{1,0:T(8,128)(2,1)S(1)}, bf16[96,1024]{1,0:T(8,128)(2,1)S(1)}, u32[]{:S(2)}, u32[]{:S(2)}) collective-permute-start(bf16[96,1024]{1,0:T(8,128)(2,1)S(1)} %stack.7.refs_8_), channel_id=1, source_target_pairs={{0,4},{1,5},{2,6},{3,7},{4,0},{5,1},{6,2},{7,3},{8,12},{9,13},{10,... | collective-permute-start | bytes 589832 | tf_op jit(solution)/shard_map/ppermute | solution.py:17
  48.6 3.7 %collective-permute-start.21 = (bf16[96,1024]{1,0:T(8,128)(2,1)S(1)}, bf16[96,1024]{1,0:T(8,128)(2,1)S(1)}, u32[]{:S(2)}, u32[]{:S(2)}) collective-permute-start(bf16[96,1024]{1,0:T(8,128)(2,1)S(1)} %stack.10), channel_id=1, source_target_pairs={{0,1},{1,0},{2,3},{3,2},{4,5},{5,4},{6,7},{7,6},{8,9},{9,8},{10,11... | collective-permute-start | bytes 589832 | tf_op jit(solution)/shard_map/ppermute | solution.py:17
  48.7 8.2 %collective-permute-start.26 = (bf16[112,1024]{1,0:T(8,128)(2,1)S(1)}, bf16[112,1024]{1,0:T(8,128)(2,1)S(1)}, u32[]{:S(2)}, u32[]{:S(2)}) collective-permute-start(bf16[112,1024]{1,0:T(8,128)(2,1)S(1)} %copy.11.refs_2_), channel_id=1, source_target_pairs={{0,4},{1,5},{2,6},{3,7},{4,0},{5,1},{6,2},{7,3},{8,12},{9,13},{10,... | collective-permute-start | bytes 688136 | tf_op jit(solution)/shard_map/ppermute | solution.py:17
  50.2 7.7 %collective-permute-start.27 = (bf16[112,1024]{1,0:T(8,128)(2,1)S(1)}, bf16[112,1024]{1,0:T(8,128)(2,1)S(1)}, u32[]{:S(2)}, u32[]{:S(2)}) collective-permute-start(bf16[112,1024]{1,0:T(8,128)(2,1)S(1)} %copy.12.refs_3_), channel_id=1, source_target_pairs={{0,2},{1,3},{2,0},{3,1},{4,6},{5,7},{6,4},{7,5},{8,10},{9,11},{10,... | collective-permute-start | bytes 688136 | tf_op jit(solution)/shard_map/ppermute | solution.py:17
  (8 other events, 20.9 us)

commit v20 on v17

--- a/solution.py
+++ b/solution.py
@@ -173,7 +173,7 @@
 
 
 def tiles_of(cand_ref):
-    return [slice(t, t + TILE) for t in range(0, cand_ref.shape[0], TILE)]
+    return [slice(t, t + 2 * TILE) for t in range(0, cand_ref.shape[0], 2 * TILE)]
 
 
 def lay_out(parts, rows_ref):

time: 57.5 us -> 57.5 us (level)
  no operation moved by 1% of the time
where the time goes in v20:
time: 57.5 us; the launch traced here: 57.3 us
  starting transfers between devices  26.1 us (45%)
  Pallas kernels  14.6 us (25%)
  waiting for transfers between devices  14.6 us (25%)
  between operations  1.48 us (3%)
    ppermute x25, starting transfers between devices, flip_permute(): return lax.ppermute(block, 'mem', [(m, m ^ flip) for m in range(size)])  20.6 us
    pallas_call x23, Pallas kernels, call(): pl.pallas_call(run, out_shape=out_shape, in_specs=(specs or vmem_specs(co...  14.6 us
    ppermute x25, waiting for transfers between devices, flip_permute(): return lax.ppermute(block, 'mem', [(m, m ^ flip) for m in range(size)])  10.7 us
    ppermute x3, starting transfers between devices, body(): lax.ppermute(picked, 'grp', [(g, (g + k) % groups) for g in range(groups)])  5.51 us
    ppermute x3, waiting for transfers between devices, body(): lax.ppermute(picked, 'grp', [(g, (g + k) % groups) for g in range(groups)])  3.91 us
  transfers between devices with their start and end apart: 28, of which 14 were waited for; matrix products, arithmetic and copies ran while one was open for 0% of the time, Pallas kernels for 21%

profile of v20, /device:TPU:0, one launch (start us, length us, event | category | flops | bytes accessed | tf_op | source)
XLA Modules:
  0.0 57.3 jit_solution(14635179028167402217)
XLA Ops:
  2.9 2.6 %collective-permute-start.1 = (s32[8,128]{1,0:T(8,128)S(1)}, s32[8,128]{1,0:T(8,128)S(1)}, u32[]{:S(2)}, u32[]{:S(2)}) collective-permute-start(s32[8,128]{1,0:T(8,128)S(1)} %pair.1.refs_1_), channel_id=1, source_target_pairs={{0,2},{1,3},{2,0},{3,1},{4,6},{5,7},{6,4},{7,5},{8,10},{9,11},{10,... | collective-permute-start | bytes 12296 | tf_op jit(solution)/shard_map/ppermute | solution.py:17
  5.5 1.5 %collective-permute-start.2 = (s32[8,128]{1,0:T(8,128)S(1)}, s32[8,128]{1,0:T(8,128)S(1)}, u32[]{:S(2)}, u32[]{:S(2)}) collective-permute-start(s32[8,128]{1,0:T(8,128)S(1)} %pair.1.refs_1_), channel_id=1, source_target_pairs={{0,4},{1,5},{2,6},{3,7},{4,0},{5,1},{6,2},{7,3},{8,12},{9,13},{10,... | collective-permute-start | bytes 12296 | tf_op jit(solution)/shard_map/ppermute | solution.py:17
  7.1 2.0 %collective-permute-done.2.refs_3_ = s32[8,128]{1,0:T(8,128)S(1)} collective-permute-done((s32[8,128]{1,0:T(8,128)S(1)}, s32[8,128]{1,0:T(8,128)S(1)}, u32[]{:S(2)}, u32[]{:S(2)}) %collective-permute-start.2) | collective-permute-done | bytes 4128 | tf_op jit(solution)/shard_map/ppermute | solution.py:17
  9.1 2.4 %collective-permute-done.3.refs_4_ = s32[8,128]{1,0:T(8,128)S(1)} collective-permute-done((s32[8,128]{1,0:T(8,128)S(1)}, s32[8,128]{1,0:T(8,128)S(1)}, u32[]{:S(2)}, u32[]{:S(2)}) %collective-permute-start.3) | collective-permute-done | bytes 4128 | tf_op jit(solution)/shard_map/ppermute | solution.py:17
  12.7 2.9 %collective-permute-start.7 = (bf16[48,2048]{1,0:T(8,128)(2,1)S(1)}, bf16[48,2048]{1,0:T(8,128)(2,1)S(1)}, u32[]{:S(2)}, u32[]{:S(2)}) collective-permute-start(bf16[48,2048]{1,0:T(8,128)(2,1)S(1)} %get-tuple-element.21), channel_id=1, source_target_pairs={{0,6},{1,7},{2,4},{3,5},{4,2},{5,3},{6,0},{7,1},{8,14},{9,15},{10,... | collective-permute-start | bytes 589832 | tf_op jit(solution)/shard_map/ppermute | solution.py:17
  15.6 4.0 %load.1 = (bf16[1024,4096]{1,0:T(8,128)(2,1)S(1)}, f32[1,1024]{1,0:T(1,128)S(1)}) custom-call(bf16[1024,4096]{1,0:T(8,128)(2,1)} %refs_0_.6, bf16[48,2048]{1,0:T(8,128)(2,1)S(1)} %get-tuple-element.16.refs_1_.refs_0_), custom_call_target="tpu_custom_call" | custom-call | flops 10000000000 | bytes 16781312 | tf_op jit(solution)/shard_map/load/pallas_call | solution.py:36
  19.8 2.4 %collective-permute-done.6.refs_2_ = bf16[48,2048]{1,0:T(8,128)(2,1)S(1)} collective-permute-done((bf16[48,2048]{1,0:T(8,128)(2,1)S(1)}, bf16[48,2048]{1,0:T(8,128)(2,1)S(1)}, u32[]{:S(2)}, u32[]{:S(2)}) %collective-permute-start.6) | collective-permute-done | bytes 196640 | tf_op jit(solution)/shard_map/ppermute | solution.py:17
  22.2 1.6 %collective-permute-start.8 = (bf16[48,2048]{1,0:T(8,128)(2,1)S(1)}, bf16[48,2048]{1,0:T(8,128)(2,1)S(1)}, u32[]{:S(2)}, u32[]{:S(2)}) collective-permute-start(bf16[48,2048]{1,0:T(8,128)(2,1)S(1)} %get-tuple-element.22.refs_0_), channel_id=1, source_target_pairs={{0,2},{1,3},{2,0},{3,1},{4,6},{5,7},{6,4},{7,5},{8,10},{9,11},{10,... | collective-permute-start | bytes 589832 | tf_op jit(solution)/shard_map/ppermute | solution.py:17
  24.5 1.6 %collective-permute-start.12 = (bf16[32,2048]{1,0:T(8,128)(2,1)S(1)}, bf16[32,2048]{1,0:T(8,128)(2,1)S(1)}, u32[]{:S(2)}, u32[]{:S(2)}) collective-permute-start(bf16[32,2048]{1,0:T(8,128)(2,1)S(1)} %get-tuple-element.23), channel_id=1, source_target_pairs={{0,8},{8,16},{16,24},{24,0},{1,9},{9,17},{17,25},{25,1},{2,10},{10... | collective-permute-start | bytes 393224 | tf_op jit(solution)/shard_map/ppermute | solution.py:291
  26.1 2.6 %collective-permute-start.13 = (bf16[32,2048]{1,0:T(8,128)(2,1)S(1)}, bf16[32,2048]{1,0:T(8,128)(2,1)S(1)}, u32[]{:S(2)}, u32[]{:S(2)}) collective-permute-start(bf16[32,2048]{1,0:T(8,128)(2,1)S(1)} %get-tuple-element.23), channel_id=1, source_target_pairs={{0,16},{8,24},{16,0},{24,8},{1,17},{9,25},{17,1},{25,9},{2,18},{10... | collective-permute-start | bytes 393224 | tf_op jit(solution)/shard_map/ppermute | solution.py:291
  28.6 1.3 %collective-permute-start.14 = (bf16[32,2048]{1,0:T(8,128)(2,1)S(1)}, bf16[32,2048]{1,0:T(8,128)(2,1)S(1)}, u32[]{:S(2)}, u32[]{:S(2)}) collective-permute-start(bf16[32,2048]{1,0:T(8,128)(2,1)S(1)} %get-tuple-element.23), channel_id=1, source_target_pairs={{0,24},{8,0},{16,8},{24,16},{1,25},{9,1},{17,9},{25,17},{2,26},{10... | collective-permute-start | bytes 393224 | tf_op jit(solution)/shard_map/ppermute | solution.py:291
  30.0 1.4 %collective-permute-start.10 = (bf16[48,1024]{1,0:T(8,128)(2,1)S(1)}, bf16[48,1024]{1,0:T(8,128)(2,1)S(1)}, u32[]{:S(2)}, u32[]{:S(2)}) collective-permute-start(bf16[48,1024]{1,0:T(8,128)(2,1)S(1)} %stack.9), channel_id=1, source_target_pairs={{0,4},{1,5},{2,6},{3,7},{4,0},{5,1},{6,2},{7,3},{8,12},{9,13},{10,... | collective-permute-start | bytes 294920 | tf_op jit(solution)/shard_map/ppermute | solution.py:17
  32.0 3.9 %collective-permute-done.13.refs_1_ = bf16[32,2048]{1,0:T(8,128)(2,1)S(1)} collective-permute-done((bf16[32,2048]{1,0:T(8,128)(2,1)S(1)}, bf16[32,2048]{1,0:T(8,128)(2,1)S(1)}, u32[]{:S(2)}, u32[]{:S(2)}) %collective-permute-start.13) | collective-permute-done | bytes 131104 | tf_op jit(solution)/shard_map/ppermute | solution.py:291
  36.3 0.8 %collective-permute-start.16 = (bf16[96,1024]{1,0:T(8,128)(2,1)S(1)}, bf16[96,1024]{1,0:T(8,128)(2,1)S(1)}, u32[]{:S(2)}, u32[]{:S(2)}) collective-permute-start(bf16[96,1024]{1,0:T(8,128)(2,1)S(1)} %stack.11.refs_5_), channel_id=1, source_target_pairs={{0,2},{1,3},{2,0},{3,1},{4,6},{5,7},{6,4},{7,5},{8,10},{9,11},{10,... | collective-permute-start | bytes 589832 | tf_op jit(solution)/shard_map/ppermute | solution.py:17
  37.0 1.0 %collective-permute-start.18 = (bf16[96,1024]{1,0:T(8,128)(2,1)S(1)}, bf16[96,1024]{1,0:T(8,128)(2,1)S(1)}, u32[]{:S(2)}, u32[]{:S(2)}) collective-permute-start(bf16[96,1024]{1,0:T(8,128)(2,1)S(1)} %stack.12.refs_6_), channel_id=1, source_target_pairs={{0,4},{1,5},{2,6},{3,7},{4,0},{5,1},{6,2},{7,3},{8,12},{9,13},{10,... | collective-permute-start | bytes 589832 | tf_op jit(solution)/shard_map/ppermute | solution.py:17
  38.1 1.0 %collective-permute-start.17 = (bf16[96,1024]{1,0:T(8,128)(2,1)S(1)}, bf16[96,1024]{1,0:T(8,128)(2,1)S(1)}, u32[]{:S(2)}, u32[]{:S(2)}) collective-permute-start(bf16[96,1024]{1,0:T(8,128)(2,1)S(1)} %stack.12.refs_6_), channel_id=1, source_target_pairs={{0,2},{1,3},{2,0},{3,1},{4,6},{5,7},{6,4},{7,5},{8,10},{9,11},{10,... | collective-permute-start | bytes 589832 | tf_op jit(solution)/shard_map/ppermute | solution.py:17
  39.1 1.3 %collective-permute-start.21 = (bf16[96,1024]{1,0:T(8,128)(2,1)S(1)}, bf16[96,1024]{1,0:T(8,128)(2,1)S(1)}, u32[]{:S(2)}, u32[]{:S(2)}) collective-permute-start(bf16[96,1024]{1,0:T(8,128)(2,1)S(1)} %stack.11.refs_5_), channel_id=1, source_target_pairs={{0,4},{1,5},{2,6},{3,7},{4,0},{5,1},{6,2},{7,3},{8,12},{9,13},{10,... | collective-permute-start | bytes 589832 | tf_op jit(solution)/shard_map/ppermute | solution.py:17
  40.4 3.3 %products.1 = (f32[1,1024]{1,0:T(1,128)}, f32[1,1024]{1,0:T(1,128)S(1)}) custom-call(bf16[1024,4096]{1,0:T(8,128)(2,1)S(1)} %get-tuple-element.17.refs_0_, f32[1,1024]{1,0:T(1,128)S(1)} %get-tuple-element.18.refs_4_.refs_1_, bf16[288,2048]{1,0:T(8,128)(2,1)S(1)} %stack.13.refs_2_, bf16[288,2048]{1,0:T(8,128)(2,1)S(1)} %collective-permute-done.15.refs_3_), custom_call_target="tpu_custom_call" | custom-call | flops 1000000000 | bytes 10760192 | tf_op jit(solution)/shard_map/products/pallas_call | solution.py:36
  44.9 1.1 %collective-permute-start.24 = (bf16[112,1024]{1,0:T(8,128)(2,1)S(1)}, bf16[112,1024]{1,0:T(8,128)(2,1)S(1)}, u32[]{:S(2)}, u32[]{:S(2)}) collective-permute-start(bf16[112,1024]{1,0:T(8,128)(2,1)S(1)} %copy.11.refs_2_), channel_id=1, source_target_pairs={{0,4},{1,5},{2,6},{3,7},{4,0},{5,1},{6,2},{7,3},{8,12},{9,13},{10,... | collective-permute-start | bytes 688136 | tf_op jit(solution)/shard_map/ppermute | solution.py:17
  46.0 1.0 %collective-permute-start.25 = (bf16[112,1024]{1,0:T(8,128)(2,1)S(1)}, bf16[112,1024]{1,0:T(8,128)(2,1)S(1)}, u32[]{:S(2)}, u32[]{:S(2)}) collective-permute-start(bf16[112,1024]{1,0:T(8,128)(2,1)S(1)} %copy.12.refs_3_), channel_id=1, source_target_pairs={{0,2},{1,3},{2,0},{3,1},{4,6},{5,7},{6,4},{7,5},{8,10},{9,11},{10,... | collective-permute-start | bytes 688136 | tf_op jit(solution)/shard_map/ppermute | solution.py:17
  47.0 0.8 %collective-permute-done.17.refs_0_.refs_3_ = bf16[96,1024]{1,0:T(8,128)(2,1)S(1)} collective-permute-done((bf16[96,1024]{1,0:T(8,128)(2,1)S(1)}, bf16[96,1024]{1,0:T(8,128)(2,1)S(1)}, u32[]{:S(2)}, u32[]{:S(2)}) %collective-permute-start.17) | collective-permute-done | bytes 196640 | tf_op jit(solution)/shard_map/ppermute | solution.py:17
  50.2 3.0 %products_next.1.refs_3_.refs_1_.refs_2_ = f32[1,1024]{1,0:T(1,128)S(1)} custom-call(bf16[1024,4096]{1,0:T(8,128)(2,1)S(1)} %get-tuple-element.17.refs_0_, f32[1,1024]{1,0:T(1,128)S(1)} %get-tuple-element.25.refs_1_, bf16[96,1024]{1,0:T(8,128)(2,1)S(1)} %collective-permute-done.16.refs_0_.refs_2_, ...), custom_call_target="tpu_custom_call" | custom-call | bytes 9969664 | tf_op jit(solution)/shard_map/products_next/pallas_call | solution.py:36
  53.8 1.4 %products_half.1.refs_3_ = f32[96,1024]{1,0:T(8,128)S(1)} custom-call(bf16[1024,4096]{1,0:T(8,128)(2,1)S(1)} %get-tuple-element.17.refs_0_, bf16[112,1024]{1,0:T(8,128)(2,1)S(1)} %collective-permute-done.24.refs_1_.refs_0_, bf16[112,1024]{1,0:T(8,128)(2,1)S(1)} %collective-permute-done.25.refs_2_.refs_0_, f32[1,1024]{1,0:T(1,128)S(1)} %products_next.1.refs_3_.refs_1_.refs_2_), custom_call_target="tpu_custom_call" | custom-call | flops 10000000000 | bytes 9240576 | tf_op jit(solution)/shard_map/products_half/pallas_call | solution.py:36
  55.3 2.0 %products_last.1 = f32[1,1024]{1,0:T(1,128)} custom-call(bf16[1024,4096]{1,0:T(8,128)(2,1)S(1)} %get-tuple-element.17.refs_0_, f32[1,1024]{1,0:T(1,128)S(1)} %get-tuple-element.18.refs_4_.refs_1_, f32[1,1024]{1,0:T(1,128)S(1)} %products_next.1.refs_3_.refs_1_.refs_2_, f32[96,1024]{1,0:T(8,128)S(1)} %products_half.1.refs_3_, ...), custom_call_target="tpu_custom_call" | custom-call | flops 10000000000 | bytes 9187328 | tf_op jit(solution)/shard_map/products_last/pallas_call | solution.py:36
  (59 shorter events, 9.0 us)
Async XLA Ops:
  2.4 9.1 %collective-permute-start.4 = (bf16[64,2048]{1,0:T(8,128)(2,1)S(1)}, bf16[64,2048]{1,0:T(8,128)(2,1)S(1)}, u32[]{:S(2)}, u32[]{:S(2)}) collective-permute-start(bf16[64,2048]{1,0:T(8,128)(2,1)S(1)} %get-tuple-element.15), channel_id=1, source_target_pairs={{0,1},{1,0},{2,3},{3,2},{4,5},{5,4},{6,7},{7,6},{8,9},{9,8},{10,11... | collective-permute-start | bytes 786440 | tf_op jit(solution)/shard_map/ppermute | solution.py:17
  2.9 4.2 %collective-permute-start.1 = (s32[8,128]{1,0:T(8,128)S(1)}, s32[8,128]{1,0:T(8,128)S(1)}, u32[]{:S(2)}, u32[]{:S(2)}) collective-permute-start(s32[8,128]{1,0:T(8,128)S(1)} %pair.1.refs_1_), channel_id=1, source_target_pairs={{0,2},{1,3},{2,0},{3,1},{4,6},{5,7},{6,4},{7,5},{8,10},{9,11},{10,... | collective-permute-start | bytes 12296 | tf_op jit(solution)/shard_map/ppermute | solution.py:17
  5.5 3.6 %collective-permute-start.2 = (s32[8,128]{1,0:T(8,128)S(1)}, s32[8,128]{1,0:T(8,128)S(1)}, u32[]{:S(2)}, u32[]{:S(2)}) collective-permute-start(s32[8,128]{1,0:T(8,128)S(1)} %pair.1.refs_1_), channel_id=1, source_target_pairs={{0,4},{1,5},{2,6},{3,7},{4,0},{5,1},{6,2},{7,3},{8,12},{9,13},{10,... | collective-permute-start | bytes 12296 | tf_op jit(solution)/shard_map/ppermute | solution.py:17
  7.0 4.5 %collective-permute-start.3 = (s32[8,128]{1,0:T(8,128)S(1)}, s32[8,128]{1,0:T(8,128)S(1)}, u32[]{:S(2)}, u32[]{:S(2)}) collective-permute-start(s32[8,128]{1,0:T(8,128)S(1)} %pair.1.refs_1_), channel_id=1, source_target_pairs={{0,6},{1,7},{2,4},{3,5},{4,2},{5,3},{6,0},{7,1},{8,14},{9,15},{10,... | collective-permute-start | bytes 12296 | tf_op jit(solution)/shard_map/ppermute | solution.py:17
  12.1 7.7 %collective-permute-start.5 = (bf16[48,2048]{1,0:T(8,128)(2,1)S(1)}, bf16[48,2048]{1,0:T(8,128)(2,1)S(1)}, u32[]{:S(2)}, u32[]{:S(2)}) collective-permute-start(bf16[48,2048]{1,0:T(8,128)(2,1)S(1)} %get-tuple-element.19), channel_id=1, source_target_pairs={{0,2},{1,3},{2,0},{3,1},{4,6},{5,7},{6,4},{7,5},{8,10},{9,11},{10,... | collective-permute-start | bytes 589832 | tf_op jit(solution)/shard_map/ppermute | solution.py:17
  12.7 9.5 %collective-permute-start.6 = (bf16[48,2048]{1,0:T(8,128)(2,1)S(1)}, bf16[48,2048]{1,0:T(8,128)(2,1)S(1)}, u32[]{:S(2)}, u32[]{:S(2)}) collective-permute-start(bf16[48,2048]{1,0:T(8,128)(2,1)S(1)} %get-tuple-element.20), channel_id=1, source_target_pairs={{0,4},{1,5},{2,6},{3,7},{4,0},{5,1},{6,2},{7,3},{8,12},{9,13},{10,... | collective-permute-start | bytes 589832 | tf_op jit(solution)/shard_map/ppermute | solution.py:17
  12.7 9.4 %collective-permute-start.7 = (bf16[48,2048]{1,0:T(8,128)(2,1)S(1)}, bf16[48,2048]{1,0:T(8,128)(2,1)S(1)}, u32[]{:S(2)}, u32[]{:S(2)}) collective-permute-start(bf16[48,2048]{1,0:T(8,128)(2,1)S(1)} %get-tuple-element.21), channel_id=1, source_target_pairs={{0,6},{1,7},{2,4},{3,5},{4,2},{5,3},{6,0},{7,1},{8,14},{9,15},{10,... | collective-permute-start | bytes 589832 | tf_op jit(solution)/shard_map/ppermute | solution.py:17
  22.2 7.8 %collective-permute-start.8 = (bf16[48,2048]{1,0:T(8,128)(2,1)S(1)}, bf16[48,2048]{1,0:T(8,128)(2,1)S(1)}, u32[]{:S(2)}, u32[]{:S(2)}) collective-permute-start(bf16[48,2048]{1,0:T(8,128)(2,1)S(1)} %get-tuple-element.22.refs_0_), channel_id=1, source_target_pairs={{0,2},{1,3},{2,0},{3,1},{4,6},{5,7},{6,4},{7,5},{8,10},{9,11},{10,... | collective-permute-start | bytes 589832 | tf_op jit(solution)/shard_map/ppermute | solution.py:17
  23.7 7.6 %collective-permute-start.9 = (bf16[48,2048]{1,0:T(8,128)(2,1)S(1)}, bf16[48,2048]{1,0:T(8,128)(2,1)S(1)}, u32[]{:S(2)}, u32[]{:S(2)}) collective-permute-start(bf16[48,2048]{1,0:T(8,128)(2,1)S(1)} %get-tuple-element.22.refs_0_), channel_id=1, source_target_pairs={{0,4},{1,5},{2,6},{3,7},{4,0},{5,1},{6,2},{7,3},{8,12},{9,13},{10,... | collective-permute-start | bytes 589832 | tf_op jit(solution)/shard_map/ppermute | solution.py:17
  24.5 7.5 %collective-permute-start.12 = (bf16[32,2048]{1,0:T(8,128)(2,1)S(1)}, bf16[32,2048]{1,0:T(8,128)(2,1)S(1)}, u32[]{:S(2)}, u32[]{:S(2)}) collective-permute-start(bf16[32,2048]{1,0:T(8,128)(2,1)S(1)} %get-tuple-element.23), channel_id=1, source_target_pairs={{0,8},{8,16},{16,24},{24,0},{1,9},{9,17},{17,25},{25,1},{2,10},{10... | collective-permute-start | bytes 393224 | tf_op jit(solution)/shard_map/ppermute | solution.py:291
  26.1 9.8 %collective-permute-start.13 = (bf16[32,2048]{1,0:T(8,128)(2,1)S(1)}, bf16[32,2048]{1,0:T(8,128)(2,1)S(1)}, u32[]{:S(2)}, u32[]{:S(2)}) collective-permute-start(bf16[32,2048]{1,0:T(8,128)(2,1)S(1)} %get-tuple-element.23), channel_id=1, source_target_pairs={{0,16},{8,24},{16,0},{24,8},{1,17},{9,25},{17,1},{25,9},{2,18},{10... | collective-permute-start | bytes 393224 | tf_op jit(solution)/shard_map/ppermute | solution.py:291
  28.6 7.2 %collective-permute-start.14 = (bf16[32,2048]{1,0:T(8,128)(2,1)S(1)}, bf16[32,2048]{1,0:T(8,128)(2,1)S(1)}, u32[]{:S(2)}, u32[]{:S(2)}) collective-permute-start(bf16[32,2048]{1,0:T(8,128)(2,1)S(1)} %get-tuple-element.23), channel_id=1, source_target_pairs={{0,24},{8,0},{16,8},{24,16},{1,25},{9,1},{17,9},{25,17},{2,26},{10... | collective-permute-start | bytes 393224 | tf_op jit(solution)/shard_map/ppermute | solution.py:291
  30.0 5.9 %collective-permute-start.10 = (bf16[48,1024]{1,0:T(8,128)(2,1)S(1)}, bf16[48,1024]{1,0:T(8,128)(2,1)S(1)}, u32[]{:S(2)}, u32[]{:S(2)}) collective-permute-start(bf16[48,1024]{1,0:T(8,128)(2,1)S(1)} %stack.9), channel_id=1, source_target_pairs={{0,4},{1,5},{2,6},{3,7},{4,0},{5,1},{6,2},{7,3},{8,12},{9,13},{10,... | collective-permute-start | bytes 294920 | tf_op jit(solution)/shard_map/ppermute | solution.py:17
  31.4 4.7 %collective-permute-start.11 = (bf16[48,1024]{1,0:T(8,128)(2,1)S(1)}, bf16[48,1024]{1,0:T(8,128)(2,1)S(1)}, u32[]{:S(2)}, u32[]{:S(2)}) collective-permute-start(bf16[48,1024]{1,0:T(8,128)(2,1)S(1)} %stack.10), channel_id=1, source_target_pairs={{0,2},{1,3},{2,0},{3,1},{4,6},{5,7},{6,4},{7,5},{8,10},{9,11},{10,... | collective-permute-start | bytes 294920 | tf_op jit(solution)/shard_map/ppermute | solution.py:17
  36.2 4.2 %collective-permute-start.15 = (bf16[288,2048]{1,0:T(8,128)(2,1)S(1)}, bf16[288,2048]{1,0:T(8,128)(2,1)S(1)}, u32[]{:S(2)}, u32[]{:S(2)}) collective-permute-start(bf16[288,2048]{1,0:T(8,128)(2,1)S(1)} %stack.13.refs_2_), channel_id=1, source_target_pairs={{0,1},{1,0},{2,3},{3,2},{4,5},{5,4},{6,7},{7,6},{8,9},{9,8},{10,11... | collective-permute-start | bytes 3538952 | tf_op jit(solution)/shard_map/ppermute | solution.py:17
  36.3 7.8 %collective-permute-start.16 = (bf16[96,1024]{1,0:T(8,128)(2,1)S(1)}, bf16[96,1024]{1,0:T(8,128)(2,1)S(1)}, u32[]{:S(2)}, u32[]{:S(2)}) collective-permute-start(bf16[96,1024]{1,0:T(8,128)(2,1)S(1)} %stack.11.refs_5_), channel_id=1, source_target_pairs={{0,2},{1,3},{2,0},{3,1},{4,6},{5,7},{6,4},{7,5},{8,10},{9,11},{10,... | collective-permute-start | bytes 589832 | tf_op jit(solution)/shard_map/ppermute | solution.py:17
  37.0 7.7 %collective-permute-start.18 = (bf16[96,1024]{1,0:T(8,128)(2,1)S(1)}, bf16[96,1024]{1,0:T(8,128)(2,1)S(1)}, u32[]{:S(2)}, u32[]{:S(2)}) collective-permute-start(bf16[96,1024]{1,0:T(8,128)(2,1)S(1)} %stack.12.refs_6_), channel_id=1, source_target_pairs={{0,4},{1,5},{2,6},{3,7},{4,0},{5,1},{6,2},{7,3},{8,12},{9,13},{10,... | collective-permute-start | bytes 589832 | tf_op jit(solution)/shard_map/ppermute | solution.py:17
  38.1 9.7 %collective-permute-start.17 = (bf16[96,1024]{1,0:T(8,128)(2,1)S(1)}, bf16[96,1024]{1,0:T(8,128)(2,1)S(1)}, u32[]{:S(2)}, u32[]{:S(2)}) collective-permute-start(bf16[96,1024]{1,0:T(8,128)(2,1)S(1)} %stack.12.refs_6_), channel_id=1, source_target_pairs={{0,2},{1,3},{2,0},{3,1},{4,6},{5,7},{6,4},{7,5},{8,10},{9,11},{10,... | collective-permute-start | bytes 589832 | tf_op jit(solution)/shard_map/ppermute | solution.py:17
  39.1 9.3 %collective-permute-start.21 = (bf16[96,1024]{1,0:T(8,128)(2,1)S(1)}, bf16[96,1024]{1,0:T(8,128)(2,1)S(1)}, u32[]{:S(2)}, u32[]{:S(2)}) collective-permute-start(bf16[96,1024]{1,0:T(8,128)(2,1)S(1)} %stack.11.refs_5_), channel_id=1, source_target_pairs={{0,4},{1,5},{2,6},{3,7},{4,0},{5,1},{6,2},{7,3},{8,12},{9,13},{10,... | collective-permute-start | bytes 589832 | tf_op jit(solution)/shard_map/ppermute | solution.py:17
  44.8 3.7 %collective-permute-start.19 = (bf16[96,1024]{1,0:T(8,128)(2,1)S(1)}, bf16[96,1024]{1,0:T(8,128)(2,1)S(1)}, u32[]{:S(2)}, u32[]{:S(2)}) collective-permute-start(bf16[96,1024]{1,0:T(8,128)(2,1)S(1)} %stack.14), channel_id=1, source_target_pairs={{0,1},{1,0},{2,3},{3,2},{4,5},{5,4},{6,7},{7,6},{8,9},{9,8},{10,11... | collective-permute-start | bytes 589832 | tf_op jit(solution)/shard_map/ppermute | solution.py:17
  44.9 8.2 %collective-permute-start.24 = (bf16[112,1024]{1,0:T(8,128)(2,1)S(1)}, bf16[112,1024]{1,0:T(8,128)(2,1)S(1)}, u32[]{:S(2)}, u32[]{:S(2)}) collective-permute-start(bf16[112,1024]{1,0:T(8,128)(2,1)S(1)} %copy.11.refs_2_), channel_id=1, source_target_pairs={{0,4},{1,5},{2,6},{3,7},{4,0},{5,1},{6,2},{7,3},{8,12},{9,13},{10,... | collective-permute-start | bytes 688136 | tf_op jit(solution)/shard_map/ppermute | solution.py:17
  46.0 7.7 %collective-permute-start.25 = (bf16[112,1024]{1,0:T(8,128)(2,1)S(1)}, bf16[112,1024]{1,0:T(8,128)(2,1)S(1)}, u32[]{:S(2)}, u32[]{:S(2)}) collective-permute-start(bf16[112,1024]{1,0:T(8,128)(2,1)S(1)} %copy.12.refs_3_), channel_id=1, source_target_pairs={{0,2},{1,3},{2,0},{3,1},{4,6},{5,7},{6,4},{7,5},{8,10},{9,11},{10,... | collective-permute-start | bytes 688136 | tf_op jit(solution)/shard_map/ppermute | solution.py:17
  48.5 1.7 %collective-permute-start.23 = (bf16[96,1024]{1,0:T(8,128)(2,1)S(1)}, bf16[96,1024]{1,0:T(8,128)(2,1)S(1)}, u32[]{:S(2)}, u32[]{:S(2)}) collective-permute-start(bf16[96,1024]{1,0:T(8,128)(2,1)S(1)} %stack.17), channel_id=1, source_target_pairs={{0,1},{1,0},{2,3},{3,2},{4,5},{5,4},{6,7},{7,6},{8,9},{9,8},{10,11... | collective-permute-start | bytes 589832 | tf_op jit(solution)/shard_map/ppermute | solution.py:17
  53.2 2.1 %collective-permute-start.26 = (bf16[96,1024]{1,0:T(8,128)(2,1)S(1)}, bf16[96,1024]{1,0:T(8,128)(2,1)S(1)}, u32[]{:S(2)}, u32[]{:S(2)}) collective-permute-start(bf16[96,1024]{1,0:T(8,128)(2,1)S(1)} %copy.13), channel_id=1, source_target_pairs={{0,1},{1,0},{2,3},{3,2},{4,5},{5,4},{6,7},{7,6},{8,9},{9,8},{10,11... | collective-permute-start | bytes 589832 | tf_op jit(solution)/shard_map/ppermute | solution.py:17
  (6 other events, 16.4 us)

commit v21 on v17

--- a/solution.py
+++ b/solution.py
@@ -289,7 +289,7 @@
 
     shifted = [
         lax.ppermute(picked, "grp", [(g, (g + k) % groups) for g in range(groups)])
-        for k in range(1, groups)
+        for k in sorted(range(1, groups), key=lambda k: abs(2 * k - groups))
     ]
 
     if chips == 4:

time: 57.5 us -> 58.4 us (1.016)
  starting transfers between devices: 26.1 us -> 27.1 us
    ppermute x3, waiting for transfers between devices: 3.91 us -> 2.98 us  [body(): lax.ppermute(picked, 'grp', [(g, (g + k) % groups) for g in range(groups)])]
    ppermute x3, starting transfers between devices: 5.51 us -> 6.41 us  [body(): lax.ppermute(picked, 'grp', [(g, (g + k) % groups) for g in range(groups)])]
    ppermute x25, waiting for transfers between devices: 10.7 us -> 11.5 us  [flip_permute(): return lax.ppermute(block, 'mem', [(m, m ^ flip) for m in range(size)])]
  transfers between devices with their start and end apart: 28 -> 28, of which waited for: 14 -> 15; matrix products, arithmetic and copies ran while one was open for 0% -> 0% of each run, Pallas kernels for 21% -> 20%
where the time goes in v21:
time: 58.4 us; the launch traced here: 58.1 us
  starting transfers between devices  27.1 us (46%)
  Pallas kernels  14.6 us (25%)
  waiting for transfers between devices  14.5 us (25%)
  between operations  1.48 us (3%)
    ppermute x25, starting transfers between devices, flip_permute(): return lax.ppermute(block, 'mem', [(m, m ^ flip) for m in range(size)])  20.7 us
    pallas_call x23, Pallas kernels, call(): pl.pallas_call(run, out_shape=out_shape, in_specs=(specs or vmem_specs(co...  14.6 us
    ppermute x25, waiting for transfers between devices, flip_permute(): return lax.ppermute(block, 'mem', [(m, m ^ flip) for m in range(size)])  11.5 us
    ppermute x3, starting transfers between devices, body(): lax.ppermute(picked, 'grp', [(g, (g + k) % groups) for g in range(groups)])  6.41 us
    ppermute x3, waiting for transfers between devices, body(): lax.ppermute(picked, 'grp', [(g, (g + k) % groups) for g in range(groups)])  2.98 us
  transfers between devices with their start and end apart: 28, of which 15 were waited for; matrix products, arithmetic and copies ran while one was open for 0% of the time, Pallas kernels for 20%

profile of v21, /device:TPU:0, one launch (start us, length us, event | category | flops | bytes accessed | tf_op | source)
XLA Modules:
  0.0 58.1 jit_solution(17092951777345639946)
XLA Ops:
  2.9 2.6 %collective-permute-start.1 = (s32[8,128]{1,0:T(8,128)S(1)}, s32[8,128]{1,0:T(8,128)S(1)}, u32[]{:S(2)}, u32[]{:S(2)}) collective-permute-start(s32[8,128]{1,0:T(8,128)S(1)} %pair.1.refs_1_), channel_id=1, source_target_pairs={{0,2},{1,3},{2,0},{3,1},{4,6},{5,7},{6,4},{7,5},{8,10},{9,11},{10,... | collective-permute-start | bytes 12296 | tf_op jit(solution)/shard_map/ppermute | solution.py:17
  5.5 1.5 %collective-permute-start.2 = (s32[8,128]{1,0:T(8,128)S(1)}, s32[8,128]{1,0:T(8,128)S(1)}, u32[]{:S(2)}, u32[]{:S(2)}) collective-permute-start(s32[8,128]{1,0:T(8,128)S(1)} %pair.1.refs_1_), channel_id=1, source_target_pairs={{0,4},{1,5},{2,6},{3,7},{4,0},{5,1},{6,2},{7,3},{8,12},{9,13},{10,... | collective-permute-start | bytes 12296 | tf_op jit(solution)/shard_map/ppermute | solution.py:17
  7.1 2.0 %collective-permute-done.2.refs_3_ = s32[8,128]{1,0:T(8,128)S(1)} collective-permute-done((s32[8,128]{1,0:T(8,128)S(1)}, s32[8,128]{1,0:T(8,128)S(1)}, u32[]{:S(2)}, u32[]{:S(2)}) %collective-permute-start.2) | collective-permute-done | bytes 4128 | tf_op jit(solution)/shard_map/ppermute | solution.py:17
  9.1 2.4 %collective-permute-done.3.refs_4_ = s32[8,128]{1,0:T(8,128)S(1)} collective-permute-done((s32[8,128]{1,0:T(8,128)S(1)}, s32[8,128]{1,0:T(8,128)S(1)}, u32[]{:S(2)}, u32[]{:S(2)}) %collective-permute-start.3) | collective-permute-done | bytes 4128 | tf_op jit(solution)/shard_map/ppermute | solution.py:17
  12.7 2.9 %collective-permute-start.7 = (bf16[48,2048]{1,0:T(8,128)(2,1)S(1)}, bf16[48,2048]{1,0:T(8,128)(2,1)S(1)}, u32[]{:S(2)}, u32[]{:S(2)}) collective-permute-start(bf16[48,2048]{1,0:T(8,128)(2,1)S(1)} %get-tuple-element.21), channel_id=1, source_target_pairs={{0,6},{1,7},{2,4},{3,5},{4,2},{5,3},{6,0},{7,1},{8,14},{9,15},{10,... | collective-permute-start | bytes 589832 | tf_op jit(solution)/shard_map/ppermute | solution.py:17
  15.6 4.0 %load.1 = (bf16[1024,4096]{1,0:T(8,128)(2,1)S(1)}, f32[1,1024]{1,0:T(1,128)S(1)}) custom-call(bf16[1024,4096]{1,0:T(8,128)(2,1)} %refs_0_.6, bf16[48,2048]{1,0:T(8,128)(2,1)S(1)} %get-tuple-element.16.refs_1_.refs_0_), custom_call_target="tpu_custom_call" | custom-call | flops 10000000000 | bytes 16781312 | tf_op jit(solution)/shard_map/load/pallas_call | solution.py:36
  19.8 2.4 %collective-permute-done.6.refs_2_ = bf16[48,2048]{1,0:T(8,128)(2,1)S(1)} collective-permute-done((bf16[48,2048]{1,0:T(8,128)(2,1)S(1)}, bf16[48,2048]{1,0:T(8,128)(2,1)S(1)}, u32[]{:S(2)}, u32[]{:S(2)}) %collective-permute-start.6) | collective-permute-done | bytes 196640 | tf_op jit(solution)/shard_map/ppermute | solution.py:17
  22.2 1.6 %collective-permute-start.8 = (bf16[48,2048]{1,0:T(8,128)(2,1)S(1)}, bf16[48,2048]{1,0:T(8,128)(2,1)S(1)}, u32[]{:S(2)}, u32[]{:S(2)}) collective-permute-start(bf16[48,2048]{1,0:T(8,128)(2,1)S(1)} %get-tuple-element.22.refs_0_), channel_id=1, source_target_pairs={{0,2},{1,3},{2,0},{3,1},{4,6},{5,7},{6,4},{7,5},{8,10},{9,11},{10,... | collective-permute-start | bytes 589832 | tf_op jit(solution)/shard_map/ppermute | solution.py:17
  24.5 2.6 %collective-permute-start.12 = (bf16[32,2048]{1,0:T(8,128)(2,1)S(1)}, bf16[32,2048]{1,0:T(8,128)(2,1)S(1)}, u32[]{:S(2)}, u32[]{:S(2)}) collective-permute-start(bf16[32,2048]{1,0:T(8,128)(2,1)S(1)} %get-tuple-element.23), channel_id=1, source_target_pairs={{0,16},{8,24},{16,0},{24,8},{1,17},{9,25},{17,1},{25,9},{2,18},{10... | collective-permute-start | bytes 393224 | tf_op jit(solution)/shard_map/ppermute | solution.py:291
  27.1 1.6 %collective-permute-start.13 = (bf16[32,2048]{1,0:T(8,128)(2,1)S(1)}, bf16[32,2048]{1,0:T(8,128)(2,1)S(1)}, u32[]{:S(2)}, u32[]{:S(2)}) collective-permute-start(bf16[32,2048]{1,0:T(8,128)(2,1)S(1)} %get-tuple-element.23), channel_id=1, source_target_pairs={{0,8},{8,16},{16,24},{24,0},{1,9},{9,17},{17,25},{25,1},{2,10},{10... | collective-permute-start | bytes 393224 | tf_op jit(solution)/shard_map/ppermute | solution.py:291
  28.6 2.2 %collective-permute-start.14 = (bf16[32,2048]{1,0:T(8,128)(2,1)S(1)}, bf16[32,2048]{1,0:T(8,128)(2,1)S(1)}, u32[]{:S(2)}, u32[]{:S(2)}) collective-permute-start(bf16[32,2048]{1,0:T(8,128)(2,1)S(1)} %get-tuple-element.23), channel_id=1, source_target_pairs={{0,24},{8,0},{16,8},{24,16},{1,25},{9,1},{17,9},{25,17},{2,26},{10... | collective-permute-start | bytes 393224 | tf_op jit(solution)/shard_map/ppermute | solution.py:291
  30.9 1.4 %collective-permute-start.10 = (bf16[48,1024]{1,0:T(8,128)(2,1)S(1)}, bf16[48,1024]{1,0:T(8,128)(2,1)S(1)}, u32[]{:S(2)}, u32[]{:S(2)}) collective-permute-start(bf16[48,1024]{1,0:T(8,128)(2,1)S(1)} %stack.9), channel_id=1, source_target_pairs={{0,4},{1,5},{2,6},{3,7},{4,0},{5,1},{6,2},{7,3},{8,12},{9,13},{10,... | collective-permute-start | bytes 294920 | tf_op jit(solution)/shard_map/ppermute | solution.py:17
  32.9 2.2 %collective-permute-done.12.refs_0_ = bf16[32,2048]{1,0:T(8,128)(2,1)S(1)} collective-permute-done((bf16[32,2048]{1,0:T(8,128)(2,1)S(1)}, bf16[32,2048]{1,0:T(8,128)(2,1)S(1)}, u32[]{:S(2)}, u32[]{:S(2)}) %collective-permute-start.12) | collective-permute-done | bytes 131104 | tf_op jit(solution)/shard_map/ppermute | solution.py:291
  35.9 1.1 %collective-permute-done.11.refs_4_ = bf16[48,1024]{1,0:T(8,128)(2,1)S(1)} collective-permute-done((bf16[48,1024]{1,0:T(8,128)(2,1)S(1)}, bf16[48,1024]{1,0:T(8,128)(2,1)S(1)}, u32[]{:S(2)}, u32[]{:S(2)}) %collective-permute-start.11) | collective-permute-done | bytes 98336 | tf_op jit(solution)/shard_map/ppermute | solution.py:17
  37.8 1.2 %collective-permute-start.18 = (bf16[96,1024]{1,0:T(8,128)(2,1)S(1)}, bf16[96,1024]{1,0:T(8,128)(2,1)S(1)}, u32[]{:S(2)}, u32[]{:S(2)}) collective-permute-start(bf16[96,1024]{1,0:T(8,128)(2,1)S(1)} %stack.12.refs_6_), channel_id=1, source_target_pairs={{0,4},{1,5},{2,6},{3,7},{4,0},{5,1},{6,2},{7,3},{8,12},{9,13},{10,... | collective-permute-start | bytes 589832 | tf_op jit(solution)/shard_map/ppermute | solution.py:17
  39.0 1.0 %collective-permute-start.17 = (bf16[96,1024]{1,0:T(8,128)(2,1)S(1)}, bf16[96,1024]{1,0:T(8,128)(2,1)S(1)}, u32[]{:S(2)}, u32[]{:S(2)}) collective-permute-start(bf16[96,1024]{1,0:T(8,128)(2,1)S(1)} %stack.12.refs_6_), channel_id=1, source_target_pairs={{0,2},{1,3},{2,0},{3,1},{4,6},{5,7},{6,4},{7,5},{8,10},{9,11},{10,... | collective-permute-start | bytes 589832 | tf_op jit(solution)/shard_map/ppermute | solution.py:17
  40.0 1.3 %collective-permute-start.21 = (bf16[96,1024]{1,0:T(8,128)(2,1)S(1)}, bf16[96,1024]{1,0:T(8,128)(2,1)S(1)}, u32[]{:S(2)}, u32[]{:S(2)}) collective-permute-start(bf16[96,1024]{1,0:T(8,128)(2,1)S(1)} %stack.11.refs_5_), channel_id=1, source_target_pairs={{0,4},{1,5},{2,6},{3,7},{4,0},{5,1},{6,2},{7,3},{8,12},{9,13},{10,... | collective-permute-start | bytes 589832 | tf_op jit(solution)/shard_map/ppermute | solution.py:17
  41.3 3.3 %products.1 = (f32[1,1024]{1,0:T(1,128)}, f32[1,1024]{1,0:T(1,128)S(1)}) custom-call(bf16[1024,4096]{1,0:T(8,128)(2,1)S(1)} %get-tuple-element.17.refs_0_, f32[1,1024]{1,0:T(1,128)S(1)} %get-tuple-element.18.refs_4_.refs_1_, bf16[288,2048]{1,0:T(8,128)(2,1)S(1)} %stack.13.refs_2_, bf16[288,2048]{1,0:T(8,128)(2,1)S(1)} %collective-permute-done.15.refs_3_), custom_call_target="tpu_custom_call" | custom-call | flops 1000000000 | bytes 10760192 | tf_op jit(solution)/shard_map/products/pallas_call | solution.py:36
  45.6 1.3 %collective-permute-start.24 = (bf16[112,1024]{1,0:T(8,128)(2,1)S(1)}, bf16[112,1024]{1,0:T(8,128)(2,1)S(1)}, u32[]{:S(2)}, u32[]{:S(2)}) collective-permute-start(bf16[112,1024]{1,0:T(8,128)(2,1)S(1)} %copy.11.refs_2_), channel_id=1, source_target_pairs={{0,4},{1,5},{2,6},{3,7},{4,0},{5,1},{6,2},{7,3},{8,12},{9,13},{10,... | collective-permute-start | bytes 688136 | tf_op jit(solution)/shard_map/ppermute | solution.py:17
  46.9 1.0 %collective-permute-start.25 = (bf16[112,1024]{1,0:T(8,128)(2,1)S(1)}, bf16[112,1024]{1,0:T(8,128)(2,1)S(1)}, u32[]{:S(2)}, u32[]{:S(2)}) collective-permute-start(bf16[112,1024]{1,0:T(8,128)(2,1)S(1)} %copy.12.refs_3_), channel_id=1, source_target_pairs={{0,2},{1,3},{2,0},{3,1},{4,6},{5,7},{6,4},{7,5},{8,10},{9,11},{10,... | collective-permute-start | bytes 688136 | tf_op jit(solution)/shard_map/ppermute | solution.py:17
  47.9 0.8 %collective-permute-done.17.refs_0_.refs_3_ = bf16[96,1024]{1,0:T(8,128)(2,1)S(1)} collective-permute-done((bf16[96,1024]{1,0:T(8,128)(2,1)S(1)}, bf16[96,1024]{1,0:T(8,128)(2,1)S(1)}, u32[]{:S(2)}, u32[]{:S(2)}) %collective-permute-start.17) | collective-permute-done | bytes 196640 | tf_op jit(solution)/shard_map/ppermute | solution.py:17
  50.9 2.9 %products_next.1.refs_3_.refs_1_.refs_2_ = f32[1,1024]{1,0:T(1,128)S(1)} custom-call(bf16[1024,4096]{1,0:T(8,128)(2,1)S(1)} %get-tuple-element.17.refs_0_, f32[1,1024]{1,0:T(1,128)S(1)} %get-tuple-element.25.refs_1_, bf16[96,1024]{1,0:T(8,128)(2,1)S(1)} %collective-permute-done.16.refs_0_.refs_2_, ...), custom_call_target="tpu_custom_call" | custom-call | bytes 9969664 | tf_op jit(solution)/shard_map/products_next/pallas_call | solution.py:36
  54.7 1.4 %products_half.1.refs_3_ = f32[96,1024]{1,0:T(8,128)S(1)} custom-call(bf16[1024,4096]{1,0:T(8,128)(2,1)S(1)} %get-tuple-element.17.refs_0_, bf16[112,1024]{1,0:T(8,128)(2,1)S(1)} %collective-permute-done.24.refs_1_.refs_0_, bf16[112,1024]{1,0:T(8,128)(2,1)S(1)} %collective-permute-done.25.refs_2_.refs_0_, f32[1,1024]{1,0:T(1,128)S(1)} %products_next.1.refs_3_.refs_1_.refs_2_), custom_call_target="tpu_custom_call" | custom-call | flops 10000000000 | bytes 9240576 | tf_op jit(solution)/shard_map/products_half/pallas_call | solution.py:36
  56.1 2.0 %products_last.1 = f32[1,1024]{1,0:T(1,128)} custom-call(bf16[1024,4096]{1,0:T(8,128)(2,1)S(1)} %get-tuple-element.17.refs_0_, f32[1,1024]{1,0:T(1,128)S(1)} %get-tuple-element.18.refs_4_.refs_1_, f32[1,1024]{1,0:T(1,128)S(1)} %products_next.1.refs_3_.refs_1_.refs_2_, f32[96,1024]{1,0:T(8,128)S(1)} %products_half.1.refs_3_, ...), custom_call_target="tpu_custom_call" | custom-call | flops 10000000000 | bytes 9187328 | tf_op jit(solution)/shard_map/products_last/pallas_call | solution.py:36
  (59 shorter events, 9.9 us)
Async XLA Ops:
  1.3 1.6 %collective-permute-start = (s32[8,128]{1,0:T(8,128)S(1)}, s32[8,128]{1,0:T(8,128)S(1)}, u32[]{:S(2)}, u32[]{:S(2)}) collective-permute-start(s32[8,128]{1,0:T(8,128)S(1)} %spread.1.refs_0_), channel_id=1, source_target_pairs={{0,1},{1,0},{2,3},{3,2},{4,5},{5,4},{6,7},{7,6},{8,9},{9,8},{10,11... | collective-permute-start | bytes 12296 | tf_op jit(solution)/shard_map/ppermute | solution.py:17
  2.4 9.1 %collective-permute-start.4 = (bf16[64,2048]{1,0:T(8,128)(2,1)S(1)}, bf16[64,2048]{1,0:T(8,128)(2,1)S(1)}, u32[]{:S(2)}, u32[]{:S(2)}) collective-permute-start(bf16[64,2048]{1,0:T(8,128)(2,1)S(1)} %get-tuple-element.15), channel_id=1, source_target_pairs={{0,1},{1,0},{2,3},{3,2},{4,5},{5,4},{6,7},{7,6},{8,9},{9,8},{10,11... | collective-permute-start | bytes 786440 | tf_op jit(solution)/shard_map/ppermute | solution.py:17
  2.9 4.2 %collective-permute-start.1 = (s32[8,128]{1,0:T(8,128)S(1)}, s32[8,128]{1,0:T(8,128)S(1)}, u32[]{:S(2)}, u32[]{:S(2)}) collective-permute-start(s32[8,128]{1,0:T(8,128)S(1)} %pair.1.refs_1_), channel_id=1, source_target_pairs={{0,2},{1,3},{2,0},{3,1},{4,6},{5,7},{6,4},{7,5},{8,10},{9,11},{10,... | collective-permute-start | bytes 12296 | tf_op jit(solution)/shard_map/ppermute | solution.py:17
  5.5 3.6 %collective-permute-start.2 = (s32[8,128]{1,0:T(8,128)S(1)}, s32[8,128]{1,0:T(8,128)S(1)}, u32[]{:S(2)}, u32[]{:S(2)}) collective-permute-start(s32[8,128]{1,0:T(8,128)S(1)} %pair.1.refs_1_), channel_id=1, source_target_pairs={{0,4},{1,5},{2,6},{3,7},{4,0},{5,1},{6,2},{7,3},{8,12},{9,13},{10,... | collective-permute-start | bytes 12296 | tf_op jit(solution)/shard_map/ppermute | solution.py:17
  7.0 4.5 %collective-permute-start.3 = (s32[8,128]{1,0:T(8,128)S(1)}, s32[8,128]{1,0:T(8,128)S(1)}, u32[]{:S(2)}, u32[]{:S(2)}) collective-permute-start(s32[8,128]{1,0:T(8,128)S(1)} %pair.1.refs_1_), channel_id=1, source_target_pairs={{0,6},{1,7},{2,4},{3,5},{4,2},{5,3},{6,0},{7,1},{8,14},{9,15},{10,... | collective-permute-start | bytes 12296 | tf_op jit(solution)/shard_map/ppermute | solution.py:17
  12.1 7.7 %collective-permute-start.5 = (bf16[48,2048]{1,0:T(8,128)(2,1)S(1)}, bf16[48,2048]{1,0:T(8,128)(2,1)S(1)}, u32[]{:S(2)}, u32[]{:S(2)}) collective-permute-start(bf16[48,2048]{1,0:T(8,128)(2,1)S(1)} %get-tuple-element.19), channel_id=1, source_target_pairs={{0,2},{1,3},{2,0},{3,1},{4,6},{5,7},{6,4},{7,5},{8,10},{9,11},{10,... | collective-permute-start | bytes 589832 | tf_op jit(solution)/shard_map/ppermute | solution.py:17
  12.7 9.5 %collective-permute-start.6 = (bf16[48,2048]{1,0:T(8,128)(2,1)S(1)}, bf16[48,2048]{1,0:T(8,128)(2,1)S(1)}, u32[]{:S(2)}, u32[]{:S(2)}) collective-permute-start(bf16[48,2048]{1,0:T(8,128)(2,1)S(1)} %get-tuple-element.20), channel_id=1, source_target_pairs={{0,4},{1,5},{2,6},{3,7},{4,0},{5,1},{6,2},{7,3},{8,12},{9,13},{10,... | collective-permute-start | bytes 589832 | tf_op jit(solution)/shard_map/ppermute | solution.py:17
  12.7 9.4 %collective-permute-start.7 = (bf16[48,2048]{1,0:T(8,128)(2,1)S(1)}, bf16[48,2048]{1,0:T(8,128)(2,1)S(1)}, u32[]{:S(2)}, u32[]{:S(2)}) collective-permute-start(bf16[48,2048]{1,0:T(8,128)(2,1)S(1)} %get-tuple-element.21), channel_id=1, source_target_pairs={{0,6},{1,7},{2,4},{3,5},{4,2},{5,3},{6,0},{7,1},{8,14},{9,15},{10,... | collective-permute-start | bytes 589832 | tf_op jit(solution)/shard_map/ppermute | solution.py:17
  22.2 8.7 %collective-permute-start.8 = (bf16[48,2048]{1,0:T(8,128)(2,1)S(1)}, bf16[48,2048]{1,0:T(8,128)(2,1)S(1)}, u32[]{:S(2)}, u32[]{:S(2)}) collective-permute-start(bf16[48,2048]{1,0:T(8,128)(2,1)S(1)} %get-tuple-element.22.refs_0_), channel_id=1, source_target_pairs={{0,2},{1,3},{2,0},{3,1},{4,6},{5,7},{6,4},{7,5},{8,10},{9,11},{10,... | collective-permute-start | bytes 589832 | tf_op jit(solution)/shard_map/ppermute | solution.py:17
  23.7 8.5 %collective-permute-start.9 = (bf16[48,2048]{1,0:T(8,128)(2,1)S(1)}, bf16[48,2048]{1,0:T(8,128)(2,1)S(1)}, u32[]{:S(2)}, u32[]{:S(2)}) collective-permute-start(bf16[48,2048]{1,0:T(8,128)(2,1)S(1)} %get-tuple-element.22.refs_0_), channel_id=1, source_target_pairs={{0,4},{1,5},{2,6},{3,7},{4,0},{5,1},{6,2},{7,3},{8,12},{9,13},{10,... | collective-permute-start | bytes 589832 | tf_op jit(solution)/shard_map/ppermute | solution.py:17
  24.5 10.6 %collective-permute-start.12 = (bf16[32,2048]{1,0:T(8,128)(2,1)S(1)}, bf16[32,2048]{1,0:T(8,128)(2,1)S(1)}, u32[]{:S(2)}, u32[]{:S(2)}) collective-permute-start(bf16[32,2048]{1,0:T(8,128)(2,1)S(1)} %get-tuple-element.23), channel_id=1, source_target_pairs={{0,16},{8,24},{16,0},{24,8},{1,17},{9,25},{17,1},{25,9},{2,18},{10... | collective-permute-start | bytes 393224 | tf_op jit(solution)/shard_map/ppermute | solution.py:291
  27.1 8.0 %collective-permute-start.13 = (bf16[32,2048]{1,0:T(8,128)(2,1)S(1)}, bf16[32,2048]{1,0:T(8,128)(2,1)S(1)}, u32[]{:S(2)}, u32[]{:S(2)}) collective-permute-start(bf16[32,2048]{1,0:T(8,128)(2,1)S(1)} %get-tuple-element.23), channel_id=1, source_target_pairs={{0,8},{8,16},{16,24},{24,0},{1,9},{9,17},{17,25},{25,1},{2,10},{10... | collective-permute-start | bytes 393224 | tf_op jit(solution)/shard_map/ppermute | solution.py:291
  28.6 7.2 %collective-permute-start.14 = (bf16[32,2048]{1,0:T(8,128)(2,1)S(1)}, bf16[32,2048]{1,0:T(8,128)(2,1)S(1)}, u32[]{:S(2)}, u32[]{:S(2)}) collective-permute-start(bf16[32,2048]{1,0:T(8,128)(2,1)S(1)} %get-tuple-element.23), channel_id=1, source_target_pairs={{0,24},{8,0},{16,8},{24,16},{1,25},{9,1},{17,9},{25,17},{2,26},{10... | collective-permute-start | bytes 393224 | tf_op jit(solution)/shard_map/ppermute | solution.py:291
  30.9 5.0 %collective-permute-start.10 = (bf16[48,1024]{1,0:T(8,128)(2,1)S(1)}, bf16[48,1024]{1,0:T(8,128)(2,1)S(1)}, u32[]{:S(2)}, u32[]{:S(2)}) collective-permute-start(bf16[48,1024]{1,0:T(8,128)(2,1)S(1)} %stack.9), channel_id=1, source_target_pairs={{0,4},{1,5},{2,6},{3,7},{4,0},{5,1},{6,2},{7,3},{8,12},{9,13},{10,... | collective-permute-start | bytes 294920 | tf_op jit(solution)/shard_map/ppermute | solution.py:17
  32.3 4.7 %collective-permute-start.11 = (bf16[48,1024]{1,0:T(8,128)(2,1)S(1)}, bf16[48,1024]{1,0:T(8,128)(2,1)S(1)}, u32[]{:S(2)}, u32[]{:S(2)}) collective-permute-start(bf16[48,1024]{1,0:T(8,128)(2,1)S(1)} %stack.10), channel_id=1, source_target_pairs={{0,2},{1,3},{2,0},{3,1},{4,6},{5,7},{6,4},{7,5},{8,10},{9,11},{10,... | collective-permute-start | bytes 294920 | tf_op jit(solution)/shard_map/ppermute | solution.py:17
  37.1 4.2 %collective-permute-start.15 = (bf16[288,2048]{1,0:T(8,128)(2,1)S(1)}, bf16[288,2048]{1,0:T(8,128)(2,1)S(1)}, u32[]{:S(2)}, u32[]{:S(2)}) collective-permute-start(bf16[288,2048]{1,0:T(8,128)(2,1)S(1)} %stack.13.refs_2_), channel_id=1, source_target_pairs={{0,1},{1,0},{2,3},{3,2},{4,5},{5,4},{6,7},{7,6},{8,9},{9,8},{10,11... | collective-permute-start | bytes 3538952 | tf_op jit(solution)/shard_map/ppermute | solution.py:17
  37.2 7.8 %collective-permute-start.16 = (bf16[96,1024]{1,0:T(8,128)(2,1)S(1)}, bf16[96,1024]{1,0:T(8,128)(2,1)S(1)}, u32[]{:S(2)}, u32[]{:S(2)}) collective-permute-start(bf16[96,1024]{1,0:T(8,128)(2,1)S(1)} %stack.11.refs_5_), channel_id=1, source_target_pairs={{0,2},{1,3},{2,0},{3,1},{4,6},{5,7},{6,4},{7,5},{8,10},{9,11},{10,... | collective-permute-start | bytes 589832 | tf_op jit(solution)/shard_map/ppermute | solution.py:17
  37.8 7.7 %collective-permute-start.18 = (bf16[96,1024]{1,0:T(8,128)(2,1)S(1)}, bf16[96,1024]{1,0:T(8,128)(2,1)S(1)}, u32[]{:S(2)}, u32[]{:S(2)}) collective-permute-start(bf16[96,1024]{1,0:T(8,128)(2,1)S(1)} %stack.12.refs_6_), channel_id=1, source_target_pairs={{0,4},{1,5},{2,6},{3,7},{4,0},{5,1},{6,2},{7,3},{8,12},{9,13},{10,... | collective-permute-start | bytes 589832 | tf_op jit(solution)/shard_map/ppermute | solution.py:17
  39.0 9.7 %collective-permute-start.17 = (bf16[96,1024]{1,0:T(8,128)(2,1)S(1)}, bf16[96,1024]{1,0:T(8,128)(2,1)S(1)}, u32[]{:S(2)}, u32[]{:S(2)}) collective-permute-start(bf16[96,1024]{1,0:T(8,128)(2,1)S(1)} %stack.12.refs_6_), channel_id=1, source_target_pairs={{0,2},{1,3},{2,0},{3,1},{4,6},{5,7},{6,4},{7,5},{8,10},{9,11},{10,... | collective-permute-start | bytes 589832 | tf_op jit(solution)/shard_map/ppermute | solution.py:17
  40.0 9.1 %collective-permute-start.21 = (bf16[96,1024]{1,0:T(8,128)(2,1)S(1)}, bf16[96,1024]{1,0:T(8,128)(2,1)S(1)}, u32[]{:S(2)}, u32[]{:S(2)}) collective-permute-start(bf16[96,1024]{1,0:T(8,128)(2,1)S(1)} %stack.11.refs_5_), channel_id=1, source_target_pairs={{0,4},{1,5},{2,6},{3,7},{4,0},{5,1},{6,2},{7,3},{8,12},{9,13},{10,... | collective-permute-start | bytes 589832 | tf_op jit(solution)/shard_map/ppermute | solution.py:17
  45.6 3.8 %collective-permute-start.19 = (bf16[96,1024]{1,0:T(8,128)(2,1)S(1)}, bf16[96,1024]{1,0:T(8,128)(2,1)S(1)}, u32[]{:S(2)}, u32[]{:S(2)}) collective-permute-start(bf16[96,1024]{1,0:T(8,128)(2,1)S(1)} %stack.14), channel_id=1, source_target_pairs={{0,1},{1,0},{2,3},{3,2},{4,5},{5,4},{6,7},{7,6},{8,9},{9,8},{10,11... | collective-permute-start | bytes 589832 | tf_op jit(solution)/shard_map/ppermute | solution.py:17
  45.6 8.2 %collective-permute-start.24 = (bf16[112,1024]{1,0:T(8,128)(2,1)S(1)}, bf16[112,1024]{1,0:T(8,128)(2,1)S(1)}, u32[]{:S(2)}, u32[]{:S(2)}) collective-permute-start(bf16[112,1024]{1,0:T(8,128)(2,1)S(1)} %copy.11.refs_2_), channel_id=1, source_target_pairs={{0,4},{1,5},{2,6},{3,7},{4,0},{5,1},{6,2},{7,3},{8,12},{9,13},{10,... | collective-permute-start | bytes 688136 | tf_op jit(solution)/shard_map/ppermute | solution.py:17
  46.9 7.7 %collective-permute-start.25 = (bf16[112,1024]{1,0:T(8,128)(2,1)S(1)}, bf16[112,1024]{1,0:T(8,128)(2,1)S(1)}, u32[]{:S(2)}, u32[]{:S(2)}) collective-permute-start(bf16[112,1024]{1,0:T(8,128)(2,1)S(1)} %copy.12.refs_3_), channel_id=1, source_target_pairs={{0,2},{1,3},{2,0},{3,1},{4,6},{5,7},{6,4},{7,5},{8,10},{9,11},{10,... | collective-permute-start | bytes 688136 | tf_op jit(solution)/shard_map/ppermute | solution.py:17
  53.9 2.2 %collective-permute-start.26 = (bf16[96,1024]{1,0:T(8,128)(2,1)S(1)}, bf16[96,1024]{1,0:T(8,128)(2,1)S(1)}, u32[]{:S(2)}, u32[]{:S(2)}) collective-permute-start(bf16[96,1024]{1,0:T(8,128)(2,1)S(1)} %copy.13), channel_id=1, source_target_pairs={{0,1},{1,0},{2,3},{3,2},{4,5},{5,4},{6,7},{7,6},{8,9},{9,8},{10,11... | collective-permute-start | bytes 589832 | tf_op jit(solution)/shard_map/ppermute | solution.py:17
  (6 other events, 16.2 us)

commit v22 on v17

--- a/solution.py
+++ b/solution.py
@@ -281,7 +281,7 @@
         specs=[pl.BlockSpec(memory_space=pltpu.HBM)], after=parts[:1],
         scratch=[pltpu.SemaphoreType.DMA((rows // TILE * 2,))], limit=42 * MIB,
     )
-    got = [flip_permute(parts[d], size, 2 * d) for d in range(1, chips)]
+    got = [flip_permute(parts[d], size, 2 * d) for d in range(chips - 1, 0, -1)]
     owned, picked = call(
         sum_kernel, "owned", [bf16(rows_chip, half), bf16(picks_chip, half)], (parts[0], *got),
         after=(norm,),

time: 57.5 us -> 59 us (1.026); the launches traced: 57.3 us -> 58.1 us
  transfers between devices with their start and end apart: 28 -> 28, of which waited for: 14 -> 12; matrix products, arithmetic and copies ran while one was open for 0% -> 0% of each run, Pallas kernels for 21% -> 20%
where the time goes in v22:
time: 59 us; the launch traced here: 58.1 us
  starting transfers between devices  26.3 us (45%)
  waiting for transfers between devices  15.2 us (26%)
  Pallas kernels  14.6 us (25%)
  between operations  1.49 us (3%)
    ppermute x25, starting transfers between devices, flip_permute(): return lax.ppermute(block, 'mem', [(m, m ^ flip) for m in range(size)])  20.8 us
    pallas_call x23, Pallas kernels, call(): pl.pallas_call(run, out_shape=out_shape, in_specs=(specs or vmem_specs(co...  14.6 us
    ppermute x25, waiting for transfers between devices, flip_permute(): return lax.ppermute(block, 'mem', [(m, m ^ flip) for m in range(size)])  11.2 us
    ppermute x3, starting transfers between devices, body(): lax.ppermute(picked, 'grp', [(g, (g + k) % groups) for g in range(groups)])  5.51 us
    ppermute x3, waiting for transfers between devices, body(): lax.ppermute(picked, 'grp', [(g, (g + k) % groups) for g in range(groups)])  3.98 us
  transfers between devices with their start and end apart: 28, of which 12 were waited for; matrix products, arithmetic and copies ran while one was open for 0% of the time, Pallas kernels for 20%

profile of v22, /device:TPU:0, one launch (start us, length us, event | category | flops | bytes accessed | tf_op | source)
XLA Modules:
  0.0 58.1 jit_solution(5262377150320173178)
XLA Ops:
  2.9 2.6 %collective-permute-start.1 = (s32[8,128]{1,0:T(8,128)S(1)}, s32[8,128]{1,0:T(8,128)S(1)}, u32[]{:S(2)}, u32[]{:S(2)}) collective-permute-start(s32[8,128]{1,0:T(8,128)S(1)} %pair.1.refs_1_), channel_id=1, source_target_pairs={{0,2},{1,3},{2,0},{3,1},{4,6},{5,7},{6,4},{7,5},{8,10},{9,11},{10,... | collective-permute-start | bytes 12296 | tf_op jit(solution)/shard_map/ppermute | solution.py:17
  5.5 1.5 %collective-permute-start.2 = (s32[8,128]{1,0:T(8,128)S(1)}, s32[8,128]{1,0:T(8,128)S(1)}, u32[]{:S(2)}, u32[]{:S(2)}) collective-permute-start(s32[8,128]{1,0:T(8,128)S(1)} %pair.1.refs_1_), channel_id=1, source_target_pairs={{0,4},{1,5},{2,6},{3,7},{4,0},{5,1},{6,2},{7,3},{8,12},{9,13},{10,... | collective-permute-start | bytes 12296 | tf_op jit(solution)/shard_map/ppermute | solution.py:17
  7.1 2.0 %collective-permute-done.2.refs_3_ = s32[8,128]{1,0:T(8,128)S(1)} collective-permute-done((s32[8,128]{1,0:T(8,128)S(1)}, s32[8,128]{1,0:T(8,128)S(1)}, u32[]{:S(2)}, u32[]{:S(2)}) %collective-permute-start.2) | collective-permute-done | bytes 4128 | tf_op jit(solution)/shard_map/ppermute | solution.py:17
  9.1 2.4 %collective-permute-done.3.refs_4_ = s32[8,128]{1,0:T(8,128)S(1)} collective-permute-done((s32[8,128]{1,0:T(8,128)S(1)}, s32[8,128]{1,0:T(8,128)S(1)}, u32[]{:S(2)}, u32[]{:S(2)}) %collective-permute-start.3) | collective-permute-done | bytes 4128 | tf_op jit(solution)/shard_map/ppermute | solution.py:17
  12.1 2.0 %collective-permute-start.6 = (bf16[48,2048]{1,0:T(8,128)(2,1)S(1)}, bf16[48,2048]{1,0:T(8,128)(2,1)S(1)}, u32[]{:S(2)}, u32[]{:S(2)}) collective-permute-start(bf16[48,2048]{1,0:T(8,128)(2,1)S(1)} %get-tuple-element.20), channel_id=1, source_target_pairs={{0,4},{1,5},{2,6},{3,7},{4,0},{5,1},{6,2},{7,3},{8,12},{9,13},{10,... | collective-permute-start | bytes 589832 | tf_op jit(solution)/shard_map/ppermute | solution.py:17
  14.1 1.5 %collective-permute-start.7 = (bf16[48,2048]{1,0:T(8,128)(2,1)S(1)}, bf16[48,2048]{1,0:T(8,128)(2,1)S(1)}, u32[]{:S(2)}, u32[]{:S(2)}) collective-permute-start(bf16[48,2048]{1,0:T(8,128)(2,1)S(1)} %get-tuple-element.21), channel_id=1, source_target_pairs={{0,2},{1,3},{2,0},{3,1},{4,6},{5,7},{6,4},{7,5},{8,10},{9,11},{10,... | collective-permute-start | bytes 589832 | tf_op jit(solution)/shard_map/ppermute | solution.py:17
  15.6 4.0 %load.1 = (bf16[1024,4096]{1,0:T(8,128)(2,1)S(1)}, f32[1,1024]{1,0:T(1,128)S(1)}) custom-call(bf16[1024,4096]{1,0:T(8,128)(2,1)} %refs_0_.6, bf16[48,2048]{1,0:T(8,128)(2,1)S(1)} %get-tuple-element.16.refs_1_.refs_0_), custom_call_target="tpu_custom_call" | custom-call | flops 10000000000 | bytes 16781312 | tf_op jit(solution)/shard_map/load/pallas_call | solution.py:36
  19.6 1.1 %collective-permute-done.5.refs_1_ = bf16[48,2048]{1,0:T(8,128)(2,1)S(1)} collective-permute-done((bf16[48,2048]{1,0:T(8,128)(2,1)S(1)}, bf16[48,2048]{1,0:T(8,128)(2,1)S(1)}, u32[]{:S(2)}, u32[]{:S(2)}) %collective-permute-start.5) | collective-permute-done | bytes 196640 | tf_op jit(solution)/shard_map/ppermute | solution.py:17
  20.7 1.2 %collective-permute-done.6.refs_2_ = bf16[48,2048]{1,0:T(8,128)(2,1)S(1)} collective-permute-done((bf16[48,2048]{1,0:T(8,128)(2,1)S(1)}, bf16[48,2048]{1,0:T(8,128)(2,1)S(1)}, u32[]{:S(2)}, u32[]{:S(2)}) %collective-permute-start.6) | collective-permute-done | bytes 196640 | tf_op jit(solution)/shard_map/ppermute | solution.py:17
  22.0 1.4 %collective-permute-start.8 = (bf16[48,2048]{1,0:T(8,128)(2,1)S(1)}, bf16[48,2048]{1,0:T(8,128)(2,1)S(1)}, u32[]{:S(2)}, u32[]{:S(2)}) collective-permute-start(bf16[48,2048]{1,0:T(8,128)(2,1)S(1)} %get-tuple-element.22.refs_0_), channel_id=1, source_target_pairs={{0,2},{1,3},{2,0},{3,1},{4,6},{5,7},{6,4},{7,5},{8,10},{9,11},{10,... | collective-permute-start | bytes 589832 | tf_op jit(solution)/shard_map/ppermute | solution.py:17
  24.0 1.6 %collective-permute-start.12 = (bf16[32,2048]{1,0:T(8,128)(2,1)S(1)}, bf16[32,2048]{1,0:T(8,128)(2,1)S(1)}, u32[]{:S(2)}, u32[]{:S(2)}) collective-permute-start(bf16[32,2048]{1,0:T(8,128)(2,1)S(1)} %get-tuple-element.23), channel_id=1, source_target_pairs={{0,8},{8,16},{16,24},{24,0},{1,9},{9,17},{17,25},{25,1},{2,10},{10... | collective-permute-start | bytes 393224 | tf_op jit(solution)/shard_map/ppermute | solution.py:291
  25.6 2.6 %collective-permute-start.13 = (bf16[32,2048]{1,0:T(8,128)(2,1)S(1)}, bf16[32,2048]{1,0:T(8,128)(2,1)S(1)}, u32[]{:S(2)}, u32[]{:S(2)}) collective-permute-start(bf16[32,2048]{1,0:T(8,128)(2,1)S(1)} %get-tuple-element.23), channel_id=1, source_target_pairs={{0,16},{8,24},{16,0},{24,8},{1,17},{9,25},{17,1},{25,9},{2,18},{10... | collective-permute-start | bytes 393224 | tf_op jit(solution)/shard_map/ppermute | solution.py:291
  28.2 1.3 %collective-permute-start.14 = (bf16[32,2048]{1,0:T(8,128)(2,1)S(1)}, bf16[32,2048]{1,0:T(8,128)(2,1)S(1)}, u32[]{:S(2)}, u32[]{:S(2)}) collective-permute-start(bf16[32,2048]{1,0:T(8,128)(2,1)S(1)} %get-tuple-element.23), channel_id=1, source_target_pairs={{0,24},{8,0},{16,8},{24,16},{1,25},{9,1},{17,9},{25,17},{2,26},{10... | collective-permute-start | bytes 393224 | tf_op jit(solution)/shard_map/ppermute | solution.py:291
  29.6 1.5 %collective-permute-start.10 = (bf16[48,1024]{1,0:T(8,128)(2,1)S(1)}, bf16[48,1024]{1,0:T(8,128)(2,1)S(1)}, u32[]{:S(2)}, u32[]{:S(2)}) collective-permute-start(bf16[48,1024]{1,0:T(8,128)(2,1)S(1)} %stack.9), channel_id=1, source_target_pairs={{0,4},{1,5},{2,6},{3,7},{4,0},{5,1},{6,2},{7,3},{8,12},{9,13},{10,... | collective-permute-start | bytes 294920 | tf_op jit(solution)/shard_map/ppermute | solution.py:17
  32.3 3.5 %collective-permute-done.13.refs_1_ = bf16[32,2048]{1,0:T(8,128)(2,1)S(1)} collective-permute-done((bf16[32,2048]{1,0:T(8,128)(2,1)S(1)}, bf16[32,2048]{1,0:T(8,128)(2,1)S(1)}, u32[]{:S(2)}, u32[]{:S(2)}) %collective-permute-start.13) | collective-permute-done | bytes 131104 | tf_op jit(solution)/shard_map/ppermute | solution.py:291
  36.1 1.7 %collective-permute-start.16 = (bf16[96,1024]{1,0:T(8,128)(2,1)S(1)}, bf16[96,1024]{1,0:T(8,128)(2,1)S(1)}, u32[]{:S(2)}, u32[]{:S(2)}) collective-permute-start(bf16[96,1024]{1,0:T(8,128)(2,1)S(1)} %stack.11.refs_5_), channel_id=1, source_target_pairs={{0,2},{1,3},{2,0},{3,1},{4,6},{5,7},{6,4},{7,5},{8,10},{9,11},{10,... | collective-permute-start | bytes 589832 | tf_op jit(solution)/shard_map/ppermute | solution.py:17
  38.3 1.6 %collective-permute-start.17 = (bf16[96,1024]{1,0:T(8,128)(2,1)S(1)}, bf16[96,1024]{1,0:T(8,128)(2,1)S(1)}, u32[]{:S(2)}, u32[]{:S(2)}) collective-permute-start(bf16[96,1024]{1,0:T(8,128)(2,1)S(1)} %stack.12.refs_6_), channel_id=1, source_target_pairs={{0,2},{1,3},{2,0},{3,1},{4,6},{5,7},{6,4},{7,5},{8,10},{9,11},{10,... | collective-permute-start | bytes 589832 | tf_op jit(solution)/shard_map/ppermute | solution.py:17
  40.2 3.3 %products.1 = (f32[1,1024]{1,0:T(1,128)}, f32[1,1024]{1,0:T(1,128)S(1)}) custom-call(bf16[1024,4096]{1,0:T(8,128)(2,1)S(1)} %get-tuple-element.17.refs_0_, f32[1,1024]{1,0:T(1,128)S(1)} %get-tuple-element.18.refs_4_.refs_1_, bf16[288,2048]{1,0:T(8,128)(2,1)S(1)} %stack.13.refs_2_, bf16[288,2048]{1,0:T(8,128)(2,1)S(1)} %collective-permute-done.15.refs_3_), custom_call_target="tpu_custom_call" | custom-call | flops 1000000000 | bytes 10760192 | tf_op jit(solution)/shard_map/products/pallas_call | solution.py:36
  43.9 1.7 %collective-permute-done.18.refs_0_.refs_7_ = bf16[96,1024]{1,0:T(8,128)(2,1)S(1)} collective-permute-done((bf16[96,1024]{1,0:T(8,128)(2,1)S(1)}, bf16[96,1024]{1,0:T(8,128)(2,1)S(1)}, u32[]{:S(2)}, u32[]{:S(2)}) %collective-permute-start.18) | collective-permute-done | bytes 196640 | tf_op jit(solution)/shard_map/ppermute | solution.py:17
  46.3 1.6 %collective-permute-start.25 = (bf16[112,1024]{1,0:T(8,128)(2,1)S(1)}, bf16[112,1024]{1,0:T(8,128)(2,1)S(1)}, u32[]{:S(2)}, u32[]{:S(2)}) collective-permute-start(bf16[112,1024]{1,0:T(8,128)(2,1)S(1)} %copy.12.refs_3_), channel_id=1, source_target_pairs={{0,2},{1,3},{2,0},{3,1},{4,6},{5,7},{6,4},{7,5},{8,10},{9,11},{10,... | collective-permute-start | bytes 688136 | tf_op jit(solution)/shard_map/ppermute | solution.py:17
  48.0 1.2 %collective-permute-done.21.refs_0_.refs_6_ = bf16[96,1024]{1,0:T(8,128)(2,1)S(1)} collective-permute-done((bf16[96,1024]{1,0:T(8,128)(2,1)S(1)}, bf16[96,1024]{1,0:T(8,128)(2,1)S(1)}, u32[]{:S(2)}, u32[]{:S(2)}) %collective-permute-start.21) | collective-permute-done | bytes 196640 | tf_op jit(solution)/shard_map/ppermute | solution.py:17
  51.0 3.0 %products_next.1.refs_3_.refs_1_.refs_2_ = f32[1,1024]{1,0:T(1,128)S(1)} custom-call(bf16[1024,4096]{1,0:T(8,128)(2,1)S(1)} %get-tuple-element.17.refs_0_, f32[1,1024]{1,0:T(1,128)S(1)} %get-tuple-element.25.refs_1_, bf16[96,1024]{1,0:T(8,128)(2,1)S(1)} %collective-permute-done.16.refs_0_.refs_2_, ...), custom_call_target="tpu_custom_call" | custom-call | bytes 9969664 | tf_op jit(solution)/shard_map/products_next/pallas_call | solution.py:36
  54.6 1.4 %products_half.1.refs_3_ = f32[96,1024]{1,0:T(8,128)S(1)} custom-call(bf16[1024,4096]{1,0:T(8,128)(2,1)S(1)} %get-tuple-element.17.refs_0_, bf16[112,1024]{1,0:T(8,128)(2,1)S(1)} %collective-permute-done.24.refs_1_.refs_0_, bf16[112,1024]{1,0:T(8,128)(2,1)S(1)} %collective-permute-done.25.refs_2_.refs_0_, f32[1,1024]{1,0:T(1,128)S(1)} %products_next.1.refs_3_.refs_1_.refs_2_), custom_call_target="tpu_custom_call" | custom-call | flops 10000000000 | bytes 9240576 | tf_op jit(solution)/shard_map/products_half/pallas_call | solution.py:36
  56.1 2.0 %products_last.1 = f32[1,1024]{1,0:T(1,128)} custom-call(bf16[1024,4096]{1,0:T(8,128)(2,1)S(1)} %get-tuple-element.17.refs_0_, f32[1,1024]{1,0:T(1,128)S(1)} %get-tuple-element.18.refs_4_.refs_1_, f32[1,1024]{1,0:T(1,128)S(1)} %products_next.1.refs_3_.refs_1_.refs_2_, f32[96,1024]{1,0:T(8,128)S(1)} %products_half.1.refs_3_, ...), custom_call_target="tpu_custom_call" | custom-call | flops 10000000000 | bytes 9187328 | tf_op jit(solution)/shard_map/products_last/pallas_call | solution.py:36
  (59 shorter events, 8.8 us)
Async XLA Ops:
  2.4 9.1 %collective-permute-start.4 = (bf16[64,2048]{1,0:T(8,128)(2,1)S(1)}, bf16[64,2048]{1,0:T(8,128)(2,1)S(1)}, u32[]{:S(2)}, u32[]{:S(2)}) collective-permute-start(bf16[64,2048]{1,0:T(8,128)(2,1)S(1)} %get-tuple-element.15), channel_id=1, source_target_pairs={{0,1},{1,0},{2,3},{3,2},{4,5},{5,4},{6,7},{7,6},{8,9},{9,8},{10,11... | collective-permute-start | bytes 786440 | tf_op jit(solution)/shard_map/ppermute | solution.py:17
  2.9 4.2 %collective-permute-start.1 = (s32[8,128]{1,0:T(8,128)S(1)}, s32[8,128]{1,0:T(8,128)S(1)}, u32[]{:S(2)}, u32[]{:S(2)}) collective-permute-start(s32[8,128]{1,0:T(8,128)S(1)} %pair.1.refs_1_), channel_id=1, source_target_pairs={{0,2},{1,3},{2,0},{3,1},{4,6},{5,7},{6,4},{7,5},{8,10},{9,11},{10,... | collective-permute-start | bytes 12296 | tf_op jit(solution)/shard_map/ppermute | solution.py:17
  5.5 3.6 %collective-permute-start.2 = (s32[8,128]{1,0:T(8,128)S(1)}, s32[8,128]{1,0:T(8,128)S(1)}, u32[]{:S(2)}, u32[]{:S(2)}) collective-permute-start(s32[8,128]{1,0:T(8,128)S(1)} %pair.1.refs_1_), channel_id=1, source_target_pairs={{0,4},{1,5},{2,6},{3,7},{4,0},{5,1},{6,2},{7,3},{8,12},{9,13},{10,... | collective-permute-start | bytes 12296 | tf_op jit(solution)/shard_map/ppermute | solution.py:17
  7.0 4.5 %collective-permute-start.3 = (s32[8,128]{1,0:T(8,128)S(1)}, s32[8,128]{1,0:T(8,128)S(1)}, u32[]{:S(2)}, u32[]{:S(2)}) collective-permute-start(s32[8,128]{1,0:T(8,128)S(1)} %pair.1.refs_1_), channel_id=1, source_target_pairs={{0,6},{1,7},{2,4},{3,5},{4,2},{5,3},{6,0},{7,1},{8,14},{9,15},{10,... | collective-permute-start | bytes 12296 | tf_op jit(solution)/shard_map/ppermute | solution.py:17
  12.1 8.7 %collective-permute-start.5 = (bf16[48,2048]{1,0:T(8,128)(2,1)S(1)}, bf16[48,2048]{1,0:T(8,128)(2,1)S(1)}, u32[]{:S(2)}, u32[]{:S(2)}) collective-permute-start(bf16[48,2048]{1,0:T(8,128)(2,1)S(1)} %get-tuple-element.19), channel_id=1, source_target_pairs={{0,6},{1,7},{2,4},{3,5},{4,2},{5,3},{6,0},{7,1},{8,14},{9,15},{10,... | collective-permute-start | bytes 589832 | tf_op jit(solution)/shard_map/ppermute | solution.py:17
  12.1 9.8 %collective-permute-start.6 = (bf16[48,2048]{1,0:T(8,128)(2,1)S(1)}, bf16[48,2048]{1,0:T(8,128)(2,1)S(1)}, u32[]{:S(2)}, u32[]{:S(2)}) collective-permute-start(bf16[48,2048]{1,0:T(8,128)(2,1)S(1)} %get-tuple-element.20), channel_id=1, source_target_pairs={{0,4},{1,5},{2,6},{3,7},{4,0},{5,1},{6,2},{7,3},{8,12},{9,13},{10,... | collective-permute-start | bytes 589832 | tf_op jit(solution)/shard_map/ppermute | solution.py:17
  14.1 7.8 %collective-permute-start.7 = (bf16[48,2048]{1,0:T(8,128)(2,1)S(1)}, bf16[48,2048]{1,0:T(8,128)(2,1)S(1)}, u32[]{:S(2)}, u32[]{:S(2)}) collective-permute-start(bf16[48,2048]{1,0:T(8,128)(2,1)S(1)} %get-tuple-element.21), channel_id=1, source_target_pairs={{0,2},{1,3},{2,0},{3,1},{4,6},{5,7},{6,4},{7,5},{8,10},{9,11},{10,... | collective-permute-start | bytes 589832 | tf_op jit(solution)/shard_map/ppermute | solution.py:17
  22.0 7.5 %collective-permute-start.8 = (bf16[48,2048]{1,0:T(8,128)(2,1)S(1)}, bf16[48,2048]{1,0:T(8,128)(2,1)S(1)}, u32[]{:S(2)}, u32[]{:S(2)}) collective-permute-start(bf16[48,2048]{1,0:T(8,128)(2,1)S(1)} %get-tuple-element.22.refs_0_), channel_id=1, source_target_pairs={{0,2},{1,3},{2,0},{3,1},{4,6},{5,7},{6,4},{7,5},{8,10},{9,11},{10,... | collective-permute-start | bytes 589832 | tf_op jit(solution)/shard_map/ppermute | solution.py:17
  23.4 7.6 %collective-permute-start.9 = (bf16[48,2048]{1,0:T(8,128)(2,1)S(1)}, bf16[48,2048]{1,0:T(8,128)(2,1)S(1)}, u32[]{:S(2)}, u32[]{:S(2)}) collective-permute-start(bf16[48,2048]{1,0:T(8,128)(2,1)S(1)} %get-tuple-element.22.refs_0_), channel_id=1, source_target_pairs={{0,4},{1,5},{2,6},{3,7},{4,0},{5,1},{6,2},{7,3},{8,12},{9,13},{10,... | collective-permute-start | bytes 589832 | tf_op jit(solution)/shard_map/ppermute | solution.py:17
  24.0 8.3 %collective-permute-start.12 = (bf16[32,2048]{1,0:T(8,128)(2,1)S(1)}, bf16[32,2048]{1,0:T(8,128)(2,1)S(1)}, u32[]{:S(2)}, u32[]{:S(2)}) collective-permute-start(bf16[32,2048]{1,0:T(8,128)(2,1)S(1)} %get-tuple-element.23), channel_id=1, source_target_pairs={{0,8},{8,16},{16,24},{24,0},{1,9},{9,17},{17,25},{25,1},{2,10},{10... | collective-permute-start | bytes 393224 | tf_op jit(solution)/shard_map/ppermute | solution.py:291
  25.6 10.2 %collective-permute-start.13 = (bf16[32,2048]{1,0:T(8,128)(2,1)S(1)}, bf16[32,2048]{1,0:T(8,128)(2,1)S(1)}, u32[]{:S(2)}, u32[]{:S(2)}) collective-permute-start(bf16[32,2048]{1,0:T(8,128)(2,1)S(1)} %get-tuple-element.23), channel_id=1, source_target_pairs={{0,16},{8,24},{16,0},{24,8},{1,17},{9,25},{17,1},{25,9},{2,18},{10... | collective-permute-start | bytes 393224 | tf_op jit(solution)/shard_map/ppermute | solution.py:291
  28.2 7.7 %collective-permute-start.14 = (bf16[32,2048]{1,0:T(8,128)(2,1)S(1)}, bf16[32,2048]{1,0:T(8,128)(2,1)S(1)}, u32[]{:S(2)}, u32[]{:S(2)}) collective-permute-start(bf16[32,2048]{1,0:T(8,128)(2,1)S(1)} %get-tuple-element.23), channel_id=1, source_target_pairs={{0,24},{8,0},{16,8},{24,16},{1,25},{9,1},{17,9},{25,17},{2,26},{10... | collective-permute-start | bytes 393224 | tf_op jit(solution)/shard_map/ppermute | solution.py:291
  29.6 6.3 %collective-permute-start.10 = (bf16[48,1024]{1,0:T(8,128)(2,1)S(1)}, bf16[48,1024]{1,0:T(8,128)(2,1)S(1)}, u32[]{:S(2)}, u32[]{:S(2)}) collective-permute-start(bf16[48,1024]{1,0:T(8,128)(2,1)S(1)} %stack.9), channel_id=1, source_target_pairs={{0,4},{1,5},{2,6},{3,7},{4,0},{5,1},{6,2},{7,3},{8,12},{9,13},{10,... | collective-permute-start | bytes 294920 | tf_op jit(solution)/shard_map/ppermute | solution.py:17
  31.1 4.8 %collective-permute-start.11 = (bf16[48,1024]{1,0:T(8,128)(2,1)S(1)}, bf16[48,1024]{1,0:T(8,128)(2,1)S(1)}, u32[]{:S(2)}, u32[]{:S(2)}) collective-permute-start(bf16[48,1024]{1,0:T(8,128)(2,1)S(1)} %stack.10), channel_id=1, source_target_pairs={{0,2},{1,3},{2,0},{3,1},{4,6},{5,7},{6,4},{7,5},{8,10},{9,11},{10,... | collective-permute-start | bytes 294920 | tf_op jit(solution)/shard_map/ppermute | solution.py:17
  36.0 4.2 %collective-permute-start.15 = (bf16[288,2048]{1,0:T(8,128)(2,1)S(1)}, bf16[288,2048]{1,0:T(8,128)(2,1)S(1)}, u32[]{:S(2)}, u32[]{:S(2)}) collective-permute-start(bf16[288,2048]{1,0:T(8,128)(2,1)S(1)} %stack.13.refs_2_), channel_id=1, source_target_pairs={{0,1},{1,0},{2,3},{3,2},{4,5},{5,4},{6,7},{7,6},{8,9},{9,8},{10,11... | collective-permute-start | bytes 3538952 | tf_op jit(solution)/shard_map/ppermute | solution.py:17
  36.1 7.8 %collective-permute-start.16 = (bf16[96,1024]{1,0:T(8,128)(2,1)S(1)}, bf16[96,1024]{1,0:T(8,128)(2,1)S(1)}, u32[]{:S(2)}, u32[]{:S(2)}) collective-permute-start(bf16[96,1024]{1,0:T(8,128)(2,1)S(1)} %stack.11.refs_5_), channel_id=1, source_target_pairs={{0,2},{1,3},{2,0},{3,1},{4,6},{5,7},{6,4},{7,5},{8,10},{9,11},{10,... | collective-permute-start | bytes 589832 | tf_op jit(solution)/shard_map/ppermute | solution.py:17
  37.9 7.7 %collective-permute-start.18 = (bf16[96,1024]{1,0:T(8,128)(2,1)S(1)}, bf16[96,1024]{1,0:T(8,128)(2,1)S(1)}, u32[]{:S(2)}, u32[]{:S(2)}) collective-permute-start(bf16[96,1024]{1,0:T(8,128)(2,1)S(1)} %stack.12.refs_6_), channel_id=1, source_target_pairs={{0,4},{1,5},{2,6},{3,7},{4,0},{5,1},{6,2},{7,3},{8,12},{9,13},{10,... | collective-permute-start | bytes 589832 | tf_op jit(solution)/shard_map/ppermute | solution.py:17
  38.3 9.5 %collective-permute-start.17 = (bf16[96,1024]{1,0:T(8,128)(2,1)S(1)}, bf16[96,1024]{1,0:T(8,128)(2,1)S(1)}, u32[]{:S(2)}, u32[]{:S(2)}) collective-permute-start(bf16[96,1024]{1,0:T(8,128)(2,1)S(1)} %stack.12.refs_6_), channel_id=1, source_target_pairs={{0,2},{1,3},{2,0},{3,1},{4,6},{5,7},{6,4},{7,5},{8,10},{9,11},{10,... | collective-permute-start | bytes 589832 | tf_op jit(solution)/shard_map/ppermute | solution.py:17
  39.9 9.2 %collective-permute-start.21 = (bf16[96,1024]{1,0:T(8,128)(2,1)S(1)}, bf16[96,1024]{1,0:T(8,128)(2,1)S(1)}, u32[]{:S(2)}, u32[]{:S(2)}) collective-permute-start(bf16[96,1024]{1,0:T(8,128)(2,1)S(1)} %stack.11.refs_5_), channel_id=1, source_target_pairs={{0,4},{1,5},{2,6},{3,7},{4,0},{5,1},{6,2},{7,3},{8,12},{9,13},{10,... | collective-permute-start | bytes 589832 | tf_op jit(solution)/shard_map/ppermute | solution.py:17
  45.6 3.7 %collective-permute-start.19 = (bf16[96,1024]{1,0:T(8,128)(2,1)S(1)}, bf16[96,1024]{1,0:T(8,128)(2,1)S(1)}, u32[]{:S(2)}, u32[]{:S(2)}) collective-permute-start(bf16[96,1024]{1,0:T(8,128)(2,1)S(1)} %stack.14), channel_id=1, source_target_pairs={{0,1},{1,0},{2,3},{3,2},{4,5},{5,4},{6,7},{7,6},{8,9},{9,8},{10,11... | collective-permute-start | bytes 589832 | tf_op jit(solution)/shard_map/ppermute | solution.py:17
  45.7 8.2 %collective-permute-start.24 = (bf16[112,1024]{1,0:T(8,128)(2,1)S(1)}, bf16[112,1024]{1,0:T(8,128)(2,1)S(1)}, u32[]{:S(2)}, u32[]{:S(2)}) collective-permute-start(bf16[112,1024]{1,0:T(8,128)(2,1)S(1)} %copy.11.refs_2_), channel_id=1, source_target_pairs={{0,4},{1,5},{2,6},{3,7},{4,0},{5,1},{6,2},{7,3},{8,12},{9,13},{10,... | collective-permute-start | bytes 688136 | tf_op jit(solution)/shard_map/ppermute | solution.py:17
  46.3 8.1 %collective-permute-start.25 = (bf16[112,1024]{1,0:T(8,128)(2,1)S(1)}, bf16[112,1024]{1,0:T(8,128)(2,1)S(1)}, u32[]{:S(2)}, u32[]{:S(2)}) collective-permute-start(bf16[112,1024]{1,0:T(8,128)(2,1)S(1)} %copy.12.refs_3_), channel_id=1, source_target_pairs={{0,2},{1,3},{2,0},{3,1},{4,6},{5,7},{6,4},{7,5},{8,10},{9,11},{10,... | collective-permute-start | bytes 688136 | tf_op jit(solution)/shard_map/ppermute | solution.py:17
  47.9 2.0 %collective-permute-start.20 = (bf16[96,1024]{1,0:T(8,128)(2,1)S(1)}, bf16[96,1024]{1,0:T(8,128)(2,1)S(1)}, u32[]{:S(2)}, u32[]{:S(2)}) collective-permute-start(bf16[96,1024]{1,0:T(8,128)(2,1)S(1)} %stack.15), channel_id=1, source_target_pairs={{0,1},{1,0},{2,3},{3,2},{4,5},{5,4},{6,7},{7,6},{8,9},{9,8},{10,11... | collective-permute-start | bytes 589832 | tf_op jit(solution)/shard_map/ppermute | solution.py:17
  54.0 2.1 %collective-permute-start.26 = (bf16[96,1024]{1,0:T(8,128)(2,1)S(1)}, bf16[96,1024]{1,0:T(8,128)(2,1)S(1)}, u32[]{:S(2)}, u32[]{:S(2)}) collective-permute-start(bf16[96,1024]{1,0:T(8,128)(2,1)S(1)} %copy.13), channel_id=1, source_target_pairs={{0,1},{1,0},{2,3},{3,2},{4,5},{5,4},{6,7},{7,6},{8,9},{9,8},{10,11... | collective-permute-start | bytes 589832 | tf_op jit(solution)/shard_map/ppermute | solution.py:17
  (6 other events, 16.7 us)
